TPU v7x, 32 devices: a whole 2x2x4 slice. The times are simulated.
32 devices in a mesh: gx: 8 (over z, core), gy: 4 (over y, x).
Axes of the slice: x: 2, y: 2, z: 4, core: 2. Of those that a mesh axis runs over, the one named last changes fastest.
Arguments:
- right_side: float32 [2, 2, 128, 64, 128], P(None, None, 'gx', 'gy'), may hold values from -7 to 7
- slowness: float32 [128, 64, 128], P('gx', 'gy'), may hold values from 0.7 to 1.4
- source_cells: int32 [2, 16], replicated, may hold values from 0 to 1048575
- source_amplitudes: float32 [2, 16, 2], replicated, may hold values from -24 to 24
Outputs:
- wavefield: float32 [2, 2, 128, 64, 128], P(None, None, 'gx', 'gy')
- residual: float32 [2, 2, 128, 64, 128], P(None, None, 'gx', 'gy')
Inputs may be any that keep to these rules, and one draw needn't show every extreme that they name: `source_cells`: flat indices (x * 64 + y) * 128 + z of cells; points may coincide.
All inputs are finite; a program needn't handle non-finite values.
Results may differ from a plain program's by a relative error of at most 0.0003.
Values sent between devices are 32-bit elements; how exact they have to be, the bound alone decides.
No kernel may reach another device: no remote copies, remote signals or barrier semaphores. Data moves between devices by JAX's collectives and lax.ppermute only.
A program may use at most 64 MiB of HBM per device.

v0:
```python
import math

import jax
import jax.numpy as jnp
from jax import lax
from jax.sharding import PartitionSpec as P

KAPPA = 0.12
DAMPING = 0.3
HIGHEST = lax.Precision.HIGHEST


def passed_along(array, axis, by):
    size = lax.axis_size(axis)
    pairs = [(i, i + by) for i in range(size) if 0 <= i + by < size]
    return lax.ppermute(array, axis, pairs)


def extended(cells, sides, width):
    for axis, dim in sides:
        count = lax.axis_size(axis)
        ends = count - 1
        head = lax.slice_in_dim(cells, 0, width, axis=dim)
        tail = lax.slice_in_dim(cells, cells.shape[dim] - width, cells.shape[dim], axis=dim)
        cells = jnp.concatenate(
            [
                lax.ppermute(tail, axis, [(i, (i + 1) % count) for i in range(ends)]),
                cells,
                lax.ppermute(head, axis, [((i + 1) % count, i) for i in range(ends)]),
            ],
            axis=dim,
        )
    return cells


def sine_basis(length):
    positions = jnp.arange(1, length + 1).astype(jnp.float32)
    angles = positions * (math.pi / (length + 1))
    sine_rows = math.sqrt(2.0 / (length + 1)) * jnp.sin(angles[:, None] * positions[None, :])
    return (sine_rows, angles)


def build_tables(size_x, size_y, cells_z):
    sine_x, angle_x = sine_basis(size_x)
    sine_y, angle_y = sine_basis(size_y)
    sine_z, angle_z = sine_basis(cells_z)
    symbol_x = 2.5 - 8.0 / 3.0 * jnp.cos(angle_x) + 1.0 / 6.0 * jnp.cos(2.0 * angle_x)
    symbol_y = 2.5 - 8.0 / 3.0 * jnp.cos(angle_y) + 1.0 / 6.0 * jnp.cos(2.0 * angle_y)
    symbol_z = 2.0 - 2.0 * jnp.cos(angle_z)
    real_part = symbol_x[:, None, None] + symbol_y[None, :, None] + symbol_z[None, None, :] - KAPPA
    denominator = real_part * real_part + (KAPPA * DAMPING) ** 2
    return (sine_x, sine_y, sine_z, real_part / denominator, KAPPA * DAMPING / denominator)


def transform(wavefield, sine_x, sine_y, sine_z):
    result = jnp.einsum("scxyz,zw->scxyw", wavefield, sine_z, precision=HIGHEST)
    result = jnp.einsum("scxyz,xa->scayz", result, sine_x, precision=HIGHEST)
    return jnp.einsum("scxyz,yb->scxbz", result, sine_y, precision=HIGHEST)


def fast_solve(wavefield, tables):
    sine_x, sine_y, sine_z, inverse_real, inverse_imag = tables
    spectrum = transform(wavefield, sine_x, sine_y, sine_z)
    real_part = inverse_real * spectrum[:, 0] - inverse_imag * spectrum[:, 1]
    imag_part = inverse_real * spectrum[:, 1] + inverse_imag * spectrum[:, 0]
    return transform(jnp.stack([real_part, imag_part], axis=1), sine_x, sine_y, sine_z)


def apply_operator(padded, slowness):
    size_x = padded.shape[2] - 4
    size_y = padded.shape[3] - 4
    center = padded[:, :, 2 : 2 + size_x, 2 : 2 + size_y]
    weights = (1.0, -16.0, 30.0, -16.0, 1.0)
    lateral = jnp.zeros_like(center)
    for offset in range(5):
        lateral = lateral + weights[offset] / 12.0 * (
            padded[:, :, offset : offset + size_x, 2 : 2 + size_y]
            + padded[:, :, 2 : 2 + size_x, offset : offset + size_y]
        )
    vertical = jnp.pad(center, ((0, 0), (0, 0), (0, 0), (0, 0), (1, 1)))
    lateral = lateral + 2.0 * center - vertical[..., :-2] - vertical[..., 2:]
    scaled = KAPPA * slowness
    real_part = lateral[:, 0] - scaled * (center[:, 0] - DAMPING * center[:, 1])
    imag_part = lateral[:, 1] - scaled * (center[:, 1] + DAMPING * center[:, 0])
    return jnp.stack([real_part, imag_part], axis=1)


def tile_solve(source_term, trace_x, trace_y, slowness, tables):
    source_term = source_term.at[:, :, 0].add((16.0 * trace_x[:, :, 1] - trace_x[:, :, 0]) / 12.0)
    source_term = source_term.at[:, :, 1].add(-trace_x[:, :, 1] / 12.0)
    source_term = source_term.at[:, :, :, 0].add(
        (16.0 * trace_y[:, :, :, 1] - trace_y[:, :, :, 0]) / 12.0
    )
    source_term = source_term.at[:, :, :, 1].add(-trace_y[:, :, :, 1] / 12.0)
    wavefield = fast_solve(source_term, tables)
    for sweep_step in range(2):
        padded = jnp.pad(wavefield, ((0, 0), (0, 0), (2, 2), (2, 2), (0, 0)))
        wavefield = wavefield + fast_solve(source_term - apply_operator(padded, slowness), tables)
    return wavefield


def point_sources(flat_cells, amplitudes, start_x, start_y, size_x, size_y, cells_z, total_y):
    plane_cells = total_y * cells_z
    coord_x = flat_cells // plane_cells - start_x
    coord_y = flat_cells // cells_z % total_y - start_y
    coord_z = flat_cells % cells_z
    match_x = (coord_x[:, :, None] == jnp.arange(size_x, dtype=jnp.int32)[None, None, :]).astype(
        jnp.float32
    )
    match_y = (coord_y[:, :, None] == jnp.arange(size_y, dtype=jnp.int32)[None, None, :]).astype(
        jnp.float32
    )
    match_z = (coord_z[:, :, None] == jnp.arange(cells_z, dtype=jnp.int32)[None, None, :]).astype(
        jnp.float32
    )
    return jnp.einsum(
        "spc,spx,spy,spz->scxyz", amplitudes, match_x, match_y, match_z, precision=HIGHEST
    )


def body(right_side, slowness, source_cells, source_amplitudes):
    sources = right_side.shape[0]
    size_x = right_side.shape[2]
    size_y = right_side.shape[3]
    cells_z = right_side.shape[4]
    grid_rows = lax.axis_size("gx")
    grid_cols = lax.axis_size("gy")
    tile_row = lax.axis_index("gx")
    tile_col = lax.axis_index("gy")
    forcing = right_side + point_sources(
        source_cells,
        source_amplitudes,
        tile_row * size_x,
        tile_col * size_y,
        size_x,
        size_y,
        cells_z,
        size_y * grid_cols,
    )
    tables = build_tables(size_x, size_y, cells_z)
    wavefield = jnp.zeros_like(forcing)
    trace_x = jnp.zeros((sources, 2, 2, size_y, cells_z), jnp.float32)
    trace_y = jnp.zeros((sources, 2, size_x, 2, cells_z), jnp.float32)

    def advance(beat_index, loop_state):
        current, prior_x, prior_y, outbound_x, outbound_y = loop_state
        inbound_x = passed_along(outbound_x, "gx", 1)
        inbound_y = passed_along(outbound_y, "gy", 1)
        slot_index = beat_index - tile_row - tile_col
        active = jnp.logical_and(slot_index >= 0, slot_index < sources)
        clamped = jnp.clip(slot_index, 0, sources - 1)
        solved = tile_solve(
            lax.dynamic_slice_in_dim(forcing, clamped, 1, 0), inbound_x, inbound_y, slowness, tables
        )
        solved = jnp.where(active, solved, lax.dynamic_slice_in_dim(current, clamped, 1, 0))
        kept_x = jnp.where(active, inbound_x, lax.dynamic_slice_in_dim(prior_x, clamped, 1, 0))
        kept_y = jnp.where(active, inbound_y, lax.dynamic_slice_in_dim(prior_y, clamped, 1, 0))
        current = lax.dynamic_update_slice_in_dim(current, solved, clamped, 0)
        prior_x = lax.dynamic_update_slice_in_dim(prior_x, kept_x, clamped, 0)
        prior_y = lax.dynamic_update_slice_in_dim(prior_y, kept_y, clamped, 0)
        return (
            current,
            prior_x,
            prior_y,
            solved[:, :, size_x - 2 :],
            solved[:, :, :, size_y - 2 :],
        )

    start_x = jnp.zeros((1, 2, 2, size_y, cells_z), jnp.float32)
    start_y = jnp.zeros((1, 2, size_x, 2, cells_z), jnp.float32)
    wavefield, trace_x, trace_y, start_x, start_y = lax.fori_loop(
        0,
        grid_rows + grid_cols + sources - 2,
        advance,
        (wavefield, trace_x, trace_y, start_x, start_y),
    )
    padded = extended(wavefield, (("gx", 2), ("gy", 3)), 2)
    residual = forcing - apply_operator(padded, slowness)
    return (wavefield, residual)


def solution(mesh):
    return jax.shard_map(
        body,
        mesh=mesh,
        in_specs=(P(None, None, "gx", "gy", None), P("gx", "gy", None), P(), P()),
        out_specs=(P(None, None, "gx", "gy", None), P(None, None, "gx", "gy", None)),
        check_vma=False,
    )
```

profile of v0, /device:TPU:10, one launch (start us, length us, event | category | flops | bytes accessed | tf_op | source)
XLA Modules:
  0.0 269.5 jit_solution(10990419118916808154)
XLA Ops:
  0.8 0.7 copy-done.3
  1.6 0.7 copy-done.2
  2.2 1.8 fusion.165
  4.5 0.8 copy-done
  5.3 240.1 %while.27 = (s32[]{:T(128)}, f32[2,2,16,16,128]{4,3,2,1,0:T(8,128)S(1)}, f32[1,2,2,16,128]{4,3,2,1,0:T(8,128)S(1)}, f32[1,2,16,2,128]{4,3,2,1,0:T(2,128)S(1)}, s...) while((s32[]{:T(128)}, ...), condition=%wide.region_1.2_spmd.clone.clone.clone, body=%wide.region_0.1_spmd.clone.clone.clone.sunk | while | flops 760018944 | bytes 19575128 | solution.py:171
  5.3 1.9 collective-permute-start
  7.2 3.4 %collective-permute-start.1 = (f32[1,2,16,2,128]{4,3,2,1,0:T(2,128)S(1)}, f32[1,2,16,2,128]{4,3,2,1,0:T(2,128)S(1)}, u32[]{:S(2)}, u32[]{:S(2)}) collective-permute-start(f32[1,2,16,2,128]{4,3,2,1,0:T(2,128)S(1)} %get-tuple-element.865), channel_id=1, source_target_pairs={{0,1},{1,2},{2,3},{4,5},{5,6},{6,7},{8,9},{9,10},{10,11},{12,13},{... | collective-permute-start | bytes 98312 | tf_op jit(solution)/shard_map/while/body/eval_jaxpr/ppermute | solution.py:16
  10.8 2.3 collective-permute-done.1
  24.4 2.4 collective-permute-start
  26.8 4.3 %collective-permute-start.1 = (f32[1,2,16,2,128]{4,3,2,1,0:T(2,128)S(1)}, f32[1,2,16,2,128]{4,3,2,1,0:T(2,128)S(1)}, u32[]{:S(2)}, u32[]{:S(2)}) collective-permute-start(f32[1,2,16,2,128]{4,3,2,1,0:T(2,128)S(1)} %get-tuple-element.865), channel_id=1, source_target_pairs={{0,1},{1,2},{2,3},{4,5},{5,6},{6,7},{8,9},{9,10},{10,11},{12,13},{... | collective-permute-start | bytes 98312 | tf_op jit(solution)/shard_map/while/body/eval_jaxpr/ppermute | solution.py:16
  31.2 1.6 collective-permute-done.1
  44.1 2.1 collective-permute-start
  46.3 5.1 %collective-permute-start.1 = (f32[1,2,16,2,128]{4,3,2,1,0:T(2,128)S(1)}, f32[1,2,16,2,128]{4,3,2,1,0:T(2,128)S(1)}, u32[]{:S(2)}, u32[]{:S(2)}) collective-permute-start(f32[1,2,16,2,128]{4,3,2,1,0:T(2,128)S(1)} %get-tuple-element.865), channel_id=1, source_target_pairs={{0,1},{1,2},{2,3},{4,5},{5,6},{6,7},{8,9},{9,10},{10,11},{12,13},{... | collective-permute-start | bytes 98312 | tf_op jit(solution)/shard_map/while/body/eval_jaxpr/ppermute | solution.py:16
  51.5 1.5 collective-permute-done.1
  64.3 2.6 collective-permute-start
  66.9 4.8 %collective-permute-start.1 = (f32[1,2,16,2,128]{4,3,2,1,0:T(2,128)S(1)}, f32[1,2,16,2,128]{4,3,2,1,0:T(2,128)S(1)}, u32[]{:S(2)}, u32[]{:S(2)}) collective-permute-start(f32[1,2,16,2,128]{4,3,2,1,0:T(2,128)S(1)} %get-tuple-element.865), channel_id=1, source_target_pairs={{0,1},{1,2},{2,3},{4,5},{5,6},{6,7},{8,9},{9,10},{10,11},{12,13},{... | collective-permute-start | bytes 98312 | tf_op jit(solution)/shard_map/while/body/eval_jaxpr/ppermute | solution.py:16
  71.8 1.5 collective-permute-done.1
  84.7 2.6 collective-permute-start
  87.3 4.8 %collective-permute-start.1 = (f32[1,2,16,2,128]{4,3,2,1,0:T(2,128)S(1)}, f32[1,2,16,2,128]{4,3,2,1,0:T(2,128)S(1)}, u32[]{:S(2)}, u32[]{:S(2)}) collective-permute-start(f32[1,2,16,2,128]{4,3,2,1,0:T(2,128)S(1)} %get-tuple-element.865), channel_id=1, source_target_pairs={{0,1},{1,2},{2,3},{4,5},{5,6},{6,7},{8,9},{9,10},{10,11},{12,13},{... | collective-permute-start | bytes 98312 | tf_op jit(solution)/shard_map/while/body/eval_jaxpr/ppermute | solution.py:16
  92.2 1.5 collective-permute-done.1
  105.0 2.2 collective-permute-start
  107.3 5.0 %collective-permute-start.1 = (f32[1,2,16,2,128]{4,3,2,1,0:T(2,128)S(1)}, f32[1,2,16,2,128]{4,3,2,1,0:T(2,128)S(1)}, u32[]{:S(2)}, u32[]{:S(2)}) collective-permute-start(f32[1,2,16,2,128]{4,3,2,1,0:T(2,128)S(1)} %get-tuple-element.865), channel_id=1, source_target_pairs={{0,1},{1,2},{2,3},{4,5},{5,6},{6,7},{8,9},{9,10},{10,11},{12,13},{... | collective-permute-start | bytes 98312 | tf_op jit(solution)/shard_map/while/body/eval_jaxpr/ppermute | solution.py:16
  112.4 1.7 collective-permute-done.1
  125.4 2.0 collective-permute-start
  127.4 5.3 %collective-permute-start.1 = (f32[1,2,16,2,128]{4,3,2,1,0:T(2,128)S(1)}, f32[1,2,16,2,128]{4,3,2,1,0:T(2,128)S(1)}, u32[]{:S(2)}, u32[]{:S(2)}) collective-permute-start(f32[1,2,16,2,128]{4,3,2,1,0:T(2,128)S(1)} %get-tuple-element.865), channel_id=1, source_target_pairs={{0,1},{1,2},{2,3},{4,5},{5,6},{6,7},{8,9},{9,10},{10,11},{12,13},{... | collective-permute-start | bytes 98312 | tf_op jit(solution)/shard_map/while/body/eval_jaxpr/ppermute | solution.py:16
  132.8 1.5 collective-permute-done.1
  145.6 1.9 collective-permute-start
  147.5 5.1 %collective-permute-start.1 = (f32[1,2,16,2,128]{4,3,2,1,0:T(2,128)S(1)}, f32[1,2,16,2,128]{4,3,2,1,0:T(2,128)S(1)}, u32[]{:S(2)}, u32[]{:S(2)}) collective-permute-start(f32[1,2,16,2,128]{4,3,2,1,0:T(2,128)S(1)} %get-tuple-element.865), channel_id=1, source_target_pairs={{0,1},{1,2},{2,3},{4,5},{5,6},{6,7},{8,9},{9,10},{10,11},{12,13},{... | collective-permute-start | bytes 98312 | tf_op jit(solution)/shard_map/while/body/eval_jaxpr/ppermute | solution.py:16
  152.8 1.5 collective-permute-done.1
  165.6 1.9 collective-permute-start
  167.5 5.1 %collective-permute-start.1 = (f32[1,2,16,2,128]{4,3,2,1,0:T(2,128)S(1)}, f32[1,2,16,2,128]{4,3,2,1,0:T(2,128)S(1)}, u32[]{:S(2)}, u32[]{:S(2)}) collective-permute-start(f32[1,2,16,2,128]{4,3,2,1,0:T(2,128)S(1)} %get-tuple-element.865), channel_id=1, source_target_pairs={{0,1},{1,2},{2,3},{4,5},{5,6},{6,7},{8,9},{9,10},{10,11},{12,13},{... | collective-permute-start | bytes 98312 | tf_op jit(solution)/shard_map/while/body/eval_jaxpr/ppermute | solution.py:16
  172.7 1.5 collective-permute-done.1
  185.5 1.9 collective-permute-start
  187.5 5.1 %collective-permute-start.1 = (f32[1,2,16,2,128]{4,3,2,1,0:T(2,128)S(1)}, f32[1,2,16,2,128]{4,3,2,1,0:T(2,128)S(1)}, u32[]{:S(2)}, u32[]{:S(2)}) collective-permute-start(f32[1,2,16,2,128]{4,3,2,1,0:T(2,128)S(1)} %get-tuple-element.865), channel_id=1, source_target_pairs={{0,1},{1,2},{2,3},{4,5},{5,6},{6,7},{8,9},{9,10},{10,11},{12,13},{... | collective-permute-start | bytes 98312 | tf_op jit(solution)/shard_map/while/body/eval_jaxpr/ppermute | solution.py:16
  192.7 1.5 collective-permute-done.1
  205.5 1.9 collective-permute-start
  207.4 5.1 %collective-permute-start.1 = (f32[1,2,16,2,128]{4,3,2,1,0:T(2,128)S(1)}, f32[1,2,16,2,128]{4,3,2,1,0:T(2,128)S(1)}, u32[]{:S(2)}, u32[]{:S(2)}) collective-permute-start(f32[1,2,16,2,128]{4,3,2,1,0:T(2,128)S(1)} %get-tuple-element.865), channel_id=1, source_target_pairs={{0,1},{1,2},{2,3},{4,5},{5,6},{6,7},{8,9},{9,10},{10,11},{12,13},{... | collective-permute-start | bytes 98312 | tf_op jit(solution)/shard_map/while/body/eval_jaxpr/ppermute | solution.py:16
  212.7 1.5 collective-permute-done.1
  225.5 1.9 collective-permute-start
  227.4 5.1 %collective-permute-start.1 = (f32[1,2,16,2,128]{4,3,2,1,0:T(2,128)S(1)}, f32[1,2,16,2,128]{4,3,2,1,0:T(2,128)S(1)}, u32[]{:S(2)}, u32[]{:S(2)}) collective-permute-start(f32[1,2,16,2,128]{4,3,2,1,0:T(2,128)S(1)} %get-tuple-element.865), channel_id=1, source_target_pairs={{0,1},{1,2},{2,3},{4,5},{5,6},{6,7},{8,9},{9,10},{10,11},{12,13},{... | collective-permute-start | bytes 98312 | tf_op jit(solution)/shard_map/while/body/eval_jaxpr/ppermute | solution.py:16
  232.6 1.5 collective-permute-done.1
  246.3 2.8 %collective-permute-start.3 = (f32[2,2,2,16,128]{4,2,1,3,0:T(2,128)S(1)}, f32[2,2,2,16,128]{4,2,1,3,0:T(2,128)S(1)}, u32[]{:S(2)}, u32[]{:S(2)}) collective-permute-start(f32[2,2,2,16,128]{4,2,1,3,0:T(2,128)S(1)} %get-tuple-element.731), channel_id=1, source_target_pairs={{4,0},{8,4},{12,8},{16,12},{20,16},{24,20},{28,24},{5,1},{9,5},{13... | collective-permute-start | bytes 196616 | tf_op jit(solution)/shard_map/ppermute | solution.py:29
  249.1 1.9 collective-permute-start.2
  251.1 3.6 %collective-permute-done.2 = f32[2,2,2,16,128]{4,2,1,3,0:T(2,128)S(1)} collective-permute-done((f32[2,2,2,16,128]{4,2,1,3,0:T(2,128)S(1)}, f32[2,2,2,16,128]{4,2,1,3,0:T(2,128)S(1)}, u32[]{:S(2)}, u32[]{:S(2)}) %collective-permute-start.2) | collective-permute-done | bytes 65568 | tf_op jit(solution)/shard_map/ppermute | solution.py:27
  254.7 5.3 %collective-permute-start.4 = (f32[2,2,20,2,128]{4,2,1,3,0:T(8,128)S(1)}, f32[2,2,20,2,128]{4,2,1,3,0:T(8,128)S(1)}, u32[]{:S(2)}, u32[]{:S(2)}) collective-permute-start(f32[2,2,20,2,128]{4,2,1,3,0:T(8,128)S(1)} %get-tuple-element.727), channel_id=1, source_target_pairs={{0,1},{1,2},{2,3},{4,5},{5,6},{6,7},{8,9},{9,10},{10,11},{12,13},{... | collective-permute-start | bytes 245768 | tf_op jit(solution)/shard_map/ppermute | solution.py:27
  260.0 1.9 collective-permute-start.5
  262.2 5.2 %collective-permute-done.5 = f32[2,2,20,2,128]{4,2,1,3,0:T(8,128)S(1)} collective-permute-done((f32[2,2,20,2,128]{4,2,1,3,0:T(8,128)S(1)}, f32[2,2,20,2,128]{4,2,1,3,0:T(8,128)S(1)}, u32[]{:S(2)}, u32[]{:S(2)}) %collective-permute-start.5) | collective-permute-done | bytes 81952 | tf_op jit(solution)/shard_map/ppermute | solution.py:29
  268.4 1.1 copy.26
  (522 shorter events, 135.9 us)
Async XLA Ops:
  0.8 0.7 copy-start.3
  1.6 0.7 copy-start.2
  4.4 0.9 copy-start
  5.3 5.4 %collective-permute-start = (f32[1,2,2,16,128]{4,3,2,1,0:T(8,128)S(1)}, f32[1,2,2,16,128]{4,3,2,1,0:T(8,128)S(1)}, u32[]{:S(2)}, u32[]{:S(2)}) collective-permute-start(f32[1,2,2,16,128]{4,3,2,1,0:T(8,128)S(1)} %get-tuple-element.864), channel_id=1, source_target_pairs={{0,4},{4,8},{8,12},{12,16},{16,20},{20,24},{24,28},{1,5},{5,9},{9,... | collective-permute-start | bytes 98312 | tf_op jit(solution)/shard_map/while/body/eval_jaxpr/ppermute | solution.py:16
  7.2 5.8 %collective-permute-start.1 = (f32[1,2,16,2,128]{4,3,2,1,0:T(2,128)S(1)}, f32[1,2,16,2,128]{4,3,2,1,0:T(2,128)S(1)}, u32[]{:S(2)}, u32[]{:S(2)}) collective-permute-start(f32[1,2,16,2,128]{4,3,2,1,0:T(2,128)S(1)} %get-tuple-element.865), channel_id=1, source_target_pairs={{0,1},{1,2},{2,3},{4,5},{5,6},{6,7},{8,9},{9,10},{10,11},{12,13},{... | collective-permute-start | bytes 98312 | tf_op jit(solution)/shard_map/while/body/eval_jaxpr/ppermute | solution.py:16
  24.4 6.8 %collective-permute-start = (f32[1,2,2,16,128]{4,3,2,1,0:T(8,128)S(1)}, f32[1,2,2,16,128]{4,3,2,1,0:T(8,128)S(1)}, u32[]{:S(2)}, u32[]{:S(2)}) collective-permute-start(f32[1,2,2,16,128]{4,3,2,1,0:T(8,128)S(1)} %get-tuple-element.864), channel_id=1, source_target_pairs={{0,4},{4,8},{8,12},{12,16},{16,20},{20,24},{24,28},{1,5},{5,9},{9,... | collective-permute-start | bytes 98312 | tf_op jit(solution)/shard_map/while/body/eval_jaxpr/ppermute | solution.py:16
  26.8 6.0 %collective-permute-start.1 = (f32[1,2,16,2,128]{4,3,2,1,0:T(2,128)S(1)}, f32[1,2,16,2,128]{4,3,2,1,0:T(2,128)S(1)}, u32[]{:S(2)}, u32[]{:S(2)}) collective-permute-start(f32[1,2,16,2,128]{4,3,2,1,0:T(2,128)S(1)} %get-tuple-element.865), channel_id=1, source_target_pairs={{0,1},{1,2},{2,3},{4,5},{5,6},{6,7},{8,9},{9,10},{10,11},{12,13},{... | collective-permute-start | bytes 98312 | tf_op jit(solution)/shard_map/while/body/eval_jaxpr/ppermute | solution.py:16
  44.1 7.3 %collective-permute-start = (f32[1,2,2,16,128]{4,3,2,1,0:T(8,128)S(1)}, f32[1,2,2,16,128]{4,3,2,1,0:T(8,128)S(1)}, u32[]{:S(2)}, u32[]{:S(2)}) collective-permute-start(f32[1,2,2,16,128]{4,3,2,1,0:T(8,128)S(1)} %get-tuple-element.864), channel_id=1, source_target_pairs={{0,4},{4,8},{8,12},{12,16},{16,20},{20,24},{24,28},{1,5},{5,9},{9,... | collective-permute-start | bytes 98312 | tf_op jit(solution)/shard_map/while/body/eval_jaxpr/ppermute | solution.py:16
  46.3 6.7 %collective-permute-start.1 = (f32[1,2,16,2,128]{4,3,2,1,0:T(2,128)S(1)}, f32[1,2,16,2,128]{4,3,2,1,0:T(2,128)S(1)}, u32[]{:S(2)}, u32[]{:S(2)}) collective-permute-start(f32[1,2,16,2,128]{4,3,2,1,0:T(2,128)S(1)} %get-tuple-element.865), channel_id=1, source_target_pairs={{0,1},{1,2},{2,3},{4,5},{5,6},{6,7},{8,9},{9,10},{10,11},{12,13},{... | collective-permute-start | bytes 98312 | tf_op jit(solution)/shard_map/while/body/eval_jaxpr/ppermute | solution.py:16
  64.3 7.5 %collective-permute-start = (f32[1,2,2,16,128]{4,3,2,1,0:T(8,128)S(1)}, f32[1,2,2,16,128]{4,3,2,1,0:T(8,128)S(1)}, u32[]{:S(2)}, u32[]{:S(2)}) collective-permute-start(f32[1,2,2,16,128]{4,3,2,1,0:T(8,128)S(1)} %get-tuple-element.864), channel_id=1, source_target_pairs={{0,4},{4,8},{8,12},{12,16},{16,20},{20,24},{24,28},{1,5},{5,9},{9,... | collective-permute-start | bytes 98312 | tf_op jit(solution)/shard_map/while/body/eval_jaxpr/ppermute | solution.py:16
  66.9 6.4 %collective-permute-start.1 = (f32[1,2,16,2,128]{4,3,2,1,0:T(2,128)S(1)}, f32[1,2,16,2,128]{4,3,2,1,0:T(2,128)S(1)}, u32[]{:S(2)}, u32[]{:S(2)}) collective-permute-start(f32[1,2,16,2,128]{4,3,2,1,0:T(2,128)S(1)} %get-tuple-element.865), channel_id=1, source_target_pairs={{0,1},{1,2},{2,3},{4,5},{5,6},{6,7},{8,9},{9,10},{10,11},{12,13},{... | collective-permute-start | bytes 98312 | tf_op jit(solution)/shard_map/while/body/eval_jaxpr/ppermute | solution.py:16
  84.7 7.5 %collective-permute-start = (f32[1,2,2,16,128]{4,3,2,1,0:T(8,128)S(1)}, f32[1,2,2,16,128]{4,3,2,1,0:T(8,128)S(1)}, u32[]{:S(2)}, u32[]{:S(2)}) collective-permute-start(f32[1,2,2,16,128]{4,3,2,1,0:T(8,128)S(1)} %get-tuple-element.864), channel_id=1, source_target_pairs={{0,4},{4,8},{8,12},{12,16},{16,20},{20,24},{24,28},{1,5},{5,9},{9,... | collective-permute-start | bytes 98312 | tf_op jit(solution)/shard_map/while/body/eval_jaxpr/ppermute | solution.py:16
  87.3 6.4 %collective-permute-start.1 = (f32[1,2,16,2,128]{4,3,2,1,0:T(2,128)S(1)}, f32[1,2,16,2,128]{4,3,2,1,0:T(2,128)S(1)}, u32[]{:S(2)}, u32[]{:S(2)}) collective-permute-start(f32[1,2,16,2,128]{4,3,2,1,0:T(2,128)S(1)} %get-tuple-element.865), channel_id=1, source_target_pairs={{0,1},{1,2},{2,3},{4,5},{5,6},{6,7},{8,9},{9,10},{10,11},{12,13},{... | collective-permute-start | bytes 98312 | tf_op jit(solution)/shard_map/while/body/eval_jaxpr/ppermute | solution.py:16
  105.0 7.3 %collective-permute-start = (f32[1,2,2,16,128]{4,3,2,1,0:T(8,128)S(1)}, f32[1,2,2,16,128]{4,3,2,1,0:T(8,128)S(1)}, u32[]{:S(2)}, u32[]{:S(2)}) collective-permute-start(f32[1,2,2,16,128]{4,3,2,1,0:T(8,128)S(1)} %get-tuple-element.864), channel_id=1, source_target_pairs={{0,4},{4,8},{8,12},{12,16},{16,20},{20,24},{24,28},{1,5},{5,9},{9,... | collective-permute-start | bytes 98312 | tf_op jit(solution)/shard_map/while/body/eval_jaxpr/ppermute | solution.py:16
  107.3 6.8 %collective-permute-start.1 = (f32[1,2,16,2,128]{4,3,2,1,0:T(2,128)S(1)}, f32[1,2,16,2,128]{4,3,2,1,0:T(2,128)S(1)}, u32[]{:S(2)}, u32[]{:S(2)}) collective-permute-start(f32[1,2,16,2,128]{4,3,2,1,0:T(2,128)S(1)} %get-tuple-element.865), channel_id=1, source_target_pairs={{0,1},{1,2},{2,3},{4,5},{5,6},{6,7},{8,9},{9,10},{10,11},{12,13},{... | collective-permute-start | bytes 98312 | tf_op jit(solution)/shard_map/while/body/eval_jaxpr/ppermute | solution.py:16
  125.4 7.4 %collective-permute-start = (f32[1,2,2,16,128]{4,3,2,1,0:T(8,128)S(1)}, f32[1,2,2,16,128]{4,3,2,1,0:T(8,128)S(1)}, u32[]{:S(2)}, u32[]{:S(2)}) collective-permute-start(f32[1,2,2,16,128]{4,3,2,1,0:T(8,128)S(1)} %get-tuple-element.864), channel_id=1, source_target_pairs={{0,4},{4,8},{8,12},{12,16},{16,20},{20,24},{24,28},{1,5},{5,9},{9,... | collective-permute-start | bytes 98312 | tf_op jit(solution)/shard_map/while/body/eval_jaxpr/ppermute | solution.py:16
  127.4 6.9 %collective-permute-start.1 = (f32[1,2,16,2,128]{4,3,2,1,0:T(2,128)S(1)}, f32[1,2,16,2,128]{4,3,2,1,0:T(2,128)S(1)}, u32[]{:S(2)}, u32[]{:S(2)}) collective-permute-start(f32[1,2,16,2,128]{4,3,2,1,0:T(2,128)S(1)} %get-tuple-element.865), channel_id=1, source_target_pairs={{0,1},{1,2},{2,3},{4,5},{5,6},{6,7},{8,9},{9,10},{10,11},{12,13},{... | collective-permute-start | bytes 98312 | tf_op jit(solution)/shard_map/while/body/eval_jaxpr/ppermute | solution.py:16
  145.6 7.1 %collective-permute-start = (f32[1,2,2,16,128]{4,3,2,1,0:T(8,128)S(1)}, f32[1,2,2,16,128]{4,3,2,1,0:T(8,128)S(1)}, u32[]{:S(2)}, u32[]{:S(2)}) collective-permute-start(f32[1,2,2,16,128]{4,3,2,1,0:T(8,128)S(1)} %get-tuple-element.864), channel_id=1, source_target_pairs={{0,4},{4,8},{8,12},{12,16},{16,20},{20,24},{24,28},{1,5},{5,9},{9,... | collective-permute-start | bytes 98312 | tf_op jit(solution)/shard_map/while/body/eval_jaxpr/ppermute | solution.py:16
  147.5 6.7 %collective-permute-start.1 = (f32[1,2,16,2,128]{4,3,2,1,0:T(2,128)S(1)}, f32[1,2,16,2,128]{4,3,2,1,0:T(2,128)S(1)}, u32[]{:S(2)}, u32[]{:S(2)}) collective-permute-start(f32[1,2,16,2,128]{4,3,2,1,0:T(2,128)S(1)} %get-tuple-element.865), channel_id=1, source_target_pairs={{0,1},{1,2},{2,3},{4,5},{5,6},{6,7},{8,9},{9,10},{10,11},{12,13},{... | collective-permute-start | bytes 98312 | tf_op jit(solution)/shard_map/while/body/eval_jaxpr/ppermute | solution.py:16
  165.6 7.1 %collective-permute-start = (f32[1,2,2,16,128]{4,3,2,1,0:T(8,128)S(1)}, f32[1,2,2,16,128]{4,3,2,1,0:T(8,128)S(1)}, u32[]{:S(2)}, u32[]{:S(2)}) collective-permute-start(f32[1,2,2,16,128]{4,3,2,1,0:T(8,128)S(1)} %get-tuple-element.864), channel_id=1, source_target_pairs={{0,4},{4,8},{8,12},{12,16},{16,20},{20,24},{24,28},{1,5},{5,9},{9,... | collective-permute-start | bytes 98312 | tf_op jit(solution)/shard_map/while/body/eval_jaxpr/ppermute | solution.py:16
  167.5 6.7 %collective-permute-start.1 = (f32[1,2,16,2,128]{4,3,2,1,0:T(2,128)S(1)}, f32[1,2,16,2,128]{4,3,2,1,0:T(2,128)S(1)}, u32[]{:S(2)}, u32[]{:S(2)}) collective-permute-start(f32[1,2,16,2,128]{4,3,2,1,0:T(2,128)S(1)} %get-tuple-element.865), channel_id=1, source_target_pairs={{0,1},{1,2},{2,3},{4,5},{5,6},{6,7},{8,9},{9,10},{10,11},{12,13},{... | collective-permute-start | bytes 98312 | tf_op jit(solution)/shard_map/while/body/eval_jaxpr/ppermute | solution.py:16
  185.5 7.1 %collective-permute-start = (f32[1,2,2,16,128]{4,3,2,1,0:T(8,128)S(1)}, f32[1,2,2,16,128]{4,3,2,1,0:T(8,128)S(1)}, u32[]{:S(2)}, u32[]{:S(2)}) collective-permute-start(f32[1,2,2,16,128]{4,3,2,1,0:T(8,128)S(1)} %get-tuple-element.864), channel_id=1, source_target_pairs={{0,4},{4,8},{8,12},{12,16},{16,20},{20,24},{24,28},{1,5},{5,9},{9,... | collective-permute-start | bytes 98312 | tf_op jit(solution)/shard_map/while/body/eval_jaxpr/ppermute | solution.py:16
  187.5 6.7 %collective-permute-start.1 = (f32[1,2,16,2,128]{4,3,2,1,0:T(2,128)S(1)}, f32[1,2,16,2,128]{4,3,2,1,0:T(2,128)S(1)}, u32[]{:S(2)}, u32[]{:S(2)}) collective-permute-start(f32[1,2,16,2,128]{4,3,2,1,0:T(2,128)S(1)} %get-tuple-element.865), channel_id=1, source_target_pairs={{0,1},{1,2},{2,3},{4,5},{5,6},{6,7},{8,9},{9,10},{10,11},{12,13},{... | collective-permute-start | bytes 98312 | tf_op jit(solution)/shard_map/while/body/eval_jaxpr/ppermute | solution.py:16
  205.5 7.1 %collective-permute-start = (f32[1,2,2,16,128]{4,3,2,1,0:T(8,128)S(1)}, f32[1,2,2,16,128]{4,3,2,1,0:T(8,128)S(1)}, u32[]{:S(2)}, u32[]{:S(2)}) collective-permute-start(f32[1,2,2,16,128]{4,3,2,1,0:T(8,128)S(1)} %get-tuple-element.864), channel_id=1, source_target_pairs={{0,4},{4,8},{8,12},{12,16},{16,20},{20,24},{24,28},{1,5},{5,9},{9,... | collective-permute-start | bytes 98312 | tf_op jit(solution)/shard_map/while/body/eval_jaxpr/ppermute | solution.py:16
  207.4 6.7 %collective-permute-start.1 = (f32[1,2,16,2,128]{4,3,2,1,0:T(2,128)S(1)}, f32[1,2,16,2,128]{4,3,2,1,0:T(2,128)S(1)}, u32[]{:S(2)}, u32[]{:S(2)}) collective-permute-start(f32[1,2,16,2,128]{4,3,2,1,0:T(2,128)S(1)} %get-tuple-element.865), channel_id=1, source_target_pairs={{0,1},{1,2},{2,3},{4,5},{5,6},{6,7},{8,9},{9,10},{10,11},{12,13},{... | collective-permute-start | bytes 98312 | tf_op jit(solution)/shard_map/while/body/eval_jaxpr/ppermute | solution.py:16
  225.5 7.1 %collective-permute-start = (f32[1,2,2,16,128]{4,3,2,1,0:T(8,128)S(1)}, f32[1,2,2,16,128]{4,3,2,1,0:T(8,128)S(1)}, u32[]{:S(2)}, u32[]{:S(2)}) collective-permute-start(f32[1,2,2,16,128]{4,3,2,1,0:T(8,128)S(1)} %get-tuple-element.864), channel_id=1, source_target_pairs={{0,4},{4,8},{8,12},{12,16},{16,20},{20,24},{24,28},{1,5},{5,9},{9,... | collective-permute-start | bytes 98312 | tf_op jit(solution)/shard_map/while/body/eval_jaxpr/ppermute | solution.py:16
  227.4 6.7 %collective-permute-start.1 = (f32[1,2,16,2,128]{4,3,2,1,0:T(2,128)S(1)}, f32[1,2,16,2,128]{4,3,2,1,0:T(2,128)S(1)}, u32[]{:S(2)}, u32[]{:S(2)}) collective-permute-start(f32[1,2,16,2,128]{4,3,2,1,0:T(2,128)S(1)} %get-tuple-element.865), channel_id=1, source_target_pairs={{0,1},{1,2},{2,3},{4,5},{5,6},{6,7},{8,9},{9,10},{10,11},{12,13},{... | collective-permute-start | bytes 98312 | tf_op jit(solution)/shard_map/while/body/eval_jaxpr/ppermute | solution.py:16
  245.4 0.8 copy-start.1
  246.3 4.8 %collective-permute-start.3 = (f32[2,2,2,16,128]{4,2,1,3,0:T(2,128)S(1)}, f32[2,2,2,16,128]{4,2,1,3,0:T(2,128)S(1)}, u32[]{:S(2)}, u32[]{:S(2)}) collective-permute-start(f32[2,2,2,16,128]{4,2,1,3,0:T(2,128)S(1)} %get-tuple-element.731), channel_id=1, source_target_pairs={{4,0},{8,4},{12,8},{16,12},{20,16},{24,20},{28,24},{5,1},{9,5},{13... | collective-permute-start | bytes 196616 | tf_op jit(solution)/shard_map/ppermute | solution.py:29
  249.1 5.6 %collective-permute-start.2 = (f32[2,2,2,16,128]{4,2,1,3,0:T(2,128)S(1)}, f32[2,2,2,16,128]{4,2,1,3,0:T(2,128)S(1)}, u32[]{:S(2)}, u32[]{:S(2)}) collective-permute-start(f32[2,2,2,16,128]{4,2,1,3,0:T(2,128)S(1)} %get-tuple-element.732), channel_id=1, source_target_pairs={{0,4},{4,8},{8,12},{12,16},{16,20},{20,24},{24,28},{1,5},{5,9},{9,... | collective-permute-start | bytes 196616 | tf_op jit(solution)/shard_map/ppermute | solution.py:27
  254.7 7.5 %collective-permute-start.4 = (f32[2,2,20,2,128]{4,2,1,3,0:T(8,128)S(1)}, f32[2,2,20,2,128]{4,2,1,3,0:T(8,128)S(1)}, u32[]{:S(2)}, u32[]{:S(2)}) collective-permute-start(f32[2,2,20,2,128]{4,2,1,3,0:T(8,128)S(1)} %get-tuple-element.727), channel_id=1, source_target_pairs={{0,1},{1,2},{2,3},{4,5},{5,6},{6,7},{8,9},{9,10},{10,11},{12,13},{... | collective-permute-start | bytes 245768 | tf_op jit(solution)/shard_map/ppermute | solution.py:27
  260.0 7.4 %collective-permute-start.5 = (f32[2,2,20,2,128]{4,2,1,3,0:T(8,128)S(1)}, f32[2,2,20,2,128]{4,2,1,3,0:T(8,128)S(1)}, u32[]{:S(2)}, u32[]{:S(2)}) collective-permute-start(f32[2,2,20,2,128]{4,2,1,3,0:T(8,128)S(1)} %get-tuple-element.728), channel_id=1, source_target_pairs={{1,0},{2,1},{3,2},{5,4},{6,5},{7,6},{9,8},{10,9},{11,10},{13,12},{... | collective-permute-start | bytes 245768 | tf_op jit(solution)/shard_map/ppermute | solution.py:29
where the time goes:
time: 270 us; the launch traced here: 269 us
  matrix products  118 us (44%)
  starting transfers between devices  95.9 us (36%)
  waiting for transfers between devices  27.9 us (10%)
  other arithmetic  15.7 us (6%)
  local copies, waits for them, and re-layouts  7.37 us (3%)
  loops' own time  4.18 us (2%)
    ppermute x24, starting transfers between devices, passed_along(): return lax.ppermute(array, axis, pairs)  84 us
    dot_general x72, matrix products, transform(): result = jnp.einsum('scxyz,zw->scxyw', wavefield, sine_z, precision=HIGHEST)  47.5 us
    dot_general x72, matrix products, transform(): return jnp.einsum('scxyz,yb->scxbz', result, sine_y, precision=HIGHEST)  35.2 us
    dot_general x72, matrix products, transform(): result = jnp.einsum('scxyz,xa->scayz', result, sine_x, precision=HIGHEST)  33.2 us
    ppermute x24, waiting for transfers between devices, passed_along(): return lax.ppermute(array, axis, pairs)  18.8 us
    ppermute x2, starting transfers between devices, extended(): lax.ppermute(tail, axis, [(i, (i + 1) % count) for i in range(ends)])  7.2 us
    sub x25, other arithmetic, apply_operator(): lateral = lateral + 2.0 * center - vertical[..., :-2] - vertical[..., 2:]  6.54 us
  transfers between devices with their start and end apart: 28, of which 15 were waited for; matrix products, arithmetic and copies ran while one was open for 0% of the time, Pallas kernels for 0%

commit v1 on v0

v1 whole, which is shorter than its diff:
```python
import functools
import math

import jax
import jax.numpy as jnp
import ml_dtypes
import numpy as np
from jax import lax
from jax.experimental import pallas as pl
from jax.experimental.pallas import tpu as pltpu
from jax.sharding import PartitionSpec as P

KAPPA = 0.12
DAMPING = 0.3
BF16 = jnp.bfloat16
F32 = jnp.float32


def sine_matrix(length):
    index = np.arange(1, length + 1)
    angles = index * (math.pi / (length + 1))
    return math.sqrt(2.0 / (length + 1)) * np.sin(angles[:, None] * index[None, :]), angles


def halves(matrix):
    high = matrix.astype(np.float32).astype(ml_dtypes.bfloat16)
    low = (matrix - high.astype(np.float64)).astype(np.float32).astype(ml_dtypes.bfloat16)
    return high, low


def left_factor(matrix):
    high, low = halves(matrix)
    return np.concatenate(
        [np.concatenate([high, high], axis=1), np.concatenate([low, low], axis=1)], axis=0
    )


def tables(size_x, size_y, cells_z):
    sine_x, angle_x = sine_matrix(size_x)
    sine_y, angle_y = sine_matrix(size_y)
    sine_z, angle_z = sine_matrix(cells_z)
    half = size_x // 2
    order = np.concatenate([np.arange(0, size_x, 2), np.arange(1, size_x, 2)])
    cells = np.concatenate([np.arange(half), np.arange(size_x - 1, half - 1, -1)])

    def symbol(angle):
        return 2.5 - 8.0 / 3.0 * np.cos(angle) + 1.0 / 6.0 * np.cos(2.0 * angle)

    real_part = (
        symbol(angle_x)[order][:, None, None]
        + symbol(angle_y)[None, :, None]
        + (2.0 - 2.0 * np.cos(angle_z))[None, None, :]
        - KAPPA
    ).reshape(size_x * size_y, cells_z)
    denominator = real_part**2 + (KAPPA * DAMPING) ** 2
    inverse = np.stack([real_part / denominator, KAPPA * DAMPING / denominator]).astype(np.float32)

    parity = [np.kron(sine_x[order[p * half : (p + 1) * half]][:, :half], sine_y) for p in (0, 1)]
    forward = np.stack([left_factor(m) for m in parity])
    backward = np.stack([left_factor(m.T) for m in parity])
    high_z, low_z = halves(sine_z)
    right_z = np.concatenate([np.concatenate([high_z, low_z], axis=1)] * 2, axis=0)

    full = np.kron(sine_x[order], sine_y)
    by_cell = full.reshape(-1, size_x, size_y)
    enter_x = np.stack([-by_cell[:, 0] / 12.0, (16.0 * by_cell[:, 0] - by_cell[:, 1]) / 12.0], 1)
    enter_y = np.stack(
        [-by_cell[:, :, 0] / 12.0, (16.0 * by_cell[:, :, 0] - by_cell[:, :, 1]) / 12.0], 1
    )
    enter = left_factor(
        np.concatenate([enter_x.reshape(len(full), -1), enter_y.reshape(len(full), -1)], axis=1)
    )
    leave = left_factor(
        np.concatenate(
            [
                by_cell[:, size_x - 2 :].reshape(len(full), -1),
                by_cell[:, :, size_y - 2 :].transpose(0, 2, 1).reshape(len(full), -1),
            ],
            axis=1,
        ).T
    )
    edge = np.zeros((size_x, size_y, 1))
    edge[0] += 1.0 / 12.0
    edge[-1] += 1.0 / 12.0
    edge[:, 0] += 1.0 / 12.0
    edge[:, -1] += 1.0 / 12.0
    edge = edge[cells].reshape(size_x * size_y, 1).astype(np.float32)
    return dict(
        inverse=inverse, forward=forward, backward=backward, right_z=right_z,
        enter=enter, leave=leave, edge=edge,
    ), cells


def split(values):
    high = values.astype(BF16)
    return high, (values - high.astype(F32)).astype(BF16)


def left_product(matrix, values):
    high, low = split(values)
    both = jnp.dot(matrix, jnp.concatenate([high, low], axis=0), preferred_element_type=F32)
    count = both.shape[0] // 2
    return both[:count] + both[count:]


def z_transform(field, right_z):
    rows = field.shape[0]
    cells_z = field.shape[1] // 2
    high, low = split(jnp.concatenate([field[:, :cells_z], field[:, cells_z:]], axis=0))
    both = jnp.dot(jnp.concatenate([high, low], axis=1), right_z, preferred_element_type=F32)
    total = both[:, :cells_z] + both[:, cells_z:]
    return jnp.concatenate([total[:rows], total[rows:]], axis=1)


def to_modes(field, forward):
    count = field.shape[0] // 2
    first, second = field[:count], field[count:]
    return jnp.concatenate(
        [left_product(forward[0], first + second), left_product(forward[1], first - second)], axis=0
    )


def to_cells(modes, backward):
    count = modes.shape[0] // 2
    even = left_product(backward[0], modes[:count])
    odd = left_product(backward[1], modes[count:])
    return jnp.concatenate([even + odd, even - odd], axis=0)


def times(real_part, imag_part, field):
    lanes = field.shape[1] // 2
    real, imag = field[:, :lanes], field[:, lanes:]
    return jnp.concatenate(
        [real_part * real - imag_part * imag, real_part * imag + imag_part * real], axis=1
    )


def solve_modes(source_modes, contrast, t):
    term = times(t["inverse"][0], t["inverse"][1], source_modes)
    total = term
    for _ in range(2):
        cells = z_transform(to_cells(term, t["backward"]), t["right_z"])
        cells = times(contrast[0], contrast[1], cells)
        term = times(t["inverse"][0], t["inverse"][1], to_modes(z_transform(cells, t["right_z"]), t["forward"]))
        total = total + term
    return total, term


PREP = ("edge", "forward", "right_z")
BEAT = ("inverse", "forward", "backward", "right_z", "enter", "leave")
LAST = ("inverse", "forward", "backward", "right_z", "enter")


def prep_kernel(cells_x, right_ref, slow_ref, place_ref, depth_ref, amp_ref, edge_ref, forward_ref, z_ref,
                modes_ref, contrast_ref):
    sources, _, size_x, size_y, cells_z = right_ref.shape
    rows = size_x * size_y
    scaled = jnp.concatenate([slow_ref[x] for x in cells_x], axis=0)
    scaled = KAPPA * (scaled - 1.0)
    contrast_ref[0] = scaled - edge_ref[...]
    contrast_ref[1] = DAMPING * scaled
    row_ids = lax.broadcasted_iota(jnp.int32, (rows, place_ref.shape[2]), 0)
    lane_ids = lax.broadcasted_iota(jnp.int32, (cells_z, place_ref.shape[2]), 0)
    forward = (forward_ref[0], forward_ref[1])
    for s in range(sources):
        at_row = (row_ids == place_ref[s]).astype(F32).astype(BF16)
        at_lane = (lane_ids == depth_ref[s]).astype(F32)
        parts = []
        for c in range(2):
            dense = jnp.concatenate([right_ref[s, c, x] for x in cells_x], axis=0)
            amp = amp_ref[s, c]
            one = amp.astype(BF16).astype(F32)
            two = (amp - one).astype(BF16).astype(F32)
            weights = [at_lane * part for part in (one, two, amp - one - two)]
            spread = jnp.concatenate(weights, axis=1).astype(BF16)
            points = lax.dot_general(
                jnp.concatenate([at_row] * 3, axis=1), spread, (((1,), (1,)), ((), ())),
                preferred_element_type=F32,
            )
            parts.append(dense + points)
        field = z_transform(jnp.concatenate(parts, axis=1), z_ref[...])
        modes_ref[s] = to_modes(field, forward)


def source_modes(modes_ref, trace_x_ref, trace_y_ref, enter_ref, s):
    trace = jnp.concatenate([trace_x_ref[s], trace_y_ref[s]], axis=0)
    return modes_ref[s] + left_product(enter_ref[...], trace)


def beat_kernel(active_ref, modes_ref, contrast_ref, trace_x_ref, trace_y_ref, *refs):
    t = {name: ref for name, ref in zip(BEAT, refs)}
    out_x_ref, out_y_ref = refs[len(BEAT) :]

    @pl.when(active_ref[0] == 1)
    def _():
        right_z = t["right_z"][...]
        local = dict(inverse=t["inverse"], forward=t["forward"], backward=t["backward"], right_z=right_z)
        for s in range(modes_ref.shape[0]):
            total, _ = solve_modes(
                source_modes(modes_ref, trace_x_ref, trace_y_ref, t["enter"], s), contrast_ref, local
            )
            out = left_product(t["leave"][...], total)
            count = out_x_ref.shape[1]
            out_x_ref[s] = out[:count]
            out_y_ref[s] = out[count:]


def last_kernel(cells_x, modes_ref, contrast_ref, trace_x_ref, trace_y_ref, *refs):
    t = {name: ref for name, ref in zip(LAST, refs)}
    wave_ref, rest_ref = refs[len(LAST) :]
    size_y, cells_z = wave_ref.shape[3], wave_ref.shape[4]
    local = dict(t, right_z=t["right_z"][...])
    for s in range(modes_ref.shape[0]):
        total, term = solve_modes(
            source_modes(modes_ref, trace_x_ref, trace_y_ref, t["enter"], s), contrast_ref, local
        )
        wave = z_transform(to_cells(total, t["backward"]), local["right_z"])
        rest = z_transform(to_cells(term, t["backward"]), local["right_z"])
        rest = times(contrast_ref[0], contrast_ref[1], rest)
        for place, x in enumerate(cells_x):
            here = slice(place * size_y, (place + 1) * size_y)
            for c in range(2):
                there = slice(c * cells_z, (c + 1) * cells_z)
                wave_ref[s, c, x] = wave[here, there]
                rest_ref[s, c, x] = rest[here, there]


def whole():
    return pl.BlockSpec(memory_space=pltpu.VMEM)


PARAMS = pltpu.CompilerParams(vmem_limit_bytes=40 * 1024 * 1024)


def body(right_side, slowness, source_cells, source_amplitudes):
    sources, _, size_x, size_y, cells_z = right_side.shape
    grid_rows, grid_cols = lax.axis_size("gx"), lax.axis_size("gy")
    row, col = lax.axis_index("gx"), lax.axis_index("gy")
    t, cells_x = tables(size_x, size_y, cells_z)
    t = {name: jnp.asarray(value) for name, value in t.items()}
    cells_x = tuple(int(x) for x in cells_x)
    rows = size_x * size_y

    total_y = size_y * grid_cols
    near_x = source_cells // (total_y * cells_z) - row * size_x
    near_y = source_cells // cells_z % total_y - col * size_y
    inside = (near_x >= 0) & (near_x < size_x) & (near_y >= 0) & (near_y < size_y)
    place_x = jnp.where(near_x < size_x // 2, near_x, size_x + size_x // 2 - 1 - near_x)
    place = jnp.where(inside, place_x * size_y + near_y, -1)[:, None, :]
    depth = (source_cells % cells_z)[:, None, :]
    amplitudes = source_amplitudes.transpose(0, 2, 1)[:, :, None, :]

    modes, contrast = pl.pallas_call(
        functools.partial(prep_kernel, cells_x),
        out_shape=(
            jax.ShapeDtypeStruct((sources, rows, 2 * cells_z), F32),
            jax.ShapeDtypeStruct((2, rows, cells_z), F32),
        ),
        in_specs=[whole()] * 8,
        out_specs=(whole(), whole()),
        compiler_params=PARAMS,
        name="prep",
    )(right_side, slowness, place, depth, amplitudes, *[t[name] for name in PREP])

    trace_x = jnp.zeros((sources, 2 * size_y, 2 * cells_z), F32)
    trace_y = jnp.zeros((sources, 2 * size_x, 2 * cells_z), F32)
    sum_x, sum_y = [], []
    for beat in range(grid_rows + grid_cols - 2):
        active = (row + col == beat).astype(jnp.int32)[None]
        out_x, out_y = pl.pallas_call(
            beat_kernel,
            out_shape=(
                jax.ShapeDtypeStruct(trace_x.shape, F32),
                jax.ShapeDtypeStruct(trace_y.shape, F32),
            ),
            in_specs=[pl.BlockSpec(memory_space=pltpu.SMEM)] + [whole()] * (4 + len(BEAT)),
            out_specs=(whole(), whole()),
            compiler_params=PARAMS,
            name="beat",
        )(active, modes, contrast, trace_x, trace_y, *[t[name] for name in BEAT])
        pairs_x = []
        pairs_y = []
        for i in range(grid_rows):
            j = beat - i
            if 0 <= j < grid_cols:
                here = i * grid_cols + j
                if i + 1 < grid_rows:
                    pairs_x.append((here, here + grid_cols))
                if j + 1 < grid_cols:
                    pairs_y.append((here, here + 1))
        trace_x = lax.ppermute(out_x, ("gx", "gy"), pairs_x)
        trace_y = lax.ppermute(out_y, ("gx", "gy"), pairs_y)
        sum_x.append(trace_x)
        sum_y.append(trace_y)

    wavefield, rest = pl.pallas_call(
        functools.partial(last_kernel, cells_x),
        out_shape=(
            jax.ShapeDtypeStruct(right_side.shape, F32),
            jax.ShapeDtypeStruct(right_side.shape, F32),
        ),
        in_specs=[whole()] * (4 + len(LAST)),
        out_specs=(whole(), whole()),
        compiler_params=PARAMS,
        name="last",
    )(modes, contrast, sum(sum_x), sum(sum_y), *[t[name] for name in LAST])

    after_x = lax.ppermute(wavefield[:, :, :2], "gx", [(i + 1, i) for i in range(grid_rows - 1)])
    after_y = lax.ppermute(wavefield[:, :, :, :2], "gy", [(j + 1, j) for j in range(grid_cols - 1)])
    near, far = after_x[:, :, :1], after_x[:, :, 1:]
    rest = rest + jnp.pad(
        jnp.concatenate([-near, 16.0 * near - far], axis=2) / 12.0,
        ((0, 0), (0, 0), (size_x - 2, 0), (0, 0), (0, 0)),
    )
    near, far = after_y[:, :, :, :1], after_y[:, :, :, 1:]
    rest = rest + jnp.pad(
        jnp.concatenate([-near, 16.0 * near - far], axis=3) / 12.0,
        ((0, 0), (0, 0), (0, 0), (size_y - 2, 0), (0, 0)),
    )
    return wavefield, rest


def solution(mesh):
    return jax.shard_map(
        body,
        mesh=mesh,
        in_specs=(P(None, None, "gx", "gy", None), P("gx", "gy", None), P(), P()),
        out_specs=(P(None, None, "gx", "gy", None), P(None, None, "gx", "gy", None)),
        check_vma=False,
    )
```

time: 270 us -> 101 us (0.37)
  the two profiles are of different devices: /device:TPU:10 before, /device:TPU:29 now
where the time goes in v1:
time: 101 us; the launch traced here: 100 us
  waiting for transfers between devices  60.5 us (60%)
  starting transfers between devices  18.6 us (18%)
  Pallas kernels  11 us (11%)
  local copies, waits for them, and re-layouts  7.9 us (8%)
  between operations  1.22 us (1%)
  other arithmetic  1.11 us (1%)
    ppermute x10, waiting for transfers between devices, body(): trace_x = lax.ppermute(out_x, ('gx', 'gy'), pairs_x)  53.4 us
    ppermute x10, starting transfers between devices, body(): trace_y = lax.ppermute(out_y, ('gx', 'gy'), pairs_y)  7.9 us
    ppermute x10, starting transfers between devices, body(): trace_x = lax.ppermute(out_x, ('gx', 'gy'), pairs_x)  7.5 us
    unnamed x26, local copies, waits for them, and re-layouts  6.08 us
    ppermute x1, waiting for transfers between devices, body(): lax.ppermute(wavefield[:, :, :, :2], 'gy', [(j + 1, j) for j in range(gri...  5.86 us
    pallas_call x1, Pallas kernels, body(): pl.pallas_call(functools.partial(last_kernel, cells_x), out_shape=(jax.Sh...  5.42 us
    pallas_call x10, Pallas kernels, body(): pl.pallas_call(beat_kernel, out_shape=(jax.ShapeDtypeStruct(trace_x.shape...  4.37 us
  transfers between devices with their start and end apart: 22, of which 3 were waited for; matrix products, arithmetic and copies ran while one was open for 1% of the time, Pallas kernels for 0%

profile of v1, /device:TPU:29, one launch (start us, length us, event | category | flops | bytes accessed | tf_op | source)
XLA Modules:
  0.0 100.4 jit_solution(8885544458309130010)
XLA Ops:
  0.6 0.7 copy-done.12
  1.3 0.0 copy-start.11
  1.4 0.7 copy-done.11
  2.0 0.9 copy-done
  3.0 0.9 copy-done.4
  3.9 1.0 %copy-done.8 = f32[2,2,16,16,128]{4,3,2,1,0:T(8,128)S(1)} copy-done((f32[2,2,16,16,128]{4,3,2,1,0:T(8,128)S(1)}, f32[2,2,16,16,128]{4,3,2,1,0:T(8,128)}, u32[]{:S(2)}) %copy-start.8) | copy-done | bytes 524312
  4.9 0.9 copy-done.9
  5.8 0.9 copy-done.10
  6.7 0.0 copy-start.6
  6.8 0.0 copy-start.7
  6.8 1.2 %prep.1 = (f32[2,256,256]{2,1,0:T(8,128)S(1)}, f32[2,256,128]{2,1,0:T(8,128)S(1)}) custom-call(f32[2,2,16,16,128]{4,3,2,1,0:T(8,128)S(1)} %copy-done.8, f32[16,16,128]{2,1,0:T(8,128)S(1)} %copy-done.9, s32[2,1,16]{2,1,0:T(1,128)S(1)} %bitcast.22, s32[2,1,16]{2,1,0:T(1,128)S(1)} %bitcast.21, f32[2,2,1,16]{3,2,1,0:T(1,128)S(1)} %bitcast.23, ...), custom_call_target="tpu_custom_call" | custom-call | tf_op jit(solution)/shard_map/prep/pallas_call | solution.py:253
  8.1 0.7 collective-permute-start
  8.8 0.7 collective-permute-start.1
  9.5 0.0 collective-permute-done.trace_x_ref
  9.5 0.7 collective-permute-start.2
  10.2 0.7 collective-permute-start.3
  10.8 0.0 collective-permute-done.2.trace_x_ref
  10.9 0.0 collective-permute-done.3.trace_y_ref
  10.9 0.7 collective-permute-start.4
  11.6 0.7 collective-permute-start.5
  12.2 0.0 collective-permute-done.5.trace_y_ref
  12.3 0.7 collective-permute-start.6
  12.9 0.7 collective-permute-start.7
  13.6 0.2 beat.14
  13.8 0.7 collective-permute-start.8
  14.5 0.7 collective-permute-start.9
  15.2 0.7 collective-permute-start.10
  15.9 0.7 collective-permute-start.11
  16.6 0.7 collective-permute-start.12
  17.3 0.7 collective-permute-start.13
  18.0 0.7 collective-permute-start.14
  18.7 0.7 collective-permute-start.15
  19.4 1.5 %collective-permute-start.16 = (f32[2,32,256]{2,1,0:T(8,128)S(1)}, f32[2,32,256]{2,1,0:T(8,128)S(1)}, u32[]{:S(2)}, u32[]{:S(2)}) collective-permute-start(f32[2,32,256]{2,1,0:T(8,128)S(1)} %get-tuple-element.44), channel_id=1, source_target_pairs={{23,27},{26,30}} | collective-permute-start | bytes 196616 | tf_op jit(solution)/shard_map/ppermute | solution.py:291
  20.9 1.3 %collective-permute-start.17 = (f32[2,32,256]{2,1,0:T(8,128)S(1)}, f32[2,32,256]{2,1,0:T(8,128)S(1)}, u32[]{:S(2)}, u32[]{:S(2)}) collective-permute-start(f32[2,32,256]{2,1,0:T(8,128)S(1)} %get-tuple-element.45), channel_id=1, source_target_pairs={{26,27},{29,30}} | collective-permute-start | bytes 196616 | tf_op jit(solution)/shard_map/ppermute | solution.py:292
  22.2 53.3 %collective-permute-done.16.trace_x_ref = f32[2,32,256]{2,1,0:T(8,128)S(1)} collective-permute-done((f32[2,32,256]{2,1,0:T(8,128)S(1)}, f32[2,32,256]{2,1,0:T(8,128)S(1)}, u32[]{:S(2)}, u32[]{:S(2)}) %collective-permute-start.16) | collective-permute-done | bytes 65568 | tf_op jit(solution)/shard_map/ppermute | solution.py:291
  75.6 4.1 %beat.19 = (f32[2,32,256]{2,1,0:T(8,128)S(1)}, f32[2,32,256]{2,1,0:T(8,128)S(1)}) custom-call(s32[1]{0:T(128)} %bitcast.16.active_ref, f32[2,256,256]{2,1,0:T(8,128)S(1)} %get-tuple-element.26.modes_ref, f32[2,256,128]{2,1,0:T(8,128)S(1)} %get-tuple-element.27.contrast_ref, f32[2,32,256]{2,1,0:T(8,128)S(1)} %collective-permute-done.16.trace_x_ref, ...), custom_call_target="tpu_custom_call" | custom-call | tf_op jit(solution)/shard_map/beat/pallas_call | solution.py:270
  79.7 0.7 collective-permute-start.18
  80.4 1.3 %collective-permute-start.19 = (f32[2,32,256]{2,1,0:T(8,128)S(1)}, f32[2,32,256]{2,1,0:T(8,128)S(1)}, u32[]{:S(2)}, u32[]{:S(2)}) collective-permute-start(f32[2,32,256]{2,1,0:T(8,128)S(1)} %get-tuple-element.47), channel_id=1, source_target_pairs={{30,31}} | collective-permute-start | bytes 196616 | tf_op jit(solution)/shard_map/ppermute | solution.py:292
  81.7 1.2 %collective-permute-done.19 = f32[2,32,256]{2,1,0:T(8,128)S(1)} collective-permute-done((f32[2,32,256]{2,1,0:T(8,128)S(1)}, f32[2,32,256]{2,1,0:T(8,128)S(1)}, u32[]{:S(2)}, u32[]{:S(2)}) %collective-permute-start.19) | collective-permute-done | bytes 65568 | tf_op jit(solution)/shard_map/ppermute | solution.py:292
  83.0 5.4 %last.1 = (f32[2,2,16,16,128]{4,3,2,1,0:T(8,128)}, f32[2,2,16,16,128]{4,3,2,1,0:T(8,128)S(1)}) custom-call(f32[2,256,256]{2,1,0:T(8,128)S(1)} %get-tuple-element.26.modes_ref, f32[2,256,128]{2,1,0:T(8,128)S(1)} %get-tuple-element.27.contrast_ref, f32[2,32,256]{2,1,0:T(8,128)S(1)} %add_add_fusion.1.trace_x_ref, f32[2,32,256]{2,1,0:T(8,128)S(1)} %add_add_fusion.trace_y_ref, ...), custom_call_target="tpu_custom_call" | custom-call | tf_op jit(solution)/shard_map/last/pallas_call | solution.py:296
  88.4 0.8 slice.18
  89.3 1.3 %collective-permute-start.20 = (f32[2,2,2,16,128]{4,3,2,1,0:T(8,128)S(1)}, f32[2,2,2,16,128]{4,3,2,1,0:T(8,128)S(1)}, u32[]{:S(2)}, u32[]{:S(2)}) collective-permute-start(f32[2,2,2,16,128]{4,3,2,1,0:T(8,128)S(1)} %slice.18), channel_id=1, source_target_pairs={{4,0},{8,4},{12,8},{16,12},{20,16},{24,20},{28,24},{5,1},{9,5},{13... | collective-permute-start | bytes 196616 | tf_op jit(solution)/shard_map/ppermute | solution.py:308
  90.6 1.0 slice.21
  91.5 1.9 %collective-permute-start.21 = (f32[2,2,16,2,128]{4,3,2,1,0:T(2,128)S(1)}, f32[2,2,16,2,128]{4,3,2,1,0:T(2,128)S(1)}, u32[]{:S(2)}, u32[]{:S(2)}) collective-permute-start(f32[2,2,16,2,128]{4,3,2,1,0:T(2,128)S(1)} %slice.21), channel_id=1, source_target_pairs={{1,0},{2,1},{3,2},{5,4},{6,5},{7,6},{9,8},{10,9},{11,10},{13,12},{... | collective-permute-start | bytes 196616 | tf_op jit(solution)/shard_map/ppermute | solution.py:309
  93.5 5.9 %collective-permute-done.21 = f32[2,2,16,2,128]{4,3,2,1,0:T(2,128)S(1)} collective-permute-done((f32[2,2,16,2,128]{4,3,2,1,0:T(2,128)S(1)}, f32[2,2,16,2,128]{4,3,2,1,0:T(2,128)S(1)}, u32[]{:S(2)}, u32[]{:S(2)}) %collective-permute-start.21) | collective-permute-done | bytes 65568 | tf_op jit(solution)/shard_map/ppermute | solution.py:309
  99.4 0.1 slice_negate_fusion.1
  99.4 0.1 maximum_multiply_fusion.1
  99.5 0.9 pad_add_fusion
  (45 shorter events, 0.3 us)
Async XLA Ops:
  0.6 0.7 copy-start.12
  1.3 0.7 copy-start.11
  2.0 0.9 copy-start
  3.0 0.9 copy-start.4
  3.9 1.0 %copy-start.8 = (f32[2,2,16,16,128]{4,3,2,1,0:T(8,128)S(1)}, f32[2,2,16,16,128]{4,3,2,1,0:T(8,128)}, u32[]{:S(2)}) copy-start(f32[2,2,16,16,128]{4,3,2,1,0:T(8,128)} %right_ref.1) | copy-start | bytes 1572868
  4.9 0.9 copy-start.9
  5.8 0.9 copy-start.10
  6.7 1.3 %copy-start.1 = (bf16[2,256,256]{2,1,0:T(8,128)(2,1)S(1)}, bf16[2,256,256]{2,1,0:T(8,128)(2,1)}, u32[]{:S(2)}) copy-start(bf16[2,256,256]{2,1,0:T(8,128)(2,1)} %constant.110.clone.forward_ref.refs_1_) | copy-start | bytes 786436
  6.7 1.3 %copy-start.2 = (bf16[2,256,256]{2,1,0:T(8,128)(2,1)S(1)}, bf16[2,256,256]{2,1,0:T(8,128)(2,1)}, u32[]{:S(2)}) copy-start(bf16[2,256,256]{2,1,0:T(8,128)(2,1)} %constant.111.clone.refs_2_) | copy-start | bytes 786436
  6.7 1.3 %copy-start.3 = (f32[2,256,128]{2,1,0:T(8,128)S(1)}, f32[2,256,128]{2,1,0:T(8,128)}, u32[]{:S(2)}) copy-start(f32[2,256,128]{2,1,0:T(8,128)} %constant.109.clone.refs_0_) | copy-start | bytes 786436
  6.7 1.3 %copy-start.5 = (bf16[256,256]{1,0:T(8,128)(2,1)S(1)}, bf16[256,256]{1,0:T(8,128)(2,1)}, u32[]{:S(2)}) copy-start(bf16[256,256]{1,0:T(8,128)(2,1)} %constant.112.clone.z_ref.refs_3_) | copy-start | bytes 393220
  6.7 1.3 %copy-start.6 = (bf16[512,128]{1,0:T(8,128)(2,1)S(1)}, bf16[512,128]{1,0:T(8,128)(2,1)}, u32[]{:S(2)}) copy-start(bf16[512,128]{1,0:T(8,128)(2,1)} %constant.113.clone.refs_4_) | copy-start | bytes 393220
  6.8 1.3 %copy-start.7 = (bf16[128,512]{1,0:T(8,128)(2,1)S(1)}, bf16[128,512]{1,0:T(8,128)(2,1)}, u32[]{:S(2)}) copy-start(bf16[128,512]{1,0:T(8,128)(2,1)} %constant.114.clone.refs_5_) | copy-start | bytes 393220
  8.1 1.4 %collective-permute-start = (f32[2,32,256]{2,1,0:T(8,128)S(1)}, f32[2,32,256]{2,1,0:T(8,128)S(1)}, u32[]{:S(2)}, u32[]{:S(2)}) collective-permute-start(f32[2,32,256]{2,1,0:T(8,128)S(1)} %get-tuple-element.28), channel_id=1, source_target_pairs={{0,4}} | collective-permute-start | bytes 196616 | tf_op jit(solution)/shard_map/ppermute | solution.py:291
  8.8 0.7 collective-permute-start.1
  9.5 1.4 %collective-permute-start.2 = (f32[2,32,256]{2,1,0:T(8,128)S(1)}, f32[2,32,256]{2,1,0:T(8,128)S(1)}, u32[]{:S(2)}, u32[]{:S(2)}) collective-permute-start(f32[2,32,256]{2,1,0:T(8,128)S(1)} %get-tuple-element.30), channel_id=1, source_target_pairs={{1,5},{4,8}} | collective-permute-start | bytes 196616 | tf_op jit(solution)/shard_map/ppermute | solution.py:291
  10.2 0.7 collective-permute-start.3
  10.9 1.4 %collective-permute-start.4 = (f32[2,32,256]{2,1,0:T(8,128)S(1)}, f32[2,32,256]{2,1,0:T(8,128)S(1)}, u32[]{:S(2)}, u32[]{:S(2)}) collective-permute-start(f32[2,32,256]{2,1,0:T(8,128)S(1)} %get-tuple-element.32), channel_id=1, source_target_pairs={{2,6},{5,9},{8,12}} | collective-permute-start | bytes 196616 | tf_op jit(solution)/shard_map/ppermute | solution.py:291
  11.6 0.7 collective-permute-start.5
  12.3 1.4 %collective-permute-start.6 = (f32[2,32,256]{2,1,0:T(8,128)S(1)}, f32[2,32,256]{2,1,0:T(8,128)S(1)}, u32[]{:S(2)}, u32[]{:S(2)}) collective-permute-start(f32[2,32,256]{2,1,0:T(8,128)S(1)} %get-tuple-element.34), channel_id=1, source_target_pairs={{3,7},{6,10},{9,13},{12,16}} | collective-permute-start | bytes 196616 | tf_op jit(solution)/shard_map/ppermute | solution.py:291
  12.9 0.7 collective-permute-start.7
  13.8 1.4 %collective-permute-start.8 = (f32[2,32,256]{2,1,0:T(8,128)S(1)}, f32[2,32,256]{2,1,0:T(8,128)S(1)}, u32[]{:S(2)}, u32[]{:S(2)}) collective-permute-start(f32[2,32,256]{2,1,0:T(8,128)S(1)} %get-tuple-element.36), channel_id=1, source_target_pairs={{7,11},{10,14},{13,17},{16,20}} | collective-permute-start | bytes 196616 | tf_op jit(solution)/shard_map/ppermute | solution.py:291
  14.5 0.7 collective-permute-start.9
  15.2 1.4 %collective-permute-start.10 = (f32[2,32,256]{2,1,0:T(8,128)S(1)}, f32[2,32,256]{2,1,0:T(8,128)S(1)}, u32[]{:S(2)}, u32[]{:S(2)}) collective-permute-start(f32[2,32,256]{2,1,0:T(8,128)S(1)} %get-tuple-element.38), channel_id=1, source_target_pairs={{11,15},{14,18},{17,21},{20,24}} | collective-permute-start | bytes 196616 | tf_op jit(solution)/shard_map/ppermute | solution.py:291
  15.9 0.7 collective-permute-start.11
  16.6 1.4 %collective-permute-start.12 = (f32[2,32,256]{2,1,0:T(8,128)S(1)}, f32[2,32,256]{2,1,0:T(8,128)S(1)}, u32[]{:S(2)}, u32[]{:S(2)}) collective-permute-start(f32[2,32,256]{2,1,0:T(8,128)S(1)} %get-tuple-element.40), channel_id=1, source_target_pairs={{15,19},{18,22},{21,25},{24,28}} | collective-permute-start | bytes 196616 | tf_op jit(solution)/shard_map/ppermute | solution.py:291
  17.3 0.7 collective-permute-start.13
  18.0 1.4 %collective-permute-start.14 = (f32[2,32,256]{2,1,0:T(8,128)S(1)}, f32[2,32,256]{2,1,0:T(8,128)S(1)}, u32[]{:S(2)}, u32[]{:S(2)}) collective-permute-start(f32[2,32,256]{2,1,0:T(8,128)S(1)} %get-tuple-element.42), channel_id=1, source_target_pairs={{19,23},{22,26},{25,29}} | collective-permute-start | bytes 196616 | tf_op jit(solution)/shard_map/ppermute | solution.py:291
  18.7 0.7 collective-permute-start.15
  19.4 56.2 %collective-permute-start.16 = (f32[2,32,256]{2,1,0:T(8,128)S(1)}, f32[2,32,256]{2,1,0:T(8,128)S(1)}, u32[]{:S(2)}, u32[]{:S(2)}) collective-permute-start(f32[2,32,256]{2,1,0:T(8,128)S(1)} %get-tuple-element.44), channel_id=1, source_target_pairs={{23,27},{26,30}} | collective-permute-start | bytes 196616 | tf_op jit(solution)/shard_map/ppermute | solution.py:291
  20.9 54.6 %collective-permute-start.17 = (f32[2,32,256]{2,1,0:T(8,128)S(1)}, f32[2,32,256]{2,1,0:T(8,128)S(1)}, u32[]{:S(2)}, u32[]{:S(2)}) collective-permute-start(f32[2,32,256]{2,1,0:T(8,128)S(1)} %get-tuple-element.45), channel_id=1, source_target_pairs={{26,27},{29,30}} | collective-permute-start | bytes 196616 | tf_op jit(solution)/shard_map/ppermute | solution.py:292
  79.7 2.0 %collective-permute-start.18 = (f32[2,32,256]{2,1,0:T(8,128)S(1)}, f32[2,32,256]{2,1,0:T(8,128)S(1)}, u32[]{:S(2)}, u32[]{:S(2)}) collective-permute-start(f32[2,32,256]{2,1,0:T(8,128)S(1)} %get-tuple-element.46), channel_id=1, source_target_pairs={{27,31}} | collective-permute-start | bytes 196616 | tf_op jit(solution)/shard_map/ppermute | solution.py:291
  80.4 2.6 %collective-permute-start.19 = (f32[2,32,256]{2,1,0:T(8,128)S(1)}, f32[2,32,256]{2,1,0:T(8,128)S(1)}, u32[]{:S(2)}, u32[]{:S(2)}) collective-permute-start(f32[2,32,256]{2,1,0:T(8,128)S(1)} %get-tuple-element.47), channel_id=1, source_target_pairs={{30,31}} | collective-permute-start | bytes 196616 | tf_op jit(solution)/shard_map/ppermute | solution.py:292
  89.3 4.2 %collective-permute-start.20 = (f32[2,2,2,16,128]{4,3,2,1,0:T(8,128)S(1)}, f32[2,2,2,16,128]{4,3,2,1,0:T(8,128)S(1)}, u32[]{:S(2)}, u32[]{:S(2)}) collective-permute-start(f32[2,2,2,16,128]{4,3,2,1,0:T(8,128)S(1)} %slice.18), channel_id=1, source_target_pairs={{4,0},{8,4},{12,8},{16,12},{20,16},{24,20},{28,24},{5,1},{9,5},{13... | collective-permute-start | bytes 196616 | tf_op jit(solution)/shard_map/ppermute | solution.py:308
  91.5 7.8 %collective-permute-start.21 = (f32[2,2,16,2,128]{4,3,2,1,0:T(2,128)S(1)}, f32[2,2,16,2,128]{4,3,2,1,0:T(2,128)S(1)}, u32[]{:S(2)}, u32[]{:S(2)}) collective-permute-start(f32[2,2,16,2,128]{4,3,2,1,0:T(2,128)S(1)} %slice.21), channel_id=1, source_target_pairs={{1,0},{2,1},{3,2},{5,4},{6,5},{7,6},{9,8},{10,9},{11,10},{13,12},{... | collective-permute-start | bytes 196616 | tf_op jit(solution)/shard_map/ppermute | solution.py:309

commit v2 on v1

v2 whole, which is shorter than its diff:
```python
import functools
import math

import jax
import jax.numpy as jnp
import ml_dtypes
import numpy as np
from jax import lax
from jax.experimental import pallas as pl
from jax.experimental.pallas import tpu as pltpu
from jax.sharding import PartitionSpec as P

KAPPA = 0.12
DAMPING = 0.3
BF16 = jnp.bfloat16
F32 = jnp.float32


def sine_matrix(length):
    index = np.arange(1, length + 1)
    angles = index * (math.pi / (length + 1))
    return math.sqrt(2.0 / (length + 1)) * np.sin(angles[:, None] * index[None, :]), angles


def halves(matrix):
    high = matrix.astype(np.float32).astype(ml_dtypes.bfloat16)
    low = (matrix - high.astype(np.float64)).astype(np.float32).astype(ml_dtypes.bfloat16)
    return high, low


def left_factor(matrix):
    high, low = halves(matrix)
    return np.concatenate(
        [np.concatenate([high, high], axis=1), np.concatenate([low, low], axis=1)], axis=0
    )


def tables(size_x, size_y, cells_z):
    sine_x, angle_x = sine_matrix(size_x)
    sine_y, angle_y = sine_matrix(size_y)
    sine_z, angle_z = sine_matrix(cells_z)
    half = size_x // 2
    order = np.concatenate([np.arange(0, size_x, 2), np.arange(1, size_x, 2)])
    cells = np.concatenate([np.arange(half), np.arange(size_x - 1, half - 1, -1)])

    def symbol(angle):
        return 2.5 - 8.0 / 3.0 * np.cos(angle) + 1.0 / 6.0 * np.cos(2.0 * angle)

    real_part = (
        symbol(angle_x)[order][:, None, None]
        + symbol(angle_y)[None, :, None]
        + (2.0 - 2.0 * np.cos(angle_z))[None, None, :]
        - KAPPA
    ).reshape(size_x * size_y, cells_z)
    denominator = real_part**2 + (KAPPA * DAMPING) ** 2
    inverse = np.stack([real_part / denominator, KAPPA * DAMPING / denominator]).astype(np.float32)

    parity = [np.kron(sine_x[order[p * half : (p + 1) * half]][:, :half], sine_y) for p in (0, 1)]
    forward = np.stack([left_factor(m) for m in parity])
    backward = np.stack([left_factor(m.T) for m in parity])
    high_z, low_z = halves(sine_z)
    right_z = np.concatenate([np.concatenate([high_z, low_z], axis=1)] * 2, axis=0)

    full = np.kron(sine_x[order], sine_y)
    by_cell = full.reshape(-1, size_x, size_y)
    enter_x = np.stack([-by_cell[:, 0] / 12.0, (16.0 * by_cell[:, 0] - by_cell[:, 1]) / 12.0], 1)
    enter_y = np.stack(
        [-by_cell[:, :, 0] / 12.0, (16.0 * by_cell[:, :, 0] - by_cell[:, :, 1]) / 12.0], 1
    )
    enter = left_factor(
        np.concatenate([enter_x.reshape(len(full), -1), enter_y.reshape(len(full), -1)], axis=1)
    )
    leave = left_factor(
        np.concatenate(
            [
                by_cell[:, size_x - 2 :].reshape(len(full), -1),
                by_cell[:, :, size_y - 2 :].transpose(0, 2, 1).reshape(len(full), -1),
            ],
            axis=1,
        ).T
    )
    edge = np.zeros((size_x, size_y, 1))
    edge[0] += 1.0 / 12.0
    edge[-1] += 1.0 / 12.0
    edge[:, 0] += 1.0 / 12.0
    edge[:, -1] += 1.0 / 12.0
    edge = edge[cells].reshape(size_x * size_y, 1).astype(np.float32)
    return dict(
        inverse=inverse, forward=forward, backward=backward, right_z=right_z,
        enter=enter, leave=leave, edge=edge,
    ), cells


def split(values):
    high = values.astype(BF16)
    return high, (values - high.astype(F32)).astype(BF16)


def left_product(matrix, values):
    high, low = split(values)
    both = jnp.dot(matrix, jnp.concatenate([high, low], axis=0), preferred_element_type=F32)
    count = both.shape[0] // 2
    return both[:count] + both[count:]


def z_transform(field, right_z):
    rows = field.shape[0]
    cells_z = field.shape[1] // 2
    high, low = split(jnp.concatenate([field[:, :cells_z], field[:, cells_z:]], axis=0))
    both = jnp.dot(jnp.concatenate([high, low], axis=1), right_z, preferred_element_type=F32)
    total = both[:, :cells_z] + both[:, cells_z:]
    return jnp.concatenate([total[:rows], total[rows:]], axis=1)


def to_modes(field, forward):
    count = field.shape[0] // 2
    first, second = field[:count], field[count:]
    return jnp.concatenate(
        [left_product(forward[0], first + second), left_product(forward[1], first - second)], axis=0
    )


def to_cells(modes, backward):
    count = modes.shape[0] // 2
    even = left_product(backward[0], modes[:count])
    odd = left_product(backward[1], modes[count:])
    return jnp.concatenate([even + odd, even - odd], axis=0)


def times(real_part, imag_part, field):
    lanes = field.shape[1] // 2
    real, imag = field[:, :lanes], field[:, lanes:]
    return jnp.concatenate(
        [real_part * real - imag_part * imag, real_part * imag + imag_part * real], axis=1
    )


def solve_modes(source_modes, contrast, t):
    term = times(t["inverse"][0], t["inverse"][1], source_modes)
    total = term
    for _ in range(2):
        cells = z_transform(to_cells(term, t["backward"]), t["right_z"])
        cells = times(contrast[0], contrast[1], cells)
        term = times(t["inverse"][0], t["inverse"][1], to_modes(z_transform(cells, t["right_z"]), t["forward"]))
        total = total + term
    return total, term


PREP = ("edge", "forward", "right_z")
BEAT = ("inverse", "forward", "backward", "right_z", "enter", "leave")


def prep_kernel(cells_x, core_ref, right_ref, slow_ref, swap_ref, place_ref, depth_ref, amp_ref, edge_ref,
                forward_ref, z_ref, modes_ref, contrast_ref):
    _, _, size_x, size_y, cells_z = right_ref.shape
    rows = size_x * size_y
    core = core_ref[0]
    points = place_ref.shape[2]
    row_ids = lax.broadcasted_iota(jnp.int32, (rows, points), 0)
    lane_ids = lax.broadcasted_iota(jnp.int32, (cells_z, points), 0)
    at_lane = (lane_ids == depth_ref[...]).astype(F32)
    spread = []
    for c in range(2):
        amp = amp_ref[c]
        one = amp.astype(BF16).astype(F32)
        two = (amp - one).astype(BF16).astype(F32)
        parts = [at_lane * part for part in (one, two, amp - one - two)]
        spread.append(jnp.concatenate(parts, axis=1).astype(BF16))
    spread = jnp.concatenate(spread, axis=0)
    for other in range(2):
        tile = core if other == 0 else 1 - core
        if other == 0:
            slow = [slow_ref[x] for x in cells_x]
            dense = [[right_ref[core, c, x] for x in cells_x] for c in range(2)]
        else:
            slow = [swap_ref[2, x] for x in cells_x]
            dense = [[swap_ref[c, x] for x in cells_x] for c in range(2)]
        scaled = KAPPA * (jnp.concatenate(slow, axis=0) - 1.0)
        contrast_ref[tile, 0] = scaled - edge_ref[...]
        contrast_ref[tile, 1] = DAMPING * scaled
        at_row = (row_ids == place_ref[other]).astype(F32).astype(BF16)
        field = lax.dot_general(
            jnp.concatenate([at_row] * 3, axis=1), spread, (((1,), (1,)), ((), ())),
            preferred_element_type=F32,
        )
        field = field + jnp.concatenate([jnp.concatenate(d, axis=0) for d in dense], axis=1)
        modes_ref[tile] = to_modes(z_transform(field, z_ref[...]), forward_ref)


def source_modes(modes, trace_x, trace_y, enter):
    return modes + left_product(enter, jnp.concatenate([trace_x, trace_y], axis=0))


def beat_kernel(tile, active_ref, modes_ref, contrast_ref, trace_x_ref, trace_y_ref, *refs):
    t = {name: ref for name, ref in zip(BEAT, refs)}
    out_x_ref, out_y_ref = refs[len(BEAT) :]

    @pl.when(active_ref[0] == 1)
    def _():
        local = dict(t, right_z=t["right_z"][...])
        source = source_modes(modes_ref[tile], trace_x_ref[...], trace_y_ref[...], t["enter"][...])
        total, _ = solve_modes(source, contrast_ref.at[tile], local)
        out = left_product(t["leave"][...], total)
        count = out_x_ref.shape[0]
        out_x_ref[...] = out[:count]
        out_y_ref[...] = out[count:]


def last_kernel(cells_x, modes_ref, contrast_ref, trace_x_ref, trace_y0_ref, trace_y1_ref, *refs):
    t = {name: ref for name, ref in zip(BEAT, refs)}
    both_ref, edge_x_ref, edge_y_ref = refs[len(BEAT) :]
    size_y, cells_z = both_ref.shape[4], both_ref.shape[5]
    size_x = both_ref.shape[3]
    local = dict(t, right_z=t["right_z"][...])
    trace_x = trace_x_ref[...]
    for tile, trace_y_ref in enumerate((trace_y0_ref, trace_y1_ref)):
        source = source_modes(modes_ref[tile], trace_x, trace_y_ref[...], t["enter"][...])
        total, term = solve_modes(source, contrast_ref.at[tile], local)
        if tile == 0:
            trace_x = left_product(t["leave"][...], total)[: trace_x_ref.shape[0]]
        wave = z_transform(to_cells(total, t["backward"]), local["right_z"])
        rest = z_transform(to_cells(term, t["backward"]), local["right_z"])
        rest = times(contrast_ref[tile, 0], contrast_ref[tile, 1], rest)
        for place, x in enumerate(cells_x):
            here = slice(place * size_y, (place + 1) * size_y)
            for c in range(2):
                there = slice(c * cells_z, (c + 1) * cells_z)
                both_ref[tile, 0, c, x] = wave[here, there]
                both_ref[tile, 1, c, x] = rest[here, there]
                edge_y_ref[tile, c, x] = wave[place * size_y : place * size_y + 2, there]
                if tile == 0 and x < 2:
                    edge_x_ref[c, x] = wave[here, there]
                if tile == 1 and x < 2:
                    layer = wave[here, there]
                    if x == 0:
                        both_ref[0, 1, c, size_x - 2] += layer * (-1.0 / 12.0)
                        both_ref[0, 1, c, size_x - 1] += layer * (16.0 / 12.0)
                    else:
                        both_ref[0, 1, c, size_x - 1] += layer * (-1.0 / 12.0)


def fix_kernel(core_ref, both_ref, edge_x_ref, edge_y_ref, keep_ref, give_ref):
    core = core_ref[0]
    _, _, _, size_x, size_y, _ = both_ref.shape
    for out_ref, tile in ((keep_ref, core), (give_ref, 1 - core)):
        out_ref[...] = both_ref[tile]
        lower = (tile == 1).astype(F32)
        for c in range(2):
            near, far = edge_x_ref[c, 0] * lower, edge_x_ref[c, 1] * lower
            out_ref[1, c, size_x - 2] += near * (-1.0 / 12.0)
            out_ref[1, c, size_x - 1] += (16.0 * near - far) * (1.0 / 12.0)
            near, far = edge_y_ref[tile, c, :, 0:1], edge_y_ref[tile, c, :, 1:2]
            out_ref[1, c, :, size_y - 2 : size_y - 1] += near * (-1.0 / 12.0)
            out_ref[1, c, :, size_y - 1 : size_y] += (16.0 * near - far) * (1.0 / 12.0)


def place_kernel(core_ref, keep_ref, got_ref, wave_ref, rest_ref, sems):
    core = core_ref[0]
    copies = [
        pltpu.make_async_copy(source.at[which], out.at[index], sems.at[2 * pair + which])
        for pair, (source, index) in enumerate(((keep_ref, core), (got_ref, 1 - core)))
        for which, out in enumerate((wave_ref, rest_ref))
    ]
    for copy in copies:
        copy.start()
    for copy in copies:
        copy.wait()


def whole():
    return pl.BlockSpec(memory_space=pltpu.VMEM)


def scalars():
    return pl.BlockSpec(memory_space=pltpu.SMEM)


def anywhere():
    return pl.BlockSpec(memory_space=pl.ANY)


PARAMS = pltpu.CompilerParams(vmem_limit_bytes=40 * 1024 * 1024)


def shaped(*shape):
    return jax.ShapeDtypeStruct(shape, F32)


def body(right_side, slowness, source_cells, source_amplitudes):
    sources, _, size_x, size_y, cells_z = right_side.shape
    grid_rows, grid_cols = lax.axis_size("gx"), lax.axis_size("gy")
    assert sources == 2 and grid_rows % 2 == 0 and size_x % 2 == 0
    chips = grid_rows // 2
    row, col = lax.axis_index("gx"), lax.axis_index("gy")
    core = row % 2
    core_ref = core[None]
    t, cells_x = tables(size_x, size_y, cells_z)
    t = {name: jnp.asarray(value) for name, value in t.items()}
    cells_x = tuple(int(x) for x in cells_x)
    rows = size_x * size_y

    def device(chip, core, column):
        return (2 * chip + core) * grid_cols + column

    def between(pairs):
        return [
            (device(a, r, b), device(c, r, d)) for (a, b), (c, d) in pairs for r in range(2)
        ]

    own = [
        (device(k, r, j), device(k, 1 - r, j))
        for k in range(chips) for j in range(grid_cols) for r in range(2)
    ]
    axes = ("gx", "gy")
    other = lax.dynamic_index_in_dim(right_side, 1 - core, 0, keepdims=False)
    swapped = lax.ppermute(jnp.concatenate([other, slowness[None]], axis=0), axes, own)

    total_y = size_y * grid_cols
    cells = lax.dynamic_index_in_dim(source_cells, core, 0, keepdims=True)
    near_y = cells // cells_z % total_y - col * size_y
    places = []
    for tile_row in (row, row + 1 - 2 * core):
        near_x = cells // (total_y * cells_z) - tile_row * size_x
        inside = (near_x >= 0) & (near_x < size_x) & (near_y >= 0) & (near_y < size_y)
        folded = jnp.where(near_x < size_x // 2, near_x, size_x + size_x // 2 - 1 - near_x)
        places.append(jnp.where(inside, folded * size_y + near_y, -1))
    amplitudes = lax.dynamic_index_in_dim(source_amplitudes, core, 0, keepdims=False).T[:, None, :]

    modes, contrast = pl.pallas_call(
        functools.partial(prep_kernel, cells_x),
        out_shape=(shaped(2, rows, 2 * cells_z), shaped(2, 2, rows, cells_z)),
        in_specs=[scalars()] + [whole()] * 9,
        out_specs=(whole(), whole()),
        compiler_params=PARAMS,
        name="prep",
    )(core_ref, right_side, slowness, swapped, jnp.stack(places), cells % cells_z, amplitudes,
      *[t[name] for name in PREP])

    beat_tables = [t[name] for name in BEAT]

    def solve(tile, active, trace_x, trace_y):
        return pl.pallas_call(
            functools.partial(beat_kernel, tile),
            out_shape=(shaped(*zero_x.shape), shaped(*zero_y.shape)),
            in_specs=[scalars()] + [whole()] * (4 + len(BEAT)),
            out_specs=(whole(), whole()),
            compiler_params=PARAMS,
            name="upper" if tile == 0 else "lower",
        )(active, modes, contrast, trace_x, trace_y, *beat_tables)

    zero_x = jnp.zeros((2 * size_y, 2 * cells_z), F32)
    zero_y = jnp.zeros((2 * size_x, 2 * cells_z), F32)
    trace_x, trace_y0, trace_y1 = zero_x, zero_y, zero_y
    sums = ([], [], [])
    for beat in range(chips + grid_cols - 2):
        active = (row // 2 + col == beat).astype(jnp.int32)[None]
        here = [(k, beat - k) for k in range(chips) if 0 <= beat - k < grid_cols]
        along_x = between([((k, j), (k + 1, j)) for k, j in here if k + 1 < chips])
        along_y = between([((k, j), (k, j + 1)) for k, j in here if j + 1 < grid_cols])
        inner_x, out_y0 = solve(0, active, trace_x, trace_y0)
        trace_y0 = lax.ppermute(out_y0, axes, along_y)
        out_x, out_y1 = solve(1, active, inner_x, trace_y1)
        trace_x = lax.ppermute(out_x, axes, along_x)
        trace_y1 = lax.ppermute(out_y1, axes, along_y)
        for held, trace in zip(sums, (trace_x, trace_y0, trace_y1)):
            held.append(trace)

    both, edge_x, edge_y = pl.pallas_call(
        functools.partial(last_kernel, cells_x),
        out_shape=(
            shaped(2, 2, 2, size_x, size_y, cells_z),
            shaped(2, 2, size_y, cells_z),
            shaped(2, 2, size_x, 2, cells_z),
        ),
        in_specs=[whole()] * (5 + len(BEAT)),
        out_specs=(whole(),) * 3,
        compiler_params=PARAMS,
        name="last",
    )(modes, contrast, *[sum(held) for held in sums], *beat_tables)

    every = [(k, j) for k in range(chips) for j in range(grid_cols)]
    after_x = lax.ppermute(edge_x, axes, between([((k, j), (k - 1, j)) for k, j in every if k]))
    after_y = lax.ppermute(edge_y, axes, between([((k, j), (k, j - 1)) for k, j in every if j]))
    half = shaped(2, 2, size_x, size_y, cells_z)
    keep, give = pl.pallas_call(
        fix_kernel,
        out_shape=(half, half),
        in_specs=[scalars()] + [whole()] * 3,
        out_specs=(whole(), whole()),
        compiler_params=PARAMS,
        name="fix",
    )(core_ref, both, after_x, after_y)
    got = lax.ppermute(give, axes, own)
    return pl.pallas_call(
        place_kernel,
        out_shape=(shaped(*right_side.shape), shaped(*right_side.shape)),
        in_specs=[scalars(), anywhere(), anywhere()],
        out_specs=(anywhere(), anywhere()),
        scratch_shapes=[pltpu.SemaphoreType.DMA((4,))],
        compiler_params=PARAMS,
        name="place",
    )(core_ref, keep, got)


def solution(mesh):
    return jax.shard_map(
        body,
        mesh=mesh,
        in_specs=(P(None, None, "gx", "gy", None), P("gx", "gy", None), P(), P()),
        out_specs=(P(None, None, "gx", "gy", None), P(None, None, "gx", "gy", None)),
        check_vma=False,
    )
```

time: 101 us -> 73.3 us (0.73)
  waiting for transfers between devices: 60.5 us -> 31.5 us
  starting transfers between devices: 18.6 us -> 25 us
  local copies, waits for them, and re-layouts: 7.9 us -> 1.79 us
    ppermute x22, waiting for transfers between devices: 60.5 us -> 31.5 us  [the longest x6 26.6 us: body(): trace_x = lax.ppermute(out_x, axes, along_x)]
    ppermute x22, starting transfers between devices: 18.6 us -> 25 us  [the longest x1 5.99 us: body(): got = lax.ppermute(give, axes, own)]
    unnamed x26 -> x22, local copies, waits for them, and re-layouts: 6.08 us -> 0.74 us
    slice x2 -> x0, local copies, waits for them, and re-layouts: 1.82 us -> none  [the longest x1 0.97 us: body(): wavefield[:, :, :, :2]]
    squeeze x0 -> x1, local copies, waits for them, and re-layouts: none -> 1.04 us  [body(): other = lax.dynamic_index_in_dim(right_side, 1 - core, 0, keepdims=False)]
    pallas_call x12 -> x16, Pallas kernels: 11 us -> 12 us  [the longest x1 4.92 us: body(): pl.pallas_call(functools.partial(last_kernel, cells_x), out_shape=(shaped...]
  transfers between devices with their start and end apart: 22 -> 22, of which waited for: 3 -> 6; matrix products, arithmetic and copies ran while one was open for 1% -> 0% of each run, Pallas kernels for 0% -> 3%
where the time goes in v2:
time: 73.3 us; the launch traced here: 71.9 us
  waiting for transfers between devices  31.5 us (43%)
  starting transfers between devices  25 us (34%)
  Pallas kernels  12 us (16%)
  local copies, waits for them, and re-layouts  1.79 us (2%)
  between operations  1.42 us (2%)
    ppermute x6, waiting for transfers between devices, body(): trace_x = lax.ppermute(out_x, axes, along_x)  26.6 us
    ppermute x1, starting transfers between devices, body(): got = lax.ppermute(give, axes, own)  5.99 us
    ppermute x6, starting transfers between devices, body(): trace_y1 = lax.ppermute(out_y1, axes, along_y)  5.24 us
    ppermute x6, starting transfers between devices, body(): trace_y0 = lax.ppermute(out_y0, axes, along_y)  5.24 us
    pallas_call x1, Pallas kernels, body(): pl.pallas_call(functools.partial(last_kernel, cells_x), out_shape=(shaped...  4.92 us
    pallas_call x12, Pallas kernels, solve(): pl.pallas_call(functools.partial(beat_kernel, tile), out_shape=(shaped(*z...  4.78 us
    ppermute x6, starting transfers between devices, body(): trace_x = lax.ppermute(out_x, axes, along_x)  4.61 us
    ppermute x1, starting transfers between devices, body(): lax.ppermute(edge_y, axes, between([((k, j), (k, j - 1)) for k, j in ever...  1.92 us
  transfers between devices with their start and end apart: 22, of which 6 were waited for; matrix products, arithmetic and copies ran while one was open for 0% of the time, Pallas kernels for 3%

profile of v2, /device:TPU:29, one launch (start us, length us, event | category | flops | bytes accessed | tf_op | source)
XLA Modules:
  0.0 71.9 jit_solution(8538992748345234790)
XLA Ops:
  0.6 0.0 copy-start
  0.7 1.0 %dynamic-slice_bitcast_fusion = f32[2,16,16,128]{3,2,1,0:T(8,128)S(1)} fusion(f32[2,2,16,16,128]{4,3,2,1,0:T(8,128)} %right_ref.1, s32[]{:T(128)S(6)} %select_n.59), kind=kLoop, calls=%fused_computation.1 | loop fusion | bytes 524292 | tf_op jit(solution)/shard_map/jit(dynamic_index_in_dim)/squeeze | solution.py:315
  1.7 0.0 copy-start.1
  1.7 0.0 copy-start.4
  1.8 0.0 copy-start.9
  1.8 0.7 %collective-permute-start = (f32[3,16,16,128]{3,2,1,0:T(8,128)S(1)}, f32[3,16,16,128]{3,2,1,0:T(8,128)S(1)}, u32[]{:S(2)}, u32[]{:S(2)}) collective-permute-start(f32[3,16,16,128]{3,2,1,0:T(8,128)S(1)} %pad_maximum_fusion), channel_id=1, source_target_pairs={{0,4},{4,0},{1,5},{5,1},{2,6},{6,2},{3,7},{7,3},{8,12},{12,8},{9,1... | collective-permute-start | bytes 1179656 | tf_op jit(solution)/shard_map/ppermute | solution.py:316
  2.6 0.7 copy-done.10
  3.3 0.6 collective-permute-done.swap_ref
  3.9 0.0 copy-start.2
  3.9 0.0 copy-start.3
  3.9 0.0 copy-start.5
  4.0 0.0 copy-start.6
  4.0 1.2 %prep.1 = (f32[2,256,256]{2,1,0:T(8,128)S(1)}, f32[2,2,256,128]{3,2,1,0:T(8,128)S(1)}) custom-call(s32[1]{0:T(128)} %bitcast.core_ref, f32[2,2,16,16,128]{4,3,2,1,0:T(8,128)S(1)} %copy-done.7, f32[16,16,128]{2,1,0:T(8,128)S(1)} %copy-done.8, f32[3,16,16,128]{3,2,1,0:T(8,128)S(1)} %collective-permute-done.swap_ref, s32[2,1,16]{2,1,0:T(1,128)S(1)} %pad_add_fusion.place_ref, ...), custom_call_target="tpu_custom_call" | custom-call | tf_op jit(solution)/shard_map/prep/pallas_call | solution.py:329
  5.2 0.7 collective-permute-start.1
  5.9 0.7 collective-permute-start.2
  6.6 0.7 collective-permute-start.3
  7.2 0.0 collective-permute-done.1.trace_x_ref
  7.3 0.0 collective-permute-done.3.trace_y_ref
  7.3 0.7 collective-permute-start.4
  8.0 0.7 collective-permute-start.5
  8.7 0.7 collective-permute-start.6
  9.3 0.0 collective-permute-done.4.trace_x_ref
  9.4 0.7 collective-permute-start.7
  10.1 0.7 collective-permute-start.8
  10.8 0.7 collective-permute-start.9
  11.5 0.7 collective-permute-start.10
  12.2 0.7 collective-permute-start.11
  12.8 0.7 collective-permute-start.12
  13.5 0.2 upper.10
  13.8 1.3 %collective-permute-start.13 = (f32[32,256]{1,0:T(8,128)S(1)}, f32[32,256]{1,0:T(8,128)S(1)}, u32[]{:S(2)}, u32[]{:S(2)}) collective-permute-start(f32[32,256]{1,0:T(8,128)S(1)} %get-tuple-element.52), channel_id=1, source_target_pairs={{11,19},{15,23},{18,26},{22,30}} | collective-permute-start | bytes 98312 | tf_op jit(solution)/shard_map/ppermute | solution.py:363
  15.1 1.3 %collective-permute-start.14 = (f32[32,256]{1,0:T(8,128)S(1)}, f32[32,256]{1,0:T(8,128)S(1)}, u32[]{:S(2)}, u32[]{:S(2)}) collective-permute-start(f32[32,256]{1,0:T(8,128)S(1)} %get-tuple-element.53), channel_id=1, source_target_pairs={{18,19},{22,23},{25,26},{29,30}} | collective-permute-start | bytes 98312 | tf_op jit(solution)/shard_map/ppermute | solution.py:361
  16.4 1.3 %collective-permute-start.15 = (f32[32,256]{1,0:T(8,128)S(1)}, f32[32,256]{1,0:T(8,128)S(1)}, u32[]{:S(2)}, u32[]{:S(2)}) collective-permute-start(f32[32,256]{1,0:T(8,128)S(1)} %get-tuple-element.55), channel_id=1, source_target_pairs={{18,19},{22,23},{25,26},{29,30}} | collective-permute-start | bytes 98312 | tf_op jit(solution)/shard_map/ppermute | solution.py:364
  17.7 26.6 %collective-permute-done.13.trace_x_ref = f32[32,256]{1,0:T(8,128)S(1)} collective-permute-done((f32[32,256]{1,0:T(8,128)S(1)}, f32[32,256]{1,0:T(8,128)S(1)}, u32[]{:S(2)}, u32[]{:S(2)}) %collective-permute-start.13) | collective-permute-done | bytes 32800 | tf_op jit(solution)/shard_map/ppermute | solution.py:363
  44.3 2.2 %upper.11 = (f32[32,256]{1,0:T(8,128)S(1)}, f32[32,256]{1,0:T(8,128)S(1)}) custom-call(s32[1]{0:T(128)} %bitcast.14.active_ref, f32[2,256,256]{2,1,0:T(8,128)S(1)} %get-tuple-element.33.modes_ref, f32[2,2,256,128]{3,2,1,0:T(8,128)S(1)} %get-tuple-element.34.contrast_ref, f32[32,256]{1,0:T(8,128)S(1)} %collective-permute-done.13.trace_x_ref, ...), custom_call_target="tpu_custom_call" | custom-call | tf_op jit(solution)/shard_map/upper/pallas_call | solution.py:342
  46.5 2.2 %lower.11 = (f32[32,256]{1,0:T(8,128)S(1)}, f32[32,256]{1,0:T(8,128)S(1)}) custom-call(s32[1]{0:T(128)} %bitcast.14.active_ref, f32[2,256,256]{2,1,0:T(8,128)S(1)} %get-tuple-element.33.modes_ref, f32[2,2,256,128]{3,2,1,0:T(8,128)S(1)} %get-tuple-element.34.contrast_ref, f32[32,256]{1,0:T(8,128)S(1)} %get-tuple-element.54.trace_x_ref, ...), custom_call_target="tpu_custom_call" | custom-call | tf_op jit(solution)/shard_map/lower/pallas_call | solution.py:342
  48.8 0.7 collective-permute-start.16
  49.5 1.3 %collective-permute-start.18 = (f32[32,256]{1,0:T(8,128)S(1)}, f32[32,256]{1,0:T(8,128)S(1)}, u32[]{:S(2)}, u32[]{:S(2)}) collective-permute-start(f32[32,256]{1,0:T(8,128)S(1)} %get-tuple-element.58), channel_id=1, source_target_pairs={{26,27},{30,31}} | collective-permute-start | bytes 98312 | tf_op jit(solution)/shard_map/ppermute | solution.py:364
  50.8 1.3 %collective-permute-start.17 = (f32[32,256]{1,0:T(8,128)S(1)}, f32[32,256]{1,0:T(8,128)S(1)}, u32[]{:S(2)}, u32[]{:S(2)}) collective-permute-start(f32[32,256]{1,0:T(8,128)S(1)} %get-tuple-element.57), channel_id=1, source_target_pairs={{26,27},{30,31}} | collective-permute-start | bytes 98312 | tf_op jit(solution)/shard_map/ppermute | solution.py:361
  52.1 0.9 %collective-permute-done.17 = f32[32,256]{1,0:T(8,128)S(1)} collective-permute-done((f32[32,256]{1,0:T(8,128)S(1)}, f32[32,256]{1,0:T(8,128)S(1)}, u32[]{:S(2)}, u32[]{:S(2)}) %collective-permute-start.17) | collective-permute-done | bytes 32800 | tf_op jit(solution)/shard_map/ppermute | solution.py:361
  53.1 4.9 %last.1 = (f32[2,2,2,16,16,128]{5,4,3,2,1,0:T(8,128)S(1)}, f32[2,2,16,128]{3,2,1,0:T(8,128)S(1)}, f32[2,2,16,2,128]{4,3,2,1,0:T(2,128)S(1)}) custom-call(f32[2,256,256]{2,1,0:T(8,128)S(1)} %get-tuple-element.33.modes_ref, f32[2,2,256,128]{3,2,1,0:T(8,128)S(1)} %get-tuple-element.34.contrast_ref, f32[32,256]{1,0:T(8,128)S(1)} %add_add_fusion.2.trace_x_ref, ...), custom_call_target="tpu_custom_call" | custom-call | tf_op jit(solution)/shard_map/last/pallas_call | solution.py:368
  58.0 1.9 %collective-permute-start.20 = (f32[2,2,16,2,128]{4,3,2,1,0:T(2,128)S(1)}, f32[2,2,16,2,128]{4,3,2,1,0:T(2,128)S(1)}, u32[]{:S(2)}, u32[]{:S(2)}) collective-permute-start(f32[2,2,16,2,128]{4,3,2,1,0:T(2,128)S(1)} %get-tuple-element.61), channel_id=1, source_target_pairs={{1,0},{5,4},{2,1},{6,5},{3,2},{7,6},{9,8},{13,12},{10,9},{14,13},{... | collective-permute-start | bytes 196616 | tf_op jit(solution)/shard_map/ppermute | solution.py:383
  59.9 1.3 %collective-permute-start.19 = (f32[2,2,16,128]{3,2,1,0:T(8,128)S(1)}, f32[2,2,16,128]{3,2,1,0:T(8,128)S(1)}, u32[]{:S(2)}, u32[]{:S(2)}) collective-permute-start(f32[2,2,16,128]{3,2,1,0:T(8,128)S(1)} %get-tuple-element.60), channel_id=1, source_target_pairs={{8,0},{12,4},{9,1},{13,5},{10,2},{14,6},{11,3},{15,7},{16,8},{20,1... | collective-permute-start | bytes 98312 | tf_op jit(solution)/shard_map/ppermute | solution.py:382
  61.2 1.0 %collective-permute-done.19.edge_x_ref = f32[2,2,16,128]{3,2,1,0:T(8,128)S(1)} collective-permute-done((f32[2,2,16,128]{3,2,1,0:T(8,128)S(1)}, f32[2,2,16,128]{3,2,1,0:T(8,128)S(1)}, u32[]{:S(2)}, u32[]{:S(2)}) %collective-permute-start.19) | collective-permute-done | bytes 32800 | tf_op jit(solution)/shard_map/ppermute | solution.py:382
  62.2 0.8 %collective-permute-done.20.edge_y_ref = f32[2,2,16,2,128]{4,3,2,1,0:T(2,128)S(1)} collective-permute-done((f32[2,2,16,2,128]{4,3,2,1,0:T(2,128)S(1)}, f32[2,2,16,2,128]{4,3,2,1,0:T(2,128)S(1)}, u32[]{:S(2)}, u32[]{:S(2)}) %collective-permute-start.20) | collective-permute-done | bytes 65568 | tf_op jit(solution)/shard_map/ppermute | solution.py:383
  63.0 0.2 fix.1
  63.2 6.0 %collective-permute-start.21 = (f32[2,2,16,16,128]{4,3,2,1,0:T(8,128)S(1)}, f32[2,2,16,16,128]{4,3,2,1,0:T(8,128)S(1)}, u32[]{:S(2)}, u32[]{:S(2)}) collective-permute-start(f32[2,2,16,16,128]{4,3,2,1,0:T(8,128)S(1)} %get-tuple-element.63), channel_id=1, source_target_pairs={{0,4},{4,0},{1,5},{5,1},{2,6},{6,2},{3,7},{7,3},{8,12},{12,8},{9,1... | collective-permute-start | bytes 1572872 | tf_op jit(solution)/shard_map/ppermute | solution.py:393
  69.2 1.5 %collective-permute-done.21.got_ref = f32[2,2,16,16,128]{4,3,2,1,0:T(8,128)S(1)} collective-permute-done((f32[2,2,16,16,128]{4,3,2,1,0:T(8,128)S(1)}, f32[2,2,16,16,128]{4,3,2,1,0:T(8,128)S(1)}, u32[]{:S(2)}, u32[]{:S(2)}) %collective-permute-start.21) | collective-permute-done | bytes 524320 | tf_op jit(solution)/shard_map/ppermute | solution.py:393
  70.7 1.0 %place.1 = (f32[2,2,16,16,128]{4,3,2,1,0:T(8,128)}, f32[2,2,16,16,128]{4,3,2,1,0:T(8,128)}) custom-call(s32[1]{0:T(128)} %bitcast.core_ref, f32[2,2,16,16,128]{4,3,2,1,0:T(8,128)S(1)} %get-tuple-element.62.keep_ref, f32[2,2,16,16,128]{4,3,2,1,0:T(8,128)S(1)} %collective-permute-done.21.got_ref), custom_call_target="tpu_custom_call" | custom-call | tf_op jit(solution)/shard_map/place/pallas_call | solution.py:394
  (45 shorter events, 0.3 us)
Async XLA Ops:
  0.6 2.6 %copy-start = (f32[2,16,2]{1,2,0:T(2,128)S(1)}, f32[2,16,2]{1,2,0:T(2,128)}, u32[]{:S(2)}) copy-start(f32[2,16,2]{1,2,0:T(2,128)} %param.14) | copy-start | bytes 772
  0.7 1.1 %copy-start.8 = (f32[16,16,128]{2,1,0:T(8,128)S(1)}, f32[16,16,128]{2,1,0:T(8,128)}, u32[]{:S(2)}) copy-start(f32[16,16,128]{2,1,0:T(8,128)} %slow_ref.1) | copy-start | bytes 393220
  0.7 3.2 %copy-start.7 = (f32[2,2,16,16,128]{4,3,2,1,0:T(8,128)S(1)}, f32[2,2,16,16,128]{4,3,2,1,0:T(8,128)}, u32[]{:S(2)}) copy-start(f32[2,2,16,16,128]{4,3,2,1,0:T(8,128)} %right_ref.1) | copy-start | bytes 1572868
  1.7 2.2 %copy-start.1 = (bf16[2,256,256]{2,1,0:T(8,128)(2,1)S(1)}, bf16[2,256,256]{2,1,0:T(8,128)(2,1)}, u32[]{:S(2)}) copy-start(bf16[2,256,256]{2,1,0:T(8,128)(2,1)} %constant.139.clone.forward_ref.refs_1_) | copy-start | bytes 786436
  1.7 2.2 %copy-start.4 = (bf16[256,256]{1,0:T(8,128)(2,1)S(1)}, bf16[256,256]{1,0:T(8,128)(2,1)}, u32[]{:S(2)}) copy-start(bf16[256,256]{1,0:T(8,128)(2,1)} %constant.141.clone.z_ref.refs_3_) | copy-start | bytes 393220
  1.8 2.1 %copy-start.9 = (f32[256,1]{1,0:T(8,128)S(1)}, f32[256,1]{1,0:T(8,128)}, u32[]{:S(2)}) copy-start(f32[256,1]{1,0:T(8,128)} %constant.144.clone.edge_ref) | copy-start | bytes 3076
  1.8 2.1 %collective-permute-start = (f32[3,16,16,128]{3,2,1,0:T(8,128)S(1)}, f32[3,16,16,128]{3,2,1,0:T(8,128)S(1)}, u32[]{:S(2)}, u32[]{:S(2)}) collective-permute-start(f32[3,16,16,128]{3,2,1,0:T(8,128)S(1)} %pad_maximum_fusion), channel_id=1, source_target_pairs={{0,4},{4,0},{1,5},{5,1},{2,6},{6,2},{3,7},{7,3},{8,12},{12,8},{9,1... | collective-permute-start | bytes 1179656 | tf_op jit(solution)/shard_map/ppermute | solution.py:316
  2.5 0.7 copy-start.10
  3.9 1.2 %copy-start.2 = (bf16[2,256,256]{2,1,0:T(8,128)(2,1)S(1)}, bf16[2,256,256]{2,1,0:T(8,128)(2,1)}, u32[]{:S(2)}) copy-start(bf16[2,256,256]{2,1,0:T(8,128)(2,1)} %constant.140.clone.refs_2_) | copy-start | bytes 786436
  3.9 1.2 %copy-start.3 = (f32[2,256,128]{2,1,0:T(8,128)S(1)}, f32[2,256,128]{2,1,0:T(8,128)}, u32[]{:S(2)}) copy-start(f32[2,256,128]{2,1,0:T(8,128)} %constant.138.clone.refs_0_) | copy-start | bytes 786436
  3.9 1.2 %copy-start.5 = (bf16[128,512]{1,0:T(8,128)(2,1)S(1)}, bf16[128,512]{1,0:T(8,128)(2,1)}, u32[]{:S(2)}) copy-start(bf16[128,512]{1,0:T(8,128)(2,1)} %constant.143.clone.refs_5_) | copy-start | bytes 393220
  4.0 1.2 %copy-start.6 = (bf16[512,128]{1,0:T(8,128)(2,1)S(1)}, bf16[512,128]{1,0:T(8,128)(2,1)}, u32[]{:S(2)}) copy-start(bf16[512,128]{1,0:T(8,128)(2,1)} %constant.142.clone.refs_4_) | copy-start | bytes 393220
  5.2 2.0 %collective-permute-start.1 = (f32[32,256]{1,0:T(8,128)S(1)}, f32[32,256]{1,0:T(8,128)S(1)}, u32[]{:S(2)}, u32[]{:S(2)}) collective-permute-start(f32[32,256]{1,0:T(8,128)S(1)} %get-tuple-element.36), channel_id=1, source_target_pairs={{0,8},{4,12}} | collective-permute-start | bytes 98312 | tf_op jit(solution)/shard_map/ppermute | solution.py:363
  5.9 1.4 %collective-permute-start.2 = (f32[32,256]{1,0:T(8,128)S(1)}, f32[32,256]{1,0:T(8,128)S(1)}, u32[]{:S(2)}, u32[]{:S(2)}) collective-permute-start(f32[32,256]{1,0:T(8,128)S(1)} %get-tuple-element.37), channel_id=1, source_target_pairs={{0,1},{4,5}} | collective-permute-start | bytes 98312 | tf_op jit(solution)/shard_map/ppermute | solution.py:361
  6.6 0.7 %collective-permute-start.3 = (f32[32,256]{1,0:T(8,128)S(1)}, f32[32,256]{1,0:T(8,128)S(1)}, u32[]{:S(2)}, u32[]{:S(2)}) collective-permute-start(f32[32,256]{1,0:T(8,128)S(1)} %get-tuple-element.39), channel_id=1, source_target_pairs={{0,1},{4,5}} | collective-permute-start | bytes 98312 | tf_op jit(solution)/shard_map/ppermute | solution.py:364
  7.3 2.0 %collective-permute-start.4 = (f32[32,256]{1,0:T(8,128)S(1)}, f32[32,256]{1,0:T(8,128)S(1)}, u32[]{:S(2)}, u32[]{:S(2)}) collective-permute-start(f32[32,256]{1,0:T(8,128)S(1)} %get-tuple-element.40), channel_id=1, source_target_pairs={{1,9},{5,13},{8,16},{12,20}} | collective-permute-start | bytes 98312 | tf_op jit(solution)/shard_map/ppermute | solution.py:363
  8.0 1.4 %collective-permute-start.5 = (f32[32,256]{1,0:T(8,128)S(1)}, f32[32,256]{1,0:T(8,128)S(1)}, u32[]{:S(2)}, u32[]{:S(2)}) collective-permute-start(f32[32,256]{1,0:T(8,128)S(1)} %get-tuple-element.41), channel_id=1, source_target_pairs={{1,2},{5,6},{8,9},{12,13}} | collective-permute-start | bytes 98312 | tf_op jit(solution)/shard_map/ppermute | solution.py:361
  8.7 0.7 %collective-permute-start.6 = (f32[32,256]{1,0:T(8,128)S(1)}, f32[32,256]{1,0:T(8,128)S(1)}, u32[]{:S(2)}, u32[]{:S(2)}) collective-permute-start(f32[32,256]{1,0:T(8,128)S(1)} %get-tuple-element.43), channel_id=1, source_target_pairs={{1,2},{5,6},{8,9},{12,13}} | collective-permute-start | bytes 98312 | tf_op jit(solution)/shard_map/ppermute | solution.py:364
  9.4 2.0 %collective-permute-start.7 = (f32[32,256]{1,0:T(8,128)S(1)}, f32[32,256]{1,0:T(8,128)S(1)}, u32[]{:S(2)}, u32[]{:S(2)}) collective-permute-start(f32[32,256]{1,0:T(8,128)S(1)} %get-tuple-element.44), channel_id=1, source_target_pairs={{2,10},{6,14},{9,17},{13,21},{16,24},{20,28}} | collective-permute-start | bytes 98312 | tf_op jit(solution)/shard_map/ppermute | solution.py:363
  10.1 1.4 %collective-permute-start.8 = (f32[32,256]{1,0:T(8,128)S(1)}, f32[32,256]{1,0:T(8,128)S(1)}, u32[]{:S(2)}, u32[]{:S(2)}) collective-permute-start(f32[32,256]{1,0:T(8,128)S(1)} %get-tuple-element.45), channel_id=1, source_target_pairs={{2,3},{6,7},{9,10},{13,14},{16,17},{20,21}} | collective-permute-start | bytes 98312 | tf_op jit(solution)/shard_map/ppermute | solution.py:361
  10.8 0.7 %collective-permute-start.9 = (f32[32,256]{1,0:T(8,128)S(1)}, f32[32,256]{1,0:T(8,128)S(1)}, u32[]{:S(2)}, u32[]{:S(2)}) collective-permute-start(f32[32,256]{1,0:T(8,128)S(1)} %get-tuple-element.47), channel_id=1, source_target_pairs={{2,3},{6,7},{9,10},{13,14},{16,17},{20,21}} | collective-permute-start | bytes 98312 | tf_op jit(solution)/shard_map/ppermute | solution.py:364
  11.5 2.0 %collective-permute-start.10 = (f32[32,256]{1,0:T(8,128)S(1)}, f32[32,256]{1,0:T(8,128)S(1)}, u32[]{:S(2)}, u32[]{:S(2)}) collective-permute-start(f32[32,256]{1,0:T(8,128)S(1)} %get-tuple-element.48), channel_id=1, source_target_pairs={{3,11},{7,15},{10,18},{14,22},{17,25},{21,29}} | collective-permute-start | bytes 98312 | tf_op jit(solution)/shard_map/ppermute | solution.py:363
  12.2 1.4 %collective-permute-start.11 = (f32[32,256]{1,0:T(8,128)S(1)}, f32[32,256]{1,0:T(8,128)S(1)}, u32[]{:S(2)}, u32[]{:S(2)}) collective-permute-start(f32[32,256]{1,0:T(8,128)S(1)} %get-tuple-element.49), channel_id=1, source_target_pairs={{10,11},{14,15},{17,18},{21,22},{24,25},{28,29}} | collective-permute-start | bytes 98312 | tf_op jit(solution)/shard_map/ppermute | solution.py:361
  12.8 0.9 %collective-permute-start.12 = (f32[32,256]{1,0:T(8,128)S(1)}, f32[32,256]{1,0:T(8,128)S(1)}, u32[]{:S(2)}, u32[]{:S(2)}) collective-permute-start(f32[32,256]{1,0:T(8,128)S(1)} %get-tuple-element.51), channel_id=1, source_target_pairs={{10,11},{14,15},{17,18},{21,22},{24,25},{28,29}} | collective-permute-start | bytes 98312 | tf_op jit(solution)/shard_map/ppermute | solution.py:364
  13.8 30.5 %collective-permute-start.13 = (f32[32,256]{1,0:T(8,128)S(1)}, f32[32,256]{1,0:T(8,128)S(1)}, u32[]{:S(2)}, u32[]{:S(2)}) collective-permute-start(f32[32,256]{1,0:T(8,128)S(1)} %get-tuple-element.52), channel_id=1, source_target_pairs={{11,19},{15,23},{18,26},{22,30}} | collective-permute-start | bytes 98312 | tf_op jit(solution)/shard_map/ppermute | solution.py:363
  15.1 29.2 %collective-permute-start.14 = (f32[32,256]{1,0:T(8,128)S(1)}, f32[32,256]{1,0:T(8,128)S(1)}, u32[]{:S(2)}, u32[]{:S(2)}) collective-permute-start(f32[32,256]{1,0:T(8,128)S(1)} %get-tuple-element.53), channel_id=1, source_target_pairs={{18,19},{22,23},{25,26},{29,30}} | collective-permute-start | bytes 98312 | tf_op jit(solution)/shard_map/ppermute | solution.py:361
  16.4 30.1 %collective-permute-start.15 = (f32[32,256]{1,0:T(8,128)S(1)}, f32[32,256]{1,0:T(8,128)S(1)}, u32[]{:S(2)}, u32[]{:S(2)}) collective-permute-start(f32[32,256]{1,0:T(8,128)S(1)} %get-tuple-element.55), channel_id=1, source_target_pairs={{18,19},{22,23},{25,26},{29,30}} | collective-permute-start | bytes 98312 | tf_op jit(solution)/shard_map/ppermute | solution.py:364
  48.8 3.3 %collective-permute-start.16 = (f32[32,256]{1,0:T(8,128)S(1)}, f32[32,256]{1,0:T(8,128)S(1)}, u32[]{:S(2)}, u32[]{:S(2)}) collective-permute-start(f32[32,256]{1,0:T(8,128)S(1)} %get-tuple-element.56), channel_id=1, source_target_pairs={{19,27},{23,31}} | collective-permute-start | bytes 98312 | tf_op jit(solution)/shard_map/ppermute | solution.py:363
  49.5 2.6 %collective-permute-start.18 = (f32[32,256]{1,0:T(8,128)S(1)}, f32[32,256]{1,0:T(8,128)S(1)}, u32[]{:S(2)}, u32[]{:S(2)}) collective-permute-start(f32[32,256]{1,0:T(8,128)S(1)} %get-tuple-element.58), channel_id=1, source_target_pairs={{26,27},{30,31}} | collective-permute-start | bytes 98312 | tf_op jit(solution)/shard_map/ppermute | solution.py:364
  50.8 2.3 %collective-permute-start.17 = (f32[32,256]{1,0:T(8,128)S(1)}, f32[32,256]{1,0:T(8,128)S(1)}, u32[]{:S(2)}, u32[]{:S(2)}) collective-permute-start(f32[32,256]{1,0:T(8,128)S(1)} %get-tuple-element.57), channel_id=1, source_target_pairs={{26,27},{30,31}} | collective-permute-start | bytes 98312 | tf_op jit(solution)/shard_map/ppermute | solution.py:361
  58.0 5.0 %collective-permute-start.20 = (f32[2,2,16,2,128]{4,3,2,1,0:T(2,128)S(1)}, f32[2,2,16,2,128]{4,3,2,1,0:T(2,128)S(1)}, u32[]{:S(2)}, u32[]{:S(2)}) collective-permute-start(f32[2,2,16,2,128]{4,3,2,1,0:T(2,128)S(1)} %get-tuple-element.61), channel_id=1, source_target_pairs={{1,0},{5,4},{2,1},{6,5},{3,2},{7,6},{9,8},{13,12},{10,9},{14,13},{... | collective-permute-start | bytes 196616 | tf_op jit(solution)/shard_map/ppermute | solution.py:383
  59.9 2.3 %collective-permute-start.19 = (f32[2,2,16,128]{3,2,1,0:T(8,128)S(1)}, f32[2,2,16,128]{3,2,1,0:T(8,128)S(1)}, u32[]{:S(2)}, u32[]{:S(2)}) collective-permute-start(f32[2,2,16,128]{3,2,1,0:T(8,128)S(1)} %get-tuple-element.60), channel_id=1, source_target_pairs={{8,0},{12,4},{9,1},{13,5},{10,2},{14,6},{11,3},{15,7},{16,8},{20,1... | collective-permute-start | bytes 98312 | tf_op jit(solution)/shard_map/ppermute | solution.py:382
  63.2 7.5 %collective-permute-start.21 = (f32[2,2,16,16,128]{4,3,2,1,0:T(8,128)S(1)}, f32[2,2,16,16,128]{4,3,2,1,0:T(8,128)S(1)}, u32[]{:S(2)}, u32[]{:S(2)}) collective-permute-start(f32[2,2,16,16,128]{4,3,2,1,0:T(8,128)S(1)} %get-tuple-element.63), channel_id=1, source_target_pairs={{0,4},{4,0},{1,5},{5,1},{2,6},{6,2},{3,7},{7,3},{8,12},{12,8},{9,1... | collective-permute-start | bytes 1572872 | tf_op jit(solution)/shard_map/ppermute | solution.py:393

commit v3 on v2

--- a/solution.py
+++ b/solution.py
@@ -139,15 +139,34 @@
     term = times(t["inverse"][0], t["inverse"][1], source_modes)
     total = term
     for _ in range(2):
-        cells = z_transform(to_cells(term, t["backward"]), t["right_z"])
-        cells = times(contrast[0], contrast[1], cells)
-        term = times(t["inverse"][0], t["inverse"][1], to_modes(z_transform(cells, t["right_z"]), t["forward"]))
+        cells = apply_contrast(to_cells(term, t["backward"]), contrast, t["right_z"])
+        term = times(t["inverse"][0], t["inverse"][1], to_modes(cells, t["forward"]))
         total = total + term
     return total, term
 
 
+def apply_contrast(field, contrast, right_z, block=64):
+    done = []
+    for start in range(0, field.shape[0], block):
+        here = slice(start, start + block)
+        cells = times(contrast[0, here], contrast[1, here], z_transform(field[here], right_z))
+        done.append(z_transform(cells, right_z))
+    return jnp.concatenate(done, axis=0)
+
+
 PREP = ("edge", "forward", "right_z")
 BEAT = ("inverse", "forward", "backward", "right_z", "enter", "leave")
+
+
+def gather_kernel(core_ref, right_ref, slow_ref, swap_ref, sems):
+    copies = [
+        pltpu.make_async_copy(right_ref.at[1 - core_ref[0]], swap_ref.at[pl.ds(0, 2)], sems.at[0]),
+        pltpu.make_async_copy(slow_ref, swap_ref.at[2], sems.at[1]),
+    ]
+    for copy in copies:
+        copy.start()
+    for copy in copies:
+        copy.wait()
 
 
 def prep_kernel(cells_x, core_ref, right_ref, slow_ref, swap_ref, place_ref, depth_ref, amp_ref, edge_ref,
@@ -206,9 +225,9 @@
         out_y_ref[...] = out[count:]
 
 
-def last_kernel(cells_x, modes_ref, contrast_ref, trace_x_ref, trace_y0_ref, trace_y1_ref, *refs):
+def last_kernel(cells_x, core_ref, modes_ref, contrast_ref, trace_x_ref, trace_y0_ref, trace_y1_ref, *refs):
     t = {name: ref for name, ref in zip(BEAT, refs)}
-    both_ref, edge_x_ref, edge_y_ref = refs[len(BEAT) :]
+    keep_ref, give_ref, edge_x_ref, edge_y_ref, both_ref = refs[len(BEAT) :]
     size_y, cells_z = both_ref.shape[4], both_ref.shape[5]
     size_x = both_ref.shape[3]
     local = dict(t, right_z=t["right_z"][...])
@@ -237,32 +256,31 @@
                         both_ref[0, 1, c, size_x - 1] += layer * (16.0 / 12.0)
                     else:
                         both_ref[0, 1, c, size_x - 1] += layer * (-1.0 / 12.0)
-
-
-def fix_kernel(core_ref, both_ref, edge_x_ref, edge_y_ref, keep_ref, give_ref):
+    keep_ref[...] = both_ref[core_ref[0]]
+    give_ref[...] = both_ref[1 - core_ref[0]]
+
+
+def place_kernel(core_ref, keep_ref, got_ref, keep_x_ref, keep_y_ref, got_x_ref, got_y_ref,
+                 wave_ref, rest_ref, work_ref, sems):
     core = core_ref[0]
-    _, _, _, size_x, size_y, _ = both_ref.shape
-    for out_ref, tile in ((keep_ref, core), (give_ref, 1 - core)):
-        out_ref[...] = both_ref[tile]
-        lower = (tile == 1).astype(F32)
+    _, _, size_x, size_y, _ = keep_ref.shape
+    lower = (core == 1).astype(F32)
+    parts = ((keep_ref, keep_x_ref, keep_y_ref, core), (got_ref, got_x_ref, got_y_ref, 1 - core))
+    copies = []
+    for n, (part, _, _, index) in enumerate(parts):
+        copies.append(pltpu.make_async_copy(part.at[0], wave_ref.at[index], sems.at[n]))
+        copies[-1].start()
+    for n, (part, edge_x, edge_y, index) in enumerate(parts):
+        work_ref[n] = part[1]
         for c in range(2):
-            near, far = edge_x_ref[c, 0] * lower, edge_x_ref[c, 1] * lower
-            out_ref[1, c, size_x - 2] += near * (-1.0 / 12.0)
-            out_ref[1, c, size_x - 1] += (16.0 * near - far) * (1.0 / 12.0)
-            near, far = edge_y_ref[tile, c, :, 0:1], edge_y_ref[tile, c, :, 1:2]
-            out_ref[1, c, :, size_y - 2 : size_y - 1] += near * (-1.0 / 12.0)
-            out_ref[1, c, :, size_y - 1 : size_y] += (16.0 * near - far) * (1.0 / 12.0)
-
-
-def place_kernel(core_ref, keep_ref, got_ref, wave_ref, rest_ref, sems):
-    core = core_ref[0]
-    copies = [
-        pltpu.make_async_copy(source.at[which], out.at[index], sems.at[2 * pair + which])
-        for pair, (source, index) in enumerate(((keep_ref, core), (got_ref, 1 - core)))
-        for which, out in enumerate((wave_ref, rest_ref))
-    ]
-    for copy in copies:
-        copy.start()
+            near, far = edge_x[c, 0] * lower, edge_x[c, 1] * lower
+            work_ref[n, c, size_x - 2] += near * (-1.0 / 12.0)
+            work_ref[n, c, size_x - 1] += (16.0 * near - far) * (1.0 / 12.0)
+            near, far = edge_y[c, :, 0:1], edge_y[c, :, 1:2]
+            work_ref[n, c, :, size_y - 2 : size_y - 1] += near * (-1.0 / 12.0)
+            work_ref[n, c, :, size_y - 1 : size_y] += (16.0 * near - far) * (1.0 / 12.0)
+        copies.append(pltpu.make_async_copy(work_ref.at[n], rest_ref.at[index], sems.at[2 + n]))
+        copies[-1].start()
     for copy in copies:
         copy.wait()
 
@@ -312,8 +330,16 @@
         for k in range(chips) for j in range(grid_cols) for r in range(2)
     ]
     axes = ("gx", "gy")
-    other = lax.dynamic_index_in_dim(right_side, 1 - core, 0, keepdims=False)
-    swapped = lax.ppermute(jnp.concatenate([other, slowness[None]], axis=0), axes, own)
+    swapped = pl.pallas_call(
+        gather_kernel,
+        out_shape=shaped(3, size_x, size_y, cells_z),
+        in_specs=[scalars(), anywhere(), anywhere()],
+        out_specs=anywhere(),
+        scratch_shapes=[pltpu.SemaphoreType.DMA((2,))],
+        compiler_params=PARAMS,
+        name="gather",
+    )(core_ref, right_side, slowness)
+    swapped = lax.ppermute(swapped, axes, own)
 
     total_y = size_y * grid_cols
     cells = lax.dynamic_index_in_dim(source_cells, core, 0, keepdims=True)
@@ -360,46 +386,50 @@
         inner_x, out_y0 = solve(0, active, trace_x, trace_y0)
         trace_y0 = lax.ppermute(out_y0, axes, along_y)
         out_x, out_y1 = solve(1, active, inner_x, trace_y1)
+        out_x, trace_y0 = lax.optimization_barrier((out_x, trace_y0))
         trace_x = lax.ppermute(out_x, axes, along_x)
         trace_y1 = lax.ppermute(out_y1, axes, along_y)
         for held, trace in zip(sums, (trace_x, trace_y0, trace_y1)):
             held.append(trace)
 
-    both, edge_x, edge_y = pl.pallas_call(
+    half = shaped(2, 2, size_x, size_y, cells_z)
+    keep, give, edge_x, edge_y = pl.pallas_call(
         functools.partial(last_kernel, cells_x),
         out_shape=(
-            shaped(2, 2, 2, size_x, size_y, cells_z),
+            half,
+            half,
             shaped(2, 2, size_y, cells_z),
             shaped(2, 2, size_x, 2, cells_z),
         ),
-        in_specs=[whole()] * (5 + len(BEAT)),
-        out_specs=(whole(),) * 3,
+        in_specs=[scalars()] + [whole()] * (5 + len(BEAT)),
+        out_specs=(whole(),) * 4,
+        scratch_shapes=[pltpu.VMEM((2, 2, 2, size_x, size_y, cells_z), F32)],
         compiler_params=PARAMS,
         name="last",
-    )(modes, contrast, *[sum(held) for held in sums], *beat_tables)
+    )(core_ref, modes, contrast, *[sum(held) for held in sums], *beat_tables)
 
     every = [(k, j) for k in range(chips) for j in range(grid_cols)]
     after_x = lax.ppermute(edge_x, axes, between([((k, j), (k - 1, j)) for k, j in every if k]))
     after_y = lax.ppermute(edge_y, axes, between([((k, j), (k, j - 1)) for k, j in every if j]))
-    half = shaped(2, 2, size_x, size_y, cells_z)
-    keep, give = pl.pallas_call(
-        fix_kernel,
-        out_shape=(half, half),
-        in_specs=[scalars()] + [whole()] * 3,
-        out_specs=(whole(), whole()),
-        compiler_params=PARAMS,
-        name="fix",
-    )(core_ref, both, after_x, after_y)
     got = lax.ppermute(give, axes, own)
+    keep_y = lax.dynamic_index_in_dim(after_y, core, 0, keepdims=False)
+    pass_y = lax.dynamic_index_in_dim(after_y, 1 - core, 0, keepdims=False)
+    passed = jnp.concatenate([after_x, pass_y.transpose(0, 2, 1, 3)], axis=2)
+    passed = lax.ppermute(passed, axes, own)
+    got_x = passed[:, :, :size_y]
+    got_y = passed[:, :, size_y:].transpose(0, 2, 1, 3)
     return pl.pallas_call(
         place_kernel,
         out_shape=(shaped(*right_side.shape), shaped(*right_side.shape)),
-        in_specs=[scalars(), anywhere(), anywhere()],
+        in_specs=[scalars()] + [whole()] * 6,
         out_specs=(anywhere(), anywhere()),
-        scratch_shapes=[pltpu.SemaphoreType.DMA((4,))],
+        scratch_shapes=[
+            pltpu.VMEM((2, 2, size_x, size_y, cells_z), F32),
+            pltpu.SemaphoreType.DMA((4,)),
+        ],
         compiler_params=PARAMS,
         name="place",
-    )(core_ref, keep, got)
+    )(core_ref, keep, got, after_x, keep_y, got_x, got_y)
 
 
 def solution(mesh):

time: 73.3 us -> 85 us (1.16)
  the two profiles are of different devices: /device:TPU:29 before, /device:TPU:23 now
where the time goes in v3:
time: 85 us; the launch traced here: 84.6 us
  waiting for transfers between devices  39.1 us (46%)
  starting transfers between devices  28.6 us (34%)
  Pallas kernels  11.7 us (14%)
  local copies, waits for them, and re-layouts  3.62 us (4%)
  between operations  1.39 us (2%)
    ppermute x6, waiting for transfers between devices, body(): trace_y0 = lax.ppermute(out_y0, axes, along_y)  31.9 us
    ppermute x1, starting transfers between devices, body(): got = lax.ppermute(give, axes, own)  9 us
    ppermute x6, starting transfers between devices, body(): trace_x = lax.ppermute(out_x, axes, along_x)  5.22 us
    pallas_call x1, Pallas kernels, body(): pl.pallas_call(functools.partial(last_kernel, cells_x), out_shape=(half,...  4.74 us
    ppermute x6, starting transfers between devices, body(): trace_y0 = lax.ppermute(out_y0, axes, along_y)  4.61 us
    ppermute x6, starting transfers between devices, body(): trace_y1 = lax.ppermute(out_y1, axes, along_y)  4.61 us
    pallas_call x12, Pallas kernels, solve(): pl.pallas_call(functools.partial(beat_kernel, tile), out_shape=(shaped(*z...  4.56 us
    unnamed x26, local copies, waits for them, and re-layouts  3.56 us
  transfers between devices with their start and end apart: 23, of which 6 were waited for; matrix products, arithmetic and copies ran while one was open for 0% of the time, Pallas kernels for 5%

profile of v3, /device:TPU:23, one launch (start us, length us, event | category | flops | bytes accessed | tf_op | source)
XLA Modules:
  0.0 84.6 jit_solution(6923531198999608037)
XLA Ops:
  0.6 0.0 copy-start
  0.7 1.0 %copy-done.7 = f32[2,2,16,16,128]{4,3,2,1,0:T(8,128)S(1)} copy-done((f32[2,2,16,16,128]{4,3,2,1,0:T(8,128)S(1)}, f32[2,2,16,16,128]{4,3,2,1,0:T(8,128)}, u32[]{:S(2)}) %copy-start.7) | copy-done | bytes 524312
  1.7 0.9 %copy-done.9 = f32[16,16,128]{2,1,0:T(8,128)S(1)} copy-done((f32[16,16,128]{2,1,0:T(8,128)S(1)}, f32[16,16,128]{2,1,0:T(8,128)}, u32[]{:S(2)}) %copy-start.9) | copy-done | bytes 131096
  2.6 0.2 gather.1
  2.8 0.7 collective-permute-start
  3.6 0.7 copy-done.12
  4.4 0.6 collective-permute-done.swap_ref
  4.9 0.0 copy-start.11
  5.0 0.9 %copy-done.11 = f32[256,1]{1,0:T(8,128)S(1)} copy-done((f32[256,1]{1,0:T(8,128)S(1)}, f32[256,1]{1,0:T(8,128)}, u32[]{:S(2)}) %copy-start.11) | copy-done | bytes 1048
  5.9 1.2 %prep.1 = (f32[2,256,256]{2,1,0:T(8,128)S(1)}, f32[2,2,256,128]{3,2,1,0:T(8,128)S(1)}) custom-call(s32[1]{0:T(128)} %bitcast.core_ref, f32[2,2,16,16,128]{4,3,2,1,0:T(8,128)S(1)} %copy-done.8, f32[16,16,128]{2,1,0:T(8,128)S(1)} %copy-done.10, f32[3,16,16,128]{3,2,1,0:T(8,128)S(1)} %collective-permute-done.swap_ref, s32[2,1,16]{2,1,0:T(1,128)S(1)} %pad_add_fusion.place_ref, ...), custom_call_target="tpu_custom_call" | custom-call | tf_op jit(solution)/shard_map/prep/pallas_call | solution.py:355
  7.1 0.7 collective-permute-start.1
  7.8 0.0 collective-permute-done.1.trace_y_ref
  7.8 0.7 collective-permute-start.2
  8.5 0.7 collective-permute-start.3
  9.2 0.0 collective-permute-done.2.trace_x_ref
  9.2 0.7 collective-permute-start.4
  9.9 0.7 collective-permute-start.5
  10.6 0.7 collective-permute-start.6
  11.3 0.0 collective-permute-done.5.trace_x_ref
  11.3 0.7 collective-permute-start.7
  12.0 0.0 collective-permute-done.6.trace_y_ref
  12.0 0.0 collective-permute-done.7.trace_y_ref
  12.0 0.7 collective-permute-start.8
  12.7 0.7 collective-permute-start.9
  13.4 0.7 collective-permute-start.10
  14.0 0.0 collective-permute-done.9.trace_y_ref
  14.1 0.2 lower.9
  14.3 0.7 collective-permute-start.11
  14.9 0.7 collective-permute-start.12
  15.7 1.3 %collective-permute-start.13 = (f32[32,256]{1,0:T(8,128)S(1)}, f32[32,256]{1,0:T(8,128)S(1)}, u32[]{:S(2)}, u32[]{:S(2)}) collective-permute-start(f32[32,256]{1,0:T(8,128)S(1)} %get-tuple-element.72), channel_id=1, source_target_pairs={{18,19},{22,23},{25,26},{29,30}} | collective-permute-start | bytes 98312 | tf_op jit(solution)/shard_map/ppermute | solution.py:387
  17.0 31.9 %collective-permute-done.13.trace_y_ref = f32[32,256]{1,0:T(8,128)S(1)} collective-permute-done((f32[32,256]{1,0:T(8,128)S(1)}, f32[32,256]{1,0:T(8,128)S(1)}, u32[]{:S(2)}, u32[]{:S(2)}) %collective-permute-start.13) | collective-permute-done | bytes 32800 | tf_op jit(solution)/shard_map/ppermute | solution.py:387
  48.9 1.3 %collective-permute-start.14 = (f32[32,256]{1,0:T(8,128)S(1)}, f32[32,256]{1,0:T(8,128)S(1)}, u32[]{:S(2)}, u32[]{:S(2)}) collective-permute-start(f32[32,256]{1,0:T(8,128)S(1)} %get-tuple-element.73), channel_id=1, source_target_pairs={{11,19},{15,23},{18,26},{22,30}} | collective-permute-start | bytes 98312 | tf_op jit(solution)/shard_map/ppermute | solution.py:390
  50.2 1.3 %collective-permute-start.15 = (f32[32,256]{1,0:T(8,128)S(1)}, f32[32,256]{1,0:T(8,128)S(1)}, u32[]{:S(2)}, u32[]{:S(2)}) collective-permute-start(f32[32,256]{1,0:T(8,128)S(1)} %get-tuple-element.76), channel_id=1, source_target_pairs={{18,19},{22,23},{25,26},{29,30}} | collective-permute-start | bytes 98312 | tf_op jit(solution)/shard_map/ppermute | solution.py:391
  51.5 2.1 %collective-permute-done.14.trace_x_ref = f32[32,256]{1,0:T(8,128)S(1)} collective-permute-done((f32[32,256]{1,0:T(8,128)S(1)}, f32[32,256]{1,0:T(8,128)S(1)}, u32[]{:S(2)}, u32[]{:S(2)}) %collective-permute-start.14) | collective-permute-done | bytes 32800 | tf_op jit(solution)/shard_map/ppermute | solution.py:390
  53.5 2.1 %upper.11 = (f32[32,256]{1,0:T(8,128)S(1)}, f32[32,256]{1,0:T(8,128)S(1)}) custom-call(s32[1]{0:T(128)} %bitcast.12.active_ref, f32[2,256,256]{2,1,0:T(8,128)S(1)} %get-tuple-element.44.modes_ref, f32[2,2,256,128]{3,2,1,0:T(8,128)S(1)} %get-tuple-element.45.contrast_ref, f32[32,256]{1,0:T(8,128)S(1)} %collective-permute-done.14.trace_x_ref, ...), custom_call_target="tpu_custom_call" | custom-call | tf_op jit(solution)/shard_map/upper/pallas_call | solution.py:368
  55.6 0.7 collective-permute-start.16
  56.3 2.1 %lower.11 = (f32[32,256]{1,0:T(8,128)S(1)}, f32[32,256]{1,0:T(8,128)S(1)}) custom-call(s32[1]{0:T(128)} %bitcast.12.active_ref, f32[2,256,256]{2,1,0:T(8,128)S(1)} %get-tuple-element.44.modes_ref, f32[2,2,256,128]{3,2,1,0:T(8,128)S(1)} %get-tuple-element.45.contrast_ref, f32[32,256]{1,0:T(8,128)S(1)} %get-tuple-element.75.trace_x_ref, ...), custom_call_target="tpu_custom_call" | custom-call | tf_op jit(solution)/shard_map/lower/pallas_call | solution.py:368
  58.5 0.7 collective-permute-start.18
  59.2 1.3 %collective-permute-start.17 = (f32[32,256]{1,0:T(8,128)S(1)}, f32[32,256]{1,0:T(8,128)S(1)}, u32[]{:S(2)}, u32[]{:S(2)}) collective-permute-start(f32[32,256]{1,0:T(8,128)S(1)} %get-tuple-element.79), channel_id=1, source_target_pairs={{19,27},{23,31}} | collective-permute-start | bytes 98312 | tf_op jit(solution)/shard_map/ppermute | solution.py:390
  60.5 1.0 %collective-permute-done.17 = f32[32,256]{1,0:T(8,128)S(1)} collective-permute-done((f32[32,256]{1,0:T(8,128)S(1)}, f32[32,256]{1,0:T(8,128)S(1)}, u32[]{:S(2)}, u32[]{:S(2)}) %collective-permute-start.17) | collective-permute-done | bytes 32800 | tf_op jit(solution)/shard_map/ppermute | solution.py:390
  61.5 4.7 %last.1 = (f32[2,2,16,16,128]{4,3,2,1,0:T(8,128)S(1)}, f32[2,2,16,16,128]{4,3,2,1,0:T(8,128)S(1)}, f32[2,2,16,128]{3,2,1,0:T(8,128)S(1)}, f32[2,2,16,2,128]{4,3,2,1,0:T(2,128)S(1)}) custom-call(s32[1]{0:T(128)} %bitcast.core_ref, f32[2,256,256]{2,1,0:T(8,128)S(1)} %get-tuple-element.44.modes_ref, f32[2,2,256,128]{3,2,1,0:T(8,128)S(1)} %get-tuple-element.45.contrast_ref, ...), custom_call_target="tpu_custom_call" | custom-call | tf_op jit(solution)/shard_map/last/pallas_call | solution.py:396
  66.2 1.3 %collective-permute-start.21 = (f32[2,2,16,2,128]{4,3,2,1,0:T(2,128)S(1)}, f32[2,2,16,2,128]{4,3,2,1,0:T(2,128)S(1)}, u32[]{:S(2)}, u32[]{:S(2)}) collective-permute-start(f32[2,2,16,2,128]{4,3,2,1,0:T(2,128)S(1)} %get-tuple-element.85), channel_id=1, source_target_pairs={{1,0},{5,4},{2,1},{6,5},{3,2},{7,6},{9,8},{13,12},{10,9},{14,13},{... | collective-permute-start | bytes 196616 | tf_op jit(solution)/shard_map/ppermute | solution.py:413
  67.5 9.0 %collective-permute-start.19 = (f32[2,2,16,16,128]{4,3,2,1,0:T(8,128)S(1)}, f32[2,2,16,16,128]{4,3,2,1,0:T(8,128)S(1)}, u32[]{:S(2)}, u32[]{:S(2)}) collective-permute-start(f32[2,2,16,16,128]{4,3,2,1,0:T(8,128)S(1)} %get-tuple-element.83), channel_id=1, source_target_pairs={{0,4},{4,0},{1,5},{5,1},{2,6},{6,2},{3,7},{7,3},{8,12},{12,8},{9,1... | collective-permute-start | bytes 1572872 | tf_op jit(solution)/shard_map/ppermute | solution.py:414
  76.6 1.9 %collective-permute-start.20 = (f32[2,2,16,128]{3,1,2,0:T(2,128)S(1)}, f32[2,2,16,128]{3,1,2,0:T(2,128)S(1)}, u32[]{:S(2)}, u32[]{:S(2)}) collective-permute-start(f32[2,2,16,128]{3,1,2,0:T(2,128)S(1)} %copy.14), channel_id=1, source_target_pairs={{8,0},{12,4},{9,1},{13,5},{10,2},{14,6},{11,3},{15,7},{16,8},{20,1... | collective-permute-start | bytes 98312 | tf_op jit(solution)/shard_map/ppermute | solution.py:412
  78.5 2.7 %collective-permute-done.20 = f32[2,2,16,128]{3,1,2,0:T(2,128)S(1)} collective-permute-done((f32[2,2,16,128]{3,1,2,0:T(2,128)S(1)}, f32[2,2,16,128]{3,1,2,0:T(2,128)S(1)}, u32[]{:S(2)}, u32[]{:S(2)}) %collective-permute-start.20) | collective-permute-done | bytes 32800 | tf_op jit(solution)/shard_map/ppermute | solution.py:412
  81.3 1.2 %collective-permute-start.22 = (f32[2,2,32,128]{3,1,2,0:T(2,128)S(1)}, f32[2,2,32,128]{3,1,2,0:T(2,128)S(1)}, u32[]{:S(2)}, u32[]{:S(2)}) collective-permute-start(f32[2,2,32,128]{3,1,2,0:T(2,128)S(1)} %pad_maximum_fusion), channel_id=1, source_target_pairs={{0,4},{4,0},{1,5},{5,1},{2,6},{6,2},{3,7},{7,3},{8,12},{12,8},{9,1... | collective-permute-start | bytes 196616 | tf_op jit(solution)/shard_map/ppermute | solution.py:418
  82.5 0.9 %collective-permute-done.22 = f32[2,2,32,128]{3,1,2,0:T(2,128)S(1)} collective-permute-done((f32[2,2,32,128]{3,1,2,0:T(2,128)S(1)}, f32[2,2,32,128]{3,1,2,0:T(2,128)S(1)}, u32[]{:S(2)}, u32[]{:S(2)}) %collective-permute-start.22) | collective-permute-done | bytes 65568 | tf_op jit(solution)/shard_map/ppermute | solution.py:418
  83.4 1.0 %place.1 = (f32[2,2,16,16,128]{4,3,2,1,0:T(8,128)}, f32[2,2,16,16,128]{4,3,2,1,0:T(8,128)}) custom-call(s32[1]{0:T(128)} %bitcast.core_ref, f32[2,2,16,16,128]{4,3,2,1,0:T(8,128)S(1)} %get-tuple-element.82.keep_ref, f32[2,2,16,16,128]{4,3,2,1,0:T(8,128)S(1)} %collective-permute-done.19.got_ref, f32[2,2,16,128]{3,2,1,0:T(8,128)S(1)} %copy.15.keep_x_ref, ...), custom_call_target="tpu_custom_call" | custom-call | tf_op jit(solution)/shard_map/place/pallas_call | solution.py:421
  (55 shorter events, 0.4 us)
Async XLA Ops:
  0.6 3.7 %copy-start = (f32[2,16,2]{1,2,0:T(2,128)S(1)}, f32[2,16,2]{1,2,0:T(2,128)}, u32[]{:S(2)}) copy-start(f32[2,16,2]{1,2,0:T(2,128)} %param.14) | copy-start | bytes 772
  0.7 1.0 %copy-start.7 = (f32[2,2,16,16,128]{4,3,2,1,0:T(8,128)S(1)}, f32[2,2,16,16,128]{4,3,2,1,0:T(8,128)}, u32[]{:S(2)}) copy-start(f32[2,2,16,16,128]{4,3,2,1,0:T(8,128)} %right_ref.3) | copy-start | bytes 1572868
  1.7 0.9 %copy-start.9 = (f32[16,16,128]{2,1,0:T(8,128)S(1)}, f32[16,16,128]{2,1,0:T(8,128)}, u32[]{:S(2)}) copy-start(f32[16,16,128]{2,1,0:T(8,128)} %slow_ref.3) | copy-start | bytes 393220
  2.6 2.3 %copy-start.1 = (bf16[2,256,256]{2,1,0:T(8,128)(2,1)S(1)}, bf16[2,256,256]{2,1,0:T(8,128)(2,1)}, u32[]{:S(2)}) copy-start(bf16[2,256,256]{2,1,0:T(8,128)(2,1)} %constant.141.clone.forward_ref.refs_1_) | copy-start | bytes 786436
  2.6 2.3 %copy-start.4 = (bf16[256,256]{1,0:T(8,128)(2,1)S(1)}, bf16[256,256]{1,0:T(8,128)(2,1)}, u32[]{:S(2)}) copy-start(bf16[256,256]{1,0:T(8,128)(2,1)} %constant.143.clone.z_ref.refs_3_) | copy-start | bytes 393220
  2.6 2.3 %copy-start.8 = (f32[2,2,16,16,128]{4,3,2,1,0:T(8,128)S(1)}, f32[2,2,16,16,128]{4,3,2,1,0:T(8,128)}, u32[]{:S(2)}) copy-start(f32[2,2,16,16,128]{4,3,2,1,0:T(8,128)} %right_ref.3) | copy-start | bytes 1572868
  2.6 2.3 %copy-start.10 = (f32[16,16,128]{2,1,0:T(8,128)S(1)}, f32[16,16,128]{2,1,0:T(8,128)}, u32[]{:S(2)}) copy-start(f32[16,16,128]{2,1,0:T(8,128)} %slow_ref.3) | copy-start | bytes 393220
  2.8 2.1 %collective-permute-start = (f32[3,16,16,128]{3,2,1,0:T(8,128)S(1)}, f32[3,16,16,128]{3,2,1,0:T(8,128)S(1)}, u32[]{:S(2)}, u32[]{:S(2)}) collective-permute-start(f32[3,16,16,128]{3,2,1,0:T(8,128)S(1)} %gather.1), channel_id=1, source_target_pairs={{0,4},{4,0},{1,5},{5,1},{2,6},{6,2},{3,7},{7,3},{8,12},{12,8},{9,1... | collective-permute-start | bytes 1179656 | tf_op jit(solution)/shard_map/ppermute | solution.py:342
  3.6 0.7 copy-start.12
  4.9 0.9 %copy-start.11 = (f32[256,1]{1,0:T(8,128)S(1)}, f32[256,1]{1,0:T(8,128)}, u32[]{:S(2)}) copy-start(f32[256,1]{1,0:T(8,128)} %constant.146.clone.edge_ref) | copy-start | bytes 3076
  5.9 1.2 %copy-start.2 = (f32[2,256,128]{2,1,0:T(8,128)S(1)}, f32[2,256,128]{2,1,0:T(8,128)}, u32[]{:S(2)}) copy-start(f32[2,256,128]{2,1,0:T(8,128)} %constant.140.clone.refs_0_) | copy-start | bytes 786436
  5.9 1.2 %copy-start.3 = (bf16[2,256,256]{2,1,0:T(8,128)(2,1)S(1)}, bf16[2,256,256]{2,1,0:T(8,128)(2,1)}, u32[]{:S(2)}) copy-start(bf16[2,256,256]{2,1,0:T(8,128)(2,1)} %constant.142.clone.refs_2_) | copy-start | bytes 786436
  5.9 1.2 %copy-start.5 = (bf16[512,128]{1,0:T(8,128)(2,1)S(1)}, bf16[512,128]{1,0:T(8,128)(2,1)}, u32[]{:S(2)}) copy-start(bf16[512,128]{1,0:T(8,128)(2,1)} %constant.144.clone.refs_4_) | copy-start | bytes 393220
  5.9 1.2 %copy-start.6 = (bf16[128,512]{1,0:T(8,128)(2,1)S(1)}, bf16[128,512]{1,0:T(8,128)(2,1)}, u32[]{:S(2)}) copy-start(bf16[128,512]{1,0:T(8,128)(2,1)} %constant.145.clone.refs_5_) | copy-start | bytes 393220
  7.1 0.7 collective-permute-start.1
  7.8 1.4 %collective-permute-start.2 = (f32[32,256]{1,0:T(8,128)S(1)}, f32[32,256]{1,0:T(8,128)S(1)}, u32[]{:S(2)}, u32[]{:S(2)}) collective-permute-start(f32[32,256]{1,0:T(8,128)S(1)} %get-tuple-element.49), channel_id=1, source_target_pairs={{0,8},{4,12}} | collective-permute-start | bytes 98312 | tf_op jit(solution)/shard_map/ppermute | solution.py:390
  8.5 1.4 %collective-permute-start.3 = (f32[32,256]{1,0:T(8,128)S(1)}, f32[32,256]{1,0:T(8,128)S(1)}, u32[]{:S(2)}, u32[]{:S(2)}) collective-permute-start(f32[32,256]{1,0:T(8,128)S(1)} %get-tuple-element.52), channel_id=1, source_target_pairs={{0,1},{4,5}} | collective-permute-start | bytes 98312 | tf_op jit(solution)/shard_map/ppermute | solution.py:391
  9.2 0.7 collective-permute-start.4
  9.9 1.4 %collective-permute-start.5 = (f32[32,256]{1,0:T(8,128)S(1)}, f32[32,256]{1,0:T(8,128)S(1)}, u32[]{:S(2)}, u32[]{:S(2)}) collective-permute-start(f32[32,256]{1,0:T(8,128)S(1)} %get-tuple-element.55), channel_id=1, source_target_pairs={{1,9},{5,13},{8,16},{12,20}} | collective-permute-start | bytes 98312 | tf_op jit(solution)/shard_map/ppermute | solution.py:390
  10.6 1.4 %collective-permute-start.6 = (f32[32,256]{1,0:T(8,128)S(1)}, f32[32,256]{1,0:T(8,128)S(1)}, u32[]{:S(2)}, u32[]{:S(2)}) collective-permute-start(f32[32,256]{1,0:T(8,128)S(1)} %get-tuple-element.58), channel_id=1, source_target_pairs={{1,2},{5,6},{8,9},{12,13}} | collective-permute-start | bytes 98312 | tf_op jit(solution)/shard_map/ppermute | solution.py:391
  11.3 0.7 collective-permute-start.7
  12.0 1.4 %collective-permute-start.8 = (f32[32,256]{1,0:T(8,128)S(1)}, f32[32,256]{1,0:T(8,128)S(1)}, u32[]{:S(2)}, u32[]{:S(2)}) collective-permute-start(f32[32,256]{1,0:T(8,128)S(1)} %get-tuple-element.61), channel_id=1, source_target_pairs={{2,10},{6,14},{9,17},{13,21},{16,24},{20,28}} | collective-permute-start | bytes 98312 | tf_op jit(solution)/shard_map/ppermute | solution.py:390
  12.7 1.4 %collective-permute-start.9 = (f32[32,256]{1,0:T(8,128)S(1)}, f32[32,256]{1,0:T(8,128)S(1)}, u32[]{:S(2)}, u32[]{:S(2)}) collective-permute-start(f32[32,256]{1,0:T(8,128)S(1)} %get-tuple-element.64), channel_id=1, source_target_pairs={{2,3},{6,7},{9,10},{13,14},{16,17},{20,21}} | collective-permute-start | bytes 98312 | tf_op jit(solution)/shard_map/ppermute | solution.py:391
  13.4 0.9 %collective-permute-start.10 = (f32[32,256]{1,0:T(8,128)S(1)}, f32[32,256]{1,0:T(8,128)S(1)}, u32[]{:S(2)}, u32[]{:S(2)}) collective-permute-start(f32[32,256]{1,0:T(8,128)S(1)} %get-tuple-element.66), channel_id=1, source_target_pairs={{10,11},{14,15},{17,18},{21,22},{24,25},{28,29}} | collective-permute-start | bytes 98312 | tf_op jit(solution)/shard_map/ppermute | solution.py:387
  14.3 1.4 %collective-permute-start.11 = (f32[32,256]{1,0:T(8,128)S(1)}, f32[32,256]{1,0:T(8,128)S(1)}, u32[]{:S(2)}, u32[]{:S(2)}) collective-permute-start(f32[32,256]{1,0:T(8,128)S(1)} %get-tuple-element.67), channel_id=1, source_target_pairs={{3,11},{7,15},{10,18},{14,22},{17,25},{21,29}} | collective-permute-start | bytes 98312 | tf_op jit(solution)/shard_map/ppermute | solution.py:390
  14.9 2.0 %collective-permute-start.12 = (f32[32,256]{1,0:T(8,128)S(1)}, f32[32,256]{1,0:T(8,128)S(1)}, u32[]{:S(2)}, u32[]{:S(2)}) collective-permute-start(f32[32,256]{1,0:T(8,128)S(1)} %get-tuple-element.70), channel_id=1, source_target_pairs={{10,11},{14,15},{17,18},{21,22},{24,25},{28,29}} | collective-permute-start | bytes 98312 | tf_op jit(solution)/shard_map/ppermute | solution.py:391
  15.7 33.2 %collective-permute-start.13 = (f32[32,256]{1,0:T(8,128)S(1)}, f32[32,256]{1,0:T(8,128)S(1)}, u32[]{:S(2)}, u32[]{:S(2)}) collective-permute-start(f32[32,256]{1,0:T(8,128)S(1)} %get-tuple-element.72), channel_id=1, source_target_pairs={{18,19},{22,23},{25,26},{29,30}} | collective-permute-start | bytes 98312 | tf_op jit(solution)/shard_map/ppermute | solution.py:387
  48.9 4.6 %collective-permute-start.14 = (f32[32,256]{1,0:T(8,128)S(1)}, f32[32,256]{1,0:T(8,128)S(1)}, u32[]{:S(2)}, u32[]{:S(2)}) collective-permute-start(f32[32,256]{1,0:T(8,128)S(1)} %get-tuple-element.73), channel_id=1, source_target_pairs={{11,19},{15,23},{18,26},{22,30}} | collective-permute-start | bytes 98312 | tf_op jit(solution)/shard_map/ppermute | solution.py:390
  50.2 6.2 %collective-permute-start.15 = (f32[32,256]{1,0:T(8,128)S(1)}, f32[32,256]{1,0:T(8,128)S(1)}, u32[]{:S(2)}, u32[]{:S(2)}) collective-permute-start(f32[32,256]{1,0:T(8,128)S(1)} %get-tuple-element.76), channel_id=1, source_target_pairs={{18,19},{22,23},{25,26},{29,30}} | collective-permute-start | bytes 98312 | tf_op jit(solution)/shard_map/ppermute | solution.py:391
  55.6 3.5 %collective-permute-start.16 = (f32[32,256]{1,0:T(8,128)S(1)}, f32[32,256]{1,0:T(8,128)S(1)}, u32[]{:S(2)}, u32[]{:S(2)}) collective-permute-start(f32[32,256]{1,0:T(8,128)S(1)} %get-tuple-element.78), channel_id=1, source_target_pairs={{26,27},{30,31}} | collective-permute-start | bytes 98312 | tf_op jit(solution)/shard_map/ppermute | solution.py:387
  58.5 2.0 %collective-permute-start.18 = (f32[32,256]{1,0:T(8,128)S(1)}, f32[32,256]{1,0:T(8,128)S(1)}, u32[]{:S(2)}, u32[]{:S(2)}) collective-permute-start(f32[32,256]{1,0:T(8,128)S(1)} %get-tuple-element.81), channel_id=1, source_target_pairs={{26,27},{30,31}} | collective-permute-start | bytes 98312 | tf_op jit(solution)/shard_map/ppermute | solution.py:391
  59.2 2.3 %collective-permute-start.17 = (f32[32,256]{1,0:T(8,128)S(1)}, f32[32,256]{1,0:T(8,128)S(1)}, u32[]{:S(2)}, u32[]{:S(2)}) collective-permute-start(f32[32,256]{1,0:T(8,128)S(1)} %get-tuple-element.79), channel_id=1, source_target_pairs={{19,27},{23,31}} | collective-permute-start | bytes 98312 | tf_op jit(solution)/shard_map/ppermute | solution.py:390
  66.2 12.3 %collective-permute-start.21 = (f32[2,2,16,2,128]{4,3,2,1,0:T(2,128)S(1)}, f32[2,2,16,2,128]{4,3,2,1,0:T(2,128)S(1)}, u32[]{:S(2)}, u32[]{:S(2)}) collective-permute-start(f32[2,2,16,2,128]{4,3,2,1,0:T(2,128)S(1)} %get-tuple-element.85), channel_id=1, source_target_pairs={{1,0},{5,4},{2,1},{6,5},{3,2},{7,6},{9,8},{13,12},{10,9},{14,13},{... | collective-permute-start | bytes 196616 | tf_op jit(solution)/shard_map/ppermute | solution.py:413
  67.5 15.9 %collective-permute-start.19 = (f32[2,2,16,16,128]{4,3,2,1,0:T(8,128)S(1)}, f32[2,2,16,16,128]{4,3,2,1,0:T(8,128)S(1)}, u32[]{:S(2)}, u32[]{:S(2)}) collective-permute-start(f32[2,2,16,16,128]{4,3,2,1,0:T(8,128)S(1)} %get-tuple-element.83), channel_id=1, source_target_pairs={{0,4},{4,0},{1,5},{5,1},{2,6},{6,2},{3,7},{7,3},{8,12},{12,8},{9,1... | collective-permute-start | bytes 1572872 | tf_op jit(solution)/shard_map/ppermute | solution.py:414
  76.6 4.7 %collective-permute-start.20 = (f32[2,2,16,128]{3,1,2,0:T(2,128)S(1)}, f32[2,2,16,128]{3,1,2,0:T(2,128)S(1)}, u32[]{:S(2)}, u32[]{:S(2)}) collective-permute-start(f32[2,2,16,128]{3,1,2,0:T(2,128)S(1)} %copy.14), channel_id=1, source_target_pairs={{8,0},{12,4},{9,1},{13,5},{10,2},{14,6},{11,3},{15,7},{16,8},{20,1... | collective-permute-start | bytes 98312 | tf_op jit(solution)/shard_map/ppermute | solution.py:412
  81.3 2.1 %collective-permute-start.22 = (f32[2,2,32,128]{3,1,2,0:T(2,128)S(1)}, f32[2,2,32,128]{3,1,2,0:T(2,128)S(1)}, u32[]{:S(2)}, u32[]{:S(2)}) collective-permute-start(f32[2,2,32,128]{3,1,2,0:T(2,128)S(1)} %pad_maximum_fusion), channel_id=1, source_target_pairs={{0,4},{4,0},{1,5},{5,1},{2,6},{6,2},{3,7},{7,3},{8,12},{12,8},{9,1... | collective-permute-start | bytes 196616 | tf_op jit(solution)/shard_map/ppermute | solution.py:418

commit v4 on v2

--- a/solution.py
+++ b/solution.py
@@ -79,6 +79,15 @@
             axis=1,
         ).T
     )
+    first = left_factor(
+        np.concatenate(
+            [
+                by_cell[:, :2].reshape(len(full), -1),
+                by_cell[:, :, :2].transpose(0, 2, 1).reshape(len(full), -1),
+            ],
+            axis=1,
+        ).T
+    )
     edge = np.zeros((size_x, size_y, 1))
     edge[0] += 1.0 / 12.0
     edge[-1] += 1.0 / 12.0
@@ -87,7 +96,7 @@
     edge = edge[cells].reshape(size_x * size_y, 1).astype(np.float32)
     return dict(
         inverse=inverse, forward=forward, backward=backward, right_z=right_z,
-        enter=enter, leave=leave, edge=edge,
+        enter=enter, leave=leave, first=first, edge=edge,
     ), cells
 
 
@@ -139,52 +148,74 @@
     term = times(t["inverse"][0], t["inverse"][1], source_modes)
     total = term
     for _ in range(2):
-        cells = z_transform(to_cells(term, t["backward"]), t["right_z"])
-        cells = times(contrast[0], contrast[1], cells)
-        term = times(t["inverse"][0], t["inverse"][1], to_modes(z_transform(cells, t["right_z"]), t["forward"]))
+        cells = apply_contrast(to_cells(term, t["backward"]), contrast, t["right_z"])
+        term = times(t["inverse"][0], t["inverse"][1], to_modes(cells, t["forward"]))
         total = total + term
     return total, term
 
 
+def apply_contrast(field, contrast, right_z, block=64):
+    done = []
+    for start in range(0, field.shape[0], block):
+        here = slice(start, start + block)
+        cells = times(contrast[0, here], contrast[1, here], z_transform(field[here], right_z))
+        done.append(z_transform(cells, right_z))
+    return jnp.concatenate(done, axis=0)
+
+
 PREP = ("edge", "forward", "right_z")
 BEAT = ("inverse", "forward", "backward", "right_z", "enter", "leave")
 
 
-def prep_kernel(cells_x, core_ref, right_ref, slow_ref, swap_ref, place_ref, depth_ref, amp_ref, edge_ref,
-                forward_ref, z_ref, modes_ref, contrast_ref):
-    _, _, size_x, size_y, cells_z = right_ref.shape
-    rows = size_x * size_y
-    core = core_ref[0]
-    points = place_ref.shape[2]
+def hand_on_kernel(in_ref, out_ref):
+    out_ref[...] = in_ref[...]
+
+
+def prepare(dense, slow, place, depth, amplitude, edge, forward, right_z, modes_ref, contrast_ref):
+    rows, cells_z = contrast_ref.shape[1:]
+    points = place.shape[1]
     row_ids = lax.broadcasted_iota(jnp.int32, (rows, points), 0)
     lane_ids = lax.broadcasted_iota(jnp.int32, (cells_z, points), 0)
-    at_lane = (lane_ids == depth_ref[...]).astype(F32)
+    at_lane = (lane_ids == depth).astype(F32)
     spread = []
     for c in range(2):
-        amp = amp_ref[c]
+        amp = amplitude[c]
         one = amp.astype(BF16).astype(F32)
         two = (amp - one).astype(BF16).astype(F32)
         parts = [at_lane * part for part in (one, two, amp - one - two)]
         spread.append(jnp.concatenate(parts, axis=1).astype(BF16))
-    spread = jnp.concatenate(spread, axis=0)
-    for other in range(2):
-        tile = core if other == 0 else 1 - core
-        if other == 0:
-            slow = [slow_ref[x] for x in cells_x]
-            dense = [[right_ref[core, c, x] for x in cells_x] for c in range(2)]
-        else:
-            slow = [swap_ref[2, x] for x in cells_x]
-            dense = [[swap_ref[c, x] for x in cells_x] for c in range(2)]
-        scaled = KAPPA * (jnp.concatenate(slow, axis=0) - 1.0)
-        contrast_ref[tile, 0] = scaled - edge_ref[...]
-        contrast_ref[tile, 1] = DAMPING * scaled
-        at_row = (row_ids == place_ref[other]).astype(F32).astype(BF16)
-        field = lax.dot_general(
-            jnp.concatenate([at_row] * 3, axis=1), spread, (((1,), (1,)), ((), ())),
-            preferred_element_type=F32,
-        )
-        field = field + jnp.concatenate([jnp.concatenate(d, axis=0) for d in dense], axis=1)
-        modes_ref[tile] = to_modes(z_transform(field, z_ref[...]), forward_ref)
+    scaled = KAPPA * (slow - 1.0)
+    contrast_ref[0] = scaled - edge
+    contrast_ref[1] = DAMPING * scaled
+    at_row = (row_ids == place).astype(F32).astype(BF16)
+    field = lax.dot_general(
+        jnp.concatenate([at_row] * 3, axis=1), jnp.concatenate(spread, axis=0),
+        (((1,), (1,)), ((), ())), preferred_element_type=F32,
+    )
+    modes_ref[...] = to_modes(z_transform(field + dense, right_z), forward)
+
+
+def prep_kernel(cells_x, core_ref, right_ref, slow_ref, place_ref, depth_ref, amp_ref, edge_ref,
+                forward_ref, z_ref, modes_ref, contrast_ref):
+    dense = [jnp.concatenate([right_ref[core_ref[0], c, x] for x in cells_x], axis=0) for c in range(2)]
+    slow = jnp.concatenate([slow_ref[x] for x in cells_x], axis=0)
+    prepare(
+        jnp.concatenate(dense, axis=1), slow, place_ref[...], depth_ref[...], amp_ref, edge_ref[...],
+        forward_ref, z_ref[...], modes_ref, contrast_ref,
+    )
+
+
+def prep_other_kernel(cells_x, core_ref, swap_ref, own_modes_ref, own_contrast_ref, place_ref, depth_ref,
+                      amp_ref, edge_ref, forward_ref, z_ref, modes_ref, contrast_ref):
+    core = core_ref[0]
+    other = 1 - core
+    modes_ref[core] = own_modes_ref[...]
+    contrast_ref[core] = own_contrast_ref[...]
+    parts = [jnp.concatenate([swap_ref[c, x] for x in cells_x], axis=0) for c in range(3)]
+    prepare(
+        jnp.concatenate(parts[:2], axis=1), parts[2], place_ref[...], depth_ref[...], amp_ref,
+        edge_ref[...], forward_ref, z_ref[...], modes_ref.at[other], contrast_ref.at[other],
+    )
 
 
 def source_modes(modes, trace_x, trace_y, enter):
@@ -206,20 +237,33 @@
         out_y_ref[...] = out[count:]
 
 
-def last_kernel(cells_x, modes_ref, contrast_ref, trace_x_ref, trace_y0_ref, trace_y1_ref, *refs):
-    t = {name: ref for name, ref in zip(BEAT, refs)}
-    both_ref, edge_x_ref, edge_y_ref = refs[len(BEAT) :]
-    size_y, cells_z = both_ref.shape[4], both_ref.shape[5]
-    size_x = both_ref.shape[3]
+LAST = BEAT + ("first",)
+FINISH = ("backward", "right_z")
+
+
+def last_kernel(tile, modes_ref, contrast_ref, trace_x_ref, trace_y_ref, *refs):
+    t = {name: ref for name, ref in zip(LAST, refs)}
+    total_ref, term_ref, edge_x_ref, edge_y_ref, out_x_ref = refs[len(LAST) :]
     local = dict(t, right_z=t["right_z"][...])
-    trace_x = trace_x_ref[...]
-    for tile, trace_y_ref in enumerate((trace_y0_ref, trace_y1_ref)):
-        source = source_modes(modes_ref[tile], trace_x, trace_y_ref[...], t["enter"][...])
-        total, term = solve_modes(source, contrast_ref.at[tile], local)
-        if tile == 0:
-            trace_x = left_product(t["leave"][...], total)[: trace_x_ref.shape[0]]
-        wave = z_transform(to_cells(total, t["backward"]), local["right_z"])
-        rest = z_transform(to_cells(term, t["backward"]), local["right_z"])
+    count = trace_x_ref.shape[0]
+    source = source_modes(modes_ref[tile], trace_x_ref[...], trace_y_ref[...], t["enter"][...])
+    total, term = solve_modes(source, contrast_ref.at[tile], local)
+    total_ref[...] = total
+    term_ref[...] = term
+    edges = z_transform(left_product(t["first"][...], total), local["right_z"])
+    edge_x_ref[...] = edges[:count]
+    edge_y_ref[...] = edges[count:]
+    if tile == 0:
+        out_x_ref[...] = left_product(t["leave"][...], total)[:count]
+
+
+def finish_kernel(cells_x, core_ref, total0_ref, term0_ref, total1_ref, term1_ref, contrast_ref, backward_ref,
+                  z_ref, keep_ref, give_ref, both_ref):
+    _, _, _, size_x, size_y, cells_z = both_ref.shape
+    right_z = z_ref[...]
+    for tile, (total_ref, term_ref) in enumerate(((total0_ref, term0_ref), (total1_ref, term1_ref))):
+        wave = z_transform(to_cells(total_ref[...], backward_ref), right_z)
+        rest = z_transform(to_cells(term_ref[...], backward_ref), right_z)
         rest = times(contrast_ref[tile, 0], contrast_ref[tile, 1], rest)
         for place, x in enumerate(cells_x):
             here = slice(place * size_y, (place + 1) * size_y)
@@ -227,9 +271,6 @@
                 there = slice(c * cells_z, (c + 1) * cells_z)
                 both_ref[tile, 0, c, x] = wave[here, there]
                 both_ref[tile, 1, c, x] = rest[here, there]
-                edge_y_ref[tile, c, x] = wave[place * size_y : place * size_y + 2, there]
-                if tile == 0 and x < 2:
-                    edge_x_ref[c, x] = wave[here, there]
                 if tile == 1 and x < 2:
                     layer = wave[here, there]
                     if x == 0:
@@ -237,32 +278,41 @@
                         both_ref[0, 1, c, size_x - 1] += layer * (16.0 / 12.0)
                     else:
                         both_ref[0, 1, c, size_x - 1] += layer * (-1.0 / 12.0)
-
-
-def fix_kernel(core_ref, both_ref, edge_x_ref, edge_y_ref, keep_ref, give_ref):
+    keep_ref[...] = both_ref[core_ref[0]]
+    give_ref[...] = both_ref[1 - core_ref[0]]
+
+
+def add_later(rest_ref, edge_x, edge_y, lower):
+    _, size_x, size_y, cells_z = rest_ref.shape
+    for c in range(2):
+        there = slice(c * cells_z, (c + 1) * cells_z)
+        near, far = edge_x[:size_y, there] * lower, edge_x[size_y:, there] * lower
+        rest_ref[c, size_x - 2] += near * (-1.0 / 12.0)
+        rest_ref[c, size_x - 1] += (16.0 * near - far) * (1.0 / 12.0)
+        near, far = edge_y[:size_x, there], edge_y[size_x:, there]
+        two = jnp.stack([near * (-1.0 / 12.0), (16.0 * near - far) * (1.0 / 12.0)], axis=1)
+        rest_ref[c, :, size_y - 2 :] += two
+
+
+def keep_kernel(core_ref, keep_ref, edge_x_ref, edge_y_ref, rest_ref):
+    rest_ref[...] = keep_ref[1]
+    add_later(rest_ref, edge_x_ref[...], edge_y_ref[...], (core_ref[0] == 1).astype(F32))
+
+
+def place_kernel(core_ref, keep_ref, keep_rest_ref, got_ref, got_edge_ref, wave_ref, rest_ref, work_ref, sems):
     core = core_ref[0]
-    _, _, _, size_x, size_y, _ = both_ref.shape
-    for out_ref, tile in ((keep_ref, core), (give_ref, 1 - core)):
-        out_ref[...] = both_ref[tile]
-        lower = (tile == 1).astype(F32)
-        for c in range(2):
-            near, far = edge_x_ref[c, 0] * lower, edge_x_ref[c, 1] * lower
-            out_ref[1, c, size_x - 2] += near * (-1.0 / 12.0)
-            out_ref[1, c, size_x - 1] += (16.0 * near - far) * (1.0 / 12.0)
-            near, far = edge_y_ref[tile, c, :, 0:1], edge_y_ref[tile, c, :, 1:2]
-            out_ref[1, c, :, size_y - 2 : size_y - 1] += near * (-1.0 / 12.0)
-            out_ref[1, c, :, size_y - 1 : size_y] += (16.0 * near - far) * (1.0 / 12.0)
-
-
-def place_kernel(core_ref, keep_ref, got_ref, wave_ref, rest_ref, sems):
-    core = core_ref[0]
+    count = got_edge_ref.shape[0] // 2
     copies = [
-        pltpu.make_async_copy(source.at[which], out.at[index], sems.at[2 * pair + which])
-        for pair, (source, index) in enumerate(((keep_ref, core), (got_ref, 1 - core)))
-        for which, out in enumerate((wave_ref, rest_ref))
+        pltpu.make_async_copy(keep_ref.at[0], wave_ref.at[core], sems.at[0]),
+        pltpu.make_async_copy(got_ref.at[0], wave_ref.at[1 - core], sems.at[1]),
+        pltpu.make_async_copy(keep_rest_ref, rest_ref.at[core], sems.at[2]),
     ]
     for copy in copies:
         copy.start()
+    work_ref[...] = got_ref[1]
+    add_later(work_ref, got_edge_ref[:count], got_edge_ref[count:], (core == 1).astype(F32))
+    copies.append(pltpu.make_async_copy(work_ref, rest_ref.at[1 - core], sems.at[3]))
+    copies[-1].start()
     for copy in copies:
         copy.wait()
 
@@ -279,6 +329,8 @@
     return pl.BlockSpec(memory_space=pl.ANY)
 
 
+SOLVE_COST = pl.CostEstimate(flops=2 * 10**9, bytes_accessed=2 * 10**6, transcendentals=0)
+KEEP_COST = pl.CostEstimate(flops=10**10, bytes_accessed=10**6, transcendentals=0)
 PARAMS = pltpu.CompilerParams(vmem_limit_bytes=40 * 1024 * 1024)
 
 
@@ -326,15 +378,25 @@
         places.append(jnp.where(inside, folded * size_y + near_y, -1))
     amplitudes = lax.dynamic_index_in_dim(source_amplitudes, core, 0, keepdims=False).T[:, None, :]
 
+    depth = cells % cells_z
+    prep_tables = [t[name] for name in PREP]
+    one = (shaped(rows, 2 * cells_z), shaped(2, rows, cells_z))
+    own_modes, own_contrast = pl.pallas_call(
+        functools.partial(prep_kernel, cells_x),
+        out_shape=one,
+        in_specs=[scalars()] + [whole()] * 8,
+        out_specs=(whole(), whole()),
+        compiler_params=PARAMS,
+        name="prep",
+    )(core_ref, right_side, slowness, places[0], depth, amplitudes, *prep_tables)
     modes, contrast = pl.pallas_call(
-        functools.partial(prep_kernel, cells_x),
+        functools.partial(prep_other_kernel, cells_x),
         out_shape=(shaped(2, rows, 2 * cells_z), shaped(2, 2, rows, cells_z)),
         in_specs=[scalars()] + [whole()] * 9,
         out_specs=(whole(), whole()),
         compiler_params=PARAMS,
-        name="prep",
-    )(core_ref, right_side, slowness, swapped, jnp.stack(places), cells % cells_z, amplitudes,
-      *[t[name] for name in PREP])
+        name="prep_other",
+    )(core_ref, swapped, own_modes, own_contrast, places[1], depth, amplitudes, *prep_tables)
 
     beat_tables = [t[name] for name in BEAT]
 
@@ -345,8 +407,19 @@
             in_specs=[scalars()] + [whole()] * (4 + len(BEAT)),
             out_specs=(whole(), whole()),
             compiler_params=PARAMS,
+            cost_estimate=SOLVE_COST,
             name="upper" if tile == 0 else "lower",
         )(active, modes, contrast, trace_x, trace_y, *beat_tables)
+
+    def hand_on(trace):
+        return pl.pallas_call(
+            hand_on_kernel,
+            out_shape=shaped(*trace.shape),
+            in_specs=[whole()],
+            out_specs=whole(),
+            compiler_params=PARAMS,
+            name="hand_on",
+        )(trace)
 
     zero_x = jnp.zeros((2 * size_y, 2 * cells_z), F32)
     zero_y = jnp.zeros((2 * size_x, 2 * cells_z), F32)
@@ -358,48 +431,76 @@
         along_x = between([((k, j), (k + 1, j)) for k, j in here if k + 1 < chips])
         along_y = between([((k, j), (k, j + 1)) for k, j in here if j + 1 < grid_cols])
         inner_x, out_y0 = solve(0, active, trace_x, trace_y0)
-        trace_y0 = lax.ppermute(out_y0, axes, along_y)
+        trace_y0 = hand_on(lax.ppermute(out_y0, axes, along_y))
         out_x, out_y1 = solve(1, active, inner_x, trace_y1)
         trace_x = lax.ppermute(out_x, axes, along_x)
         trace_y1 = lax.ppermute(out_y1, axes, along_y)
         for held, trace in zip(sums, (trace_x, trace_y0, trace_y1)):
             held.append(trace)
 
-    both, edge_x, edge_y = pl.pallas_call(
-        functools.partial(last_kernel, cells_x),
-        out_shape=(
-            shaped(2, 2, 2, size_x, size_y, cells_z),
-            shaped(2, 2, size_y, cells_z),
-            shaped(2, 2, size_x, 2, cells_z),
-        ),
-        in_specs=[whole()] * (5 + len(BEAT)),
-        out_specs=(whole(),) * 3,
-        compiler_params=PARAMS,
-        name="last",
-    )(modes, contrast, *[sum(held) for held in sums], *beat_tables)
+    def solve_last(tile, trace_x, trace_y):
+        return pl.pallas_call(
+            functools.partial(last_kernel, tile),
+            out_shape=(
+                shaped(rows, 2 * cells_z),
+                shaped(rows, 2 * cells_z),
+                shaped(*zero_x.shape),
+                shaped(*zero_y.shape),
+                shaped(*zero_x.shape),
+            ),
+            in_specs=[whole()] * (4 + len(LAST)),
+            out_specs=(whole(),) * 5,
+            compiler_params=PARAMS,
+            cost_estimate=SOLVE_COST,
+            name="last_upper" if tile == 0 else "last_lower",
+        )(modes, contrast, trace_x, trace_y, *[t[name] for name in LAST])
+
+    all_x, all_y0, all_y1 = [sum(held) for held in sums]
+    total0, term0, edge_x, edge_y0, inner_x = solve_last(0, all_x, all_y0)
+    total1, term1, _, edge_y1, _ = solve_last(1, inner_x, all_y1)
 
     every = [(k, j) for k in range(chips) for j in range(grid_cols)]
     after_x = lax.ppermute(edge_x, axes, between([((k, j), (k - 1, j)) for k, j in every if k]))
-    after_y = lax.ppermute(edge_y, axes, between([((k, j), (k, j - 1)) for k, j in every if j]))
+    after_y = lax.ppermute(
+        jnp.stack([edge_y0, edge_y1]), axes, between([((k, j), (k, j - 1)) for k, j in every if j])
+    )
+
     half = shaped(2, 2, size_x, size_y, cells_z)
     keep, give = pl.pallas_call(
-        fix_kernel,
+        functools.partial(finish_kernel, cells_x),
         out_shape=(half, half),
+        in_specs=[scalars()] + [whole()] * (5 + len(FINISH)),
+        out_specs=(whole(), whole()),
+        scratch_shapes=[pltpu.VMEM((2, 2, 2, size_x, size_y, cells_z), F32)],
+        compiler_params=PARAMS,
+        name="finish",
+    )(core_ref, total0, term0, total1, term1, contrast, *[t[name] for name in FINISH])
+    got = lax.ppermute(give, axes, own)
+
+    keep_y = lax.dynamic_index_in_dim(after_y, core, 0, keepdims=False)
+    pass_y = lax.dynamic_index_in_dim(after_y, 1 - core, 0, keepdims=False)
+    got_edge = lax.ppermute(jnp.concatenate([after_x, pass_y], axis=0), axes, own)
+    keep_rest = pl.pallas_call(
+        keep_kernel,
+        out_shape=shaped(*half.shape[1:]),
         in_specs=[scalars()] + [whole()] * 3,
-        out_specs=(whole(), whole()),
+        out_specs=whole(),
         compiler_params=PARAMS,
-        name="fix",
-    )(core_ref, both, after_x, after_y)
-    got = lax.ppermute(give, axes, own)
+        cost_estimate=KEEP_COST,
+        name="keep",
+    )(core_ref, keep, after_x, keep_y)
     return pl.pallas_call(
         place_kernel,
         out_shape=(shaped(*right_side.shape), shaped(*right_side.shape)),
-        in_specs=[scalars(), anywhere(), anywhere()],
+        in_specs=[scalars()] + [whole()] * 4,
         out_specs=(anywhere(), anywhere()),
-        scratch_shapes=[pltpu.SemaphoreType.DMA((4,))],
+        scratch_shapes=[
+            pltpu.VMEM((2, size_x, size_y, cells_z), F32),
+            pltpu.SemaphoreType.DMA((4,)),
+        ],
         compiler_params=PARAMS,
         name="place",
-    )(core_ref, keep, got)
+    )(core_ref, keep, keep_rest, got, got_edge)
 
 
 def solution(mesh):

time: 73.3 us -> 71.5 us (0.975)
  waiting for transfers between devices: 31.5 us -> 26.8 us
  Pallas kernels: 12 us -> 13.4 us
  local copies, waits for them, and re-layouts: 1.79 us -> 2.9 us
    ppermute x6, waiting for transfers between devices: 26.6 us -> 1.34 us  [body(): trace_x = lax.ppermute(out_x, axes, along_x)]
    ppermute x7 -> x8, waiting for transfers between devices: 1.73 us -> 25.5 us  [the longest x6 24.6 us: body(): trace_y0 = hand_on(lax.ppermute(out_y0, axes, along_y))]
    ppermute x7 -> x8, starting transfers between devices: 7.16 us -> 9.04 us  [the longest x6 5.22 us: body(): trace_y0 = hand_on(lax.ppermute(out_y0, axes, along_y))]
    pallas_call x3 -> x12, Pallas kernels: 6.26 us -> 7.84 us  [the longest x2 5.2 us: solve_last(): pl.pallas_call(functools.partial(last_kernel, tile), out_shape=(shaped(ro...]
    ppermute x1, waiting for transfers between devices: 1.54 us -> 0.01 us  [body(): got = lax.ppermute(give, axes, own)]
    ppermute x1, starting transfers between devices: 5.99 us -> 4.49 us  [body(): got = lax.ppermute(give, axes, own)]
    unnamed x22 -> x24, local copies, waits for them, and re-layouts: 0.74 us -> 1.87 us
    ppermute x1, waiting for transfers between devices: 1 us -> 0.01 us  [body(): lax.ppermute(edge_x, axes, between([((k, j), (k - 1, j)) for k, j in ever...]
  transfers between devices with their start and end apart: 22 -> 23, of which waited for: 6 -> 3; matrix products, arithmetic and copies ran while one was open for 0% -> 0% of each run, Pallas kernels for 3% -> 12%
where the time goes in v4:
time: 71.5 us; the launch traced here: 70.1 us
  waiting for transfers between devices  26.8 us (37%)
  starting transfers between devices  25.4 us (36%)
  Pallas kernels  13.4 us (19%)
  local copies, waits for them, and re-layouts  2.9 us (4%)
  between operations  1.48 us (2%)
    ppermute x6, waiting for transfers between devices, body(): trace_y0 = hand_on(lax.ppermute(out_y0, axes, along_y))  24.6 us
    ppermute x6, starting transfers between devices, body(): trace_y1 = lax.ppermute(out_y1, axes, along_y)  5.24 us
    ppermute x6, starting transfers between devices, body(): trace_y0 = hand_on(lax.ppermute(out_y0, axes, along_y))  5.22 us
    pallas_call x2, Pallas kernels, solve_last(): pl.pallas_call(functools.partial(last_kernel, tile), out_shape=(shaped(ro...  5.2 us
    ppermute x6, starting transfers between devices, body(): trace_x = lax.ppermute(out_x, axes, along_x)  4.61 us
    pallas_call x12, Pallas kernels, solve(): pl.pallas_call(functools.partial(beat_kernel, tile), out_shape=(shaped(*z...  4.56 us
    ppermute x1, starting transfers between devices, body(): got = lax.ppermute(give, axes, own)  4.49 us
    ppermute x1, starting transfers between devices, body(): lax.ppermute(jnp.stack([edge_y0, edge_y1]), axes, between([((k, j), (k, j...  1.91 us
  transfers between devices with their start and end apart: 23, of which 3 were waited for; matrix products, arithmetic and copies ran while one was open for 0% of the time, Pallas kernels for 12%

profile of v4, /device:TPU:29, one launch (start us, length us, event | category | flops | bytes accessed | tf_op | source)
XLA Modules:
  0.0 70.1 jit_solution(8012365106569784509)
XLA Ops:
  0.6 0.0 copy-start
  0.7 0.0 copy-start.3
  0.7 1.0 %dynamic-slice_bitcast_fusion = f32[2,16,16,128]{3,2,1,0:T(8,128)S(1)} fusion(f32[2,2,16,16,128]{4,3,2,1,0:T(8,128)} %right_ref.1, s32[]{:T(128)S(6)} %select_n.62), kind=kLoop, calls=%fused_computation.1 | loop fusion | bytes 524292 | tf_op jit(solution)/shard_map/jit(dynamic_index_in_dim)/squeeze | solution.py:367
  1.7 0.0 copy-start.2
  1.7 0.0 copy-start.5
  1.8 0.7 %collective-permute-start = (f32[3,16,16,128]{3,2,1,0:T(8,128)S(1)}, f32[3,16,16,128]{3,2,1,0:T(8,128)S(1)}, u32[]{:S(2)}, u32[]{:S(2)}) collective-permute-start(f32[3,16,16,128]{3,2,1,0:T(8,128)S(1)} %pad_maximum_fusion), channel_id=1, source_target_pairs={{0,4},{4,0},{1,5},{5,1},{2,6},{6,2},{3,7},{7,3},{8,12},{12,8},{9,1... | collective-permute-start | bytes 1179656 | tf_op jit(solution)/shard_map/ppermute | solution.py:368
  2.5 0.7 copy-done.11
  3.3 0.8 %prep.1 = (f32[256,256]{1,0:T(8,128)S(1)}, f32[2,256,128]{2,1,0:T(8,128)S(1)}) custom-call(s32[1]{0:T(128)} %bitcast.core_ref, f32[2,2,16,16,128]{4,3,2,1,0:T(8,128)S(1)} %copy-done.1, f32[16,16,128]{2,1,0:T(8,128)S(1)} %copy-done.4, s32[1,16]{1,0:T(1,128)S(1)} %and_select_fusion.2.place_ref, s32[1,16]{1,0:T(1,128)S(1)} %and_select_fusion.1.depth_ref, ...), custom_call_target="tpu_custom_call" | custom-call | tf_op jit(solution)/shard_map/prep/pallas_call | solution.py:384
  4.1 0.0 copy-start.6
  4.1 0.8 %prep_other.1 = (f32[2,256,256]{2,1,0:T(8,128)S(1)}, f32[2,2,256,128]{3,2,1,0:T(8,128)S(1)}) custom-call(s32[1]{0:T(128)} %bitcast.core_ref, f32[3,16,16,128]{3,2,1,0:T(8,128)S(1)} %collective-permute-done.swap_ref, f32[256,256]{1,0:T(8,128)S(1)} %get-tuple-element.40.own_modes_ref, f32[2,256,128]{2,1,0:T(8,128)S(1)} %get-tuple-element.41.own_contrast_ref, ...), custom_call_target="tpu_custom_call" | custom-call | tf_op jit(solution)/shard_map/prep_other/pallas_call | solution.py:392
  4.9 0.1 copy-done.6
  5.0 0.1 copy-done.7
  5.1 0.0 copy-done.8
  5.2 0.0 copy-done.9
  5.2 0.7 collective-permute-start.2
  5.9 0.7 collective-permute-start.1
  6.5 0.7 collective-permute-start.3
  7.3 0.7 collective-permute-start.5
  8.0 0.7 collective-permute-start.4
  8.6 0.7 collective-permute-start.6
  9.4 0.7 collective-permute-start.8
  10.1 0.7 collective-permute-start.7
  10.8 0.7 collective-permute-start.9
  11.5 0.7 collective-permute-start.11
  12.2 0.2 lower.9
  12.4 0.7 collective-permute-start.10
  13.0 0.7 collective-permute-start.12
  13.8 1.3 %collective-permute-start.14 = (f32[32,256]{1,0:T(8,128)S(1)}, f32[32,256]{1,0:T(8,128)S(1)}, u32[]{:S(2)}, u32[]{:S(2)}) collective-permute-start(f32[32,256]{1,0:T(8,128)S(1)} %get-tuple-element.62), channel_id=1, source_target_pairs={{18,19},{22,23},{25,26},{29,30}} | collective-permute-start | bytes 98312 | tf_op jit(solution)/shard_map/ppermute | solution.py:434
  15.1 1.3 %collective-permute-start.13 = (f32[32,256]{1,0:T(8,128)S(1)}, f32[32,256]{1,0:T(8,128)S(1)}, u32[]{:S(2)}, u32[]{:S(2)}) collective-permute-start(f32[32,256]{1,0:T(8,128)S(1)} %get-tuple-element.61), channel_id=1, source_target_pairs={{11,19},{15,23},{18,26},{22,30}} | collective-permute-start | bytes 98312 | tf_op jit(solution)/shard_map/ppermute | solution.py:436
  16.4 1.3 %collective-permute-start.15 = (f32[32,256]{1,0:T(8,128)S(1)}, f32[32,256]{1,0:T(8,128)S(1)}, u32[]{:S(2)}, u32[]{:S(2)}) collective-permute-start(f32[32,256]{1,0:T(8,128)S(1)} %get-tuple-element.64), channel_id=1, source_target_pairs={{18,19},{22,23},{25,26},{29,30}} | collective-permute-start | bytes 98312 | tf_op jit(solution)/shard_map/ppermute | solution.py:437
  17.7 24.6 %collective-permute-done.14.in_ref = f32[32,256]{1,0:T(8,128)S(1)} collective-permute-done((f32[32,256]{1,0:T(8,128)S(1)}, f32[32,256]{1,0:T(8,128)S(1)}, u32[]{:S(2)}, u32[]{:S(2)}) %collective-permute-start.14) | collective-permute-done | bytes 32800 | tf_op jit(solution)/shard_map/ppermute | solution.py:434
  42.3 1.3 %collective-permute-done.13.trace_x_ref = f32[32,256]{1,0:T(8,128)S(1)} collective-permute-done((f32[32,256]{1,0:T(8,128)S(1)}, f32[32,256]{1,0:T(8,128)S(1)}, u32[]{:S(2)}, u32[]{:S(2)}) %collective-permute-start.13) | collective-permute-done | bytes 32800 | tf_op jit(solution)/shard_map/ppermute | solution.py:436
  43.6 2.1 %upper.11 = (f32[32,256]{1,0:T(8,128)S(1)}, f32[32,256]{1,0:T(8,128)S(1)}) custom-call(s32[1]{0:T(128)} %bitcast.12.active_ref, f32[2,256,256]{2,1,0:T(8,128)S(1)} %get-tuple-element.42.modes_ref, f32[2,2,256,128]{3,2,1,0:T(8,128)S(1)} %get-tuple-element.43.contrast_ref, f32[32,256]{1,0:T(8,128)S(1)} %collective-permute-done.13.trace_x_ref, ...), custom_call_target="tpu_custom_call" | custom-call | flops 2000000000 | bytes 2000000 | tf_op jit(solution)/shard_map/upper/pallas_call | solution.py:404
  45.8 1.3 %collective-permute-start.17 = (f32[32,256]{1,0:T(8,128)S(1)}, f32[32,256]{1,0:T(8,128)S(1)}, u32[]{:S(2)}, u32[]{:S(2)}) collective-permute-start(f32[32,256]{1,0:T(8,128)S(1)} %get-tuple-element.66), channel_id=1, source_target_pairs={{26,27},{30,31}} | collective-permute-start | bytes 98312 | tf_op jit(solution)/shard_map/ppermute | solution.py:434
  47.1 2.1 %lower.11 = (f32[32,256]{1,0:T(8,128)S(1)}, f32[32,256]{1,0:T(8,128)S(1)}) custom-call(s32[1]{0:T(128)} %bitcast.12.active_ref, f32[2,256,256]{2,1,0:T(8,128)S(1)} %get-tuple-element.42.modes_ref, f32[2,2,256,128]{3,2,1,0:T(8,128)S(1)} %get-tuple-element.43.contrast_ref, f32[32,256]{1,0:T(8,128)S(1)} %get-tuple-element.63.trace_x_ref, ...), custom_call_target="tpu_custom_call" | custom-call | flops 2000000000 | bytes 2000000 | tf_op jit(solution)/shard_map/lower/pallas_call | solution.py:404
  49.2 0.7 collective-permute-start.16
  49.9 1.3 %collective-permute-start.18 = (f32[32,256]{1,0:T(8,128)S(1)}, f32[32,256]{1,0:T(8,128)S(1)}, u32[]{:S(2)}, u32[]{:S(2)}) collective-permute-start(f32[32,256]{1,0:T(8,128)S(1)} %get-tuple-element.70), channel_id=1, source_target_pairs={{26,27},{30,31}} | collective-permute-start | bytes 98312 | tf_op jit(solution)/shard_map/ppermute | solution.py:437
  51.3 0.9 %copy-done.10 = bf16[128,512]{1,0:T(8,128)(2,1)S(1)} copy-done((bf16[128,512]{1,0:T(8,128)(2,1)S(1)}, bf16[128,512]{1,0:T(8,128)(2,1)}, u32[]{:S(2)}) %copy-start.10) | copy-done | bytes 131096
  52.1 2.3 %last_upper.1 = (f32[256,256]{1,0:T(8,128)S(1)}, f32[256,256]{1,0:T(8,128)S(1)}, f32[32,256]{1,0:T(8,128)S(1)}, f32[32,256]{1,0:T(8,128)S(1)}, f32[32,256]{1,0:T(8,128)S(1)}) custom-call(f32[2,256,256]{2,1,0:T(8,128)S(1)} %get-tuple-element.42.modes_ref, f32[2,2,256,128]{3,2,1,0:T(8,128)S(1)} %get-tuple-element.43.contrast_ref, ...), custom_call_target="tpu_custom_call" | custom-call | flops 2000000000 | bytes 2000000 | tf_op jit(solution)/shard_map/last_upper/pallas_call | solution.py:442
  54.5 2.9 %last_lower.1 = (f32[256,256]{1,0:T(8,128)S(1)}, f32[256,256]{1,0:T(8,128)S(1)}, f32[32,256]{1,0:T(8,128)}, f32[32,256]{1,0:T(8,128)S(1)}, f32[32,256]{1,0:T(8,128)}) custom-call(f32[2,256,256]{2,1,0:T(8,128)S(1)} %get-tuple-element.42.modes_ref, f32[2,2,256,128]{3,2,1,0:T(8,128)S(1)} %get-tuple-element.43.contrast_ref, ...), custom_call_target="tpu_custom_call" | custom-call | flops 2000000000 | bytes 2000000 | tf_op jit(solution)/shard_map/last_lower/pallas_call | solution.py:442
  57.4 1.9 %collective-permute-start.20 = (f32[2,32,256]{2,1,0:T(8,128)S(1)}, f32[2,32,256]{2,1,0:T(8,128)S(1)}, u32[]{:S(2)}, u32[]{:S(2)}) collective-permute-start(f32[2,32,256]{2,1,0:T(8,128)S(1)} %pad_maximum_fusion.1), channel_id=1, source_target_pairs={{1,0},{5,4},{2,1},{6,5},{3,2},{7,6},{9,8},{13,12},{10,9},{14,13},{... | collective-permute-start | bytes 196616 | tf_op jit(solution)/shard_map/ppermute | solution.py:464
  59.3 1.3 %collective-permute-start.19 = (f32[32,256]{1,0:T(8,128)S(1)}, f32[32,256]{1,0:T(8,128)S(1)}, u32[]{:S(2)}, u32[]{:S(2)}) collective-permute-start(f32[32,256]{1,0:T(8,128)S(1)} %get-tuple-element.74), channel_id=1, source_target_pairs={{8,0},{12,4},{9,1},{13,5},{10,2},{14,6},{11,3},{15,7},{16,8},{20,1... | collective-permute-start | bytes 98312 | tf_op jit(solution)/shard_map/ppermute | solution.py:463
  60.6 1.0 %finish.1 = (f32[2,2,16,16,128]{4,3,2,1,0:T(8,128)S(1)}, f32[2,2,16,16,128]{4,3,2,1,0:T(8,128)S(1)}) custom-call(s32[1]{0:T(128)} %bitcast.core_ref, f32[256,256]{1,0:T(8,128)S(1)} %get-tuple-element.67.total0_ref, f32[256,256]{1,0:T(8,128)S(1)} %get-tuple-element.68.term0_ref, f32[256,256]{1,0:T(8,128)S(1)} %get-tuple-element.71.total1_ref, ...), custom_call_target="tpu_custom_call" | custom-call | tf_op jit(solution)/shard_map/finish/pallas_call | solution.py:469
  61.6 4.5 %collective-permute-start.21 = (f32[2,2,16,16,128]{4,3,2,1,0:T(8,128)S(1)}, f32[2,2,16,16,128]{4,3,2,1,0:T(8,128)S(1)}, u32[]{:S(2)}, u32[]{:S(2)}) collective-permute-start(f32[2,2,16,16,128]{4,3,2,1,0:T(8,128)S(1)} %get-tuple-element.77), channel_id=1, source_target_pairs={{0,4},{4,0},{1,5},{5,1},{2,6},{6,2},{3,7},{7,3},{8,12},{12,8},{9,1... | collective-permute-start | bytes 1572872 | tf_op jit(solution)/shard_map/ppermute | solution.py:478
  66.2 1.9 %collective-permute-start.22 = (f32[64,256]{1,0:T(8,128)S(1)}, f32[64,256]{1,0:T(8,128)S(1)}, u32[]{:S(2)}, u32[]{:S(2)}) collective-permute-start(f32[64,256]{1,0:T(8,128)S(1)} %pad_maximum_fusion.2), channel_id=1, source_target_pairs={{0,4},{4,0},{1,5},{5,1},{2,6},{6,2},{3,7},{7,3},{8,12},{12,8},{9,1... | collective-permute-start | bytes 196616 | tf_op jit(solution)/shard_map/ppermute | solution.py:482
  68.1 0.1 keep.1.keep_rest_ref
  68.1 0.8 %collective-permute-done.22.got_edge_ref = f32[64,256]{1,0:T(8,128)S(1)} collective-permute-done((f32[64,256]{1,0:T(8,128)S(1)}, f32[64,256]{1,0:T(8,128)S(1)}, u32[]{:S(2)}, u32[]{:S(2)}) %collective-permute-start.22) | collective-permute-done | bytes 65568 | tf_op jit(solution)/shard_map/ppermute | solution.py:482
  69.0 1.0 %place.1 = (f32[2,2,16,16,128]{4,3,2,1,0:T(8,128)}, f32[2,2,16,16,128]{4,3,2,1,0:T(8,128)}) custom-call(s32[1]{0:T(128)} %bitcast.core_ref, f32[2,2,16,16,128]{4,3,2,1,0:T(8,128)S(1)} %get-tuple-element.73.keep_ref, f32[2,16,16,128]{3,2,1,0:T(8,128)S(1)} %keep.1.keep_rest_ref, f32[2,2,16,16,128]{4,3,2,1,0:T(8,128)S(1)} %collective-permute-done.21.got_ref, ...), custom_call_target="tpu_custom_call" | custom-call | tf_op jit(solution)/shard_map/place/pallas_call | solution.py:492
  (60 shorter events, 0.4 us)
Async XLA Ops:
  0.6 1.9 %copy-start = (f32[2,16,2]{1,2,0:T(2,128)S(1)}, f32[2,16,2]{1,2,0:T(2,128)}, u32[]{:S(2)}) copy-start(f32[2,16,2]{1,2,0:T(2,128)} %param.15) | copy-start | bytes 772
  0.7 1.1 %copy-start.4 = (f32[16,16,128]{2,1,0:T(8,128)S(1)}, f32[16,16,128]{2,1,0:T(8,128)}, u32[]{:S(2)}) copy-start(f32[16,16,128]{2,1,0:T(8,128)} %slow_ref.1) | copy-start | bytes 393220
  0.7 2.6 %copy-start.3 = (bf16[2,256,256]{2,1,0:T(8,128)(2,1)S(1)}, bf16[2,256,256]{2,1,0:T(8,128)(2,1)}, u32[]{:S(2)}) copy-start(bf16[2,256,256]{2,1,0:T(8,128)(2,1)} %constant.147.clone.forward_ref.refs_1_) | copy-start | bytes 786436
  1.7 1.6 %copy-start.1 = (f32[2,2,16,16,128]{4,3,2,1,0:T(8,128)S(1)}, f32[2,2,16,16,128]{4,3,2,1,0:T(8,128)}, u32[]{:S(2)}) copy-start(f32[2,2,16,16,128]{4,3,2,1,0:T(8,128)} %right_ref.1) | copy-start | bytes 1572868
  1.7 1.6 %copy-start.2 = (bf16[256,256]{1,0:T(8,128)(2,1)S(1)}, bf16[256,256]{1,0:T(8,128)(2,1)}, u32[]{:S(2)}) copy-start(bf16[256,256]{1,0:T(8,128)(2,1)} %constant.149.clone.z_ref.refs_3_) | copy-start | bytes 393220
  1.7 1.6 %copy-start.5 = (f32[256,1]{1,0:T(8,128)S(1)}, f32[256,1]{1,0:T(8,128)}, u32[]{:S(2)}) copy-start(f32[256,1]{1,0:T(8,128)} %constant.153.clone.edge_ref) | copy-start | bytes 3076
  1.8 2.3 %collective-permute-start = (f32[3,16,16,128]{3,2,1,0:T(8,128)S(1)}, f32[3,16,16,128]{3,2,1,0:T(8,128)S(1)}, u32[]{:S(2)}, u32[]{:S(2)}) collective-permute-start(f32[3,16,16,128]{3,2,1,0:T(8,128)S(1)} %pad_maximum_fusion), channel_id=1, source_target_pairs={{0,4},{4,0},{1,5},{5,1},{2,6},{6,2},{3,7},{7,3},{8,12},{12,8},{9,1... | collective-permute-start | bytes 1179656 | tf_op jit(solution)/shard_map/ppermute | solution.py:368
  2.5 0.7 copy-start.11
  4.1 1.0 %copy-start.6 = (bf16[2,256,256]{2,1,0:T(8,128)(2,1)S(1)}, bf16[2,256,256]{2,1,0:T(8,128)(2,1)}, u32[]{:S(2)}) copy-start(bf16[2,256,256]{2,1,0:T(8,128)(2,1)} %constant.148.clone.refs_2_.backward_ref) | copy-start | bytes 786436
  4.1 1.0 %copy-start.7 = (f32[2,256,128]{2,1,0:T(8,128)S(1)}, f32[2,256,128]{2,1,0:T(8,128)}, u32[]{:S(2)}) copy-start(f32[2,256,128]{2,1,0:T(8,128)} %constant.146.clone.refs_0_) | copy-start | bytes 786436
  4.1 1.0 %copy-start.8 = (bf16[128,512]{1,0:T(8,128)(2,1)S(1)}, bf16[128,512]{1,0:T(8,128)(2,1)}, u32[]{:S(2)}) copy-start(bf16[128,512]{1,0:T(8,128)(2,1)} %constant.151.clone.refs_5_) | copy-start | bytes 393220
  4.1 1.1 %copy-start.9 = (bf16[512,128]{1,0:T(8,128)(2,1)S(1)}, bf16[512,128]{1,0:T(8,128)(2,1)}, u32[]{:S(2)}) copy-start(bf16[512,128]{1,0:T(8,128)(2,1)} %constant.150.clone.refs_4_) | copy-start | bytes 393220
  5.2 2.0 %collective-permute-start.2 = (f32[32,256]{1,0:T(8,128)S(1)}, f32[32,256]{1,0:T(8,128)S(1)}, u32[]{:S(2)}, u32[]{:S(2)}) collective-permute-start(f32[32,256]{1,0:T(8,128)S(1)} %get-tuple-element.46), channel_id=1, source_target_pairs={{0,1},{4,5}} | collective-permute-start | bytes 98312 | tf_op jit(solution)/shard_map/ppermute | solution.py:434
  5.9 1.4 %collective-permute-start.1 = (f32[32,256]{1,0:T(8,128)S(1)}, f32[32,256]{1,0:T(8,128)S(1)}, u32[]{:S(2)}, u32[]{:S(2)}) collective-permute-start(f32[32,256]{1,0:T(8,128)S(1)} %get-tuple-element.45), channel_id=1, source_target_pairs={{0,8},{4,12}} | collective-permute-start | bytes 98312 | tf_op jit(solution)/shard_map/ppermute | solution.py:436
  6.5 1.4 %collective-permute-start.3 = (f32[32,256]{1,0:T(8,128)S(1)}, f32[32,256]{1,0:T(8,128)S(1)}, u32[]{:S(2)}, u32[]{:S(2)}) collective-permute-start(f32[32,256]{1,0:T(8,128)S(1)} %get-tuple-element.48), channel_id=1, source_target_pairs={{0,1},{4,5}} | collective-permute-start | bytes 98312 | tf_op jit(solution)/shard_map/ppermute | solution.py:437
  7.3 2.1 %collective-permute-start.5 = (f32[32,256]{1,0:T(8,128)S(1)}, f32[32,256]{1,0:T(8,128)S(1)}, u32[]{:S(2)}, u32[]{:S(2)}) collective-permute-start(f32[32,256]{1,0:T(8,128)S(1)} %get-tuple-element.50), channel_id=1, source_target_pairs={{1,2},{5,6},{8,9},{12,13}} | collective-permute-start | bytes 98312 | tf_op jit(solution)/shard_map/ppermute | solution.py:434
  8.0 1.4 %collective-permute-start.4 = (f32[32,256]{1,0:T(8,128)S(1)}, f32[32,256]{1,0:T(8,128)S(1)}, u32[]{:S(2)}, u32[]{:S(2)}) collective-permute-start(f32[32,256]{1,0:T(8,128)S(1)} %get-tuple-element.49), channel_id=1, source_target_pairs={{1,9},{5,13},{8,16},{12,20}} | collective-permute-start | bytes 98312 | tf_op jit(solution)/shard_map/ppermute | solution.py:436
  8.6 1.4 %collective-permute-start.6 = (f32[32,256]{1,0:T(8,128)S(1)}, f32[32,256]{1,0:T(8,128)S(1)}, u32[]{:S(2)}, u32[]{:S(2)}) collective-permute-start(f32[32,256]{1,0:T(8,128)S(1)} %get-tuple-element.52), channel_id=1, source_target_pairs={{1,2},{5,6},{8,9},{12,13}} | collective-permute-start | bytes 98312 | tf_op jit(solution)/shard_map/ppermute | solution.py:437
  9.4 2.1 %collective-permute-start.8 = (f32[32,256]{1,0:T(8,128)S(1)}, f32[32,256]{1,0:T(8,128)S(1)}, u32[]{:S(2)}, u32[]{:S(2)}) collective-permute-start(f32[32,256]{1,0:T(8,128)S(1)} %get-tuple-element.54), channel_id=1, source_target_pairs={{2,3},{6,7},{9,10},{13,14},{16,17},{20,21}} | collective-permute-start | bytes 98312 | tf_op jit(solution)/shard_map/ppermute | solution.py:434
  10.1 1.4 %collective-permute-start.7 = (f32[32,256]{1,0:T(8,128)S(1)}, f32[32,256]{1,0:T(8,128)S(1)}, u32[]{:S(2)}, u32[]{:S(2)}) collective-permute-start(f32[32,256]{1,0:T(8,128)S(1)} %get-tuple-element.53), channel_id=1, source_target_pairs={{2,10},{6,14},{9,17},{13,21},{16,24},{20,28}} | collective-permute-start | bytes 98312 | tf_op jit(solution)/shard_map/ppermute | solution.py:436
  10.8 1.4 %collective-permute-start.9 = (f32[32,256]{1,0:T(8,128)S(1)}, f32[32,256]{1,0:T(8,128)S(1)}, u32[]{:S(2)}, u32[]{:S(2)}) collective-permute-start(f32[32,256]{1,0:T(8,128)S(1)} %get-tuple-element.56), channel_id=1, source_target_pairs={{2,3},{6,7},{9,10},{13,14},{16,17},{20,21}} | collective-permute-start | bytes 98312 | tf_op jit(solution)/shard_map/ppermute | solution.py:437
  11.5 2.2 %collective-permute-start.11 = (f32[32,256]{1,0:T(8,128)S(1)}, f32[32,256]{1,0:T(8,128)S(1)}, u32[]{:S(2)}, u32[]{:S(2)}) collective-permute-start(f32[32,256]{1,0:T(8,128)S(1)} %get-tuple-element.58), channel_id=1, source_target_pairs={{10,11},{14,15},{17,18},{21,22},{24,25},{28,29}} | collective-permute-start | bytes 98312 | tf_op jit(solution)/shard_map/ppermute | solution.py:434
  12.4 1.4 %collective-permute-start.10 = (f32[32,256]{1,0:T(8,128)S(1)}, f32[32,256]{1,0:T(8,128)S(1)}, u32[]{:S(2)}, u32[]{:S(2)}) collective-permute-start(f32[32,256]{1,0:T(8,128)S(1)} %get-tuple-element.57), channel_id=1, source_target_pairs={{3,11},{7,15},{10,18},{14,22},{17,25},{21,29}} | collective-permute-start | bytes 98312 | tf_op jit(solution)/shard_map/ppermute | solution.py:436
  13.0 2.0 %collective-permute-start.12 = (f32[32,256]{1,0:T(8,128)S(1)}, f32[32,256]{1,0:T(8,128)S(1)}, u32[]{:S(2)}, u32[]{:S(2)}) collective-permute-start(f32[32,256]{1,0:T(8,128)S(1)} %get-tuple-element.60), channel_id=1, source_target_pairs={{10,11},{14,15},{17,18},{21,22},{24,25},{28,29}} | collective-permute-start | bytes 98312 | tf_op jit(solution)/shard_map/ppermute | solution.py:437
  13.8 28.5 %collective-permute-start.14 = (f32[32,256]{1,0:T(8,128)S(1)}, f32[32,256]{1,0:T(8,128)S(1)}, u32[]{:S(2)}, u32[]{:S(2)}) collective-permute-start(f32[32,256]{1,0:T(8,128)S(1)} %get-tuple-element.62), channel_id=1, source_target_pairs={{18,19},{22,23},{25,26},{29,30}} | collective-permute-start | bytes 98312 | tf_op jit(solution)/shard_map/ppermute | solution.py:434
  15.1 28.5 %collective-permute-start.13 = (f32[32,256]{1,0:T(8,128)S(1)}, f32[32,256]{1,0:T(8,128)S(1)}, u32[]{:S(2)}, u32[]{:S(2)}) collective-permute-start(f32[32,256]{1,0:T(8,128)S(1)} %get-tuple-element.61), channel_id=1, source_target_pairs={{11,19},{15,23},{18,26},{22,30}} | collective-permute-start | bytes 98312 | tf_op jit(solution)/shard_map/ppermute | solution.py:436
  16.4 30.7 %collective-permute-start.15 = (f32[32,256]{1,0:T(8,128)S(1)}, f32[32,256]{1,0:T(8,128)S(1)}, u32[]{:S(2)}, u32[]{:S(2)}) collective-permute-start(f32[32,256]{1,0:T(8,128)S(1)} %get-tuple-element.64), channel_id=1, source_target_pairs={{18,19},{22,23},{25,26},{29,30}} | collective-permute-start | bytes 98312 | tf_op jit(solution)/shard_map/ppermute | solution.py:437
  45.8 5.4 %collective-permute-start.17 = (f32[32,256]{1,0:T(8,128)S(1)}, f32[32,256]{1,0:T(8,128)S(1)}, u32[]{:S(2)}, u32[]{:S(2)}) collective-permute-start(f32[32,256]{1,0:T(8,128)S(1)} %get-tuple-element.66), channel_id=1, source_target_pairs={{26,27},{30,31}} | collective-permute-start | bytes 98312 | tf_op jit(solution)/shard_map/ppermute | solution.py:434
  49.2 2.0 %collective-permute-start.16 = (f32[32,256]{1,0:T(8,128)S(1)}, f32[32,256]{1,0:T(8,128)S(1)}, u32[]{:S(2)}, u32[]{:S(2)}) collective-permute-start(f32[32,256]{1,0:T(8,128)S(1)} %get-tuple-element.65), channel_id=1, source_target_pairs={{19,27},{23,31}} | collective-permute-start | bytes 98312 | tf_op jit(solution)/shard_map/ppermute | solution.py:436
  49.9 4.6 %collective-permute-start.18 = (f32[32,256]{1,0:T(8,128)S(1)}, f32[32,256]{1,0:T(8,128)S(1)}, u32[]{:S(2)}, u32[]{:S(2)}) collective-permute-start(f32[32,256]{1,0:T(8,128)S(1)} %get-tuple-element.70), channel_id=1, source_target_pairs={{26,27},{30,31}} | collective-permute-start | bytes 98312 | tf_op jit(solution)/shard_map/ppermute | solution.py:437
  51.2 0.9 %copy-start.10 = (bf16[128,512]{1,0:T(8,128)(2,1)S(1)}, bf16[128,512]{1,0:T(8,128)(2,1)}, u32[]{:S(2)}) copy-start(bf16[128,512]{1,0:T(8,128)(2,1)} %constant.152.clone.refs_6_) | copy-start | bytes 393220
  57.4 8.7 %collective-permute-start.20 = (f32[2,32,256]{2,1,0:T(8,128)S(1)}, f32[2,32,256]{2,1,0:T(8,128)S(1)}, u32[]{:S(2)}, u32[]{:S(2)}) collective-permute-start(f32[2,32,256]{2,1,0:T(8,128)S(1)} %pad_maximum_fusion.1), channel_id=1, source_target_pairs={{1,0},{5,4},{2,1},{6,5},{3,2},{7,6},{9,8},{13,12},{10,9},{14,13},{... | collective-permute-start | bytes 196616 | tf_op jit(solution)/shard_map/ppermute | solution.py:464
  59.3 6.8 %collective-permute-start.19 = (f32[32,256]{1,0:T(8,128)S(1)}, f32[32,256]{1,0:T(8,128)S(1)}, u32[]{:S(2)}, u32[]{:S(2)}) collective-permute-start(f32[32,256]{1,0:T(8,128)S(1)} %get-tuple-element.74), channel_id=1, source_target_pairs={{8,0},{12,4},{9,1},{13,5},{10,2},{14,6},{11,3},{15,7},{16,8},{20,1... | collective-permute-start | bytes 98312 | tf_op jit(solution)/shard_map/ppermute | solution.py:463
  61.6 7.3 %collective-permute-start.21 = (f32[2,2,16,16,128]{4,3,2,1,0:T(8,128)S(1)}, f32[2,2,16,16,128]{4,3,2,1,0:T(8,128)S(1)}, u32[]{:S(2)}, u32[]{:S(2)}) collective-permute-start(f32[2,2,16,16,128]{4,3,2,1,0:T(8,128)S(1)} %get-tuple-element.77), channel_id=1, source_target_pairs={{0,4},{4,0},{1,5},{5,1},{2,6},{6,2},{3,7},{7,3},{8,12},{12,8},{9,1... | collective-permute-start | bytes 1572872 | tf_op jit(solution)/shard_map/ppermute | solution.py:478
  66.2 2.8 %collective-permute-start.22 = (f32[64,256]{1,0:T(8,128)S(1)}, f32[64,256]{1,0:T(8,128)S(1)}, u32[]{:S(2)}, u32[]{:S(2)}) collective-permute-start(f32[64,256]{1,0:T(8,128)S(1)} %pad_maximum_fusion.2), channel_id=1, source_target_pairs={{0,4},{4,0},{1,5},{5,1},{2,6},{6,2},{3,7},{7,3},{8,12},{12,8},{9,1... | collective-permute-start | bytes 196616 | tf_op jit(solution)/shard_map/ppermute | solution.py:482

commit v5 on v4

--- a/solution.py
+++ b/solution.py
@@ -205,15 +205,16 @@
     )
 
 
-def prep_other_kernel(cells_x, core_ref, swap_ref, own_modes_ref, own_contrast_ref, place_ref, depth_ref,
+def prep_other_kernel(cells_x, core_ref, swap_ref, slow_ref, own_modes_ref, own_contrast_ref, place_ref, depth_ref,
                       amp_ref, edge_ref, forward_ref, z_ref, modes_ref, contrast_ref):
     core = core_ref[0]
     other = 1 - core
     modes_ref[core] = own_modes_ref[...]
     contrast_ref[core] = own_contrast_ref[...]
-    parts = [jnp.concatenate([swap_ref[c, x] for x in cells_x], axis=0) for c in range(3)]
+    dense = [jnp.concatenate([swap_ref[core, c, x] for x in cells_x], axis=0) for c in range(2)]
+    slow = jnp.concatenate([slow_ref[x] for x in cells_x], axis=0)
     prepare(
-        jnp.concatenate(parts[:2], axis=1), parts[2], place_ref[...], depth_ref[...], amp_ref,
+        jnp.concatenate(dense, axis=1), slow, place_ref[...], depth_ref[...], amp_ref,
         edge_ref[...], forward_ref, z_ref[...], modes_ref.at[other], contrast_ref.at[other],
     )
 
@@ -222,39 +223,39 @@
     return modes + left_product(enter, jnp.concatenate([trace_x, trace_y], axis=0))
 
 
-def beat_kernel(tile, active_ref, modes_ref, contrast_ref, trace_x_ref, trace_y_ref, *refs):
+def beat_kernel(tile, active_ref, modes_ref, contrast_ref, trace_x_ref, trace_y_ref, total_ref, term_ref, *refs):
     t = {name: ref for name, ref in zip(BEAT, refs)}
-    out_x_ref, out_y_ref = refs[len(BEAT) :]
+    out_x_ref, out_y_ref, new_total_ref, new_term_ref = refs[len(BEAT) :]
 
     @pl.when(active_ref[0] == 1)
     def _():
         local = dict(t, right_z=t["right_z"][...])
         source = source_modes(modes_ref[tile], trace_x_ref[...], trace_y_ref[...], t["enter"][...])
-        total, _ = solve_modes(source, contrast_ref.at[tile], local)
+        total, term = solve_modes(source, contrast_ref.at[tile], local)
+        new_total_ref[...] = total
+        new_term_ref[...] = term
         out = left_product(t["leave"][...], total)
         count = out_x_ref.shape[0]
         out_x_ref[...] = out[:count]
         out_y_ref[...] = out[count:]
 
-
-LAST = BEAT + ("first",)
+    @pl.when(active_ref[0] == 0)
+    def _():
+        new_total_ref[...] = total_ref[...]
+        new_term_ref[...] = term_ref[...]
+
+
+def edge_kernel(total0_ref, total1_ref, first_ref, z_ref, edge_x_ref, edge_y_ref):
+    count = edge_x_ref.shape[0]
+    right_z = z_ref[...]
+    for tile, total_ref in enumerate((total0_ref, total1_ref)):
+        edges = z_transform(left_product(first_ref[...], total_ref[...]), right_z)
+        edge_y_ref[tile] = edges[count:]
+        if tile == 0:
+            edge_x_ref[...] = edges[:count]
+
+
 FINISH = ("backward", "right_z")
-
-
-def last_kernel(tile, modes_ref, contrast_ref, trace_x_ref, trace_y_ref, *refs):
-    t = {name: ref for name, ref in zip(LAST, refs)}
-    total_ref, term_ref, edge_x_ref, edge_y_ref, out_x_ref = refs[len(LAST) :]
-    local = dict(t, right_z=t["right_z"][...])
-    count = trace_x_ref.shape[0]
-    source = source_modes(modes_ref[tile], trace_x_ref[...], trace_y_ref[...], t["enter"][...])
-    total, term = solve_modes(source, contrast_ref.at[tile], local)
-    total_ref[...] = total
-    term_ref[...] = term
-    edges = z_transform(left_product(t["first"][...], total), local["right_z"])
-    edge_x_ref[...] = edges[:count]
-    edge_y_ref[...] = edges[count:]
-    if tile == 0:
-        out_x_ref[...] = left_product(t["leave"][...], total)[:count]
 
 
 def finish_kernel(cells_x, core_ref, total0_ref, term0_ref, total1_ref, term1_ref, contrast_ref, backward_ref,
@@ -364,8 +365,8 @@
         for k in range(chips) for j in range(grid_cols) for r in range(2)
     ]
     axes = ("gx", "gy")
-    other = lax.dynamic_index_in_dim(right_side, 1 - core, 0, keepdims=False)
-    swapped = lax.ppermute(jnp.concatenate([other, slowness[None]], axis=0), axes, own)
+    swapped = lax.ppermute(right_side, axes, own)
+    swapped_slow = lax.ppermute(slowness, axes, own)
 
     total_y = size_y * grid_cols
     cells = lax.dynamic_index_in_dim(source_cells, core, 0, keepdims=True)
@@ -392,24 +393,26 @@
     modes, contrast = pl.pallas_call(
         functools.partial(prep_other_kernel, cells_x),
         out_shape=(shaped(2, rows, 2 * cells_z), shaped(2, 2, rows, cells_z)),
-        in_specs=[scalars()] + [whole()] * 9,
+        in_specs=[scalars()] + [whole()] * 10,
         out_specs=(whole(), whole()),
         compiler_params=PARAMS,
         name="prep_other",
-    )(core_ref, swapped, own_modes, own_contrast, places[1], depth, amplitudes, *prep_tables)
+    )(core_ref, swapped, swapped_slow, own_modes, own_contrast, places[1], depth, amplitudes, *prep_tables)
 
     beat_tables = [t[name] for name in BEAT]
 
-    def solve(tile, active, trace_x, trace_y):
-        return pl.pallas_call(
+    def solve(tile, active, trace_x, trace_y, state):
+        out_x, out_y, *state = pl.pallas_call(
             functools.partial(beat_kernel, tile),
-            out_shape=(shaped(*zero_x.shape), shaped(*zero_y.shape)),
-            in_specs=[scalars()] + [whole()] * (4 + len(BEAT)),
-            out_specs=(whole(), whole()),
+            out_shape=(shaped(*zero_x.shape), shaped(*zero_y.shape)) + (shaped(rows, 2 * cells_z),) * 2,
+            in_specs=[scalars()] + [whole()] * (6 + len(BEAT)),
+            out_specs=(whole(),) * 4,
+            input_output_aliases={5: 2, 6: 3},
             compiler_params=PARAMS,
             cost_estimate=SOLVE_COST,
             name="upper" if tile == 0 else "lower",
-        )(active, modes, contrast, trace_x, trace_y, *beat_tables)
+        )(active, modes, contrast, trace_x, trace_y, *state, *beat_tables)
+        return out_x, out_y, state
 
     def hand_on(trace):
         return pl.pallas_call(
@@ -424,46 +427,33 @@
     zero_x = jnp.zeros((2 * size_y, 2 * cells_z), F32)
     zero_y = jnp.zeros((2 * size_x, 2 * cells_z), F32)
     trace_x, trace_y0, trace_y1 = zero_x, zero_y, zero_y
-    sums = ([], [], [])
-    for beat in range(chips + grid_cols - 2):
+    states = [[jnp.zeros((rows, 2 * cells_z), F32)] * 2 for _ in range(2)]
+    for beat in range(chips + grid_cols - 1):
         active = (row // 2 + col == beat).astype(jnp.int32)[None]
         here = [(k, beat - k) for k in range(chips) if 0 <= beat - k < grid_cols]
         along_x = between([((k, j), (k + 1, j)) for k, j in here if k + 1 < chips])
         along_y = between([((k, j), (k, j + 1)) for k, j in here if j + 1 < grid_cols])
-        inner_x, out_y0 = solve(0, active, trace_x, trace_y0)
-        trace_y0 = hand_on(lax.ppermute(out_y0, axes, along_y))
-        out_x, out_y1 = solve(1, active, inner_x, trace_y1)
-        trace_x = lax.ppermute(out_x, axes, along_x)
-        trace_y1 = lax.ppermute(out_y1, axes, along_y)
-        for held, trace in zip(sums, (trace_x, trace_y0, trace_y1)):
-            held.append(trace)
-
-    def solve_last(tile, trace_x, trace_y):
-        return pl.pallas_call(
-            functools.partial(last_kernel, tile),
-            out_shape=(
-                shaped(rows, 2 * cells_z),
-                shaped(rows, 2 * cells_z),
-                shaped(*zero_x.shape),
-                shaped(*zero_y.shape),
-                shaped(*zero_x.shape),
-            ),
-            in_specs=[whole()] * (4 + len(LAST)),
-            out_specs=(whole(),) * 5,
-            compiler_params=PARAMS,
-            cost_estimate=SOLVE_COST,
-            name="last_upper" if tile == 0 else "last_lower",
-        )(modes, contrast, trace_x, trace_y, *[t[name] for name in LAST])
-
-    all_x, all_y0, all_y1 = [sum(held) for held in sums]
-    total0, term0, edge_x, edge_y0, inner_x = solve_last(0, all_x, all_y0)
-    total1, term1, _, edge_y1, _ = solve_last(1, inner_x, all_y1)
+        inner_x, out_y0, states[0] = solve(0, active, trace_x, trace_y0, states[0])
+        if along_y:
+            trace_y0 = hand_on(lax.ppermute(out_y0, axes, along_y))
+        out_x, out_y1, states[1] = solve(1, active, inner_x, trace_y1, states[1])
+        if along_x:
+            trace_x = lax.ppermute(out_x, axes, along_x)
+        if along_y:
+            trace_y1 = lax.ppermute(out_y1, axes, along_y)
+
+    edge_x, edge_y = pl.pallas_call(
+        edge_kernel,
+        out_shape=(shaped(*zero_x.shape), shaped(2, *zero_y.shape)),
+        in_specs=[whole()] * 4,
+        out_specs=(whole(), whole()),
+        compiler_params=PARAMS,
+        name="edges",
+    )(states[0][0], states[1][0], t["first"], t["right_z"])
 
     every = [(k, j) for k in range(chips) for j in range(grid_cols)]
     after_x = lax.ppermute(edge_x, axes, between([((k, j), (k - 1, j)) for k, j in every if k]))
-    after_y = lax.ppermute(
-        jnp.stack([edge_y0, edge_y1]), axes, between([((k, j), (k, j - 1)) for k, j in every if j])
-    )
+    after_y = lax.ppermute(edge_y, axes, between([((k, j), (k, j - 1)) for k, j in every if j]))
 
     half = shaped(2, 2, size_x, size_y, cells_z)
     keep, give = pl.pallas_call(
@@ -474,7 +464,7 @@
         scratch_shapes=[pltpu.VMEM((2, 2, 2, size_x, size_y, cells_z), F32)],
         compiler_params=PARAMS,
         name="finish",
-    )(core_ref, total0, term0, total1, term1, contrast, *[t[name] for name in FINISH])
+    )(core_ref, *states[0], *states[1], contrast, *[t[name] for name in FINISH])
     got = lax.ppermute(give, axes, own)
 
     keep_y = lax.dynamic_index_in_dim(after_y, core, 0, keepdims=False)

time: 71.5 us -> 75.5 us (1.056)
  the two profiles are of different devices: /device:TPU:29 before, /device:TPU:23 now
where the time goes in v5:
time: 75.5 us; the launch traced here: 74.9 us
  starting transfers between devices  30.7 us (41%)
  waiting for transfers between devices  25 us (33%)
  Pallas kernels  10.7 us (14%)
  local copies, waits for them, and re-layouts  6.96 us (9%)
  between operations  1.42 us (2%)
    ppermute x6, waiting for transfers between devices, body(): trace_y0 = hand_on(lax.ppermute(out_y0, axes, along_y))  21.9 us
    unnamed x30, local copies, waits for them, and re-layouts  6.86 us
    pallas_call x14, Pallas kernels, solve(): pl.pallas_call(functools.partial(beat_kernel, tile), out_shape=(shaped(*z...  6.57 us
    ppermute x1, starting transfers between devices, body(): lax.ppermute(jnp.concatenate([after_x, pass_y], axis=0), axes, own)  6.48 us
    ppermute x1, starting transfers between devices, body(): got = lax.ppermute(give, axes, own)  5.77 us
    ppermute x6, starting transfers between devices, body(): trace_x = lax.ppermute(out_x, axes, along_x)  5.24 us
    ppermute x6, starting transfers between devices, body(): trace_y0 = hand_on(lax.ppermute(out_y0, axes, along_y))  4.61 us
    ppermute x6, starting transfers between devices, body(): trace_y1 = lax.ppermute(out_y1, axes, along_y)  4.61 us
  transfers between devices with their start and end apart: 24, of which 5 were waited for; matrix products, arithmetic and copies ran while one was open for 0% of the time, Pallas kernels for 10%

profile of v5, /device:TPU:23, one launch (start us, length us, event | category | flops | bytes accessed | tf_op | source)
XLA Modules:
  0.0 74.9 jit_solution(184661519477622204)
XLA Ops:
  0.6 0.7 collective-permute-start
  1.5 0.7 copy-done.14
  2.3 0.9 %copy-done.1 = bf16[256,256]{1,0:T(8,128)(2,1)S(1)} copy-done((bf16[256,256]{1,0:T(8,128)(2,1)S(1)}, bf16[256,256]{1,0:T(8,128)(2,1)}, u32[]{:S(2)}) %copy-start.1) | copy-done | bytes 131096
  3.2 0.9 %copy-done.3 = bf16[2,256,256]{2,1,0:T(8,128)(2,1)S(1)} copy-done((bf16[2,256,256]{2,1,0:T(8,128)(2,1)S(1)}, bf16[2,256,256]{2,1,0:T(8,128)(2,1)}, u32[]{:S(2)}) %copy-start.3) | copy-done | bytes 262168
  4.1 0.9 %copy-done.5 = f32[256,1]{1,0:T(8,128)S(1)} copy-done((f32[256,1]{1,0:T(8,128)S(1)}, f32[256,1]{1,0:T(8,128)}, u32[]{:S(2)}) %copy-start.5) | copy-done | bytes 1048
  5.0 1.0 %copy-done.7 = f32[2,2,16,16,128]{4,3,2,1,0:T(8,128)S(1)} copy-done((f32[2,2,16,16,128]{4,3,2,1,0:T(8,128)S(1)}, f32[2,2,16,16,128]{4,3,2,1,0:T(8,128)}, u32[]{:S(2)}) %copy-start.7) | copy-done | bytes 524312
  6.1 0.9 %copy-done.9 = f32[16,16,128]{2,1,0:T(8,128)S(1)} copy-done((f32[16,16,128]{2,1,0:T(8,128)S(1)}, f32[16,16,128]{2,1,0:T(8,128)}, u32[]{:S(2)}) %copy-start.9) | copy-done | bytes 131096
  7.0 0.8 %prep.1 = (f32[256,256]{1,0:T(8,128)S(1)}, f32[2,256,128]{2,1,0:T(8,128)S(1)}) custom-call(s32[1]{0:T(128)} %bitcast.core_ref, f32[2,2,16,16,128]{4,3,2,1,0:T(8,128)S(1)} %copy-done.7, f32[16,16,128]{2,1,0:T(8,128)S(1)} %copy-done.9, s32[1,16]{1,0:T(1,128)S(1)} %and_select_fusion.2.place_ref, s32[1,16]{1,0:T(1,128)S(1)} %and_select_fusion.1.depth_ref, ...), custom_call_target="tpu_custom_call" | custom-call | tf_op jit(solution)/shard_map/prep/pallas_call | solution.py:385
  7.8 0.1 copy-done.2
  7.9 0.1 copy-done.4
  8.0 0.8 %prep_other.1 = (f32[2,256,256]{2,1,0:T(8,128)S(1)}, f32[2,2,256,128]{3,2,1,0:T(8,128)S(1)}) custom-call(s32[1]{0:T(128)} %bitcast.core_ref, f32[2,2,16,16,128]{4,3,2,1,0:T(8,128)S(1)} %collective-permute-done.swap_ref, f32[16,16,128]{2,1,0:T(8,128)S(1)} %collective-permute-done.1.slow_ref, f32[256,256]{1,0:T(8,128)S(1)} %get-tuple-element.63.own_modes_ref, ...), custom_call_target="tpu_custom_call" | custom-call | tf_op jit(solution)/shard_map/prep_other/pallas_call | solution.py:393
  9.0 0.8 %copy-done.8 = bf16[2,256,256]{2,1,0:T(8,128)(2,1)S(1)} copy-done((bf16[2,256,256]{2,1,0:T(8,128)(2,1)S(1)}, bf16[2,256,256]{2,1,0:T(8,128)(2,1)}, u32[]{:S(2)}) %copy-start.8) | copy-done | bytes 262168
  9.9 0.7 collective-permute-start.3
  10.7 0.7 collective-permute-start.2
  11.4 0.7 collective-permute-start.4
  12.2 0.7 collective-permute-start.6
  13.0 0.7 collective-permute-start.5
  13.6 0.7 collective-permute-start.7
  14.4 0.7 collective-permute-start.9
  15.2 0.7 collective-permute-start.8
  15.9 0.7 collective-permute-start.10
  16.7 0.7 collective-permute-start.12
  17.3 0.3 lower.10
  17.6 0.7 collective-permute-start.11
  18.3 0.7 collective-permute-start.13
  19.1 1.3 %collective-permute-start.15 = (f32[32,256]{1,0:T(8,128)S(1)}, f32[32,256]{1,0:T(8,128)S(1)}, u32[]{:S(2)}, u32[]{:S(2)}) collective-permute-start(f32[32,256]{1,0:T(8,128)S(1)} %get-tuple-element.101), channel_id=1, source_target_pairs={{18,19},{22,23},{25,26},{29,30}} | collective-permute-start | bytes 98312 | tf_op jit(solution)/shard_map/ppermute | solution.py:438
  20.5 1.3 %collective-permute-start.14 = (f32[32,256]{1,0:T(8,128)S(1)}, f32[32,256]{1,0:T(8,128)S(1)}, u32[]{:S(2)}, u32[]{:S(2)}) collective-permute-start(f32[32,256]{1,0:T(8,128)S(1)} %get-tuple-element.100), channel_id=1, source_target_pairs={{11,19},{15,23},{18,26},{22,30}} | collective-permute-start | bytes 98312 | tf_op jit(solution)/shard_map/ppermute | solution.py:441
  21.8 1.3 %collective-permute-start.16 = (f32[32,256]{1,0:T(8,128)S(1)}, f32[32,256]{1,0:T(8,128)S(1)}, u32[]{:S(2)}, u32[]{:S(2)}) collective-permute-start(f32[32,256]{1,0:T(8,128)S(1)} %get-tuple-element.105), channel_id=1, source_target_pairs={{18,19},{22,23},{25,26},{29,30}} | collective-permute-start | bytes 98312 | tf_op jit(solution)/shard_map/ppermute | solution.py:443
  23.1 21.9 %collective-permute-done.15.in_ref = f32[32,256]{1,0:T(8,128)S(1)} collective-permute-done((f32[32,256]{1,0:T(8,128)S(1)}, f32[32,256]{1,0:T(8,128)S(1)}, u32[]{:S(2)}, u32[]{:S(2)}) %collective-permute-start.15) | collective-permute-done | bytes 32800 | tf_op jit(solution)/shard_map/ppermute | solution.py:438
  44.9 1.5 %collective-permute-done.14.trace_x_ref = f32[32,256]{1,0:T(8,128)S(1)} collective-permute-done((f32[32,256]{1,0:T(8,128)S(1)}, f32[32,256]{1,0:T(8,128)S(1)}, u32[]{:S(2)}, u32[]{:S(2)}) %collective-permute-start.14) | collective-permute-done | bytes 32800 | tf_op jit(solution)/shard_map/ppermute | solution.py:441
  46.4 2.1 %upper.12 = (f32[32,256]{1,0:T(8,128)S(1)}, f32[32,256]{1,0:T(8,128)S(1)}, f32[256,256]{1,0:T(8,128)S(1)}, f32[256,256]{1,0:T(8,128)S(1)}) custom-call(s32[1]{0:T(128)} %bitcast.6.active_ref, f32[2,256,256]{2,1,0:T(8,128)S(1)} %get-tuple-element.65.modes_ref, ...), custom_call_target="tpu_custom_call", output_to_operand_aliasing={{2}: (5, {}), {3}: (6, {})} | custom-call | flops 2000000000 | bytes 2000000 | tf_op jit(solution)/shard_map/upper/pallas_call | solution.py:405
  48.6 0.7 collective-permute-start.18
  49.2 0.5 collective-permute-done.16.trace_y_ref
  49.7 2.1 %lower.12 = (f32[32,256]{1,0:T(8,128)S(1)}, f32[32,256]{1,0:T(8,128)S(1)}, f32[256,256]{1,0:T(8,128)S(1)}, f32[256,256]{1,0:T(8,128)S(1)}) custom-call(s32[1]{0:T(128)} %bitcast.6.active_ref, f32[2,256,256]{2,1,0:T(8,128)S(1)} %get-tuple-element.65.modes_ref, ...), custom_call_target="tpu_custom_call", output_to_operand_aliasing={{2}: (5, {}), {3}: (6, {})} | custom-call | flops 2000000000 | bytes 2000000 | tf_op jit(solution)/shard_map/lower/pallas_call | solution.py:405
  51.8 1.3 %collective-permute-start.17 = (f32[32,256]{1,0:T(8,128)S(1)}, f32[32,256]{1,0:T(8,128)S(1)}, u32[]{:S(2)}, u32[]{:S(2)}) collective-permute-start(f32[32,256]{1,0:T(8,128)S(1)} %get-tuple-element.108), channel_id=1, source_target_pairs={{19,27},{23,31}} | collective-permute-start | bytes 98312 | tf_op jit(solution)/shard_map/ppermute | solution.py:441
  53.1 0.7 collective-permute-start.19
  53.8 0.3 collective-permute-done.17.trace_x_ref
  54.1 0.7 upper.13
  54.8 0.7 lower.13
  55.5 0.2 copy-done.10
  55.7 0.6 edges.1
  56.3 1.3 %collective-permute-start.21 = (f32[2,32,256]{2,1,0:T(8,128)S(1)}, f32[2,32,256]{2,1,0:T(8,128)S(1)}, u32[]{:S(2)}, u32[]{:S(2)}) collective-permute-start(f32[2,32,256]{2,1,0:T(8,128)S(1)} %get-tuple-element.122), channel_id=1, source_target_pairs={{1,0},{5,4},{2,1},{6,5},{3,2},{7,6},{9,8},{13,12},{10,9},{14,13},{... | collective-permute-start | bytes 196616 | tf_op jit(solution)/shard_map/ppermute | solution.py:456
  57.6 1.9 %collective-permute-start.20 = (f32[32,256]{1,0:T(8,128)S(1)}, f32[32,256]{1,0:T(8,128)S(1)}, u32[]{:S(2)}, u32[]{:S(2)}) collective-permute-start(f32[32,256]{1,0:T(8,128)S(1)} %get-tuple-element.121), channel_id=1, source_target_pairs={{8,0},{12,4},{9,1},{13,5},{10,2},{14,6},{11,3},{15,7},{16,8},{20,1... | collective-permute-start | bytes 98312 | tf_op jit(solution)/shard_map/ppermute | solution.py:455
  59.5 1.0 %finish.1 = (f32[2,2,16,16,128]{4,3,2,1,0:T(8,128)S(1)}, f32[2,2,16,16,128]{4,3,2,1,0:T(8,128)S(1)}) custom-call(s32[1]{0:T(128)} %bitcast.core_ref, f32[256,256]{1,0:T(8,128)S(1)} %get-tuple-element.112.total0_ref, f32[256,256]{1,0:T(8,128)S(1)} %get-tuple-element.113.term0_ref, f32[256,256]{1,0:T(8,128)S(1)} %get-tuple-element.118.total1_ref, ...), custom_call_target="tpu_custom_call" | custom-call | tf_op jit(solution)/shard_map/finish/pallas_call | solution.py:459
  60.5 5.8 %collective-permute-start.22 = (f32[2,2,16,16,128]{4,3,2,1,0:T(8,128)S(1)}, f32[2,2,16,16,128]{4,3,2,1,0:T(8,128)S(1)}, u32[]{:S(2)}, u32[]{:S(2)}) collective-permute-start(f32[2,2,16,16,128]{4,3,2,1,0:T(8,128)S(1)} %get-tuple-element.123), channel_id=1, source_target_pairs={{0,4},{4,0},{1,5},{5,1},{2,6},{6,2},{3,7},{7,3},{8,12},{12,8},{9,1... | collective-permute-start | bytes 1572872 | tf_op jit(solution)/shard_map/ppermute | solution.py:468
  66.3 6.5 %collective-permute-start.23 = (f32[64,256]{1,0:T(8,128)S(1)}, f32[64,256]{1,0:T(8,128)S(1)}, u32[]{:S(2)}, u32[]{:S(2)}) collective-permute-start(f32[64,256]{1,0:T(8,128)S(1)} %pad_maximum_fusion), channel_id=1, source_target_pairs={{0,4},{4,0},{1,5},{5,1},{2,6},{6,2},{3,7},{7,3},{8,12},{12,8},{9,1... | collective-permute-start | bytes 196616 | tf_op jit(solution)/shard_map/ppermute | solution.py:472
  72.9 0.8 %collective-permute-done.23.got_edge_ref = f32[64,256]{1,0:T(8,128)S(1)} collective-permute-done((f32[64,256]{1,0:T(8,128)S(1)}, f32[64,256]{1,0:T(8,128)S(1)}, u32[]{:S(2)}, u32[]{:S(2)}) %collective-permute-start.23) | collective-permute-done | bytes 65568 | tf_op jit(solution)/shard_map/ppermute | solution.py:472
  73.7 1.0 %place.1 = (f32[2,2,16,16,128]{4,3,2,1,0:T(8,128)}, f32[2,2,16,16,128]{4,3,2,1,0:T(8,128)}) custom-call(s32[1]{0:T(128)} %bitcast.core_ref, f32[2,2,16,16,128]{4,3,2,1,0:T(8,128)S(1)} %get-tuple-element.120.keep_ref, f32[2,16,16,128]{3,2,1,0:T(8,128)S(1)} %keep.1.keep_rest_ref, f32[2,2,16,16,128]{4,3,2,1,0:T(8,128)S(1)} %collective-permute-done.22.got_ref, ...), custom_call_target="tpu_custom_call" | custom-call | tf_op jit(solution)/shard_map/place/pallas_call | solution.py:482
  (67 shorter events, 1.3 us)
Async XLA Ops:
  0.6 1.6 %copy-start = (f32[2,16,2]{1,2,0:T(2,128)S(1)}, f32[2,16,2]{1,2,0:T(2,128)}, u32[]{:S(2)}) copy-start(f32[2,16,2]{1,2,0:T(2,128)} %param.15) | copy-start | bytes 772
  0.6 7.1 %collective-permute-start = (f32[2,2,16,16,128]{4,3,2,1,0:T(8,128)}, f32[2,2,16,16,128]{4,3,2,1,0:T(8,128)S(1)}, u32[]{:S(2)}, u32[]{:S(2)}) collective-permute-start(f32[2,2,16,16,128]{4,3,2,1,0:T(8,128)} %right_ref.1), channel_id=1, source_target_pairs={{0,4},{4,0},{1,5},{5,1},{2,6},{6,2},{3,7},{7,3},{8,12},{12,8},{9,1... | collective-permute-start | bytes 1572872 | tf_op jit(solution)/shard_map/ppermute | solution.py:368
  1.4 6.3 %collective-permute-start.1 = (f32[16,16,128]{2,1,0:T(8,128)}, f32[16,16,128]{2,1,0:T(8,128)S(1)}, u32[]{:S(2)}, u32[]{:S(2)}) collective-permute-start(f32[16,16,128]{2,1,0:T(8,128)} %slow_ref.1), channel_id=1, source_target_pairs={{0,4},{4,0},{1,5},{5,1},{2,6},{6,2},{3,7},{7,3},{8,12},{12,8},{9,1... | collective-permute-start | bytes 393224 | tf_op jit(solution)/shard_map/ppermute | solution.py:369
  1.5 0.7 copy-start.14
  2.3 0.9 %copy-start.1 = (bf16[256,256]{1,0:T(8,128)(2,1)S(1)}, bf16[256,256]{1,0:T(8,128)(2,1)}, u32[]{:S(2)}) copy-start(bf16[256,256]{1,0:T(8,128)(2,1)} %constant.150.clone.z_ref.refs_3_) | copy-start | bytes 393220
  3.2 0.9 %copy-start.3 = (bf16[2,256,256]{2,1,0:T(8,128)(2,1)S(1)}, bf16[2,256,256]{2,1,0:T(8,128)(2,1)}, u32[]{:S(2)}) copy-start(bf16[2,256,256]{2,1,0:T(8,128)(2,1)} %constant.148.clone.forward_ref.refs_1_) | copy-start | bytes 786436
  4.1 0.9 %copy-start.5 = (f32[256,1]{1,0:T(8,128)S(1)}, f32[256,1]{1,0:T(8,128)}, u32[]{:S(2)}) copy-start(f32[256,1]{1,0:T(8,128)} %constant.154.clone.edge_ref) | copy-start | bytes 3076
  5.0 1.0 %copy-start.7 = (f32[2,2,16,16,128]{4,3,2,1,0:T(8,128)S(1)}, f32[2,2,16,16,128]{4,3,2,1,0:T(8,128)}, u32[]{:S(2)}) copy-start(f32[2,2,16,16,128]{4,3,2,1,0:T(8,128)} %right_ref.1) | copy-start | bytes 1572868
  6.1 0.9 %copy-start.9 = (f32[16,16,128]{2,1,0:T(8,128)S(1)}, f32[16,16,128]{2,1,0:T(8,128)}, u32[]{:S(2)}) copy-start(f32[16,16,128]{2,1,0:T(8,128)} %slow_ref.1) | copy-start | bytes 393220
  7.0 0.9 %copy-start.2 = (bf16[256,256]{1,0:T(8,128)(2,1)S(1)}, bf16[256,256]{1,0:T(8,128)(2,1)}, u32[]{:S(2)}) copy-start(bf16[256,256]{1,0:T(8,128)(2,1)} %constant.150.clone.z_ref.refs_3_) | copy-start | bytes 393220
  7.0 1.0 %copy-start.4 = (bf16[2,256,256]{2,1,0:T(8,128)(2,1)S(1)}, bf16[2,256,256]{2,1,0:T(8,128)(2,1)}, u32[]{:S(2)}) copy-start(bf16[2,256,256]{2,1,0:T(8,128)(2,1)} %constant.148.clone.forward_ref.refs_1_) | copy-start | bytes 786436
  7.0 1.0 %copy-start.6 = (f32[256,1]{1,0:T(8,128)S(1)}, f32[256,1]{1,0:T(8,128)}, u32[]{:S(2)}) copy-start(f32[256,1]{1,0:T(8,128)} %constant.154.clone.edge_ref) | copy-start | bytes 3076
  8.0 0.9 %copy-start.12 = (bf16[512,128]{1,0:T(8,128)(2,1)S(1)}, bf16[512,128]{1,0:T(8,128)(2,1)}, u32[]{:S(2)}) copy-start(bf16[512,128]{1,0:T(8,128)(2,1)} %constant.151.clone.refs_4_) | copy-start | bytes 393220
  8.0 1.0 %copy-start.13 = (bf16[128,512]{1,0:T(8,128)(2,1)S(1)}, bf16[128,512]{1,0:T(8,128)(2,1)}, u32[]{:S(2)}) copy-start(bf16[128,512]{1,0:T(8,128)(2,1)} %constant.152.clone.refs_5_) | copy-start | bytes 393220
  8.8 1.0 %copy-start.8 = (bf16[2,256,256]{2,1,0:T(8,128)(2,1)S(1)}, bf16[2,256,256]{2,1,0:T(8,128)(2,1)}, u32[]{:S(2)}) copy-start(bf16[2,256,256]{2,1,0:T(8,128)(2,1)} %constant.149.clone.refs_2_.backward_ref) | copy-start | bytes 786436
  8.8 1.1 %copy-start.11 = (f32[2,256,128]{2,1,0:T(8,128)S(1)}, f32[2,256,128]{2,1,0:T(8,128)}, u32[]{:S(2)}) copy-start(f32[2,256,128]{2,1,0:T(8,128)} %constant.147.clone.refs_0_) | copy-start | bytes 786436
  9.9 2.2 %collective-permute-start.3 = (f32[32,256]{1,0:T(8,128)S(1)}, f32[32,256]{1,0:T(8,128)S(1)}, u32[]{:S(2)}, u32[]{:S(2)}) collective-permute-start(f32[32,256]{1,0:T(8,128)S(1)} %get-tuple-element.69), channel_id=1, source_target_pairs={{0,1},{4,5}} | collective-permute-start | bytes 98312 | tf_op jit(solution)/shard_map/ppermute | solution.py:438
  10.7 1.4 %collective-permute-start.2 = (f32[32,256]{1,0:T(8,128)S(1)}, f32[32,256]{1,0:T(8,128)S(1)}, u32[]{:S(2)}, u32[]{:S(2)}) collective-permute-start(f32[32,256]{1,0:T(8,128)S(1)} %get-tuple-element.68), channel_id=1, source_target_pairs={{0,8},{4,12}} | collective-permute-start | bytes 98312 | tf_op jit(solution)/shard_map/ppermute | solution.py:441
  11.4 1.5 %collective-permute-start.4 = (f32[32,256]{1,0:T(8,128)S(1)}, f32[32,256]{1,0:T(8,128)S(1)}, u32[]{:S(2)}, u32[]{:S(2)}) collective-permute-start(f32[32,256]{1,0:T(8,128)S(1)} %get-tuple-element.73), channel_id=1, source_target_pairs={{0,1},{4,5}} | collective-permute-start | bytes 98312 | tf_op jit(solution)/shard_map/ppermute | solution.py:443
  12.2 2.1 %collective-permute-start.6 = (f32[32,256]{1,0:T(8,128)S(1)}, f32[32,256]{1,0:T(8,128)S(1)}, u32[]{:S(2)}, u32[]{:S(2)}) collective-permute-start(f32[32,256]{1,0:T(8,128)S(1)} %get-tuple-element.77), channel_id=1, source_target_pairs={{1,2},{5,6},{8,9},{12,13}} | collective-permute-start | bytes 98312 | tf_op jit(solution)/shard_map/ppermute | solution.py:438
  13.0 1.4 %collective-permute-start.5 = (f32[32,256]{1,0:T(8,128)S(1)}, f32[32,256]{1,0:T(8,128)S(1)}, u32[]{:S(2)}, u32[]{:S(2)}) collective-permute-start(f32[32,256]{1,0:T(8,128)S(1)} %get-tuple-element.76), channel_id=1, source_target_pairs={{1,9},{5,13},{8,16},{12,20}} | collective-permute-start | bytes 98312 | tf_op jit(solution)/shard_map/ppermute | solution.py:441
  13.6 1.5 %collective-permute-start.7 = (f32[32,256]{1,0:T(8,128)S(1)}, f32[32,256]{1,0:T(8,128)S(1)}, u32[]{:S(2)}, u32[]{:S(2)}) collective-permute-start(f32[32,256]{1,0:T(8,128)S(1)} %get-tuple-element.81), channel_id=1, source_target_pairs={{1,2},{5,6},{8,9},{12,13}} | collective-permute-start | bytes 98312 | tf_op jit(solution)/shard_map/ppermute | solution.py:443
  14.4 2.1 %collective-permute-start.9 = (f32[32,256]{1,0:T(8,128)S(1)}, f32[32,256]{1,0:T(8,128)S(1)}, u32[]{:S(2)}, u32[]{:S(2)}) collective-permute-start(f32[32,256]{1,0:T(8,128)S(1)} %get-tuple-element.85), channel_id=1, source_target_pairs={{2,3},{6,7},{9,10},{13,14},{16,17},{20,21}} | collective-permute-start | bytes 98312 | tf_op jit(solution)/shard_map/ppermute | solution.py:438
  15.2 1.4 %collective-permute-start.8 = (f32[32,256]{1,0:T(8,128)S(1)}, f32[32,256]{1,0:T(8,128)S(1)}, u32[]{:S(2)}, u32[]{:S(2)}) collective-permute-start(f32[32,256]{1,0:T(8,128)S(1)} %get-tuple-element.84), channel_id=1, source_target_pairs={{2,10},{6,14},{9,17},{13,21},{16,24},{20,28}} | collective-permute-start | bytes 98312 | tf_op jit(solution)/shard_map/ppermute | solution.py:441
  15.9 1.5 %collective-permute-start.10 = (f32[32,256]{1,0:T(8,128)S(1)}, f32[32,256]{1,0:T(8,128)S(1)}, u32[]{:S(2)}, u32[]{:S(2)}) collective-permute-start(f32[32,256]{1,0:T(8,128)S(1)} %get-tuple-element.89), channel_id=1, source_target_pairs={{2,3},{6,7},{9,10},{13,14},{16,17},{20,21}} | collective-permute-start | bytes 98312 | tf_op jit(solution)/shard_map/ppermute | solution.py:443
  16.7 2.3 %collective-permute-start.12 = (f32[32,256]{1,0:T(8,128)S(1)}, f32[32,256]{1,0:T(8,128)S(1)}, u32[]{:S(2)}, u32[]{:S(2)}) collective-permute-start(f32[32,256]{1,0:T(8,128)S(1)} %get-tuple-element.93), channel_id=1, source_target_pairs={{10,11},{14,15},{17,18},{21,22},{24,25},{28,29}} | collective-permute-start | bytes 98312 | tf_op jit(solution)/shard_map/ppermute | solution.py:438
  17.6 1.4 %collective-permute-start.11 = (f32[32,256]{1,0:T(8,128)S(1)}, f32[32,256]{1,0:T(8,128)S(1)}, u32[]{:S(2)}, u32[]{:S(2)}) collective-permute-start(f32[32,256]{1,0:T(8,128)S(1)} %get-tuple-element.92), channel_id=1, source_target_pairs={{3,11},{7,15},{10,18},{14,22},{17,25},{21,29}} | collective-permute-start | bytes 98312 | tf_op jit(solution)/shard_map/ppermute | solution.py:441
  18.3 2.1 %collective-permute-start.13 = (f32[32,256]{1,0:T(8,128)S(1)}, f32[32,256]{1,0:T(8,128)S(1)}, u32[]{:S(2)}, u32[]{:S(2)}) collective-permute-start(f32[32,256]{1,0:T(8,128)S(1)} %get-tuple-element.97), channel_id=1, source_target_pairs={{10,11},{14,15},{17,18},{21,22},{24,25},{28,29}} | collective-permute-start | bytes 98312 | tf_op jit(solution)/shard_map/ppermute | solution.py:443
  19.1 25.9 %collective-permute-start.15 = (f32[32,256]{1,0:T(8,128)S(1)}, f32[32,256]{1,0:T(8,128)S(1)}, u32[]{:S(2)}, u32[]{:S(2)}) collective-permute-start(f32[32,256]{1,0:T(8,128)S(1)} %get-tuple-element.101), channel_id=1, source_target_pairs={{18,19},{22,23},{25,26},{29,30}} | collective-permute-start | bytes 98312 | tf_op jit(solution)/shard_map/ppermute | solution.py:438
  20.5 25.9 %collective-permute-start.14 = (f32[32,256]{1,0:T(8,128)S(1)}, f32[32,256]{1,0:T(8,128)S(1)}, u32[]{:S(2)}, u32[]{:S(2)}) collective-permute-start(f32[32,256]{1,0:T(8,128)S(1)} %get-tuple-element.100), channel_id=1, source_target_pairs={{11,19},{15,23},{18,26},{22,30}} | collective-permute-start | bytes 98312 | tf_op jit(solution)/shard_map/ppermute | solution.py:441
  21.8 27.9 %collective-permute-start.16 = (f32[32,256]{1,0:T(8,128)S(1)}, f32[32,256]{1,0:T(8,128)S(1)}, u32[]{:S(2)}, u32[]{:S(2)}) collective-permute-start(f32[32,256]{1,0:T(8,128)S(1)} %get-tuple-element.105), channel_id=1, source_target_pairs={{18,19},{22,23},{25,26},{29,30}} | collective-permute-start | bytes 98312 | tf_op jit(solution)/shard_map/ppermute | solution.py:443
  48.6 5.3 %collective-permute-start.18 = (f32[32,256]{1,0:T(8,128)S(1)}, f32[32,256]{1,0:T(8,128)S(1)}, u32[]{:S(2)}, u32[]{:S(2)}) collective-permute-start(f32[32,256]{1,0:T(8,128)S(1)} %get-tuple-element.109), channel_id=1, source_target_pairs={{26,27},{30,31}} | collective-permute-start | bytes 98312 | tf_op jit(solution)/shard_map/ppermute | solution.py:438
  51.8 2.3 %collective-permute-start.17 = (f32[32,256]{1,0:T(8,128)S(1)}, f32[32,256]{1,0:T(8,128)S(1)}, u32[]{:S(2)}, u32[]{:S(2)}) collective-permute-start(f32[32,256]{1,0:T(8,128)S(1)} %get-tuple-element.108), channel_id=1, source_target_pairs={{19,27},{23,31}} | collective-permute-start | bytes 98312 | tf_op jit(solution)/shard_map/ppermute | solution.py:441
  53.1 1.7 %collective-permute-start.19 = (f32[32,256]{1,0:T(8,128)S(1)}, f32[32,256]{1,0:T(8,128)S(1)}, u32[]{:S(2)}, u32[]{:S(2)}) collective-permute-start(f32[32,256]{1,0:T(8,128)S(1)} %get-tuple-element.115), channel_id=1, source_target_pairs={{26,27},{30,31}} | collective-permute-start | bytes 98312 | tf_op jit(solution)/shard_map/ppermute | solution.py:443
  54.8 0.9 %copy-start.10 = (bf16[128,512]{1,0:T(8,128)(2,1)S(1)}, bf16[128,512]{1,0:T(8,128)(2,1)}, u32[]{:S(2)}) copy-start(bf16[128,512]{1,0:T(8,128)(2,1)} %constant.153.clone.first_ref) | copy-start | bytes 393220
  56.3 10.0 %collective-permute-start.21 = (f32[2,32,256]{2,1,0:T(8,128)S(1)}, f32[2,32,256]{2,1,0:T(8,128)S(1)}, u32[]{:S(2)}, u32[]{:S(2)}) collective-permute-start(f32[2,32,256]{2,1,0:T(8,128)S(1)} %get-tuple-element.122), channel_id=1, source_target_pairs={{1,0},{5,4},{2,1},{6,5},{3,2},{7,6},{9,8},{13,12},{10,9},{14,13},{... | collective-permute-start | bytes 196616 | tf_op jit(solution)/shard_map/ppermute | solution.py:456
  57.6 8.7 %collective-permute-start.20 = (f32[32,256]{1,0:T(8,128)S(1)}, f32[32,256]{1,0:T(8,128)S(1)}, u32[]{:S(2)}, u32[]{:S(2)}) collective-permute-start(f32[32,256]{1,0:T(8,128)S(1)} %get-tuple-element.121), channel_id=1, source_target_pairs={{8,0},{12,4},{9,1},{13,5},{10,2},{14,6},{11,3},{15,7},{16,8},{20,1... | collective-permute-start | bytes 98312 | tf_op jit(solution)/shard_map/ppermute | solution.py:455
  60.5 13.2 %collective-permute-start.22 = (f32[2,2,16,16,128]{4,3,2,1,0:T(8,128)S(1)}, f32[2,2,16,16,128]{4,3,2,1,0:T(8,128)S(1)}, u32[]{:S(2)}, u32[]{:S(2)}) collective-permute-start(f32[2,2,16,16,128]{4,3,2,1,0:T(8,128)S(1)} %get-tuple-element.123), channel_id=1, source_target_pairs={{0,4},{4,0},{1,5},{5,1},{2,6},{6,2},{3,7},{7,3},{8,12},{12,8},{9,1... | collective-permute-start | bytes 1572872 | tf_op jit(solution)/shard_map/ppermute | solution.py:468
  66.3 7.4 %collective-permute-start.23 = (f32[64,256]{1,0:T(8,128)S(1)}, f32[64,256]{1,0:T(8,128)S(1)}, u32[]{:S(2)}, u32[]{:S(2)}) collective-permute-start(f32[64,256]{1,0:T(8,128)S(1)} %pad_maximum_fusion), channel_id=1, source_target_pairs={{0,4},{4,0},{1,5},{5,1},{2,6},{6,2},{3,7},{7,3},{8,12},{12,8},{9,1... | collective-permute-start | bytes 196616 | tf_op jit(solution)/shard_map/ppermute | solution.py:472

commit v6 on v5

--- a/solution.py
+++ b/solution.py
@@ -30,9 +30,7 @@
 
 def left_factor(matrix):
     high, low = halves(matrix)
-    return np.concatenate(
-        [np.concatenate([high, high], axis=1), np.concatenate([low, low], axis=1)], axis=0
-    )
+    return np.concatenate([high, high, low], axis=1)
 
 
 def tables(size_x, size_y, cells_z):
@@ -107,9 +105,7 @@
 
 def left_product(matrix, values):
     high, low = split(values)
-    both = jnp.dot(matrix, jnp.concatenate([high, low], axis=0), preferred_element_type=F32)
-    count = both.shape[0] // 2
-    return both[:count] + both[count:]
+    return jnp.dot(matrix, jnp.concatenate([high, low, high], axis=0), preferred_element_type=F32)
 
 
 def z_transform(field, right_z):
@@ -195,9 +191,9 @@
     modes_ref[...] = to_modes(z_transform(field + dense, right_z), forward)
 
 
-def prep_kernel(cells_x, core_ref, right_ref, slow_ref, place_ref, depth_ref, amp_ref, edge_ref,
+def prep_kernel(cells_x, rhs_ref, right_ref, slow_ref, place_ref, depth_ref, amp_ref, edge_ref,
                 forward_ref, z_ref, modes_ref, contrast_ref):
-    dense = [jnp.concatenate([right_ref[core_ref[0], c, x] for x in cells_x], axis=0) for c in range(2)]
+    dense = [jnp.concatenate([right_ref[rhs_ref[0], c, x] for x in cells_x], axis=0) for c in range(2)]
     slow = jnp.concatenate([slow_ref[x] for x in cells_x], axis=0)
     prepare(
         jnp.concatenate(dense, axis=1), slow, place_ref[...], depth_ref[...], amp_ref, edge_ref[...],
@@ -205,16 +201,15 @@
     )
 
 
-def prep_other_kernel(cells_x, core_ref, swap_ref, slow_ref, own_modes_ref, own_contrast_ref, place_ref, depth_ref,
+def prep_other_kernel(cells_x, core_ref, swap_ref, own_modes_ref, own_contrast_ref, place_ref, depth_ref,
                       amp_ref, edge_ref, forward_ref, z_ref, modes_ref, contrast_ref):
     core = core_ref[0]
     other = 1 - core
     modes_ref[core] = own_modes_ref[...]
     contrast_ref[core] = own_contrast_ref[...]
-    dense = [jnp.concatenate([swap_ref[core, c, x] for x in cells_x], axis=0) for c in range(2)]
-    slow = jnp.concatenate([slow_ref[x] for x in cells_x], axis=0)
+    parts = [jnp.concatenate([swap_ref[c, x] for x in cells_x], axis=0) for c in range(3)]
     prepare(
-        jnp.concatenate(dense, axis=1), slow, place_ref[...], depth_ref[...], amp_ref,
+        jnp.concatenate(parts[:2], axis=1), parts[2], place_ref[...], depth_ref[...], amp_ref,
         edge_ref[...], forward_ref, z_ref[...], modes_ref.at[other], contrast_ref.at[other],
     )
 
@@ -300,19 +295,19 @@
     add_later(rest_ref, edge_x_ref[...], edge_y_ref[...], (core_ref[0] == 1).astype(F32))
 
 
-def place_kernel(core_ref, keep_ref, keep_rest_ref, got_ref, got_edge_ref, wave_ref, rest_ref, work_ref, sems):
-    core = core_ref[0]
+def place_kernel(core_ref, rhs_ref, keep_ref, keep_rest_ref, got_ref, got_edge_ref, wave_ref, rest_ref, work_ref, sems):
+    rhs = rhs_ref[0]
     count = got_edge_ref.shape[0] // 2
     copies = [
-        pltpu.make_async_copy(keep_ref.at[0], wave_ref.at[core], sems.at[0]),
-        pltpu.make_async_copy(got_ref.at[0], wave_ref.at[1 - core], sems.at[1]),
-        pltpu.make_async_copy(keep_rest_ref, rest_ref.at[core], sems.at[2]),
+        pltpu.make_async_copy(keep_ref.at[0], wave_ref.at[rhs], sems.at[0]),
+        pltpu.make_async_copy(got_ref.at[0], wave_ref.at[1 - rhs], sems.at[1]),
+        pltpu.make_async_copy(keep_rest_ref, rest_ref.at[rhs], sems.at[2]),
     ]
     for copy in copies:
         copy.start()
     work_ref[...] = got_ref[1]
-    add_later(work_ref, got_edge_ref[:count], got_edge_ref[count:], (core == 1).astype(F32))
-    copies.append(pltpu.make_async_copy(work_ref, rest_ref.at[1 - core], sems.at[3]))
+    add_later(work_ref, got_edge_ref[:count], got_edge_ref[count:], (core_ref[0] == 1).astype(F32))
+    copies.append(pltpu.make_async_copy(work_ref, rest_ref.at[1 - rhs], sems.at[3]))
     copies[-1].start()
     for copy in copies:
         copy.wait()
@@ -332,7 +327,7 @@
 
 SOLVE_COST = pl.CostEstimate(flops=2 * 10**9, bytes_accessed=2 * 10**6, transcendentals=0)
 KEEP_COST = pl.CostEstimate(flops=10**10, bytes_accessed=10**6, transcendentals=0)
-PARAMS = pltpu.CompilerParams(vmem_limit_bytes=40 * 1024 * 1024)
+PARAMS = pltpu.CompilerParams(vmem_limit_bytes=24 * 1024 * 1024)
 
 
 def shaped(*shape):
@@ -346,7 +341,8 @@
     chips = grid_rows // 2
     row, col = lax.axis_index("gx"), lax.axis_index("gy")
     core = row % 2
-    core_ref = core[None]
+    rhs = (core + row // 2 + col) % 2
+    core_ref, rhs_ref = core[None], rhs[None]
     t, cells_x = tables(size_x, size_y, cells_z)
     t = {name: jnp.asarray(value) for name, value in t.items()}
     cells_x = tuple(int(x) for x in cells_x)
@@ -357,7 +353,7 @@
 
     def between(pairs):
         return [
-            (device(a, r, b), device(c, r, d)) for (a, b), (c, d) in pairs for r in range(2)
+            (device(a, r, b), device(c, 1 - r, d)) for (a, b), (c, d) in pairs for r in range(2)
         ]
 
     own = [
@@ -365,11 +361,11 @@
         for k in range(chips) for j in range(grid_cols) for r in range(2)
     ]
     axes = ("gx", "gy")
-    swapped = lax.ppermute(right_side, axes, own)
-    swapped_slow = lax.ppermute(slowness, axes, own)
+    other = lax.dynamic_index_in_dim(right_side, 1 - rhs, 0, keepdims=False)
+    swapped = lax.ppermute(jnp.concatenate([other, slowness[None]], axis=0), axes, own)
 
     total_y = size_y * grid_cols
-    cells = lax.dynamic_index_in_dim(source_cells, core, 0, keepdims=True)
+    cells = lax.dynamic_index_in_dim(source_cells, rhs, 0, keepdims=True)
     near_y = cells // cells_z % total_y - col * size_y
     places = []
     for tile_row in (row, row + 1 - 2 * core):
@@ -377,7 +373,7 @@
         inside = (near_x >= 0) & (near_x < size_x) & (near_y >= 0) & (near_y < size_y)
         folded = jnp.where(near_x < size_x // 2, near_x, size_x + size_x // 2 - 1 - near_x)
         places.append(jnp.where(inside, folded * size_y + near_y, -1))
-    amplitudes = lax.dynamic_index_in_dim(source_amplitudes, core, 0, keepdims=False).T[:, None, :]
+    amplitudes = lax.dynamic_index_in_dim(source_amplitudes, rhs, 0, keepdims=False).T[:, None, :]
 
     depth = cells % cells_z
     prep_tables = [t[name] for name in PREP]
@@ -389,15 +385,15 @@
         out_specs=(whole(), whole()),
         compiler_params=PARAMS,
         name="prep",
-    )(core_ref, right_side, slowness, places[0], depth, amplitudes, *prep_tables)
+    )(rhs_ref, right_side, slowness, places[0], depth, amplitudes, *prep_tables)
     modes, contrast = pl.pallas_call(
         functools.partial(prep_other_kernel, cells_x),
         out_shape=(shaped(2, rows, 2 * cells_z), shaped(2, 2, rows, cells_z)),
-        in_specs=[scalars()] + [whole()] * 10,
+        in_specs=[scalars()] + [whole()] * 9,
         out_specs=(whole(), whole()),
         compiler_params=PARAMS,
         name="prep_other",
-    )(core_ref, swapped, swapped_slow, own_modes, own_contrast, places[1], depth, amplitudes, *prep_tables)
+    )(core_ref, swapped, own_modes, own_contrast, places[1], depth, amplitudes, *prep_tables)
 
     beat_tables = [t[name] for name in BEAT]
 
@@ -482,7 +478,7 @@
     return pl.pallas_call(
         place_kernel,
         out_shape=(shaped(*right_side.shape), shaped(*right_side.shape)),
-        in_specs=[scalars()] + [whole()] * 4,
+        in_specs=[scalars()] * 2 + [whole()] * 4,
         out_specs=(anywhere(), anywhere()),
         scratch_shapes=[
             pltpu.VMEM((2, size_x, size_y, cells_z), F32),
@@ -490,7 +486,7 @@
         ],
         compiler_params=PARAMS,
         name="place",
-    )(core_ref, keep, keep_rest, got, got_edge)
+    )(core_ref, rhs_ref, keep, keep_rest, got, got_edge)
 
 
 def solution(mesh):

time: 75.5 us -> 67.5 us (0.89)
  the two profiles are of different devices: /device:TPU:23 before, /device:TPU:29 now
where the time goes in v6:
time: 67.5 us; the launch traced here: 66.2 us
  waiting for transfers between devices  30.7 us (45%)
  starting transfers between devices  20.1 us (30%)
  Pallas kernels  10.8 us (16%)
  local copies, waits for them, and re-layouts  3 us (4%)
  between operations  1.52 us (2%)
    ppermute x6, waiting for transfers between devices, body(): trace_y0 = hand_on(lax.ppermute(out_y0, axes, along_y))  25.8 us
    pallas_call x14, Pallas kernels, solve(): pl.pallas_call(functools.partial(beat_kernel, tile), out_shape=(shaped(*z...  6.47 us
    ppermute x6, starting transfers between devices, body(): trace_y1 = lax.ppermute(out_y1, axes, along_y)  5.24 us
    ppermute x6, starting transfers between devices, body(): trace_y0 = hand_on(lax.ppermute(out_y0, axes, along_y))  5.24 us
    ppermute x6, starting transfers between devices, body(): trace_x = lax.ppermute(out_x, axes, along_x)  4.61 us
    ppermute x1, waiting for transfers between devices, body(): lax.ppermute(edge_y, axes, between([((k, j), (k, j - 1)) for k, j in ever...  2.34 us
    ppermute x1, starting transfers between devices, body(): lax.ppermute(edge_y, axes, between([((k, j), (k, j - 1)) for k, j in ever...  1.92 us
    unnamed x24, local copies, waits for them, and re-layouts  1.9 us
  transfers between devices with their start and end apart: 23, of which 5 were waited for; matrix products, arithmetic and copies ran while one was open for 0% of the time, Pallas kernels for 12%

profile of v6, /device:TPU:29, one launch (start us, length us, event | category | flops | bytes accessed | tf_op | source)
XLA Modules:
  0.0 66.2 jit_solution(6874663036652094448)
XLA Ops:
  0.7 1.0 %dynamic-slice_bitcast_fusion = f32[2,16,16,128]{3,2,1,0:T(8,128)S(1)} fusion(f32[2,2,16,16,128]{4,3,2,1,0:T(8,128)} %right_ref.1, s32[]{:T(128)S(6)} %select_n.74), kind=kLoop, calls=%fused_computation.1 | loop fusion | bytes 524292 | tf_op jit(solution)/shard_map/jit(dynamic_index_in_dim)/squeeze | solution.py:364
  1.8 0.7 %collective-permute-start = (f32[3,16,16,128]{3,2,1,0:T(8,128)S(1)}, f32[3,16,16,128]{3,2,1,0:T(8,128)S(1)}, u32[]{:S(2)}, u32[]{:S(2)}) collective-permute-start(f32[3,16,16,128]{3,2,1,0:T(8,128)S(1)} %pad_maximum_fusion), channel_id=1, source_target_pairs={{0,4},{4,0},{1,5},{5,1},{2,6},{6,2},{3,7},{7,3},{8,12},{12,8},{9,1... | collective-permute-start | bytes 1179656 | tf_op jit(solution)/shard_map/ppermute | solution.py:365
  2.6 0.7 %copy-done.11 = s32[2,16]{1,0:T(2,128)S(1)} copy-done((s32[2,16]{1,0:T(2,128)S(1)}, s32[2,16]{1,0:T(2,128)}, u32[]{:S(2)}) %copy-start.11) | copy-done | bytes 152
  3.3 0.8 %prep.1 = (f32[256,256]{1,0:T(8,128)S(1)}, f32[2,256,128]{2,1,0:T(8,128)S(1)}) custom-call(s32[1]{0:T(128)} %bitcast.1.rhs_ref, f32[2,2,16,16,128]{4,3,2,1,0:T(8,128)S(1)} %copy-done.2, f32[16,16,128]{2,1,0:T(8,128)S(1)} %copy-done.5, s32[1,16]{1,0:T(1,128)S(1)} %and_select_fusion.2.place_ref, s32[1,16]{1,0:T(1,128)S(1)} %and_select_fusion.1.depth_ref, ...), custom_call_target="tpu_custom_call" | custom-call | tf_op jit(solution)/shard_map/prep/pallas_call | solution.py:381
  4.1 0.8 %prep_other.1 = (f32[2,256,256]{2,1,0:T(8,128)S(1)}, f32[2,2,256,128]{3,2,1,0:T(8,128)S(1)}) custom-call(s32[1]{0:T(128)} %bitcast.core_ref, f32[3,16,16,128]{3,2,1,0:T(8,128)S(1)} %collective-permute-done.swap_ref, f32[256,256]{1,0:T(8,128)S(1)} %get-tuple-element.63.own_modes_ref, f32[2,256,128]{2,1,0:T(8,128)S(1)} %get-tuple-element.64.own_contrast_ref, ...), custom_call_target="tpu_custom_call" | custom-call | tf_op jit(solution)/shard_map/prep_other/pallas_call | solution.py:389
  5.1 0.8 %copy-done.8 = f32[2,256,128]{2,1,0:T(8,128)S(1)} copy-done((f32[2,256,128]{2,1,0:T(8,128)S(1)}, f32[2,256,128]{2,1,0:T(8,128)}, u32[]{:S(2)}) %copy-start.8) | copy-done | bytes 262168
  6.0 0.7 %collective-permute-start.2 = (f32[32,256]{1,0:T(8,128)S(1)}, f32[32,256]{1,0:T(8,128)S(1)}, u32[]{:S(2)}, u32[]{:S(2)}) collective-permute-start(f32[32,256]{1,0:T(8,128)S(1)} %get-tuple-element.69), channel_id=1, source_target_pairs={{0,5},{4,1}} | collective-permute-start | bytes 98312 | tf_op jit(solution)/shard_map/ppermute | solution.py:434
  6.7 0.1 lower.7
  6.8 0.7 %collective-permute-start.1 = (f32[32,256]{1,0:T(8,128)S(1)}, f32[32,256]{1,0:T(8,128)S(1)}, u32[]{:S(2)}, u32[]{:S(2)}) collective-permute-start(f32[32,256]{1,0:T(8,128)S(1)} %get-tuple-element.68), channel_id=1, source_target_pairs={{0,12},{4,8}} | collective-permute-start | bytes 98312 | tf_op jit(solution)/shard_map/ppermute | solution.py:437
  7.5 0.7 %collective-permute-start.3 = (f32[32,256]{1,0:T(8,128)S(1)}, f32[32,256]{1,0:T(8,128)S(1)}, u32[]{:S(2)}, u32[]{:S(2)}) collective-permute-start(f32[32,256]{1,0:T(8,128)S(1)} %get-tuple-element.73), channel_id=1, source_target_pairs={{0,5},{4,1}} | collective-permute-start | bytes 98312 | tf_op jit(solution)/shard_map/ppermute | solution.py:439
  8.2 0.1 upper.8
  8.3 0.7 %collective-permute-start.5 = (f32[32,256]{1,0:T(8,128)S(1)}, f32[32,256]{1,0:T(8,128)S(1)}, u32[]{:S(2)}, u32[]{:S(2)}) collective-permute-start(f32[32,256]{1,0:T(8,128)S(1)} %get-tuple-element.77), channel_id=1, source_target_pairs={{1,6},{5,2},{8,13},{12,9}} | collective-permute-start | bytes 98312 | tf_op jit(solution)/shard_map/ppermute | solution.py:434
  9.0 0.1 lower.8
  9.1 0.7 %collective-permute-start.4 = (f32[32,256]{1,0:T(8,128)S(1)}, f32[32,256]{1,0:T(8,128)S(1)}, u32[]{:S(2)}, u32[]{:S(2)}) collective-permute-start(f32[32,256]{1,0:T(8,128)S(1)} %get-tuple-element.76), channel_id=1, source_target_pairs={{1,13},{5,9},{8,20},{12,16}} | collective-permute-start | bytes 98312 | tf_op jit(solution)/shard_map/ppermute | solution.py:437
  9.7 0.7 %collective-permute-start.6 = (f32[32,256]{1,0:T(8,128)S(1)}, f32[32,256]{1,0:T(8,128)S(1)}, u32[]{:S(2)}, u32[]{:S(2)}) collective-permute-start(f32[32,256]{1,0:T(8,128)S(1)} %get-tuple-element.81), channel_id=1, source_target_pairs={{1,6},{5,2},{8,13},{12,9}} | collective-permute-start | bytes 98312 | tf_op jit(solution)/shard_map/ppermute | solution.py:439
  10.4 0.1 upper.9
  10.5 0.7 %collective-permute-start.8 = (f32[32,256]{1,0:T(8,128)S(1)}, f32[32,256]{1,0:T(8,128)S(1)}, u32[]{:S(2)}, u32[]{:S(2)}) collective-permute-start(f32[32,256]{1,0:T(8,128)S(1)} %get-tuple-element.85), channel_id=1, source_target_pairs={{2,7},{6,3},{9,14},{13,10},{16,21},{20,17}} | collective-permute-start | bytes 98312 | tf_op jit(solution)/shard_map/ppermute | solution.py:434
  11.3 0.7 %collective-permute-start.7 = (f32[32,256]{1,0:T(8,128)S(1)}, f32[32,256]{1,0:T(8,128)S(1)}, u32[]{:S(2)}, u32[]{:S(2)}) collective-permute-start(f32[32,256]{1,0:T(8,128)S(1)} %get-tuple-element.84), channel_id=1, source_target_pairs={{2,14},{6,10},{9,21},{13,17},{16,28},{20,24}} | collective-permute-start | bytes 98312 | tf_op jit(solution)/shard_map/ppermute | solution.py:437
  12.0 0.7 %collective-permute-start.9 = (f32[32,256]{1,0:T(8,128)S(1)}, f32[32,256]{1,0:T(8,128)S(1)}, u32[]{:S(2)}, u32[]{:S(2)}) collective-permute-start(f32[32,256]{1,0:T(8,128)S(1)} %get-tuple-element.89), channel_id=1, source_target_pairs={{2,7},{6,3},{9,14},{13,10},{16,21},{20,17}} | collective-permute-start | bytes 98312 | tf_op jit(solution)/shard_map/ppermute | solution.py:439
  12.7 0.1 upper.10
  12.8 0.7 %collective-permute-start.11 = (f32[32,256]{1,0:T(8,128)S(1)}, f32[32,256]{1,0:T(8,128)S(1)}, u32[]{:S(2)}, u32[]{:S(2)}) collective-permute-start(f32[32,256]{1,0:T(8,128)S(1)} %get-tuple-element.93), channel_id=1, source_target_pairs={{10,15},{14,11},{17,22},{21,18},{24,29},{28,25}} | collective-permute-start | bytes 98312 | tf_op jit(solution)/shard_map/ppermute | solution.py:434
  13.5 0.3 lower.10
  13.7 0.7 %collective-permute-start.10 = (f32[32,256]{1,0:T(8,128)S(1)}, f32[32,256]{1,0:T(8,128)S(1)}, u32[]{:S(2)}, u32[]{:S(2)}) collective-permute-start(f32[32,256]{1,0:T(8,128)S(1)} %get-tuple-element.92), channel_id=1, source_target_pairs={{3,15},{7,11},{10,22},{14,18},{17,29},{21,25}} | collective-permute-start | bytes 98312 | tf_op jit(solution)/shard_map/ppermute | solution.py:437
  14.4 0.7 %collective-permute-start.12 = (f32[32,256]{1,0:T(8,128)S(1)}, f32[32,256]{1,0:T(8,128)S(1)}, u32[]{:S(2)}, u32[]{:S(2)}) collective-permute-start(f32[32,256]{1,0:T(8,128)S(1)} %get-tuple-element.97), channel_id=1, source_target_pairs={{10,15},{14,11},{17,22},{21,18},{24,29},{28,25}} | collective-permute-start | bytes 98312 | tf_op jit(solution)/shard_map/ppermute | solution.py:439
  15.2 1.3 %collective-permute-start.14 = (f32[32,256]{1,0:T(8,128)S(1)}, f32[32,256]{1,0:T(8,128)S(1)}, u32[]{:S(2)}, u32[]{:S(2)}) collective-permute-start(f32[32,256]{1,0:T(8,128)S(1)} %get-tuple-element.101), channel_id=1, source_target_pairs={{18,23},{22,19},{25,30},{29,26}} | collective-permute-start | bytes 98312 | tf_op jit(solution)/shard_map/ppermute | solution.py:434
  16.5 0.1 lower.11
  16.6 1.3 %collective-permute-start.13 = (f32[32,256]{1,0:T(8,128)S(1)}, f32[32,256]{1,0:T(8,128)S(1)}, u32[]{:S(2)}, u32[]{:S(2)}) collective-permute-start(f32[32,256]{1,0:T(8,128)S(1)} %get-tuple-element.100), channel_id=1, source_target_pairs={{11,23},{15,19},{18,30},{22,26}} | collective-permute-start | bytes 98312 | tf_op jit(solution)/shard_map/ppermute | solution.py:437
  17.9 1.3 %collective-permute-start.15 = (f32[32,256]{1,0:T(8,128)S(1)}, f32[32,256]{1,0:T(8,128)S(1)}, u32[]{:S(2)}, u32[]{:S(2)}) collective-permute-start(f32[32,256]{1,0:T(8,128)S(1)} %get-tuple-element.105), channel_id=1, source_target_pairs={{18,23},{22,19},{25,30},{29,26}} | collective-permute-start | bytes 98312 | tf_op jit(solution)/shard_map/ppermute | solution.py:439
  19.2 25.8 %collective-permute-done.14.in_ref = f32[32,256]{1,0:T(8,128)S(1)} collective-permute-done((f32[32,256]{1,0:T(8,128)S(1)}, f32[32,256]{1,0:T(8,128)S(1)}, u32[]{:S(2)}, u32[]{:S(2)}) %collective-permute-start.14) | collective-permute-done | bytes 32800 | tf_op jit(solution)/shard_map/ppermute | solution.py:434
  44.9 1.3 %collective-permute-done.13.trace_x_ref = f32[32,256]{1,0:T(8,128)S(1)} collective-permute-done((f32[32,256]{1,0:T(8,128)S(1)}, f32[32,256]{1,0:T(8,128)S(1)}, u32[]{:S(2)}, u32[]{:S(2)}) %collective-permute-start.13) | collective-permute-done | bytes 32800 | tf_op jit(solution)/shard_map/ppermute | solution.py:437
  46.3 2.1 %upper.12 = (f32[32,256]{1,0:T(8,128)S(1)}, f32[32,256]{1,0:T(8,128)S(1)}, f32[256,256]{1,0:T(8,128)S(1)}, f32[256,256]{1,0:T(8,128)S(1)}) custom-call(s32[1]{0:T(128)} %bitcast.9.active_ref, f32[2,256,256]{2,1,0:T(8,128)S(1)} %get-tuple-element.65.modes_ref, ...), custom_call_target="tpu_custom_call", output_to_operand_aliasing={{2}: (5, {}), {3}: (6, {})} | custom-call | flops 2000000000 | bytes 2000000 | tf_op jit(solution)/shard_map/upper/pallas_call | solution.py:401
  48.3 1.3 %collective-permute-start.17 = (f32[32,256]{1,0:T(8,128)S(1)}, f32[32,256]{1,0:T(8,128)S(1)}, u32[]{:S(2)}, u32[]{:S(2)}) collective-permute-start(f32[32,256]{1,0:T(8,128)S(1)} %get-tuple-element.109), channel_id=1, source_target_pairs={{26,31},{30,27}} | collective-permute-start | bytes 98312 | tf_op jit(solution)/shard_map/ppermute | solution.py:434
  49.6 2.1 %lower.12 = (f32[32,256]{1,0:T(8,128)S(1)}, f32[32,256]{1,0:T(8,128)S(1)}, f32[256,256]{1,0:T(8,128)S(1)}, f32[256,256]{1,0:T(8,128)S(1)}) custom-call(s32[1]{0:T(128)} %bitcast.9.active_ref, f32[2,256,256]{2,1,0:T(8,128)S(1)} %get-tuple-element.65.modes_ref, ...), custom_call_target="tpu_custom_call", output_to_operand_aliasing={{2}: (5, {}), {3}: (6, {})} | custom-call | flops 2000000000 | bytes 2000000 | tf_op jit(solution)/shard_map/lower/pallas_call | solution.py:401
  51.7 0.7 %collective-permute-start.16 = (f32[32,256]{1,0:T(8,128)S(1)}, f32[32,256]{1,0:T(8,128)S(1)}, u32[]{:S(2)}, u32[]{:S(2)}) collective-permute-start(f32[32,256]{1,0:T(8,128)S(1)} %get-tuple-element.108), channel_id=1, source_target_pairs={{19,31},{23,27}} | collective-permute-start | bytes 98312 | tf_op jit(solution)/shard_map/ppermute | solution.py:437
  52.4 1.3 %collective-permute-start.18 = (f32[32,256]{1,0:T(8,128)S(1)}, f32[32,256]{1,0:T(8,128)S(1)}, u32[]{:S(2)}, u32[]{:S(2)}) collective-permute-start(f32[32,256]{1,0:T(8,128)S(1)} %get-tuple-element.115), channel_id=1, source_target_pairs={{26,31},{30,27}} | collective-permute-start | bytes 98312 | tf_op jit(solution)/shard_map/ppermute | solution.py:439
  53.7 0.7 %upper.13 = (f32[32,256]{1,0:T(8,128)S(1)}, f32[32,256]{1,0:T(8,128)}, f32[256,256]{1,0:T(8,128)S(1)}, f32[256,256]{1,0:T(8,128)S(1)}) custom-call(s32[1]{0:T(128)} %bitcast.2.active_ref, f32[2,256,256]{2,1,0:T(8,128)S(1)} %get-tuple-element.65.modes_ref, ...), custom_call_target="tpu_custom_call", output_to_operand_aliasing={{2}: (5, {}), {3}: (6, {})} | custom-call | flops 2000000000 | bytes 2000000 | tf_op jit(solution)/shard_map/upper/pallas_call | solution.py:401
  54.4 0.3 collective-permute-done.18.trace_y_ref
  54.7 0.7 %lower.13 = (f32[32,256]{1,0:T(8,128)}, f32[32,256]{1,0:T(8,128)}, f32[256,256]{1,0:T(8,128)S(1)}, f32[256,256]{1,0:T(8,128)S(1)}) custom-call(s32[1]{0:T(128)} %bitcast.2.active_ref, f32[2,256,256]{2,1,0:T(8,128)S(1)} %get-tuple-element.65.modes_ref, ...), custom_call_target="tpu_custom_call", output_to_operand_aliasing={{2}: (5, {}), {3}: (6, {})} | custom-call | flops 2000000000 | bytes 2000000 | tf_op jit(solution)/shard_map/lower/pallas_call | solution.py:401
  55.4 0.2 copy-done.7
  55.6 0.6 edges.1
  56.2 1.9 %collective-permute-start.20 = (f32[2,32,256]{2,1,0:T(8,128)S(1)}, f32[2,32,256]{2,1,0:T(8,128)S(1)}, u32[]{:S(2)}, u32[]{:S(2)}) collective-permute-start(f32[2,32,256]{2,1,0:T(8,128)S(1)} %get-tuple-element.122), channel_id=1, source_target_pairs={{1,4},{5,0},{2,5},{6,1},{3,6},{7,2},{9,12},{13,8},{10,13},{14,9},{... | collective-permute-start | bytes 196616 | tf_op jit(solution)/shard_map/ppermute | solution.py:452
  58.1 1.3 %collective-permute-start.19 = (f32[32,256]{1,0:T(8,128)S(1)}, f32[32,256]{1,0:T(8,128)S(1)}, u32[]{:S(2)}, u32[]{:S(2)}) collective-permute-start(f32[32,256]{1,0:T(8,128)S(1)} %get-tuple-element.121), channel_id=1, source_target_pairs={{8,4},{12,0},{9,5},{13,1},{10,6},{14,2},{11,7},{15,3},{16,12},{20,... | collective-permute-start | bytes 98312 | tf_op jit(solution)/shard_map/ppermute | solution.py:451
  59.4 1.1 %finish.1 = (f32[2,2,16,16,128]{4,3,2,1,0:T(8,128)S(1)}, f32[2,2,16,16,128]{4,3,2,1,0:T(8,128)S(1)}) custom-call(s32[1]{0:T(128)} %bitcast.core_ref, f32[256,256]{1,0:T(8,128)S(1)} %get-tuple-element.112.total0_ref, f32[256,256]{1,0:T(8,128)S(1)} %get-tuple-element.113.term0_ref, f32[256,256]{1,0:T(8,128)S(1)} %get-tuple-element.118.total1_ref, ...), custom_call_target="tpu_custom_call" | custom-call | tf_op jit(solution)/shard_map/finish/pallas_call | solution.py:455
  60.6 0.8 %collective-permute-start.21 = (f32[2,2,16,16,128]{4,3,2,1,0:T(8,128)S(1)}, f32[2,2,16,16,128]{4,3,2,1,0:T(8,128)S(1)}, u32[]{:S(2)}, u32[]{:S(2)}) collective-permute-start(f32[2,2,16,16,128]{4,3,2,1,0:T(8,128)S(1)} %get-tuple-element.123), channel_id=1, source_target_pairs={{0,4},{4,0},{1,5},{5,1},{2,6},{6,2},{3,7},{7,3},{8,12},{12,8},{9,1... | collective-permute-start | bytes 1572872 | tf_op jit(solution)/shard_map/ppermute | solution.py:464
  61.4 2.3 %collective-permute-done.20 = f32[2,32,256]{2,1,0:T(8,128)S(1)} collective-permute-done((f32[2,32,256]{2,1,0:T(8,128)S(1)}, f32[2,32,256]{2,1,0:T(8,128)S(1)}, u32[]{:S(2)}, u32[]{:S(2)}) %collective-permute-start.20) | collective-permute-done | bytes 65568 | tf_op jit(solution)/shard_map/ppermute | solution.py:452
  63.8 0.3 collective-permute-start.22
  64.1 1.0 %collective-permute-done.22.got_edge_ref = f32[64,256]{1,0:T(8,128)S(1)} collective-permute-done((f32[64,256]{1,0:T(8,128)S(1)}, f32[64,256]{1,0:T(8,128)S(1)}, u32[]{:S(2)}, u32[]{:S(2)}) %collective-permute-start.22) | collective-permute-done | bytes 65568 | tf_op jit(solution)/shard_map/ppermute | solution.py:468
  65.1 1.0 %place.1 = (f32[2,2,16,16,128]{4,3,2,1,0:T(8,128)}, f32[2,2,16,16,128]{4,3,2,1,0:T(8,128)}) custom-call(s32[1]{0:T(128)} %bitcast.core_ref, s32[1]{0:T(128)} %bitcast.1.rhs_ref, f32[2,2,16,16,128]{4,3,2,1,0:T(8,128)S(1)} %get-tuple-element.120.keep_ref, f32[2,16,16,128]{3,2,1,0:T(8,128)S(1)} %keep.1.keep_rest_ref, ...), custom_call_target="tpu_custom_call" | custom-call | tf_op jit(solution)/shard_map/place/pallas_call | solution.py:478
  (61 shorter events, 0.7 us)
Async XLA Ops:
  0.6 1.9 %copy-start = (f32[2,16,2]{1,2,0:T(2,128)S(1)}, f32[2,16,2]{1,2,0:T(2,128)}, u32[]{:S(2)}) copy-start(f32[2,16,2]{1,2,0:T(2,128)} %param.15) | copy-start | bytes 772
  0.7 1.1 %copy-start.5 = (f32[16,16,128]{2,1,0:T(8,128)S(1)}, f32[16,16,128]{2,1,0:T(8,128)}, u32[]{:S(2)}) copy-start(f32[16,16,128]{2,1,0:T(8,128)} %slow_ref.1) | copy-start | bytes 393220
  0.7 2.6 %copy-start.3 = (bf16[2,128,384]{2,1,0:T(8,128)(2,1)S(1)}, bf16[2,128,384]{2,1,0:T(8,128)(2,1)}, u32[]{:S(2)}) copy-start(bf16[2,128,384]{2,1,0:T(8,128)(2,1)} %constant.159.clone.forward_ref.refs_1_) | copy-start | bytes 589828
  1.7 1.6 %copy-start.2 = (f32[2,2,16,16,128]{4,3,2,1,0:T(8,128)S(1)}, f32[2,2,16,16,128]{4,3,2,1,0:T(8,128)}, u32[]{:S(2)}) copy-start(f32[2,2,16,16,128]{4,3,2,1,0:T(8,128)} %right_ref.1) | copy-start | bytes 1572868
  1.8 1.6 %copy-start.1 = (bf16[256,256]{1,0:T(8,128)(2,1)S(1)}, bf16[256,256]{1,0:T(8,128)(2,1)}, u32[]{:S(2)}) copy-start(bf16[256,256]{1,0:T(8,128)(2,1)} %constant.161.clone.z_ref.refs_3_) | copy-start | bytes 393220
  1.8 1.6 %copy-start.4 = (f32[256,1]{1,0:T(8,128)S(1)}, f32[256,1]{1,0:T(8,128)}, u32[]{:S(2)}) copy-start(f32[256,1]{1,0:T(8,128)} %constant.165.clone.edge_ref) | copy-start | bytes 3076
  1.8 2.3 %collective-permute-start = (f32[3,16,16,128]{3,2,1,0:T(8,128)S(1)}, f32[3,16,16,128]{3,2,1,0:T(8,128)S(1)}, u32[]{:S(2)}, u32[]{:S(2)}) collective-permute-start(f32[3,16,16,128]{3,2,1,0:T(8,128)S(1)} %pad_maximum_fusion), channel_id=1, source_target_pairs={{0,4},{4,0},{1,5},{5,1},{2,6},{6,2},{3,7},{7,3},{8,12},{12,8},{9,1... | collective-permute-start | bytes 1179656 | tf_op jit(solution)/shard_map/ppermute | solution.py:365
  2.6 0.7 %copy-start.11 = (s32[2,16]{1,0:T(2,128)S(1)}, s32[2,16]{1,0:T(2,128)}, u32[]{:S(2)}) copy-start(s32[2,16]{1,0:T(2,128)} %param.14) | copy-start | bytes 388
  4.1 0.9 %copy-start.9 = (bf16[256,192]{1,0:T(8,128)(2,1)S(1)}, bf16[256,192]{1,0:T(8,128)(2,1)}, u32[]{:S(2)}) copy-start(bf16[256,192]{1,0:T(8,128)(2,1)} %constant.162.clone.refs_4_) | copy-start | bytes 294916
  4.1 1.0 %copy-start.10 = (bf16[64,768]{1,0:T(8,128)(2,1)S(1)}, bf16[64,768]{1,0:T(8,128)(2,1)}, u32[]{:S(2)}) copy-start(bf16[64,768]{1,0:T(8,128)(2,1)} %constant.163.clone.refs_5_) | copy-start | bytes 294916
  4.9 1.0 %copy-start.8 = (f32[2,256,128]{2,1,0:T(8,128)S(1)}, f32[2,256,128]{2,1,0:T(8,128)}, u32[]{:S(2)}) copy-start(f32[2,256,128]{2,1,0:T(8,128)} %constant.158.clone.refs_0_) | copy-start | bytes 786436
  5.0 1.0 %copy-start.6 = (bf16[2,128,384]{2,1,0:T(8,128)(2,1)S(1)}, bf16[2,128,384]{2,1,0:T(8,128)(2,1)}, u32[]{:S(2)}) copy-start(bf16[2,128,384]{2,1,0:T(8,128)(2,1)} %constant.160.clone.refs_2_.backward_ref) | copy-start | bytes 589828
  6.0 2.2 %collective-permute-start.2 = (f32[32,256]{1,0:T(8,128)S(1)}, f32[32,256]{1,0:T(8,128)S(1)}, u32[]{:S(2)}, u32[]{:S(2)}) collective-permute-start(f32[32,256]{1,0:T(8,128)S(1)} %get-tuple-element.69), channel_id=1, source_target_pairs={{0,5},{4,1}} | collective-permute-start | bytes 98312 | tf_op jit(solution)/shard_map/ppermute | solution.py:434
  6.8 1.4 %collective-permute-start.1 = (f32[32,256]{1,0:T(8,128)S(1)}, f32[32,256]{1,0:T(8,128)S(1)}, u32[]{:S(2)}, u32[]{:S(2)}) collective-permute-start(f32[32,256]{1,0:T(8,128)S(1)} %get-tuple-element.68), channel_id=1, source_target_pairs={{0,12},{4,8}} | collective-permute-start | bytes 98312 | tf_op jit(solution)/shard_map/ppermute | solution.py:437
  7.5 1.5 %collective-permute-start.3 = (f32[32,256]{1,0:T(8,128)S(1)}, f32[32,256]{1,0:T(8,128)S(1)}, u32[]{:S(2)}, u32[]{:S(2)}) collective-permute-start(f32[32,256]{1,0:T(8,128)S(1)} %get-tuple-element.73), channel_id=1, source_target_pairs={{0,5},{4,1}} | collective-permute-start | bytes 98312 | tf_op jit(solution)/shard_map/ppermute | solution.py:439
  8.3 2.1 %collective-permute-start.5 = (f32[32,256]{1,0:T(8,128)S(1)}, f32[32,256]{1,0:T(8,128)S(1)}, u32[]{:S(2)}, u32[]{:S(2)}) collective-permute-start(f32[32,256]{1,0:T(8,128)S(1)} %get-tuple-element.77), channel_id=1, source_target_pairs={{1,6},{5,2},{8,13},{12,9}} | collective-permute-start | bytes 98312 | tf_op jit(solution)/shard_map/ppermute | solution.py:434
  9.1 1.4 %collective-permute-start.4 = (f32[32,256]{1,0:T(8,128)S(1)}, f32[32,256]{1,0:T(8,128)S(1)}, u32[]{:S(2)}, u32[]{:S(2)}) collective-permute-start(f32[32,256]{1,0:T(8,128)S(1)} %get-tuple-element.76), channel_id=1, source_target_pairs={{1,13},{5,9},{8,20},{12,16}} | collective-permute-start | bytes 98312 | tf_op jit(solution)/shard_map/ppermute | solution.py:437
  9.7 1.5 %collective-permute-start.6 = (f32[32,256]{1,0:T(8,128)S(1)}, f32[32,256]{1,0:T(8,128)S(1)}, u32[]{:S(2)}, u32[]{:S(2)}) collective-permute-start(f32[32,256]{1,0:T(8,128)S(1)} %get-tuple-element.81), channel_id=1, source_target_pairs={{1,6},{5,2},{8,13},{12,9}} | collective-permute-start | bytes 98312 | tf_op jit(solution)/shard_map/ppermute | solution.py:439
  10.5 2.1 %collective-permute-start.8 = (f32[32,256]{1,0:T(8,128)S(1)}, f32[32,256]{1,0:T(8,128)S(1)}, u32[]{:S(2)}, u32[]{:S(2)}) collective-permute-start(f32[32,256]{1,0:T(8,128)S(1)} %get-tuple-element.85), channel_id=1, source_target_pairs={{2,7},{6,3},{9,14},{13,10},{16,21},{20,17}} | collective-permute-start | bytes 98312 | tf_op jit(solution)/shard_map/ppermute | solution.py:434
  11.3 1.4 %collective-permute-start.7 = (f32[32,256]{1,0:T(8,128)S(1)}, f32[32,256]{1,0:T(8,128)S(1)}, u32[]{:S(2)}, u32[]{:S(2)}) collective-permute-start(f32[32,256]{1,0:T(8,128)S(1)} %get-tuple-element.84), channel_id=1, source_target_pairs={{2,14},{6,10},{9,21},{13,17},{16,28},{20,24}} | collective-permute-start | bytes 98312 | tf_op jit(solution)/shard_map/ppermute | solution.py:437
  12.0 1.5 %collective-permute-start.9 = (f32[32,256]{1,0:T(8,128)S(1)}, f32[32,256]{1,0:T(8,128)S(1)}, u32[]{:S(2)}, u32[]{:S(2)}) collective-permute-start(f32[32,256]{1,0:T(8,128)S(1)} %get-tuple-element.89), channel_id=1, source_target_pairs={{2,7},{6,3},{9,14},{13,10},{16,21},{20,17}} | collective-permute-start | bytes 98312 | tf_op jit(solution)/shard_map/ppermute | solution.py:439
  12.8 2.3 %collective-permute-start.11 = (f32[32,256]{1,0:T(8,128)S(1)}, f32[32,256]{1,0:T(8,128)S(1)}, u32[]{:S(2)}, u32[]{:S(2)}) collective-permute-start(f32[32,256]{1,0:T(8,128)S(1)} %get-tuple-element.93), channel_id=1, source_target_pairs={{10,15},{14,11},{17,22},{21,18},{24,29},{28,25}} | collective-permute-start | bytes 98312 | tf_op jit(solution)/shard_map/ppermute | solution.py:434
  13.7 1.4 %collective-permute-start.10 = (f32[32,256]{1,0:T(8,128)S(1)}, f32[32,256]{1,0:T(8,128)S(1)}, u32[]{:S(2)}, u32[]{:S(2)}) collective-permute-start(f32[32,256]{1,0:T(8,128)S(1)} %get-tuple-element.92), channel_id=1, source_target_pairs={{3,15},{7,11},{10,22},{14,18},{17,29},{21,25}} | collective-permute-start | bytes 98312 | tf_op jit(solution)/shard_map/ppermute | solution.py:437
  14.4 2.1 %collective-permute-start.12 = (f32[32,256]{1,0:T(8,128)S(1)}, f32[32,256]{1,0:T(8,128)S(1)}, u32[]{:S(2)}, u32[]{:S(2)}) collective-permute-start(f32[32,256]{1,0:T(8,128)S(1)} %get-tuple-element.97), channel_id=1, source_target_pairs={{10,15},{14,11},{17,22},{21,18},{24,29},{28,25}} | collective-permute-start | bytes 98312 | tf_op jit(solution)/shard_map/ppermute | solution.py:439
  15.2 29.8 %collective-permute-start.14 = (f32[32,256]{1,0:T(8,128)S(1)}, f32[32,256]{1,0:T(8,128)S(1)}, u32[]{:S(2)}, u32[]{:S(2)}) collective-permute-start(f32[32,256]{1,0:T(8,128)S(1)} %get-tuple-element.101), channel_id=1, source_target_pairs={{18,23},{22,19},{25,30},{29,26}} | collective-permute-start | bytes 98312 | tf_op jit(solution)/shard_map/ppermute | solution.py:434
  16.6 29.7 %collective-permute-start.13 = (f32[32,256]{1,0:T(8,128)S(1)}, f32[32,256]{1,0:T(8,128)S(1)}, u32[]{:S(2)}, u32[]{:S(2)}) collective-permute-start(f32[32,256]{1,0:T(8,128)S(1)} %get-tuple-element.100), channel_id=1, source_target_pairs={{11,23},{15,19},{18,30},{22,26}} | collective-permute-start | bytes 98312 | tf_op jit(solution)/shard_map/ppermute | solution.py:437
  17.9 31.7 %collective-permute-start.15 = (f32[32,256]{1,0:T(8,128)S(1)}, f32[32,256]{1,0:T(8,128)S(1)}, u32[]{:S(2)}, u32[]{:S(2)}) collective-permute-start(f32[32,256]{1,0:T(8,128)S(1)} %get-tuple-element.105), channel_id=1, source_target_pairs={{18,23},{22,19},{25,30},{29,26}} | collective-permute-start | bytes 98312 | tf_op jit(solution)/shard_map/ppermute | solution.py:439
  48.3 5.4 %collective-permute-start.17 = (f32[32,256]{1,0:T(8,128)S(1)}, f32[32,256]{1,0:T(8,128)S(1)}, u32[]{:S(2)}, u32[]{:S(2)}) collective-permute-start(f32[32,256]{1,0:T(8,128)S(1)} %get-tuple-element.109), channel_id=1, source_target_pairs={{26,31},{30,27}} | collective-permute-start | bytes 98312 | tf_op jit(solution)/shard_map/ppermute | solution.py:434
  51.7 2.0 %collective-permute-start.16 = (f32[32,256]{1,0:T(8,128)S(1)}, f32[32,256]{1,0:T(8,128)S(1)}, u32[]{:S(2)}, u32[]{:S(2)}) collective-permute-start(f32[32,256]{1,0:T(8,128)S(1)} %get-tuple-element.108), channel_id=1, source_target_pairs={{19,31},{23,27}} | collective-permute-start | bytes 98312 | tf_op jit(solution)/shard_map/ppermute | solution.py:437
  52.4 2.3 %collective-permute-start.18 = (f32[32,256]{1,0:T(8,128)S(1)}, f32[32,256]{1,0:T(8,128)S(1)}, u32[]{:S(2)}, u32[]{:S(2)}) collective-permute-start(f32[32,256]{1,0:T(8,128)S(1)} %get-tuple-element.115), channel_id=1, source_target_pairs={{26,31},{30,27}} | collective-permute-start | bytes 98312 | tf_op jit(solution)/shard_map/ppermute | solution.py:439
  54.7 0.9 %copy-start.7 = (bf16[64,768]{1,0:T(8,128)(2,1)S(1)}, bf16[64,768]{1,0:T(8,128)(2,1)}, u32[]{:S(2)}) copy-start(bf16[64,768]{1,0:T(8,128)(2,1)} %constant.164.clone.first_ref) | copy-start | bytes 294916
  56.2 7.5 %collective-permute-start.20 = (f32[2,32,256]{2,1,0:T(8,128)S(1)}, f32[2,32,256]{2,1,0:T(8,128)S(1)}, u32[]{:S(2)}, u32[]{:S(2)}) collective-permute-start(f32[2,32,256]{2,1,0:T(8,128)S(1)} %get-tuple-element.122), channel_id=1, source_target_pairs={{1,4},{5,0},{2,5},{6,1},{3,6},{7,2},{9,12},{13,8},{10,13},{14,9},{... | collective-permute-start | bytes 196616 | tf_op jit(solution)/shard_map/ppermute | solution.py:452
  58.1 5.6 %collective-permute-start.19 = (f32[32,256]{1,0:T(8,128)S(1)}, f32[32,256]{1,0:T(8,128)S(1)}, u32[]{:S(2)}, u32[]{:S(2)}) collective-permute-start(f32[32,256]{1,0:T(8,128)S(1)} %get-tuple-element.121), channel_id=1, source_target_pairs={{8,4},{12,0},{9,5},{13,1},{10,6},{14,2},{11,7},{15,3},{16,12},{20,... | collective-permute-start | bytes 98312 | tf_op jit(solution)/shard_map/ppermute | solution.py:451
  60.6 4.5 %collective-permute-start.21 = (f32[2,2,16,16,128]{4,3,2,1,0:T(8,128)S(1)}, f32[2,2,16,16,128]{4,3,2,1,0:T(8,128)S(1)}, u32[]{:S(2)}, u32[]{:S(2)}) collective-permute-start(f32[2,2,16,16,128]{4,3,2,1,0:T(8,128)S(1)} %get-tuple-element.123), channel_id=1, source_target_pairs={{0,4},{4,0},{1,5},{5,1},{2,6},{6,2},{3,7},{7,3},{8,12},{12,8},{9,1... | collective-permute-start | bytes 1572872 | tf_op jit(solution)/shard_map/ppermute | solution.py:464
  63.8 1.3 %collective-permute-start.22 = (f32[64,256]{1,0:T(8,128)S(1)}, f32[64,256]{1,0:T(8,128)S(1)}, u32[]{:S(2)}, u32[]{:S(2)}) collective-permute-start(f32[64,256]{1,0:T(8,128)S(1)} %pad_maximum_fusion.1), channel_id=1, source_target_pairs={{0,4},{4,0},{1,5},{5,1},{2,6},{6,2},{3,7},{7,3},{8,12},{12,8},{9,1... | collective-permute-start | bytes 196616 | tf_op jit(solution)/shard_map/ppermute | solution.py:468

commit v7 on v6

--- a/solution.py
+++ b/solution.py
@@ -54,8 +54,11 @@
     inverse = np.stack([real_part / denominator, KAPPA * DAMPING / denominator]).astype(np.float32)
 
     parity = [np.kron(sine_x[order[p * half : (p + 1) * half]][:, :half], sine_y) for p in (0, 1)]
-    forward = np.stack([left_factor(m) for m in parity])
-    backward = np.stack([left_factor(m.T) for m in parity])
+    cut = half * size_y // 2
+    forward, backward = [
+        np.stack([[left_factor(m[:, :cut]), left_factor(m[:, cut:])] for m in matrices])
+        for matrices in (parity, [m.T for m in parity])
+    ]
     high_z, low_z = halves(sine_z)
     right_z = np.concatenate([np.concatenate([high_z, low_z], axis=1)] * 2, axis=0)
 
@@ -103,9 +106,13 @@
     return high, (values - high.astype(F32)).astype(BF16)
 
 
+def stacked(values):
+    high, low = split(values)
+    return jnp.concatenate([high, low, high], axis=0)
+
+
 def left_product(matrix, values):
-    high, low = split(values)
-    return jnp.dot(matrix, jnp.concatenate([high, low, high], axis=0), preferred_element_type=F32)
+    return jnp.dot(matrix, stacked(values), preferred_element_type=F32)
 
 
 def z_transform(field, right_z):
@@ -117,19 +124,31 @@
     return jnp.concatenate([total[:rows], total[rows:]], axis=1)
 
 
-def to_modes(field, forward):
-    count = field.shape[0] // 2
-    first, second = field[:count], field[count:]
-    return jnp.concatenate(
-        [left_product(forward[0], first + second), left_product(forward[1], first - second)], axis=0
-    )
+def to_modes(first, second, forward):
+    return [
+        sum(left_product(forward[p, h], join(first[h], second[h])) for h in range(2))
+        for p, join in enumerate((jnp.add, jnp.subtract))
+    ]
 
 
 def to_cells(modes, backward):
-    count = modes.shape[0] // 2
-    even = left_product(backward[0], modes[:count])
-    odd = left_product(backward[1], modes[count:])
-    return jnp.concatenate([even + odd, even - odd], axis=0)
+    even, odd = [
+        sum(left_product(backward[p, h], modes[p][h]) for h in range(2)) for p in range(2)
+    ]
+    return even + odd, even - odd
+
+
+def in_two(values):
+    count = values.shape[0] // 2
+    return values[:count], values[count:]
+
+
+def in_parities(modes):
+    return [in_two(part) for part in in_two(modes)]
+
+
+def whole_field(first, second):
+    return jnp.concatenate([first, second], axis=0)
 
 
 def times(real_part, imag_part, field):
@@ -141,22 +160,27 @@
 
 
 def solve_modes(source_modes, contrast, t):
-    term = times(t["inverse"][0], t["inverse"][1], source_modes)
+    count = source_modes.shape[0] // 4
+    term = in_parities(times(t["inverse"][0], t["inverse"][1], source_modes))
     total = term
     for _ in range(2):
-        cells = apply_contrast(to_cells(term, t["backward"]), contrast, t["right_z"])
-        term = times(t["inverse"][0], t["inverse"][1], to_modes(cells, t["forward"]))
-        total = total + term
-    return total, term
-
-
-def apply_contrast(field, contrast, right_z, block=64):
-    done = []
-    for start in range(0, field.shape[0], block):
-        here = slice(start, start + block)
-        cells = times(contrast[0, here], contrast[1, here], z_transform(field[here], right_z))
-        done.append(z_transform(cells, right_z))
-    return jnp.concatenate(done, axis=0)
+        first, second = [in_two(cells) for cells in to_cells(term, t["backward"])]
+        parts = []
+        for h in range(2):
+            here = [slice(at, at + count) for at in (h * count, (h + 2) * count)]
+            factor = [jnp.concatenate([contrast[c, rows] for rows in here], axis=0) for c in range(2)]
+            cells = z_transform(jnp.concatenate([first[h], second[h]], axis=0), t["right_z"])
+            parts.append(in_two(z_transform(times(*factor, cells), t["right_z"])))
+        modes = to_modes(*zip(*parts), t["forward"])
+        term = []
+        for p in range(2):
+            halves = []
+            for h, part in enumerate(in_two(modes[p])):
+                here = slice((2 * p + h) * count, (2 * p + h + 1) * count)
+                halves.append(times(t["inverse"][0, here], t["inverse"][1, here], part))
+            term.append(halves)
+        total = [[a + b for a, b in zip(*pair)] for pair in zip(total, term)]
+    return [jnp.concatenate([part for pair in both for part in pair], axis=0) for both in (total, term)]
 
 
 PREP = ("edge", "forward", "right_z")
@@ -188,7 +212,8 @@
         jnp.concatenate([at_row] * 3, axis=1), jnp.concatenate(spread, axis=0),
         (((1,), (1,)), ((), ())), preferred_element_type=F32,
     )
-    modes_ref[...] = to_modes(z_transform(field + dense, right_z), forward)
+    first, second = [in_two(part) for part in in_two(z_transform(field + dense, right_z))]
+    modes_ref[...] = jnp.concatenate(to_modes(first, second, forward), axis=0)
 
 
 def prep_kernel(cells_x, rhs_ref, right_ref, slow_ref, place_ref, depth_ref, amp_ref, edge_ref,
@@ -218,9 +243,9 @@
     return modes + left_product(enter, jnp.concatenate([trace_x, trace_y], axis=0))
 
 
-def beat_kernel(tile, active_ref, modes_ref, contrast_ref, trace_x_ref, trace_y_ref, total_ref, term_ref, *refs):
+def beat_kernel(tile, sends, active_ref, modes_ref, contrast_ref, trace_x_ref, trace_y_ref, total_ref, term_ref, *refs):
     t = {name: ref for name, ref in zip(BEAT, refs)}
-    out_x_ref, out_y_ref, new_total_ref, new_term_ref = refs[len(BEAT) :]
+    new_total_ref, new_term_ref, *out_refs = refs[len(BEAT) :]
 
     @pl.when(active_ref[0] == 1)
     def _():
@@ -229,10 +254,11 @@
         total, term = solve_modes(source, contrast_ref.at[tile], local)
         new_total_ref[...] = total
         new_term_ref[...] = term
-        out = left_product(t["leave"][...], total)
-        count = out_x_ref.shape[0]
-        out_x_ref[...] = out[:count]
-        out_y_ref[...] = out[count:]
+        if sends:
+            count = trace_x_ref.shape[0]
+            out = left_product(t["leave"][...], total)
+            for out_ref, part in zip(out_refs, (out[:count], out[count:])):
+                out_ref[...] = part
 
     @pl.when(active_ref[0] == 0)
     def _():
@@ -258,8 +284,10 @@
     _, _, _, size_x, size_y, cells_z = both_ref.shape
     right_z = z_ref[...]
     for tile, (total_ref, term_ref) in enumerate(((total0_ref, term0_ref), (total1_ref, term1_ref))):
-        wave = z_transform(to_cells(total_ref[...], backward_ref), right_z)
-        rest = z_transform(to_cells(term_ref[...], backward_ref), right_z)
+        wave, rest = [
+            z_transform(whole_field(*to_cells(in_parities(ref[...]), backward_ref)), right_z)
+            for ref in (total_ref, term_ref)
+        ]
         rest = times(contrast_ref[tile, 0], contrast_ref[tile, 1], rest)
         for place, x in enumerate(cells_x):
             here = slice(place * size_y, (place + 1) * size_y)
@@ -295,20 +323,27 @@
     add_later(rest_ref, edge_x_ref[...], edge_y_ref[...], (core_ref[0] == 1).astype(F32))
 
 
-def place_kernel(core_ref, rhs_ref, keep_ref, keep_rest_ref, got_ref, got_edge_ref, wave_ref, rest_ref, work_ref, sems):
+def place_wave_kernel(rhs_ref, keep_ref, got_ref, wave_ref, sems):
     rhs = rhs_ref[0]
-    count = got_edge_ref.shape[0] // 2
     copies = [
         pltpu.make_async_copy(keep_ref.at[0], wave_ref.at[rhs], sems.at[0]),
         pltpu.make_async_copy(got_ref.at[0], wave_ref.at[1 - rhs], sems.at[1]),
-        pltpu.make_async_copy(keep_rest_ref, rest_ref.at[rhs], sems.at[2]),
     ]
     for copy in copies:
         copy.start()
+    for copy in copies:
+        copy.wait()
+
+
+def place_rest_kernel(core_ref, rhs_ref, keep_rest_ref, got_ref, got_edge_ref, rest_ref, work_ref, sems):
+    rhs = rhs_ref[0]
+    count = got_edge_ref.shape[0] // 2
+    copies = [pltpu.make_async_copy(keep_rest_ref, rest_ref.at[rhs], sems.at[0])]
+    copies[0].start()
     work_ref[...] = got_ref[1]
     add_later(work_ref, got_edge_ref[:count], got_edge_ref[count:], (core_ref[0] == 1).astype(F32))
-    copies.append(pltpu.make_async_copy(work_ref, rest_ref.at[1 - rhs], sems.at[3]))
-    copies[-1].start()
+    copies.append(pltpu.make_async_copy(work_ref, rest_ref.at[1 - rhs], sems.at[1]))
+    copies[1].start()
     for copy in copies:
         copy.wait()
 
@@ -384,6 +419,7 @@
         in_specs=[scalars()] + [whole()] * 8,
         out_specs=(whole(), whole()),
         compiler_params=PARAMS,
+        cost_estimate=SOLVE_COST,
         name="prep",
     )(rhs_ref, right_side, slowness, places[0], depth, amplitudes, *prep_tables)
     modes, contrast = pl.pallas_call(
@@ -392,23 +428,24 @@
         in_specs=[scalars()] + [whole()] * 9,
         out_specs=(whole(), whole()),
         compiler_params=PARAMS,
+        cost_estimate=SOLVE_COST,
         name="prep_other",
     )(core_ref, swapped, own_modes, own_contrast, places[1], depth, amplitudes, *prep_tables)
 
     beat_tables = [t[name] for name in BEAT]
 
-    def solve(tile, active, trace_x, trace_y, state):
-        out_x, out_y, *state = pl.pallas_call(
-            functools.partial(beat_kernel, tile),
-            out_shape=(shaped(*zero_x.shape), shaped(*zero_y.shape)) + (shaped(rows, 2 * cells_z),) * 2,
+    def solve(tile, active, trace_x, trace_y, state, sends):
+        total, term, *out = pl.pallas_call(
+            functools.partial(beat_kernel, tile, sends),
+            out_shape=(shaped(rows, 2 * cells_z),) * 2 + (shaped(*zero_x.shape), shaped(*zero_y.shape))[:sends],
             in_specs=[scalars()] + [whole()] * (6 + len(BEAT)),
-            out_specs=(whole(),) * 4,
-            input_output_aliases={5: 2, 6: 3},
+            out_specs=(whole(),) * (2 + sends),
+            input_output_aliases={5: 0, 6: 1},
             compiler_params=PARAMS,
             cost_estimate=SOLVE_COST,
             name="upper" if tile == 0 else "lower",
         )(active, modes, contrast, trace_x, trace_y, *state, *beat_tables)
-        return out_x, out_y, state
+        return (total, term), out
 
     def hand_on(trace):
         return pl.pallas_call(
@@ -429,14 +466,15 @@
         here = [(k, beat - k) for k in range(chips) if 0 <= beat - k < grid_cols]
         along_x = between([((k, j), (k + 1, j)) for k, j in here if k + 1 < chips])
         along_y = between([((k, j), (k, j + 1)) for k, j in here if j + 1 < grid_cols])
-        inner_x, out_y0, states[0] = solve(0, active, trace_x, trace_y0, states[0])
+        more = beat < chips + grid_cols - 2
+        states[0], (inner_x, *out_y0) = solve(0, active, trace_x, trace_y0, states[0], 1 + more)
         if along_y:
-            trace_y0 = hand_on(lax.ppermute(out_y0, axes, along_y))
-        out_x, out_y1, states[1] = solve(1, active, inner_x, trace_y1, states[1])
+            trace_y0 = hand_on(lax.ppermute(out_y0[0], axes, along_y))
+        states[1], out = solve(1, active, inner_x, trace_y1, states[1], 2 * more)
         if along_x:
-            trace_x = lax.ppermute(out_x, axes, along_x)
+            trace_x = lax.ppermute(out[0], axes, along_x)
         if along_y:
-            trace_y1 = lax.ppermute(out_y1, axes, along_y)
+            trace_y1 = lax.ppermute(out[1], axes, along_y)
 
     edge_x, edge_y = pl.pallas_call(
         edge_kernel,
@@ -475,18 +513,29 @@
         cost_estimate=KEEP_COST,
         name="keep",
     )(core_ref, keep, after_x, keep_y)
-    return pl.pallas_call(
-        place_kernel,
-        out_shape=(shaped(*right_side.shape), shaped(*right_side.shape)),
-        in_specs=[scalars()] * 2 + [whole()] * 4,
-        out_specs=(anywhere(), anywhere()),
+    wavefield = pl.pallas_call(
+        place_wave_kernel,
+        out_shape=shaped(*right_side.shape),
+        in_specs=[scalars()] + [whole()] * 2,
+        out_specs=anywhere(),
+        scratch_shapes=[pltpu.SemaphoreType.DMA((2,))],
+        compiler_params=PARAMS,
+        cost_estimate=KEEP_COST,
+        name="place_wave",
+    )(rhs_ref, keep, got)
+    residual = pl.pallas_call(
+        place_rest_kernel,
+        out_shape=shaped(*right_side.shape),
+        in_specs=[scalars()] * 2 + [whole()] * 3,
+        out_specs=anywhere(),
         scratch_shapes=[
             pltpu.VMEM((2, size_x, size_y, cells_z), F32),
-            pltpu.SemaphoreType.DMA((4,)),
+            pltpu.SemaphoreType.DMA((2,)),
         ],
         compiler_params=PARAMS,
-        name="place",
-    )(core_ref, rhs_ref, keep, keep_rest, got, got_edge)
+        name="place_rest",
+    )(core_ref, rhs_ref, keep_rest, got, got_edge)
+    return wavefield, residual
 
 
 def solution(mesh):

time: 67.5 us -> 66.8 us (0.990)
  waiting for transfers between devices: 30.7 us -> 29.9 us
    ppermute x18, waiting for transfers between devices: 27.4 us -> 28.2 us  [the longest x6 26 us: body(): trace_y0 = hand_on(lax.ppermute(out_y0[0], axes, along_y))]
    ppermute x1, waiting for transfers between devices: 0.96 us -> 0.13 us  [body(): lax.ppermute(jnp.concatenate([after_x, pass_y], axis=0), axes, own)]
    ppermute x1, waiting for transfers between devices: 2.34 us -> 1.53 us  [body(): lax.ppermute(edge_y, axes, between([((k, j), (k, j - 1)) for k, j in ever...]
    pallas_call x15 -> x16, Pallas kernels: 7.46 us -> 6.87 us  [the longest x14 5.26 us: solve(): pl.pallas_call(functools.partial(beat_kernel, tile, sends), out_shape=(sh...]
where the time goes in v7:
time: 66.8 us; the launch traced here: 65.6 us
  waiting for transfers between devices  29.9 us (45%)
  starting transfers between devices  20.2 us (30%)
  Pallas kernels  10.2 us (15%)
  local copies, waits for them, and re-layouts  3.65 us (5%)
  between operations  1.55 us (2%)
    ppermute x6, waiting for transfers between devices, body(): trace_y0 = hand_on(lax.ppermute(out_y0[0], axes, along_y))  26 us
    pallas_call x14, Pallas kernels, solve(): pl.pallas_call(functools.partial(beat_kernel, tile, sends), out_shape=(sh...  5.26 us
    ppermute x6, starting transfers between devices, body(): trace_y0 = hand_on(lax.ppermute(out_y0[0], axes, along_y))  5.24 us
    ppermute x6, starting transfers between devices, body(): trace_y1 = lax.ppermute(out[1], axes, along_y)  5.24 us
    ppermute x6, starting transfers between devices, body(): trace_x = lax.ppermute(out[0], axes, along_x)  4.62 us
    unnamed x24, local copies, waits for them, and re-layouts  2.55 us
    ppermute x1, starting transfers between devices, body(): lax.ppermute(edge_y, axes, between([((k, j), (k, j - 1)) for k, j in ever...  1.92 us
    ppermute x1, waiting for transfers between devices, body(): lax.ppermute(edge_y, axes, between([((k, j), (k, j - 1)) for k, j in ever...  1.53 us
  transfers between devices with their start and end apart: 23, of which 5 were waited for; matrix products, arithmetic and copies ran while one was open for 0% of the time, Pallas kernels for 12%

profile of v7, /device:TPU:29, one launch (start us, length us, event | category | flops | bytes accessed | tf_op | source)
XLA Modules:
  0.0 65.6 jit_solution(3312942111372020858)
XLA Ops:
  0.7 1.0 %dynamic-slice_bitcast_fusion = f32[2,16,16,128]{3,2,1,0:T(8,128)S(1)} fusion(f32[2,2,16,16,128]{4,3,2,1,0:T(8,128)} %right_ref.1, s32[]{:T(128)S(6)} %select_n.74), kind=kLoop, calls=%fused_computation.1 | loop fusion | bytes 524292 | tf_op jit(solution)/shard_map/jit(dynamic_index_in_dim)/squeeze | solution.py:399
  1.8 0.7 %collective-permute-start = (f32[3,16,16,128]{3,2,1,0:T(8,128)S(1)}, f32[3,16,16,128]{3,2,1,0:T(8,128)S(1)}, u32[]{:S(2)}, u32[]{:S(2)}) collective-permute-start(f32[3,16,16,128]{3,2,1,0:T(8,128)S(1)} %pad_maximum_fusion), channel_id=1, source_target_pairs={{0,4},{4,0},{1,5},{5,1},{2,6},{6,2},{3,7},{7,3},{8,12},{12,8},{9,1... | collective-permute-start | bytes 1179656 | tf_op jit(solution)/shard_map/ppermute | solution.py:400
  2.6 0.7 %copy-done.11 = s32[2,16]{1,0:T(2,128)S(1)} copy-done((s32[2,16]{1,0:T(2,128)S(1)}, s32[2,16]{1,0:T(2,128)}, u32[]{:S(2)}) %copy-start.11) | copy-done | bytes 152
  3.3 0.8 %prep.1 = (f32[256,256]{1,0:T(8,128)S(1)}, f32[2,256,128]{2,1,0:T(8,128)S(1)}) custom-call(s32[1]{0:T(128)} %bitcast.rhs_ref, f32[2,2,16,16,128]{4,3,2,1,0:T(8,128)S(1)} %copy-done.3, f32[16,16,128]{2,1,0:T(8,128)S(1)} %copy-done.4, s32[1,16]{1,0:T(1,128)S(1)} %and_select_fusion.2.place_ref, s32[1,16]{1,0:T(1,128)S(1)} %and_select_fusion.1.depth_ref, ...), custom_call_target="tpu_custom_call" | custom-call | flops 2000000000 | bytes 2000000 | tf_op jit(solution)/shard_map/prep/pallas_call | solution.py:416
  4.1 0.8 %prep_other.1 = (f32[2,256,256]{2,1,0:T(8,128)S(1)}, f32[2,2,256,128]{3,2,1,0:T(8,128)S(1)}) custom-call(s32[1]{0:T(128)} %bitcast.1.core_ref, f32[3,16,16,128]{3,2,1,0:T(8,128)S(1)} %collective-permute-done.swap_ref, f32[256,256]{1,0:T(8,128)S(1)} %get-tuple-element.63.own_modes_ref, f32[2,256,128]{2,1,0:T(8,128)S(1)} %get-tuple-element.64.own_contrast_ref, ...), custom_call_target="tpu_custom_call" | custom-call | flops 2000000000 | bytes 2000000 | tf_op jit(solution)/shard_map/prep_other/pallas_call | solution.py:425
  5.1 0.8 %copy-done.2 = bf16[2,2,128,192]{3,2,1,0:T(8,128)(2,1)S(1)} copy-done((bf16[2,2,128,192]{3,2,1,0:T(8,128)(2,1)S(1)}, bf16[2,2,128,192]{3,2,1,0:T(8,128)(2,1)}, u32[]{:S(2)}) %copy-start.2) | copy-done | bytes 196632
  6.1 0.7 %collective-permute-start.2 = (f32[32,256]{1,0:T(8,128)S(1)}, f32[32,256]{1,0:T(8,128)S(1)}, u32[]{:S(2)}, u32[]{:S(2)}) collective-permute-start(f32[32,256]{1,0:T(8,128)S(1)} %get-tuple-element.69), channel_id=1, source_target_pairs={{0,5},{4,1}} | collective-permute-start | bytes 98312 | tf_op jit(solution)/shard_map/ppermute | solution.py:472
  6.8 0.1 lower.7
  6.9 0.7 %collective-permute-start.1 = (f32[32,256]{1,0:T(8,128)S(1)}, f32[32,256]{1,0:T(8,128)S(1)}, u32[]{:S(2)}, u32[]{:S(2)}) collective-permute-start(f32[32,256]{1,0:T(8,128)S(1)} %get-tuple-element.68), channel_id=1, source_target_pairs={{0,12},{4,8}} | collective-permute-start | bytes 98312 | tf_op jit(solution)/shard_map/ppermute | solution.py:475
  7.5 0.7 %collective-permute-start.3 = (f32[32,256]{1,0:T(8,128)S(1)}, f32[32,256]{1,0:T(8,128)S(1)}, u32[]{:S(2)}, u32[]{:S(2)}) collective-permute-start(f32[32,256]{1,0:T(8,128)S(1)} %get-tuple-element.73), channel_id=1, source_target_pairs={{0,5},{4,1}} | collective-permute-start | bytes 98312 | tf_op jit(solution)/shard_map/ppermute | solution.py:477
  8.3 0.1 upper.8
  8.3 0.7 %collective-permute-start.5 = (f32[32,256]{1,0:T(8,128)S(1)}, f32[32,256]{1,0:T(8,128)S(1)}, u32[]{:S(2)}, u32[]{:S(2)}) collective-permute-start(f32[32,256]{1,0:T(8,128)S(1)} %get-tuple-element.77), channel_id=1, source_target_pairs={{1,6},{5,2},{8,13},{12,9}} | collective-permute-start | bytes 98312 | tf_op jit(solution)/shard_map/ppermute | solution.py:472
  9.0 0.1 lower.8
  9.1 0.7 %collective-permute-start.4 = (f32[32,256]{1,0:T(8,128)S(1)}, f32[32,256]{1,0:T(8,128)S(1)}, u32[]{:S(2)}, u32[]{:S(2)}) collective-permute-start(f32[32,256]{1,0:T(8,128)S(1)} %get-tuple-element.76), channel_id=1, source_target_pairs={{1,13},{5,9},{8,20},{12,16}} | collective-permute-start | bytes 98312 | tf_op jit(solution)/shard_map/ppermute | solution.py:475
  9.8 0.7 %collective-permute-start.6 = (f32[32,256]{1,0:T(8,128)S(1)}, f32[32,256]{1,0:T(8,128)S(1)}, u32[]{:S(2)}, u32[]{:S(2)}) collective-permute-start(f32[32,256]{1,0:T(8,128)S(1)} %get-tuple-element.81), channel_id=1, source_target_pairs={{1,6},{5,2},{8,13},{12,9}} | collective-permute-start | bytes 98312 | tf_op jit(solution)/shard_map/ppermute | solution.py:477
  10.5 0.1 upper.9
  10.6 0.7 %collective-permute-start.8 = (f32[32,256]{1,0:T(8,128)S(1)}, f32[32,256]{1,0:T(8,128)S(1)}, u32[]{:S(2)}, u32[]{:S(2)}) collective-permute-start(f32[32,256]{1,0:T(8,128)S(1)} %get-tuple-element.85), channel_id=1, source_target_pairs={{2,7},{6,3},{9,14},{13,10},{16,21},{20,17}} | collective-permute-start | bytes 98312 | tf_op jit(solution)/shard_map/ppermute | solution.py:472
  11.3 0.1 lower.9
  11.3 0.7 %collective-permute-start.7 = (f32[32,256]{1,0:T(8,128)S(1)}, f32[32,256]{1,0:T(8,128)S(1)}, u32[]{:S(2)}, u32[]{:S(2)}) collective-permute-start(f32[32,256]{1,0:T(8,128)S(1)} %get-tuple-element.84), channel_id=1, source_target_pairs={{2,14},{6,10},{9,21},{13,17},{16,28},{20,24}} | collective-permute-start | bytes 98312 | tf_op jit(solution)/shard_map/ppermute | solution.py:475
  12.0 0.7 %collective-permute-start.9 = (f32[32,256]{1,0:T(8,128)S(1)}, f32[32,256]{1,0:T(8,128)S(1)}, u32[]{:S(2)}, u32[]{:S(2)}) collective-permute-start(f32[32,256]{1,0:T(8,128)S(1)} %get-tuple-element.89), channel_id=1, source_target_pairs={{2,7},{6,3},{9,14},{13,10},{16,21},{20,17}} | collective-permute-start | bytes 98312 | tf_op jit(solution)/shard_map/ppermute | solution.py:477
  12.7 0.1 upper.10
  12.8 0.7 %collective-permute-start.11 = (f32[32,256]{1,0:T(8,128)S(1)}, f32[32,256]{1,0:T(8,128)S(1)}, u32[]{:S(2)}, u32[]{:S(2)}) collective-permute-start(f32[32,256]{1,0:T(8,128)S(1)} %get-tuple-element.93), channel_id=1, source_target_pairs={{10,15},{14,11},{17,22},{21,18},{24,29},{28,25}} | collective-permute-start | bytes 98312 | tf_op jit(solution)/shard_map/ppermute | solution.py:472
  13.5 0.3 lower.10
  13.8 0.7 %collective-permute-start.10 = (f32[32,256]{1,0:T(8,128)S(1)}, f32[32,256]{1,0:T(8,128)S(1)}, u32[]{:S(2)}, u32[]{:S(2)}) collective-permute-start(f32[32,256]{1,0:T(8,128)S(1)} %get-tuple-element.92), channel_id=1, source_target_pairs={{3,15},{7,11},{10,22},{14,18},{17,29},{21,25}} | collective-permute-start | bytes 98312 | tf_op jit(solution)/shard_map/ppermute | solution.py:475
  14.4 0.7 %collective-permute-start.12 = (f32[32,256]{1,0:T(8,128)S(1)}, f32[32,256]{1,0:T(8,128)S(1)}, u32[]{:S(2)}, u32[]{:S(2)}) collective-permute-start(f32[32,256]{1,0:T(8,128)S(1)} %get-tuple-element.97), channel_id=1, source_target_pairs={{10,15},{14,11},{17,22},{21,18},{24,29},{28,25}} | collective-permute-start | bytes 98312 | tf_op jit(solution)/shard_map/ppermute | solution.py:477
  15.2 1.3 %collective-permute-start.14 = (f32[32,256]{1,0:T(8,128)S(1)}, f32[32,256]{1,0:T(8,128)S(1)}, u32[]{:S(2)}, u32[]{:S(2)}) collective-permute-start(f32[32,256]{1,0:T(8,128)S(1)} %get-tuple-element.101), channel_id=1, source_target_pairs={{18,23},{22,19},{25,30},{29,26}} | collective-permute-start | bytes 98312 | tf_op jit(solution)/shard_map/ppermute | solution.py:472
  16.5 0.1 lower.11
  16.6 1.3 %collective-permute-start.13 = (f32[32,256]{1,0:T(8,128)S(1)}, f32[32,256]{1,0:T(8,128)S(1)}, u32[]{:S(2)}, u32[]{:S(2)}) collective-permute-start(f32[32,256]{1,0:T(8,128)S(1)} %get-tuple-element.100), channel_id=1, source_target_pairs={{11,23},{15,19},{18,30},{22,26}} | collective-permute-start | bytes 98312 | tf_op jit(solution)/shard_map/ppermute | solution.py:475
  17.9 1.3 %collective-permute-start.15 = (f32[32,256]{1,0:T(8,128)S(1)}, f32[32,256]{1,0:T(8,128)S(1)}, u32[]{:S(2)}, u32[]{:S(2)}) collective-permute-start(f32[32,256]{1,0:T(8,128)S(1)} %get-tuple-element.105), channel_id=1, source_target_pairs={{18,23},{22,19},{25,30},{29,26}} | collective-permute-start | bytes 98312 | tf_op jit(solution)/shard_map/ppermute | solution.py:477
  19.2 26.0 %collective-permute-done.14.in_ref = f32[32,256]{1,0:T(8,128)S(1)} collective-permute-done((f32[32,256]{1,0:T(8,128)S(1)}, f32[32,256]{1,0:T(8,128)S(1)}, u32[]{:S(2)}, u32[]{:S(2)}) %collective-permute-start.14) | collective-permute-done | bytes 32800 | tf_op jit(solution)/shard_map/ppermute | solution.py:472
  45.2 1.3 %collective-permute-done.13.trace_x_ref = f32[32,256]{1,0:T(8,128)S(1)} collective-permute-done((f32[32,256]{1,0:T(8,128)S(1)}, f32[32,256]{1,0:T(8,128)S(1)}, u32[]{:S(2)}, u32[]{:S(2)}) %collective-permute-start.13) | collective-permute-done | bytes 32800 | tf_op jit(solution)/shard_map/ppermute | solution.py:475
  46.5 2.1 %upper.12 = (f32[256,256]{1,0:T(8,128)S(1)}, f32[256,256]{1,0:T(8,128)S(1)}, f32[32,256]{1,0:T(8,128)S(1)}, f32[32,256]{1,0:T(8,128)S(1)}) custom-call(s32[1]{0:T(128)} %bitcast.9.active_ref, f32[2,256,256]{2,1,0:T(8,128)S(1)} %get-tuple-element.65.modes_ref, ...), custom_call_target="tpu_custom_call", output_to_operand_aliasing={{0}: (5, {}), {1}: (6, {})} | custom-call | flops 2000000000 | bytes 2000000 | tf_op jit(solution)/shard_map/upper/pallas_call | solution.py:438
  48.6 1.3 %collective-permute-start.17 = (f32[32,256]{1,0:T(8,128)S(1)}, f32[32,256]{1,0:T(8,128)S(1)}, u32[]{:S(2)}, u32[]{:S(2)}) collective-permute-start(f32[32,256]{1,0:T(8,128)S(1)} %get-tuple-element.109), channel_id=1, source_target_pairs={{26,31},{30,27}} | collective-permute-start | bytes 98312 | tf_op jit(solution)/shard_map/ppermute | solution.py:472
  49.9 2.1 %lower.12 = (f32[256,256]{1,0:T(8,128)S(1)}, f32[256,256]{1,0:T(8,128)S(1)}, f32[32,256]{1,0:T(8,128)S(1)}, f32[32,256]{1,0:T(8,128)S(1)}) custom-call(s32[1]{0:T(128)} %bitcast.9.active_ref, f32[2,256,256]{2,1,0:T(8,128)S(1)} %get-tuple-element.65.modes_ref, ...), custom_call_target="tpu_custom_call", output_to_operand_aliasing={{0}: (5, {}), {1}: (6, {})} | custom-call | flops 2000000000 | bytes 2000000 | tf_op jit(solution)/shard_map/lower/pallas_call | solution.py:438
  52.0 0.7 %collective-permute-start.16 = (f32[32,256]{1,0:T(8,128)S(1)}, f32[32,256]{1,0:T(8,128)S(1)}, u32[]{:S(2)}, u32[]{:S(2)}) collective-permute-start(f32[32,256]{1,0:T(8,128)S(1)} %get-tuple-element.108), channel_id=1, source_target_pairs={{19,31},{23,27}} | collective-permute-start | bytes 98312 | tf_op jit(solution)/shard_map/ppermute | solution.py:475
  52.7 1.3 %collective-permute-start.18 = (f32[32,256]{1,0:T(8,128)S(1)}, f32[32,256]{1,0:T(8,128)S(1)}, u32[]{:S(2)}, u32[]{:S(2)}) collective-permute-start(f32[32,256]{1,0:T(8,128)S(1)} %get-tuple-element.115), channel_id=1, source_target_pairs={{26,31},{30,27}} | collective-permute-start | bytes 98312 | tf_op jit(solution)/shard_map/ppermute | solution.py:477
  54.1 0.9 %collective-permute-done.18.trace_y_ref = f32[32,256]{1,0:T(8,128)S(1)} collective-permute-done((f32[32,256]{1,0:T(8,128)S(1)}, f32[32,256]{1,0:T(8,128)S(1)}, u32[]{:S(2)}, u32[]{:S(2)}) %collective-permute-start.18) | collective-permute-done | bytes 32800 | tf_op jit(solution)/shard_map/ppermute | solution.py:477
  55.1 0.8 %copy-done.5 = bf16[64,768]{1,0:T(8,128)(2,1)S(1)} copy-done((bf16[64,768]{1,0:T(8,128)(2,1)S(1)}, bf16[64,768]{1,0:T(8,128)(2,1)}, u32[]{:S(2)}) %copy-start.5) | copy-done | bytes 98328
  55.9 0.6 edges.1
  56.5 1.9 %collective-permute-start.21 = (f32[2,32,256]{2,1,0:T(8,128)S(1)}, f32[2,32,256]{2,1,0:T(8,128)S(1)}, u32[]{:S(2)}, u32[]{:S(2)}) collective-permute-start(f32[2,32,256]{2,1,0:T(8,128)S(1)} %get-tuple-element.123), channel_id=1, source_target_pairs={{1,4},{5,0},{2,5},{6,1},{3,6},{7,2},{9,12},{13,8},{10,13},{14,9},{... | collective-permute-start | bytes 196616 | tf_op jit(solution)/shard_map/ppermute | solution.py:490
  58.5 1.3 %collective-permute-start.20 = (f32[32,256]{1,0:T(8,128)S(1)}, f32[32,256]{1,0:T(8,128)S(1)}, u32[]{:S(2)}, u32[]{:S(2)}) collective-permute-start(f32[32,256]{1,0:T(8,128)S(1)} %get-tuple-element.122), channel_id=1, source_target_pairs={{8,4},{12,0},{9,5},{13,1},{10,6},{14,2},{11,7},{15,3},{16,12},{20,... | collective-permute-start | bytes 98312 | tf_op jit(solution)/shard_map/ppermute | solution.py:489
  59.8 1.1 %finish.1 = (f32[2,2,16,16,128]{4,3,2,1,0:T(8,128)S(1)}, f32[2,2,16,16,128]{4,3,2,1,0:T(8,128)S(1)}) custom-call(s32[1]{0:T(128)} %bitcast.1.core_ref, f32[256,256]{1,0:T(8,128)S(1)} %get-tuple-element.112.total0_ref, f32[256,256]{1,0:T(8,128)S(1)} %get-tuple-element.113.term0_ref, f32[256,256]{1,0:T(8,128)S(1)} %get-tuple-element.118.total1_ref, ...), custom_call_target="tpu_custom_call" | custom-call | tf_op jit(solution)/shard_map/finish/pallas_call | solution.py:493
  60.9 0.8 %collective-permute-start.19 = (f32[2,2,16,16,128]{4,3,2,1,0:T(8,128)S(1)}, f32[2,2,16,16,128]{4,3,2,1,0:T(8,128)S(1)}, u32[]{:S(2)}, u32[]{:S(2)}) collective-permute-start(f32[2,2,16,16,128]{4,3,2,1,0:T(8,128)S(1)} %get-tuple-element.121), channel_id=1, source_target_pairs={{0,4},{4,0},{1,5},{5,1},{2,6},{6,2},{3,7},{7,3},{8,12},{12,8},{9,1... | collective-permute-start | bytes 1572872 | tf_op jit(solution)/shard_map/ppermute | solution.py:502
  61.7 1.5 %collective-permute-done.21 = f32[2,32,256]{2,1,0:T(8,128)S(1)} collective-permute-done((f32[2,32,256]{2,1,0:T(8,128)S(1)}, f32[2,32,256]{2,1,0:T(8,128)S(1)}, u32[]{:S(2)}, u32[]{:S(2)}) %collective-permute-start.21) | collective-permute-done | bytes 65568 | tf_op jit(solution)/shard_map/ppermute | solution.py:490
  63.3 0.3 collective-permute-start.22
  63.6 0.8 %place_wave.1 = f32[2,2,16,16,128]{4,3,2,1,0:T(8,128)} custom-call(s32[1]{0:T(128)} %bitcast.rhs_ref, f32[2,2,16,16,128]{4,3,2,1,0:T(8,128)S(1)} %get-tuple-element.120.keep_ref, f32[2,2,16,16,128]{4,3,2,1,0:T(8,128)S(1)} %collective-permute-done.19.got_ref), custom_call_target="tpu_custom_call" | custom-call | flops 10000000000 | bytes 1000000 | tf_op jit(solution)/shard_map/place_wave/pallas_call | solution.py:516
  64.5 0.1 collective-permute-done.22.got_edge_ref
  64.6 0.8 %place_rest.1 = f32[2,2,16,16,128]{4,3,2,1,0:T(8,128)} custom-call(s32[1]{0:T(128)} %bitcast.1.core_ref, s32[1]{0:T(128)} %bitcast.rhs_ref, f32[2,16,16,128]{3,2,1,0:T(8,128)S(1)} %keep.1.keep_rest_ref, f32[2,2,16,16,128]{4,3,2,1,0:T(8,128)S(1)} %collective-permute-done.19.got_ref, f32[64,256]{1,0:T(8,128)S(1)} %collective-permute-done.22.got_edge_ref), custom_call_target="tpu_custom_call" | custom-call | tf_op jit(solution)/shard_map/place_rest/pallas_call | solution.py:526
  (62 shorter events, 0.8 us)
Async XLA Ops:
  0.6 1.9 %copy-start = (f32[2,16,2]{1,2,0:T(2,128)S(1)}, f32[2,16,2]{1,2,0:T(2,128)}, u32[]{:S(2)}) copy-start(f32[2,16,2]{1,2,0:T(2,128)} %param.15) | copy-start | bytes 772
  0.7 1.1 %copy-start.4 = (f32[16,16,128]{2,1,0:T(8,128)S(1)}, f32[16,16,128]{2,1,0:T(8,128)}, u32[]{:S(2)}) copy-start(f32[16,16,128]{2,1,0:T(8,128)} %slow_ref.1) | copy-start | bytes 393220
  0.7 2.6 %copy-start.6 = (bf16[2,2,128,192]{3,2,1,0:T(8,128)(2,1)S(1)}, bf16[2,2,128,192]{3,2,1,0:T(8,128)(2,1)}, u32[]{:S(2)}) copy-start(bf16[2,2,128,192]{3,2,1,0:T(8,128)(2,1)} %constant.159.clone.forward_ref.refs_1_) | copy-start | bytes 589828
  1.7 1.6 %copy-start.3 = (f32[2,2,16,16,128]{4,3,2,1,0:T(8,128)S(1)}, f32[2,2,16,16,128]{4,3,2,1,0:T(8,128)}, u32[]{:S(2)}) copy-start(f32[2,2,16,16,128]{4,3,2,1,0:T(8,128)} %right_ref.1) | copy-start | bytes 1572868
  1.8 1.6 %copy-start.1 = (bf16[256,256]{1,0:T(8,128)(2,1)S(1)}, bf16[256,256]{1,0:T(8,128)(2,1)}, u32[]{:S(2)}) copy-start(bf16[256,256]{1,0:T(8,128)(2,1)} %constant.161.clone.z_ref.refs_3_) | copy-start | bytes 393220
  1.8 1.6 %copy-start.9 = (f32[256,1]{1,0:T(8,128)S(1)}, f32[256,1]{1,0:T(8,128)}, u32[]{:S(2)}) copy-start(f32[256,1]{1,0:T(8,128)} %constant.165.clone.edge_ref) | copy-start | bytes 3076
  1.8 2.3 %collective-permute-start = (f32[3,16,16,128]{3,2,1,0:T(8,128)S(1)}, f32[3,16,16,128]{3,2,1,0:T(8,128)S(1)}, u32[]{:S(2)}, u32[]{:S(2)}) collective-permute-start(f32[3,16,16,128]{3,2,1,0:T(8,128)S(1)} %pad_maximum_fusion), channel_id=1, source_target_pairs={{0,4},{4,0},{1,5},{5,1},{2,6},{6,2},{3,7},{7,3},{8,12},{12,8},{9,1... | collective-permute-start | bytes 1179656 | tf_op jit(solution)/shard_map/ppermute | solution.py:400
  2.6 0.7 %copy-start.11 = (s32[2,16]{1,0:T(2,128)S(1)}, s32[2,16]{1,0:T(2,128)}, u32[]{:S(2)}) copy-start(s32[2,16]{1,0:T(2,128)} %param.14) | copy-start | bytes 388
  4.1 0.9 %copy-start.8 = (bf16[256,192]{1,0:T(8,128)(2,1)S(1)}, bf16[256,192]{1,0:T(8,128)(2,1)}, u32[]{:S(2)}) copy-start(bf16[256,192]{1,0:T(8,128)(2,1)} %constant.162.clone.refs_4_) | copy-start | bytes 294916
  4.1 1.0 %copy-start.10 = (bf16[64,768]{1,0:T(8,128)(2,1)S(1)}, bf16[64,768]{1,0:T(8,128)(2,1)}, u32[]{:S(2)}) copy-start(bf16[64,768]{1,0:T(8,128)(2,1)} %constant.163.clone.refs_5_) | copy-start | bytes 294916
  4.9 1.0 %copy-start.2 = (bf16[2,2,128,192]{3,2,1,0:T(8,128)(2,1)S(1)}, bf16[2,2,128,192]{3,2,1,0:T(8,128)(2,1)}, u32[]{:S(2)}) copy-start(bf16[2,2,128,192]{3,2,1,0:T(8,128)(2,1)} %constant.160.clone.refs_2_.backward_ref) | copy-start | bytes 589828
  5.0 1.0 %copy-start.7 = (f32[2,256,128]{2,1,0:T(8,128)S(1)}, f32[2,256,128]{2,1,0:T(8,128)}, u32[]{:S(2)}) copy-start(f32[2,256,128]{2,1,0:T(8,128)} %constant.158.clone.refs_0_) | copy-start | bytes 786436
  6.1 2.2 %collective-permute-start.2 = (f32[32,256]{1,0:T(8,128)S(1)}, f32[32,256]{1,0:T(8,128)S(1)}, u32[]{:S(2)}, u32[]{:S(2)}) collective-permute-start(f32[32,256]{1,0:T(8,128)S(1)} %get-tuple-element.69), channel_id=1, source_target_pairs={{0,5},{4,1}} | collective-permute-start | bytes 98312 | tf_op jit(solution)/shard_map/ppermute | solution.py:472
  6.9 1.4 %collective-permute-start.1 = (f32[32,256]{1,0:T(8,128)S(1)}, f32[32,256]{1,0:T(8,128)S(1)}, u32[]{:S(2)}, u32[]{:S(2)}) collective-permute-start(f32[32,256]{1,0:T(8,128)S(1)} %get-tuple-element.68), channel_id=1, source_target_pairs={{0,12},{4,8}} | collective-permute-start | bytes 98312 | tf_op jit(solution)/shard_map/ppermute | solution.py:475
  7.5 1.5 %collective-permute-start.3 = (f32[32,256]{1,0:T(8,128)S(1)}, f32[32,256]{1,0:T(8,128)S(1)}, u32[]{:S(2)}, u32[]{:S(2)}) collective-permute-start(f32[32,256]{1,0:T(8,128)S(1)} %get-tuple-element.73), channel_id=1, source_target_pairs={{0,5},{4,1}} | collective-permute-start | bytes 98312 | tf_op jit(solution)/shard_map/ppermute | solution.py:477
  8.3 2.1 %collective-permute-start.5 = (f32[32,256]{1,0:T(8,128)S(1)}, f32[32,256]{1,0:T(8,128)S(1)}, u32[]{:S(2)}, u32[]{:S(2)}) collective-permute-start(f32[32,256]{1,0:T(8,128)S(1)} %get-tuple-element.77), channel_id=1, source_target_pairs={{1,6},{5,2},{8,13},{12,9}} | collective-permute-start | bytes 98312 | tf_op jit(solution)/shard_map/ppermute | solution.py:472
  9.1 1.4 %collective-permute-start.4 = (f32[32,256]{1,0:T(8,128)S(1)}, f32[32,256]{1,0:T(8,128)S(1)}, u32[]{:S(2)}, u32[]{:S(2)}) collective-permute-start(f32[32,256]{1,0:T(8,128)S(1)} %get-tuple-element.76), channel_id=1, source_target_pairs={{1,13},{5,9},{8,20},{12,16}} | collective-permute-start | bytes 98312 | tf_op jit(solution)/shard_map/ppermute | solution.py:475
  9.8 1.5 %collective-permute-start.6 = (f32[32,256]{1,0:T(8,128)S(1)}, f32[32,256]{1,0:T(8,128)S(1)}, u32[]{:S(2)}, u32[]{:S(2)}) collective-permute-start(f32[32,256]{1,0:T(8,128)S(1)} %get-tuple-element.81), channel_id=1, source_target_pairs={{1,6},{5,2},{8,13},{12,9}} | collective-permute-start | bytes 98312 | tf_op jit(solution)/shard_map/ppermute | solution.py:477
  10.6 2.1 %collective-permute-start.8 = (f32[32,256]{1,0:T(8,128)S(1)}, f32[32,256]{1,0:T(8,128)S(1)}, u32[]{:S(2)}, u32[]{:S(2)}) collective-permute-start(f32[32,256]{1,0:T(8,128)S(1)} %get-tuple-element.85), channel_id=1, source_target_pairs={{2,7},{6,3},{9,14},{13,10},{16,21},{20,17}} | collective-permute-start | bytes 98312 | tf_op jit(solution)/shard_map/ppermute | solution.py:472
  11.3 1.4 %collective-permute-start.7 = (f32[32,256]{1,0:T(8,128)S(1)}, f32[32,256]{1,0:T(8,128)S(1)}, u32[]{:S(2)}, u32[]{:S(2)}) collective-permute-start(f32[32,256]{1,0:T(8,128)S(1)} %get-tuple-element.84), channel_id=1, source_target_pairs={{2,14},{6,10},{9,21},{13,17},{16,28},{20,24}} | collective-permute-start | bytes 98312 | tf_op jit(solution)/shard_map/ppermute | solution.py:475
  12.0 1.5 %collective-permute-start.9 = (f32[32,256]{1,0:T(8,128)S(1)}, f32[32,256]{1,0:T(8,128)S(1)}, u32[]{:S(2)}, u32[]{:S(2)}) collective-permute-start(f32[32,256]{1,0:T(8,128)S(1)} %get-tuple-element.89), channel_id=1, source_target_pairs={{2,7},{6,3},{9,14},{13,10},{16,21},{20,17}} | collective-permute-start | bytes 98312 | tf_op jit(solution)/shard_map/ppermute | solution.py:477
  12.8 2.3 %collective-permute-start.11 = (f32[32,256]{1,0:T(8,128)S(1)}, f32[32,256]{1,0:T(8,128)S(1)}, u32[]{:S(2)}, u32[]{:S(2)}) collective-permute-start(f32[32,256]{1,0:T(8,128)S(1)} %get-tuple-element.93), channel_id=1, source_target_pairs={{10,15},{14,11},{17,22},{21,18},{24,29},{28,25}} | collective-permute-start | bytes 98312 | tf_op jit(solution)/shard_map/ppermute | solution.py:472
  13.8 1.4 %collective-permute-start.10 = (f32[32,256]{1,0:T(8,128)S(1)}, f32[32,256]{1,0:T(8,128)S(1)}, u32[]{:S(2)}, u32[]{:S(2)}) collective-permute-start(f32[32,256]{1,0:T(8,128)S(1)} %get-tuple-element.92), channel_id=1, source_target_pairs={{3,15},{7,11},{10,22},{14,18},{17,29},{21,25}} | collective-permute-start | bytes 98312 | tf_op jit(solution)/shard_map/ppermute | solution.py:475
  14.4 2.1 %collective-permute-start.12 = (f32[32,256]{1,0:T(8,128)S(1)}, f32[32,256]{1,0:T(8,128)S(1)}, u32[]{:S(2)}, u32[]{:S(2)}) collective-permute-start(f32[32,256]{1,0:T(8,128)S(1)} %get-tuple-element.97), channel_id=1, source_target_pairs={{10,15},{14,11},{17,22},{21,18},{24,29},{28,25}} | collective-permute-start | bytes 98312 | tf_op jit(solution)/shard_map/ppermute | solution.py:477
  15.2 30.0 %collective-permute-start.14 = (f32[32,256]{1,0:T(8,128)S(1)}, f32[32,256]{1,0:T(8,128)S(1)}, u32[]{:S(2)}, u32[]{:S(2)}) collective-permute-start(f32[32,256]{1,0:T(8,128)S(1)} %get-tuple-element.101), channel_id=1, source_target_pairs={{18,23},{22,19},{25,30},{29,26}} | collective-permute-start | bytes 98312 | tf_op jit(solution)/shard_map/ppermute | solution.py:472
  16.6 29.9 %collective-permute-start.13 = (f32[32,256]{1,0:T(8,128)S(1)}, f32[32,256]{1,0:T(8,128)S(1)}, u32[]{:S(2)}, u32[]{:S(2)}) collective-permute-start(f32[32,256]{1,0:T(8,128)S(1)} %get-tuple-element.100), channel_id=1, source_target_pairs={{11,23},{15,19},{18,30},{22,26}} | collective-permute-start | bytes 98312 | tf_op jit(solution)/shard_map/ppermute | solution.py:475
  17.9 32.0 %collective-permute-start.15 = (f32[32,256]{1,0:T(8,128)S(1)}, f32[32,256]{1,0:T(8,128)S(1)}, u32[]{:S(2)}, u32[]{:S(2)}) collective-permute-start(f32[32,256]{1,0:T(8,128)S(1)} %get-tuple-element.105), channel_id=1, source_target_pairs={{18,23},{22,19},{25,30},{29,26}} | collective-permute-start | bytes 98312 | tf_op jit(solution)/shard_map/ppermute | solution.py:477
  48.6 5.4 %collective-permute-start.17 = (f32[32,256]{1,0:T(8,128)S(1)}, f32[32,256]{1,0:T(8,128)S(1)}, u32[]{:S(2)}, u32[]{:S(2)}) collective-permute-start(f32[32,256]{1,0:T(8,128)S(1)} %get-tuple-element.109), channel_id=1, source_target_pairs={{26,31},{30,27}} | collective-permute-start | bytes 98312 | tf_op jit(solution)/shard_map/ppermute | solution.py:472
  52.0 2.0 %collective-permute-start.16 = (f32[32,256]{1,0:T(8,128)S(1)}, f32[32,256]{1,0:T(8,128)S(1)}, u32[]{:S(2)}, u32[]{:S(2)}) collective-permute-start(f32[32,256]{1,0:T(8,128)S(1)} %get-tuple-element.108), channel_id=1, source_target_pairs={{19,31},{23,27}} | collective-permute-start | bytes 98312 | tf_op jit(solution)/shard_map/ppermute | solution.py:475
  52.7 2.3 %collective-permute-start.18 = (f32[32,256]{1,0:T(8,128)S(1)}, f32[32,256]{1,0:T(8,128)S(1)}, u32[]{:S(2)}, u32[]{:S(2)}) collective-permute-start(f32[32,256]{1,0:T(8,128)S(1)} %get-tuple-element.115), channel_id=1, source_target_pairs={{26,31},{30,27}} | collective-permute-start | bytes 98312 | tf_op jit(solution)/shard_map/ppermute | solution.py:477
  55.0 0.9 %copy-start.5 = (bf16[64,768]{1,0:T(8,128)(2,1)S(1)}, bf16[64,768]{1,0:T(8,128)(2,1)}, u32[]{:S(2)}) copy-start(bf16[64,768]{1,0:T(8,128)(2,1)} %constant.164.clone.first_ref) | copy-start | bytes 294916
  56.5 6.7 %collective-permute-start.21 = (f32[2,32,256]{2,1,0:T(8,128)S(1)}, f32[2,32,256]{2,1,0:T(8,128)S(1)}, u32[]{:S(2)}, u32[]{:S(2)}) collective-permute-start(f32[2,32,256]{2,1,0:T(8,128)S(1)} %get-tuple-element.123), channel_id=1, source_target_pairs={{1,4},{5,0},{2,5},{6,1},{3,6},{7,2},{9,12},{13,8},{10,13},{14,9},{... | collective-permute-start | bytes 196616 | tf_op jit(solution)/shard_map/ppermute | solution.py:490
  58.5 4.8 %collective-permute-start.20 = (f32[32,256]{1,0:T(8,128)S(1)}, f32[32,256]{1,0:T(8,128)S(1)}, u32[]{:S(2)}, u32[]{:S(2)}) collective-permute-start(f32[32,256]{1,0:T(8,128)S(1)} %get-tuple-element.122), channel_id=1, source_target_pairs={{8,4},{12,0},{9,5},{13,1},{10,6},{14,2},{11,7},{15,3},{16,12},{20,... | collective-permute-start | bytes 98312 | tf_op jit(solution)/shard_map/ppermute | solution.py:489
  60.9 2.7 %collective-permute-start.19 = (f32[2,2,16,16,128]{4,3,2,1,0:T(8,128)S(1)}, f32[2,2,16,16,128]{4,3,2,1,0:T(8,128)S(1)}, u32[]{:S(2)}, u32[]{:S(2)}) collective-permute-start(f32[2,2,16,16,128]{4,3,2,1,0:T(8,128)S(1)} %get-tuple-element.121), channel_id=1, source_target_pairs={{0,4},{4,0},{1,5},{5,1},{2,6},{6,2},{3,7},{7,3},{8,12},{12,8},{9,1... | collective-permute-start | bytes 1572872 | tf_op jit(solution)/shard_map/ppermute | solution.py:502
  63.3 1.3 %collective-permute-start.22 = (f32[64,256]{1,0:T(8,128)S(1)}, f32[64,256]{1,0:T(8,128)S(1)}, u32[]{:S(2)}, u32[]{:S(2)}) collective-permute-start(f32[64,256]{1,0:T(8,128)S(1)} %pad_maximum_fusion.1), channel_id=1, source_target_pairs={{0,4},{4,0},{1,5},{5,1},{2,6},{6,2},{3,7},{7,3},{8,12},{12,8},{9,1... | collective-permute-start | bytes 196616 | tf_op jit(solution)/shard_map/ppermute | solution.py:506

commit v8 on v7

--- a/solution.py
+++ b/solution.py
@@ -124,17 +124,18 @@
     return jnp.concatenate([total[:rows], total[rows:]], axis=1)
 
 
+def sum_products(matrices, values):
+    products = [[left_product(matrices[p, h], values[p][h]) for p in range(2)] for h in range(2)]
+    return [sum(parts) for parts in zip(*products)]
+
+
 def to_modes(first, second, forward):
-    return [
-        sum(left_product(forward[p, h], join(first[h], second[h])) for h in range(2))
-        for p, join in enumerate((jnp.add, jnp.subtract))
-    ]
+    folded = [[join(f, s) for f, s in zip(first, second)] for join in (jnp.add, jnp.subtract)]
+    return sum_products(forward, folded)
 
 
 def to_cells(modes, backward):
-    even, odd = [
-        sum(left_product(backward[p, h], modes[p][h]) for h in range(2)) for p in range(2)
-    ]
+    even, odd = sum_products(backward, modes)
     return even + odd, even - odd
 
 
@@ -159,18 +160,22 @@
     )
 
 
-def solve_modes(source_modes, contrast, t):
-    count = source_modes.shape[0] // 4
-    term = in_parities(times(t["inverse"][0], t["inverse"][1], source_modes))
+def divide(modes, inverse):
+    return times(inverse[0], inverse[1], modes)
+
+
+def solve_modes(start, contrast, t):
+    count = start.shape[0] // 4
+    term = in_parities(start)
     total = term
     for _ in range(2):
         first, second = [in_two(cells) for cells in to_cells(term, t["backward"])]
+        blocks = [z_transform(jnp.concatenate(pair, axis=0), t["right_z"]) for pair in zip(first, second)]
         parts = []
-        for h in range(2):
+        for h, block in enumerate(blocks):
             here = [slice(at, at + count) for at in (h * count, (h + 2) * count)]
             factor = [jnp.concatenate([contrast[c, rows] for rows in here], axis=0) for c in range(2)]
-            cells = z_transform(jnp.concatenate([first[h], second[h]], axis=0), t["right_z"])
-            parts.append(in_two(z_transform(times(*factor, cells), t["right_z"])))
+            parts.append(in_two(z_transform(times(*factor, block), t["right_z"])))
         modes = to_modes(*zip(*parts), t["forward"])
         term = []
         for p in range(2):
@@ -183,7 +188,7 @@
     return [jnp.concatenate([part for pair in both for part in pair], axis=0) for both in (total, term)]
 
 
-PREP = ("edge", "forward", "right_z")
+PREP = ("edge", "inverse", "forward", "right_z")
 BEAT = ("inverse", "forward", "backward", "right_z", "enter", "leave")
 
 
@@ -191,7 +196,7 @@
     out_ref[...] = in_ref[...]
 
 
-def prepare(dense, slow, place, depth, amplitude, edge, forward, right_z, modes_ref, contrast_ref):
+def prepare(dense, slow, place, depth, amplitude, edge, inverse, forward, right_z, modes_ref, contrast_ref):
     rows, cells_z = contrast_ref.shape[1:]
     points = place.shape[1]
     row_ids = lax.broadcasted_iota(jnp.int32, (rows, points), 0)
@@ -213,21 +218,21 @@
         (((1,), (1,)), ((), ())), preferred_element_type=F32,
     )
     first, second = [in_two(part) for part in in_two(z_transform(field + dense, right_z))]
-    modes_ref[...] = jnp.concatenate(to_modes(first, second, forward), axis=0)
+    modes_ref[...] = divide(jnp.concatenate(to_modes(first, second, forward), axis=0), inverse)
 
 
 def prep_kernel(cells_x, rhs_ref, right_ref, slow_ref, place_ref, depth_ref, amp_ref, edge_ref,
-                forward_ref, z_ref, modes_ref, contrast_ref):
+                inverse_ref, forward_ref, z_ref, modes_ref, contrast_ref):
     dense = [jnp.concatenate([right_ref[rhs_ref[0], c, x] for x in cells_x], axis=0) for c in range(2)]
     slow = jnp.concatenate([slow_ref[x] for x in cells_x], axis=0)
     prepare(
         jnp.concatenate(dense, axis=1), slow, place_ref[...], depth_ref[...], amp_ref, edge_ref[...],
-        forward_ref, z_ref[...], modes_ref, contrast_ref,
+        inverse_ref, forward_ref, z_ref[...], modes_ref, contrast_ref,
     )
 
 
 def prep_other_kernel(cells_x, core_ref, swap_ref, own_modes_ref, own_contrast_ref, place_ref, depth_ref,
-                      amp_ref, edge_ref, forward_ref, z_ref, modes_ref, contrast_ref):
+                      amp_ref, edge_ref, inverse_ref, forward_ref, z_ref, modes_ref, contrast_ref):
     core = core_ref[0]
     other = 1 - core
     modes_ref[core] = own_modes_ref[...]
@@ -235,29 +240,28 @@
     parts = [jnp.concatenate([swap_ref[c, x] for x in cells_x], axis=0) for c in range(3)]
     prepare(
         jnp.concatenate(parts[:2], axis=1), parts[2], place_ref[...], depth_ref[...], amp_ref,
-        edge_ref[...], forward_ref, z_ref[...], modes_ref.at[other], contrast_ref.at[other],
-    )
-
-
-def source_modes(modes, trace_x, trace_y, enter):
-    return modes + left_product(enter, jnp.concatenate([trace_x, trace_y], axis=0))
-
-
-def beat_kernel(tile, sends, active_ref, modes_ref, contrast_ref, trace_x_ref, trace_y_ref, total_ref, term_ref, *refs):
-    t = {name: ref for name, ref in zip(BEAT, refs)}
-    new_total_ref, new_term_ref, *out_refs = refs[len(BEAT) :]
+        edge_ref[...], inverse_ref, forward_ref, z_ref[...], modes_ref.at[other], contrast_ref.at[other],
+    )
+
+
+def beat_kernel(tile, final, active_ref, modes_ref, contrast_ref, trace_x_ref, trace_y_ref, total_ref, term_ref,
+                *refs):
+    names = LAST if final else BEAT
+    t = {name: ref for name, ref in zip(names, refs)}
+    new_total_ref, new_term_ref, *out_refs = refs[len(names) :]
+    count = trace_x_ref.shape[0]
 
     @pl.when(active_ref[0] == 1)
     def _():
         local = dict(t, right_z=t["right_z"][...])
-        source = source_modes(modes_ref[tile], trace_x_ref[...], trace_y_ref[...], t["enter"][...])
-        total, term = solve_modes(source, contrast_ref.at[tile], local)
+        trace = jnp.concatenate([trace_x_ref[...], trace_y_ref[...]], axis=0)
+        start = modes_ref[tile] + divide(left_product(t["enter"][...], trace), t["inverse"])
+        total, term = solve_modes(start, contrast_ref.at[tile], local)
         new_total_ref[...] = total
         new_term_ref[...] = term
-        if sends:
-            count = trace_x_ref.shape[0]
+        if not (final and tile == 1):
             out = left_product(t["leave"][...], total)
-            for out_ref, part in zip(out_refs, (out[:count], out[count:])):
+            for out_ref, part in zip(out_refs[:1] if final else out_refs, (out[:count], out[count:])):
                 out_ref[...] = part
 
     @pl.when(active_ref[0] == 0)
@@ -265,17 +269,15 @@
         new_total_ref[...] = total_ref[...]
         new_term_ref[...] = term_ref[...]
 
-
-def edge_kernel(total0_ref, total1_ref, first_ref, z_ref, edge_x_ref, edge_y_ref):
-    count = edge_x_ref.shape[0]
-    right_z = z_ref[...]
-    for tile, total_ref in enumerate((total0_ref, total1_ref)):
-        edges = z_transform(left_product(first_ref[...], total_ref[...]), right_z)
-        edge_y_ref[tile] = edges[count:]
+    if final:
+        out = left_product(t["first"][...], new_total_ref[...])
+        edge_refs = out_refs[1 - tile :]
+        edge_refs[-1][...] = out[count:]
         if tile == 0:
-            edge_x_ref[...] = edges[:count]
-
-
+            edge_refs[0][...] = out[:count]
+
+
+LAST = BEAT + ("first",)
 FINISH = ("backward", "right_z")
 
 
@@ -318,9 +320,12 @@
         rest_ref[c, :, size_y - 2 :] += two
 
 
-def keep_kernel(core_ref, keep_ref, edge_x_ref, edge_y_ref, rest_ref):
+def keep_kernel(core_ref, keep_ref, edge_x_ref, edge_y_ref, z_ref, rest_ref):
     rest_ref[...] = keep_ref[1]
-    add_later(rest_ref, edge_x_ref[...], edge_y_ref[...], (core_ref[0] == 1).astype(F32))
+    count = edge_x_ref.shape[0]
+    edges = jnp.concatenate([edge_x_ref[...], edge_y_ref[core_ref[0]]], axis=0)
+    edges = z_transform(edges, z_ref[...])
+    add_later(rest_ref, edges[:count], edges[count:], (core_ref[0] == 1).astype(F32))
 
 
 def place_wave_kernel(rhs_ref, keep_ref, got_ref, wave_ref, sems):
@@ -335,13 +340,14 @@
         copy.wait()
 
 
-def place_rest_kernel(core_ref, rhs_ref, keep_rest_ref, got_ref, got_edge_ref, rest_ref, work_ref, sems):
+def place_rest_kernel(core_ref, rhs_ref, keep_rest_ref, got_ref, got_edge_ref, z_ref, rest_ref, work_ref, sems):
     rhs = rhs_ref[0]
     count = got_edge_ref.shape[0] // 2
     copies = [pltpu.make_async_copy(keep_rest_ref, rest_ref.at[rhs], sems.at[0])]
     copies[0].start()
     work_ref[...] = got_ref[1]
-    add_later(work_ref, got_edge_ref[:count], got_edge_ref[count:], (core_ref[0] == 1).astype(F32))
+    edges = z_transform(got_edge_ref[...], z_ref[...])
+    add_later(work_ref, edges[:count], edges[count:], (core_ref[0] == 1).astype(F32))
     copies.append(pltpu.make_async_copy(work_ref, rest_ref.at[1 - rhs], sems.at[1]))
     copies[1].start()
     for copy in copies:
@@ -416,7 +422,7 @@
     own_modes, own_contrast = pl.pallas_call(
         functools.partial(prep_kernel, cells_x),
         out_shape=one,
-        in_specs=[scalars()] + [whole()] * 8,
+        in_specs=[scalars()] + [whole()] * 9,
         out_specs=(whole(), whole()),
         compiler_params=PARAMS,
         cost_estimate=SOLVE_COST,
@@ -425,27 +431,27 @@
     modes, contrast = pl.pallas_call(
         functools.partial(prep_other_kernel, cells_x),
         out_shape=(shaped(2, rows, 2 * cells_z), shaped(2, 2, rows, cells_z)),
-        in_specs=[scalars()] + [whole()] * 9,
+        in_specs=[scalars()] + [whole()] * 10,
         out_specs=(whole(), whole()),
         compiler_params=PARAMS,
         cost_estimate=SOLVE_COST,
         name="prep_other",
     )(core_ref, swapped, own_modes, own_contrast, places[1], depth, amplitudes, *prep_tables)
 
-    beat_tables = [t[name] for name in BEAT]
-
-    def solve(tile, active, trace_x, trace_y, state, sends):
-        total, term, *out = pl.pallas_call(
-            functools.partial(beat_kernel, tile, sends),
-            out_shape=(shaped(rows, 2 * cells_z),) * 2 + (shaped(*zero_x.shape), shaped(*zero_y.shape))[:sends],
-            in_specs=[scalars()] + [whole()] * (6 + len(BEAT)),
-            out_specs=(whole(),) * (2 + sends),
+    def solve(tile, active, trace_x, trace_y, state, final):
+        x, y = shaped(*zero_x.shape), shaped(*zero_y.shape)
+        outs = ((x, x, y), (y,))[tile] if final else (x, y)
+        total, term, *outs = pl.pallas_call(
+            functools.partial(beat_kernel, tile, final),
+            out_shape=(shaped(rows, 2 * cells_z),) * 2 + outs,
+            in_specs=[scalars()] + [whole()] * (6 + len(LAST if final else BEAT)),
+            out_specs=(whole(),) * (2 + len(outs)),
             input_output_aliases={5: 0, 6: 1},
             compiler_params=PARAMS,
             cost_estimate=SOLVE_COST,
             name="upper" if tile == 0 else "lower",
-        )(active, modes, contrast, trace_x, trace_y, *state, *beat_tables)
-        return (total, term), out
+        )(active, modes, contrast, trace_x, trace_y, *state, *[t[name] for name in (LAST if final else BEAT)])
+        return (total, term), outs
 
     def hand_on(trace):
         return pl.pallas_call(
@@ -466,24 +472,17 @@
         here = [(k, beat - k) for k in range(chips) if 0 <= beat - k < grid_cols]
         along_x = between([((k, j), (k + 1, j)) for k, j in here if k + 1 < chips])
         along_y = between([((k, j), (k, j + 1)) for k, j in here if j + 1 < grid_cols])
-        more = beat < chips + grid_cols - 2
-        states[0], (inner_x, *out_y0) = solve(0, active, trace_x, trace_y0, states[0], 1 + more)
+        final = beat == chips + grid_cols - 2
+        states[0], (inner_x, *outs0) = solve(0, active, trace_x, trace_y0, states[0], final)
         if along_y:
-            trace_y0 = hand_on(lax.ppermute(out_y0[0], axes, along_y))
-        states[1], out = solve(1, active, inner_x, trace_y1, states[1], 2 * more)
+            trace_y0 = hand_on(lax.ppermute(outs0[0], axes, along_y))
+        states[1], outs1 = solve(1, active, inner_x, trace_y1, states[1], final)
         if along_x:
-            trace_x = lax.ppermute(out[0], axes, along_x)
+            trace_x = lax.ppermute(outs1[0], axes, along_x)
         if along_y:
-            trace_y1 = lax.ppermute(out[1], axes, along_y)
-
-    edge_x, edge_y = pl.pallas_call(
-        edge_kernel,
-        out_shape=(shaped(*zero_x.shape), shaped(2, *zero_y.shape)),
-        in_specs=[whole()] * 4,
-        out_specs=(whole(), whole()),
-        compiler_params=PARAMS,
-        name="edges",
-    )(states[0][0], states[1][0], t["first"], t["right_z"])
+            trace_y1 = lax.ppermute(outs1[1], axes, along_y)
+    edge_x, edge_y0 = outs0
+    edge_y = jnp.stack([edge_y0, outs1[0]])
 
     every = [(k, j) for k in range(chips) for j in range(grid_cols)]
     after_x = lax.ppermute(edge_x, axes, between([((k, j), (k - 1, j)) for k, j in every if k]))
@@ -501,18 +500,17 @@
     )(core_ref, *states[0], *states[1], contrast, *[t[name] for name in FINISH])
     got = lax.ppermute(give, axes, own)
 
-    keep_y = lax.dynamic_index_in_dim(after_y, core, 0, keepdims=False)
     pass_y = lax.dynamic_index_in_dim(after_y, 1 - core, 0, keepdims=False)
     got_edge = lax.ppermute(jnp.concatenate([after_x, pass_y], axis=0), axes, own)
     keep_rest = pl.pallas_call(
         keep_kernel,
         out_shape=shaped(*half.shape[1:]),
-        in_specs=[scalars()] + [whole()] * 3,
+        in_specs=[scalars()] + [whole()] * 4,
         out_specs=whole(),
         compiler_params=PARAMS,
         cost_estimate=KEEP_COST,
         name="keep",
-    )(core_ref, keep, after_x, keep_y)
+    )(core_ref, keep, after_x, after_y, t["right_z"])
     wavefield = pl.pallas_call(
         place_wave_kernel,
         out_shape=shaped(*right_side.shape),
@@ -526,7 +524,7 @@
     residual = pl.pallas_call(
         place_rest_kernel,
         out_shape=shaped(*right_side.shape),
-        in_specs=[scalars()] * 2 + [whole()] * 3,
+        in_specs=[scalars()] * 2 + [whole()] * 4,
         out_specs=anywhere(),
         scratch_shapes=[
             pltpu.VMEM((2, size_x, size_y, cells_z), F32),
@@ -534,7 +532,7 @@
         ],
         compiler_params=PARAMS,
         name="place_rest",
-    )(core_ref, rhs_ref, keep_rest, got, got_edge)
+    )(core_ref, rhs_ref, keep_rest, got, got_edge, t["right_z"])
     return wavefield, residual
 
 

time: 66.8 us -> 67.4 us (level)
  waiting for transfers between devices: 29.9 us -> 31.5 us
  local copies, waits for them, and re-layouts: 3.65 us -> 2.35 us
    unnamed x24, local copies, waits for them, and re-layouts: 2.55 us -> 1.2 us
    ppermute x1, waiting for transfers between devices: 1.53 us -> 2.48 us  [body(): lax.ppermute(edge_y, axes, between([((k, j), (k, j - 1)) for k, j in ever...]
    pallas_call x15 -> x14, Pallas kernels: 5.85 us -> 5.84 us  [solve(): pl.pallas_call(functools.partial(beat_kernel, tile, final), out_shape=(sh...]
  transfers between devices with their start and end apart: 23 -> 23, of which waited for: 5 -> 5; matrix products, arithmetic and copies ran while one was open for 0% -> 0% of each run, Pallas kernels for 12% -> 13%
where the time goes in v8:
time: 67.4 us; the launch traced here: 66.4 us
  waiting for transfers between devices  31.5 us (47%)
  starting transfers between devices  20.5 us (30%)
  Pallas kernels  10.4 us (15%)
  local copies, waits for them, and re-layouts  2.35 us (3%)
  between operations  1.56 us (2%)
    ppermute x6, waiting for transfers between devices, body(): trace_y0 = hand_on(lax.ppermute(outs0[0], axes, along_y))  26.7 us
    pallas_call x14, Pallas kernels, solve(): pl.pallas_call(functools.partial(beat_kernel, tile, final), out_shape=(sh...  5.84 us
    ppermute x6, starting transfers between devices, body(): trace_y0 = hand_on(lax.ppermute(outs0[0], axes, along_y))  5.24 us
    ppermute x6, starting transfers between devices, body(): trace_y1 = lax.ppermute(outs1[1], axes, along_y)  5.24 us
    ppermute x6, starting transfers between devices, body(): trace_x = lax.ppermute(outs1[0], axes, along_x)  4.61 us
    ppermute x1, waiting for transfers between devices, body(): lax.ppermute(edge_y, axes, between([((k, j), (k, j - 1)) for k, j in ever...  2.48 us
    ppermute x1, starting transfers between devices, body(): lax.ppermute(edge_y, axes, between([((k, j), (k, j - 1)) for k, j in ever...  1.92 us
  transfers between devices with their start and end apart: 23, of which 5 were waited for; matrix products, arithmetic and copies ran while one was open for 0% of the time, Pallas kernels for 13%

profile of v8, /device:TPU:29, one launch (start us, length us, event | category | flops | bytes accessed | tf_op | source)
XLA Modules:
  0.0 66.4 jit_solution(14002735670954583469)
XLA Ops:
  0.7 1.1 %dynamic-slice_bitcast_fusion = f32[2,16,16,128]{3,2,1,0:T(8,128)S(1)} fusion(f32[2,2,16,16,128]{4,3,2,1,0:T(8,128)} %right_ref.1, s32[]{:T(128)S(6)} %select_n.71), kind=kLoop, calls=%fused_computation.1 | loop fusion | bytes 524292 | tf_op jit(solution)/shard_map/jit(dynamic_index_in_dim)/squeeze | solution.py:405
  1.9 0.7 %collective-permute-start = (f32[3,16,16,128]{3,2,1,0:T(8,128)S(1)}, f32[3,16,16,128]{3,2,1,0:T(8,128)S(1)}, u32[]{:S(2)}, u32[]{:S(2)}) collective-permute-start(f32[3,16,16,128]{3,2,1,0:T(8,128)S(1)} %pad_maximum_fusion), channel_id=1, source_target_pairs={{0,4},{4,0},{1,5},{5,1},{2,6},{6,2},{3,7},{7,3},{8,12},{12,8},{9,1... | collective-permute-start | bytes 1179656 | tf_op jit(solution)/shard_map/ppermute | solution.py:406
  2.7 0.2 copy-done.3
  2.9 0.8 %prep.1 = (f32[256,256]{1,0:T(8,128)S(1)}, f32[2,256,128]{2,1,0:T(8,128)S(1)}) custom-call(s32[1]{0:T(128)} %bitcast.rhs_ref, f32[2,2,16,16,128]{4,3,2,1,0:T(8,128)S(1)} %copy-done.3, f32[16,16,128]{2,1,0:T(8,128)S(1)} %copy-done.4, s32[1,16]{1,0:T(1,128)S(1)} %and_select_fusion.2.place_ref, s32[1,16]{1,0:T(1,128)S(1)} %and_select_fusion.1.depth_ref, ...), custom_call_target="tpu_custom_call" | custom-call | flops 2000000000 | bytes 2000000 | tf_op jit(solution)/shard_map/prep/pallas_call | solution.py:422
  3.7 0.3 collective-permute-done.swap_ref
  4.0 0.8 %prep_other.1 = (f32[2,256,256]{2,1,0:T(8,128)S(1)}, f32[2,2,256,128]{3,2,1,0:T(8,128)S(1)}) custom-call(s32[1]{0:T(128)} %bitcast.1.core_ref, f32[3,16,16,128]{3,2,1,0:T(8,128)S(1)} %collective-permute-done.swap_ref, f32[256,256]{1,0:T(8,128)S(1)} %get-tuple-element.64.own_modes_ref, f32[2,256,128]{2,1,0:T(8,128)S(1)} %get-tuple-element.65.own_contrast_ref, ...), custom_call_target="tpu_custom_call" | custom-call | flops 2000000000 | bytes 2000000 | tf_op jit(solution)/shard_map/prep_other/pallas_call | solution.py:431
  4.9 0.9 %copy-done.2 = bf16[2,2,128,192]{3,2,1,0:T(8,128)(2,1)S(1)} copy-done((bf16[2,2,128,192]{3,2,1,0:T(8,128)(2,1)S(1)}, bf16[2,2,128,192]{3,2,1,0:T(8,128)(2,1)}, u32[]{:S(2)}) %copy-start.2) | copy-done | bytes 196632
  5.9 0.7 collective-permute-start.2
  6.6 0.1 lower.7
  6.7 0.7 collective-permute-start.1
  7.4 0.7 collective-permute-start.3
  8.1 0.1 upper.8
  8.2 0.7 collective-permute-start.5
  8.8 0.1 lower.8
  8.9 0.7 collective-permute-start.4
  9.6 0.7 collective-permute-start.6
  10.3 0.1 upper.9
  10.4 0.7 collective-permute-start.8
  11.1 0.1 lower.9
  11.2 0.7 collective-permute-start.7
  11.8 0.7 collective-permute-start.9
  12.5 0.1 upper.10
  12.6 0.7 collective-permute-start.11
  13.3 0.3 lower.10
  13.6 0.7 collective-permute-start.10
  14.2 0.7 collective-permute-start.12
  15.0 1.3 %collective-permute-start.14 = (f32[32,256]{1,0:T(8,128)S(1)}, f32[32,256]{1,0:T(8,128)S(1)}, u32[]{:S(2)}, u32[]{:S(2)}) collective-permute-start(f32[32,256]{1,0:T(8,128)S(1)} %get-tuple-element.102), channel_id=1, source_target_pairs={{18,23},{22,19},{25,30},{29,26}} | collective-permute-start | bytes 98312 | tf_op jit(solution)/shard_map/ppermute | solution.py:478
  16.4 1.3 %collective-permute-start.13 = (f32[32,256]{1,0:T(8,128)S(1)}, f32[32,256]{1,0:T(8,128)S(1)}, u32[]{:S(2)}, u32[]{:S(2)}) collective-permute-start(f32[32,256]{1,0:T(8,128)S(1)} %get-tuple-element.101), channel_id=1, source_target_pairs={{11,23},{15,19},{18,30},{22,26}} | collective-permute-start | bytes 98312 | tf_op jit(solution)/shard_map/ppermute | solution.py:481
  17.7 1.3 %collective-permute-start.15 = (f32[32,256]{1,0:T(8,128)S(1)}, f32[32,256]{1,0:T(8,128)S(1)}, u32[]{:S(2)}, u32[]{:S(2)}) collective-permute-start(f32[32,256]{1,0:T(8,128)S(1)} %get-tuple-element.106), channel_id=1, source_target_pairs={{18,23},{22,19},{25,30},{29,26}} | collective-permute-start | bytes 98312 | tf_op jit(solution)/shard_map/ppermute | solution.py:483
  19.0 26.7 %collective-permute-done.14.in_ref = f32[32,256]{1,0:T(8,128)S(1)} collective-permute-done((f32[32,256]{1,0:T(8,128)S(1)}, f32[32,256]{1,0:T(8,128)S(1)}, u32[]{:S(2)}, u32[]{:S(2)}) %collective-permute-start.14) | collective-permute-done | bytes 32800 | tf_op jit(solution)/shard_map/ppermute | solution.py:478
  45.7 1.3 %collective-permute-done.13.trace_x_ref = f32[32,256]{1,0:T(8,128)S(1)} collective-permute-done((f32[32,256]{1,0:T(8,128)S(1)}, f32[32,256]{1,0:T(8,128)S(1)}, u32[]{:S(2)}, u32[]{:S(2)}) %collective-permute-start.13) | collective-permute-done | bytes 32800 | tf_op jit(solution)/shard_map/ppermute | solution.py:481
  47.0 2.2 %upper.12 = (f32[256,256]{1,0:T(8,128)S(1)}, f32[256,256]{1,0:T(8,128)S(1)}, f32[32,256]{1,0:T(8,128)S(1)}, f32[32,256]{1,0:T(8,128)S(1)}) custom-call(s32[1]{0:T(128)} %bitcast.9.active_ref, f32[2,256,256]{2,1,0:T(8,128)S(1)} %get-tuple-element.66.modes_ref, ...), custom_call_target="tpu_custom_call", output_to_operand_aliasing={{0}: (5, {}), {1}: (6, {})} | custom-call | flops 2000000000 | bytes 2000000 | tf_op jit(solution)/shard_map/upper/pallas_call | solution.py:444
  49.2 1.3 %collective-permute-start.17 = (f32[32,256]{1,0:T(8,128)S(1)}, f32[32,256]{1,0:T(8,128)S(1)}, u32[]{:S(2)}, u32[]{:S(2)}) collective-permute-start(f32[32,256]{1,0:T(8,128)S(1)} %get-tuple-element.110), channel_id=1, source_target_pairs={{26,31},{30,27}} | collective-permute-start | bytes 98312 | tf_op jit(solution)/shard_map/ppermute | solution.py:478
  50.5 2.2 %lower.12 = (f32[256,256]{1,0:T(8,128)S(1)}, f32[256,256]{1,0:T(8,128)S(1)}, f32[32,256]{1,0:T(8,128)S(1)}, f32[32,256]{1,0:T(8,128)S(1)}) custom-call(s32[1]{0:T(128)} %bitcast.9.active_ref, f32[2,256,256]{2,1,0:T(8,128)S(1)} %get-tuple-element.66.modes_ref, ...), custom_call_target="tpu_custom_call", output_to_operand_aliasing={{0}: (5, {}), {1}: (6, {})} | custom-call | flops 2000000000 | bytes 2000000 | tf_op jit(solution)/shard_map/lower/pallas_call | solution.py:444
  52.7 0.7 collective-permute-start.16
  53.4 1.3 %collective-permute-start.18 = (f32[32,256]{1,0:T(8,128)S(1)}, f32[32,256]{1,0:T(8,128)S(1)}, u32[]{:S(2)}, u32[]{:S(2)}) collective-permute-start(f32[32,256]{1,0:T(8,128)S(1)} %get-tuple-element.116), channel_id=1, source_target_pairs={{26,31},{30,27}} | collective-permute-start | bytes 98312 | tf_op jit(solution)/shard_map/ppermute | solution.py:483
  54.7 0.3 upper.13
  55.0 0.7 %collective-permute-done.18.trace_y_ref = f32[32,256]{1,0:T(8,128)S(1)} collective-permute-done((f32[32,256]{1,0:T(8,128)S(1)}, f32[32,256]{1,0:T(8,128)S(1)}, u32[]{:S(2)}, u32[]{:S(2)}) %collective-permute-start.18) | collective-permute-done | bytes 32800 | tf_op jit(solution)/shard_map/ppermute | solution.py:483
  55.7 0.3 lower.13
  56.0 1.9 %collective-permute-start.21 = (f32[2,32,256]{2,1,0:T(8,128)S(1)}, f32[2,32,256]{2,1,0:T(8,128)S(1)}, u32[]{:S(2)}, u32[]{:S(2)}) collective-permute-start(f32[2,32,256]{2,1,0:T(8,128)S(1)} %pad_maximum_fusion.1), channel_id=1, source_target_pairs={{1,4},{5,0},{2,5},{6,1},{3,6},{7,2},{9,12},{13,8},{10,13},{14,9},{... | collective-permute-start | bytes 196616 | tf_op jit(solution)/shard_map/ppermute | solution.py:489
  57.9 1.3 %collective-permute-start.20 = (f32[32,256]{1,0:T(8,128)S(1)}, f32[32,256]{1,0:T(8,128)S(1)}, u32[]{:S(2)}, u32[]{:S(2)}) collective-permute-start(f32[32,256]{1,0:T(8,128)S(1)} %get-tuple-element.123), channel_id=1, source_target_pairs={{8,4},{12,0},{9,5},{13,1},{10,6},{14,2},{11,7},{15,3},{16,12},{20,... | collective-permute-start | bytes 98312 | tf_op jit(solution)/shard_map/ppermute | solution.py:488
  59.2 1.1 %finish.1 = (f32[2,2,16,16,128]{4,3,2,1,0:T(8,128)S(1)}, f32[2,2,16,16,128]{4,3,2,1,0:T(8,128)S(1)}) custom-call(s32[1]{0:T(128)} %bitcast.1.core_ref, f32[256,256]{1,0:T(8,128)S(1)} %get-tuple-element.113.total0_ref, f32[256,256]{1,0:T(8,128)S(1)} %get-tuple-element.114.term0_ref, f32[256,256]{1,0:T(8,128)S(1)} %get-tuple-element.119.total1_ref, ...), custom_call_target="tpu_custom_call" | custom-call | tf_op jit(solution)/shard_map/finish/pallas_call | solution.py:492
  60.3 1.0 %collective-permute-start.19 = (f32[2,2,16,16,128]{4,3,2,1,0:T(8,128)S(1)}, f32[2,2,16,16,128]{4,3,2,1,0:T(8,128)S(1)}, u32[]{:S(2)}, u32[]{:S(2)}) collective-permute-start(f32[2,2,16,16,128]{4,3,2,1,0:T(8,128)S(1)} %get-tuple-element.122), channel_id=1, source_target_pairs={{0,4},{4,0},{1,5},{5,1},{2,6},{6,2},{3,7},{7,3},{8,12},{12,8},{9,1... | collective-permute-start | bytes 1572872 | tf_op jit(solution)/shard_map/ppermute | solution.py:501
  61.4 2.5 %collective-permute-done.21.edge_y_ref = f32[2,32,256]{2,1,0:T(8,128)S(1)} collective-permute-done((f32[2,32,256]{2,1,0:T(8,128)S(1)}, f32[2,32,256]{2,1,0:T(8,128)S(1)}, u32[]{:S(2)}, u32[]{:S(2)}) %collective-permute-start.21) | collective-permute-done | bytes 65568 | tf_op jit(solution)/shard_map/ppermute | solution.py:489
  63.8 0.4 collective-permute-start.22
  64.3 0.2 keep.1.keep_rest_ref
  64.5 0.8 %place_wave.1 = f32[2,2,16,16,128]{4,3,2,1,0:T(8,128)} custom-call(s32[1]{0:T(128)} %bitcast.rhs_ref, f32[2,2,16,16,128]{4,3,2,1,0:T(8,128)S(1)} %get-tuple-element.121.keep_ref, f32[2,2,16,16,128]{4,3,2,1,0:T(8,128)S(1)} %collective-permute-done.19.got_ref), custom_call_target="tpu_custom_call" | custom-call | flops 10000000000 | bytes 1000000 | tf_op jit(solution)/shard_map/place_wave/pallas_call | solution.py:514
  65.3 0.9 %place_rest.1 = f32[2,2,16,16,128]{4,3,2,1,0:T(8,128)} custom-call(s32[1]{0:T(128)} %bitcast.1.core_ref, s32[1]{0:T(128)} %bitcast.rhs_ref, f32[2,16,16,128]{3,2,1,0:T(8,128)S(1)} %keep.1.keep_rest_ref, f32[2,2,16,16,128]{4,3,2,1,0:T(8,128)S(1)} %collective-permute-done.19.got_ref, f32[64,256]{1,0:T(8,128)S(1)} %collective-permute-done.22.got_edge_ref, ...), custom_call_target="tpu_custom_call" | custom-call | tf_op jit(solution)/shard_map/place_rest/pallas_call | solution.py:524
  (62 shorter events, 0.6 us)
Async XLA Ops:
  0.6 2.0 %copy-start = (f32[2,16,2]{1,2,0:T(2,128)S(1)}, f32[2,16,2]{1,2,0:T(2,128)}, u32[]{:S(2)}) copy-start(f32[2,16,2]{1,2,0:T(2,128)} %param.15) | copy-start | bytes 772
  0.6 2.1 %copy-start.8 = (f32[256,1]{1,0:T(8,128)S(1)}, f32[256,1]{1,0:T(8,128)}, u32[]{:S(2)}) copy-start(f32[256,1]{1,0:T(8,128)} %constant.163.clone.edge_ref) | copy-start | bytes 3076
  0.7 1.1 %copy-start.4 = (f32[16,16,128]{2,1,0:T(8,128)S(1)}, f32[16,16,128]{2,1,0:T(8,128)}, u32[]{:S(2)}) copy-start(f32[16,16,128]{2,1,0:T(8,128)} %slow_ref.1) | copy-start | bytes 393220
  0.7 1.9 %copy-start.11 = (s32[2,16]{1,0:T(2,128)S(1)}, s32[2,16]{1,0:T(2,128)}, u32[]{:S(2)}) copy-start(s32[2,16]{1,0:T(2,128)} %param.14) | copy-start | bytes 388
  0.7 2.0 %copy-start.5 = (f32[2,256,128]{2,1,0:T(8,128)S(1)}, f32[2,256,128]{2,1,0:T(8,128)}, u32[]{:S(2)}) copy-start(f32[2,256,128]{2,1,0:T(8,128)} %constant.156.clone.inverse_ref.refs_0_) | copy-start | bytes 786436
  0.7 2.0 %copy-start.6 = (bf16[2,2,128,192]{3,2,1,0:T(8,128)(2,1)S(1)}, bf16[2,2,128,192]{3,2,1,0:T(8,128)(2,1)}, u32[]{:S(2)}) copy-start(bf16[2,2,128,192]{3,2,1,0:T(8,128)(2,1)} %constant.157.clone.forward_ref.refs_1_) | copy-start | bytes 589828
  1.8 1.1 %copy-start.3 = (f32[2,2,16,16,128]{4,3,2,1,0:T(8,128)S(1)}, f32[2,2,16,16,128]{4,3,2,1,0:T(8,128)}, u32[]{:S(2)}) copy-start(f32[2,2,16,16,128]{4,3,2,1,0:T(8,128)} %right_ref.1) | copy-start | bytes 1572868
  1.8 1.1 %copy-start.1 = (bf16[256,256]{1,0:T(8,128)(2,1)S(1)}, bf16[256,256]{1,0:T(8,128)(2,1)}, u32[]{:S(2)}) copy-start(bf16[256,256]{1,0:T(8,128)(2,1)} %constant.159.clone.z_ref.refs_3_) | copy-start | bytes 393220
  1.9 2.1 %collective-permute-start = (f32[3,16,16,128]{3,2,1,0:T(8,128)S(1)}, f32[3,16,16,128]{3,2,1,0:T(8,128)S(1)}, u32[]{:S(2)}, u32[]{:S(2)}) collective-permute-start(f32[3,16,16,128]{3,2,1,0:T(8,128)S(1)} %pad_maximum_fusion), channel_id=1, source_target_pairs={{0,4},{4,0},{1,5},{5,1},{2,6},{6,2},{3,7},{7,3},{8,12},{12,8},{9,1... | collective-permute-start | bytes 1179656 | tf_op jit(solution)/shard_map/ppermute | solution.py:406
  4.8 1.0 %copy-start.2 = (bf16[2,2,128,192]{3,2,1,0:T(8,128)(2,1)S(1)}, bf16[2,2,128,192]{3,2,1,0:T(8,128)(2,1)}, u32[]{:S(2)}) copy-start(bf16[2,2,128,192]{3,2,1,0:T(8,128)(2,1)} %constant.158.clone.refs_2_.backward_ref) | copy-start | bytes 589828
  4.8 0.9 %copy-start.7 = (bf16[256,192]{1,0:T(8,128)(2,1)S(1)}, bf16[256,192]{1,0:T(8,128)(2,1)}, u32[]{:S(2)}) copy-start(bf16[256,192]{1,0:T(8,128)(2,1)} %constant.160.clone.refs_4_) | copy-start | bytes 294916
  4.8 1.0 %copy-start.9 = (bf16[64,768]{1,0:T(8,128)(2,1)S(1)}, bf16[64,768]{1,0:T(8,128)(2,1)}, u32[]{:S(2)}) copy-start(bf16[64,768]{1,0:T(8,128)(2,1)} %constant.161.clone.refs_5_) | copy-start | bytes 294916
  5.9 2.2 %collective-permute-start.2 = (f32[32,256]{1,0:T(8,128)S(1)}, f32[32,256]{1,0:T(8,128)S(1)}, u32[]{:S(2)}, u32[]{:S(2)}) collective-permute-start(f32[32,256]{1,0:T(8,128)S(1)} %get-tuple-element.70), channel_id=1, source_target_pairs={{0,5},{4,1}} | collective-permute-start | bytes 98312 | tf_op jit(solution)/shard_map/ppermute | solution.py:478
  6.7 1.4 %collective-permute-start.1 = (f32[32,256]{1,0:T(8,128)S(1)}, f32[32,256]{1,0:T(8,128)S(1)}, u32[]{:S(2)}, u32[]{:S(2)}) collective-permute-start(f32[32,256]{1,0:T(8,128)S(1)} %get-tuple-element.69), channel_id=1, source_target_pairs={{0,12},{4,8}} | collective-permute-start | bytes 98312 | tf_op jit(solution)/shard_map/ppermute | solution.py:481
  7.4 1.5 %collective-permute-start.3 = (f32[32,256]{1,0:T(8,128)S(1)}, f32[32,256]{1,0:T(8,128)S(1)}, u32[]{:S(2)}, u32[]{:S(2)}) collective-permute-start(f32[32,256]{1,0:T(8,128)S(1)} %get-tuple-element.74), channel_id=1, source_target_pairs={{0,5},{4,1}} | collective-permute-start | bytes 98312 | tf_op jit(solution)/shard_map/ppermute | solution.py:483
  8.2 2.1 %collective-permute-start.5 = (f32[32,256]{1,0:T(8,128)S(1)}, f32[32,256]{1,0:T(8,128)S(1)}, u32[]{:S(2)}, u32[]{:S(2)}) collective-permute-start(f32[32,256]{1,0:T(8,128)S(1)} %get-tuple-element.78), channel_id=1, source_target_pairs={{1,6},{5,2},{8,13},{12,9}} | collective-permute-start | bytes 98312 | tf_op jit(solution)/shard_map/ppermute | solution.py:478
  8.9 1.4 %collective-permute-start.4 = (f32[32,256]{1,0:T(8,128)S(1)}, f32[32,256]{1,0:T(8,128)S(1)}, u32[]{:S(2)}, u32[]{:S(2)}) collective-permute-start(f32[32,256]{1,0:T(8,128)S(1)} %get-tuple-element.77), channel_id=1, source_target_pairs={{1,13},{5,9},{8,20},{12,16}} | collective-permute-start | bytes 98312 | tf_op jit(solution)/shard_map/ppermute | solution.py:481
  9.6 1.5 %collective-permute-start.6 = (f32[32,256]{1,0:T(8,128)S(1)}, f32[32,256]{1,0:T(8,128)S(1)}, u32[]{:S(2)}, u32[]{:S(2)}) collective-permute-start(f32[32,256]{1,0:T(8,128)S(1)} %get-tuple-element.82), channel_id=1, source_target_pairs={{1,6},{5,2},{8,13},{12,9}} | collective-permute-start | bytes 98312 | tf_op jit(solution)/shard_map/ppermute | solution.py:483
  10.4 2.1 %collective-permute-start.8 = (f32[32,256]{1,0:T(8,128)S(1)}, f32[32,256]{1,0:T(8,128)S(1)}, u32[]{:S(2)}, u32[]{:S(2)}) collective-permute-start(f32[32,256]{1,0:T(8,128)S(1)} %get-tuple-element.86), channel_id=1, source_target_pairs={{2,7},{6,3},{9,14},{13,10},{16,21},{20,17}} | collective-permute-start | bytes 98312 | tf_op jit(solution)/shard_map/ppermute | solution.py:478
  11.2 1.4 %collective-permute-start.7 = (f32[32,256]{1,0:T(8,128)S(1)}, f32[32,256]{1,0:T(8,128)S(1)}, u32[]{:S(2)}, u32[]{:S(2)}) collective-permute-start(f32[32,256]{1,0:T(8,128)S(1)} %get-tuple-element.85), channel_id=1, source_target_pairs={{2,14},{6,10},{9,21},{13,17},{16,28},{20,24}} | collective-permute-start | bytes 98312 | tf_op jit(solution)/shard_map/ppermute | solution.py:481
  11.8 1.5 %collective-permute-start.9 = (f32[32,256]{1,0:T(8,128)S(1)}, f32[32,256]{1,0:T(8,128)S(1)}, u32[]{:S(2)}, u32[]{:S(2)}) collective-permute-start(f32[32,256]{1,0:T(8,128)S(1)} %get-tuple-element.90), channel_id=1, source_target_pairs={{2,7},{6,3},{9,14},{13,10},{16,21},{20,17}} | collective-permute-start | bytes 98312 | tf_op jit(solution)/shard_map/ppermute | solution.py:483
  12.6 2.3 %collective-permute-start.11 = (f32[32,256]{1,0:T(8,128)S(1)}, f32[32,256]{1,0:T(8,128)S(1)}, u32[]{:S(2)}, u32[]{:S(2)}) collective-permute-start(f32[32,256]{1,0:T(8,128)S(1)} %get-tuple-element.94), channel_id=1, source_target_pairs={{10,15},{14,11},{17,22},{21,18},{24,29},{28,25}} | collective-permute-start | bytes 98312 | tf_op jit(solution)/shard_map/ppermute | solution.py:478
  13.6 1.4 %collective-permute-start.10 = (f32[32,256]{1,0:T(8,128)S(1)}, f32[32,256]{1,0:T(8,128)S(1)}, u32[]{:S(2)}, u32[]{:S(2)}) collective-permute-start(f32[32,256]{1,0:T(8,128)S(1)} %get-tuple-element.93), channel_id=1, source_target_pairs={{3,15},{7,11},{10,22},{14,18},{17,29},{21,25}} | collective-permute-start | bytes 98312 | tf_op jit(solution)/shard_map/ppermute | solution.py:481
  14.2 2.1 %collective-permute-start.12 = (f32[32,256]{1,0:T(8,128)S(1)}, f32[32,256]{1,0:T(8,128)S(1)}, u32[]{:S(2)}, u32[]{:S(2)}) collective-permute-start(f32[32,256]{1,0:T(8,128)S(1)} %get-tuple-element.98), channel_id=1, source_target_pairs={{10,15},{14,11},{17,22},{21,18},{24,29},{28,25}} | collective-permute-start | bytes 98312 | tf_op jit(solution)/shard_map/ppermute | solution.py:483
  15.0 30.7 %collective-permute-start.14 = (f32[32,256]{1,0:T(8,128)S(1)}, f32[32,256]{1,0:T(8,128)S(1)}, u32[]{:S(2)}, u32[]{:S(2)}) collective-permute-start(f32[32,256]{1,0:T(8,128)S(1)} %get-tuple-element.102), channel_id=1, source_target_pairs={{18,23},{22,19},{25,30},{29,26}} | collective-permute-start | bytes 98312 | tf_op jit(solution)/shard_map/ppermute | solution.py:478
  16.4 30.6 %collective-permute-start.13 = (f32[32,256]{1,0:T(8,128)S(1)}, f32[32,256]{1,0:T(8,128)S(1)}, u32[]{:S(2)}, u32[]{:S(2)}) collective-permute-start(f32[32,256]{1,0:T(8,128)S(1)} %get-tuple-element.101), channel_id=1, source_target_pairs={{11,23},{15,19},{18,30},{22,26}} | collective-permute-start | bytes 98312 | tf_op jit(solution)/shard_map/ppermute | solution.py:481
  17.7 32.8 %collective-permute-start.15 = (f32[32,256]{1,0:T(8,128)S(1)}, f32[32,256]{1,0:T(8,128)S(1)}, u32[]{:S(2)}, u32[]{:S(2)}) collective-permute-start(f32[32,256]{1,0:T(8,128)S(1)} %get-tuple-element.106), channel_id=1, source_target_pairs={{18,23},{22,19},{25,30},{29,26}} | collective-permute-start | bytes 98312 | tf_op jit(solution)/shard_map/ppermute | solution.py:483
  49.2 5.5 %collective-permute-start.17 = (f32[32,256]{1,0:T(8,128)S(1)}, f32[32,256]{1,0:T(8,128)S(1)}, u32[]{:S(2)}, u32[]{:S(2)}) collective-permute-start(f32[32,256]{1,0:T(8,128)S(1)} %get-tuple-element.110), channel_id=1, source_target_pairs={{26,31},{30,27}} | collective-permute-start | bytes 98312 | tf_op jit(solution)/shard_map/ppermute | solution.py:478
  50.5 4.2 %copy-start.10 = (bf16[64,768]{1,0:T(8,128)(2,1)S(1)}, bf16[64,768]{1,0:T(8,128)(2,1)}, u32[]{:S(2)}) copy-start(bf16[64,768]{1,0:T(8,128)(2,1)} %constant.162.clone.refs_6_) | copy-start | bytes 294916
  52.7 2.0 %collective-permute-start.16 = (f32[32,256]{1,0:T(8,128)S(1)}, f32[32,256]{1,0:T(8,128)S(1)}, u32[]{:S(2)}, u32[]{:S(2)}) collective-permute-start(f32[32,256]{1,0:T(8,128)S(1)} %get-tuple-element.109), channel_id=1, source_target_pairs={{19,31},{23,27}} | collective-permute-start | bytes 98312 | tf_op jit(solution)/shard_map/ppermute | solution.py:481
  53.4 2.3 %collective-permute-start.18 = (f32[32,256]{1,0:T(8,128)S(1)}, f32[32,256]{1,0:T(8,128)S(1)}, u32[]{:S(2)}, u32[]{:S(2)}) collective-permute-start(f32[32,256]{1,0:T(8,128)S(1)} %get-tuple-element.116), channel_id=1, source_target_pairs={{26,31},{30,27}} | collective-permute-start | bytes 98312 | tf_op jit(solution)/shard_map/ppermute | solution.py:483
  56.0 7.9 %collective-permute-start.21 = (f32[2,32,256]{2,1,0:T(8,128)S(1)}, f32[2,32,256]{2,1,0:T(8,128)S(1)}, u32[]{:S(2)}, u32[]{:S(2)}) collective-permute-start(f32[2,32,256]{2,1,0:T(8,128)S(1)} %pad_maximum_fusion.1), channel_id=1, source_target_pairs={{1,4},{5,0},{2,5},{6,1},{3,6},{7,2},{9,12},{13,8},{10,13},{14,9},{... | collective-permute-start | bytes 196616 | tf_op jit(solution)/shard_map/ppermute | solution.py:489
  57.9 5.9 %collective-permute-start.20 = (f32[32,256]{1,0:T(8,128)S(1)}, f32[32,256]{1,0:T(8,128)S(1)}, u32[]{:S(2)}, u32[]{:S(2)}) collective-permute-start(f32[32,256]{1,0:T(8,128)S(1)} %get-tuple-element.123), channel_id=1, source_target_pairs={{8,4},{12,0},{9,5},{13,1},{10,6},{14,2},{11,7},{15,3},{16,12},{20,... | collective-permute-start | bytes 98312 | tf_op jit(solution)/shard_map/ppermute | solution.py:488
  60.3 4.1 %collective-permute-start.19 = (f32[2,2,16,16,128]{4,3,2,1,0:T(8,128)S(1)}, f32[2,2,16,16,128]{4,3,2,1,0:T(8,128)S(1)}, u32[]{:S(2)}, u32[]{:S(2)}) collective-permute-start(f32[2,2,16,16,128]{4,3,2,1,0:T(8,128)S(1)} %get-tuple-element.122), channel_id=1, source_target_pairs={{0,4},{4,0},{1,5},{5,1},{2,6},{6,2},{3,7},{7,3},{8,12},{12,8},{9,1... | collective-permute-start | bytes 1572872 | tf_op jit(solution)/shard_map/ppermute | solution.py:501
  63.8 1.5 %collective-permute-start.22 = (f32[64,256]{1,0:T(8,128)S(1)}, f32[64,256]{1,0:T(8,128)S(1)}, u32[]{:S(2)}, u32[]{:S(2)}) collective-permute-start(f32[64,256]{1,0:T(8,128)S(1)} %pad_maximum_fusion.2), channel_id=1, source_target_pairs={{0,4},{4,0},{1,5},{5,1},{2,6},{6,2},{3,7},{7,3},{8,12},{12,8},{9,1... | collective-permute-start | bytes 196616 | tf_op jit(solution)/shard_map/ppermute | solution.py:504

commit v9 on v8

--- a/solution.py
+++ b/solution.py
@@ -54,11 +54,8 @@
     inverse = np.stack([real_part / denominator, KAPPA * DAMPING / denominator]).astype(np.float32)
 
     parity = [np.kron(sine_x[order[p * half : (p + 1) * half]][:, :half], sine_y) for p in (0, 1)]
-    cut = half * size_y // 2
-    forward, backward = [
-        np.stack([[left_factor(m[:, :cut]), left_factor(m[:, cut:])] for m in matrices])
-        for matrices in (parity, [m.T for m in parity])
-    ]
+    forward = [left_factor(m) for m in parity]
+    backward = [left_factor(m.T) for m in parity]
     high_z, low_z = halves(sine_z)
     right_z = np.concatenate([np.concatenate([high_z, low_z], axis=1)] * 2, axis=0)
 
@@ -94,11 +91,38 @@
     edge[-1] += 1.0 / 12.0
     edge[:, 0] += 1.0 / 12.0
     edge[:, -1] += 1.0 / 12.0
-    edge = edge[cells].reshape(size_x * size_y, 1).astype(np.float32)
-    return dict(
-        inverse=inverse, forward=forward, backward=backward, right_z=right_z,
-        enter=enter, leave=leave, first=first, edge=edge,
-    ), cells
+    edge = edge[cells].reshape(1, size_x * size_y, 1) + np.zeros((1, 1, cells_z))
+    fields = np.concatenate([inverse, edge.astype(np.float32)], axis=0)
+
+    matrices = dict(
+        forward0=forward[0], forward1=forward[1], backward0=backward[0], backward1=backward[1],
+        right_z=right_z, enter=enter, leave=leave, first=first,
+    )
+    width = 128 * max(-(-m.shape[1] // 128) for m in matrices.values())
+    places, rows, at = {}, 0, 0
+    height = 0
+    for name, m in sorted(matrices.items(), key=lambda item: -item[1].shape[0]):
+        if at + m.shape[1] > width:
+            rows, at, height = rows + height, 0, 0
+        places[name] = (rows, at, *m.shape)
+        height = max(height, -(-m.shape[0] // 16) * 16)
+        at += -(-m.shape[1] // 128) * 128
+    packed = np.zeros((rows + height, width), ml_dtypes.bfloat16)
+    for name, (row, lane, count, lanes) in places.items():
+        packed[row : row + count, lane : lane + lanes] = matrices[name]
+    return fields, packed, places, tuple(int(x) for x in cells)
+
+
+class Tables:
+    def __init__(self, places, fields_ref, packed_ref):
+        self.places, self.fields, self.packed = places, fields_ref, packed_ref
+
+    def __getitem__(self, name):
+        row, lane, count, lanes = self.places[name]
+        return self.packed[row : row + count, lane : lane + lanes]
+
+    def divide(self, modes):
+        return times(self.fields[0], self.fields[1], modes)
 
 
 def split(values):
@@ -115,41 +139,28 @@
     return jnp.dot(matrix, stacked(values), preferred_element_type=F32)
 
 
-def z_transform(field, right_z):
+def z_transform(field, t):
     rows = field.shape[0]
     cells_z = field.shape[1] // 2
     high, low = split(jnp.concatenate([field[:, :cells_z], field[:, cells_z:]], axis=0))
-    both = jnp.dot(jnp.concatenate([high, low], axis=1), right_z, preferred_element_type=F32)
+    both = jnp.dot(jnp.concatenate([high, low], axis=1), t["right_z"], preferred_element_type=F32)
     total = both[:, :cells_z] + both[:, cells_z:]
     return jnp.concatenate([total[:rows], total[rows:]], axis=1)
 
 
-def sum_products(matrices, values):
-    products = [[left_product(matrices[p, h], values[p][h]) for p in range(2)] for h in range(2)]
-    return [sum(parts) for parts in zip(*products)]
-
-
-def to_modes(first, second, forward):
-    folded = [[join(f, s) for f, s in zip(first, second)] for join in (jnp.add, jnp.subtract)]
-    return sum_products(forward, folded)
-
-
-def to_cells(modes, backward):
-    even, odd = sum_products(backward, modes)
-    return even + odd, even - odd
-
-
-def in_two(values):
-    count = values.shape[0] // 2
-    return values[:count], values[count:]
-
-
-def in_parities(modes):
-    return [in_two(part) for part in in_two(modes)]
-
-
-def whole_field(first, second):
-    return jnp.concatenate([first, second], axis=0)
+def to_modes(field, t):
+    count = field.shape[0] // 2
+    first, second = field[:count], field[count:]
+    return jnp.concatenate(
+        [left_product(t["forward0"], first + second), left_product(t["forward1"], first - second)], axis=0
+    )
+
+
+def to_cells(modes, t):
+    count = modes.shape[0] // 2
+    even = left_product(t["backward0"], modes[:count])
+    odd = left_product(t["backward1"], modes[count:])
+    return jnp.concatenate([even + odd, even - odd], axis=0)
 
 
 def times(real_part, imag_part, field):
@@ -160,43 +171,24 @@
     )
 
 
-def divide(modes, inverse):
-    return times(inverse[0], inverse[1], modes)
+def apply_contrast(field, contrast, t, block=64):
+    done = []
+    for start in range(0, field.shape[0], block):
+        here = slice(start, start + block)
+        cells = times(contrast[0, here], contrast[1, here], z_transform(field[here], t))
+        done.append(z_transform(cells, t))
+    return jnp.concatenate(done, axis=0)
 
 
 def solve_modes(start, contrast, t):
-    count = start.shape[0] // 4
-    term = in_parities(start)
-    total = term
+    term = total = start
     for _ in range(2):
-        first, second = [in_two(cells) for cells in to_cells(term, t["backward"])]
-        blocks = [z_transform(jnp.concatenate(pair, axis=0), t["right_z"]) for pair in zip(first, second)]
-        parts = []
-        for h, block in enumerate(blocks):
-            here = [slice(at, at + count) for at in (h * count, (h + 2) * count)]
-            factor = [jnp.concatenate([contrast[c, rows] for rows in here], axis=0) for c in range(2)]
-            parts.append(in_two(z_transform(times(*factor, block), t["right_z"])))
-        modes = to_modes(*zip(*parts), t["forward"])
-        term = []
-        for p in range(2):
-            halves = []
-            for h, part in enumerate(in_two(modes[p])):
-                here = slice((2 * p + h) * count, (2 * p + h + 1) * count)
-                halves.append(times(t["inverse"][0, here], t["inverse"][1, here], part))
-            term.append(halves)
-        total = [[a + b for a, b in zip(*pair)] for pair in zip(total, term)]
-    return [jnp.concatenate([part for pair in both for part in pair], axis=0) for both in (total, term)]
-
-
-PREP = ("edge", "inverse", "forward", "right_z")
-BEAT = ("inverse", "forward", "backward", "right_z", "enter", "leave")
-
-
-def hand_on_kernel(in_ref, out_ref):
-    out_ref[...] = in_ref[...]
-
-
-def prepare(dense, slow, place, depth, amplitude, edge, inverse, forward, right_z, modes_ref, contrast_ref):
+        term = t.divide(to_modes(apply_contrast(to_cells(term, t), contrast, t), t))
+        total = total + term
+    return total, term
+
+
+def prepare(dense, slow, place, depth, amplitude, t, modes_ref, contrast_ref):
     rows, cells_z = contrast_ref.shape[1:]
     points = place.shape[1]
     row_ids = lax.broadcasted_iota(jnp.int32, (rows, points), 0)
@@ -210,29 +202,32 @@
         parts = [at_lane * part for part in (one, two, amp - one - two)]
         spread.append(jnp.concatenate(parts, axis=1).astype(BF16))
     scaled = KAPPA * (slow - 1.0)
-    contrast_ref[0] = scaled - edge
+    contrast_ref[0] = scaled - t.fields[2]
     contrast_ref[1] = DAMPING * scaled
     at_row = (row_ids == place).astype(F32).astype(BF16)
     field = lax.dot_general(
         jnp.concatenate([at_row] * 3, axis=1), jnp.concatenate(spread, axis=0),
         (((1,), (1,)), ((), ())), preferred_element_type=F32,
     )
-    first, second = [in_two(part) for part in in_two(z_transform(field + dense, right_z))]
-    modes_ref[...] = divide(jnp.concatenate(to_modes(first, second, forward), axis=0), inverse)
-
-
-def prep_kernel(cells_x, rhs_ref, right_ref, slow_ref, place_ref, depth_ref, amp_ref, edge_ref,
-                inverse_ref, forward_ref, z_ref, modes_ref, contrast_ref):
+    modes_ref[...] = t.divide(to_modes(z_transform(field + dense, t), t))
+
+
+def hand_on_kernel(in_ref, out_ref):
+    out_ref[...] = in_ref[...]
+
+
+def prep_kernel(cells_x, places, rhs_ref, right_ref, slow_ref, place_ref, depth_ref, amp_ref, fields_ref,
+                packed_ref, modes_ref, contrast_ref):
     dense = [jnp.concatenate([right_ref[rhs_ref[0], c, x] for x in cells_x], axis=0) for c in range(2)]
     slow = jnp.concatenate([slow_ref[x] for x in cells_x], axis=0)
     prepare(
-        jnp.concatenate(dense, axis=1), slow, place_ref[...], depth_ref[...], amp_ref, edge_ref[...],
-        inverse_ref, forward_ref, z_ref[...], modes_ref, contrast_ref,
-    )
-
-
-def prep_other_kernel(cells_x, core_ref, swap_ref, own_modes_ref, own_contrast_ref, place_ref, depth_ref,
-                      amp_ref, edge_ref, inverse_ref, forward_ref, z_ref, modes_ref, contrast_ref):
+        jnp.concatenate(dense, axis=1), slow, place_ref[...], depth_ref[...], amp_ref,
+        Tables(places, fields_ref, packed_ref), modes_ref, contrast_ref,
+    )
+
+
+def prep_other_kernel(cells_x, places, core_ref, swap_ref, own_modes_ref, own_contrast_ref, place_ref, depth_ref,
+                      amp_ref, fields_ref, packed_ref, modes_ref, contrast_ref):
     core = core_ref[0]
     other = 1 - core
     modes_ref[core] = own_modes_ref[...]
@@ -240,27 +235,24 @@
     parts = [jnp.concatenate([swap_ref[c, x] for x in cells_x], axis=0) for c in range(3)]
     prepare(
         jnp.concatenate(parts[:2], axis=1), parts[2], place_ref[...], depth_ref[...], amp_ref,
-        edge_ref[...], inverse_ref, forward_ref, z_ref[...], modes_ref.at[other], contrast_ref.at[other],
-    )
-
-
-def beat_kernel(tile, final, active_ref, modes_ref, contrast_ref, trace_x_ref, trace_y_ref, total_ref, term_ref,
-                *refs):
-    names = LAST if final else BEAT
-    t = {name: ref for name, ref in zip(names, refs)}
-    new_total_ref, new_term_ref, *out_refs = refs[len(names) :]
+        Tables(places, fields_ref, packed_ref), modes_ref.at[other], contrast_ref.at[other],
+    )
+
+
+def beat_kernel(tile, final, places, active_ref, modes_ref, contrast_ref, trace_x_ref, trace_y_ref, total_ref,
+                term_ref, fields_ref, packed_ref, new_total_ref, new_term_ref, *out_refs):
+    t = Tables(places, fields_ref, packed_ref)
     count = trace_x_ref.shape[0]
 
     @pl.when(active_ref[0] == 1)
     def _():
-        local = dict(t, right_z=t["right_z"][...])
         trace = jnp.concatenate([trace_x_ref[...], trace_y_ref[...]], axis=0)
-        start = modes_ref[tile] + divide(left_product(t["enter"][...], trace), t["inverse"])
-        total, term = solve_modes(start, contrast_ref.at[tile], local)
+        start = modes_ref[tile] + t.divide(left_product(t["enter"], trace))
+        total, term = solve_modes(start, contrast_ref.at[tile], t)
         new_total_ref[...] = total
         new_term_ref[...] = term
         if not (final and tile == 1):
-            out = left_product(t["leave"][...], total)
+            out = left_product(t["leave"], total)
             for out_ref, part in zip(out_refs[:1] if final else out_refs, (out[:count], out[count:])):
                 out_ref[...] = part
 
@@ -270,26 +262,19 @@
         new_term_ref[...] = term_ref[...]
 
     if final:
-        out = left_product(t["first"][...], new_total_ref[...])
+        out = left_product(t["first"], new_total_ref[...])
         edge_refs = out_refs[1 - tile :]
         edge_refs[-1][...] = out[count:]
         if tile == 0:
             edge_refs[0][...] = out[:count]
 
 
-LAST = BEAT + ("first",)
-FINISH = ("backward", "right_z")
-
-
-def finish_kernel(cells_x, core_ref, total0_ref, term0_ref, total1_ref, term1_ref, contrast_ref, backward_ref,
-                  z_ref, keep_ref, give_ref, both_ref):
+def finish_kernel(cells_x, places, core_ref, total0_ref, term0_ref, total1_ref, term1_ref, contrast_ref,
+                  fields_ref, packed_ref, keep_ref, give_ref, both_ref):
     _, _, _, size_x, size_y, cells_z = both_ref.shape
-    right_z = z_ref[...]
+    t = Tables(places, fields_ref, packed_ref)
     for tile, (total_ref, term_ref) in enumerate(((total0_ref, term0_ref), (total1_ref, term1_ref))):
-        wave, rest = [
-            z_transform(whole_field(*to_cells(in_parities(ref[...]), backward_ref)), right_z)
-            for ref in (total_ref, term_ref)
-        ]
+        wave, rest = [z_transform(to_cells(ref[...], t), t) for ref in (total_ref, term_ref)]
         rest = times(contrast_ref[tile, 0], contrast_ref[tile, 1], rest)
         for place, x in enumerate(cells_x):
             here = slice(place * size_y, (place + 1) * size_y)
@@ -320,11 +305,11 @@
         rest_ref[c, :, size_y - 2 :] += two
 
 
-def keep_kernel(core_ref, keep_ref, edge_x_ref, edge_y_ref, z_ref, rest_ref):
+def keep_kernel(places, core_ref, keep_ref, edge_x_ref, edge_y_ref, packed_ref, rest_ref):
     rest_ref[...] = keep_ref[1]
     count = edge_x_ref.shape[0]
     edges = jnp.concatenate([edge_x_ref[...], edge_y_ref[core_ref[0]]], axis=0)
-    edges = z_transform(edges, z_ref[...])
+    edges = z_transform(edges, Tables(places, None, packed_ref))
     add_later(rest_ref, edges[:count], edges[count:], (core_ref[0] == 1).astype(F32))
 
 
@@ -340,13 +325,14 @@
         copy.wait()
 
 
-def place_rest_kernel(core_ref, rhs_ref, keep_rest_ref, got_ref, got_edge_ref, z_ref, rest_ref, work_ref, sems):
+def place_rest_kernel(places, core_ref, rhs_ref, keep_rest_ref, got_ref, got_edge_ref, packed_ref, rest_ref, work_ref,
+                      sems):
     rhs = rhs_ref[0]
     count = got_edge_ref.shape[0] // 2
     copies = [pltpu.make_async_copy(keep_rest_ref, rest_ref.at[rhs], sems.at[0])]
     copies[0].start()
     work_ref[...] = got_ref[1]
-    edges = z_transform(got_edge_ref[...], z_ref[...])
+    edges = z_transform(got_edge_ref[...], Tables(places, None, packed_ref))
     add_later(work_ref, edges[:count], edges[count:], (core_ref[0] == 1).astype(F32))
     copies.append(pltpu.make_async_copy(work_ref, rest_ref.at[1 - rhs], sems.at[1]))
     copies[1].start()
@@ -384,9 +370,8 @@
     core = row % 2
     rhs = (core + row // 2 + col) % 2
     core_ref, rhs_ref = core[None], rhs[None]
-    t, cells_x = tables(size_x, size_y, cells_z)
-    t = {name: jnp.asarray(value) for name, value in t.items()}
-    cells_x = tuple(int(x) for x in cells_x)
+    fields, packed, table_places, cells_x = tables(size_x, size_y, cells_z)
+    fields, packed = jnp.asarray(fields), jnp.asarray(packed)
     rows = size_x * size_y
 
     def device(chip, core, column):
@@ -417,40 +402,39 @@
     amplitudes = lax.dynamic_index_in_dim(source_amplitudes, rhs, 0, keepdims=False).T[:, None, :]
 
     depth = cells % cells_z
-    prep_tables = [t[name] for name in PREP]
     one = (shaped(rows, 2 * cells_z), shaped(2, rows, cells_z))
     own_modes, own_contrast = pl.pallas_call(
-        functools.partial(prep_kernel, cells_x),
+        functools.partial(prep_kernel, cells_x, table_places),
         out_shape=one,
-        in_specs=[scalars()] + [whole()] * 9,
+        in_specs=[scalars()] + [whole()] * 7,
         out_specs=(whole(), whole()),
         compiler_params=PARAMS,
         cost_estimate=SOLVE_COST,
         name="prep",
-    )(rhs_ref, right_side, slowness, places[0], depth, amplitudes, *prep_tables)
+    )(rhs_ref, right_side, slowness, places[0], depth, amplitudes, fields, packed)
     modes, contrast = pl.pallas_call(
-        functools.partial(prep_other_kernel, cells_x),
+        functools.partial(prep_other_kernel, cells_x, table_places),
         out_shape=(shaped(2, rows, 2 * cells_z), shaped(2, 2, rows, cells_z)),
-        in_specs=[scalars()] + [whole()] * 10,
+        in_specs=[scalars()] + [whole()] * 8,
         out_specs=(whole(), whole()),
         compiler_params=PARAMS,
         cost_estimate=SOLVE_COST,
         name="prep_other",
-    )(core_ref, swapped, own_modes, own_contrast, places[1], depth, amplitudes, *prep_tables)
+    )(core_ref, swapped, own_modes, own_contrast, places[1], depth, amplitudes, fields, packed)
 
     def solve(tile, active, trace_x, trace_y, state, final):
         x, y = shaped(*zero_x.shape), shaped(*zero_y.shape)
         outs = ((x, x, y), (y,))[tile] if final else (x, y)
         total, term, *outs = pl.pallas_call(
-            functools.partial(beat_kernel, tile, final),
+            functools.partial(beat_kernel, tile, final, table_places),
             out_shape=(shaped(rows, 2 * cells_z),) * 2 + outs,
-            in_specs=[scalars()] + [whole()] * (6 + len(LAST if final else BEAT)),
+            in_specs=[scalars()] + [whole()] * 8,
             out_specs=(whole(),) * (2 + len(outs)),
             input_output_aliases={5: 0, 6: 1},
             compiler_params=PARAMS,
             cost_estimate=SOLVE_COST,
             name="upper" if tile == 0 else "lower",
-        )(active, modes, contrast, trace_x, trace_y, *state, *[t[name] for name in (LAST if final else BEAT)])
+        )(active, modes, contrast, trace_x, trace_y, *state, fields, packed)
         return (total, term), outs
 
     def hand_on(trace):
@@ -490,27 +474,27 @@
 
     half = shaped(2, 2, size_x, size_y, cells_z)
     keep, give = pl.pallas_call(
-        functools.partial(finish_kernel, cells_x),
+        functools.partial(finish_kernel, cells_x, table_places),
         out_shape=(half, half),
-        in_specs=[scalars()] + [whole()] * (5 + len(FINISH)),
+        in_specs=[scalars()] + [whole()] * 7,
         out_specs=(whole(), whole()),
         scratch_shapes=[pltpu.VMEM((2, 2, 2, size_x, size_y, cells_z), F32)],
         compiler_params=PARAMS,
         name="finish",
-    )(core_ref, *states[0], *states[1], contrast, *[t[name] for name in FINISH])
+    )(core_ref, *states[0], *states[1], contrast, fields, packed)
     got = lax.ppermute(give, axes, own)
 
     pass_y = lax.dynamic_index_in_dim(after_y, 1 - core, 0, keepdims=False)
     got_edge = lax.ppermute(jnp.concatenate([after_x, pass_y], axis=0), axes, own)
     keep_rest = pl.pallas_call(
-        keep_kernel,
+        functools.partial(keep_kernel, table_places),
         out_shape=shaped(*half.shape[1:]),
         in_specs=[scalars()] + [whole()] * 4,
         out_specs=whole(),
         compiler_params=PARAMS,
         cost_estimate=KEEP_COST,
         name="keep",
-    )(core_ref, keep, after_x, after_y, t["right_z"])
+    )(core_ref, keep, after_x, after_y, packed)
     wavefield = pl.pallas_call(
         place_wave_kernel,
         out_shape=shaped(*right_side.shape),
@@ -522,7 +506,7 @@
         name="place_wave",
     )(rhs_ref, keep, got)
     residual = pl.pallas_call(
-        place_rest_kernel,
+        functools.partial(place_rest_kernel, table_places),
         out_shape=shaped(*right_side.shape),
         in_specs=[scalars()] * 2 + [whole()] * 4,
         out_specs=anywhere(),
@@ -532,7 +516,7 @@
         ],
         compiler_params=PARAMS,
         name="place_rest",
-    )(core_ref, rhs_ref, keep_rest, got, got_edge, t["right_z"])
+    )(core_ref, rhs_ref, keep_rest, got, got_edge, packed)
     return wavefield, residual
 
 

time: 67.4 us -> 71.7 us (1.064)
  the two profiles are of different devices: /device:TPU:29 before, /device:TPU:23 now
where the time goes in v9:
time: 71.7 us; the launch traced here: 70.9 us
  waiting for transfers between devices  29 us (40%)
  starting transfers between devices  19.3 us (27%)
  Pallas kernels  10.1 us (14%)
  local copies, waits for them, and re-layouts  10 us (14%)
  between operations  1.5 us (2%)
  other arithmetic  1.04 us (1%)
    ppermute x6, waiting for transfers between devices, body(): trace_y0 = hand_on(lax.ppermute(outs0[0], axes, along_y))  21.9 us
    unnamed x26, local copies, waits for them, and re-layouts  8.88 us
    ppermute x1, waiting for transfers between devices, body(): lax.ppermute(edge_x, axes, between([((k, j), (k - 1, j)) for k, j in ever...  5.67 us
    pallas_call x14, Pallas kernels, solve(): pl.pallas_call(functools.partial(beat_kernel, tile, final, table_places),...  5.49 us
    ppermute x6, starting transfers between devices, body(): trace_x = lax.ppermute(outs1[0], axes, along_x)  5.24 us
    ppermute x6, starting transfers between devices, body(): trace_y0 = hand_on(lax.ppermute(outs0[0], axes, along_y))  4.61 us
    ppermute x6, starting transfers between devices, body(): trace_y1 = lax.ppermute(outs1[1], axes, along_y)  4.61 us
    ppermute x1, starting transfers between devices, body(): lax.ppermute(edge_x, axes, between([((k, j), (k - 1, j)) for k, j in ever...  1.92 us
  transfers between devices with their start and end apart: 23, of which 6 were waited for; matrix products, arithmetic and copies ran while one was open for 0% of the time, Pallas kernels for 11%

profile of v9, /device:TPU:23, one launch (start us, length us, event | category | flops | bytes accessed | tf_op | source)
XLA Modules:
  0.0 70.9 jit_solution(1289885783513478662)
XLA Ops:
  0.7 1.0 %dynamic-slice_bitcast_fusion = f32[2,16,16,128]{3,2,1,0:T(8,128)S(1)} fusion(f32[2,2,16,16,128]{4,3,2,1,0:T(8,128)} %right_ref.1, s32[]{:T(128)S(6)} %select_n.71), kind=kLoop, calls=%fused_computation.1 | loop fusion | bytes 524292 | tf_op jit(solution)/shard_map/jit(dynamic_index_in_dim)/squeeze | solution.py:390
  1.8 1.0 %pad_maximum_fusion = f32[3,16,16,128]{3,2,1,0:T(8,128)S(1)} fusion(f32[1,16,16,128]{3,2,1,0:T(8,128)} %bitcast.23, f32[2,16,16,128]{3,2,1,0:T(8,128)S(1)} %dynamic-slice_bitcast_fusion), kind=kLoop, calls=%fused_computation | loop fusion | flops 98304 | bytes 786432 | tf_op jit(solution)/shard_map/concatenate | solution.py:391
  2.8 0.7 %collective-permute-start = (f32[3,16,16,128]{3,2,1,0:T(8,128)S(1)}, f32[3,16,16,128]{3,2,1,0:T(8,128)S(1)}, u32[]{:S(2)}, u32[]{:S(2)}) collective-permute-start(f32[3,16,16,128]{3,2,1,0:T(8,128)S(1)} %pad_maximum_fusion), channel_id=1, source_target_pairs={{0,4},{4,0},{1,5},{5,1},{2,6},{6,2},{3,7},{7,3},{8,12},{12,8},{9,1... | collective-permute-start | bytes 1179656 | tf_op jit(solution)/shard_map/ppermute | solution.py:391
  3.5 0.7 copy-done.12
  4.3 1.0 %copy-done.3 = f32[2,2,16,16,128]{4,3,2,1,0:T(8,128)S(1)} copy-done((f32[2,2,16,16,128]{4,3,2,1,0:T(8,128)S(1)}, f32[2,2,16,16,128]{4,3,2,1,0:T(8,128)}, u32[]{:S(2)}) %copy-start.3) | copy-done | bytes 524312
  5.3 0.9 %copy-done.4 = f32[16,16,128]{2,1,0:T(8,128)S(1)} copy-done((f32[16,16,128]{2,1,0:T(8,128)S(1)}, f32[16,16,128]{2,1,0:T(8,128)}, u32[]{:S(2)}) %copy-start.4) | copy-done | bytes 131096
  6.2 0.8 %prep.1 = (f32[256,256]{1,0:T(8,128)S(1)}, f32[2,256,128]{2,1,0:T(8,128)S(1)}) custom-call(s32[1]{0:T(128)} %bitcast.rhs_ref, f32[2,2,16,16,128]{4,3,2,1,0:T(8,128)S(1)} %copy-done.3, f32[16,16,128]{2,1,0:T(8,128)S(1)} %copy-done.4, s32[1,16]{1,0:T(1,128)S(1)} %and_select_fusion.2.place_ref, s32[1,16]{1,0:T(1,128)S(1)} %and_select_fusion.1.depth_ref, ...), custom_call_target="tpu_custom_call" | custom-call | flops 2000000000 | bytes 2000000 | tf_op jit(solution)/shard_map/prep/pallas_call | solution.py:406
  7.0 0.8 %prep_other.1 = (f32[2,256,256]{2,1,0:T(8,128)S(1)}, f32[2,2,256,128]{3,2,1,0:T(8,128)S(1)}) custom-call(s32[1]{0:T(128)} %bitcast.1.core_ref, f32[3,16,16,128]{3,2,1,0:T(8,128)S(1)} %collective-permute-done.swap_ref, f32[256,256]{1,0:T(8,128)S(1)} %get-tuple-element.64.own_modes_ref, f32[2,256,128]{2,1,0:T(8,128)S(1)} %get-tuple-element.65.own_contrast_ref, ...), custom_call_target="tpu_custom_call" | custom-call | flops 2000000000 | bytes 2000000 | tf_op jit(solution)/shard_map/prep_other/pallas_call | solution.py:415
  7.9 0.7 collective-permute-start.2
  8.7 0.7 collective-permute-start.1
  9.4 0.7 collective-permute-start.3
  10.1 1.0 %copy-done.6 = f32[2,256,256]{2,1,0:T(8,128)S(1)} copy-done((f32[2,256,256]{2,1,0:T(8,128)S(1)}, f32[2,256,256]{2,1,0:T(8,128)}, u32[]{:S(2)}) %copy-start.6) | copy-done | bytes 524312
  11.2 0.7 collective-permute-start.5
  12.0 0.7 collective-permute-start.4
  12.7 0.7 collective-permute-start.6
  13.4 1.0 %copy-done.7 = f32[2,256,256]{2,1,0:T(8,128)S(1)} copy-done((f32[2,256,256]{2,1,0:T(8,128)S(1)}, f32[2,256,256]{2,1,0:T(8,128)}, u32[]{:S(2)}) %copy-start.7) | copy-done | bytes 524312
  14.5 0.7 collective-permute-start.8
  15.2 0.7 collective-permute-start.7
  15.9 0.7 collective-permute-start.9
  16.6 1.0 %copy-done.8 = f32[2,256,256]{2,1,0:T(8,128)S(1)} copy-done((f32[2,256,256]{2,1,0:T(8,128)S(1)}, f32[2,256,256]{2,1,0:T(8,128)}, u32[]{:S(2)}) %copy-start.8) | copy-done | bytes 524312
  17.7 0.7 collective-permute-start.11
  18.4 0.3 lower.10
  18.7 0.7 collective-permute-start.10
  19.4 0.7 collective-permute-start.12
  20.1 1.0 %copy-done.9 = f32[2,256,256]{2,1,0:T(8,128)S(1)} copy-done((f32[2,256,256]{2,1,0:T(8,128)S(1)}, f32[2,256,256]{2,1,0:T(8,128)}, u32[]{:S(2)}) %copy-start.9) | copy-done | bytes 524312
  21.2 1.3 %collective-permute-start.14 = (f32[32,256]{1,0:T(8,128)S(1)}, f32[32,256]{1,0:T(8,128)S(1)}, u32[]{:S(2)}, u32[]{:S(2)}) collective-permute-start(f32[32,256]{1,0:T(8,128)S(1)} %get-tuple-element.102), channel_id=1, source_target_pairs={{18,23},{22,19},{25,30},{29,26}} | collective-permute-start | bytes 98312 | tf_op jit(solution)/shard_map/ppermute | solution.py:462
  22.6 1.3 %collective-permute-start.13 = (f32[32,256]{1,0:T(8,128)S(1)}, f32[32,256]{1,0:T(8,128)S(1)}, u32[]{:S(2)}, u32[]{:S(2)}) collective-permute-start(f32[32,256]{1,0:T(8,128)S(1)} %get-tuple-element.101), channel_id=1, source_target_pairs={{11,23},{15,19},{18,30},{22,26}} | collective-permute-start | bytes 98312 | tf_op jit(solution)/shard_map/ppermute | solution.py:465
  23.9 1.3 %collective-permute-start.15 = (f32[32,256]{1,0:T(8,128)S(1)}, f32[32,256]{1,0:T(8,128)S(1)}, u32[]{:S(2)}, u32[]{:S(2)}) collective-permute-start(f32[32,256]{1,0:T(8,128)S(1)} %get-tuple-element.106), channel_id=1, source_target_pairs={{18,23},{22,19},{25,30},{29,26}} | collective-permute-start | bytes 98312 | tf_op jit(solution)/shard_map/ppermute | solution.py:467
  25.2 21.9 %collective-permute-done.14.in_ref = f32[32,256]{1,0:T(8,128)S(1)} collective-permute-done((f32[32,256]{1,0:T(8,128)S(1)}, f32[32,256]{1,0:T(8,128)S(1)}, u32[]{:S(2)}, u32[]{:S(2)}) %collective-permute-start.14) | collective-permute-done | bytes 32800 | tf_op jit(solution)/shard_map/ppermute | solution.py:462
  47.1 0.3 collective-permute-done.13.trace_x_ref
  47.4 1.0 %copy-done.10 = f32[2,256,256]{2,1,0:T(8,128)S(1)} copy-done((f32[2,256,256]{2,1,0:T(8,128)S(1)}, f32[2,256,256]{2,1,0:T(8,128)}, u32[]{:S(2)}) %copy-start.10) | copy-done | bytes 524312
  48.4 2.1 %upper.12 = (f32[256,256]{1,0:T(8,128)S(1)}, f32[256,256]{1,0:T(8,128)S(1)}, f32[32,256]{1,0:T(8,128)S(1)}, f32[32,256]{1,0:T(8,128)S(1)}) custom-call(s32[1]{0:T(128)} %bitcast.9.active_ref, f32[2,256,256]{2,1,0:T(8,128)S(1)} %copy-done.10, f32[2,2,256,128]{3,2,1,0:T(8,128)S(1)} %get-tuple-element.67.contrast_ref, ...), custom_call_target="tpu_custom_call", output_to_operand_aliasing={{0}: (5, {}), {1}: (6, {})} | custom-call | flops 2000000000 | bytes 2000000 | tf_op jit(solution)/shard_map/upper/pallas_call | solution.py:428
  50.5 0.7 collective-permute-start.17
  51.1 0.7 collective-permute-done.15.trace_y_ref
  51.8 2.1 %lower.12 = (f32[256,256]{1,0:T(8,128)S(1)}, f32[256,256]{1,0:T(8,128)S(1)}, f32[32,256]{1,0:T(8,128)S(1)}, f32[32,256]{1,0:T(8,128)S(1)}) custom-call(s32[1]{0:T(128)} %bitcast.9.active_ref, f32[2,256,256]{2,1,0:T(8,128)S(1)} %copy-done.10, f32[2,2,256,128]{3,2,1,0:T(8,128)S(1)} %get-tuple-element.67.contrast_ref, ...), custom_call_target="tpu_custom_call", output_to_operand_aliasing={{0}: (5, {}), {1}: (6, {})} | custom-call | flops 2000000000 | bytes 2000000 | tf_op jit(solution)/shard_map/lower/pallas_call | solution.py:428
  53.9 1.3 %collective-permute-start.16 = (f32[32,256]{1,0:T(8,128)S(1)}, f32[32,256]{1,0:T(8,128)S(1)}, u32[]{:S(2)}, u32[]{:S(2)}) collective-permute-start(f32[32,256]{1,0:T(8,128)S(1)} %get-tuple-element.109), channel_id=1, source_target_pairs={{19,31},{23,27}} | collective-permute-start | bytes 98312 | tf_op jit(solution)/shard_map/ppermute | solution.py:465
  55.2 0.7 collective-permute-start.18
  55.9 0.3 collective-permute-done.16.trace_x_ref
  56.2 1.0 %copy-done.11 = f32[2,256,256]{2,1,0:T(8,128)S(1)} copy-done((f32[2,256,256]{2,1,0:T(8,128)S(1)}, f32[2,256,256]{2,1,0:T(8,128)}, u32[]{:S(2)}) %copy-start.11) | copy-done | bytes 524312
  57.2 0.3 upper.13
  57.5 0.3 lower.13
  57.8 1.3 %collective-permute-start.21 = (f32[2,32,256]{2,1,0:T(8,128)S(1)}, f32[2,32,256]{2,1,0:T(8,128)S(1)}, u32[]{:S(2)}, u32[]{:S(2)}) collective-permute-start(f32[2,32,256]{2,1,0:T(8,128)S(1)} %pad_maximum_fusion.1), channel_id=1, source_target_pairs={{1,4},{5,0},{2,5},{6,1},{3,6},{7,2},{9,12},{13,8},{10,13},{14,9},{... | collective-permute-start | bytes 196616 | tf_op jit(solution)/shard_map/ppermute | solution.py:473
  59.1 1.9 %collective-permute-start.20 = (f32[32,256]{1,0:T(8,128)S(1)}, f32[32,256]{1,0:T(8,128)S(1)}, u32[]{:S(2)}, u32[]{:S(2)}) collective-permute-start(f32[32,256]{1,0:T(8,128)S(1)} %get-tuple-element.123), channel_id=1, source_target_pairs={{8,4},{12,0},{9,5},{13,1},{10,6},{14,2},{11,7},{15,3},{16,12},{20,... | collective-permute-start | bytes 98312 | tf_op jit(solution)/shard_map/ppermute | solution.py:472
  61.0 1.1 %finish.1 = (f32[2,2,16,16,128]{4,3,2,1,0:T(8,128)S(1)}, f32[2,2,16,16,128]{4,3,2,1,0:T(8,128)S(1)}) custom-call(s32[1]{0:T(128)} %bitcast.1.core_ref, f32[256,256]{1,0:T(8,128)S(1)} %get-tuple-element.113.total0_ref, f32[256,256]{1,0:T(8,128)S(1)} %get-tuple-element.114.term0_ref, f32[256,256]{1,0:T(8,128)S(1)} %get-tuple-element.119.total1_ref, ...), custom_call_target="tpu_custom_call" | custom-call | tf_op jit(solution)/shard_map/finish/pallas_call | solution.py:476
  62.2 0.8 %collective-permute-start.19 = (f32[2,2,16,16,128]{4,3,2,1,0:T(8,128)S(1)}, f32[2,2,16,16,128]{4,3,2,1,0:T(8,128)S(1)}, u32[]{:S(2)}, u32[]{:S(2)}) collective-permute-start(f32[2,2,16,16,128]{4,3,2,1,0:T(8,128)S(1)} %get-tuple-element.122), channel_id=1, source_target_pairs={{0,4},{4,0},{1,5},{5,1},{2,6},{6,2},{3,7},{7,3},{8,12},{12,8},{9,1... | collective-permute-start | bytes 1572872 | tf_op jit(solution)/shard_map/ppermute | solution.py:485
  62.9 5.7 %collective-permute-done.20.edge_x_ref = f32[32,256]{1,0:T(8,128)S(1)} collective-permute-done((f32[32,256]{1,0:T(8,128)S(1)}, f32[32,256]{1,0:T(8,128)S(1)}, u32[]{:S(2)}, u32[]{:S(2)}) %collective-permute-start.20) | collective-permute-done | bytes 32800 | tf_op jit(solution)/shard_map/ppermute | solution.py:472
  68.9 0.8 %place_wave.1 = f32[2,2,16,16,128]{4,3,2,1,0:T(8,128)} custom-call(s32[1]{0:T(128)} %bitcast.rhs_ref, f32[2,2,16,16,128]{4,3,2,1,0:T(8,128)S(1)} %get-tuple-element.121.keep_ref, f32[2,2,16,16,128]{4,3,2,1,0:T(8,128)S(1)} %collective-permute-done.19.got_ref), custom_call_target="tpu_custom_call" | custom-call | flops 10000000000 | bytes 1000000 | tf_op jit(solution)/shard_map/place_wave/pallas_call | solution.py:498
  69.8 0.9 %place_rest.1 = f32[2,2,16,16,128]{4,3,2,1,0:T(8,128)} custom-call(s32[1]{0:T(128)} %bitcast.1.core_ref, s32[1]{0:T(128)} %bitcast.rhs_ref, f32[2,16,16,128]{3,2,1,0:T(8,128)S(1)} %keep.1.keep_rest_ref, f32[2,2,16,16,128]{4,3,2,1,0:T(8,128)S(1)} %collective-permute-done.19.got_ref, f32[64,256]{1,0:T(8,128)S(1)} %collective-permute-done.22.got_edge_ref, ...), custom_call_target="tpu_custom_call" | custom-call | tf_op jit(solution)/shard_map/place_rest/pallas_call | solution.py:508
  (64 shorter events, 1.3 us)
Async XLA Ops:
  0.6 2.9 %copy-start = (f32[2,16,2]{1,2,0:T(2,128)S(1)}, f32[2,16,2]{1,2,0:T(2,128)}, u32[]{:S(2)}) copy-start(f32[2,16,2]{1,2,0:T(2,128)} %param.9) | copy-start | bytes 772
  0.6 3.6 %copy-start.1 = (bf16[640,768]{1,0:T(8,128)(2,1)S(1)}, bf16[640,768]{1,0:T(8,128)(2,1)}, u32[]{:S(2)}) copy-start(bf16[640,768]{1,0:T(8,128)(2,1)} %constant.145.clone.packed_ref) | copy-start | bytes 2949124
  1.8 2.5 %copy-start.2 = (f32[3,256,128]{2,1,0:T(8,128)S(1)}, f32[3,256,128]{2,1,0:T(8,128)}, u32[]{:S(2)}) copy-start(f32[3,256,128]{2,1,0:T(8,128)} %constant.144.clone.fields_ref) | copy-start | bytes 1179652
  2.8 4.2 %collective-permute-start = (f32[3,16,16,128]{3,2,1,0:T(8,128)S(1)}, f32[3,16,16,128]{3,2,1,0:T(8,128)S(1)}, u32[]{:S(2)}, u32[]{:S(2)}) collective-permute-start(f32[3,16,16,128]{3,2,1,0:T(8,128)S(1)} %pad_maximum_fusion), channel_id=1, source_target_pairs={{0,4},{4,0},{1,5},{5,1},{2,6},{6,2},{3,7},{7,3},{8,12},{12,8},{9,1... | collective-permute-start | bytes 1179656 | tf_op jit(solution)/shard_map/ppermute | solution.py:391
  3.5 0.7 copy-start.12
  4.3 1.0 %copy-start.3 = (f32[2,2,16,16,128]{4,3,2,1,0:T(8,128)S(1)}, f32[2,2,16,16,128]{4,3,2,1,0:T(8,128)}, u32[]{:S(2)}) copy-start(f32[2,2,16,16,128]{4,3,2,1,0:T(8,128)} %right_ref.1) | copy-start | bytes 1572868
  5.3 0.9 %copy-start.4 = (f32[16,16,128]{2,1,0:T(8,128)S(1)}, f32[16,16,128]{2,1,0:T(8,128)}, u32[]{:S(2)}) copy-start(f32[16,16,128]{2,1,0:T(8,128)} %slow_ref.1) | copy-start | bytes 393220
  7.8 0.9 %copy-start.5 = (f32[2,256,256]{2,1,0:T(8,128)}, f32[2,256,256]{2,1,0:T(8,128)S(1)}, u32[]{:S(2)}) copy-start(f32[2,256,256]{2,1,0:T(8,128)S(1)} %get-tuple-element.66.modes_ref) | copy-start | bytes 1572868
  7.9 2.2 %collective-permute-start.2 = (f32[32,256]{1,0:T(8,128)S(1)}, f32[32,256]{1,0:T(8,128)S(1)}, u32[]{:S(2)}, u32[]{:S(2)}) collective-permute-start(f32[32,256]{1,0:T(8,128)S(1)} %get-tuple-element.70), channel_id=1, source_target_pairs={{0,5},{4,1}} | collective-permute-start | bytes 98312 | tf_op jit(solution)/shard_map/ppermute | solution.py:462
  8.7 1.4 %collective-permute-start.1 = (f32[32,256]{1,0:T(8,128)S(1)}, f32[32,256]{1,0:T(8,128)S(1)}, u32[]{:S(2)}, u32[]{:S(2)}) collective-permute-start(f32[32,256]{1,0:T(8,128)S(1)} %get-tuple-element.69), channel_id=1, source_target_pairs={{0,12},{4,8}} | collective-permute-start | bytes 98312 | tf_op jit(solution)/shard_map/ppermute | solution.py:465
  9.4 2.5 %collective-permute-start.3 = (f32[32,256]{1,0:T(8,128)S(1)}, f32[32,256]{1,0:T(8,128)S(1)}, u32[]{:S(2)}, u32[]{:S(2)}) collective-permute-start(f32[32,256]{1,0:T(8,128)S(1)} %get-tuple-element.74), channel_id=1, source_target_pairs={{0,5},{4,1}} | collective-permute-start | bytes 98312 | tf_op jit(solution)/shard_map/ppermute | solution.py:467
  10.1 1.0 %copy-start.6 = (f32[2,256,256]{2,1,0:T(8,128)S(1)}, f32[2,256,256]{2,1,0:T(8,128)}, u32[]{:S(2)}) copy-start(f32[2,256,256]{2,1,0:T(8,128)} %copy-done.5) | copy-start | bytes 1572868
  11.2 2.1 %collective-permute-start.5 = (f32[32,256]{1,0:T(8,128)S(1)}, f32[32,256]{1,0:T(8,128)S(1)}, u32[]{:S(2)}, u32[]{:S(2)}) collective-permute-start(f32[32,256]{1,0:T(8,128)S(1)} %get-tuple-element.78), channel_id=1, source_target_pairs={{1,6},{5,2},{8,13},{12,9}} | collective-permute-start | bytes 98312 | tf_op jit(solution)/shard_map/ppermute | solution.py:462
  12.0 1.4 %collective-permute-start.4 = (f32[32,256]{1,0:T(8,128)S(1)}, f32[32,256]{1,0:T(8,128)S(1)}, u32[]{:S(2)}, u32[]{:S(2)}) collective-permute-start(f32[32,256]{1,0:T(8,128)S(1)} %get-tuple-element.77), channel_id=1, source_target_pairs={{1,13},{5,9},{8,20},{12,16}} | collective-permute-start | bytes 98312 | tf_op jit(solution)/shard_map/ppermute | solution.py:465
  12.7 2.5 %collective-permute-start.6 = (f32[32,256]{1,0:T(8,128)S(1)}, f32[32,256]{1,0:T(8,128)S(1)}, u32[]{:S(2)}, u32[]{:S(2)}) collective-permute-start(f32[32,256]{1,0:T(8,128)S(1)} %get-tuple-element.82), channel_id=1, source_target_pairs={{1,6},{5,2},{8,13},{12,9}} | collective-permute-start | bytes 98312 | tf_op jit(solution)/shard_map/ppermute | solution.py:467
  13.4 1.0 %copy-start.7 = (f32[2,256,256]{2,1,0:T(8,128)S(1)}, f32[2,256,256]{2,1,0:T(8,128)}, u32[]{:S(2)}) copy-start(f32[2,256,256]{2,1,0:T(8,128)} %copy-done.5) | copy-start | bytes 1572868
  14.5 2.1 %collective-permute-start.8 = (f32[32,256]{1,0:T(8,128)S(1)}, f32[32,256]{1,0:T(8,128)S(1)}, u32[]{:S(2)}, u32[]{:S(2)}) collective-permute-start(f32[32,256]{1,0:T(8,128)S(1)} %get-tuple-element.86), channel_id=1, source_target_pairs={{2,7},{6,3},{9,14},{13,10},{16,21},{20,17}} | collective-permute-start | bytes 98312 | tf_op jit(solution)/shard_map/ppermute | solution.py:462
  15.2 1.4 %collective-permute-start.7 = (f32[32,256]{1,0:T(8,128)S(1)}, f32[32,256]{1,0:T(8,128)S(1)}, u32[]{:S(2)}, u32[]{:S(2)}) collective-permute-start(f32[32,256]{1,0:T(8,128)S(1)} %get-tuple-element.85), channel_id=1, source_target_pairs={{2,14},{6,10},{9,21},{13,17},{16,28},{20,24}} | collective-permute-start | bytes 98312 | tf_op jit(solution)/shard_map/ppermute | solution.py:465
  15.9 2.5 %collective-permute-start.9 = (f32[32,256]{1,0:T(8,128)S(1)}, f32[32,256]{1,0:T(8,128)S(1)}, u32[]{:S(2)}, u32[]{:S(2)}) collective-permute-start(f32[32,256]{1,0:T(8,128)S(1)} %get-tuple-element.90), channel_id=1, source_target_pairs={{2,7},{6,3},{9,14},{13,10},{16,21},{20,17}} | collective-permute-start | bytes 98312 | tf_op jit(solution)/shard_map/ppermute | solution.py:467
  16.6 1.0 %copy-start.8 = (f32[2,256,256]{2,1,0:T(8,128)S(1)}, f32[2,256,256]{2,1,0:T(8,128)}, u32[]{:S(2)}) copy-start(f32[2,256,256]{2,1,0:T(8,128)} %copy-done.5) | copy-start | bytes 1572868
  17.7 2.3 %collective-permute-start.11 = (f32[32,256]{1,0:T(8,128)S(1)}, f32[32,256]{1,0:T(8,128)S(1)}, u32[]{:S(2)}, u32[]{:S(2)}) collective-permute-start(f32[32,256]{1,0:T(8,128)S(1)} %get-tuple-element.94), channel_id=1, source_target_pairs={{10,15},{14,11},{17,22},{21,18},{24,29},{28,25}} | collective-permute-start | bytes 98312 | tf_op jit(solution)/shard_map/ppermute | solution.py:462
  18.7 1.4 %collective-permute-start.10 = (f32[32,256]{1,0:T(8,128)S(1)}, f32[32,256]{1,0:T(8,128)S(1)}, u32[]{:S(2)}, u32[]{:S(2)}) collective-permute-start(f32[32,256]{1,0:T(8,128)S(1)} %get-tuple-element.93), channel_id=1, source_target_pairs={{3,15},{7,11},{10,22},{14,18},{17,29},{21,25}} | collective-permute-start | bytes 98312 | tf_op jit(solution)/shard_map/ppermute | solution.py:465
  19.4 3.1 %collective-permute-start.12 = (f32[32,256]{1,0:T(8,128)S(1)}, f32[32,256]{1,0:T(8,128)S(1)}, u32[]{:S(2)}, u32[]{:S(2)}) collective-permute-start(f32[32,256]{1,0:T(8,128)S(1)} %get-tuple-element.98), channel_id=1, source_target_pairs={{10,15},{14,11},{17,22},{21,18},{24,29},{28,25}} | collective-permute-start | bytes 98312 | tf_op jit(solution)/shard_map/ppermute | solution.py:467
  20.1 1.0 %copy-start.9 = (f32[2,256,256]{2,1,0:T(8,128)S(1)}, f32[2,256,256]{2,1,0:T(8,128)}, u32[]{:S(2)}) copy-start(f32[2,256,256]{2,1,0:T(8,128)} %copy-done.5) | copy-start | bytes 1572868
  21.2 25.9 %collective-permute-start.14 = (f32[32,256]{1,0:T(8,128)S(1)}, f32[32,256]{1,0:T(8,128)S(1)}, u32[]{:S(2)}, u32[]{:S(2)}) collective-permute-start(f32[32,256]{1,0:T(8,128)S(1)} %get-tuple-element.102), channel_id=1, source_target_pairs={{18,23},{22,19},{25,30},{29,26}} | collective-permute-start | bytes 98312 | tf_op jit(solution)/shard_map/ppermute | solution.py:462
  22.6 24.8 %collective-permute-start.13 = (f32[32,256]{1,0:T(8,128)S(1)}, f32[32,256]{1,0:T(8,128)S(1)}, u32[]{:S(2)}, u32[]{:S(2)}) collective-permute-start(f32[32,256]{1,0:T(8,128)S(1)} %get-tuple-element.101), channel_id=1, source_target_pairs={{11,23},{15,19},{18,30},{22,26}} | collective-permute-start | bytes 98312 | tf_op jit(solution)/shard_map/ppermute | solution.py:465
  23.9 27.9 %collective-permute-start.15 = (f32[32,256]{1,0:T(8,128)S(1)}, f32[32,256]{1,0:T(8,128)S(1)}, u32[]{:S(2)}, u32[]{:S(2)}) collective-permute-start(f32[32,256]{1,0:T(8,128)S(1)} %get-tuple-element.106), channel_id=1, source_target_pairs={{18,23},{22,19},{25,30},{29,26}} | collective-permute-start | bytes 98312 | tf_op jit(solution)/shard_map/ppermute | solution.py:467
  47.4 1.0 %copy-start.10 = (f32[2,256,256]{2,1,0:T(8,128)S(1)}, f32[2,256,256]{2,1,0:T(8,128)}, u32[]{:S(2)}) copy-start(f32[2,256,256]{2,1,0:T(8,128)} %copy-done.5) | copy-start | bytes 1572868
  50.5 5.4 %collective-permute-start.17 = (f32[32,256]{1,0:T(8,128)S(1)}, f32[32,256]{1,0:T(8,128)S(1)}, u32[]{:S(2)}, u32[]{:S(2)}) collective-permute-start(f32[32,256]{1,0:T(8,128)S(1)} %get-tuple-element.110), channel_id=1, source_target_pairs={{26,31},{30,27}} | collective-permute-start | bytes 98312 | tf_op jit(solution)/shard_map/ppermute | solution.py:462
  53.9 2.3 %collective-permute-start.16 = (f32[32,256]{1,0:T(8,128)S(1)}, f32[32,256]{1,0:T(8,128)S(1)}, u32[]{:S(2)}, u32[]{:S(2)}) collective-permute-start(f32[32,256]{1,0:T(8,128)S(1)} %get-tuple-element.109), channel_id=1, source_target_pairs={{19,31},{23,27}} | collective-permute-start | bytes 98312 | tf_op jit(solution)/shard_map/ppermute | solution.py:465
  55.2 2.3 %collective-permute-start.18 = (f32[32,256]{1,0:T(8,128)S(1)}, f32[32,256]{1,0:T(8,128)S(1)}, u32[]{:S(2)}, u32[]{:S(2)}) collective-permute-start(f32[32,256]{1,0:T(8,128)S(1)} %get-tuple-element.116), channel_id=1, source_target_pairs={{26,31},{30,27}} | collective-permute-start | bytes 98312 | tf_op jit(solution)/shard_map/ppermute | solution.py:467
  56.2 1.0 %copy-start.11 = (f32[2,256,256]{2,1,0:T(8,128)S(1)}, f32[2,256,256]{2,1,0:T(8,128)}, u32[]{:S(2)}) copy-start(f32[2,256,256]{2,1,0:T(8,128)} %copy-done.5) | copy-start | bytes 1572868
  57.8 5.1 %collective-permute-start.21 = (f32[2,32,256]{2,1,0:T(8,128)S(1)}, f32[2,32,256]{2,1,0:T(8,128)S(1)}, u32[]{:S(2)}, u32[]{:S(2)}) collective-permute-start(f32[2,32,256]{2,1,0:T(8,128)S(1)} %pad_maximum_fusion.1), channel_id=1, source_target_pairs={{1,4},{5,0},{2,5},{6,1},{3,6},{7,2},{9,12},{13,8},{10,13},{14,9},{... | collective-permute-start | bytes 196616 | tf_op jit(solution)/shard_map/ppermute | solution.py:473
  59.1 9.5 %collective-permute-start.20 = (f32[32,256]{1,0:T(8,128)S(1)}, f32[32,256]{1,0:T(8,128)S(1)}, u32[]{:S(2)}, u32[]{:S(2)}) collective-permute-start(f32[32,256]{1,0:T(8,128)S(1)} %get-tuple-element.123), channel_id=1, source_target_pairs={{8,4},{12,0},{9,5},{13,1},{10,6},{14,2},{11,7},{15,3},{16,12},{20,... | collective-permute-start | bytes 98312 | tf_op jit(solution)/shard_map/ppermute | solution.py:472
  62.2 6.8 %collective-permute-start.19 = (f32[2,2,16,16,128]{4,3,2,1,0:T(8,128)S(1)}, f32[2,2,16,16,128]{4,3,2,1,0:T(8,128)S(1)}, u32[]{:S(2)}, u32[]{:S(2)}) collective-permute-start(f32[2,2,16,16,128]{4,3,2,1,0:T(8,128)S(1)} %get-tuple-element.122), channel_id=1, source_target_pairs={{0,4},{4,0},{1,5},{5,1},{2,6},{6,2},{3,7},{7,3},{8,12},{12,8},{9,1... | collective-permute-start | bytes 1572872 | tf_op jit(solution)/shard_map/ppermute | solution.py:485
  68.6 1.3 %collective-permute-start.22 = (f32[64,256]{1,0:T(8,128)S(1)}, f32[64,256]{1,0:T(8,128)S(1)}, u32[]{:S(2)}, u32[]{:S(2)}) collective-permute-start(f32[64,256]{1,0:T(8,128)S(1)} %pad_maximum_fusion.2), channel_id=1, source_target_pairs={{0,4},{4,0},{1,5},{5,1},{2,6},{6,2},{3,7},{7,3},{8,12},{12,8},{9,1... | collective-permute-start | bytes 196616 | tf_op jit(solution)/shard_map/ppermute | solution.py:488

commit v10 on v9

--- a/solution.py
+++ b/solution.py
@@ -91,38 +91,15 @@
     edge[-1] += 1.0 / 12.0
     edge[:, 0] += 1.0 / 12.0
     edge[:, -1] += 1.0 / 12.0
-    edge = edge[cells].reshape(1, size_x * size_y, 1) + np.zeros((1, 1, cells_z))
-    fields = np.concatenate([inverse, edge.astype(np.float32)], axis=0)
-
-    matrices = dict(
-        forward0=forward[0], forward1=forward[1], backward0=backward[0], backward1=backward[1],
+    edge = edge[cells].reshape(size_x * size_y, 1).astype(np.float32)
+    return dict(
+        inverse=inverse, edge=edge, forward=np.stack(forward), backward=np.stack(backward),
         right_z=right_z, enter=enter, leave=leave, first=first,
-    )
-    width = 128 * max(-(-m.shape[1] // 128) for m in matrices.values())
-    places, rows, at = {}, 0, 0
-    height = 0
-    for name, m in sorted(matrices.items(), key=lambda item: -item[1].shape[0]):
-        if at + m.shape[1] > width:
-            rows, at, height = rows + height, 0, 0
-        places[name] = (rows, at, *m.shape)
-        height = max(height, -(-m.shape[0] // 16) * 16)
-        at += -(-m.shape[1] // 128) * 128
-    packed = np.zeros((rows + height, width), ml_dtypes.bfloat16)
-    for name, (row, lane, count, lanes) in places.items():
-        packed[row : row + count, lane : lane + lanes] = matrices[name]
-    return fields, packed, places, tuple(int(x) for x in cells)
-
-
-class Tables:
-    def __init__(self, places, fields_ref, packed_ref):
-        self.places, self.fields, self.packed = places, fields_ref, packed_ref
-
-    def __getitem__(self, name):
-        row, lane, count, lanes = self.places[name]
-        return self.packed[row : row + count, lane : lane + lanes]
-
-    def divide(self, modes):
-        return times(self.fields[0], self.fields[1], modes)
+    ), tuple(int(x) for x in cells)
+
+
+def divide(modes, t):
+    return times(t["inverse"][0], t["inverse"][1], modes)
 
 
 def split(values):
@@ -143,7 +120,7 @@
     rows = field.shape[0]
     cells_z = field.shape[1] // 2
     high, low = split(jnp.concatenate([field[:, :cells_z], field[:, cells_z:]], axis=0))
-    both = jnp.dot(jnp.concatenate([high, low], axis=1), t["right_z"], preferred_element_type=F32)
+    both = jnp.dot(jnp.concatenate([high, low], axis=1), t["right_z"][...], preferred_element_type=F32)
     total = both[:, :cells_z] + both[:, cells_z:]
     return jnp.concatenate([total[:rows], total[rows:]], axis=1)
 
@@ -152,14 +129,14 @@
     count = field.shape[0] // 2
     first, second = field[:count], field[count:]
     return jnp.concatenate(
-        [left_product(t["forward0"], first + second), left_product(t["forward1"], first - second)], axis=0
+        [left_product(t["forward"][0], first + second), left_product(t["forward"][1], first - second)], axis=0
     )
 
 
 def to_cells(modes, t):
     count = modes.shape[0] // 2
-    even = left_product(t["backward0"], modes[:count])
-    odd = left_product(t["backward1"], modes[count:])
+    even = left_product(t["backward"][0], modes[:count])
+    odd = left_product(t["backward"][1], modes[count:])
     return jnp.concatenate([even + odd, even - odd], axis=0)
 
 
@@ -183,7 +160,7 @@
 def solve_modes(start, contrast, t):
     term = total = start
     for _ in range(2):
-        term = t.divide(to_modes(apply_contrast(to_cells(term, t), contrast, t), t))
+        term = divide(to_modes(apply_contrast(to_cells(term, t), contrast, t), t), t)
         total = total + term
     return total, term
 
@@ -202,57 +179,71 @@
         parts = [at_lane * part for part in (one, two, amp - one - two)]
         spread.append(jnp.concatenate(parts, axis=1).astype(BF16))
     scaled = KAPPA * (slow - 1.0)
-    contrast_ref[0] = scaled - t.fields[2]
+    contrast_ref[0] = scaled - t["edge"][...]
     contrast_ref[1] = DAMPING * scaled
     at_row = (row_ids == place).astype(F32).astype(BF16)
     field = lax.dot_general(
         jnp.concatenate([at_row] * 3, axis=1), jnp.concatenate(spread, axis=0),
         (((1,), (1,)), ((), ())), preferred_element_type=F32,
     )
-    modes_ref[...] = t.divide(to_modes(z_transform(field + dense, t), t))
+    modes_ref[...] = divide(to_modes(z_transform(field + dense, t), t), t)
 
 
 def hand_on_kernel(in_ref, out_ref):
     out_ref[...] = in_ref[...]
 
 
-def prep_kernel(cells_x, places, rhs_ref, right_ref, slow_ref, place_ref, depth_ref, amp_ref, fields_ref,
-                packed_ref, modes_ref, contrast_ref):
-    dense = [jnp.concatenate([right_ref[rhs_ref[0], c, x] for x in cells_x], axis=0) for c in range(2)]
+PREP = ("inverse", "edge", "forward", "right_z", "backward", "enter", "leave")
+BEAT = ("inverse", "forward", "right_z", "backward", "enter", "leave")
+FINAL = BEAT + ("first",)
+FINISH = ("right_z", "backward")
+
+
+def named(names, refs):
+    return dict(zip(names, refs))
+
+
+def prep_kernel(cells_x, mine_ref, slow_ref, place_ref, depth_ref, amp_ref, *refs):
+    modes_ref, contrast_ref = refs[len(PREP) :]
+    dense = [jnp.concatenate([mine_ref[c, x] for x in cells_x], axis=0) for c in range(2)]
     slow = jnp.concatenate([slow_ref[x] for x in cells_x], axis=0)
     prepare(
-        jnp.concatenate(dense, axis=1), slow, place_ref[...], depth_ref[...], amp_ref,
-        Tables(places, fields_ref, packed_ref), modes_ref, contrast_ref,
-    )
-
-
-def prep_other_kernel(cells_x, places, core_ref, swap_ref, own_modes_ref, own_contrast_ref, place_ref, depth_ref,
-                      amp_ref, fields_ref, packed_ref, modes_ref, contrast_ref):
-    core = core_ref[0]
+        jnp.concatenate(dense, axis=1), slow, place_ref[...], depth_ref[...], amp_ref, named(PREP, refs),
+        modes_ref, contrast_ref,
+    )
+
+
+def prep_other_kernel(cells_x, core_ref, rhs_ref, swap_ref, slow_ref, own_modes_ref, own_contrast_ref, place_ref,
+                      depth_ref, amp_ref, *refs):
+    modes_ref, contrast_ref = refs[len(PREP) :]
+    core, rhs = core_ref[0], rhs_ref[0]
     other = 1 - core
     modes_ref[core] = own_modes_ref[...]
     contrast_ref[core] = own_contrast_ref[...]
-    parts = [jnp.concatenate([swap_ref[c, x] for x in cells_x], axis=0) for c in range(3)]
+    dense = [jnp.concatenate([swap_ref[rhs, c, x] for x in cells_x], axis=0) for c in range(2)]
+    slow = jnp.concatenate([slow_ref[x] for x in cells_x], axis=0)
     prepare(
-        jnp.concatenate(parts[:2], axis=1), parts[2], place_ref[...], depth_ref[...], amp_ref,
-        Tables(places, fields_ref, packed_ref), modes_ref.at[other], contrast_ref.at[other],
-    )
-
-
-def beat_kernel(tile, final, places, active_ref, modes_ref, contrast_ref, trace_x_ref, trace_y_ref, total_ref,
-                term_ref, fields_ref, packed_ref, new_total_ref, new_term_ref, *out_refs):
-    t = Tables(places, fields_ref, packed_ref)
+        jnp.concatenate(dense, axis=1), slow, place_ref[...], depth_ref[...], amp_ref, named(PREP, refs),
+        modes_ref.at[other], contrast_ref.at[other],
+    )
+
+
+def beat_kernel(tile, final, active_ref, modes_ref, contrast_ref, trace_x_ref, trace_y_ref, total_ref, term_ref,
+                *refs):
+    names = FINAL if final else BEAT
+    t = named(names, refs)
+    new_total_ref, new_term_ref, *out_refs = refs[len(names) :]
     count = trace_x_ref.shape[0]
 
     @pl.when(active_ref[0] == 1)
     def _():
         trace = jnp.concatenate([trace_x_ref[...], trace_y_ref[...]], axis=0)
-        start = modes_ref[tile] + t.divide(left_product(t["enter"], trace))
+        start = modes_ref[tile] + divide(left_product(t["enter"][...], trace), t)
         total, term = solve_modes(start, contrast_ref.at[tile], t)
         new_total_ref[...] = total
         new_term_ref[...] = term
         if not (final and tile == 1):
-            out = left_product(t["leave"], total)
+            out = left_product(t["leave"][...], total)
             for out_ref, part in zip(out_refs[:1] if final else out_refs, (out[:count], out[count:])):
                 out_ref[...] = part
 
@@ -262,17 +253,17 @@
         new_term_ref[...] = term_ref[...]
 
     if final:
-        out = left_product(t["first"], new_total_ref[...])
+        out = left_product(t["first"][...], new_total_ref[...])
         edge_refs = out_refs[1 - tile :]
         edge_refs[-1][...] = out[count:]
         if tile == 0:
             edge_refs[0][...] = out[:count]
 
 
-def finish_kernel(cells_x, places, core_ref, total0_ref, term0_ref, total1_ref, term1_ref, contrast_ref,
-                  fields_ref, packed_ref, keep_ref, give_ref, both_ref):
+def finish_kernel(cells_x, core_ref, total0_ref, term0_ref, total1_ref, term1_ref, contrast_ref,
+                  z_ref, backward_ref, keep_ref, give_ref, both_ref):
     _, _, _, size_x, size_y, cells_z = both_ref.shape
-    t = Tables(places, fields_ref, packed_ref)
+    t = named(FINISH, (z_ref, backward_ref))
     for tile, (total_ref, term_ref) in enumerate(((total0_ref, term0_ref), (total1_ref, term1_ref))):
         wave, rest = [z_transform(to_cells(ref[...], t), t) for ref in (total_ref, term_ref)]
         rest = times(contrast_ref[tile, 0], contrast_ref[tile, 1], rest)
@@ -305,11 +296,11 @@
         rest_ref[c, :, size_y - 2 :] += two
 
 
-def keep_kernel(places, core_ref, keep_ref, edge_x_ref, edge_y_ref, packed_ref, rest_ref):
+def keep_kernel(core_ref, keep_ref, edge_x_ref, edge_y_ref, z_ref, rest_ref):
     rest_ref[...] = keep_ref[1]
     count = edge_x_ref.shape[0]
     edges = jnp.concatenate([edge_x_ref[...], edge_y_ref[core_ref[0]]], axis=0)
-    edges = z_transform(edges, Tables(places, None, packed_ref))
+    edges = z_transform(edges, dict(right_z=z_ref))
     add_later(rest_ref, edges[:count], edges[count:], (core_ref[0] == 1).astype(F32))
 
 
@@ -325,14 +316,13 @@
         copy.wait()
 
 
-def place_rest_kernel(places, core_ref, rhs_ref, keep_rest_ref, got_ref, got_edge_ref, packed_ref, rest_ref, work_ref,
-                      sems):
+def place_rest_kernel(core_ref, rhs_ref, keep_rest_ref, got_ref, got_edge_ref, z_ref, rest_ref, work_ref, sems):
     rhs = rhs_ref[0]
     count = got_edge_ref.shape[0] // 2
     copies = [pltpu.make_async_copy(keep_rest_ref, rest_ref.at[rhs], sems.at[0])]
     copies[0].start()
     work_ref[...] = got_ref[1]
-    edges = z_transform(got_edge_ref[...], Tables(places, None, packed_ref))
+    edges = z_transform(got_edge_ref[...], dict(right_z=z_ref))
     add_later(work_ref, edges[:count], edges[count:], (core_ref[0] == 1).astype(F32))
     copies.append(pltpu.make_async_copy(work_ref, rest_ref.at[1 - rhs], sems.at[1]))
     copies[1].start()
@@ -370,8 +360,8 @@
     core = row % 2
     rhs = (core + row // 2 + col) % 2
     core_ref, rhs_ref = core[None], rhs[None]
-    fields, packed, table_places, cells_x = tables(size_x, size_y, cells_z)
-    fields, packed = jnp.asarray(fields), jnp.asarray(packed)
+    t, cells_x = tables(size_x, size_y, cells_z)
+    t = {name: jnp.asarray(value) for name, value in t.items()}
     rows = size_x * size_y
 
     def device(chip, core, column):
@@ -387,8 +377,9 @@
         for k in range(chips) for j in range(grid_cols) for r in range(2)
     ]
     axes = ("gx", "gy")
-    other = lax.dynamic_index_in_dim(right_side, 1 - rhs, 0, keepdims=False)
-    swapped = lax.ppermute(jnp.concatenate([other, slowness[None]], axis=0), axes, own)
+    swapped = lax.ppermute(right_side, axes, own)
+    swapped_slow = lax.ppermute(slowness, axes, own)
+    mine = lax.dynamic_index_in_dim(right_side, rhs, 0, keepdims=False)
 
     total_y = size_y * grid_cols
     cells = lax.dynamic_index_in_dim(source_cells, rhs, 0, keepdims=True)
@@ -402,39 +393,40 @@
     amplitudes = lax.dynamic_index_in_dim(source_amplitudes, rhs, 0, keepdims=False).T[:, None, :]
 
     depth = cells % cells_z
-    one = (shaped(rows, 2 * cells_z), shaped(2, rows, cells_z))
+    prep_tables = [t[name] for name in PREP]
     own_modes, own_contrast = pl.pallas_call(
-        functools.partial(prep_kernel, cells_x, table_places),
-        out_shape=one,
-        in_specs=[scalars()] + [whole()] * 7,
+        functools.partial(prep_kernel, cells_x),
+        out_shape=(shaped(rows, 2 * cells_z), shaped(2, rows, cells_z)),
+        in_specs=[whole()] * (5 + len(PREP)),
         out_specs=(whole(), whole()),
         compiler_params=PARAMS,
         cost_estimate=SOLVE_COST,
         name="prep",
-    )(rhs_ref, right_side, slowness, places[0], depth, amplitudes, fields, packed)
+    )(mine, slowness, places[0], depth, amplitudes, *prep_tables)
     modes, contrast = pl.pallas_call(
-        functools.partial(prep_other_kernel, cells_x, table_places),
+        functools.partial(prep_other_kernel, cells_x),
         out_shape=(shaped(2, rows, 2 * cells_z), shaped(2, 2, rows, cells_z)),
-        in_specs=[scalars()] + [whole()] * 8,
+        in_specs=[scalars()] * 2 + [whole()] * (7 + len(PREP)),
         out_specs=(whole(), whole()),
         compiler_params=PARAMS,
         cost_estimate=SOLVE_COST,
         name="prep_other",
-    )(core_ref, swapped, own_modes, own_contrast, places[1], depth, amplitudes, fields, packed)
+    )(core_ref, rhs_ref, swapped, swapped_slow, own_modes, own_contrast, places[1], depth, amplitudes, *prep_tables)
 
     def solve(tile, active, trace_x, trace_y, state, final):
+        names = FINAL if final else BEAT
         x, y = shaped(*zero_x.shape), shaped(*zero_y.shape)
         outs = ((x, x, y), (y,))[tile] if final else (x, y)
         total, term, *outs = pl.pallas_call(
-            functools.partial(beat_kernel, tile, final, table_places),
+            functools.partial(beat_kernel, tile, final),
             out_shape=(shaped(rows, 2 * cells_z),) * 2 + outs,
-            in_specs=[scalars()] + [whole()] * 8,
+            in_specs=[scalars()] + [whole()] * (6 + len(names)),
             out_specs=(whole(),) * (2 + len(outs)),
             input_output_aliases={5: 0, 6: 1},
             compiler_params=PARAMS,
             cost_estimate=SOLVE_COST,
             name="upper" if tile == 0 else "lower",
-        )(active, modes, contrast, trace_x, trace_y, *state, fields, packed)
+        )(active, modes, contrast, trace_x, trace_y, *state, *[t[name] for name in names])
         return (total, term), outs
 
     def hand_on(trace):
@@ -474,27 +466,27 @@
 
     half = shaped(2, 2, size_x, size_y, cells_z)
     keep, give = pl.pallas_call(
-        functools.partial(finish_kernel, cells_x, table_places),
+        functools.partial(finish_kernel, cells_x),
         out_shape=(half, half),
         in_specs=[scalars()] + [whole()] * 7,
         out_specs=(whole(), whole()),
         scratch_shapes=[pltpu.VMEM((2, 2, 2, size_x, size_y, cells_z), F32)],
         compiler_params=PARAMS,
         name="finish",
-    )(core_ref, *states[0], *states[1], contrast, fields, packed)
+    )(core_ref, *states[0], *states[1], contrast, *[t[name] for name in FINISH])
     got = lax.ppermute(give, axes, own)
 
     pass_y = lax.dynamic_index_in_dim(after_y, 1 - core, 0, keepdims=False)
     got_edge = lax.ppermute(jnp.concatenate([after_x, pass_y], axis=0), axes, own)
     keep_rest = pl.pallas_call(
-        functools.partial(keep_kernel, table_places),
+        keep_kernel,
         out_shape=shaped(*half.shape[1:]),
         in_specs=[scalars()] + [whole()] * 4,
         out_specs=whole(),
         compiler_params=PARAMS,
         cost_estimate=KEEP_COST,
         name="keep",
-    )(core_ref, keep, after_x, after_y, packed)
+    )(core_ref, keep, after_x, after_y, t["right_z"])
     wavefield = pl.pallas_call(
         place_wave_kernel,
         out_shape=shaped(*right_side.shape),
@@ -506,7 +498,7 @@
         name="place_wave",
     )(rhs_ref, keep, got)
     residual = pl.pallas_call(
-        functools.partial(place_rest_kernel, table_places),
+        place_rest_kernel,
         out_shape=shaped(*right_side.shape),
         in_specs=[scalars()] * 2 + [whole()] * 4,
         out_specs=anywhere(),
@@ -516,7 +508,7 @@
         ],
         compiler_params=PARAMS,
         name="place_rest",
-    )(core_ref, rhs_ref, keep_rest, got, got_edge, packed)
+    )(core_ref, rhs_ref, keep_rest, got, got_edge, t["right_z"])
     return wavefield, residual
 
 

time: 71.7 us -> 69.8 us (0.974)
  the two profiles are of different devices: /device:TPU:23 before, /device:TPU:29 now
where the time goes in v10:
time: 69.8 us; the launch traced here: 68.6 us
  waiting for transfers between devices  30.4 us (44%)
  starting transfers between devices  20.6 us (30%)
  Pallas kernels  10.2 us (15%)
  local copies, waits for them, and re-layouts  5.86 us (8%)
  between operations  1.51 us (2%)
    ppermute x6, waiting for transfers between devices, body(): trace_y0 = hand_on(lax.ppermute(outs0[0], axes, along_y))  26 us
    pallas_call x14, Pallas kernels, solve(): pl.pallas_call(functools.partial(beat_kernel, tile, final), out_shape=(sh...  5.61 us
    ppermute x6, starting transfers between devices, body(): trace_y0 = hand_on(lax.ppermute(outs0[0], axes, along_y))  5.24 us
    ppermute x6, starting transfers between devices, body(): trace_y1 = lax.ppermute(outs1[1], axes, along_y)  5.24 us
    unnamed x28, local copies, waits for them, and re-layouts  4.74 us
    ppermute x6, starting transfers between devices, body(): trace_x = lax.ppermute(outs1[0], axes, along_x)  4.61 us
    ppermute x1, waiting for transfers between devices, body(): lax.ppermute(edge_y, axes, between([((k, j), (k, j - 1)) for k, j in ever...  2.33 us
    ppermute x1, starting transfers between devices, body(): lax.ppermute(edge_y, axes, between([((k, j), (k, j - 1)) for k, j in ever...  1.92 us
  transfers between devices with their start and end apart: 24, of which 4 were waited for; matrix products, arithmetic and copies ran while one was open for 2% of the time, Pallas kernels for 12%

profile of v10, /device:TPU:29, one launch (start us, length us, event | category | flops | bytes accessed | tf_op | source)
XLA Modules:
  0.0 68.6 jit_solution(2689714304874256186)
XLA Ops:
  0.7 0.7 %collective-permute-start = (f32[2,2,16,16,128]{4,3,2,1,0:T(8,128)}, f32[2,2,16,16,128]{4,3,2,1,0:T(8,128)S(1)}, u32[]{:S(2)}, u32[]{:S(2)}) collective-permute-start(f32[2,2,16,16,128]{4,3,2,1,0:T(8,128)} %param.12), channel_id=1, source_target_pairs={{0,4},{4,0},{1,5},{5,1},{2,6},{6,2},{3,7},{7,3},{8,12},{12,8},{9,1... | collective-permute-start | bytes 1572872 | tf_op jit(solution)/shard_map/ppermute | solution.py:380
  1.5 1.0 %dynamic-slice_bitcast_fusion.mine_ref = f32[2,16,16,128]{3,2,1,0:T(8,128)S(1)} fusion(f32[2,2,16,16,128]{4,3,2,1,0:T(8,128)} %param.12, s32[]{:T(128)S(6)} %select_n.69), kind=kLoop, calls=%fused_computation | loop fusion | bytes 524292 | tf_op jit(solution)/shard_map/jit(dynamic_index_in_dim)/squeeze | solution.py:382
  2.7 0.9 %copy-done.4 = f32[2,256,128]{2,1,0:T(8,128)S(1)} copy-done((f32[2,256,128]{2,1,0:T(8,128)S(1)}, f32[2,256,128]{2,1,0:T(8,128)}, u32[]{:S(2)}) %copy-start.4) | copy-done | bytes 262168
  3.6 0.9 %copy-done.7 = bf16[256,192]{1,0:T(8,128)(2,1)S(1)} copy-done((bf16[256,192]{1,0:T(8,128)(2,1)S(1)}, bf16[256,192]{1,0:T(8,128)(2,1)}, u32[]{:S(2)}) %copy-start.7) | copy-done | bytes 98328
  4.5 0.9 %copy-done.9 = f32[256,1]{1,0:T(8,128)S(1)} copy-done((f32[256,1]{1,0:T(8,128)S(1)}, f32[256,1]{1,0:T(8,128)}, u32[]{:S(2)}) %copy-start.9) | copy-done | bytes 1048
  5.4 0.9 %copy-done.10 = bf16[64,768]{1,0:T(8,128)(2,1)S(1)} copy-done((bf16[64,768]{1,0:T(8,128)(2,1)S(1)}, bf16[64,768]{1,0:T(8,128)(2,1)}, u32[]{:S(2)}) %copy-start.10) | copy-done | bytes 98328
  6.3 0.8 %prep.1 = (f32[256,256]{1,0:T(8,128)S(1)}, f32[2,256,128]{2,1,0:T(8,128)S(1)}) custom-call(f32[2,16,16,128]{3,2,1,0:T(8,128)S(1)} %dynamic-slice_bitcast_fusion.mine_ref, f32[16,16,128]{2,1,0:T(8,128)S(1)} %copy-done.3, s32[1,16]{1,0:T(1,128)S(1)} %and_select_fusion.2.place_ref, s32[1,16]{1,0:T(1,128)S(1)} %and_select_fusion.1.depth_ref, ...), custom_call_target="tpu_custom_call" | custom-call | flops 2000000000 | bytes 2000000 | tf_op jit(solution)/shard_map/prep/pallas_call | solution.py:397
  7.1 0.2 copy-done.5
  7.3 0.8 %prep_other.1 = (f32[2,256,256]{2,1,0:T(8,128)S(1)}, f32[2,2,256,128]{3,2,1,0:T(8,128)S(1)}) custom-call(s32[1]{0:T(128)} %bitcast.1.core_ref, s32[1]{0:T(128)} %bitcast.rhs_ref, f32[2,2,16,16,128]{4,3,2,1,0:T(8,128)S(1)} %collective-permute-done.swap_ref, f32[16,16,128]{2,1,0:T(8,128)S(1)} %collective-permute-done.1.slow_ref, ...), custom_call_target="tpu_custom_call" | custom-call | flops 2000000000 | bytes 2000000 | tf_op jit(solution)/shard_map/prep_other/pallas_call | solution.py:406
  8.2 0.9 %copy-done.11 = bf16[64,768]{1,0:T(8,128)(2,1)S(1)} copy-done((bf16[64,768]{1,0:T(8,128)(2,1)S(1)}, bf16[64,768]{1,0:T(8,128)(2,1)}, u32[]{:S(2)}) %copy-start.11) | copy-done | bytes 98328
  9.1 0.7 collective-permute-start.3
  9.8 0.1 lower.7
  9.9 0.7 collective-permute-start.2
  10.6 0.7 collective-permute-start.4
  11.4 0.7 collective-permute-start.6
  12.1 0.7 collective-permute-start.5
  12.8 0.7 collective-permute-start.7
  13.5 0.1 upper.9
  13.6 0.7 collective-permute-start.9
  14.3 0.1 lower.9
  14.4 0.7 collective-permute-start.8
  15.1 0.7 collective-permute-start.10
  15.8 0.7 collective-permute-start.12
  16.5 0.3 lower.10
  16.8 0.7 collective-permute-start.11
  17.5 0.7 collective-permute-start.13
  18.3 1.3 %collective-permute-start.15 = (f32[32,256]{1,0:T(8,128)S(1)}, f32[32,256]{1,0:T(8,128)S(1)}, u32[]{:S(2)}, u32[]{:S(2)}) collective-permute-start(f32[32,256]{1,0:T(8,128)S(1)} %get-tuple-element.102), channel_id=1, source_target_pairs={{18,23},{22,19},{25,30},{29,26}} | collective-permute-start | bytes 98312 | tf_op jit(solution)/shard_map/ppermute | solution.py:454
  19.7 1.3 %collective-permute-start.14 = (f32[32,256]{1,0:T(8,128)S(1)}, f32[32,256]{1,0:T(8,128)S(1)}, u32[]{:S(2)}, u32[]{:S(2)}) collective-permute-start(f32[32,256]{1,0:T(8,128)S(1)} %get-tuple-element.101), channel_id=1, source_target_pairs={{11,23},{15,19},{18,30},{22,26}} | collective-permute-start | bytes 98312 | tf_op jit(solution)/shard_map/ppermute | solution.py:457
  21.0 1.3 %collective-permute-start.16 = (f32[32,256]{1,0:T(8,128)S(1)}, f32[32,256]{1,0:T(8,128)S(1)}, u32[]{:S(2)}, u32[]{:S(2)}) collective-permute-start(f32[32,256]{1,0:T(8,128)S(1)} %get-tuple-element.106), channel_id=1, source_target_pairs={{18,23},{22,19},{25,30},{29,26}} | collective-permute-start | bytes 98312 | tf_op jit(solution)/shard_map/ppermute | solution.py:459
  22.3 26.0 %collective-permute-done.15.in_ref = f32[32,256]{1,0:T(8,128)S(1)} collective-permute-done((f32[32,256]{1,0:T(8,128)S(1)}, f32[32,256]{1,0:T(8,128)S(1)}, u32[]{:S(2)}, u32[]{:S(2)}) %collective-permute-start.15) | collective-permute-done | bytes 32800 | tf_op jit(solution)/shard_map/ppermute | solution.py:454
  48.3 1.3 %collective-permute-done.14.trace_x_ref = f32[32,256]{1,0:T(8,128)S(1)} collective-permute-done((f32[32,256]{1,0:T(8,128)S(1)}, f32[32,256]{1,0:T(8,128)S(1)}, u32[]{:S(2)}, u32[]{:S(2)}) %collective-permute-start.14) | collective-permute-done | bytes 32800 | tf_op jit(solution)/shard_map/ppermute | solution.py:457
  49.6 2.1 %upper.12 = (f32[256,256]{1,0:T(8,128)S(1)}, f32[256,256]{1,0:T(8,128)S(1)}, f32[32,256]{1,0:T(8,128)S(1)}, f32[32,256]{1,0:T(8,128)S(1)}) custom-call(s32[1]{0:T(128)} %bitcast.8.active_ref, f32[2,256,256]{2,1,0:T(8,128)S(1)} %get-tuple-element.66.modes_ref, ...), custom_call_target="tpu_custom_call", output_to_operand_aliasing={{0}: (5, {}), {1}: (6, {})} | custom-call | flops 2000000000 | bytes 2000000 | tf_op jit(solution)/shard_map/upper/pallas_call | solution.py:420
  51.6 1.3 %collective-permute-start.18 = (f32[32,256]{1,0:T(8,128)S(1)}, f32[32,256]{1,0:T(8,128)S(1)}, u32[]{:S(2)}, u32[]{:S(2)}) collective-permute-start(f32[32,256]{1,0:T(8,128)S(1)} %get-tuple-element.110), channel_id=1, source_target_pairs={{26,31},{30,27}} | collective-permute-start | bytes 98312 | tf_op jit(solution)/shard_map/ppermute | solution.py:454
  53.0 2.1 %lower.12 = (f32[256,256]{1,0:T(8,128)S(1)}, f32[256,256]{1,0:T(8,128)S(1)}, f32[32,256]{1,0:T(8,128)S(1)}, f32[32,256]{1,0:T(8,128)S(1)}) custom-call(s32[1]{0:T(128)} %bitcast.8.active_ref, f32[2,256,256]{2,1,0:T(8,128)S(1)} %get-tuple-element.66.modes_ref, ...), custom_call_target="tpu_custom_call", output_to_operand_aliasing={{0}: (5, {}), {1}: (6, {})} | custom-call | flops 2000000000 | bytes 2000000 | tf_op jit(solution)/shard_map/lower/pallas_call | solution.py:420
  55.0 0.7 collective-permute-start.17
  55.7 1.3 %collective-permute-start.19 = (f32[32,256]{1,0:T(8,128)S(1)}, f32[32,256]{1,0:T(8,128)S(1)}, u32[]{:S(2)}, u32[]{:S(2)}) collective-permute-start(f32[32,256]{1,0:T(8,128)S(1)} %get-tuple-element.116), channel_id=1, source_target_pairs={{26,31},{30,27}} | collective-permute-start | bytes 98312 | tf_op jit(solution)/shard_map/ppermute | solution.py:459
  57.1 0.3 upper.13
  57.4 0.7 collective-permute-done.19.trace_y_ref
  58.0 0.3 lower.13
  58.3 1.9 %collective-permute-start.22 = (f32[2,32,256]{2,1,0:T(8,128)S(1)}, f32[2,32,256]{2,1,0:T(8,128)S(1)}, u32[]{:S(2)}, u32[]{:S(2)}) collective-permute-start(f32[2,32,256]{2,1,0:T(8,128)S(1)} %pad_maximum_fusion), channel_id=1, source_target_pairs={{1,4},{5,0},{2,5},{6,1},{3,6},{7,2},{9,12},{13,8},{10,13},{14,9},{... | collective-permute-start | bytes 196616 | tf_op jit(solution)/shard_map/ppermute | solution.py:465
  60.2 1.3 %collective-permute-start.21 = (f32[32,256]{1,0:T(8,128)S(1)}, f32[32,256]{1,0:T(8,128)S(1)}, u32[]{:S(2)}, u32[]{:S(2)}) collective-permute-start(f32[32,256]{1,0:T(8,128)S(1)} %get-tuple-element.123), channel_id=1, source_target_pairs={{8,4},{12,0},{9,5},{13,1},{10,6},{14,2},{11,7},{15,3},{16,12},{20,... | collective-permute-start | bytes 98312 | tf_op jit(solution)/shard_map/ppermute | solution.py:464
  61.5 1.1 %finish.1 = (f32[2,2,16,16,128]{4,3,2,1,0:T(8,128)S(1)}, f32[2,2,16,16,128]{4,3,2,1,0:T(8,128)S(1)}) custom-call(s32[1]{0:T(128)} %bitcast.1.core_ref, f32[256,256]{1,0:T(8,128)S(1)} %get-tuple-element.113.total0_ref, f32[256,256]{1,0:T(8,128)S(1)} %get-tuple-element.114.term0_ref, f32[256,256]{1,0:T(8,128)S(1)} %get-tuple-element.119.total1_ref, ...), custom_call_target="tpu_custom_call" | custom-call | tf_op jit(solution)/shard_map/finish/pallas_call | solution.py:468
  62.7 1.0 %collective-permute-start.20 = (f32[2,2,16,16,128]{4,3,2,1,0:T(8,128)S(1)}, f32[2,2,16,16,128]{4,3,2,1,0:T(8,128)S(1)}, u32[]{:S(2)}, u32[]{:S(2)}) collective-permute-start(f32[2,2,16,16,128]{4,3,2,1,0:T(8,128)S(1)} %get-tuple-element.122), channel_id=1, source_target_pairs={{0,4},{4,0},{1,5},{5,1},{2,6},{6,2},{3,7},{7,3},{8,12},{12,8},{9,1... | collective-permute-start | bytes 1572872 | tf_op jit(solution)/shard_map/ppermute | solution.py:477
  63.7 2.3 %collective-permute-done.22.edge_y_ref = f32[2,32,256]{2,1,0:T(8,128)S(1)} collective-permute-done((f32[2,32,256]{2,1,0:T(8,128)S(1)}, f32[2,32,256]{2,1,0:T(8,128)S(1)}, u32[]{:S(2)}, u32[]{:S(2)}) %collective-permute-start.22) | collective-permute-done | bytes 65568 | tf_op jit(solution)/shard_map/ppermute | solution.py:465
  66.1 0.5 collective-permute-start.23
  66.5 0.2 keep.1.keep_rest_ref
  66.7 0.8 %place_wave.1 = f32[2,2,16,16,128]{4,3,2,1,0:T(8,128)} custom-call(s32[1]{0:T(128)} %bitcast.rhs_ref, f32[2,2,16,16,128]{4,3,2,1,0:T(8,128)S(1)} %get-tuple-element.121.keep_ref, f32[2,2,16,16,128]{4,3,2,1,0:T(8,128)S(1)} %collective-permute-done.20.got_ref), custom_call_target="tpu_custom_call" | custom-call | flops 10000000000 | bytes 1000000 | tf_op jit(solution)/shard_map/place_wave/pallas_call | solution.py:490
  67.5 0.9 %place_rest.1 = f32[2,2,16,16,128]{4,3,2,1,0:T(8,128)} custom-call(s32[1]{0:T(128)} %bitcast.1.core_ref, s32[1]{0:T(128)} %bitcast.rhs_ref, f32[2,16,16,128]{3,2,1,0:T(8,128)S(1)} %keep.1.keep_rest_ref, f32[2,2,16,16,128]{4,3,2,1,0:T(8,128)S(1)} %collective-permute-done.20.got_ref, f32[64,256]{1,0:T(8,128)S(1)} %collective-permute-done.23.got_edge_ref, ...), custom_call_target="tpu_custom_call" | custom-call | tf_op jit(solution)/shard_map/place_rest/pallas_call | solution.py:500
  (67 shorter events, 0.8 us)
Async XLA Ops:
  0.6 2.0 %copy-start = (f32[2,16,2]{1,2,0:T(2,128)S(1)}, f32[2,16,2]{1,2,0:T(2,128)}, u32[]{:S(2)}) copy-start(f32[2,16,2]{1,2,0:T(2,128)} %param.15) | copy-start | bytes 772
  0.6 2.0 %copy-start.6 = (bf16[2,128,384]{2,1,0:T(8,128)(2,1)S(1)}, bf16[2,128,384]{2,1,0:T(8,128)(2,1)}, u32[]{:S(2)}) copy-start(bf16[2,128,384]{2,1,0:T(8,128)(2,1)} %constant.157.clone.refs_2_.refs_1_) | copy-start | bytes 589828
  0.7 6.5 %collective-permute-start = (f32[2,2,16,16,128]{4,3,2,1,0:T(8,128)}, f32[2,2,16,16,128]{4,3,2,1,0:T(8,128)S(1)}, u32[]{:S(2)}, u32[]{:S(2)}) collective-permute-start(f32[2,2,16,16,128]{4,3,2,1,0:T(8,128)} %param.12), channel_id=1, source_target_pairs={{0,4},{4,0},{1,5},{5,1},{2,6},{6,2},{3,7},{7,3},{8,12},{12,8},{9,1... | collective-permute-start | bytes 1572872 | tf_op jit(solution)/shard_map/ppermute | solution.py:380
  1.4 5.7 %collective-permute-start.1 = (f32[16,16,128]{2,1,0:T(8,128)}, f32[16,16,128]{2,1,0:T(8,128)S(1)}, u32[]{:S(2)}, u32[]{:S(2)}) collective-permute-start(f32[16,16,128]{2,1,0:T(8,128)} %slow_ref.1), channel_id=1, source_target_pairs={{0,4},{4,0},{1,5},{5,1},{2,6},{6,2},{3,7},{7,3},{8,12},{12,8},{9,1... | collective-permute-start | bytes 393224 | tf_op jit(solution)/shard_map/ppermute | solution.py:381
  1.5 1.1 %copy-start.13 = (s32[2,16]{1,0:T(2,128)S(1)}, s32[2,16]{1,0:T(2,128)}, u32[]{:S(2)}) copy-start(s32[2,16]{1,0:T(2,128)} %param.14) | copy-start | bytes 388
  1.5 1.2 %copy-start.1 = (bf16[256,256]{1,0:T(8,128)(2,1)S(1)}, bf16[256,256]{1,0:T(8,128)(2,1)}, u32[]{:S(2)}) copy-start(bf16[256,256]{1,0:T(8,128)(2,1)} %constant.159.clone.refs_3_.refs_2_.z_ref) | copy-start | bytes 393220
  1.5 1.2 %copy-start.2 = (bf16[2,128,384]{2,1,0:T(8,128)(2,1)S(1)}, bf16[2,128,384]{2,1,0:T(8,128)(2,1)}, u32[]{:S(2)}) copy-start(bf16[2,128,384]{2,1,0:T(8,128)(2,1)} %constant.158.clone.refs_4_.refs_3_.backward_ref) | copy-start | bytes 589828
  1.5 1.2 %copy-start.3 = (f32[16,16,128]{2,1,0:T(8,128)S(1)}, f32[16,16,128]{2,1,0:T(8,128)}, u32[]{:S(2)}) copy-start(f32[16,16,128]{2,1,0:T(8,128)} %slow_ref.1) | copy-start | bytes 393220
  2.7 1.0 %copy-start.4 = (f32[2,256,128]{2,1,0:T(8,128)S(1)}, f32[2,256,128]{2,1,0:T(8,128)}, u32[]{:S(2)}) copy-start(f32[2,256,128]{2,1,0:T(8,128)} %constant.155.clone.refs_0_) | copy-start | bytes 786436
  3.6 0.9 %copy-start.7 = (bf16[256,192]{1,0:T(8,128)(2,1)S(1)}, bf16[256,192]{1,0:T(8,128)(2,1)}, u32[]{:S(2)}) copy-start(bf16[256,192]{1,0:T(8,128)(2,1)} %constant.160.clone.refs_5_.refs_4_) | copy-start | bytes 294916
  4.5 0.9 %copy-start.9 = (f32[256,1]{1,0:T(8,128)S(1)}, f32[256,1]{1,0:T(8,128)}, u32[]{:S(2)}) copy-start(f32[256,1]{1,0:T(8,128)} %constant.156.clone.refs_1_) | copy-start | bytes 3076
  5.4 0.9 %copy-start.10 = (bf16[64,768]{1,0:T(8,128)(2,1)S(1)}, bf16[64,768]{1,0:T(8,128)(2,1)}, u32[]{:S(2)}) copy-start(bf16[64,768]{1,0:T(8,128)(2,1)} %constant.161.clone.refs_6_.refs_5_) | copy-start | bytes 294916
  6.3 0.9 %copy-start.5 = (f32[2,256,128]{2,1,0:T(8,128)S(1)}, f32[2,256,128]{2,1,0:T(8,128)}, u32[]{:S(2)}) copy-start(f32[2,256,128]{2,1,0:T(8,128)} %constant.155.clone.refs_0_) | copy-start | bytes 786436
  6.3 1.0 %copy-start.8 = (bf16[256,192]{1,0:T(8,128)(2,1)S(1)}, bf16[256,192]{1,0:T(8,128)(2,1)}, u32[]{:S(2)}) copy-start(bf16[256,192]{1,0:T(8,128)(2,1)} %constant.160.clone.refs_5_.refs_4_) | copy-start | bytes 294916
  8.1 0.9 %copy-start.11 = (bf16[64,768]{1,0:T(8,128)(2,1)S(1)}, bf16[64,768]{1,0:T(8,128)(2,1)}, u32[]{:S(2)}) copy-start(bf16[64,768]{1,0:T(8,128)(2,1)} %constant.161.clone.refs_6_.refs_5_) | copy-start | bytes 294916
  9.1 2.2 %collective-permute-start.3 = (f32[32,256]{1,0:T(8,128)S(1)}, f32[32,256]{1,0:T(8,128)S(1)}, u32[]{:S(2)}, u32[]{:S(2)}) collective-permute-start(f32[32,256]{1,0:T(8,128)S(1)} %get-tuple-element.70), channel_id=1, source_target_pairs={{0,5},{4,1}} | collective-permute-start | bytes 98312 | tf_op jit(solution)/shard_map/ppermute | solution.py:454
  9.9 1.4 %collective-permute-start.2 = (f32[32,256]{1,0:T(8,128)S(1)}, f32[32,256]{1,0:T(8,128)S(1)}, u32[]{:S(2)}, u32[]{:S(2)}) collective-permute-start(f32[32,256]{1,0:T(8,128)S(1)} %get-tuple-element.69), channel_id=1, source_target_pairs={{0,12},{4,8}} | collective-permute-start | bytes 98312 | tf_op jit(solution)/shard_map/ppermute | solution.py:457
  10.6 1.5 %collective-permute-start.4 = (f32[32,256]{1,0:T(8,128)S(1)}, f32[32,256]{1,0:T(8,128)S(1)}, u32[]{:S(2)}, u32[]{:S(2)}) collective-permute-start(f32[32,256]{1,0:T(8,128)S(1)} %get-tuple-element.74), channel_id=1, source_target_pairs={{0,5},{4,1}} | collective-permute-start | bytes 98312 | tf_op jit(solution)/shard_map/ppermute | solution.py:459
  11.4 2.1 %collective-permute-start.6 = (f32[32,256]{1,0:T(8,128)S(1)}, f32[32,256]{1,0:T(8,128)S(1)}, u32[]{:S(2)}, u32[]{:S(2)}) collective-permute-start(f32[32,256]{1,0:T(8,128)S(1)} %get-tuple-element.78), channel_id=1, source_target_pairs={{1,6},{5,2},{8,13},{12,9}} | collective-permute-start | bytes 98312 | tf_op jit(solution)/shard_map/ppermute | solution.py:454
  12.1 1.4 %collective-permute-start.5 = (f32[32,256]{1,0:T(8,128)S(1)}, f32[32,256]{1,0:T(8,128)S(1)}, u32[]{:S(2)}, u32[]{:S(2)}) collective-permute-start(f32[32,256]{1,0:T(8,128)S(1)} %get-tuple-element.77), channel_id=1, source_target_pairs={{1,13},{5,9},{8,20},{12,16}} | collective-permute-start | bytes 98312 | tf_op jit(solution)/shard_map/ppermute | solution.py:457
  12.8 1.5 %collective-permute-start.7 = (f32[32,256]{1,0:T(8,128)S(1)}, f32[32,256]{1,0:T(8,128)S(1)}, u32[]{:S(2)}, u32[]{:S(2)}) collective-permute-start(f32[32,256]{1,0:T(8,128)S(1)} %get-tuple-element.82), channel_id=1, source_target_pairs={{1,6},{5,2},{8,13},{12,9}} | collective-permute-start | bytes 98312 | tf_op jit(solution)/shard_map/ppermute | solution.py:459
  13.6 2.1 %collective-permute-start.9 = (f32[32,256]{1,0:T(8,128)S(1)}, f32[32,256]{1,0:T(8,128)S(1)}, u32[]{:S(2)}, u32[]{:S(2)}) collective-permute-start(f32[32,256]{1,0:T(8,128)S(1)} %get-tuple-element.86), channel_id=1, source_target_pairs={{2,7},{6,3},{9,14},{13,10},{16,21},{20,17}} | collective-permute-start | bytes 98312 | tf_op jit(solution)/shard_map/ppermute | solution.py:454
  14.4 1.4 %collective-permute-start.8 = (f32[32,256]{1,0:T(8,128)S(1)}, f32[32,256]{1,0:T(8,128)S(1)}, u32[]{:S(2)}, u32[]{:S(2)}) collective-permute-start(f32[32,256]{1,0:T(8,128)S(1)} %get-tuple-element.85), channel_id=1, source_target_pairs={{2,14},{6,10},{9,21},{13,17},{16,28},{20,24}} | collective-permute-start | bytes 98312 | tf_op jit(solution)/shard_map/ppermute | solution.py:457
  15.1 1.5 %collective-permute-start.10 = (f32[32,256]{1,0:T(8,128)S(1)}, f32[32,256]{1,0:T(8,128)S(1)}, u32[]{:S(2)}, u32[]{:S(2)}) collective-permute-start(f32[32,256]{1,0:T(8,128)S(1)} %get-tuple-element.90), channel_id=1, source_target_pairs={{2,7},{6,3},{9,14},{13,10},{16,21},{20,17}} | collective-permute-start | bytes 98312 | tf_op jit(solution)/shard_map/ppermute | solution.py:459
  15.8 2.3 %collective-permute-start.12 = (f32[32,256]{1,0:T(8,128)S(1)}, f32[32,256]{1,0:T(8,128)S(1)}, u32[]{:S(2)}, u32[]{:S(2)}) collective-permute-start(f32[32,256]{1,0:T(8,128)S(1)} %get-tuple-element.94), channel_id=1, source_target_pairs={{10,15},{14,11},{17,22},{21,18},{24,29},{28,25}} | collective-permute-start | bytes 98312 | tf_op jit(solution)/shard_map/ppermute | solution.py:454
  16.8 1.4 %collective-permute-start.11 = (f32[32,256]{1,0:T(8,128)S(1)}, f32[32,256]{1,0:T(8,128)S(1)}, u32[]{:S(2)}, u32[]{:S(2)}) collective-permute-start(f32[32,256]{1,0:T(8,128)S(1)} %get-tuple-element.93), channel_id=1, source_target_pairs={{3,15},{7,11},{10,22},{14,18},{17,29},{21,25}} | collective-permute-start | bytes 98312 | tf_op jit(solution)/shard_map/ppermute | solution.py:457
  17.5 2.1 %collective-permute-start.13 = (f32[32,256]{1,0:T(8,128)S(1)}, f32[32,256]{1,0:T(8,128)S(1)}, u32[]{:S(2)}, u32[]{:S(2)}) collective-permute-start(f32[32,256]{1,0:T(8,128)S(1)} %get-tuple-element.98), channel_id=1, source_target_pairs={{10,15},{14,11},{17,22},{21,18},{24,29},{28,25}} | collective-permute-start | bytes 98312 | tf_op jit(solution)/shard_map/ppermute | solution.py:459
  18.3 30.0 %collective-permute-start.15 = (f32[32,256]{1,0:T(8,128)S(1)}, f32[32,256]{1,0:T(8,128)S(1)}, u32[]{:S(2)}, u32[]{:S(2)}) collective-permute-start(f32[32,256]{1,0:T(8,128)S(1)} %get-tuple-element.102), channel_id=1, source_target_pairs={{18,23},{22,19},{25,30},{29,26}} | collective-permute-start | bytes 98312 | tf_op jit(solution)/shard_map/ppermute | solution.py:454
  19.7 29.9 %collective-permute-start.14 = (f32[32,256]{1,0:T(8,128)S(1)}, f32[32,256]{1,0:T(8,128)S(1)}, u32[]{:S(2)}, u32[]{:S(2)}) collective-permute-start(f32[32,256]{1,0:T(8,128)S(1)} %get-tuple-element.101), channel_id=1, source_target_pairs={{11,23},{15,19},{18,30},{22,26}} | collective-permute-start | bytes 98312 | tf_op jit(solution)/shard_map/ppermute | solution.py:457
  21.0 32.0 %collective-permute-start.16 = (f32[32,256]{1,0:T(8,128)S(1)}, f32[32,256]{1,0:T(8,128)S(1)}, u32[]{:S(2)}, u32[]{:S(2)}) collective-permute-start(f32[32,256]{1,0:T(8,128)S(1)} %get-tuple-element.106), channel_id=1, source_target_pairs={{18,23},{22,19},{25,30},{29,26}} | collective-permute-start | bytes 98312 | tf_op jit(solution)/shard_map/ppermute | solution.py:459
  51.6 5.4 %collective-permute-start.18 = (f32[32,256]{1,0:T(8,128)S(1)}, f32[32,256]{1,0:T(8,128)S(1)}, u32[]{:S(2)}, u32[]{:S(2)}) collective-permute-start(f32[32,256]{1,0:T(8,128)S(1)} %get-tuple-element.110), channel_id=1, source_target_pairs={{26,31},{30,27}} | collective-permute-start | bytes 98312 | tf_op jit(solution)/shard_map/ppermute | solution.py:454
  53.0 4.1 %copy-start.12 = (bf16[64,768]{1,0:T(8,128)(2,1)S(1)}, bf16[64,768]{1,0:T(8,128)(2,1)}, u32[]{:S(2)}) copy-start(bf16[64,768]{1,0:T(8,128)(2,1)} %constant.162.clone.refs_6_) | copy-start | bytes 294916
  55.0 2.0 %collective-permute-start.17 = (f32[32,256]{1,0:T(8,128)S(1)}, f32[32,256]{1,0:T(8,128)S(1)}, u32[]{:S(2)}, u32[]{:S(2)}) collective-permute-start(f32[32,256]{1,0:T(8,128)S(1)} %get-tuple-element.109), channel_id=1, source_target_pairs={{19,31},{23,27}} | collective-permute-start | bytes 98312 | tf_op jit(solution)/shard_map/ppermute | solution.py:457
  55.7 2.3 %collective-permute-start.19 = (f32[32,256]{1,0:T(8,128)S(1)}, f32[32,256]{1,0:T(8,128)S(1)}, u32[]{:S(2)}, u32[]{:S(2)}) collective-permute-start(f32[32,256]{1,0:T(8,128)S(1)} %get-tuple-element.116), channel_id=1, source_target_pairs={{26,31},{30,27}} | collective-permute-start | bytes 98312 | tf_op jit(solution)/shard_map/ppermute | solution.py:459
  58.3 7.7 %collective-permute-start.22 = (f32[2,32,256]{2,1,0:T(8,128)S(1)}, f32[2,32,256]{2,1,0:T(8,128)S(1)}, u32[]{:S(2)}, u32[]{:S(2)}) collective-permute-start(f32[2,32,256]{2,1,0:T(8,128)S(1)} %pad_maximum_fusion), channel_id=1, source_target_pairs={{1,4},{5,0},{2,5},{6,1},{3,6},{7,2},{9,12},{13,8},{10,13},{14,9},{... | collective-permute-start | bytes 196616 | tf_op jit(solution)/shard_map/ppermute | solution.py:465
  60.2 5.8 %collective-permute-start.21 = (f32[32,256]{1,0:T(8,128)S(1)}, f32[32,256]{1,0:T(8,128)S(1)}, u32[]{:S(2)}, u32[]{:S(2)}) collective-permute-start(f32[32,256]{1,0:T(8,128)S(1)} %get-tuple-element.123), channel_id=1, source_target_pairs={{8,4},{12,0},{9,5},{13,1},{10,6},{14,2},{11,7},{15,3},{16,12},{20,... | collective-permute-start | bytes 98312 | tf_op jit(solution)/shard_map/ppermute | solution.py:464
  62.7 4.0 %collective-permute-start.20 = (f32[2,2,16,16,128]{4,3,2,1,0:T(8,128)S(1)}, f32[2,2,16,16,128]{4,3,2,1,0:T(8,128)S(1)}, u32[]{:S(2)}, u32[]{:S(2)}) collective-permute-start(f32[2,2,16,16,128]{4,3,2,1,0:T(8,128)S(1)} %get-tuple-element.122), channel_id=1, source_target_pairs={{0,4},{4,0},{1,5},{5,1},{2,6},{6,2},{3,7},{7,3},{8,12},{12,8},{9,1... | collective-permute-start | bytes 1572872 | tf_op jit(solution)/shard_map/ppermute | solution.py:477
  66.1 1.5 %collective-permute-start.23 = (f32[64,256]{1,0:T(8,128)S(1)}, f32[64,256]{1,0:T(8,128)S(1)}, u32[]{:S(2)}, u32[]{:S(2)}) collective-permute-start(f32[64,256]{1,0:T(8,128)S(1)} %pad_maximum_fusion.1), channel_id=1, source_target_pairs={{0,4},{4,0},{1,5},{5,1},{2,6},{6,2},{3,7},{7,3},{8,12},{12,8},{9,1... | collective-permute-start | bytes 196616 | tf_op jit(solution)/shard_map/ppermute | solution.py:480

commit v11 on v10

--- a/solution.py
+++ b/solution.py
@@ -33,6 +33,29 @@
     return np.concatenate([high, high, low], axis=1)
 
 
+def slabs(matrices, rows, lanes):
+    pieces, free = [], 0
+    for matrix in matrices:
+        for row in range(0, matrix.shape[0], rows):
+            for lane in range(0, matrix.shape[1], lanes):
+                piece = matrix[row : row + rows, lane : lane + lanes]
+                if free + piece.shape[0] > rows or not pieces:
+                    pieces.append(np.zeros((rows, lanes), matrix.dtype))
+                    free = 0
+                pieces[-1][free : free + piece.shape[0], : piece.shape[1]] = piece
+                free += piece.shape[0]
+    return np.stack(pieces)
+
+
+def enter_matrix(t, depth):
+    return jnp.concatenate([t["later"][2, :, :depth], t["later"][3, :, :depth]], axis=0)
+
+
+def leave_matrix(t):
+    count = t["later"].shape[1] // 2
+    return jnp.concatenate([t["later"][4, :count], t["later"][4, count:]], axis=1)
+
+
 def tables(size_x, size_y, cells_z):
     sine_x, angle_x = sine_matrix(size_x)
     sine_y, angle_y = sine_matrix(size_y)
@@ -86,15 +109,11 @@
             axis=1,
         ).T
     )
-    edge = np.zeros((size_x, size_y, 1))
-    edge[0] += 1.0 / 12.0
-    edge[-1] += 1.0 / 12.0
-    edge[:, 0] += 1.0 / 12.0
-    edge[:, -1] += 1.0 / 12.0
-    edge = edge[cells].reshape(size_x * size_y, 1).astype(np.float32)
+    assert enter.shape[0] == 2 * half * size_y and enter.shape[1] <= forward[0].shape[1]
+    assert 2 * leave.shape[0] == half * size_y and leave.shape[1] == 2 * forward[0].shape[1]
     return dict(
-        inverse=inverse, edge=edge, forward=np.stack(forward), backward=np.stack(backward),
-        right_z=right_z, enter=enter, leave=leave, first=first,
+        inverse=inverse, forward=np.stack(forward), right_z=right_z, first=first,
+        later=slabs(backward + [enter, leave], half * size_y, forward[0].shape[1]),
     ), tuple(int(x) for x in cells)
 
 
@@ -135,8 +154,8 @@
 
 def to_cells(modes, t):
     count = modes.shape[0] // 2
-    even = left_product(t["backward"][0], modes[:count])
-    odd = left_product(t["backward"][1], modes[count:])
+    even = left_product(t["later"][0], modes[:count])
+    odd = left_product(t["later"][1], modes[count:])
     return jnp.concatenate([even + odd, even - odd], axis=0)
 
 
@@ -165,7 +184,15 @@
     return total, term
 
 
-def prepare(dense, slow, place, depth, amplitude, t, modes_ref, contrast_ref):
+def edges(rows, lanes, layers):
+    place = lax.broadcasted_iota(jnp.int32, (rows, lanes), 0)
+    size_y = rows // layers
+    along_y = lax.rem(place, size_y)
+    outer = lax.rem(place, rows // 2) < size_y
+    return (outer.astype(F32) + ((along_y == 0) | (along_y == size_y - 1)).astype(F32)) * (1.0 / 12.0)
+
+
+def prepare(dense, slow, layers, place, depth, amplitude, t, modes_ref, contrast_ref):
     rows, cells_z = contrast_ref.shape[1:]
     points = place.shape[1]
     row_ids = lax.broadcasted_iota(jnp.int32, (rows, points), 0)
@@ -179,7 +206,7 @@
         parts = [at_lane * part for part in (one, two, amp - one - two)]
         spread.append(jnp.concatenate(parts, axis=1).astype(BF16))
     scaled = KAPPA * (slow - 1.0)
-    contrast_ref[0] = scaled - t["edge"][...]
+    contrast_ref[0] = scaled - edges(rows, cells_z, layers)
     contrast_ref[1] = DAMPING * scaled
     at_row = (row_ids == place).astype(F32).astype(BF16)
     field = lax.dot_general(
@@ -193,37 +220,46 @@
     out_ref[...] = in_ref[...]
 
 
-PREP = ("inverse", "edge", "forward", "right_z", "backward", "enter", "leave")
-BEAT = ("inverse", "forward", "right_z", "backward", "enter", "leave")
+PREP = ("inverse", "forward", "right_z")
+BEAT = ("inverse", "forward", "right_z", "later")
 FINAL = BEAT + ("first",)
-FINISH = ("right_z", "backward")
+LATER = ("later",)
+FINISH = ("right_z", "later")
 
 
 def named(names, refs):
     return dict(zip(names, refs))
 
 
-def prep_kernel(cells_x, mine_ref, slow_ref, place_ref, depth_ref, amp_ref, *refs):
-    modes_ref, contrast_ref = refs[len(PREP) :]
-    dense = [jnp.concatenate([mine_ref[c, x] for x in cells_x], axis=0) for c in range(2)]
+def prep_kernel(cells_x, right_ref, slow_ref, place_ref, depth_ref, amp_ref, *refs):
+    later_refs = refs[len(PREP) : len(PREP) + len(LATER)]
+    modes_ref, contrast_ref, *held_refs, sems = refs[len(PREP) + len(LATER) :]
+    copies = [
+        pltpu.make_async_copy(later_ref, held_ref, sems.at[n])
+        for n, (later_ref, held_ref) in enumerate(zip(later_refs, held_refs))
+    ]
+    for copy in copies:
+        copy.start()
+    dense = [jnp.concatenate([right_ref[0, c, x] for x in cells_x], axis=0) for c in range(2)]
     slow = jnp.concatenate([slow_ref[x] for x in cells_x], axis=0)
     prepare(
-        jnp.concatenate(dense, axis=1), slow, place_ref[...], depth_ref[...], amp_ref, named(PREP, refs),
+        jnp.concatenate(dense, axis=1), slow, len(cells_x), place_ref[...], depth_ref[...], amp_ref, named(PREP, refs),
         modes_ref, contrast_ref,
     )
-
-
-def prep_other_kernel(cells_x, core_ref, rhs_ref, swap_ref, slow_ref, own_modes_ref, own_contrast_ref, place_ref,
-                      depth_ref, amp_ref, *refs):
+    for copy in copies:
+        copy.wait()
+
+
+def prep_other_kernel(cells_x, core_ref, swap_ref, own_modes_ref, own_contrast_ref, place_ref, depth_ref, amp_ref,
+                      *refs):
     modes_ref, contrast_ref = refs[len(PREP) :]
-    core, rhs = core_ref[0], rhs_ref[0]
+    core = core_ref[0]
     other = 1 - core
     modes_ref[core] = own_modes_ref[...]
     contrast_ref[core] = own_contrast_ref[...]
-    dense = [jnp.concatenate([swap_ref[rhs, c, x] for x in cells_x], axis=0) for c in range(2)]
-    slow = jnp.concatenate([slow_ref[x] for x in cells_x], axis=0)
+    *dense, slow = [jnp.concatenate([swap_ref[c, x] for x in cells_x], axis=0) for c in range(3)]
     prepare(
-        jnp.concatenate(dense, axis=1), slow, place_ref[...], depth_ref[...], amp_ref, named(PREP, refs),
+        jnp.concatenate(dense, axis=1), slow, len(cells_x), place_ref[...], depth_ref[...], amp_ref, named(PREP, refs),
         modes_ref.at[other], contrast_ref.at[other],
     )
 
@@ -238,12 +274,12 @@
     @pl.when(active_ref[0] == 1)
     def _():
         trace = jnp.concatenate([trace_x_ref[...], trace_y_ref[...]], axis=0)
-        start = modes_ref[tile] + divide(left_product(t["enter"][...], trace), t)
+        start = modes_ref[tile] + divide(left_product(enter_matrix(t, 3 * trace.shape[0]), trace), t)
         total, term = solve_modes(start, contrast_ref.at[tile], t)
         new_total_ref[...] = total
         new_term_ref[...] = term
         if not (final and tile == 1):
-            out = left_product(t["leave"][...], total)
+            out = left_product(leave_matrix(t), total)
             for out_ref, part in zip(out_refs[:1] if final else out_refs, (out[:count], out[count:])):
                 out_ref[...] = part
 
@@ -261,9 +297,9 @@
 
 
 def finish_kernel(cells_x, core_ref, total0_ref, term0_ref, total1_ref, term1_ref, contrast_ref,
-                  z_ref, backward_ref, keep_ref, give_ref, both_ref):
+                  z_ref, later_ref, keep_ref, give_ref, both_ref):
     _, _, _, size_x, size_y, cells_z = both_ref.shape
-    t = named(FINISH, (z_ref, backward_ref))
+    t = named(FINISH, (z_ref, later_ref))
     for tile, (total_ref, term_ref) in enumerate(((total0_ref, term0_ref), (total1_ref, term1_ref))):
         wave, rest = [z_transform(to_cells(ref[...], t), t) for ref in (total_ref, term_ref)]
         rest = times(contrast_ref[tile, 0], contrast_ref[tile, 1], rest)
@@ -377,9 +413,8 @@
         for k in range(chips) for j in range(grid_cols) for r in range(2)
     ]
     axes = ("gx", "gy")
-    swapped = lax.ppermute(right_side, axes, own)
-    swapped_slow = lax.ppermute(slowness, axes, own)
-    mine = lax.dynamic_index_in_dim(right_side, rhs, 0, keepdims=False)
+    ordered = jnp.where(rhs == 0, right_side, right_side[::-1])
+    swapped = lax.ppermute(jnp.concatenate([ordered[1], slowness[None]], axis=0), axes, own)
 
     total_y = size_y * grid_cols
     cells = lax.dynamic_index_in_dim(source_cells, rhs, 0, keepdims=True)
@@ -394,24 +429,27 @@
 
     depth = cells % cells_z
     prep_tables = [t[name] for name in PREP]
-    own_modes, own_contrast = pl.pallas_call(
+    own_modes, own_contrast, *held = pl.pallas_call(
         functools.partial(prep_kernel, cells_x),
-        out_shape=(shaped(rows, 2 * cells_z), shaped(2, rows, cells_z)),
-        in_specs=[whole()] * (5 + len(PREP)),
-        out_specs=(whole(), whole()),
+        out_shape=(shaped(rows, 2 * cells_z), shaped(2, rows, cells_z))
+        + tuple(jax.ShapeDtypeStruct(t[name].shape, BF16) for name in LATER),
+        in_specs=[whole()] * (5 + len(PREP)) + [anywhere()] * len(LATER),
+        out_specs=(whole(),) * (2 + len(LATER)),
+        scratch_shapes=[pltpu.SemaphoreType.DMA((len(LATER),))],
         compiler_params=PARAMS,
         cost_estimate=SOLVE_COST,
         name="prep",
-    )(mine, slowness, places[0], depth, amplitudes, *prep_tables)
+    )(ordered, slowness, places[0], depth, amplitudes, *prep_tables, *[t[name] for name in LATER])
+    t.update(zip(LATER, held))
     modes, contrast = pl.pallas_call(
         functools.partial(prep_other_kernel, cells_x),
         out_shape=(shaped(2, rows, 2 * cells_z), shaped(2, 2, rows, cells_z)),
-        in_specs=[scalars()] * 2 + [whole()] * (7 + len(PREP)),
+        in_specs=[scalars()] + [whole()] * (6 + len(PREP)),
         out_specs=(whole(), whole()),
         compiler_params=PARAMS,
         cost_estimate=SOLVE_COST,
         name="prep_other",
-    )(core_ref, rhs_ref, swapped, swapped_slow, own_modes, own_contrast, places[1], depth, amplitudes, *prep_tables)
+    )(core_ref, swapped, own_modes, own_contrast, places[1], depth, amplitudes, *prep_tables)
 
     def solve(tile, active, trace_x, trace_y, state, final):
         names = FINAL if final else BEAT

time: 69.8 us -> 67 us (0.960)
  local copies, waits for them, and re-layouts: 5.86 us -> 1.14 us
  other arithmetic: 0.06 us -> 1.35 us
    unnamed x28 -> x16, local copies, waits for them, and re-layouts: 4.74 us -> 1.04 us
    select_n x0 -> x1, other arithmetic: none -> 1.27 us  [body(): ordered = jnp.where(rhs == 0, right_side, right_side[::-1])]
    squeeze x1, local copies, waits for them, and re-layouts: 1.03 us -> 0.02 us  [body(): ordered[1]]
  transfers between devices with their start and end apart: 24 -> 23, of which waited for: 4 -> 4; matrix products, arithmetic and copies ran while one was open for 2% -> 0% of each run, Pallas kernels for 12% -> 13%
where the time goes in v11:
time: 67 us; the launch traced here: 65.9 us
  waiting for transfers between devices  30.9 us (46%)
  starting transfers between devices  20.5 us (31%)
  Pallas kernels  10.5 us (16%)
  between operations  1.51 us (2%)
  other arithmetic  1.35 us (2%)
  local copies, waits for them, and re-layouts  1.14 us (2%)
    ppermute x6, waiting for transfers between devices, body(): trace_y0 = hand_on(lax.ppermute(outs0[0], axes, along_y))  26.5 us
    pallas_call x14, Pallas kernels, solve(): pl.pallas_call(functools.partial(beat_kernel, tile, final), out_shape=(sh...  5.59 us
    ppermute x6, starting transfers between devices, body(): trace_y1 = lax.ppermute(outs1[1], axes, along_y)  5.24 us
    ppermute x6, starting transfers between devices, body(): trace_y0 = hand_on(lax.ppermute(outs0[0], axes, along_y))  5.24 us
    ppermute x6, starting transfers between devices, body(): trace_x = lax.ppermute(outs1[0], axes, along_x)  4.61 us
    ppermute x1, waiting for transfers between devices, body(): lax.ppermute(edge_y, axes, between([((k, j), (k, j - 1)) for k, j in ever...  2.33 us
    ppermute x1, starting transfers between devices, body(): lax.ppermute(edge_y, axes, between([((k, j), (k, j - 1)) for k, j in ever...  1.92 us
  transfers between devices with their start and end apart: 23, of which 4 were waited for; matrix products, arithmetic and copies ran while one was open for 0% of the time, Pallas kernels for 13%

profile of v11, /device:TPU:29, one launch (start us, length us, event | category | flops | bytes accessed | tf_op | source)
XLA Modules:
  0.0 65.9 jit_solution(18325666589190524773)
XLA Ops:
  0.7 1.3 %reverse_select_fusion.right_ref = f32[2,2,16,16,128]{4,3,2,1,0:T(8,128)S(1)} fusion(f32[2,2,16,16,128]{4,3,2,1,0:T(8,128)} %param.9, pred[]{:T(512)S(6)} %eq.31), kind=kLoop, calls=%fused_computation | loop fusion | flops 131072 | bytes 1048577 | tf_op jit(solution)/shard_map/jit(_where)/select_n | solution.py:416
  2.0 0.8 %copy-done.2 = f32[16,16,128]{2,1,0:T(8,128)S(1)} copy-done((f32[16,16,128]{2,1,0:T(8,128)S(1)}, f32[16,16,128]{2,1,0:T(8,128)}, u32[]{:S(2)}) %copy-start.2) | copy-done | bytes 131096
  2.9 0.7 %collective-permute-start = (f32[3,16,16,128]{3,2,1,0:T(8,128)S(1)}, f32[3,16,16,128]{3,2,1,0:T(8,128)S(1)}, u32[]{:S(2)}, u32[]{:S(2)}) collective-permute-start(f32[3,16,16,128]{3,2,1,0:T(8,128)S(1)} %pad_maximum_fusion), channel_id=1, source_target_pairs={{0,4},{4,0},{1,5},{5,1},{2,6},{6,2},{3,7},{7,3},{8,12},{12,8},{9,1... | collective-permute-start | bytes 1179656 | tf_op jit(solution)/shard_map/ppermute | solution.py:417
  3.7 0.1 copy-done.1
  3.9 1.1 %prep.1 = (f32[256,256]{1,0:T(8,128)S(1)}, f32[2,256,128]{2,1,0:T(8,128)S(1)}, bf16[5,128,384]{2,1,0:T(8,128)(2,1)S(1)}) custom-call(f32[2,2,16,16,128]{4,3,2,1,0:T(8,128)S(1)} %reverse_select_fusion.right_ref, f32[16,16,128]{2,1,0:T(8,128)S(1)} %copy-done.2, s32[1,16]{1,0:T(1,128)S(1)} %and_select_fusion.2.place_ref, ...), custom_call_target="tpu_custom_call" | custom-call | flops 2000000000 | bytes 2000000 | tf_op jit(solution)/shard_map/prep/pallas_call | solution.py:432
  5.0 0.8 %prep_other.1 = (f32[2,256,256]{2,1,0:T(8,128)S(1)}, f32[2,2,256,128]{3,2,1,0:T(8,128)S(1)}) custom-call(s32[1]{0:T(128)} %bitcast.1.core_ref, f32[3,16,16,128]{3,2,1,0:T(8,128)S(1)} %collective-permute-done.swap_ref, f32[256,256]{1,0:T(8,128)S(1)} %get-tuple-element.65.own_modes_ref, f32[2,256,128]{2,1,0:T(8,128)S(1)} %get-tuple-element.66.own_contrast_ref, ...), custom_call_target="tpu_custom_call" | custom-call | flops 2000000000 | bytes 2000000 | tf_op jit(solution)/shard_map/prep_other/pallas_call | solution.py:444
  5.9 0.7 %collective-permute-start.2 = (f32[32,256]{1,0:T(8,128)S(1)}, f32[32,256]{1,0:T(8,128)S(1)}, u32[]{:S(2)}, u32[]{:S(2)}) collective-permute-start(f32[32,256]{1,0:T(8,128)S(1)} %get-tuple-element.72), channel_id=1, source_target_pairs={{0,5},{4,1}} | collective-permute-start | bytes 98312 | tf_op jit(solution)/shard_map/ppermute | solution.py:492
  6.6 0.1 lower.7
  6.7 0.7 %collective-permute-start.1 = (f32[32,256]{1,0:T(8,128)S(1)}, f32[32,256]{1,0:T(8,128)S(1)}, u32[]{:S(2)}, u32[]{:S(2)}) collective-permute-start(f32[32,256]{1,0:T(8,128)S(1)} %get-tuple-element.71), channel_id=1, source_target_pairs={{0,12},{4,8}} | collective-permute-start | bytes 98312 | tf_op jit(solution)/shard_map/ppermute | solution.py:495
  7.4 0.7 %collective-permute-start.3 = (f32[32,256]{1,0:T(8,128)S(1)}, f32[32,256]{1,0:T(8,128)S(1)}, u32[]{:S(2)}, u32[]{:S(2)}) collective-permute-start(f32[32,256]{1,0:T(8,128)S(1)} %get-tuple-element.76), channel_id=1, source_target_pairs={{0,5},{4,1}} | collective-permute-start | bytes 98312 | tf_op jit(solution)/shard_map/ppermute | solution.py:497
  8.1 0.1 upper.8
  8.2 0.7 %collective-permute-start.5 = (f32[32,256]{1,0:T(8,128)S(1)}, f32[32,256]{1,0:T(8,128)S(1)}, u32[]{:S(2)}, u32[]{:S(2)}) collective-permute-start(f32[32,256]{1,0:T(8,128)S(1)} %get-tuple-element.80), channel_id=1, source_target_pairs={{1,6},{5,2},{8,13},{12,9}} | collective-permute-start | bytes 98312 | tf_op jit(solution)/shard_map/ppermute | solution.py:492
  8.9 0.1 lower.8
  9.0 0.7 %collective-permute-start.4 = (f32[32,256]{1,0:T(8,128)S(1)}, f32[32,256]{1,0:T(8,128)S(1)}, u32[]{:S(2)}, u32[]{:S(2)}) collective-permute-start(f32[32,256]{1,0:T(8,128)S(1)} %get-tuple-element.79), channel_id=1, source_target_pairs={{1,13},{5,9},{8,20},{12,16}} | collective-permute-start | bytes 98312 | tf_op jit(solution)/shard_map/ppermute | solution.py:495
  9.6 0.7 %collective-permute-start.6 = (f32[32,256]{1,0:T(8,128)S(1)}, f32[32,256]{1,0:T(8,128)S(1)}, u32[]{:S(2)}, u32[]{:S(2)}) collective-permute-start(f32[32,256]{1,0:T(8,128)S(1)} %get-tuple-element.84), channel_id=1, source_target_pairs={{1,6},{5,2},{8,13},{12,9}} | collective-permute-start | bytes 98312 | tf_op jit(solution)/shard_map/ppermute | solution.py:497
  10.3 0.1 upper.9
  10.4 0.7 %collective-permute-start.8 = (f32[32,256]{1,0:T(8,128)S(1)}, f32[32,256]{1,0:T(8,128)S(1)}, u32[]{:S(2)}, u32[]{:S(2)}) collective-permute-start(f32[32,256]{1,0:T(8,128)S(1)} %get-tuple-element.88), channel_id=1, source_target_pairs={{2,7},{6,3},{9,14},{13,10},{16,21},{20,17}} | collective-permute-start | bytes 98312 | tf_op jit(solution)/shard_map/ppermute | solution.py:492
  11.1 0.1 lower.9
  11.2 0.7 %collective-permute-start.7 = (f32[32,256]{1,0:T(8,128)S(1)}, f32[32,256]{1,0:T(8,128)S(1)}, u32[]{:S(2)}, u32[]{:S(2)}) collective-permute-start(f32[32,256]{1,0:T(8,128)S(1)} %get-tuple-element.87), channel_id=1, source_target_pairs={{2,14},{6,10},{9,21},{13,17},{16,28},{20,24}} | collective-permute-start | bytes 98312 | tf_op jit(solution)/shard_map/ppermute | solution.py:495
  11.9 0.7 %collective-permute-start.9 = (f32[32,256]{1,0:T(8,128)S(1)}, f32[32,256]{1,0:T(8,128)S(1)}, u32[]{:S(2)}, u32[]{:S(2)}) collective-permute-start(f32[32,256]{1,0:T(8,128)S(1)} %get-tuple-element.92), channel_id=1, source_target_pairs={{2,7},{6,3},{9,14},{13,10},{16,21},{20,17}} | collective-permute-start | bytes 98312 | tf_op jit(solution)/shard_map/ppermute | solution.py:497
  12.6 0.1 upper.10
  12.6 0.7 %collective-permute-start.11 = (f32[32,256]{1,0:T(8,128)S(1)}, f32[32,256]{1,0:T(8,128)S(1)}, u32[]{:S(2)}, u32[]{:S(2)}) collective-permute-start(f32[32,256]{1,0:T(8,128)S(1)} %get-tuple-element.96), channel_id=1, source_target_pairs={{10,15},{14,11},{17,22},{21,18},{24,29},{28,25}} | collective-permute-start | bytes 98312 | tf_op jit(solution)/shard_map/ppermute | solution.py:492
  13.3 0.3 lower.10
  13.6 0.7 %collective-permute-start.10 = (f32[32,256]{1,0:T(8,128)S(1)}, f32[32,256]{1,0:T(8,128)S(1)}, u32[]{:S(2)}, u32[]{:S(2)}) collective-permute-start(f32[32,256]{1,0:T(8,128)S(1)} %get-tuple-element.95), channel_id=1, source_target_pairs={{3,15},{7,11},{10,22},{14,18},{17,29},{21,25}} | collective-permute-start | bytes 98312 | tf_op jit(solution)/shard_map/ppermute | solution.py:495
  14.3 0.7 %collective-permute-start.12 = (f32[32,256]{1,0:T(8,128)S(1)}, f32[32,256]{1,0:T(8,128)S(1)}, u32[]{:S(2)}, u32[]{:S(2)}) collective-permute-start(f32[32,256]{1,0:T(8,128)S(1)} %get-tuple-element.100), channel_id=1, source_target_pairs={{10,15},{14,11},{17,22},{21,18},{24,29},{28,25}} | collective-permute-start | bytes 98312 | tf_op jit(solution)/shard_map/ppermute | solution.py:497
  15.0 0.1 upper.11
  15.1 1.3 %collective-permute-start.14 = (f32[32,256]{1,0:T(8,128)S(1)}, f32[32,256]{1,0:T(8,128)S(1)}, u32[]{:S(2)}, u32[]{:S(2)}) collective-permute-start(f32[32,256]{1,0:T(8,128)S(1)} %get-tuple-element.104), channel_id=1, source_target_pairs={{18,23},{22,19},{25,30},{29,26}} | collective-permute-start | bytes 98312 | tf_op jit(solution)/shard_map/ppermute | solution.py:492
  16.4 1.3 %collective-permute-start.13 = (f32[32,256]{1,0:T(8,128)S(1)}, f32[32,256]{1,0:T(8,128)S(1)}, u32[]{:S(2)}, u32[]{:S(2)}) collective-permute-start(f32[32,256]{1,0:T(8,128)S(1)} %get-tuple-element.103), channel_id=1, source_target_pairs={{11,23},{15,19},{18,30},{22,26}} | collective-permute-start | bytes 98312 | tf_op jit(solution)/shard_map/ppermute | solution.py:495
  17.7 1.3 %collective-permute-start.15 = (f32[32,256]{1,0:T(8,128)S(1)}, f32[32,256]{1,0:T(8,128)S(1)}, u32[]{:S(2)}, u32[]{:S(2)}) collective-permute-start(f32[32,256]{1,0:T(8,128)S(1)} %get-tuple-element.108), channel_id=1, source_target_pairs={{18,23},{22,19},{25,30},{29,26}} | collective-permute-start | bytes 98312 | tf_op jit(solution)/shard_map/ppermute | solution.py:497
  19.0 26.5 %collective-permute-done.14.in_ref = f32[32,256]{1,0:T(8,128)S(1)} collective-permute-done((f32[32,256]{1,0:T(8,128)S(1)}, f32[32,256]{1,0:T(8,128)S(1)}, u32[]{:S(2)}, u32[]{:S(2)}) %collective-permute-start.14) | collective-permute-done | bytes 32800 | tf_op jit(solution)/shard_map/ppermute | solution.py:492
  45.6 1.3 %collective-permute-done.13.trace_x_ref = f32[32,256]{1,0:T(8,128)S(1)} collective-permute-done((f32[32,256]{1,0:T(8,128)S(1)}, f32[32,256]{1,0:T(8,128)S(1)}, u32[]{:S(2)}, u32[]{:S(2)}) %collective-permute-start.13) | collective-permute-done | bytes 32800 | tf_op jit(solution)/shard_map/ppermute | solution.py:495
  46.9 2.1 %upper.12 = (f32[256,256]{1,0:T(8,128)S(1)}, f32[256,256]{1,0:T(8,128)S(1)}, f32[32,256]{1,0:T(8,128)S(1)}, f32[32,256]{1,0:T(8,128)S(1)}) custom-call(s32[1]{0:T(128)} %bitcast.9.active_ref, f32[2,256,256]{2,1,0:T(8,128)S(1)} %get-tuple-element.67.modes_ref, ...), custom_call_target="tpu_custom_call", output_to_operand_aliasing={{0}: (5, {}), {1}: (6, {})} | custom-call | flops 2000000000 | bytes 2000000 | tf_op jit(solution)/shard_map/upper/pallas_call | solution.py:458
  48.9 1.3 %collective-permute-start.17 = (f32[32,256]{1,0:T(8,128)S(1)}, f32[32,256]{1,0:T(8,128)S(1)}, u32[]{:S(2)}, u32[]{:S(2)}) collective-permute-start(f32[32,256]{1,0:T(8,128)S(1)} %get-tuple-element.112), channel_id=1, source_target_pairs={{26,31},{30,27}} | collective-permute-start | bytes 98312 | tf_op jit(solution)/shard_map/ppermute | solution.py:492
  50.3 2.1 %lower.12 = (f32[256,256]{1,0:T(8,128)S(1)}, f32[256,256]{1,0:T(8,128)S(1)}, f32[32,256]{1,0:T(8,128)S(1)}, f32[32,256]{1,0:T(8,128)S(1)}) custom-call(s32[1]{0:T(128)} %bitcast.9.active_ref, f32[2,256,256]{2,1,0:T(8,128)S(1)} %get-tuple-element.67.modes_ref, ...), custom_call_target="tpu_custom_call", output_to_operand_aliasing={{0}: (5, {}), {1}: (6, {})} | custom-call | flops 2000000000 | bytes 2000000 | tf_op jit(solution)/shard_map/lower/pallas_call | solution.py:458
  52.3 0.7 %collective-permute-start.16 = (f32[32,256]{1,0:T(8,128)S(1)}, f32[32,256]{1,0:T(8,128)S(1)}, u32[]{:S(2)}, u32[]{:S(2)}) collective-permute-start(f32[32,256]{1,0:T(8,128)S(1)} %get-tuple-element.111), channel_id=1, source_target_pairs={{19,31},{23,27}} | collective-permute-start | bytes 98312 | tf_op jit(solution)/shard_map/ppermute | solution.py:495
  53.0 1.3 %collective-permute-start.18 = (f32[32,256]{1,0:T(8,128)S(1)}, f32[32,256]{1,0:T(8,128)S(1)}, u32[]{:S(2)}, u32[]{:S(2)}) collective-permute-start(f32[32,256]{1,0:T(8,128)S(1)} %get-tuple-element.118), channel_id=1, source_target_pairs={{26,31},{30,27}} | collective-permute-start | bytes 98312 | tf_op jit(solution)/shard_map/ppermute | solution.py:497
  54.4 0.3 upper.13
  54.7 0.7 %collective-permute-done.18.trace_y_ref = f32[32,256]{1,0:T(8,128)S(1)} collective-permute-done((f32[32,256]{1,0:T(8,128)S(1)}, f32[32,256]{1,0:T(8,128)S(1)}, u32[]{:S(2)}, u32[]{:S(2)}) %collective-permute-start.18) | collective-permute-done | bytes 32800 | tf_op jit(solution)/shard_map/ppermute | solution.py:497
  55.3 0.3 lower.13
  55.6 1.9 %collective-permute-start.21 = (f32[2,32,256]{2,1,0:T(8,128)S(1)}, f32[2,32,256]{2,1,0:T(8,128)S(1)}, u32[]{:S(2)}, u32[]{:S(2)}) collective-permute-start(f32[2,32,256]{2,1,0:T(8,128)S(1)} %pad_maximum_fusion.1), channel_id=1, source_target_pairs={{1,4},{5,0},{2,5},{6,1},{3,6},{7,2},{9,12},{13,8},{10,13},{14,9},{... | collective-permute-start | bytes 196616 | tf_op jit(solution)/shard_map/ppermute | solution.py:503
  57.5 1.3 %collective-permute-start.20 = (f32[32,256]{1,0:T(8,128)S(1)}, f32[32,256]{1,0:T(8,128)S(1)}, u32[]{:S(2)}, u32[]{:S(2)}) collective-permute-start(f32[32,256]{1,0:T(8,128)S(1)} %get-tuple-element.125), channel_id=1, source_target_pairs={{8,4},{12,0},{9,5},{13,1},{10,6},{14,2},{11,7},{15,3},{16,12},{20,... | collective-permute-start | bytes 98312 | tf_op jit(solution)/shard_map/ppermute | solution.py:502
  58.8 1.1 %finish.1 = (f32[2,2,16,16,128]{4,3,2,1,0:T(8,128)S(1)}, f32[2,2,16,16,128]{4,3,2,1,0:T(8,128)S(1)}) custom-call(s32[1]{0:T(128)} %bitcast.1.core_ref, f32[256,256]{1,0:T(8,128)S(1)} %get-tuple-element.115.total0_ref, f32[256,256]{1,0:T(8,128)S(1)} %get-tuple-element.116.term0_ref, f32[256,256]{1,0:T(8,128)S(1)} %get-tuple-element.121.total1_ref, ...), custom_call_target="tpu_custom_call" | custom-call | tf_op jit(solution)/shard_map/finish/pallas_call | solution.py:506
  60.0 1.0 %collective-permute-start.19 = (f32[2,2,16,16,128]{4,3,2,1,0:T(8,128)S(1)}, f32[2,2,16,16,128]{4,3,2,1,0:T(8,128)S(1)}, u32[]{:S(2)}, u32[]{:S(2)}) collective-permute-start(f32[2,2,16,16,128]{4,3,2,1,0:T(8,128)S(1)} %get-tuple-element.124), channel_id=1, source_target_pairs={{0,4},{4,0},{1,5},{5,1},{2,6},{6,2},{3,7},{7,3},{8,12},{12,8},{9,1... | collective-permute-start | bytes 1572872 | tf_op jit(solution)/shard_map/ppermute | solution.py:515
  61.0 2.3 %collective-permute-done.21.edge_y_ref = f32[2,32,256]{2,1,0:T(8,128)S(1)} collective-permute-done((f32[2,32,256]{2,1,0:T(8,128)S(1)}, f32[2,32,256]{2,1,0:T(8,128)S(1)}, u32[]{:S(2)}, u32[]{:S(2)}) %collective-permute-start.21) | collective-permute-done | bytes 65568 | tf_op jit(solution)/shard_map/ppermute | solution.py:503
  63.4 0.5 collective-permute-start.22
  63.8 0.2 keep.1.keep_rest_ref
  64.0 0.8 %place_wave.1 = f32[2,2,16,16,128]{4,3,2,1,0:T(8,128)} custom-call(s32[1]{0:T(128)} %bitcast.rhs_ref, f32[2,2,16,16,128]{4,3,2,1,0:T(8,128)S(1)} %get-tuple-element.123.keep_ref, f32[2,2,16,16,128]{4,3,2,1,0:T(8,128)S(1)} %collective-permute-done.19.got_ref), custom_call_target="tpu_custom_call" | custom-call | flops 10000000000 | bytes 1000000 | tf_op jit(solution)/shard_map/place_wave/pallas_call | solution.py:528
  64.8 0.9 %place_rest.1 = f32[2,2,16,16,128]{4,3,2,1,0:T(8,128)} custom-call(s32[1]{0:T(128)} %bitcast.1.core_ref, s32[1]{0:T(128)} %bitcast.rhs_ref, f32[2,16,16,128]{3,2,1,0:T(8,128)S(1)} %keep.1.keep_rest_ref, f32[2,2,16,16,128]{4,3,2,1,0:T(8,128)S(1)} %collective-permute-done.19.got_ref, f32[64,256]{1,0:T(8,128)S(1)} %collective-permute-done.22.got_edge_ref, ...), custom_call_target="tpu_custom_call" | custom-call | tf_op jit(solution)/shard_map/place_rest/pallas_call | solution.py:538
  (55 shorter events, 0.5 us)
Async XLA Ops:
  0.6 3.0 %copy-start = (f32[2,16,2]{1,2,0:T(2,128)S(1)}, f32[2,16,2]{1,2,0:T(2,128)}, u32[]{:S(2)}) copy-start(f32[2,16,2]{1,2,0:T(2,128)} %param.12) | copy-start | bytes 772
  2.0 0.9 %copy-start.2 = (f32[16,16,128]{2,1,0:T(8,128)S(1)}, f32[16,16,128]{2,1,0:T(8,128)}, u32[]{:S(2)}) copy-start(f32[16,16,128]{2,1,0:T(8,128)} %slow_ref.1) | copy-start | bytes 393220
  2.0 1.7 %copy-start.7 = (s32[2,16]{1,0:T(2,128)S(1)}, s32[2,16]{1,0:T(2,128)}, u32[]{:S(2)}) copy-start(s32[2,16]{1,0:T(2,128)} %param.11) | copy-start | bytes 388
  2.0 1.7 %copy-start.4 = (f32[2,256,128]{2,1,0:T(8,128)S(1)}, f32[2,256,128]{2,1,0:T(8,128)}, u32[]{:S(2)}) copy-start(f32[2,256,128]{2,1,0:T(8,128)} %constant.145.clone.refs_0_) | copy-start | bytes 786436
  2.0 1.7 %copy-start.3 = (bf16[5,128,384]{2,1,0:T(8,128)(2,1)S(1)}, bf16[5,128,384]{2,1,0:T(8,128)(2,1)}, u32[]{:S(2)}) copy-start(bf16[5,128,384]{2,1,0:T(8,128)(2,1)} %constant.149.clone.refs_3_) | copy-start | bytes 1474564
  2.9 1.0 %copy-start.1 = (bf16[256,256]{1,0:T(8,128)(2,1)S(1)}, bf16[256,256]{1,0:T(8,128)(2,1)}, u32[]{:S(2)}) copy-start(bf16[256,256]{1,0:T(8,128)(2,1)} %constant.147.clone.refs_2_.z_ref) | copy-start | bytes 393220
  2.9 1.0 %copy-start.5 = (bf16[2,128,384]{2,1,0:T(8,128)(2,1)S(1)}, bf16[2,128,384]{2,1,0:T(8,128)(2,1)}, u32[]{:S(2)}) copy-start(bf16[2,128,384]{2,1,0:T(8,128)(2,1)} %constant.146.clone.refs_1_) | copy-start | bytes 589828
  2.9 2.1 %collective-permute-start = (f32[3,16,16,128]{3,2,1,0:T(8,128)S(1)}, f32[3,16,16,128]{3,2,1,0:T(8,128)S(1)}, u32[]{:S(2)}, u32[]{:S(2)}) collective-permute-start(f32[3,16,16,128]{3,2,1,0:T(8,128)S(1)} %pad_maximum_fusion), channel_id=1, source_target_pairs={{0,4},{4,0},{1,5},{5,1},{2,6},{6,2},{3,7},{7,3},{8,12},{12,8},{9,1... | collective-permute-start | bytes 1179656 | tf_op jit(solution)/shard_map/ppermute | solution.py:417
  5.9 2.2 %collective-permute-start.2 = (f32[32,256]{1,0:T(8,128)S(1)}, f32[32,256]{1,0:T(8,128)S(1)}, u32[]{:S(2)}, u32[]{:S(2)}) collective-permute-start(f32[32,256]{1,0:T(8,128)S(1)} %get-tuple-element.72), channel_id=1, source_target_pairs={{0,5},{4,1}} | collective-permute-start | bytes 98312 | tf_op jit(solution)/shard_map/ppermute | solution.py:492
  6.7 1.4 %collective-permute-start.1 = (f32[32,256]{1,0:T(8,128)S(1)}, f32[32,256]{1,0:T(8,128)S(1)}, u32[]{:S(2)}, u32[]{:S(2)}) collective-permute-start(f32[32,256]{1,0:T(8,128)S(1)} %get-tuple-element.71), channel_id=1, source_target_pairs={{0,12},{4,8}} | collective-permute-start | bytes 98312 | tf_op jit(solution)/shard_map/ppermute | solution.py:495
  7.4 1.5 %collective-permute-start.3 = (f32[32,256]{1,0:T(8,128)S(1)}, f32[32,256]{1,0:T(8,128)S(1)}, u32[]{:S(2)}, u32[]{:S(2)}) collective-permute-start(f32[32,256]{1,0:T(8,128)S(1)} %get-tuple-element.76), channel_id=1, source_target_pairs={{0,5},{4,1}} | collective-permute-start | bytes 98312 | tf_op jit(solution)/shard_map/ppermute | solution.py:497
  8.2 2.1 %collective-permute-start.5 = (f32[32,256]{1,0:T(8,128)S(1)}, f32[32,256]{1,0:T(8,128)S(1)}, u32[]{:S(2)}, u32[]{:S(2)}) collective-permute-start(f32[32,256]{1,0:T(8,128)S(1)} %get-tuple-element.80), channel_id=1, source_target_pairs={{1,6},{5,2},{8,13},{12,9}} | collective-permute-start | bytes 98312 | tf_op jit(solution)/shard_map/ppermute | solution.py:492
  9.0 1.4 %collective-permute-start.4 = (f32[32,256]{1,0:T(8,128)S(1)}, f32[32,256]{1,0:T(8,128)S(1)}, u32[]{:S(2)}, u32[]{:S(2)}) collective-permute-start(f32[32,256]{1,0:T(8,128)S(1)} %get-tuple-element.79), channel_id=1, source_target_pairs={{1,13},{5,9},{8,20},{12,16}} | collective-permute-start | bytes 98312 | tf_op jit(solution)/shard_map/ppermute | solution.py:495
  9.6 1.5 %collective-permute-start.6 = (f32[32,256]{1,0:T(8,128)S(1)}, f32[32,256]{1,0:T(8,128)S(1)}, u32[]{:S(2)}, u32[]{:S(2)}) collective-permute-start(f32[32,256]{1,0:T(8,128)S(1)} %get-tuple-element.84), channel_id=1, source_target_pairs={{1,6},{5,2},{8,13},{12,9}} | collective-permute-start | bytes 98312 | tf_op jit(solution)/shard_map/ppermute | solution.py:497
  10.4 2.1 %collective-permute-start.8 = (f32[32,256]{1,0:T(8,128)S(1)}, f32[32,256]{1,0:T(8,128)S(1)}, u32[]{:S(2)}, u32[]{:S(2)}) collective-permute-start(f32[32,256]{1,0:T(8,128)S(1)} %get-tuple-element.88), channel_id=1, source_target_pairs={{2,7},{6,3},{9,14},{13,10},{16,21},{20,17}} | collective-permute-start | bytes 98312 | tf_op jit(solution)/shard_map/ppermute | solution.py:492
  11.2 1.4 %collective-permute-start.7 = (f32[32,256]{1,0:T(8,128)S(1)}, f32[32,256]{1,0:T(8,128)S(1)}, u32[]{:S(2)}, u32[]{:S(2)}) collective-permute-start(f32[32,256]{1,0:T(8,128)S(1)} %get-tuple-element.87), channel_id=1, source_target_pairs={{2,14},{6,10},{9,21},{13,17},{16,28},{20,24}} | collective-permute-start | bytes 98312 | tf_op jit(solution)/shard_map/ppermute | solution.py:495
  11.9 1.5 %collective-permute-start.9 = (f32[32,256]{1,0:T(8,128)S(1)}, f32[32,256]{1,0:T(8,128)S(1)}, u32[]{:S(2)}, u32[]{:S(2)}) collective-permute-start(f32[32,256]{1,0:T(8,128)S(1)} %get-tuple-element.92), channel_id=1, source_target_pairs={{2,7},{6,3},{9,14},{13,10},{16,21},{20,17}} | collective-permute-start | bytes 98312 | tf_op jit(solution)/shard_map/ppermute | solution.py:497
  12.6 2.3 %collective-permute-start.11 = (f32[32,256]{1,0:T(8,128)S(1)}, f32[32,256]{1,0:T(8,128)S(1)}, u32[]{:S(2)}, u32[]{:S(2)}) collective-permute-start(f32[32,256]{1,0:T(8,128)S(1)} %get-tuple-element.96), channel_id=1, source_target_pairs={{10,15},{14,11},{17,22},{21,18},{24,29},{28,25}} | collective-permute-start | bytes 98312 | tf_op jit(solution)/shard_map/ppermute | solution.py:492
  13.6 1.4 %collective-permute-start.10 = (f32[32,256]{1,0:T(8,128)S(1)}, f32[32,256]{1,0:T(8,128)S(1)}, u32[]{:S(2)}, u32[]{:S(2)}) collective-permute-start(f32[32,256]{1,0:T(8,128)S(1)} %get-tuple-element.95), channel_id=1, source_target_pairs={{3,15},{7,11},{10,22},{14,18},{17,29},{21,25}} | collective-permute-start | bytes 98312 | tf_op jit(solution)/shard_map/ppermute | solution.py:495
  14.3 2.1 %collective-permute-start.12 = (f32[32,256]{1,0:T(8,128)S(1)}, f32[32,256]{1,0:T(8,128)S(1)}, u32[]{:S(2)}, u32[]{:S(2)}) collective-permute-start(f32[32,256]{1,0:T(8,128)S(1)} %get-tuple-element.100), channel_id=1, source_target_pairs={{10,15},{14,11},{17,22},{21,18},{24,29},{28,25}} | collective-permute-start | bytes 98312 | tf_op jit(solution)/shard_map/ppermute | solution.py:497
  15.1 30.5 %collective-permute-start.14 = (f32[32,256]{1,0:T(8,128)S(1)}, f32[32,256]{1,0:T(8,128)S(1)}, u32[]{:S(2)}, u32[]{:S(2)}) collective-permute-start(f32[32,256]{1,0:T(8,128)S(1)} %get-tuple-element.104), channel_id=1, source_target_pairs={{18,23},{22,19},{25,30},{29,26}} | collective-permute-start | bytes 98312 | tf_op jit(solution)/shard_map/ppermute | solution.py:492
  16.4 30.4 %collective-permute-start.13 = (f32[32,256]{1,0:T(8,128)S(1)}, f32[32,256]{1,0:T(8,128)S(1)}, u32[]{:S(2)}, u32[]{:S(2)}) collective-permute-start(f32[32,256]{1,0:T(8,128)S(1)} %get-tuple-element.103), channel_id=1, source_target_pairs={{11,23},{15,19},{18,30},{22,26}} | collective-permute-start | bytes 98312 | tf_op jit(solution)/shard_map/ppermute | solution.py:495
  17.7 32.5 %collective-permute-start.15 = (f32[32,256]{1,0:T(8,128)S(1)}, f32[32,256]{1,0:T(8,128)S(1)}, u32[]{:S(2)}, u32[]{:S(2)}) collective-permute-start(f32[32,256]{1,0:T(8,128)S(1)} %get-tuple-element.108), channel_id=1, source_target_pairs={{18,23},{22,19},{25,30},{29,26}} | collective-permute-start | bytes 98312 | tf_op jit(solution)/shard_map/ppermute | solution.py:497
  48.9 5.4 %collective-permute-start.17 = (f32[32,256]{1,0:T(8,128)S(1)}, f32[32,256]{1,0:T(8,128)S(1)}, u32[]{:S(2)}, u32[]{:S(2)}) collective-permute-start(f32[32,256]{1,0:T(8,128)S(1)} %get-tuple-element.112), channel_id=1, source_target_pairs={{26,31},{30,27}} | collective-permute-start | bytes 98312 | tf_op jit(solution)/shard_map/ppermute | solution.py:492
  50.3 4.1 %copy-start.6 = (bf16[64,768]{1,0:T(8,128)(2,1)S(1)}, bf16[64,768]{1,0:T(8,128)(2,1)}, u32[]{:S(2)}) copy-start(bf16[64,768]{1,0:T(8,128)(2,1)} %constant.148.clone.refs_4_) | copy-start | bytes 294916
  52.3 2.0 %collective-permute-start.16 = (f32[32,256]{1,0:T(8,128)S(1)}, f32[32,256]{1,0:T(8,128)S(1)}, u32[]{:S(2)}, u32[]{:S(2)}) collective-permute-start(f32[32,256]{1,0:T(8,128)S(1)} %get-tuple-element.111), channel_id=1, source_target_pairs={{19,31},{23,27}} | collective-permute-start | bytes 98312 | tf_op jit(solution)/shard_map/ppermute | solution.py:495
  53.0 2.3 %collective-permute-start.18 = (f32[32,256]{1,0:T(8,128)S(1)}, f32[32,256]{1,0:T(8,128)S(1)}, u32[]{:S(2)}, u32[]{:S(2)}) collective-permute-start(f32[32,256]{1,0:T(8,128)S(1)} %get-tuple-element.118), channel_id=1, source_target_pairs={{26,31},{30,27}} | collective-permute-start | bytes 98312 | tf_op jit(solution)/shard_map/ppermute | solution.py:497
  55.6 7.7 %collective-permute-start.21 = (f32[2,32,256]{2,1,0:T(8,128)S(1)}, f32[2,32,256]{2,1,0:T(8,128)S(1)}, u32[]{:S(2)}, u32[]{:S(2)}) collective-permute-start(f32[2,32,256]{2,1,0:T(8,128)S(1)} %pad_maximum_fusion.1), channel_id=1, source_target_pairs={{1,4},{5,0},{2,5},{6,1},{3,6},{7,2},{9,12},{13,8},{10,13},{14,9},{... | collective-permute-start | bytes 196616 | tf_op jit(solution)/shard_map/ppermute | solution.py:503
  57.5 5.8 %collective-permute-start.20 = (f32[32,256]{1,0:T(8,128)S(1)}, f32[32,256]{1,0:T(8,128)S(1)}, u32[]{:S(2)}, u32[]{:S(2)}) collective-permute-start(f32[32,256]{1,0:T(8,128)S(1)} %get-tuple-element.125), channel_id=1, source_target_pairs={{8,4},{12,0},{9,5},{13,1},{10,6},{14,2},{11,7},{15,3},{16,12},{20,... | collective-permute-start | bytes 98312 | tf_op jit(solution)/shard_map/ppermute | solution.py:502
  60.0 4.0 %collective-permute-start.19 = (f32[2,2,16,16,128]{4,3,2,1,0:T(8,128)S(1)}, f32[2,2,16,16,128]{4,3,2,1,0:T(8,128)S(1)}, u32[]{:S(2)}, u32[]{:S(2)}) collective-permute-start(f32[2,2,16,16,128]{4,3,2,1,0:T(8,128)S(1)} %get-tuple-element.124), channel_id=1, source_target_pairs={{0,4},{4,0},{1,5},{5,1},{2,6},{6,2},{3,7},{7,3},{8,12},{12,8},{9,1... | collective-permute-start | bytes 1572872 | tf_op jit(solution)/shard_map/ppermute | solution.py:515
  63.4 1.5 %collective-permute-start.22 = (f32[64,256]{1,0:T(8,128)S(1)}, f32[64,256]{1,0:T(8,128)S(1)}, u32[]{:S(2)}, u32[]{:S(2)}) collective-permute-start(f32[64,256]{1,0:T(8,128)S(1)} %pad_maximum_fusion.2), channel_id=1, source_target_pairs={{0,4},{4,0},{1,5},{5,1},{2,6},{6,2},{3,7},{7,3},{8,12},{12,8},{9,1... | collective-permute-start | bytes 196616 | tf_op jit(solution)/shard_map/ppermute | solution.py:518

commit v12 on v11

--- a/solution.py
+++ b/solution.py
@@ -47,6 +47,12 @@
     return np.stack(pieces)
 
 
+def z_matrix(t, depth):
+    rows = t["onward"].shape[1]
+    pieces = [t["onward"][2 + n, :, :depth] for n in range(-(-depth // rows))]
+    return jnp.concatenate(pieces, axis=0)
+
+
 def enter_matrix(t, depth):
     return jnp.concatenate([t["later"][2, :, :depth], t["later"][3, :, :depth]], axis=0)
 
@@ -73,8 +79,6 @@
         + (2.0 - 2.0 * np.cos(angle_z))[None, None, :]
         - KAPPA
     ).reshape(size_x * size_y, cells_z)
-    denominator = real_part**2 + (KAPPA * DAMPING) ** 2
-    inverse = np.stack([real_part / denominator, KAPPA * DAMPING / denominator]).astype(np.float32)
 
     parity = [np.kron(sine_x[order[p * half : (p + 1) * half]][:, :half], sine_y) for p in (0, 1)]
     forward = [left_factor(m) for m in parity]
@@ -109,10 +113,12 @@
             axis=1,
         ).T
     )
+    assert 2 * cells_z % (half * size_y) == 0 and 2 * cells_z <= forward[0].shape[1]
     assert enter.shape[0] == 2 * half * size_y and enter.shape[1] <= forward[0].shape[1]
     assert 2 * leave.shape[0] == half * size_y and leave.shape[1] == 2 * forward[0].shape[1]
     return dict(
-        inverse=inverse, forward=np.stack(forward), right_z=right_z, first=first,
+        symbol=real_part.astype(np.float32), first=first,
+        onward=slabs(forward + [right_z], half * size_y, forward[0].shape[1]),
         later=slabs(backward + [enter, leave], half * size_y, forward[0].shape[1]),
     ), tuple(int(x) for x in cells)
 
@@ -139,7 +145,7 @@
     rows = field.shape[0]
     cells_z = field.shape[1] // 2
     high, low = split(jnp.concatenate([field[:, :cells_z], field[:, cells_z:]], axis=0))
-    both = jnp.dot(jnp.concatenate([high, low], axis=1), t["right_z"][...], preferred_element_type=F32)
+    both = jnp.dot(jnp.concatenate([high, low], axis=1), z_matrix(t, 2 * cells_z), preferred_element_type=F32)
     total = both[:, :cells_z] + both[:, cells_z:]
     return jnp.concatenate([total[:rows], total[rows:]], axis=1)
 
@@ -148,7 +154,7 @@
     count = field.shape[0] // 2
     first, second = field[:count], field[count:]
     return jnp.concatenate(
-        [left_product(t["forward"][0], first + second), left_product(t["forward"][1], first - second)], axis=0
+        [left_product(t["onward"][0], first + second), left_product(t["onward"][1], first - second)], axis=0
     )
 
 
@@ -220,11 +226,12 @@
     out_ref[...] = in_ref[...]
 
 
-PREP = ("inverse", "forward", "right_z")
-BEAT = ("inverse", "forward", "right_z", "later")
+PREP = ("symbol", "onward")
+PREP_OTHER = ("inverse", "onward")
+BEAT = ("inverse", "onward", "later")
 FINAL = BEAT + ("first",)
 LATER = ("later",)
-FINISH = ("right_z", "later")
+FINISH = ("onward", "later")
 
 
 def named(names, refs):
@@ -233,33 +240,41 @@
 
 def prep_kernel(cells_x, right_ref, slow_ref, place_ref, depth_ref, amp_ref, *refs):
     later_refs = refs[len(PREP) : len(PREP) + len(LATER)]
-    modes_ref, contrast_ref, *held_refs, sems = refs[len(PREP) + len(LATER) :]
+    modes_ref, contrast_ref, inverse_ref, *held_refs, sems = refs[len(PREP) + len(LATER) :]
     copies = [
         pltpu.make_async_copy(later_ref, held_ref, sems.at[n])
         for n, (later_ref, held_ref) in enumerate(zip(later_refs, held_refs))
     ]
     for copy in copies:
         copy.start()
-    dense = [jnp.concatenate([right_ref[0, c, x] for x in cells_x], axis=0) for c in range(2)]
+    t = named(PREP, refs)
+    symbol = t["symbol"][...]
+    damping = KAPPA * DAMPING
+    scale = 1.0 / (symbol * symbol + damping * damping)
+    inverse_ref[0] = symbol * scale
+    inverse_ref[1] = damping * scale
+    t["inverse"] = inverse_ref
+    dense = [jnp.concatenate([right_ref[c, x] for x in cells_x], axis=0) for c in range(2)]
     slow = jnp.concatenate([slow_ref[x] for x in cells_x], axis=0)
     prepare(
-        jnp.concatenate(dense, axis=1), slow, len(cells_x), place_ref[...], depth_ref[...], amp_ref, named(PREP, refs),
+        jnp.concatenate(dense, axis=1), slow, len(cells_x), place_ref[...], depth_ref[...], amp_ref, t,
         modes_ref, contrast_ref,
     )
     for copy in copies:
         copy.wait()
 
 
-def prep_other_kernel(cells_x, core_ref, swap_ref, own_modes_ref, own_contrast_ref, place_ref, depth_ref, amp_ref,
+def prep_other_kernel(cells_x, core_ref, rhs_ref, swap_ref, slow_ref, own_modes_ref, own_contrast_ref, place_ref, depth_ref, amp_ref,
                       *refs):
-    modes_ref, contrast_ref = refs[len(PREP) :]
+    modes_ref, contrast_ref = refs[len(PREP_OTHER) :]
     core = core_ref[0]
     other = 1 - core
     modes_ref[core] = own_modes_ref[...]
     contrast_ref[core] = own_contrast_ref[...]
-    *dense, slow = [jnp.concatenate([swap_ref[c, x] for x in cells_x], axis=0) for c in range(3)]
+    dense = [jnp.concatenate([swap_ref[c, x] for x in cells_x], axis=0) for c in range(2)]
+    slow = jnp.concatenate([slow_ref[x] for x in cells_x], axis=0)
     prepare(
-        jnp.concatenate(dense, axis=1), slow, len(cells_x), place_ref[...], depth_ref[...], amp_ref, named(PREP, refs),
+        jnp.concatenate(dense, axis=1), slow, len(cells_x), place_ref[...], depth_ref[...], amp_ref, named(PREP_OTHER, refs),
         modes_ref.at[other], contrast_ref.at[other],
     )
 
@@ -336,7 +351,7 @@
     rest_ref[...] = keep_ref[1]
     count = edge_x_ref.shape[0]
     edges = jnp.concatenate([edge_x_ref[...], edge_y_ref[core_ref[0]]], axis=0)
-    edges = z_transform(edges, dict(right_z=z_ref))
+    edges = z_transform(edges, dict(onward=z_ref))
     add_later(rest_ref, edges[:count], edges[count:], (core_ref[0] == 1).astype(F32))
 
 
@@ -358,7 +373,7 @@
     copies = [pltpu.make_async_copy(keep_rest_ref, rest_ref.at[rhs], sems.at[0])]
     copies[0].start()
     work_ref[...] = got_ref[1]
-    edges = z_transform(got_edge_ref[...], dict(right_z=z_ref))
+    edges = z_transform(got_edge_ref[...], dict(onward=z_ref))
     add_later(work_ref, edges[:count], edges[count:], (core_ref[0] == 1).astype(F32))
     copies.append(pltpu.make_async_copy(work_ref, rest_ref.at[1 - rhs], sems.at[1]))
     copies[1].start()
@@ -413,8 +428,10 @@
         for k in range(chips) for j in range(grid_cols) for r in range(2)
     ]
     axes = ("gx", "gy")
-    ordered = jnp.where(rhs == 0, right_side, right_side[::-1])
-    swapped = lax.ppermute(jnp.concatenate([ordered[1], slowness[None]], axis=0), axes, own)
+    other = lax.dynamic_index_in_dim(right_side, 1 - rhs, 0, keepdims=False)
+    swapped = lax.ppermute(other, axes, own)
+    swapped_slow = lax.ppermute(slowness, axes, own)
+    mine = lax.dynamic_index_in_dim(right_side, rhs, 0, keepdims=False)
 
     total_y = size_y * grid_cols
     cells = lax.dynamic_index_in_dim(source_cells, rhs, 0, keepdims=True)
@@ -428,28 +445,28 @@
     amplitudes = lax.dynamic_index_in_dim(source_amplitudes, rhs, 0, keepdims=False).T[:, None, :]
 
     depth = cells % cells_z
-    prep_tables = [t[name] for name in PREP]
-    own_modes, own_contrast, *held = pl.pallas_call(
+    own_modes, own_contrast, t["inverse"], *held = pl.pallas_call(
         functools.partial(prep_kernel, cells_x),
-        out_shape=(shaped(rows, 2 * cells_z), shaped(2, rows, cells_z))
+        out_shape=(shaped(rows, 2 * cells_z), shaped(2, rows, cells_z), shaped(2, rows, cells_z))
         + tuple(jax.ShapeDtypeStruct(t[name].shape, BF16) for name in LATER),
         in_specs=[whole()] * (5 + len(PREP)) + [anywhere()] * len(LATER),
-        out_specs=(whole(),) * (2 + len(LATER)),
+        out_specs=(whole(),) * (3 + len(LATER)),
         scratch_shapes=[pltpu.SemaphoreType.DMA((len(LATER),))],
         compiler_params=PARAMS,
         cost_estimate=SOLVE_COST,
         name="prep",
-    )(ordered, slowness, places[0], depth, amplitudes, *prep_tables, *[t[name] for name in LATER])
+    )(mine, slowness, places[0], depth, amplitudes, *[t[name] for name in PREP + LATER])
     t.update(zip(LATER, held))
     modes, contrast = pl.pallas_call(
         functools.partial(prep_other_kernel, cells_x),
         out_shape=(shaped(2, rows, 2 * cells_z), shaped(2, 2, rows, cells_z)),
-        in_specs=[scalars()] + [whole()] * (6 + len(PREP)),
+        in_specs=[scalars()] * 2 + [whole()] * (7 + len(PREP_OTHER)),
         out_specs=(whole(), whole()),
         compiler_params=PARAMS,
         cost_estimate=SOLVE_COST,
         name="prep_other",
-    )(core_ref, swapped, own_modes, own_contrast, places[1], depth, amplitudes, *prep_tables)
+    )(core_ref, rhs_ref, swapped, swapped_slow, own_modes, own_contrast, places[1], depth, amplitudes,
+      *[t[name] for name in PREP_OTHER])
 
     def solve(tile, active, trace_x, trace_y, state, final):
         names = FINAL if final else BEAT
@@ -524,7 +541,7 @@
         compiler_params=PARAMS,
         cost_estimate=KEEP_COST,
         name="keep",
-    )(core_ref, keep, after_x, after_y, t["right_z"])
+    )(core_ref, keep, after_x, after_y, t["onward"])
     wavefield = pl.pallas_call(
         place_wave_kernel,
         out_shape=shaped(*right_side.shape),
@@ -546,7 +563,7 @@
         ],
         compiler_params=PARAMS,
         name="place_rest",
-    )(core_ref, rhs_ref, keep_rest, got, got_edge, t["right_z"])
+    )(core_ref, rhs_ref, keep_rest, got, got_edge, t["onward"])
     return wavefield, residual
 
 

time: 67 us -> 65.4 us (0.976)
  other arithmetic: 1.35 us -> 0.06 us
    select_n x1 -> x0, other arithmetic: 1.27 us -> none  [body(): ordered = jnp.where(rhs == 0, right_side, right_side[::-1])]
    squeeze x1, local copies, waits for them, and re-layouts: 0.02 us -> 1.16 us  [body(): mine = lax.dynamic_index_in_dim(right_side, rhs, 0, keepdims=False)]
    unnamed x16 -> x14, local copies, waits for them, and re-layouts: 1.04 us -> 0.05 us
  transfers between devices with their start and end apart: 23 -> 24, of which waited for: 4 -> 4; matrix products, arithmetic and copies ran while one was open for 0% -> 0% of each run, Pallas kernels for 13% -> 13%
where the time goes in v12:
time: 65.4 us; the launch traced here: 64.4 us
  waiting for transfers between devices  30.4 us (46%)
  starting transfers between devices  20.6 us (31%)
  Pallas kernels  10.5 us (16%)
  between operations  1.54 us (2%)
  local copies, waits for them, and re-layouts  1.29 us (2%)
    ppermute x6, waiting for transfers between devices, body(): trace_y0 = hand_on(lax.ppermute(outs0[0], axes, along_y))  26 us
    pallas_call x14, Pallas kernels, solve(): pl.pallas_call(functools.partial(beat_kernel, tile, final), out_shape=(sh...  5.57 us
    ppermute x6, starting transfers between devices, body(): trace_y0 = hand_on(lax.ppermute(outs0[0], axes, along_y))  5.24 us
    ppermute x6, starting transfers between devices, body(): trace_y1 = lax.ppermute(outs1[1], axes, along_y)  5.24 us
    ppermute x6, starting transfers between devices, body(): trace_x = lax.ppermute(outs1[0], axes, along_x)  4.61 us
    ppermute x1, waiting for transfers between devices, body(): lax.ppermute(edge_y, axes, between([((k, j), (k, j - 1)) for k, j in ever...  2.33 us
    ppermute x1, starting transfers between devices, body(): lax.ppermute(edge_y, axes, between([((k, j), (k, j - 1)) for k, j in ever...  1.92 us
    ppermute x6, waiting for transfers between devices, body(): trace_x = lax.ppermute(outs1[0], axes, along_x)  1.32 us
  transfers between devices with their start and end apart: 24, of which 4 were waited for; matrix products, arithmetic and copies ran while one was open for 0% of the time, Pallas kernels for 13%

profile of v12, /device:TPU:29, one launch (start us, length us, event | category | flops | bytes accessed | tf_op | source)
XLA Modules:
  0.0 64.4 jit_solution(11255783934684198379)
XLA Ops:
  0.8 1.2 %dynamic-slice_bitcast_fusion = (f32[2,16,16,128]{3,2,1,0:T(8,128)S(1)}, f32[2,16,16,128]{3,2,1,0:T(8,128)S(1)}) fusion(f32[2,2,16,16,128]{4,3,2,1,0:T(8,128)} %param.8, s32[]{:T(128)S(6)} %select_n.73, s32[]{:T(128)S(6)} %select_n.72), kind=kLoop, calls=%fused_computation | loop fusion | bytes 1048584 | tf_op jit(solution)/shard_map/jit(dynamic_index_in_dim)/squeeze | solution.py:434
  1.9 0.7 %collective-permute-start = (f32[2,16,16,128]{3,2,1,0:T(8,128)S(1)}, f32[2,16,16,128]{3,2,1,0:T(8,128)S(1)}, u32[]{:S(2)}, u32[]{:S(2)}) collective-permute-start(f32[2,16,16,128]{3,2,1,0:T(8,128)S(1)} %get-tuple-element.135), channel_id=1, source_target_pairs={{0,4},{4,0},{1,5},{5,1},{2,6},{6,2},{3,7},{7,3},{8,12},{12,8},{9,1... | collective-permute-start | bytes 786440 | tf_op jit(solution)/shard_map/ppermute | solution.py:432
  2.7 0.1 collective-permute-start.1
  2.9 1.1 %prep.1 = (f32[256,256]{1,0:T(8,128)S(1)}, f32[2,256,128]{2,1,0:T(8,128)S(1)}, f32[2,256,128]{2,1,0:T(8,128)S(1)}, bf16[5,128,384]{2,1,0:T(8,128)(2,1)S(1)}) custom-call(f32[2,16,16,128]{3,2,1,0:T(8,128)S(1)} %get-tuple-element.134.right_ref, f32[16,16,128]{2,1,0:T(8,128)S(1)} %copy-done.2, s32[1,16]{1,0:T(1,128)S(1)} %and_select_fusion.2.place_ref, ...), custom_call_target="tpu_custom_call" | custom-call | flops 2000000000 | bytes 2000000 | tf_op jit(solution)/shard_map/prep/pallas_call | solution.py:448
  4.0 0.8 %prep_other.1 = (f32[2,256,256]{2,1,0:T(8,128)S(1)}, f32[2,2,256,128]{3,2,1,0:T(8,128)S(1)}) custom-call(s32[1]{0:T(128)} %bitcast.1.core_ref, s32[1]{0:T(128)} %bitcast.rhs_ref, f32[2,16,16,128]{3,2,1,0:T(8,128)S(1)} %collective-permute-done.swap_ref, f32[16,16,128]{2,1,0:T(8,128)S(1)} %collective-permute-done.1.slow_ref, ...), custom_call_target="tpu_custom_call" | custom-call | flops 2000000000 | bytes 2000000 | tf_op jit(solution)/shard_map/prep_other/pallas_call | solution.py:460
  4.8 0.1 upper.7
  4.9 0.7 %collective-permute-start.3 = (f32[32,256]{1,0:T(8,128)S(1)}, f32[32,256]{1,0:T(8,128)S(1)}, u32[]{:S(2)}, u32[]{:S(2)}) collective-permute-start(f32[32,256]{1,0:T(8,128)S(1)} %get-tuple-element.74), channel_id=1, source_target_pairs={{0,5},{4,1}} | collective-permute-start | bytes 98312 | tf_op jit(solution)/shard_map/ppermute | solution.py:509
  5.7 0.1 lower.7
  5.7 0.7 %collective-permute-start.2 = (f32[32,256]{1,0:T(8,128)S(1)}, f32[32,256]{1,0:T(8,128)S(1)}, u32[]{:S(2)}, u32[]{:S(2)}) collective-permute-start(f32[32,256]{1,0:T(8,128)S(1)} %get-tuple-element.73), channel_id=1, source_target_pairs={{0,12},{4,8}} | collective-permute-start | bytes 98312 | tf_op jit(solution)/shard_map/ppermute | solution.py:512
  6.4 0.7 %collective-permute-start.4 = (f32[32,256]{1,0:T(8,128)S(1)}, f32[32,256]{1,0:T(8,128)S(1)}, u32[]{:S(2)}, u32[]{:S(2)}) collective-permute-start(f32[32,256]{1,0:T(8,128)S(1)} %get-tuple-element.78), channel_id=1, source_target_pairs={{0,5},{4,1}} | collective-permute-start | bytes 98312 | tf_op jit(solution)/shard_map/ppermute | solution.py:514
  7.1 0.1 upper.8
  7.2 0.7 %collective-permute-start.6 = (f32[32,256]{1,0:T(8,128)S(1)}, f32[32,256]{1,0:T(8,128)S(1)}, u32[]{:S(2)}, u32[]{:S(2)}) collective-permute-start(f32[32,256]{1,0:T(8,128)S(1)} %get-tuple-element.82), channel_id=1, source_target_pairs={{1,6},{5,2},{8,13},{12,9}} | collective-permute-start | bytes 98312 | tf_op jit(solution)/shard_map/ppermute | solution.py:509
  7.9 0.1 lower.8
  8.0 0.7 %collective-permute-start.5 = (f32[32,256]{1,0:T(8,128)S(1)}, f32[32,256]{1,0:T(8,128)S(1)}, u32[]{:S(2)}, u32[]{:S(2)}) collective-permute-start(f32[32,256]{1,0:T(8,128)S(1)} %get-tuple-element.81), channel_id=1, source_target_pairs={{1,13},{5,9},{8,20},{12,16}} | collective-permute-start | bytes 98312 | tf_op jit(solution)/shard_map/ppermute | solution.py:512
  8.6 0.7 %collective-permute-start.7 = (f32[32,256]{1,0:T(8,128)S(1)}, f32[32,256]{1,0:T(8,128)S(1)}, u32[]{:S(2)}, u32[]{:S(2)}) collective-permute-start(f32[32,256]{1,0:T(8,128)S(1)} %get-tuple-element.86), channel_id=1, source_target_pairs={{1,6},{5,2},{8,13},{12,9}} | collective-permute-start | bytes 98312 | tf_op jit(solution)/shard_map/ppermute | solution.py:514
  9.3 0.1 upper.9
  9.4 0.7 %collective-permute-start.9 = (f32[32,256]{1,0:T(8,128)S(1)}, f32[32,256]{1,0:T(8,128)S(1)}, u32[]{:S(2)}, u32[]{:S(2)}) collective-permute-start(f32[32,256]{1,0:T(8,128)S(1)} %get-tuple-element.90), channel_id=1, source_target_pairs={{2,7},{6,3},{9,14},{13,10},{16,21},{20,17}} | collective-permute-start | bytes 98312 | tf_op jit(solution)/shard_map/ppermute | solution.py:509
  10.1 0.1 lower.9
  10.2 0.7 %collective-permute-start.8 = (f32[32,256]{1,0:T(8,128)S(1)}, f32[32,256]{1,0:T(8,128)S(1)}, u32[]{:S(2)}, u32[]{:S(2)}) collective-permute-start(f32[32,256]{1,0:T(8,128)S(1)} %get-tuple-element.89), channel_id=1, source_target_pairs={{2,14},{6,10},{9,21},{13,17},{16,28},{20,24}} | collective-permute-start | bytes 98312 | tf_op jit(solution)/shard_map/ppermute | solution.py:512
  10.9 0.7 %collective-permute-start.10 = (f32[32,256]{1,0:T(8,128)S(1)}, f32[32,256]{1,0:T(8,128)S(1)}, u32[]{:S(2)}, u32[]{:S(2)}) collective-permute-start(f32[32,256]{1,0:T(8,128)S(1)} %get-tuple-element.94), channel_id=1, source_target_pairs={{2,7},{6,3},{9,14},{13,10},{16,21},{20,17}} | collective-permute-start | bytes 98312 | tf_op jit(solution)/shard_map/ppermute | solution.py:514
  11.6 0.1 upper.10
  11.7 0.7 %collective-permute-start.12 = (f32[32,256]{1,0:T(8,128)S(1)}, f32[32,256]{1,0:T(8,128)S(1)}, u32[]{:S(2)}, u32[]{:S(2)}) collective-permute-start(f32[32,256]{1,0:T(8,128)S(1)} %get-tuple-element.98), channel_id=1, source_target_pairs={{10,15},{14,11},{17,22},{21,18},{24,29},{28,25}} | collective-permute-start | bytes 98312 | tf_op jit(solution)/shard_map/ppermute | solution.py:509
  12.3 0.3 lower.10
  12.6 0.7 %collective-permute-start.11 = (f32[32,256]{1,0:T(8,128)S(1)}, f32[32,256]{1,0:T(8,128)S(1)}, u32[]{:S(2)}, u32[]{:S(2)}) collective-permute-start(f32[32,256]{1,0:T(8,128)S(1)} %get-tuple-element.97), channel_id=1, source_target_pairs={{3,15},{7,11},{10,22},{14,18},{17,29},{21,25}} | collective-permute-start | bytes 98312 | tf_op jit(solution)/shard_map/ppermute | solution.py:512
  13.3 0.7 %collective-permute-start.13 = (f32[32,256]{1,0:T(8,128)S(1)}, f32[32,256]{1,0:T(8,128)S(1)}, u32[]{:S(2)}, u32[]{:S(2)}) collective-permute-start(f32[32,256]{1,0:T(8,128)S(1)} %get-tuple-element.102), channel_id=1, source_target_pairs={{10,15},{14,11},{17,22},{21,18},{24,29},{28,25}} | collective-permute-start | bytes 98312 | tf_op jit(solution)/shard_map/ppermute | solution.py:514
  14.1 1.3 %collective-permute-start.15 = (f32[32,256]{1,0:T(8,128)S(1)}, f32[32,256]{1,0:T(8,128)S(1)}, u32[]{:S(2)}, u32[]{:S(2)}) collective-permute-start(f32[32,256]{1,0:T(8,128)S(1)} %get-tuple-element.106), channel_id=1, source_target_pairs={{18,23},{22,19},{25,30},{29,26}} | collective-permute-start | bytes 98312 | tf_op jit(solution)/shard_map/ppermute | solution.py:509
  15.4 0.1 lower.11
  15.4 1.3 %collective-permute-start.14 = (f32[32,256]{1,0:T(8,128)S(1)}, f32[32,256]{1,0:T(8,128)S(1)}, u32[]{:S(2)}, u32[]{:S(2)}) collective-permute-start(f32[32,256]{1,0:T(8,128)S(1)} %get-tuple-element.105), channel_id=1, source_target_pairs={{11,23},{15,19},{18,30},{22,26}} | collective-permute-start | bytes 98312 | tf_op jit(solution)/shard_map/ppermute | solution.py:512
  16.8 1.3 %collective-permute-start.16 = (f32[32,256]{1,0:T(8,128)S(1)}, f32[32,256]{1,0:T(8,128)S(1)}, u32[]{:S(2)}, u32[]{:S(2)}) collective-permute-start(f32[32,256]{1,0:T(8,128)S(1)} %get-tuple-element.110), channel_id=1, source_target_pairs={{18,23},{22,19},{25,30},{29,26}} | collective-permute-start | bytes 98312 | tf_op jit(solution)/shard_map/ppermute | solution.py:514
  18.1 26.0 %collective-permute-done.15.in_ref = f32[32,256]{1,0:T(8,128)S(1)} collective-permute-done((f32[32,256]{1,0:T(8,128)S(1)}, f32[32,256]{1,0:T(8,128)S(1)}, u32[]{:S(2)}, u32[]{:S(2)}) %collective-permute-start.15) | collective-permute-done | bytes 32800 | tf_op jit(solution)/shard_map/ppermute | solution.py:509
  44.0 1.3 %collective-permute-done.14.trace_x_ref = f32[32,256]{1,0:T(8,128)S(1)} collective-permute-done((f32[32,256]{1,0:T(8,128)S(1)}, f32[32,256]{1,0:T(8,128)S(1)}, u32[]{:S(2)}, u32[]{:S(2)}) %collective-permute-start.14) | collective-permute-done | bytes 32800 | tf_op jit(solution)/shard_map/ppermute | solution.py:512
  45.3 2.1 %upper.12 = (f32[256,256]{1,0:T(8,128)S(1)}, f32[256,256]{1,0:T(8,128)S(1)}, f32[32,256]{1,0:T(8,128)S(1)}, f32[32,256]{1,0:T(8,128)S(1)}) custom-call(s32[1]{0:T(128)} %bitcast.9.active_ref, f32[2,256,256]{2,1,0:T(8,128)S(1)} %get-tuple-element.69.modes_ref, ...), custom_call_target="tpu_custom_call", output_to_operand_aliasing={{0}: (5, {}), {1}: (6, {})} | custom-call | flops 2000000000 | bytes 2000000 | tf_op jit(solution)/shard_map/upper/pallas_call | solution.py:475
  47.4 1.3 %collective-permute-start.18 = (f32[32,256]{1,0:T(8,128)S(1)}, f32[32,256]{1,0:T(8,128)S(1)}, u32[]{:S(2)}, u32[]{:S(2)}) collective-permute-start(f32[32,256]{1,0:T(8,128)S(1)} %get-tuple-element.114), channel_id=1, source_target_pairs={{26,31},{30,27}} | collective-permute-start | bytes 98312 | tf_op jit(solution)/shard_map/ppermute | solution.py:509
  48.7 2.1 %lower.12 = (f32[256,256]{1,0:T(8,128)S(1)}, f32[256,256]{1,0:T(8,128)S(1)}, f32[32,256]{1,0:T(8,128)S(1)}, f32[32,256]{1,0:T(8,128)S(1)}) custom-call(s32[1]{0:T(128)} %bitcast.9.active_ref, f32[2,256,256]{2,1,0:T(8,128)S(1)} %get-tuple-element.69.modes_ref, ...), custom_call_target="tpu_custom_call", output_to_operand_aliasing={{0}: (5, {}), {1}: (6, {})} | custom-call | flops 2000000000 | bytes 2000000 | tf_op jit(solution)/shard_map/lower/pallas_call | solution.py:475
  50.8 0.7 %collective-permute-start.17 = (f32[32,256]{1,0:T(8,128)S(1)}, f32[32,256]{1,0:T(8,128)S(1)}, u32[]{:S(2)}, u32[]{:S(2)}) collective-permute-start(f32[32,256]{1,0:T(8,128)S(1)} %get-tuple-element.113), channel_id=1, source_target_pairs={{19,31},{23,27}} | collective-permute-start | bytes 98312 | tf_op jit(solution)/shard_map/ppermute | solution.py:512
  51.5 1.3 %collective-permute-start.19 = (f32[32,256]{1,0:T(8,128)S(1)}, f32[32,256]{1,0:T(8,128)S(1)}, u32[]{:S(2)}, u32[]{:S(2)}) collective-permute-start(f32[32,256]{1,0:T(8,128)S(1)} %get-tuple-element.120), channel_id=1, source_target_pairs={{26,31},{30,27}} | collective-permute-start | bytes 98312 | tf_op jit(solution)/shard_map/ppermute | solution.py:514
  52.8 0.3 upper.13
  53.1 0.7 %collective-permute-done.19.trace_y_ref = f32[32,256]{1,0:T(8,128)S(1)} collective-permute-done((f32[32,256]{1,0:T(8,128)S(1)}, f32[32,256]{1,0:T(8,128)S(1)}, u32[]{:S(2)}, u32[]{:S(2)}) %collective-permute-start.19) | collective-permute-done | bytes 32800 | tf_op jit(solution)/shard_map/ppermute | solution.py:514
  53.8 0.3 lower.13
  54.0 1.9 %collective-permute-start.22 = (f32[2,32,256]{2,1,0:T(8,128)S(1)}, f32[2,32,256]{2,1,0:T(8,128)S(1)}, u32[]{:S(2)}, u32[]{:S(2)}) collective-permute-start(f32[2,32,256]{2,1,0:T(8,128)S(1)} %pad_maximum_fusion), channel_id=1, source_target_pairs={{1,4},{5,0},{2,5},{6,1},{3,6},{7,2},{9,12},{13,8},{10,13},{14,9},{... | collective-permute-start | bytes 196616 | tf_op jit(solution)/shard_map/ppermute | solution.py:520
  56.0 1.3 %collective-permute-start.21 = (f32[32,256]{1,0:T(8,128)S(1)}, f32[32,256]{1,0:T(8,128)S(1)}, u32[]{:S(2)}, u32[]{:S(2)}) collective-permute-start(f32[32,256]{1,0:T(8,128)S(1)} %get-tuple-element.127), channel_id=1, source_target_pairs={{8,4},{12,0},{9,5},{13,1},{10,6},{14,2},{11,7},{15,3},{16,12},{20,... | collective-permute-start | bytes 98312 | tf_op jit(solution)/shard_map/ppermute | solution.py:519
  57.3 1.1 %finish.1 = (f32[2,2,16,16,128]{4,3,2,1,0:T(8,128)S(1)}, f32[2,2,16,16,128]{4,3,2,1,0:T(8,128)S(1)}) custom-call(s32[1]{0:T(128)} %bitcast.1.core_ref, f32[256,256]{1,0:T(8,128)S(1)} %get-tuple-element.117.total0_ref, f32[256,256]{1,0:T(8,128)S(1)} %get-tuple-element.118.term0_ref, f32[256,256]{1,0:T(8,128)S(1)} %get-tuple-element.123.total1_ref, ...), custom_call_target="tpu_custom_call" | custom-call | tf_op jit(solution)/shard_map/finish/pallas_call | solution.py:523
  58.4 1.0 %collective-permute-start.20 = (f32[2,2,16,16,128]{4,3,2,1,0:T(8,128)S(1)}, f32[2,2,16,16,128]{4,3,2,1,0:T(8,128)S(1)}, u32[]{:S(2)}, u32[]{:S(2)}) collective-permute-start(f32[2,2,16,16,128]{4,3,2,1,0:T(8,128)S(1)} %get-tuple-element.126), channel_id=1, source_target_pairs={{0,4},{4,0},{1,5},{5,1},{2,6},{6,2},{3,7},{7,3},{8,12},{12,8},{9,1... | collective-permute-start | bytes 1572872 | tf_op jit(solution)/shard_map/ppermute | solution.py:532
  59.5 2.3 %collective-permute-done.22.edge_y_ref = f32[2,32,256]{2,1,0:T(8,128)S(1)} collective-permute-done((f32[2,32,256]{2,1,0:T(8,128)S(1)}, f32[2,32,256]{2,1,0:T(8,128)S(1)}, u32[]{:S(2)}, u32[]{:S(2)}) %collective-permute-start.22) | collective-permute-done | bytes 65568 | tf_op jit(solution)/shard_map/ppermute | solution.py:520
  61.8 0.5 collective-permute-start.23
  62.3 0.2 keep.1.keep_rest_ref
  62.5 0.8 %place_wave.1 = f32[2,2,16,16,128]{4,3,2,1,0:T(8,128)} custom-call(s32[1]{0:T(128)} %bitcast.rhs_ref, f32[2,2,16,16,128]{4,3,2,1,0:T(8,128)S(1)} %get-tuple-element.125.keep_ref, f32[2,2,16,16,128]{4,3,2,1,0:T(8,128)S(1)} %collective-permute-done.20.got_ref), custom_call_target="tpu_custom_call" | custom-call | flops 10000000000 | bytes 1000000 | tf_op jit(solution)/shard_map/place_wave/pallas_call | solution.py:545
  63.3 0.9 %place_rest.1 = f32[2,2,16,16,128]{4,3,2,1,0:T(8,128)} custom-call(s32[1]{0:T(128)} %bitcast.1.core_ref, s32[1]{0:T(128)} %bitcast.rhs_ref, f32[2,16,16,128]{3,2,1,0:T(8,128)S(1)} %keep.1.keep_rest_ref, f32[2,2,16,16,128]{4,3,2,1,0:T(8,128)S(1)} %collective-permute-done.20.got_ref, f32[64,256]{1,0:T(8,128)S(1)} %collective-permute-done.23.got_edge_ref, ...), custom_call_target="tpu_custom_call" | custom-call | tf_op jit(solution)/shard_map/place_rest/pallas_call | solution.py:555
  (53 shorter events, 0.4 us)
Async XLA Ops:
  0.6 2.2 %copy-start = (f32[2,16,2]{1,2,0:T(2,128)S(1)}, f32[2,16,2]{1,2,0:T(2,128)}, u32[]{:S(2)}) copy-start(f32[2,16,2]{1,2,0:T(2,128)} %param.11) | copy-start | bytes 772
  0.7 2.2 %copy-start.4 = (f32[256,128]{1,0:T(8,128)S(1)}, f32[256,128]{1,0:T(8,128)}, u32[]{:S(2)}) copy-start(f32[256,128]{1,0:T(8,128)} %constant.150.clone.refs_0_) | copy-start | bytes 393220
  0.7 2.0 %copy-start.6 = (s32[2,16]{1,0:T(2,128)S(1)}, s32[2,16]{1,0:T(2,128)}, u32[]{:S(2)}) copy-start(s32[2,16]{1,0:T(2,128)} %param.10) | copy-start | bytes 388
  0.7 1.9 %copy-start.2 = (f32[16,16,128]{2,1,0:T(8,128)S(1)}, f32[16,16,128]{2,1,0:T(8,128)}, u32[]{:S(2)}) copy-start(f32[16,16,128]{2,1,0:T(8,128)} %slow_ref.1) | copy-start | bytes 393220
  0.7 2.1 %copy-start.1 = (bf16[4,128,384]{2,1,0:T(8,128)(2,1)S(1)}, bf16[4,128,384]{2,1,0:T(8,128)(2,1)}, u32[]{:S(2)}) copy-start(bf16[4,128,384]{2,1,0:T(8,128)(2,1)} %constant.152.clone.refs_1_.z_ref) | copy-start | bytes 1179652
  0.7 2.1 %copy-start.3 = (bf16[5,128,384]{2,1,0:T(8,128)(2,1)S(1)}, bf16[5,128,384]{2,1,0:T(8,128)(2,1)}, u32[]{:S(2)}) copy-start(bf16[5,128,384]{2,1,0:T(8,128)(2,1)} %constant.153.clone.refs_2_) | copy-start | bytes 1474564
  1.9 2.1 %collective-permute-start = (f32[2,16,16,128]{3,2,1,0:T(8,128)S(1)}, f32[2,16,16,128]{3,2,1,0:T(8,128)S(1)}, u32[]{:S(2)}, u32[]{:S(2)}) collective-permute-start(f32[2,16,16,128]{3,2,1,0:T(8,128)S(1)} %get-tuple-element.135), channel_id=1, source_target_pairs={{0,4},{4,0},{1,5},{5,1},{2,6},{6,2},{3,7},{7,3},{8,12},{12,8},{9,1... | collective-permute-start | bytes 786440 | tf_op jit(solution)/shard_map/ppermute | solution.py:432
  2.7 1.3 %collective-permute-start.1 = (f32[16,16,128]{2,1,0:T(8,128)S(1)}, f32[16,16,128]{2,1,0:T(8,128)S(1)}, u32[]{:S(2)}, u32[]{:S(2)}) collective-permute-start(f32[16,16,128]{2,1,0:T(8,128)S(1)} %copy-done.2), channel_id=1, source_target_pairs={{0,4},{4,0},{1,5},{5,1},{2,6},{6,2},{3,7},{7,3},{8,12},{12,8},{9,1... | collective-permute-start | bytes 393224 | tf_op jit(solution)/shard_map/ppermute | solution.py:433
  4.9 2.2 %collective-permute-start.3 = (f32[32,256]{1,0:T(8,128)S(1)}, f32[32,256]{1,0:T(8,128)S(1)}, u32[]{:S(2)}, u32[]{:S(2)}) collective-permute-start(f32[32,256]{1,0:T(8,128)S(1)} %get-tuple-element.74), channel_id=1, source_target_pairs={{0,5},{4,1}} | collective-permute-start | bytes 98312 | tf_op jit(solution)/shard_map/ppermute | solution.py:509
  5.7 1.4 %collective-permute-start.2 = (f32[32,256]{1,0:T(8,128)S(1)}, f32[32,256]{1,0:T(8,128)S(1)}, u32[]{:S(2)}, u32[]{:S(2)}) collective-permute-start(f32[32,256]{1,0:T(8,128)S(1)} %get-tuple-element.73), channel_id=1, source_target_pairs={{0,12},{4,8}} | collective-permute-start | bytes 98312 | tf_op jit(solution)/shard_map/ppermute | solution.py:512
  6.4 1.5 %collective-permute-start.4 = (f32[32,256]{1,0:T(8,128)S(1)}, f32[32,256]{1,0:T(8,128)S(1)}, u32[]{:S(2)}, u32[]{:S(2)}) collective-permute-start(f32[32,256]{1,0:T(8,128)S(1)} %get-tuple-element.78), channel_id=1, source_target_pairs={{0,5},{4,1}} | collective-permute-start | bytes 98312 | tf_op jit(solution)/shard_map/ppermute | solution.py:514
  7.2 2.1 %collective-permute-start.6 = (f32[32,256]{1,0:T(8,128)S(1)}, f32[32,256]{1,0:T(8,128)S(1)}, u32[]{:S(2)}, u32[]{:S(2)}) collective-permute-start(f32[32,256]{1,0:T(8,128)S(1)} %get-tuple-element.82), channel_id=1, source_target_pairs={{1,6},{5,2},{8,13},{12,9}} | collective-permute-start | bytes 98312 | tf_op jit(solution)/shard_map/ppermute | solution.py:509
  8.0 1.4 %collective-permute-start.5 = (f32[32,256]{1,0:T(8,128)S(1)}, f32[32,256]{1,0:T(8,128)S(1)}, u32[]{:S(2)}, u32[]{:S(2)}) collective-permute-start(f32[32,256]{1,0:T(8,128)S(1)} %get-tuple-element.81), channel_id=1, source_target_pairs={{1,13},{5,9},{8,20},{12,16}} | collective-permute-start | bytes 98312 | tf_op jit(solution)/shard_map/ppermute | solution.py:512
  8.6 1.5 %collective-permute-start.7 = (f32[32,256]{1,0:T(8,128)S(1)}, f32[32,256]{1,0:T(8,128)S(1)}, u32[]{:S(2)}, u32[]{:S(2)}) collective-permute-start(f32[32,256]{1,0:T(8,128)S(1)} %get-tuple-element.86), channel_id=1, source_target_pairs={{1,6},{5,2},{8,13},{12,9}} | collective-permute-start | bytes 98312 | tf_op jit(solution)/shard_map/ppermute | solution.py:514
  9.4 2.1 %collective-permute-start.9 = (f32[32,256]{1,0:T(8,128)S(1)}, f32[32,256]{1,0:T(8,128)S(1)}, u32[]{:S(2)}, u32[]{:S(2)}) collective-permute-start(f32[32,256]{1,0:T(8,128)S(1)} %get-tuple-element.90), channel_id=1, source_target_pairs={{2,7},{6,3},{9,14},{13,10},{16,21},{20,17}} | collective-permute-start | bytes 98312 | tf_op jit(solution)/shard_map/ppermute | solution.py:509
  10.2 1.4 %collective-permute-start.8 = (f32[32,256]{1,0:T(8,128)S(1)}, f32[32,256]{1,0:T(8,128)S(1)}, u32[]{:S(2)}, u32[]{:S(2)}) collective-permute-start(f32[32,256]{1,0:T(8,128)S(1)} %get-tuple-element.89), channel_id=1, source_target_pairs={{2,14},{6,10},{9,21},{13,17},{16,28},{20,24}} | collective-permute-start | bytes 98312 | tf_op jit(solution)/shard_map/ppermute | solution.py:512
  10.9 1.5 %collective-permute-start.10 = (f32[32,256]{1,0:T(8,128)S(1)}, f32[32,256]{1,0:T(8,128)S(1)}, u32[]{:S(2)}, u32[]{:S(2)}) collective-permute-start(f32[32,256]{1,0:T(8,128)S(1)} %get-tuple-element.94), channel_id=1, source_target_pairs={{2,7},{6,3},{9,14},{13,10},{16,21},{20,17}} | collective-permute-start | bytes 98312 | tf_op jit(solution)/shard_map/ppermute | solution.py:514
  11.7 2.3 %collective-permute-start.12 = (f32[32,256]{1,0:T(8,128)S(1)}, f32[32,256]{1,0:T(8,128)S(1)}, u32[]{:S(2)}, u32[]{:S(2)}) collective-permute-start(f32[32,256]{1,0:T(8,128)S(1)} %get-tuple-element.98), channel_id=1, source_target_pairs={{10,15},{14,11},{17,22},{21,18},{24,29},{28,25}} | collective-permute-start | bytes 98312 | tf_op jit(solution)/shard_map/ppermute | solution.py:509
  12.6 1.4 %collective-permute-start.11 = (f32[32,256]{1,0:T(8,128)S(1)}, f32[32,256]{1,0:T(8,128)S(1)}, u32[]{:S(2)}, u32[]{:S(2)}) collective-permute-start(f32[32,256]{1,0:T(8,128)S(1)} %get-tuple-element.97), channel_id=1, source_target_pairs={{3,15},{7,11},{10,22},{14,18},{17,29},{21,25}} | collective-permute-start | bytes 98312 | tf_op jit(solution)/shard_map/ppermute | solution.py:512
  13.3 2.1 %collective-permute-start.13 = (f32[32,256]{1,0:T(8,128)S(1)}, f32[32,256]{1,0:T(8,128)S(1)}, u32[]{:S(2)}, u32[]{:S(2)}) collective-permute-start(f32[32,256]{1,0:T(8,128)S(1)} %get-tuple-element.102), channel_id=1, source_target_pairs={{10,15},{14,11},{17,22},{21,18},{24,29},{28,25}} | collective-permute-start | bytes 98312 | tf_op jit(solution)/shard_map/ppermute | solution.py:514
  14.1 30.0 %collective-permute-start.15 = (f32[32,256]{1,0:T(8,128)S(1)}, f32[32,256]{1,0:T(8,128)S(1)}, u32[]{:S(2)}, u32[]{:S(2)}) collective-permute-start(f32[32,256]{1,0:T(8,128)S(1)} %get-tuple-element.106), channel_id=1, source_target_pairs={{18,23},{22,19},{25,30},{29,26}} | collective-permute-start | bytes 98312 | tf_op jit(solution)/shard_map/ppermute | solution.py:509
  15.4 29.9 %collective-permute-start.14 = (f32[32,256]{1,0:T(8,128)S(1)}, f32[32,256]{1,0:T(8,128)S(1)}, u32[]{:S(2)}, u32[]{:S(2)}) collective-permute-start(f32[32,256]{1,0:T(8,128)S(1)} %get-tuple-element.105), channel_id=1, source_target_pairs={{11,23},{15,19},{18,30},{22,26}} | collective-permute-start | bytes 98312 | tf_op jit(solution)/shard_map/ppermute | solution.py:512
  16.8 31.9 %collective-permute-start.16 = (f32[32,256]{1,0:T(8,128)S(1)}, f32[32,256]{1,0:T(8,128)S(1)}, u32[]{:S(2)}, u32[]{:S(2)}) collective-permute-start(f32[32,256]{1,0:T(8,128)S(1)} %get-tuple-element.110), channel_id=1, source_target_pairs={{18,23},{22,19},{25,30},{29,26}} | collective-permute-start | bytes 98312 | tf_op jit(solution)/shard_map/ppermute | solution.py:514
  47.4 5.4 %collective-permute-start.18 = (f32[32,256]{1,0:T(8,128)S(1)}, f32[32,256]{1,0:T(8,128)S(1)}, u32[]{:S(2)}, u32[]{:S(2)}) collective-permute-start(f32[32,256]{1,0:T(8,128)S(1)} %get-tuple-element.114), channel_id=1, source_target_pairs={{26,31},{30,27}} | collective-permute-start | bytes 98312 | tf_op jit(solution)/shard_map/ppermute | solution.py:509
  48.7 4.1 %copy-start.5 = (bf16[64,768]{1,0:T(8,128)(2,1)S(1)}, bf16[64,768]{1,0:T(8,128)(2,1)}, u32[]{:S(2)}) copy-start(bf16[64,768]{1,0:T(8,128)(2,1)} %constant.151.clone.refs_3_) | copy-start | bytes 294916
  50.8 2.0 %collective-permute-start.17 = (f32[32,256]{1,0:T(8,128)S(1)}, f32[32,256]{1,0:T(8,128)S(1)}, u32[]{:S(2)}, u32[]{:S(2)}) collective-permute-start(f32[32,256]{1,0:T(8,128)S(1)} %get-tuple-element.113), channel_id=1, source_target_pairs={{19,31},{23,27}} | collective-permute-start | bytes 98312 | tf_op jit(solution)/shard_map/ppermute | solution.py:512
  51.5 2.3 %collective-permute-start.19 = (f32[32,256]{1,0:T(8,128)S(1)}, f32[32,256]{1,0:T(8,128)S(1)}, u32[]{:S(2)}, u32[]{:S(2)}) collective-permute-start(f32[32,256]{1,0:T(8,128)S(1)} %get-tuple-element.120), channel_id=1, source_target_pairs={{26,31},{30,27}} | collective-permute-start | bytes 98312 | tf_op jit(solution)/shard_map/ppermute | solution.py:514
  54.0 7.7 %collective-permute-start.22 = (f32[2,32,256]{2,1,0:T(8,128)S(1)}, f32[2,32,256]{2,1,0:T(8,128)S(1)}, u32[]{:S(2)}, u32[]{:S(2)}) collective-permute-start(f32[2,32,256]{2,1,0:T(8,128)S(1)} %pad_maximum_fusion), channel_id=1, source_target_pairs={{1,4},{5,0},{2,5},{6,1},{3,6},{7,2},{9,12},{13,8},{10,13},{14,9},{... | collective-permute-start | bytes 196616 | tf_op jit(solution)/shard_map/ppermute | solution.py:520
  56.0 5.8 %collective-permute-start.21 = (f32[32,256]{1,0:T(8,128)S(1)}, f32[32,256]{1,0:T(8,128)S(1)}, u32[]{:S(2)}, u32[]{:S(2)}) collective-permute-start(f32[32,256]{1,0:T(8,128)S(1)} %get-tuple-element.127), channel_id=1, source_target_pairs={{8,4},{12,0},{9,5},{13,1},{10,6},{14,2},{11,7},{15,3},{16,12},{20,... | collective-permute-start | bytes 98312 | tf_op jit(solution)/shard_map/ppermute | solution.py:519
  58.4 4.0 %collective-permute-start.20 = (f32[2,2,16,16,128]{4,3,2,1,0:T(8,128)S(1)}, f32[2,2,16,16,128]{4,3,2,1,0:T(8,128)S(1)}, u32[]{:S(2)}, u32[]{:S(2)}) collective-permute-start(f32[2,2,16,16,128]{4,3,2,1,0:T(8,128)S(1)} %get-tuple-element.126), channel_id=1, source_target_pairs={{0,4},{4,0},{1,5},{5,1},{2,6},{6,2},{3,7},{7,3},{8,12},{12,8},{9,1... | collective-permute-start | bytes 1572872 | tf_op jit(solution)/shard_map/ppermute | solution.py:532
  61.8 1.5 %collective-permute-start.23 = (f32[64,256]{1,0:T(8,128)S(1)}, f32[64,256]{1,0:T(8,128)S(1)}, u32[]{:S(2)}, u32[]{:S(2)}) collective-permute-start(f32[64,256]{1,0:T(8,128)S(1)} %pad_maximum_fusion.1), channel_id=1, source_target_pairs={{0,4},{4,0},{1,5},{5,1},{2,6},{6,2},{3,7},{7,3},{8,12},{12,8},{9,1... | collective-permute-start | bytes 196616 | tf_op jit(solution)/shard_map/ppermute | solution.py:535

commit v13 on v12

--- a/solution.py
+++ b/solution.py
@@ -57,9 +57,20 @@
     return jnp.concatenate([t["later"][2, :, :depth], t["later"][3, :, :depth]], axis=0)
 
 
-def leave_matrix(t):
-    count = t["later"].shape[1] // 2
-    return jnp.concatenate([t["later"][4, :count], t["later"][4, count:]], axis=1)
+def leave_product(t, values):
+    high, low = split(values)
+    rest = 2 * values.shape[0] - t["later"].shape[2]
+    matrix = t["later"][4]
+    if rest > 0:
+        matrix = jnp.concatenate([matrix, t["later"][2, :, -rest:]], axis=1)
+    both = jnp.dot(matrix, jnp.concatenate([high, low], axis=0), preferred_element_type=F32)
+    count = both.shape[0] // 2
+    return both[:count] + both[count:]
+
+
+def stacked_factor(matrix):
+    high, low = halves(matrix)
+    return np.concatenate([np.concatenate([part, part], axis=1) for part in (high, low)], axis=0)
 
 
 def tables(size_x, size_y, cells_z):
@@ -95,7 +106,7 @@
     enter = left_factor(
         np.concatenate([enter_x.reshape(len(full), -1), enter_y.reshape(len(full), -1)], axis=1)
     )
-    leave = left_factor(
+    leave = stacked_factor(
         np.concatenate(
             [
                 by_cell[:, size_x - 2 :].reshape(len(full), -1),
@@ -113,13 +124,18 @@
             axis=1,
         ).T
     )
+    later = slabs(backward + [enter, leave[:, : forward[0].shape[1]]], half * size_y, forward[0].shape[1])
+    rest = leave[:, forward[0].shape[1] :]
+    if rest.shape[1]:
+        assert enter.shape[1] <= later.shape[2] - rest.shape[1]
+        later[2, :, later.shape[2] - rest.shape[1] :] = rest
     assert 2 * cells_z % (half * size_y) == 0 and 2 * cells_z <= forward[0].shape[1]
     assert enter.shape[0] == 2 * half * size_y and enter.shape[1] <= forward[0].shape[1]
-    assert 2 * leave.shape[0] == half * size_y and leave.shape[1] == 2 * forward[0].shape[1]
+    assert leave.shape[0] == half * size_y
     return dict(
         symbol=real_part.astype(np.float32), first=first,
         onward=slabs(forward + [right_z], half * size_y, forward[0].shape[1]),
-        later=slabs(backward + [enter, leave], half * size_y, forward[0].shape[1]),
+        later=later,
     ), tuple(int(x) for x in cells)
 
 
@@ -294,7 +310,7 @@
         new_total_ref[...] = total
         new_term_ref[...] = term
         if not (final and tile == 1):
-            out = left_product(leave_matrix(t), total)
+            out = leave_product(t, total)
             for out_ref, part in zip(out_refs[:1] if final else out_refs, (out[:count], out[count:])):
                 out_ref[...] = part
 
@@ -484,13 +500,14 @@
         )(active, modes, contrast, trace_x, trace_y, *state, *[t[name] for name in names])
         return (total, term), outs
 
-    def hand_on(trace):
+    def hand_on(trace, cost=None):
         return pl.pallas_call(
             hand_on_kernel,
             out_shape=shaped(*trace.shape),
             in_specs=[whole()],
             out_specs=whole(),
             compiler_params=PARAMS,
+            cost_estimate=cost,
             name="hand_on",
         )(trace)
 
@@ -516,7 +533,9 @@
     edge_y = jnp.stack([edge_y0, outs1[0]])
 
     every = [(k, j) for k in range(chips) for j in range(grid_cols)]
-    after_x = lax.ppermute(edge_x, axes, between([((k, j), (k - 1, j)) for k, j in every if k]))
+    after_x = hand_on(
+        lax.ppermute(edge_x, axes, between([((k, j), (k - 1, j)) for k, j in every if k])), KEEP_COST
+    )
     after_y = lax.ppermute(edge_y, axes, between([((k, j), (k, j - 1)) for k, j in every if j]))
 
     half = shaped(2, 2, size_x, size_y, cells_z)

time: 65.4 us -> 65.5 us (level)
  waiting for transfers between devices: 30.4 us -> 31.7 us
    ppermute x1, waiting for transfers between devices: 2.33 us -> 4.37 us  [body(): lax.ppermute(edge_y, axes, between([((k, j), (k, j - 1)) for k, j in ever...]
    ppermute x6, waiting for transfers between devices: 0.69 us -> 0.02 us  [body(): trace_y1 = lax.ppermute(outs1[1], axes, along_y)]
  transfers between devices with their start and end apart: 24 -> 24, of which waited for: 4 -> 3; matrix products, arithmetic and copies ran while one was open for 0% -> 0% of each run, Pallas kernels for 13% -> 13%
where the time goes in v13:
time: 65.5 us; the launch traced here: 65.1 us
  waiting for transfers between devices  31.7 us (48%)
  starting transfers between devices  20 us (31%)
  Pallas kernels  10.5 us (16%)
  between operations  1.54 us (2%)
  local copies, waits for them, and re-layouts  1.29 us (2%)
    ppermute x6, waiting for transfers between devices, body(): trace_y0 = hand_on(lax.ppermute(outs0[0], axes, along_y))  25.9 us
    pallas_call x14, Pallas kernels, solve(): pl.pallas_call(functools.partial(beat_kernel, tile, final), out_shape=(sh...  5.58 us
    ppermute x6, starting transfers between devices, body(): trace_y0 = hand_on(lax.ppermute(outs0[0], axes, along_y))  5.24 us
    ppermute x6, starting transfers between devices, body(): trace_y1 = lax.ppermute(outs1[1], axes, along_y)  5.24 us
    ppermute x6, starting transfers between devices, body(): trace_x = lax.ppermute(outs1[0], axes, along_x)  4.61 us
    ppermute x1, waiting for transfers between devices, body(): lax.ppermute(edge_y, axes, between([((k, j), (k, j - 1)) for k, j in ever...  4.37 us
    ppermute x1, starting transfers between devices, body(): lax.ppermute(edge_y, axes, between([((k, j), (k, j - 1)) for k, j in ever...  1.92 us
    ppermute x6, waiting for transfers between devices, body(): trace_x = lax.ppermute(outs1[0], axes, along_x)  1.32 us
  transfers between devices with their start and end apart: 24, of which 3 were waited for; matrix products, arithmetic and copies ran while one was open for 0% of the time, Pallas kernels for 13%

profile of v13, /device:TPU:29, one launch (start us, length us, event | category | flops | bytes accessed | tf_op | source)
XLA Modules:
  0.0 65.1 jit_solution(14282112605170613168)
XLA Ops:
  0.8 1.2 %dynamic-slice_bitcast_fusion = (f32[2,16,16,128]{3,2,1,0:T(8,128)S(1)}, f32[2,16,16,128]{3,2,1,0:T(8,128)S(1)}) fusion(f32[2,2,16,16,128]{4,3,2,1,0:T(8,128)} %param.8, s32[]{:T(128)S(6)} %select_n.73, s32[]{:T(128)S(6)} %select_n.72), kind=kLoop, calls=%fused_computation | loop fusion | bytes 1048584 | tf_op jit(solution)/shard_map/jit(dynamic_index_in_dim)/squeeze | solution.py:450
  1.9 0.7 %collective-permute-start = (f32[2,16,16,128]{3,2,1,0:T(8,128)S(1)}, f32[2,16,16,128]{3,2,1,0:T(8,128)S(1)}, u32[]{:S(2)}, u32[]{:S(2)}) collective-permute-start(f32[2,16,16,128]{3,2,1,0:T(8,128)S(1)} %get-tuple-element.135), channel_id=1, source_target_pairs={{0,4},{4,0},{1,5},{5,1},{2,6},{6,2},{3,7},{7,3},{8,12},{12,8},{9,1... | collective-permute-start | bytes 786440 | tf_op jit(solution)/shard_map/ppermute | solution.py:448
  2.7 0.1 collective-permute-start.1
  2.9 1.1 %prep.1 = (f32[256,256]{1,0:T(8,128)S(1)}, f32[2,256,128]{2,1,0:T(8,128)S(1)}, f32[2,256,128]{2,1,0:T(8,128)S(1)}, bf16[5,128,384]{2,1,0:T(8,128)(2,1)S(1)}) custom-call(f32[2,16,16,128]{3,2,1,0:T(8,128)S(1)} %get-tuple-element.134.right_ref, f32[16,16,128]{2,1,0:T(8,128)S(1)} %copy-done.2, s32[1,16]{1,0:T(1,128)S(1)} %and_select_fusion.2.place_ref, ...), custom_call_target="tpu_custom_call" | custom-call | flops 2000000000 | bytes 2000000 | tf_op jit(solution)/shard_map/prep/pallas_call | solution.py:464
  4.0 0.8 %prep_other.1 = (f32[2,256,256]{2,1,0:T(8,128)S(1)}, f32[2,2,256,128]{3,2,1,0:T(8,128)S(1)}) custom-call(s32[1]{0:T(128)} %bitcast.1.core_ref, s32[1]{0:T(128)} %bitcast.rhs_ref, f32[2,16,16,128]{3,2,1,0:T(8,128)S(1)} %collective-permute-done.swap_ref, f32[16,16,128]{2,1,0:T(8,128)S(1)} %collective-permute-done.1.slow_ref, ...), custom_call_target="tpu_custom_call" | custom-call | flops 2000000000 | bytes 2000000 | tf_op jit(solution)/shard_map/prep_other/pallas_call | solution.py:476
  4.8 0.1 upper.7
  4.9 0.7 %collective-permute-start.3 = (f32[32,256]{1,0:T(8,128)S(1)}, f32[32,256]{1,0:T(8,128)S(1)}, u32[]{:S(2)}, u32[]{:S(2)}) collective-permute-start(f32[32,256]{1,0:T(8,128)S(1)} %get-tuple-element.74), channel_id=1, source_target_pairs={{0,5},{4,1}} | collective-permute-start | bytes 98312 | tf_op jit(solution)/shard_map/ppermute | solution.py:526
  5.7 0.1 lower.7
  5.7 0.7 %collective-permute-start.2 = (f32[32,256]{1,0:T(8,128)S(1)}, f32[32,256]{1,0:T(8,128)S(1)}, u32[]{:S(2)}, u32[]{:S(2)}) collective-permute-start(f32[32,256]{1,0:T(8,128)S(1)} %get-tuple-element.73), channel_id=1, source_target_pairs={{0,12},{4,8}} | collective-permute-start | bytes 98312 | tf_op jit(solution)/shard_map/ppermute | solution.py:529
  6.4 0.7 %collective-permute-start.4 = (f32[32,256]{1,0:T(8,128)S(1)}, f32[32,256]{1,0:T(8,128)S(1)}, u32[]{:S(2)}, u32[]{:S(2)}) collective-permute-start(f32[32,256]{1,0:T(8,128)S(1)} %get-tuple-element.78), channel_id=1, source_target_pairs={{0,5},{4,1}} | collective-permute-start | bytes 98312 | tf_op jit(solution)/shard_map/ppermute | solution.py:531
  7.1 0.1 upper.8
  7.2 0.7 %collective-permute-start.6 = (f32[32,256]{1,0:T(8,128)S(1)}, f32[32,256]{1,0:T(8,128)S(1)}, u32[]{:S(2)}, u32[]{:S(2)}) collective-permute-start(f32[32,256]{1,0:T(8,128)S(1)} %get-tuple-element.82), channel_id=1, source_target_pairs={{1,6},{5,2},{8,13},{12,9}} | collective-permute-start | bytes 98312 | tf_op jit(solution)/shard_map/ppermute | solution.py:526
  7.9 0.1 lower.8
  8.0 0.7 %collective-permute-start.5 = (f32[32,256]{1,0:T(8,128)S(1)}, f32[32,256]{1,0:T(8,128)S(1)}, u32[]{:S(2)}, u32[]{:S(2)}) collective-permute-start(f32[32,256]{1,0:T(8,128)S(1)} %get-tuple-element.81), channel_id=1, source_target_pairs={{1,13},{5,9},{8,20},{12,16}} | collective-permute-start | bytes 98312 | tf_op jit(solution)/shard_map/ppermute | solution.py:529
  8.6 0.7 %collective-permute-start.7 = (f32[32,256]{1,0:T(8,128)S(1)}, f32[32,256]{1,0:T(8,128)S(1)}, u32[]{:S(2)}, u32[]{:S(2)}) collective-permute-start(f32[32,256]{1,0:T(8,128)S(1)} %get-tuple-element.86), channel_id=1, source_target_pairs={{1,6},{5,2},{8,13},{12,9}} | collective-permute-start | bytes 98312 | tf_op jit(solution)/shard_map/ppermute | solution.py:531
  9.3 0.1 upper.9
  9.4 0.7 %collective-permute-start.9 = (f32[32,256]{1,0:T(8,128)S(1)}, f32[32,256]{1,0:T(8,128)S(1)}, u32[]{:S(2)}, u32[]{:S(2)}) collective-permute-start(f32[32,256]{1,0:T(8,128)S(1)} %get-tuple-element.90), channel_id=1, source_target_pairs={{2,7},{6,3},{9,14},{13,10},{16,21},{20,17}} | collective-permute-start | bytes 98312 | tf_op jit(solution)/shard_map/ppermute | solution.py:526
  10.1 0.1 lower.9
  10.2 0.7 %collective-permute-start.8 = (f32[32,256]{1,0:T(8,128)S(1)}, f32[32,256]{1,0:T(8,128)S(1)}, u32[]{:S(2)}, u32[]{:S(2)}) collective-permute-start(f32[32,256]{1,0:T(8,128)S(1)} %get-tuple-element.89), channel_id=1, source_target_pairs={{2,14},{6,10},{9,21},{13,17},{16,28},{20,24}} | collective-permute-start | bytes 98312 | tf_op jit(solution)/shard_map/ppermute | solution.py:529
  10.9 0.7 %collective-permute-start.10 = (f32[32,256]{1,0:T(8,128)S(1)}, f32[32,256]{1,0:T(8,128)S(1)}, u32[]{:S(2)}, u32[]{:S(2)}) collective-permute-start(f32[32,256]{1,0:T(8,128)S(1)} %get-tuple-element.94), channel_id=1, source_target_pairs={{2,7},{6,3},{9,14},{13,10},{16,21},{20,17}} | collective-permute-start | bytes 98312 | tf_op jit(solution)/shard_map/ppermute | solution.py:531
  11.6 0.1 upper.10
  11.7 0.7 %collective-permute-start.12 = (f32[32,256]{1,0:T(8,128)S(1)}, f32[32,256]{1,0:T(8,128)S(1)}, u32[]{:S(2)}, u32[]{:S(2)}) collective-permute-start(f32[32,256]{1,0:T(8,128)S(1)} %get-tuple-element.98), channel_id=1, source_target_pairs={{10,15},{14,11},{17,22},{21,18},{24,29},{28,25}} | collective-permute-start | bytes 98312 | tf_op jit(solution)/shard_map/ppermute | solution.py:526
  12.3 0.3 lower.10
  12.6 0.7 %collective-permute-start.11 = (f32[32,256]{1,0:T(8,128)S(1)}, f32[32,256]{1,0:T(8,128)S(1)}, u32[]{:S(2)}, u32[]{:S(2)}) collective-permute-start(f32[32,256]{1,0:T(8,128)S(1)} %get-tuple-element.97), channel_id=1, source_target_pairs={{3,15},{7,11},{10,22},{14,18},{17,29},{21,25}} | collective-permute-start | bytes 98312 | tf_op jit(solution)/shard_map/ppermute | solution.py:529
  13.3 0.7 %collective-permute-start.13 = (f32[32,256]{1,0:T(8,128)S(1)}, f32[32,256]{1,0:T(8,128)S(1)}, u32[]{:S(2)}, u32[]{:S(2)}) collective-permute-start(f32[32,256]{1,0:T(8,128)S(1)} %get-tuple-element.102), channel_id=1, source_target_pairs={{10,15},{14,11},{17,22},{21,18},{24,29},{28,25}} | collective-permute-start | bytes 98312 | tf_op jit(solution)/shard_map/ppermute | solution.py:531
  14.0 0.1 upper.11
  14.1 1.3 %collective-permute-start.15 = (f32[32,256]{1,0:T(8,128)S(1)}, f32[32,256]{1,0:T(8,128)S(1)}, u32[]{:S(2)}, u32[]{:S(2)}) collective-permute-start(f32[32,256]{1,0:T(8,128)S(1)} %get-tuple-element.106), channel_id=1, source_target_pairs={{18,23},{22,19},{25,30},{29,26}} | collective-permute-start | bytes 98312 | tf_op jit(solution)/shard_map/ppermute | solution.py:526
  15.4 0.1 lower.11
  15.4 1.3 %collective-permute-start.14 = (f32[32,256]{1,0:T(8,128)S(1)}, f32[32,256]{1,0:T(8,128)S(1)}, u32[]{:S(2)}, u32[]{:S(2)}) collective-permute-start(f32[32,256]{1,0:T(8,128)S(1)} %get-tuple-element.105), channel_id=1, source_target_pairs={{11,23},{15,19},{18,30},{22,26}} | collective-permute-start | bytes 98312 | tf_op jit(solution)/shard_map/ppermute | solution.py:529
  16.8 1.3 %collective-permute-start.16 = (f32[32,256]{1,0:T(8,128)S(1)}, f32[32,256]{1,0:T(8,128)S(1)}, u32[]{:S(2)}, u32[]{:S(2)}) collective-permute-start(f32[32,256]{1,0:T(8,128)S(1)} %get-tuple-element.110), channel_id=1, source_target_pairs={{18,23},{22,19},{25,30},{29,26}} | collective-permute-start | bytes 98312 | tf_op jit(solution)/shard_map/ppermute | solution.py:531
  18.1 25.9 %collective-permute-done.15.in_ref = f32[32,256]{1,0:T(8,128)S(1)} collective-permute-done((f32[32,256]{1,0:T(8,128)S(1)}, f32[32,256]{1,0:T(8,128)S(1)}, u32[]{:S(2)}, u32[]{:S(2)}) %collective-permute-start.15) | collective-permute-done | bytes 32800 | tf_op jit(solution)/shard_map/ppermute | solution.py:526
  44.0 1.3 %collective-permute-done.14.trace_x_ref = f32[32,256]{1,0:T(8,128)S(1)} collective-permute-done((f32[32,256]{1,0:T(8,128)S(1)}, f32[32,256]{1,0:T(8,128)S(1)}, u32[]{:S(2)}, u32[]{:S(2)}) %collective-permute-start.14) | collective-permute-done | bytes 32800 | tf_op jit(solution)/shard_map/ppermute | solution.py:529
  45.3 2.1 %upper.12 = (f32[256,256]{1,0:T(8,128)S(1)}, f32[256,256]{1,0:T(8,128)S(1)}, f32[32,256]{1,0:T(8,128)S(1)}, f32[32,256]{1,0:T(8,128)S(1)}) custom-call(s32[1]{0:T(128)} %bitcast.9.active_ref, f32[2,256,256]{2,1,0:T(8,128)S(1)} %get-tuple-element.69.modes_ref, ...), custom_call_target="tpu_custom_call", output_to_operand_aliasing={{0}: (5, {}), {1}: (6, {})} | custom-call | flops 2000000000 | bytes 2000000 | tf_op jit(solution)/shard_map/upper/pallas_call | solution.py:491
  47.3 1.3 %collective-permute-start.18 = (f32[32,256]{1,0:T(8,128)S(1)}, f32[32,256]{1,0:T(8,128)S(1)}, u32[]{:S(2)}, u32[]{:S(2)}) collective-permute-start(f32[32,256]{1,0:T(8,128)S(1)} %get-tuple-element.114), channel_id=1, source_target_pairs={{26,31},{30,27}} | collective-permute-start | bytes 98312 | tf_op jit(solution)/shard_map/ppermute | solution.py:526
  48.7 2.1 %lower.12 = (f32[256,256]{1,0:T(8,128)S(1)}, f32[256,256]{1,0:T(8,128)S(1)}, f32[32,256]{1,0:T(8,128)S(1)}, f32[32,256]{1,0:T(8,128)S(1)}) custom-call(s32[1]{0:T(128)} %bitcast.9.active_ref, f32[2,256,256]{2,1,0:T(8,128)S(1)} %get-tuple-element.69.modes_ref, ...), custom_call_target="tpu_custom_call", output_to_operand_aliasing={{0}: (5, {}), {1}: (6, {})} | custom-call | flops 2000000000 | bytes 2000000 | tf_op jit(solution)/shard_map/lower/pallas_call | solution.py:491
  50.7 0.7 %collective-permute-start.17 = (f32[32,256]{1,0:T(8,128)S(1)}, f32[32,256]{1,0:T(8,128)S(1)}, u32[]{:S(2)}, u32[]{:S(2)}) collective-permute-start(f32[32,256]{1,0:T(8,128)S(1)} %get-tuple-element.113), channel_id=1, source_target_pairs={{19,31},{23,27}} | collective-permute-start | bytes 98312 | tf_op jit(solution)/shard_map/ppermute | solution.py:529
  51.4 1.3 %collective-permute-start.19 = (f32[32,256]{1,0:T(8,128)S(1)}, f32[32,256]{1,0:T(8,128)S(1)}, u32[]{:S(2)}, u32[]{:S(2)}) collective-permute-start(f32[32,256]{1,0:T(8,128)S(1)} %get-tuple-element.120), channel_id=1, source_target_pairs={{26,31},{30,27}} | collective-permute-start | bytes 98312 | tf_op jit(solution)/shard_map/ppermute | solution.py:531
  52.8 0.3 upper.13
  53.0 1.3 %collective-permute-start.21 = (f32[32,256]{1,0:T(8,128)S(1)}, f32[32,256]{1,0:T(8,128)S(1)}, u32[]{:S(2)}, u32[]{:S(2)}) collective-permute-start(f32[32,256]{1,0:T(8,128)S(1)} %get-tuple-element.127), channel_id=1, source_target_pairs={{8,4},{12,0},{9,5},{13,1},{10,6},{14,2},{11,7},{15,3},{16,12},{20,... | collective-permute-start | bytes 98312 | tf_op jit(solution)/shard_map/ppermute | solution.py:537
  54.3 0.3 lower.13
  54.6 1.9 %collective-permute-start.22 = (f32[2,32,256]{2,1,0:T(8,128)S(1)}, f32[2,32,256]{2,1,0:T(8,128)S(1)}, u32[]{:S(2)}, u32[]{:S(2)}) collective-permute-start(f32[2,32,256]{2,1,0:T(8,128)S(1)} %pad_maximum_fusion), channel_id=1, source_target_pairs={{1,4},{5,0},{2,5},{6,1},{3,6},{7,2},{9,12},{13,8},{10,13},{14,9},{... | collective-permute-start | bytes 196616 | tf_op jit(solution)/shard_map/ppermute | solution.py:539
  56.6 1.1 %finish.1 = (f32[2,2,16,16,128]{4,3,2,1,0:T(8,128)S(1)}, f32[2,2,16,16,128]{4,3,2,1,0:T(8,128)S(1)}) custom-call(s32[1]{0:T(128)} %bitcast.1.core_ref, f32[256,256]{1,0:T(8,128)S(1)} %get-tuple-element.117.total0_ref, f32[256,256]{1,0:T(8,128)S(1)} %get-tuple-element.118.term0_ref, f32[256,256]{1,0:T(8,128)S(1)} %get-tuple-element.123.total1_ref, ...), custom_call_target="tpu_custom_call" | custom-call | tf_op jit(solution)/shard_map/finish/pallas_call | solution.py:542
  57.7 0.4 collective-permute-start.20
  58.2 4.4 %collective-permute-done.22.edge_y_ref = f32[2,32,256]{2,1,0:T(8,128)S(1)} collective-permute-done((f32[2,32,256]{2,1,0:T(8,128)S(1)}, f32[2,32,256]{2,1,0:T(8,128)S(1)}, u32[]{:S(2)}, u32[]{:S(2)}) %collective-permute-start.22) | collective-permute-done | bytes 65568 | tf_op jit(solution)/shard_map/ppermute | solution.py:539
  62.5 0.5 collective-permute-start.23
  63.0 0.2 keep.1.keep_rest_ref
  63.2 0.8 %place_wave.1 = f32[2,2,16,16,128]{4,3,2,1,0:T(8,128)} custom-call(s32[1]{0:T(128)} %bitcast.rhs_ref, f32[2,2,16,16,128]{4,3,2,1,0:T(8,128)S(1)} %get-tuple-element.125.keep_ref, f32[2,2,16,16,128]{4,3,2,1,0:T(8,128)S(1)} %collective-permute-done.20.got_ref), custom_call_target="tpu_custom_call" | custom-call | flops 10000000000 | bytes 1000000 | tf_op jit(solution)/shard_map/place_wave/pallas_call | solution.py:564
  64.0 0.9 %place_rest.1 = f32[2,2,16,16,128]{4,3,2,1,0:T(8,128)} custom-call(s32[1]{0:T(128)} %bitcast.1.core_ref, s32[1]{0:T(128)} %bitcast.rhs_ref, f32[2,16,16,128]{3,2,1,0:T(8,128)S(1)} %keep.1.keep_rest_ref, f32[2,2,16,16,128]{4,3,2,1,0:T(8,128)S(1)} %collective-permute-done.20.got_ref, f32[64,256]{1,0:T(8,128)S(1)} %collective-permute-done.23.got_edge_ref, ...), custom_call_target="tpu_custom_call" | custom-call | tf_op jit(solution)/shard_map/place_rest/pallas_call | solution.py:574
  (54 shorter events, 0.3 us)
Async XLA Ops:
  0.6 2.2 %copy-start = (f32[2,16,2]{1,2,0:T(2,128)S(1)}, f32[2,16,2]{1,2,0:T(2,128)}, u32[]{:S(2)}) copy-start(f32[2,16,2]{1,2,0:T(2,128)} %param.11) | copy-start | bytes 772
  0.7 2.2 %copy-start.4 = (f32[256,128]{1,0:T(8,128)S(1)}, f32[256,128]{1,0:T(8,128)}, u32[]{:S(2)}) copy-start(f32[256,128]{1,0:T(8,128)} %constant.150.clone.refs_0_) | copy-start | bytes 393220
  0.7 2.0 %copy-start.6 = (s32[2,16]{1,0:T(2,128)S(1)}, s32[2,16]{1,0:T(2,128)}, u32[]{:S(2)}) copy-start(s32[2,16]{1,0:T(2,128)} %param.10) | copy-start | bytes 388
  0.7 1.9 %copy-start.2 = (f32[16,16,128]{2,1,0:T(8,128)S(1)}, f32[16,16,128]{2,1,0:T(8,128)}, u32[]{:S(2)}) copy-start(f32[16,16,128]{2,1,0:T(8,128)} %slow_ref.1) | copy-start | bytes 393220
  0.7 2.1 %copy-start.1 = (bf16[4,128,384]{2,1,0:T(8,128)(2,1)S(1)}, bf16[4,128,384]{2,1,0:T(8,128)(2,1)}, u32[]{:S(2)}) copy-start(bf16[4,128,384]{2,1,0:T(8,128)(2,1)} %constant.152.clone.refs_1_.z_ref) | copy-start | bytes 1179652
  0.7 2.1 %copy-start.3 = (bf16[5,128,384]{2,1,0:T(8,128)(2,1)S(1)}, bf16[5,128,384]{2,1,0:T(8,128)(2,1)}, u32[]{:S(2)}) copy-start(bf16[5,128,384]{2,1,0:T(8,128)(2,1)} %constant.153.clone.refs_2_) | copy-start | bytes 1474564
  1.9 2.1 %collective-permute-start = (f32[2,16,16,128]{3,2,1,0:T(8,128)S(1)}, f32[2,16,16,128]{3,2,1,0:T(8,128)S(1)}, u32[]{:S(2)}, u32[]{:S(2)}) collective-permute-start(f32[2,16,16,128]{3,2,1,0:T(8,128)S(1)} %get-tuple-element.135), channel_id=1, source_target_pairs={{0,4},{4,0},{1,5},{5,1},{2,6},{6,2},{3,7},{7,3},{8,12},{12,8},{9,1... | collective-permute-start | bytes 786440 | tf_op jit(solution)/shard_map/ppermute | solution.py:448
  2.7 1.3 %collective-permute-start.1 = (f32[16,16,128]{2,1,0:T(8,128)S(1)}, f32[16,16,128]{2,1,0:T(8,128)S(1)}, u32[]{:S(2)}, u32[]{:S(2)}) collective-permute-start(f32[16,16,128]{2,1,0:T(8,128)S(1)} %copy-done.2), channel_id=1, source_target_pairs={{0,4},{4,0},{1,5},{5,1},{2,6},{6,2},{3,7},{7,3},{8,12},{12,8},{9,1... | collective-permute-start | bytes 393224 | tf_op jit(solution)/shard_map/ppermute | solution.py:449
  4.9 2.2 %collective-permute-start.3 = (f32[32,256]{1,0:T(8,128)S(1)}, f32[32,256]{1,0:T(8,128)S(1)}, u32[]{:S(2)}, u32[]{:S(2)}) collective-permute-start(f32[32,256]{1,0:T(8,128)S(1)} %get-tuple-element.74), channel_id=1, source_target_pairs={{0,5},{4,1}} | collective-permute-start | bytes 98312 | tf_op jit(solution)/shard_map/ppermute | solution.py:526
  5.7 1.4 %collective-permute-start.2 = (f32[32,256]{1,0:T(8,128)S(1)}, f32[32,256]{1,0:T(8,128)S(1)}, u32[]{:S(2)}, u32[]{:S(2)}) collective-permute-start(f32[32,256]{1,0:T(8,128)S(1)} %get-tuple-element.73), channel_id=1, source_target_pairs={{0,12},{4,8}} | collective-permute-start | bytes 98312 | tf_op jit(solution)/shard_map/ppermute | solution.py:529
  6.4 1.5 %collective-permute-start.4 = (f32[32,256]{1,0:T(8,128)S(1)}, f32[32,256]{1,0:T(8,128)S(1)}, u32[]{:S(2)}, u32[]{:S(2)}) collective-permute-start(f32[32,256]{1,0:T(8,128)S(1)} %get-tuple-element.78), channel_id=1, source_target_pairs={{0,5},{4,1}} | collective-permute-start | bytes 98312 | tf_op jit(solution)/shard_map/ppermute | solution.py:531
  7.2 2.1 %collective-permute-start.6 = (f32[32,256]{1,0:T(8,128)S(1)}, f32[32,256]{1,0:T(8,128)S(1)}, u32[]{:S(2)}, u32[]{:S(2)}) collective-permute-start(f32[32,256]{1,0:T(8,128)S(1)} %get-tuple-element.82), channel_id=1, source_target_pairs={{1,6},{5,2},{8,13},{12,9}} | collective-permute-start | bytes 98312 | tf_op jit(solution)/shard_map/ppermute | solution.py:526
  8.0 1.4 %collective-permute-start.5 = (f32[32,256]{1,0:T(8,128)S(1)}, f32[32,256]{1,0:T(8,128)S(1)}, u32[]{:S(2)}, u32[]{:S(2)}) collective-permute-start(f32[32,256]{1,0:T(8,128)S(1)} %get-tuple-element.81), channel_id=1, source_target_pairs={{1,13},{5,9},{8,20},{12,16}} | collective-permute-start | bytes 98312 | tf_op jit(solution)/shard_map/ppermute | solution.py:529
  8.6 1.5 %collective-permute-start.7 = (f32[32,256]{1,0:T(8,128)S(1)}, f32[32,256]{1,0:T(8,128)S(1)}, u32[]{:S(2)}, u32[]{:S(2)}) collective-permute-start(f32[32,256]{1,0:T(8,128)S(1)} %get-tuple-element.86), channel_id=1, source_target_pairs={{1,6},{5,2},{8,13},{12,9}} | collective-permute-start | bytes 98312 | tf_op jit(solution)/shard_map/ppermute | solution.py:531
  9.4 2.1 %collective-permute-start.9 = (f32[32,256]{1,0:T(8,128)S(1)}, f32[32,256]{1,0:T(8,128)S(1)}, u32[]{:S(2)}, u32[]{:S(2)}) collective-permute-start(f32[32,256]{1,0:T(8,128)S(1)} %get-tuple-element.90), channel_id=1, source_target_pairs={{2,7},{6,3},{9,14},{13,10},{16,21},{20,17}} | collective-permute-start | bytes 98312 | tf_op jit(solution)/shard_map/ppermute | solution.py:526
  10.2 1.4 %collective-permute-start.8 = (f32[32,256]{1,0:T(8,128)S(1)}, f32[32,256]{1,0:T(8,128)S(1)}, u32[]{:S(2)}, u32[]{:S(2)}) collective-permute-start(f32[32,256]{1,0:T(8,128)S(1)} %get-tuple-element.89), channel_id=1, source_target_pairs={{2,14},{6,10},{9,21},{13,17},{16,28},{20,24}} | collective-permute-start | bytes 98312 | tf_op jit(solution)/shard_map/ppermute | solution.py:529
  10.9 1.5 %collective-permute-start.10 = (f32[32,256]{1,0:T(8,128)S(1)}, f32[32,256]{1,0:T(8,128)S(1)}, u32[]{:S(2)}, u32[]{:S(2)}) collective-permute-start(f32[32,256]{1,0:T(8,128)S(1)} %get-tuple-element.94), channel_id=1, source_target_pairs={{2,7},{6,3},{9,14},{13,10},{16,21},{20,17}} | collective-permute-start | bytes 98312 | tf_op jit(solution)/shard_map/ppermute | solution.py:531
  11.7 2.3 %collective-permute-start.12 = (f32[32,256]{1,0:T(8,128)S(1)}, f32[32,256]{1,0:T(8,128)S(1)}, u32[]{:S(2)}, u32[]{:S(2)}) collective-permute-start(f32[32,256]{1,0:T(8,128)S(1)} %get-tuple-element.98), channel_id=1, source_target_pairs={{10,15},{14,11},{17,22},{21,18},{24,29},{28,25}} | collective-permute-start | bytes 98312 | tf_op jit(solution)/shard_map/ppermute | solution.py:526
  12.6 1.4 %collective-permute-start.11 = (f32[32,256]{1,0:T(8,128)S(1)}, f32[32,256]{1,0:T(8,128)S(1)}, u32[]{:S(2)}, u32[]{:S(2)}) collective-permute-start(f32[32,256]{1,0:T(8,128)S(1)} %get-tuple-element.97), channel_id=1, source_target_pairs={{3,15},{7,11},{10,22},{14,18},{17,29},{21,25}} | collective-permute-start | bytes 98312 | tf_op jit(solution)/shard_map/ppermute | solution.py:529
  13.3 2.1 %collective-permute-start.13 = (f32[32,256]{1,0:T(8,128)S(1)}, f32[32,256]{1,0:T(8,128)S(1)}, u32[]{:S(2)}, u32[]{:S(2)}) collective-permute-start(f32[32,256]{1,0:T(8,128)S(1)} %get-tuple-element.102), channel_id=1, source_target_pairs={{10,15},{14,11},{17,22},{21,18},{24,29},{28,25}} | collective-permute-start | bytes 98312 | tf_op jit(solution)/shard_map/ppermute | solution.py:531
  14.1 29.9 %collective-permute-start.15 = (f32[32,256]{1,0:T(8,128)S(1)}, f32[32,256]{1,0:T(8,128)S(1)}, u32[]{:S(2)}, u32[]{:S(2)}) collective-permute-start(f32[32,256]{1,0:T(8,128)S(1)} %get-tuple-element.106), channel_id=1, source_target_pairs={{18,23},{22,19},{25,30},{29,26}} | collective-permute-start | bytes 98312 | tf_op jit(solution)/shard_map/ppermute | solution.py:526
  15.4 29.8 %collective-permute-start.14 = (f32[32,256]{1,0:T(8,128)S(1)}, f32[32,256]{1,0:T(8,128)S(1)}, u32[]{:S(2)}, u32[]{:S(2)}) collective-permute-start(f32[32,256]{1,0:T(8,128)S(1)} %get-tuple-element.105), channel_id=1, source_target_pairs={{11,23},{15,19},{18,30},{22,26}} | collective-permute-start | bytes 98312 | tf_op jit(solution)/shard_map/ppermute | solution.py:529
  16.8 31.9 %collective-permute-start.16 = (f32[32,256]{1,0:T(8,128)S(1)}, f32[32,256]{1,0:T(8,128)S(1)}, u32[]{:S(2)}, u32[]{:S(2)}) collective-permute-start(f32[32,256]{1,0:T(8,128)S(1)} %get-tuple-element.110), channel_id=1, source_target_pairs={{18,23},{22,19},{25,30},{29,26}} | collective-permute-start | bytes 98312 | tf_op jit(solution)/shard_map/ppermute | solution.py:531
  47.3 5.4 %collective-permute-start.18 = (f32[32,256]{1,0:T(8,128)S(1)}, f32[32,256]{1,0:T(8,128)S(1)}, u32[]{:S(2)}, u32[]{:S(2)}) collective-permute-start(f32[32,256]{1,0:T(8,128)S(1)} %get-tuple-element.114), channel_id=1, source_target_pairs={{26,31},{30,27}} | collective-permute-start | bytes 98312 | tf_op jit(solution)/shard_map/ppermute | solution.py:526
  48.6 4.1 %copy-start.5 = (bf16[64,768]{1,0:T(8,128)(2,1)S(1)}, bf16[64,768]{1,0:T(8,128)(2,1)}, u32[]{:S(2)}) copy-start(bf16[64,768]{1,0:T(8,128)(2,1)} %constant.151.clone.refs_3_) | copy-start | bytes 294916
  50.7 2.0 %collective-permute-start.17 = (f32[32,256]{1,0:T(8,128)S(1)}, f32[32,256]{1,0:T(8,128)S(1)}, u32[]{:S(2)}, u32[]{:S(2)}) collective-permute-start(f32[32,256]{1,0:T(8,128)S(1)} %get-tuple-element.113), channel_id=1, source_target_pairs={{19,31},{23,27}} | collective-permute-start | bytes 98312 | tf_op jit(solution)/shard_map/ppermute | solution.py:529
  51.4 2.9 %collective-permute-start.19 = (f32[32,256]{1,0:T(8,128)S(1)}, f32[32,256]{1,0:T(8,128)S(1)}, u32[]{:S(2)}, u32[]{:S(2)}) collective-permute-start(f32[32,256]{1,0:T(8,128)S(1)} %get-tuple-element.120), channel_id=1, source_target_pairs={{26,31},{30,27}} | collective-permute-start | bytes 98312 | tf_op jit(solution)/shard_map/ppermute | solution.py:531
  53.0 5.1 %collective-permute-start.21 = (f32[32,256]{1,0:T(8,128)S(1)}, f32[32,256]{1,0:T(8,128)S(1)}, u32[]{:S(2)}, u32[]{:S(2)}) collective-permute-start(f32[32,256]{1,0:T(8,128)S(1)} %get-tuple-element.127), channel_id=1, source_target_pairs={{8,4},{12,0},{9,5},{13,1},{10,6},{14,2},{11,7},{15,3},{16,12},{20,... | collective-permute-start | bytes 98312 | tf_op jit(solution)/shard_map/ppermute | solution.py:537
  54.6 7.9 %collective-permute-start.22 = (f32[2,32,256]{2,1,0:T(8,128)S(1)}, f32[2,32,256]{2,1,0:T(8,128)S(1)}, u32[]{:S(2)}, u32[]{:S(2)}) collective-permute-start(f32[2,32,256]{2,1,0:T(8,128)S(1)} %pad_maximum_fusion), channel_id=1, source_target_pairs={{1,4},{5,0},{2,5},{6,1},{3,6},{7,2},{9,12},{13,8},{10,13},{14,9},{... | collective-permute-start | bytes 196616 | tf_op jit(solution)/shard_map/ppermute | solution.py:539
  57.7 5.5 %collective-permute-start.20 = (f32[2,2,16,16,128]{4,3,2,1,0:T(8,128)S(1)}, f32[2,2,16,16,128]{4,3,2,1,0:T(8,128)S(1)}, u32[]{:S(2)}, u32[]{:S(2)}) collective-permute-start(f32[2,2,16,16,128]{4,3,2,1,0:T(8,128)S(1)} %get-tuple-element.126), channel_id=1, source_target_pairs={{0,4},{4,0},{1,5},{5,1},{2,6},{6,2},{3,7},{7,3},{8,12},{12,8},{9,1... | collective-permute-start | bytes 1572872 | tf_op jit(solution)/shard_map/ppermute | solution.py:551
  62.5 1.5 %collective-permute-start.23 = (f32[64,256]{1,0:T(8,128)S(1)}, f32[64,256]{1,0:T(8,128)S(1)}, u32[]{:S(2)}, u32[]{:S(2)}) collective-permute-start(f32[64,256]{1,0:T(8,128)S(1)} %pad_maximum_fusion.1), channel_id=1, source_target_pairs={{0,4},{4,0},{1,5},{5,1},{2,6},{6,2},{3,7},{7,3},{8,12},{12,8},{9,1... | collective-permute-start | bytes 196616 | tf_op jit(solution)/shard_map/ppermute | solution.py:554

commit v14 on v13

--- a/solution.py
+++ b/solution.py
@@ -189,7 +189,7 @@
     )
 
 
-def apply_contrast(field, contrast, t, block=64):
+def apply_contrast(field, contrast, t, block=128):
     done = []
     for start in range(0, field.shape[0], block):
         here = slice(start, start + block)

time: 65.5 us -> 65.9 us (level)
  transfers between devices with their start and end apart: 24 -> 24, of which waited for: 3 -> 3; matrix products, arithmetic and copies ran while one was open for 0% -> 0% of each run, Pallas kernels for 13% -> 14%
where the time goes in v14:
time: 65.9 us; the launch traced here: 65.5 us
  waiting for transfers between devices  32 us (49%)
  starting transfers between devices  20 us (30%)
  Pallas kernels  10.6 us (16%)
  between operations  1.54 us (2%)
  local copies, waits for them, and re-layouts  1.29 us (2%)
    ppermute x6, waiting for transfers between devices, body(): trace_y0 = hand_on(lax.ppermute(outs0[0], axes, along_y))  26.3 us
    pallas_call x14, Pallas kernels, solve(): pl.pallas_call(functools.partial(beat_kernel, tile, final), out_shape=(sh...  5.66 us
    ppermute x6, starting transfers between devices, body(): trace_y0 = hand_on(lax.ppermute(outs0[0], axes, along_y))  5.24 us
    ppermute x6, starting transfers between devices, body(): trace_y1 = lax.ppermute(outs1[1], axes, along_y)  5.24 us
    ppermute x6, starting transfers between devices, body(): trace_x = lax.ppermute(outs1[0], axes, along_x)  4.61 us
    ppermute x1, waiting for transfers between devices, body(): lax.ppermute(edge_y, axes, between([((k, j), (k, j - 1)) for k, j in ever...  4.38 us
    ppermute x1, starting transfers between devices, body(): lax.ppermute(edge_y, axes, between([((k, j), (k, j - 1)) for k, j in ever...  1.92 us
  transfers between devices with their start and end apart: 24, of which 3 were waited for; matrix products, arithmetic and copies ran while one was open for 0% of the time, Pallas kernels for 14%

profile of v14, /device:TPU:29, one launch (start us, length us, event | category | flops | bytes accessed | tf_op | source)
XLA Modules:
  0.0 65.5 jit_solution(16865690825129388099)
XLA Ops:
  0.8 1.2 %dynamic-slice_bitcast_fusion = (f32[2,16,16,128]{3,2,1,0:T(8,128)S(1)}, f32[2,16,16,128]{3,2,1,0:T(8,128)S(1)}) fusion(f32[2,2,16,16,128]{4,3,2,1,0:T(8,128)} %param.8, s32[]{:T(128)S(6)} %select_n.73, s32[]{:T(128)S(6)} %select_n.72), kind=kLoop, calls=%fused_computation | loop fusion | bytes 1048584 | tf_op jit(solution)/shard_map/jit(dynamic_index_in_dim)/squeeze | solution.py:450
  1.9 0.7 %collective-permute-start = (f32[2,16,16,128]{3,2,1,0:T(8,128)S(1)}, f32[2,16,16,128]{3,2,1,0:T(8,128)S(1)}, u32[]{:S(2)}, u32[]{:S(2)}) collective-permute-start(f32[2,16,16,128]{3,2,1,0:T(8,128)S(1)} %get-tuple-element.135), channel_id=1, source_target_pairs={{0,4},{4,0},{1,5},{5,1},{2,6},{6,2},{3,7},{7,3},{8,12},{12,8},{9,1... | collective-permute-start | bytes 786440 | tf_op jit(solution)/shard_map/ppermute | solution.py:448
  2.7 0.1 collective-permute-start.1
  2.9 1.1 %prep.1 = (f32[256,256]{1,0:T(8,128)S(1)}, f32[2,256,128]{2,1,0:T(8,128)S(1)}, f32[2,256,128]{2,1,0:T(8,128)S(1)}, bf16[5,128,384]{2,1,0:T(8,128)(2,1)S(1)}) custom-call(f32[2,16,16,128]{3,2,1,0:T(8,128)S(1)} %get-tuple-element.134.right_ref, f32[16,16,128]{2,1,0:T(8,128)S(1)} %copy-done.2, s32[1,16]{1,0:T(1,128)S(1)} %and_select_fusion.2.place_ref, ...), custom_call_target="tpu_custom_call" | custom-call | flops 2000000000 | bytes 2000000 | tf_op jit(solution)/shard_map/prep/pallas_call | solution.py:464
  4.0 0.8 %prep_other.1 = (f32[2,256,256]{2,1,0:T(8,128)S(1)}, f32[2,2,256,128]{3,2,1,0:T(8,128)S(1)}) custom-call(s32[1]{0:T(128)} %bitcast.1.core_ref, s32[1]{0:T(128)} %bitcast.rhs_ref, f32[2,16,16,128]{3,2,1,0:T(8,128)S(1)} %collective-permute-done.swap_ref, f32[16,16,128]{2,1,0:T(8,128)S(1)} %collective-permute-done.1.slow_ref, ...), custom_call_target="tpu_custom_call" | custom-call | flops 2000000000 | bytes 2000000 | tf_op jit(solution)/shard_map/prep_other/pallas_call | solution.py:476
  4.8 0.1 upper.7
  4.9 0.7 %collective-permute-start.3 = (f32[32,256]{1,0:T(8,128)S(1)}, f32[32,256]{1,0:T(8,128)S(1)}, u32[]{:S(2)}, u32[]{:S(2)}) collective-permute-start(f32[32,256]{1,0:T(8,128)S(1)} %get-tuple-element.74), channel_id=1, source_target_pairs={{0,5},{4,1}} | collective-permute-start | bytes 98312 | tf_op jit(solution)/shard_map/ppermute | solution.py:526
  5.7 0.1 lower.7
  5.7 0.7 %collective-permute-start.2 = (f32[32,256]{1,0:T(8,128)S(1)}, f32[32,256]{1,0:T(8,128)S(1)}, u32[]{:S(2)}, u32[]{:S(2)}) collective-permute-start(f32[32,256]{1,0:T(8,128)S(1)} %get-tuple-element.73), channel_id=1, source_target_pairs={{0,12},{4,8}} | collective-permute-start | bytes 98312 | tf_op jit(solution)/shard_map/ppermute | solution.py:529
  6.4 0.7 %collective-permute-start.4 = (f32[32,256]{1,0:T(8,128)S(1)}, f32[32,256]{1,0:T(8,128)S(1)}, u32[]{:S(2)}, u32[]{:S(2)}) collective-permute-start(f32[32,256]{1,0:T(8,128)S(1)} %get-tuple-element.78), channel_id=1, source_target_pairs={{0,5},{4,1}} | collective-permute-start | bytes 98312 | tf_op jit(solution)/shard_map/ppermute | solution.py:531
  7.1 0.1 upper.8
  7.2 0.7 %collective-permute-start.6 = (f32[32,256]{1,0:T(8,128)S(1)}, f32[32,256]{1,0:T(8,128)S(1)}, u32[]{:S(2)}, u32[]{:S(2)}) collective-permute-start(f32[32,256]{1,0:T(8,128)S(1)} %get-tuple-element.82), channel_id=1, source_target_pairs={{1,6},{5,2},{8,13},{12,9}} | collective-permute-start | bytes 98312 | tf_op jit(solution)/shard_map/ppermute | solution.py:526
  7.9 0.1 lower.8
  8.0 0.7 %collective-permute-start.5 = (f32[32,256]{1,0:T(8,128)S(1)}, f32[32,256]{1,0:T(8,128)S(1)}, u32[]{:S(2)}, u32[]{:S(2)}) collective-permute-start(f32[32,256]{1,0:T(8,128)S(1)} %get-tuple-element.81), channel_id=1, source_target_pairs={{1,13},{5,9},{8,20},{12,16}} | collective-permute-start | bytes 98312 | tf_op jit(solution)/shard_map/ppermute | solution.py:529
  8.6 0.7 %collective-permute-start.7 = (f32[32,256]{1,0:T(8,128)S(1)}, f32[32,256]{1,0:T(8,128)S(1)}, u32[]{:S(2)}, u32[]{:S(2)}) collective-permute-start(f32[32,256]{1,0:T(8,128)S(1)} %get-tuple-element.86), channel_id=1, source_target_pairs={{1,6},{5,2},{8,13},{12,9}} | collective-permute-start | bytes 98312 | tf_op jit(solution)/shard_map/ppermute | solution.py:531
  9.3 0.1 upper.9
  9.4 0.7 %collective-permute-start.9 = (f32[32,256]{1,0:T(8,128)S(1)}, f32[32,256]{1,0:T(8,128)S(1)}, u32[]{:S(2)}, u32[]{:S(2)}) collective-permute-start(f32[32,256]{1,0:T(8,128)S(1)} %get-tuple-element.90), channel_id=1, source_target_pairs={{2,7},{6,3},{9,14},{13,10},{16,21},{20,17}} | collective-permute-start | bytes 98312 | tf_op jit(solution)/shard_map/ppermute | solution.py:526
  10.1 0.1 lower.9
  10.2 0.7 %collective-permute-start.8 = (f32[32,256]{1,0:T(8,128)S(1)}, f32[32,256]{1,0:T(8,128)S(1)}, u32[]{:S(2)}, u32[]{:S(2)}) collective-permute-start(f32[32,256]{1,0:T(8,128)S(1)} %get-tuple-element.89), channel_id=1, source_target_pairs={{2,14},{6,10},{9,21},{13,17},{16,28},{20,24}} | collective-permute-start | bytes 98312 | tf_op jit(solution)/shard_map/ppermute | solution.py:529
  10.9 0.7 %collective-permute-start.10 = (f32[32,256]{1,0:T(8,128)S(1)}, f32[32,256]{1,0:T(8,128)S(1)}, u32[]{:S(2)}, u32[]{:S(2)}) collective-permute-start(f32[32,256]{1,0:T(8,128)S(1)} %get-tuple-element.94), channel_id=1, source_target_pairs={{2,7},{6,3},{9,14},{13,10},{16,21},{20,17}} | collective-permute-start | bytes 98312 | tf_op jit(solution)/shard_map/ppermute | solution.py:531
  11.6 0.1 upper.10
  11.7 0.7 %collective-permute-start.12 = (f32[32,256]{1,0:T(8,128)S(1)}, f32[32,256]{1,0:T(8,128)S(1)}, u32[]{:S(2)}, u32[]{:S(2)}) collective-permute-start(f32[32,256]{1,0:T(8,128)S(1)} %get-tuple-element.98), channel_id=1, source_target_pairs={{10,15},{14,11},{17,22},{21,18},{24,29},{28,25}} | collective-permute-start | bytes 98312 | tf_op jit(solution)/shard_map/ppermute | solution.py:526
  12.3 0.3 lower.10
  12.6 0.7 %collective-permute-start.11 = (f32[32,256]{1,0:T(8,128)S(1)}, f32[32,256]{1,0:T(8,128)S(1)}, u32[]{:S(2)}, u32[]{:S(2)}) collective-permute-start(f32[32,256]{1,0:T(8,128)S(1)} %get-tuple-element.97), channel_id=1, source_target_pairs={{3,15},{7,11},{10,22},{14,18},{17,29},{21,25}} | collective-permute-start | bytes 98312 | tf_op jit(solution)/shard_map/ppermute | solution.py:529
  13.3 0.7 %collective-permute-start.13 = (f32[32,256]{1,0:T(8,128)S(1)}, f32[32,256]{1,0:T(8,128)S(1)}, u32[]{:S(2)}, u32[]{:S(2)}) collective-permute-start(f32[32,256]{1,0:T(8,128)S(1)} %get-tuple-element.102), channel_id=1, source_target_pairs={{10,15},{14,11},{17,22},{21,18},{24,29},{28,25}} | collective-permute-start | bytes 98312 | tf_op jit(solution)/shard_map/ppermute | solution.py:531
  14.0 0.1 upper.11
  14.1 1.3 %collective-permute-start.15 = (f32[32,256]{1,0:T(8,128)S(1)}, f32[32,256]{1,0:T(8,128)S(1)}, u32[]{:S(2)}, u32[]{:S(2)}) collective-permute-start(f32[32,256]{1,0:T(8,128)S(1)} %get-tuple-element.106), channel_id=1, source_target_pairs={{18,23},{22,19},{25,30},{29,26}} | collective-permute-start | bytes 98312 | tf_op jit(solution)/shard_map/ppermute | solution.py:526
  15.4 0.1 lower.11
  15.4 1.3 %collective-permute-start.14 = (f32[32,256]{1,0:T(8,128)S(1)}, f32[32,256]{1,0:T(8,128)S(1)}, u32[]{:S(2)}, u32[]{:S(2)}) collective-permute-start(f32[32,256]{1,0:T(8,128)S(1)} %get-tuple-element.105), channel_id=1, source_target_pairs={{11,23},{15,19},{18,30},{22,26}} | collective-permute-start | bytes 98312 | tf_op jit(solution)/shard_map/ppermute | solution.py:529
  16.8 1.3 %collective-permute-start.16 = (f32[32,256]{1,0:T(8,128)S(1)}, f32[32,256]{1,0:T(8,128)S(1)}, u32[]{:S(2)}, u32[]{:S(2)}) collective-permute-start(f32[32,256]{1,0:T(8,128)S(1)} %get-tuple-element.110), channel_id=1, source_target_pairs={{18,23},{22,19},{25,30},{29,26}} | collective-permute-start | bytes 98312 | tf_op jit(solution)/shard_map/ppermute | solution.py:531
  18.1 26.3 %collective-permute-done.15.in_ref = f32[32,256]{1,0:T(8,128)S(1)} collective-permute-done((f32[32,256]{1,0:T(8,128)S(1)}, f32[32,256]{1,0:T(8,128)S(1)}, u32[]{:S(2)}, u32[]{:S(2)}) %collective-permute-start.15) | collective-permute-done | bytes 32800 | tf_op jit(solution)/shard_map/ppermute | solution.py:526
  44.3 1.3 %collective-permute-done.14.trace_x_ref = f32[32,256]{1,0:T(8,128)S(1)} collective-permute-done((f32[32,256]{1,0:T(8,128)S(1)}, f32[32,256]{1,0:T(8,128)S(1)}, u32[]{:S(2)}, u32[]{:S(2)}) %collective-permute-start.14) | collective-permute-done | bytes 32800 | tf_op jit(solution)/shard_map/ppermute | solution.py:529
  45.6 2.1 %upper.12 = (f32[256,256]{1,0:T(8,128)S(1)}, f32[256,256]{1,0:T(8,128)S(1)}, f32[32,256]{1,0:T(8,128)S(1)}, f32[32,256]{1,0:T(8,128)S(1)}) custom-call(s32[1]{0:T(128)} %bitcast.9.active_ref, f32[2,256,256]{2,1,0:T(8,128)S(1)} %get-tuple-element.69.modes_ref, ...), custom_call_target="tpu_custom_call", output_to_operand_aliasing={{0}: (5, {}), {1}: (6, {})} | custom-call | flops 2000000000 | bytes 2000000 | tf_op jit(solution)/shard_map/upper/pallas_call | solution.py:491
  47.7 1.3 %collective-permute-start.18 = (f32[32,256]{1,0:T(8,128)S(1)}, f32[32,256]{1,0:T(8,128)S(1)}, u32[]{:S(2)}, u32[]{:S(2)}) collective-permute-start(f32[32,256]{1,0:T(8,128)S(1)} %get-tuple-element.114), channel_id=1, source_target_pairs={{26,31},{30,27}} | collective-permute-start | bytes 98312 | tf_op jit(solution)/shard_map/ppermute | solution.py:526
  49.0 2.1 %lower.12 = (f32[256,256]{1,0:T(8,128)S(1)}, f32[256,256]{1,0:T(8,128)S(1)}, f32[32,256]{1,0:T(8,128)S(1)}, f32[32,256]{1,0:T(8,128)S(1)}) custom-call(s32[1]{0:T(128)} %bitcast.9.active_ref, f32[2,256,256]{2,1,0:T(8,128)S(1)} %get-tuple-element.69.modes_ref, ...), custom_call_target="tpu_custom_call", output_to_operand_aliasing={{0}: (5, {}), {1}: (6, {})} | custom-call | flops 2000000000 | bytes 2000000 | tf_op jit(solution)/shard_map/lower/pallas_call | solution.py:491
  51.1 0.7 %collective-permute-start.17 = (f32[32,256]{1,0:T(8,128)S(1)}, f32[32,256]{1,0:T(8,128)S(1)}, u32[]{:S(2)}, u32[]{:S(2)}) collective-permute-start(f32[32,256]{1,0:T(8,128)S(1)} %get-tuple-element.113), channel_id=1, source_target_pairs={{19,31},{23,27}} | collective-permute-start | bytes 98312 | tf_op jit(solution)/shard_map/ppermute | solution.py:529
  51.8 1.3 %collective-permute-start.19 = (f32[32,256]{1,0:T(8,128)S(1)}, f32[32,256]{1,0:T(8,128)S(1)}, u32[]{:S(2)}, u32[]{:S(2)}) collective-permute-start(f32[32,256]{1,0:T(8,128)S(1)} %get-tuple-element.120), channel_id=1, source_target_pairs={{26,31},{30,27}} | collective-permute-start | bytes 98312 | tf_op jit(solution)/shard_map/ppermute | solution.py:531
  53.2 0.3 upper.13
  53.5 1.3 %collective-permute-start.21 = (f32[32,256]{1,0:T(8,128)S(1)}, f32[32,256]{1,0:T(8,128)S(1)}, u32[]{:S(2)}, u32[]{:S(2)}) collective-permute-start(f32[32,256]{1,0:T(8,128)S(1)} %get-tuple-element.127), channel_id=1, source_target_pairs={{8,4},{12,0},{9,5},{13,1},{10,6},{14,2},{11,7},{15,3},{16,12},{20,... | collective-permute-start | bytes 98312 | tf_op jit(solution)/shard_map/ppermute | solution.py:537
  54.8 0.3 lower.13
  55.1 1.9 %collective-permute-start.22 = (f32[2,32,256]{2,1,0:T(8,128)S(1)}, f32[2,32,256]{2,1,0:T(8,128)S(1)}, u32[]{:S(2)}, u32[]{:S(2)}) collective-permute-start(f32[2,32,256]{2,1,0:T(8,128)S(1)} %pad_maximum_fusion), channel_id=1, source_target_pairs={{1,4},{5,0},{2,5},{6,1},{3,6},{7,2},{9,12},{13,8},{10,13},{14,9},{... | collective-permute-start | bytes 196616 | tf_op jit(solution)/shard_map/ppermute | solution.py:539
  57.0 1.1 %finish.1 = (f32[2,2,16,16,128]{4,3,2,1,0:T(8,128)S(1)}, f32[2,2,16,16,128]{4,3,2,1,0:T(8,128)S(1)}) custom-call(s32[1]{0:T(128)} %bitcast.1.core_ref, f32[256,256]{1,0:T(8,128)S(1)} %get-tuple-element.117.total0_ref, f32[256,256]{1,0:T(8,128)S(1)} %get-tuple-element.118.term0_ref, f32[256,256]{1,0:T(8,128)S(1)} %get-tuple-element.123.total1_ref, ...), custom_call_target="tpu_custom_call" | custom-call | tf_op jit(solution)/shard_map/finish/pallas_call | solution.py:542
  58.1 0.5 collective-permute-start.20
  58.6 4.4 %collective-permute-done.22.edge_y_ref = f32[2,32,256]{2,1,0:T(8,128)S(1)} collective-permute-done((f32[2,32,256]{2,1,0:T(8,128)S(1)}, f32[2,32,256]{2,1,0:T(8,128)S(1)}, u32[]{:S(2)}, u32[]{:S(2)}) %collective-permute-start.22) | collective-permute-done | bytes 65568 | tf_op jit(solution)/shard_map/ppermute | solution.py:539
  63.0 0.4 collective-permute-start.23
  63.4 0.2 keep.1.keep_rest_ref
  63.6 0.8 %place_wave.1 = f32[2,2,16,16,128]{4,3,2,1,0:T(8,128)} custom-call(s32[1]{0:T(128)} %bitcast.rhs_ref, f32[2,2,16,16,128]{4,3,2,1,0:T(8,128)S(1)} %get-tuple-element.125.keep_ref, f32[2,2,16,16,128]{4,3,2,1,0:T(8,128)S(1)} %collective-permute-done.20.got_ref), custom_call_target="tpu_custom_call" | custom-call | flops 10000000000 | bytes 1000000 | tf_op jit(solution)/shard_map/place_wave/pallas_call | solution.py:564
  64.5 0.9 %place_rest.1 = f32[2,2,16,16,128]{4,3,2,1,0:T(8,128)} custom-call(s32[1]{0:T(128)} %bitcast.1.core_ref, s32[1]{0:T(128)} %bitcast.rhs_ref, f32[2,16,16,128]{3,2,1,0:T(8,128)S(1)} %keep.1.keep_rest_ref, f32[2,2,16,16,128]{4,3,2,1,0:T(8,128)S(1)} %collective-permute-done.20.got_ref, f32[64,256]{1,0:T(8,128)S(1)} %collective-permute-done.23.got_edge_ref, ...), custom_call_target="tpu_custom_call" | custom-call | tf_op jit(solution)/shard_map/place_rest/pallas_call | solution.py:574
  (54 shorter events, 0.3 us)
Async XLA Ops:
  0.6 2.2 %copy-start = (f32[2,16,2]{1,2,0:T(2,128)S(1)}, f32[2,16,2]{1,2,0:T(2,128)}, u32[]{:S(2)}) copy-start(f32[2,16,2]{1,2,0:T(2,128)} %param.11) | copy-start | bytes 772
  0.7 2.2 %copy-start.4 = (f32[256,128]{1,0:T(8,128)S(1)}, f32[256,128]{1,0:T(8,128)}, u32[]{:S(2)}) copy-start(f32[256,128]{1,0:T(8,128)} %constant.150.clone.refs_0_) | copy-start | bytes 393220
  0.7 2.0 %copy-start.6 = (s32[2,16]{1,0:T(2,128)S(1)}, s32[2,16]{1,0:T(2,128)}, u32[]{:S(2)}) copy-start(s32[2,16]{1,0:T(2,128)} %param.10) | copy-start | bytes 388
  0.7 1.9 %copy-start.2 = (f32[16,16,128]{2,1,0:T(8,128)S(1)}, f32[16,16,128]{2,1,0:T(8,128)}, u32[]{:S(2)}) copy-start(f32[16,16,128]{2,1,0:T(8,128)} %slow_ref.1) | copy-start | bytes 393220
  0.7 2.1 %copy-start.1 = (bf16[4,128,384]{2,1,0:T(8,128)(2,1)S(1)}, bf16[4,128,384]{2,1,0:T(8,128)(2,1)}, u32[]{:S(2)}) copy-start(bf16[4,128,384]{2,1,0:T(8,128)(2,1)} %constant.152.clone.refs_1_.z_ref) | copy-start | bytes 1179652
  0.7 2.1 %copy-start.3 = (bf16[5,128,384]{2,1,0:T(8,128)(2,1)S(1)}, bf16[5,128,384]{2,1,0:T(8,128)(2,1)}, u32[]{:S(2)}) copy-start(bf16[5,128,384]{2,1,0:T(8,128)(2,1)} %constant.153.clone.refs_2_) | copy-start | bytes 1474564
  1.9 2.1 %collective-permute-start = (f32[2,16,16,128]{3,2,1,0:T(8,128)S(1)}, f32[2,16,16,128]{3,2,1,0:T(8,128)S(1)}, u32[]{:S(2)}, u32[]{:S(2)}) collective-permute-start(f32[2,16,16,128]{3,2,1,0:T(8,128)S(1)} %get-tuple-element.135), channel_id=1, source_target_pairs={{0,4},{4,0},{1,5},{5,1},{2,6},{6,2},{3,7},{7,3},{8,12},{12,8},{9,1... | collective-permute-start | bytes 786440 | tf_op jit(solution)/shard_map/ppermute | solution.py:448
  2.7 1.3 %collective-permute-start.1 = (f32[16,16,128]{2,1,0:T(8,128)S(1)}, f32[16,16,128]{2,1,0:T(8,128)S(1)}, u32[]{:S(2)}, u32[]{:S(2)}) collective-permute-start(f32[16,16,128]{2,1,0:T(8,128)S(1)} %copy-done.2), channel_id=1, source_target_pairs={{0,4},{4,0},{1,5},{5,1},{2,6},{6,2},{3,7},{7,3},{8,12},{12,8},{9,1... | collective-permute-start | bytes 393224 | tf_op jit(solution)/shard_map/ppermute | solution.py:449
  4.9 2.2 %collective-permute-start.3 = (f32[32,256]{1,0:T(8,128)S(1)}, f32[32,256]{1,0:T(8,128)S(1)}, u32[]{:S(2)}, u32[]{:S(2)}) collective-permute-start(f32[32,256]{1,0:T(8,128)S(1)} %get-tuple-element.74), channel_id=1, source_target_pairs={{0,5},{4,1}} | collective-permute-start | bytes 98312 | tf_op jit(solution)/shard_map/ppermute | solution.py:526
  5.7 1.4 %collective-permute-start.2 = (f32[32,256]{1,0:T(8,128)S(1)}, f32[32,256]{1,0:T(8,128)S(1)}, u32[]{:S(2)}, u32[]{:S(2)}) collective-permute-start(f32[32,256]{1,0:T(8,128)S(1)} %get-tuple-element.73), channel_id=1, source_target_pairs={{0,12},{4,8}} | collective-permute-start | bytes 98312 | tf_op jit(solution)/shard_map/ppermute | solution.py:529
  6.4 1.5 %collective-permute-start.4 = (f32[32,256]{1,0:T(8,128)S(1)}, f32[32,256]{1,0:T(8,128)S(1)}, u32[]{:S(2)}, u32[]{:S(2)}) collective-permute-start(f32[32,256]{1,0:T(8,128)S(1)} %get-tuple-element.78), channel_id=1, source_target_pairs={{0,5},{4,1}} | collective-permute-start | bytes 98312 | tf_op jit(solution)/shard_map/ppermute | solution.py:531
  7.2 2.1 %collective-permute-start.6 = (f32[32,256]{1,0:T(8,128)S(1)}, f32[32,256]{1,0:T(8,128)S(1)}, u32[]{:S(2)}, u32[]{:S(2)}) collective-permute-start(f32[32,256]{1,0:T(8,128)S(1)} %get-tuple-element.82), channel_id=1, source_target_pairs={{1,6},{5,2},{8,13},{12,9}} | collective-permute-start | bytes 98312 | tf_op jit(solution)/shard_map/ppermute | solution.py:526
  8.0 1.4 %collective-permute-start.5 = (f32[32,256]{1,0:T(8,128)S(1)}, f32[32,256]{1,0:T(8,128)S(1)}, u32[]{:S(2)}, u32[]{:S(2)}) collective-permute-start(f32[32,256]{1,0:T(8,128)S(1)} %get-tuple-element.81), channel_id=1, source_target_pairs={{1,13},{5,9},{8,20},{12,16}} | collective-permute-start | bytes 98312 | tf_op jit(solution)/shard_map/ppermute | solution.py:529
  8.6 1.5 %collective-permute-start.7 = (f32[32,256]{1,0:T(8,128)S(1)}, f32[32,256]{1,0:T(8,128)S(1)}, u32[]{:S(2)}, u32[]{:S(2)}) collective-permute-start(f32[32,256]{1,0:T(8,128)S(1)} %get-tuple-element.86), channel_id=1, source_target_pairs={{1,6},{5,2},{8,13},{12,9}} | collective-permute-start | bytes 98312 | tf_op jit(solution)/shard_map/ppermute | solution.py:531
  9.4 2.1 %collective-permute-start.9 = (f32[32,256]{1,0:T(8,128)S(1)}, f32[32,256]{1,0:T(8,128)S(1)}, u32[]{:S(2)}, u32[]{:S(2)}) collective-permute-start(f32[32,256]{1,0:T(8,128)S(1)} %get-tuple-element.90), channel_id=1, source_target_pairs={{2,7},{6,3},{9,14},{13,10},{16,21},{20,17}} | collective-permute-start | bytes 98312 | tf_op jit(solution)/shard_map/ppermute | solution.py:526
  10.2 1.4 %collective-permute-start.8 = (f32[32,256]{1,0:T(8,128)S(1)}, f32[32,256]{1,0:T(8,128)S(1)}, u32[]{:S(2)}, u32[]{:S(2)}) collective-permute-start(f32[32,256]{1,0:T(8,128)S(1)} %get-tuple-element.89), channel_id=1, source_target_pairs={{2,14},{6,10},{9,21},{13,17},{16,28},{20,24}} | collective-permute-start | bytes 98312 | tf_op jit(solution)/shard_map/ppermute | solution.py:529
  10.9 1.5 %collective-permute-start.10 = (f32[32,256]{1,0:T(8,128)S(1)}, f32[32,256]{1,0:T(8,128)S(1)}, u32[]{:S(2)}, u32[]{:S(2)}) collective-permute-start(f32[32,256]{1,0:T(8,128)S(1)} %get-tuple-element.94), channel_id=1, source_target_pairs={{2,7},{6,3},{9,14},{13,10},{16,21},{20,17}} | collective-permute-start | bytes 98312 | tf_op jit(solution)/shard_map/ppermute | solution.py:531
  11.7 2.3 %collective-permute-start.12 = (f32[32,256]{1,0:T(8,128)S(1)}, f32[32,256]{1,0:T(8,128)S(1)}, u32[]{:S(2)}, u32[]{:S(2)}) collective-permute-start(f32[32,256]{1,0:T(8,128)S(1)} %get-tuple-element.98), channel_id=1, source_target_pairs={{10,15},{14,11},{17,22},{21,18},{24,29},{28,25}} | collective-permute-start | bytes 98312 | tf_op jit(solution)/shard_map/ppermute | solution.py:526
  12.6 1.4 %collective-permute-start.11 = (f32[32,256]{1,0:T(8,128)S(1)}, f32[32,256]{1,0:T(8,128)S(1)}, u32[]{:S(2)}, u32[]{:S(2)}) collective-permute-start(f32[32,256]{1,0:T(8,128)S(1)} %get-tuple-element.97), channel_id=1, source_target_pairs={{3,15},{7,11},{10,22},{14,18},{17,29},{21,25}} | collective-permute-start | bytes 98312 | tf_op jit(solution)/shard_map/ppermute | solution.py:529
  13.3 2.1 %collective-permute-start.13 = (f32[32,256]{1,0:T(8,128)S(1)}, f32[32,256]{1,0:T(8,128)S(1)}, u32[]{:S(2)}, u32[]{:S(2)}) collective-permute-start(f32[32,256]{1,0:T(8,128)S(1)} %get-tuple-element.102), channel_id=1, source_target_pairs={{10,15},{14,11},{17,22},{21,18},{24,29},{28,25}} | collective-permute-start | bytes 98312 | tf_op jit(solution)/shard_map/ppermute | solution.py:531
  14.1 30.3 %collective-permute-start.15 = (f32[32,256]{1,0:T(8,128)S(1)}, f32[32,256]{1,0:T(8,128)S(1)}, u32[]{:S(2)}, u32[]{:S(2)}) collective-permute-start(f32[32,256]{1,0:T(8,128)S(1)} %get-tuple-element.106), channel_id=1, source_target_pairs={{18,23},{22,19},{25,30},{29,26}} | collective-permute-start | bytes 98312 | tf_op jit(solution)/shard_map/ppermute | solution.py:526
  15.4 30.2 %collective-permute-start.14 = (f32[32,256]{1,0:T(8,128)S(1)}, f32[32,256]{1,0:T(8,128)S(1)}, u32[]{:S(2)}, u32[]{:S(2)}) collective-permute-start(f32[32,256]{1,0:T(8,128)S(1)} %get-tuple-element.105), channel_id=1, source_target_pairs={{11,23},{15,19},{18,30},{22,26}} | collective-permute-start | bytes 98312 | tf_op jit(solution)/shard_map/ppermute | solution.py:529
  16.8 32.3 %collective-permute-start.16 = (f32[32,256]{1,0:T(8,128)S(1)}, f32[32,256]{1,0:T(8,128)S(1)}, u32[]{:S(2)}, u32[]{:S(2)}) collective-permute-start(f32[32,256]{1,0:T(8,128)S(1)} %get-tuple-element.110), channel_id=1, source_target_pairs={{18,23},{22,19},{25,30},{29,26}} | collective-permute-start | bytes 98312 | tf_op jit(solution)/shard_map/ppermute | solution.py:531
  47.7 5.4 %collective-permute-start.18 = (f32[32,256]{1,0:T(8,128)S(1)}, f32[32,256]{1,0:T(8,128)S(1)}, u32[]{:S(2)}, u32[]{:S(2)}) collective-permute-start(f32[32,256]{1,0:T(8,128)S(1)} %get-tuple-element.114), channel_id=1, source_target_pairs={{26,31},{30,27}} | collective-permute-start | bytes 98312 | tf_op jit(solution)/shard_map/ppermute | solution.py:526
  49.0 4.1 %copy-start.5 = (bf16[64,768]{1,0:T(8,128)(2,1)S(1)}, bf16[64,768]{1,0:T(8,128)(2,1)}, u32[]{:S(2)}) copy-start(bf16[64,768]{1,0:T(8,128)(2,1)} %constant.151.clone.refs_3_) | copy-start | bytes 294916
  51.1 2.0 %collective-permute-start.17 = (f32[32,256]{1,0:T(8,128)S(1)}, f32[32,256]{1,0:T(8,128)S(1)}, u32[]{:S(2)}, u32[]{:S(2)}) collective-permute-start(f32[32,256]{1,0:T(8,128)S(1)} %get-tuple-element.113), channel_id=1, source_target_pairs={{19,31},{23,27}} | collective-permute-start | bytes 98312 | tf_op jit(solution)/shard_map/ppermute | solution.py:529
  51.8 2.9 %collective-permute-start.19 = (f32[32,256]{1,0:T(8,128)S(1)}, f32[32,256]{1,0:T(8,128)S(1)}, u32[]{:S(2)}, u32[]{:S(2)}) collective-permute-start(f32[32,256]{1,0:T(8,128)S(1)} %get-tuple-element.120), channel_id=1, source_target_pairs={{26,31},{30,27}} | collective-permute-start | bytes 98312 | tf_op jit(solution)/shard_map/ppermute | solution.py:531
  53.5 5.1 %collective-permute-start.21 = (f32[32,256]{1,0:T(8,128)S(1)}, f32[32,256]{1,0:T(8,128)S(1)}, u32[]{:S(2)}, u32[]{:S(2)}) collective-permute-start(f32[32,256]{1,0:T(8,128)S(1)} %get-tuple-element.127), channel_id=1, source_target_pairs={{8,4},{12,0},{9,5},{13,1},{10,6},{14,2},{11,7},{15,3},{16,12},{20,... | collective-permute-start | bytes 98312 | tf_op jit(solution)/shard_map/ppermute | solution.py:537
  55.1 7.9 %collective-permute-start.22 = (f32[2,32,256]{2,1,0:T(8,128)S(1)}, f32[2,32,256]{2,1,0:T(8,128)S(1)}, u32[]{:S(2)}, u32[]{:S(2)}) collective-permute-start(f32[2,32,256]{2,1,0:T(8,128)S(1)} %pad_maximum_fusion), channel_id=1, source_target_pairs={{1,4},{5,0},{2,5},{6,1},{3,6},{7,2},{9,12},{13,8},{10,13},{14,9},{... | collective-permute-start | bytes 196616 | tf_op jit(solution)/shard_map/ppermute | solution.py:539
  58.1 5.5 %collective-permute-start.20 = (f32[2,2,16,16,128]{4,3,2,1,0:T(8,128)S(1)}, f32[2,2,16,16,128]{4,3,2,1,0:T(8,128)S(1)}, u32[]{:S(2)}, u32[]{:S(2)}) collective-permute-start(f32[2,2,16,16,128]{4,3,2,1,0:T(8,128)S(1)} %get-tuple-element.126), channel_id=1, source_target_pairs={{0,4},{4,0},{1,5},{5,1},{2,6},{6,2},{3,7},{7,3},{8,12},{12,8},{9,1... | collective-permute-start | bytes 1572872 | tf_op jit(solution)/shard_map/ppermute | solution.py:551
  63.0 1.5 %collective-permute-start.23 = (f32[64,256]{1,0:T(8,128)S(1)}, f32[64,256]{1,0:T(8,128)S(1)}, u32[]{:S(2)}, u32[]{:S(2)}) collective-permute-start(f32[64,256]{1,0:T(8,128)S(1)} %pad_maximum_fusion.1), channel_id=1, source_target_pairs={{0,4},{4,0},{1,5},{5,1},{2,6},{6,2},{3,7},{7,3},{8,12},{12,8},{9,1... | collective-permute-start | bytes 196616 | tf_op jit(solution)/shard_map/ppermute | solution.py:554

commit v15 on v14

--- a/solution.py
+++ b/solution.py
@@ -189,19 +189,28 @@
     )
 
 
-def apply_contrast(field, contrast, t, block=128):
-    done = []
-    for start in range(0, field.shape[0], block):
-        here = slice(start, start + block)
-        cells = times(contrast[0, here], contrast[1, here], z_transform(field[here], t))
-        done.append(z_transform(cells, t))
-    return jnp.concatenate(done, axis=0)
-
-
-def solve_modes(start, contrast, t):
+def solve_modes(start, contrast, t, block=32):
+    half = start.shape[0] // 2
     term = total = start
     for _ in range(2):
-        term = divide(to_modes(apply_contrast(to_cells(term, t), contrast, t), t), t)
+        even = left_product(t["later"][0], term[:half])
+        odd = left_product(t["later"][1], term[half:])
+        folded = ([], [])
+        for at in range(0, half, block):
+            here, there = slice(at, at + block), slice(half + at, half + at + block)
+            factor = [jnp.concatenate([contrast[c, here], contrast[c, there]], axis=0) for c in range(2)]
+            cells = jnp.concatenate([even[here] + odd[here], even[here] - odd[here]], axis=0)
+            cells = z_transform(times(*factor, z_transform(cells, t)), t)
+            folded[0].append(split(cells[:block] + cells[block:]))
+            folded[1].append(split(cells[:block] - cells[block:]))
+        parts = []
+        for p in range(2):
+            high, low = [jnp.concatenate(pieces, axis=0) for pieces in zip(*folded[p])]
+            data = jnp.concatenate([high, low, high], axis=0)
+            modes = jnp.dot(t["onward"][p], data, preferred_element_type=F32)
+            here = slice(p * half, (p + 1) * half)
+            parts.append(times(t["inverse"][0, here], t["inverse"][1, here], modes))
+        term = jnp.concatenate(parts, axis=0)
         total = total + term
     return total, term
 

time: 65.9 us -> 65.6 us (level)
  transfers between devices with their start and end apart: 24 -> 24, of which waited for: 3 -> 3; matrix products, arithmetic and copies ran while one was open for 0% -> 0% of each run, Pallas kernels for 14% -> 13%
where the time goes in v15:
time: 65.6 us; the launch traced here: 65.2 us
  waiting for transfers between devices  31.7 us (48%)
  starting transfers between devices  20 us (30%)
  Pallas kernels  10.5 us (16%)
  between operations  1.54 us (2%)
  local copies, waits for them, and re-layouts  1.29 us (2%)
    ppermute x6, waiting for transfers between devices, body(): trace_y0 = hand_on(lax.ppermute(outs0[0], axes, along_y))  26 us
    pallas_call x14, Pallas kernels, solve(): pl.pallas_call(functools.partial(beat_kernel, tile, final), out_shape=(sh...  5.6 us
    ppermute x6, starting transfers between devices, body(): trace_y0 = hand_on(lax.ppermute(outs0[0], axes, along_y))  5.24 us
    ppermute x6, starting transfers between devices, body(): trace_y1 = lax.ppermute(outs1[1], axes, along_y)  5.24 us
    ppermute x6, starting transfers between devices, body(): trace_x = lax.ppermute(outs1[0], axes, along_x)  4.61 us
    ppermute x1, waiting for transfers between devices, body(): lax.ppermute(edge_y, axes, between([((k, j), (k, j - 1)) for k, j in ever...  4.37 us
    ppermute x1, starting transfers between devices, body(): lax.ppermute(edge_y, axes, between([((k, j), (k, j - 1)) for k, j in ever...  1.92 us
    ppermute x6, waiting for transfers between devices, body(): trace_x = lax.ppermute(outs1[0], axes, along_x)  1.32 us
  transfers between devices with their start and end apart: 24, of which 3 were waited for; matrix products, arithmetic and copies ran while one was open for 0% of the time, Pallas kernels for 13%

profile of v15, /device:TPU:29, one launch (start us, length us, event | category | flops | bytes accessed | tf_op | source)
XLA Modules:
  0.0 65.2 jit_solution(5958652754354844458)
XLA Ops:
  0.8 1.2 %dynamic-slice_bitcast_fusion = (f32[2,16,16,128]{3,2,1,0:T(8,128)S(1)}, f32[2,16,16,128]{3,2,1,0:T(8,128)S(1)}) fusion(f32[2,2,16,16,128]{4,3,2,1,0:T(8,128)} %param.8, s32[]{:T(128)S(6)} %select_n.73, s32[]{:T(128)S(6)} %select_n.72), kind=kLoop, calls=%fused_computation | loop fusion | bytes 1048584 | tf_op jit(solution)/shard_map/jit(dynamic_index_in_dim)/squeeze | solution.py:459
  1.9 0.7 %collective-permute-start = (f32[2,16,16,128]{3,2,1,0:T(8,128)S(1)}, f32[2,16,16,128]{3,2,1,0:T(8,128)S(1)}, u32[]{:S(2)}, u32[]{:S(2)}) collective-permute-start(f32[2,16,16,128]{3,2,1,0:T(8,128)S(1)} %get-tuple-element.135), channel_id=1, source_target_pairs={{0,4},{4,0},{1,5},{5,1},{2,6},{6,2},{3,7},{7,3},{8,12},{12,8},{9,1... | collective-permute-start | bytes 786440 | tf_op jit(solution)/shard_map/ppermute | solution.py:457
  2.7 0.1 collective-permute-start.1
  2.9 1.1 %prep.1 = (f32[256,256]{1,0:T(8,128)S(1)}, f32[2,256,128]{2,1,0:T(8,128)S(1)}, f32[2,256,128]{2,1,0:T(8,128)S(1)}, bf16[5,128,384]{2,1,0:T(8,128)(2,1)S(1)}) custom-call(f32[2,16,16,128]{3,2,1,0:T(8,128)S(1)} %get-tuple-element.134.right_ref, f32[16,16,128]{2,1,0:T(8,128)S(1)} %copy-done.2, s32[1,16]{1,0:T(1,128)S(1)} %and_select_fusion.2.place_ref, ...), custom_call_target="tpu_custom_call" | custom-call | flops 2000000000 | bytes 2000000 | tf_op jit(solution)/shard_map/prep/pallas_call | solution.py:473
  4.0 0.8 %prep_other.1 = (f32[2,256,256]{2,1,0:T(8,128)S(1)}, f32[2,2,256,128]{3,2,1,0:T(8,128)S(1)}) custom-call(s32[1]{0:T(128)} %bitcast.1.core_ref, s32[1]{0:T(128)} %bitcast.rhs_ref, f32[2,16,16,128]{3,2,1,0:T(8,128)S(1)} %collective-permute-done.swap_ref, f32[16,16,128]{2,1,0:T(8,128)S(1)} %collective-permute-done.1.slow_ref, ...), custom_call_target="tpu_custom_call" | custom-call | flops 2000000000 | bytes 2000000 | tf_op jit(solution)/shard_map/prep_other/pallas_call | solution.py:485
  4.8 0.1 upper.7
  4.9 0.7 %collective-permute-start.3 = (f32[32,256]{1,0:T(8,128)S(1)}, f32[32,256]{1,0:T(8,128)S(1)}, u32[]{:S(2)}, u32[]{:S(2)}) collective-permute-start(f32[32,256]{1,0:T(8,128)S(1)} %get-tuple-element.74), channel_id=1, source_target_pairs={{0,5},{4,1}} | collective-permute-start | bytes 98312 | tf_op jit(solution)/shard_map/ppermute | solution.py:535
  5.7 0.1 lower.7
  5.7 0.7 %collective-permute-start.2 = (f32[32,256]{1,0:T(8,128)S(1)}, f32[32,256]{1,0:T(8,128)S(1)}, u32[]{:S(2)}, u32[]{:S(2)}) collective-permute-start(f32[32,256]{1,0:T(8,128)S(1)} %get-tuple-element.73), channel_id=1, source_target_pairs={{0,12},{4,8}} | collective-permute-start | bytes 98312 | tf_op jit(solution)/shard_map/ppermute | solution.py:538
  6.4 0.7 %collective-permute-start.4 = (f32[32,256]{1,0:T(8,128)S(1)}, f32[32,256]{1,0:T(8,128)S(1)}, u32[]{:S(2)}, u32[]{:S(2)}) collective-permute-start(f32[32,256]{1,0:T(8,128)S(1)} %get-tuple-element.78), channel_id=1, source_target_pairs={{0,5},{4,1}} | collective-permute-start | bytes 98312 | tf_op jit(solution)/shard_map/ppermute | solution.py:540
  7.1 0.1 upper.8
  7.2 0.7 %collective-permute-start.6 = (f32[32,256]{1,0:T(8,128)S(1)}, f32[32,256]{1,0:T(8,128)S(1)}, u32[]{:S(2)}, u32[]{:S(2)}) collective-permute-start(f32[32,256]{1,0:T(8,128)S(1)} %get-tuple-element.82), channel_id=1, source_target_pairs={{1,6},{5,2},{8,13},{12,9}} | collective-permute-start | bytes 98312 | tf_op jit(solution)/shard_map/ppermute | solution.py:535
  7.9 0.1 lower.8
  8.0 0.7 %collective-permute-start.5 = (f32[32,256]{1,0:T(8,128)S(1)}, f32[32,256]{1,0:T(8,128)S(1)}, u32[]{:S(2)}, u32[]{:S(2)}) collective-permute-start(f32[32,256]{1,0:T(8,128)S(1)} %get-tuple-element.81), channel_id=1, source_target_pairs={{1,13},{5,9},{8,20},{12,16}} | collective-permute-start | bytes 98312 | tf_op jit(solution)/shard_map/ppermute | solution.py:538
  8.6 0.7 %collective-permute-start.7 = (f32[32,256]{1,0:T(8,128)S(1)}, f32[32,256]{1,0:T(8,128)S(1)}, u32[]{:S(2)}, u32[]{:S(2)}) collective-permute-start(f32[32,256]{1,0:T(8,128)S(1)} %get-tuple-element.86), channel_id=1, source_target_pairs={{1,6},{5,2},{8,13},{12,9}} | collective-permute-start | bytes 98312 | tf_op jit(solution)/shard_map/ppermute | solution.py:540
  9.3 0.1 upper.9
  9.4 0.7 %collective-permute-start.9 = (f32[32,256]{1,0:T(8,128)S(1)}, f32[32,256]{1,0:T(8,128)S(1)}, u32[]{:S(2)}, u32[]{:S(2)}) collective-permute-start(f32[32,256]{1,0:T(8,128)S(1)} %get-tuple-element.90), channel_id=1, source_target_pairs={{2,7},{6,3},{9,14},{13,10},{16,21},{20,17}} | collective-permute-start | bytes 98312 | tf_op jit(solution)/shard_map/ppermute | solution.py:535
  10.1 0.1 lower.9
  10.2 0.7 %collective-permute-start.8 = (f32[32,256]{1,0:T(8,128)S(1)}, f32[32,256]{1,0:T(8,128)S(1)}, u32[]{:S(2)}, u32[]{:S(2)}) collective-permute-start(f32[32,256]{1,0:T(8,128)S(1)} %get-tuple-element.89), channel_id=1, source_target_pairs={{2,14},{6,10},{9,21},{13,17},{16,28},{20,24}} | collective-permute-start | bytes 98312 | tf_op jit(solution)/shard_map/ppermute | solution.py:538
  10.9 0.7 %collective-permute-start.10 = (f32[32,256]{1,0:T(8,128)S(1)}, f32[32,256]{1,0:T(8,128)S(1)}, u32[]{:S(2)}, u32[]{:S(2)}) collective-permute-start(f32[32,256]{1,0:T(8,128)S(1)} %get-tuple-element.94), channel_id=1, source_target_pairs={{2,7},{6,3},{9,14},{13,10},{16,21},{20,17}} | collective-permute-start | bytes 98312 | tf_op jit(solution)/shard_map/ppermute | solution.py:540
  11.6 0.1 upper.10
  11.7 0.7 %collective-permute-start.12 = (f32[32,256]{1,0:T(8,128)S(1)}, f32[32,256]{1,0:T(8,128)S(1)}, u32[]{:S(2)}, u32[]{:S(2)}) collective-permute-start(f32[32,256]{1,0:T(8,128)S(1)} %get-tuple-element.98), channel_id=1, source_target_pairs={{10,15},{14,11},{17,22},{21,18},{24,29},{28,25}} | collective-permute-start | bytes 98312 | tf_op jit(solution)/shard_map/ppermute | solution.py:535
  12.3 0.3 lower.10
  12.6 0.7 %collective-permute-start.11 = (f32[32,256]{1,0:T(8,128)S(1)}, f32[32,256]{1,0:T(8,128)S(1)}, u32[]{:S(2)}, u32[]{:S(2)}) collective-permute-start(f32[32,256]{1,0:T(8,128)S(1)} %get-tuple-element.97), channel_id=1, source_target_pairs={{3,15},{7,11},{10,22},{14,18},{17,29},{21,25}} | collective-permute-start | bytes 98312 | tf_op jit(solution)/shard_map/ppermute | solution.py:538
  13.3 0.7 %collective-permute-start.13 = (f32[32,256]{1,0:T(8,128)S(1)}, f32[32,256]{1,0:T(8,128)S(1)}, u32[]{:S(2)}, u32[]{:S(2)}) collective-permute-start(f32[32,256]{1,0:T(8,128)S(1)} %get-tuple-element.102), channel_id=1, source_target_pairs={{10,15},{14,11},{17,22},{21,18},{24,29},{28,25}} | collective-permute-start | bytes 98312 | tf_op jit(solution)/shard_map/ppermute | solution.py:540
  14.0 0.1 upper.11
  14.1 1.3 %collective-permute-start.15 = (f32[32,256]{1,0:T(8,128)S(1)}, f32[32,256]{1,0:T(8,128)S(1)}, u32[]{:S(2)}, u32[]{:S(2)}) collective-permute-start(f32[32,256]{1,0:T(8,128)S(1)} %get-tuple-element.106), channel_id=1, source_target_pairs={{18,23},{22,19},{25,30},{29,26}} | collective-permute-start | bytes 98312 | tf_op jit(solution)/shard_map/ppermute | solution.py:535
  15.4 0.1 lower.11
  15.4 1.3 %collective-permute-start.14 = (f32[32,256]{1,0:T(8,128)S(1)}, f32[32,256]{1,0:T(8,128)S(1)}, u32[]{:S(2)}, u32[]{:S(2)}) collective-permute-start(f32[32,256]{1,0:T(8,128)S(1)} %get-tuple-element.105), channel_id=1, source_target_pairs={{11,23},{15,19},{18,30},{22,26}} | collective-permute-start | bytes 98312 | tf_op jit(solution)/shard_map/ppermute | solution.py:538
  16.8 1.3 %collective-permute-start.16 = (f32[32,256]{1,0:T(8,128)S(1)}, f32[32,256]{1,0:T(8,128)S(1)}, u32[]{:S(2)}, u32[]{:S(2)}) collective-permute-start(f32[32,256]{1,0:T(8,128)S(1)} %get-tuple-element.110), channel_id=1, source_target_pairs={{18,23},{22,19},{25,30},{29,26}} | collective-permute-start | bytes 98312 | tf_op jit(solution)/shard_map/ppermute | solution.py:540
  18.1 26.0 %collective-permute-done.15.in_ref = f32[32,256]{1,0:T(8,128)S(1)} collective-permute-done((f32[32,256]{1,0:T(8,128)S(1)}, f32[32,256]{1,0:T(8,128)S(1)}, u32[]{:S(2)}, u32[]{:S(2)}) %collective-permute-start.15) | collective-permute-done | bytes 32800 | tf_op jit(solution)/shard_map/ppermute | solution.py:535
  44.0 1.3 %collective-permute-done.14.trace_x_ref = f32[32,256]{1,0:T(8,128)S(1)} collective-permute-done((f32[32,256]{1,0:T(8,128)S(1)}, f32[32,256]{1,0:T(8,128)S(1)}, u32[]{:S(2)}, u32[]{:S(2)}) %collective-permute-start.14) | collective-permute-done | bytes 32800 | tf_op jit(solution)/shard_map/ppermute | solution.py:538
  45.3 2.1 %upper.12 = (f32[256,256]{1,0:T(8,128)S(1)}, f32[256,256]{1,0:T(8,128)S(1)}, f32[32,256]{1,0:T(8,128)S(1)}, f32[32,256]{1,0:T(8,128)S(1)}) custom-call(s32[1]{0:T(128)} %bitcast.9.active_ref, f32[2,256,256]{2,1,0:T(8,128)S(1)} %get-tuple-element.69.modes_ref, ...), custom_call_target="tpu_custom_call", output_to_operand_aliasing={{0}: (5, {}), {1}: (6, {})} | custom-call | flops 2000000000 | bytes 2000000 | tf_op jit(solution)/shard_map/upper/pallas_call | solution.py:500
  47.4 1.3 %collective-permute-start.18 = (f32[32,256]{1,0:T(8,128)S(1)}, f32[32,256]{1,0:T(8,128)S(1)}, u32[]{:S(2)}, u32[]{:S(2)}) collective-permute-start(f32[32,256]{1,0:T(8,128)S(1)} %get-tuple-element.114), channel_id=1, source_target_pairs={{26,31},{30,27}} | collective-permute-start | bytes 98312 | tf_op jit(solution)/shard_map/ppermute | solution.py:535
  48.7 2.1 %lower.12 = (f32[256,256]{1,0:T(8,128)S(1)}, f32[256,256]{1,0:T(8,128)S(1)}, f32[32,256]{1,0:T(8,128)S(1)}, f32[32,256]{1,0:T(8,128)S(1)}) custom-call(s32[1]{0:T(128)} %bitcast.9.active_ref, f32[2,256,256]{2,1,0:T(8,128)S(1)} %get-tuple-element.69.modes_ref, ...), custom_call_target="tpu_custom_call", output_to_operand_aliasing={{0}: (5, {}), {1}: (6, {})} | custom-call | flops 2000000000 | bytes 2000000 | tf_op jit(solution)/shard_map/lower/pallas_call | solution.py:500
  50.8 0.7 %collective-permute-start.17 = (f32[32,256]{1,0:T(8,128)S(1)}, f32[32,256]{1,0:T(8,128)S(1)}, u32[]{:S(2)}, u32[]{:S(2)}) collective-permute-start(f32[32,256]{1,0:T(8,128)S(1)} %get-tuple-element.113), channel_id=1, source_target_pairs={{19,31},{23,27}} | collective-permute-start | bytes 98312 | tf_op jit(solution)/shard_map/ppermute | solution.py:538
  51.5 1.3 %collective-permute-start.19 = (f32[32,256]{1,0:T(8,128)S(1)}, f32[32,256]{1,0:T(8,128)S(1)}, u32[]{:S(2)}, u32[]{:S(2)}) collective-permute-start(f32[32,256]{1,0:T(8,128)S(1)} %get-tuple-element.120), channel_id=1, source_target_pairs={{26,31},{30,27}} | collective-permute-start | bytes 98312 | tf_op jit(solution)/shard_map/ppermute | solution.py:540
  52.8 0.3 upper.13
  53.1 1.3 %collective-permute-start.21 = (f32[32,256]{1,0:T(8,128)S(1)}, f32[32,256]{1,0:T(8,128)S(1)}, u32[]{:S(2)}, u32[]{:S(2)}) collective-permute-start(f32[32,256]{1,0:T(8,128)S(1)} %get-tuple-element.127), channel_id=1, source_target_pairs={{8,4},{12,0},{9,5},{13,1},{10,6},{14,2},{11,7},{15,3},{16,12},{20,... | collective-permute-start | bytes 98312 | tf_op jit(solution)/shard_map/ppermute | solution.py:546
  54.4 0.3 lower.13
  54.7 1.9 %collective-permute-start.22 = (f32[2,32,256]{2,1,0:T(8,128)S(1)}, f32[2,32,256]{2,1,0:T(8,128)S(1)}, u32[]{:S(2)}, u32[]{:S(2)}) collective-permute-start(f32[2,32,256]{2,1,0:T(8,128)S(1)} %pad_maximum_fusion), channel_id=1, source_target_pairs={{1,4},{5,0},{2,5},{6,1},{3,6},{7,2},{9,12},{13,8},{10,13},{14,9},{... | collective-permute-start | bytes 196616 | tf_op jit(solution)/shard_map/ppermute | solution.py:548
  56.6 1.1 %finish.1 = (f32[2,2,16,16,128]{4,3,2,1,0:T(8,128)S(1)}, f32[2,2,16,16,128]{4,3,2,1,0:T(8,128)S(1)}) custom-call(s32[1]{0:T(128)} %bitcast.1.core_ref, f32[256,256]{1,0:T(8,128)S(1)} %get-tuple-element.117.total0_ref, f32[256,256]{1,0:T(8,128)S(1)} %get-tuple-element.118.term0_ref, f32[256,256]{1,0:T(8,128)S(1)} %get-tuple-element.123.total1_ref, ...), custom_call_target="tpu_custom_call" | custom-call | tf_op jit(solution)/shard_map/finish/pallas_call | solution.py:551
  57.8 0.5 collective-permute-start.20
  58.3 4.4 %collective-permute-done.22.edge_y_ref = f32[2,32,256]{2,1,0:T(8,128)S(1)} collective-permute-done((f32[2,32,256]{2,1,0:T(8,128)S(1)}, f32[2,32,256]{2,1,0:T(8,128)S(1)}, u32[]{:S(2)}, u32[]{:S(2)}) %collective-permute-start.22) | collective-permute-done | bytes 65568 | tf_op jit(solution)/shard_map/ppermute | solution.py:548
  62.6 0.5 collective-permute-start.23
  63.1 0.2 keep.1.keep_rest_ref
  63.3 0.8 %place_wave.1 = f32[2,2,16,16,128]{4,3,2,1,0:T(8,128)} custom-call(s32[1]{0:T(128)} %bitcast.rhs_ref, f32[2,2,16,16,128]{4,3,2,1,0:T(8,128)S(1)} %get-tuple-element.125.keep_ref, f32[2,2,16,16,128]{4,3,2,1,0:T(8,128)S(1)} %collective-permute-done.20.got_ref), custom_call_target="tpu_custom_call" | custom-call | flops 10000000000 | bytes 1000000 | tf_op jit(solution)/shard_map/place_wave/pallas_call | solution.py:573
  64.1 0.9 %place_rest.1 = f32[2,2,16,16,128]{4,3,2,1,0:T(8,128)} custom-call(s32[1]{0:T(128)} %bitcast.1.core_ref, s32[1]{0:T(128)} %bitcast.rhs_ref, f32[2,16,16,128]{3,2,1,0:T(8,128)S(1)} %keep.1.keep_rest_ref, f32[2,2,16,16,128]{4,3,2,1,0:T(8,128)S(1)} %collective-permute-done.20.got_ref, f32[64,256]{1,0:T(8,128)S(1)} %collective-permute-done.23.got_edge_ref, ...), custom_call_target="tpu_custom_call" | custom-call | tf_op jit(solution)/shard_map/place_rest/pallas_call | solution.py:583
  (54 shorter events, 0.3 us)
Async XLA Ops:
  0.6 2.2 %copy-start = (f32[2,16,2]{1,2,0:T(2,128)S(1)}, f32[2,16,2]{1,2,0:T(2,128)}, u32[]{:S(2)}) copy-start(f32[2,16,2]{1,2,0:T(2,128)} %param.11) | copy-start | bytes 772
  0.7 2.2 %copy-start.4 = (f32[256,128]{1,0:T(8,128)S(1)}, f32[256,128]{1,0:T(8,128)}, u32[]{:S(2)}) copy-start(f32[256,128]{1,0:T(8,128)} %constant.150.clone.refs_0_) | copy-start | bytes 393220
  0.7 2.0 %copy-start.6 = (s32[2,16]{1,0:T(2,128)S(1)}, s32[2,16]{1,0:T(2,128)}, u32[]{:S(2)}) copy-start(s32[2,16]{1,0:T(2,128)} %param.10) | copy-start | bytes 388
  0.7 1.9 %copy-start.2 = (f32[16,16,128]{2,1,0:T(8,128)S(1)}, f32[16,16,128]{2,1,0:T(8,128)}, u32[]{:S(2)}) copy-start(f32[16,16,128]{2,1,0:T(8,128)} %slow_ref.1) | copy-start | bytes 393220
  0.7 2.1 %copy-start.1 = (bf16[4,128,384]{2,1,0:T(8,128)(2,1)S(1)}, bf16[4,128,384]{2,1,0:T(8,128)(2,1)}, u32[]{:S(2)}) copy-start(bf16[4,128,384]{2,1,0:T(8,128)(2,1)} %constant.152.clone.refs_1_.z_ref) | copy-start | bytes 1179652
  0.7 2.1 %copy-start.3 = (bf16[5,128,384]{2,1,0:T(8,128)(2,1)S(1)}, bf16[5,128,384]{2,1,0:T(8,128)(2,1)}, u32[]{:S(2)}) copy-start(bf16[5,128,384]{2,1,0:T(8,128)(2,1)} %constant.153.clone.refs_2_) | copy-start | bytes 1474564
  1.9 2.1 %collective-permute-start = (f32[2,16,16,128]{3,2,1,0:T(8,128)S(1)}, f32[2,16,16,128]{3,2,1,0:T(8,128)S(1)}, u32[]{:S(2)}, u32[]{:S(2)}) collective-permute-start(f32[2,16,16,128]{3,2,1,0:T(8,128)S(1)} %get-tuple-element.135), channel_id=1, source_target_pairs={{0,4},{4,0},{1,5},{5,1},{2,6},{6,2},{3,7},{7,3},{8,12},{12,8},{9,1... | collective-permute-start | bytes 786440 | tf_op jit(solution)/shard_map/ppermute | solution.py:457
  2.7 1.3 %collective-permute-start.1 = (f32[16,16,128]{2,1,0:T(8,128)S(1)}, f32[16,16,128]{2,1,0:T(8,128)S(1)}, u32[]{:S(2)}, u32[]{:S(2)}) collective-permute-start(f32[16,16,128]{2,1,0:T(8,128)S(1)} %copy-done.2), channel_id=1, source_target_pairs={{0,4},{4,0},{1,5},{5,1},{2,6},{6,2},{3,7},{7,3},{8,12},{12,8},{9,1... | collective-permute-start | bytes 393224 | tf_op jit(solution)/shard_map/ppermute | solution.py:458
  4.9 2.2 %collective-permute-start.3 = (f32[32,256]{1,0:T(8,128)S(1)}, f32[32,256]{1,0:T(8,128)S(1)}, u32[]{:S(2)}, u32[]{:S(2)}) collective-permute-start(f32[32,256]{1,0:T(8,128)S(1)} %get-tuple-element.74), channel_id=1, source_target_pairs={{0,5},{4,1}} | collective-permute-start | bytes 98312 | tf_op jit(solution)/shard_map/ppermute | solution.py:535
  5.7 1.4 %collective-permute-start.2 = (f32[32,256]{1,0:T(8,128)S(1)}, f32[32,256]{1,0:T(8,128)S(1)}, u32[]{:S(2)}, u32[]{:S(2)}) collective-permute-start(f32[32,256]{1,0:T(8,128)S(1)} %get-tuple-element.73), channel_id=1, source_target_pairs={{0,12},{4,8}} | collective-permute-start | bytes 98312 | tf_op jit(solution)/shard_map/ppermute | solution.py:538
  6.4 1.5 %collective-permute-start.4 = (f32[32,256]{1,0:T(8,128)S(1)}, f32[32,256]{1,0:T(8,128)S(1)}, u32[]{:S(2)}, u32[]{:S(2)}) collective-permute-start(f32[32,256]{1,0:T(8,128)S(1)} %get-tuple-element.78), channel_id=1, source_target_pairs={{0,5},{4,1}} | collective-permute-start | bytes 98312 | tf_op jit(solution)/shard_map/ppermute | solution.py:540
  7.2 2.1 %collective-permute-start.6 = (f32[32,256]{1,0:T(8,128)S(1)}, f32[32,256]{1,0:T(8,128)S(1)}, u32[]{:S(2)}, u32[]{:S(2)}) collective-permute-start(f32[32,256]{1,0:T(8,128)S(1)} %get-tuple-element.82), channel_id=1, source_target_pairs={{1,6},{5,2},{8,13},{12,9}} | collective-permute-start | bytes 98312 | tf_op jit(solution)/shard_map/ppermute | solution.py:535
  8.0 1.4 %collective-permute-start.5 = (f32[32,256]{1,0:T(8,128)S(1)}, f32[32,256]{1,0:T(8,128)S(1)}, u32[]{:S(2)}, u32[]{:S(2)}) collective-permute-start(f32[32,256]{1,0:T(8,128)S(1)} %get-tuple-element.81), channel_id=1, source_target_pairs={{1,13},{5,9},{8,20},{12,16}} | collective-permute-start | bytes 98312 | tf_op jit(solution)/shard_map/ppermute | solution.py:538
  8.6 1.5 %collective-permute-start.7 = (f32[32,256]{1,0:T(8,128)S(1)}, f32[32,256]{1,0:T(8,128)S(1)}, u32[]{:S(2)}, u32[]{:S(2)}) collective-permute-start(f32[32,256]{1,0:T(8,128)S(1)} %get-tuple-element.86), channel_id=1, source_target_pairs={{1,6},{5,2},{8,13},{12,9}} | collective-permute-start | bytes 98312 | tf_op jit(solution)/shard_map/ppermute | solution.py:540
  9.4 2.1 %collective-permute-start.9 = (f32[32,256]{1,0:T(8,128)S(1)}, f32[32,256]{1,0:T(8,128)S(1)}, u32[]{:S(2)}, u32[]{:S(2)}) collective-permute-start(f32[32,256]{1,0:T(8,128)S(1)} %get-tuple-element.90), channel_id=1, source_target_pairs={{2,7},{6,3},{9,14},{13,10},{16,21},{20,17}} | collective-permute-start | bytes 98312 | tf_op jit(solution)/shard_map/ppermute | solution.py:535
  10.2 1.4 %collective-permute-start.8 = (f32[32,256]{1,0:T(8,128)S(1)}, f32[32,256]{1,0:T(8,128)S(1)}, u32[]{:S(2)}, u32[]{:S(2)}) collective-permute-start(f32[32,256]{1,0:T(8,128)S(1)} %get-tuple-element.89), channel_id=1, source_target_pairs={{2,14},{6,10},{9,21},{13,17},{16,28},{20,24}} | collective-permute-start | bytes 98312 | tf_op jit(solution)/shard_map/ppermute | solution.py:538
  10.9 1.5 %collective-permute-start.10 = (f32[32,256]{1,0:T(8,128)S(1)}, f32[32,256]{1,0:T(8,128)S(1)}, u32[]{:S(2)}, u32[]{:S(2)}) collective-permute-start(f32[32,256]{1,0:T(8,128)S(1)} %get-tuple-element.94), channel_id=1, source_target_pairs={{2,7},{6,3},{9,14},{13,10},{16,21},{20,17}} | collective-permute-start | bytes 98312 | tf_op jit(solution)/shard_map/ppermute | solution.py:540
  11.7 2.3 %collective-permute-start.12 = (f32[32,256]{1,0:T(8,128)S(1)}, f32[32,256]{1,0:T(8,128)S(1)}, u32[]{:S(2)}, u32[]{:S(2)}) collective-permute-start(f32[32,256]{1,0:T(8,128)S(1)} %get-tuple-element.98), channel_id=1, source_target_pairs={{10,15},{14,11},{17,22},{21,18},{24,29},{28,25}} | collective-permute-start | bytes 98312 | tf_op jit(solution)/shard_map/ppermute | solution.py:535
  12.6 1.4 %collective-permute-start.11 = (f32[32,256]{1,0:T(8,128)S(1)}, f32[32,256]{1,0:T(8,128)S(1)}, u32[]{:S(2)}, u32[]{:S(2)}) collective-permute-start(f32[32,256]{1,0:T(8,128)S(1)} %get-tuple-element.97), channel_id=1, source_target_pairs={{3,15},{7,11},{10,22},{14,18},{17,29},{21,25}} | collective-permute-start | bytes 98312 | tf_op jit(solution)/shard_map/ppermute | solution.py:538
  13.3 2.1 %collective-permute-start.13 = (f32[32,256]{1,0:T(8,128)S(1)}, f32[32,256]{1,0:T(8,128)S(1)}, u32[]{:S(2)}, u32[]{:S(2)}) collective-permute-start(f32[32,256]{1,0:T(8,128)S(1)} %get-tuple-element.102), channel_id=1, source_target_pairs={{10,15},{14,11},{17,22},{21,18},{24,29},{28,25}} | collective-permute-start | bytes 98312 | tf_op jit(solution)/shard_map/ppermute | solution.py:540
  14.1 30.0 %collective-permute-start.15 = (f32[32,256]{1,0:T(8,128)S(1)}, f32[32,256]{1,0:T(8,128)S(1)}, u32[]{:S(2)}, u32[]{:S(2)}) collective-permute-start(f32[32,256]{1,0:T(8,128)S(1)} %get-tuple-element.106), channel_id=1, source_target_pairs={{18,23},{22,19},{25,30},{29,26}} | collective-permute-start | bytes 98312 | tf_op jit(solution)/shard_map/ppermute | solution.py:535
  15.4 29.9 %collective-permute-start.14 = (f32[32,256]{1,0:T(8,128)S(1)}, f32[32,256]{1,0:T(8,128)S(1)}, u32[]{:S(2)}, u32[]{:S(2)}) collective-permute-start(f32[32,256]{1,0:T(8,128)S(1)} %get-tuple-element.105), channel_id=1, source_target_pairs={{11,23},{15,19},{18,30},{22,26}} | collective-permute-start | bytes 98312 | tf_op jit(solution)/shard_map/ppermute | solution.py:538
  16.8 32.0 %collective-permute-start.16 = (f32[32,256]{1,0:T(8,128)S(1)}, f32[32,256]{1,0:T(8,128)S(1)}, u32[]{:S(2)}, u32[]{:S(2)}) collective-permute-start(f32[32,256]{1,0:T(8,128)S(1)} %get-tuple-element.110), channel_id=1, source_target_pairs={{18,23},{22,19},{25,30},{29,26}} | collective-permute-start | bytes 98312 | tf_op jit(solution)/shard_map/ppermute | solution.py:540
  47.4 5.4 %collective-permute-start.18 = (f32[32,256]{1,0:T(8,128)S(1)}, f32[32,256]{1,0:T(8,128)S(1)}, u32[]{:S(2)}, u32[]{:S(2)}) collective-permute-start(f32[32,256]{1,0:T(8,128)S(1)} %get-tuple-element.114), channel_id=1, source_target_pairs={{26,31},{30,27}} | collective-permute-start | bytes 98312 | tf_op jit(solution)/shard_map/ppermute | solution.py:535
  48.7 4.1 %copy-start.5 = (bf16[64,768]{1,0:T(8,128)(2,1)S(1)}, bf16[64,768]{1,0:T(8,128)(2,1)}, u32[]{:S(2)}) copy-start(bf16[64,768]{1,0:T(8,128)(2,1)} %constant.151.clone.refs_3_) | copy-start | bytes 294916
  50.8 2.0 %collective-permute-start.17 = (f32[32,256]{1,0:T(8,128)S(1)}, f32[32,256]{1,0:T(8,128)S(1)}, u32[]{:S(2)}, u32[]{:S(2)}) collective-permute-start(f32[32,256]{1,0:T(8,128)S(1)} %get-tuple-element.113), channel_id=1, source_target_pairs={{19,31},{23,27}} | collective-permute-start | bytes 98312 | tf_op jit(solution)/shard_map/ppermute | solution.py:538
  51.5 2.9 %collective-permute-start.19 = (f32[32,256]{1,0:T(8,128)S(1)}, f32[32,256]{1,0:T(8,128)S(1)}, u32[]{:S(2)}, u32[]{:S(2)}) collective-permute-start(f32[32,256]{1,0:T(8,128)S(1)} %get-tuple-element.120), channel_id=1, source_target_pairs={{26,31},{30,27}} | collective-permute-start | bytes 98312 | tf_op jit(solution)/shard_map/ppermute | solution.py:540
  53.1 5.1 %collective-permute-start.21 = (f32[32,256]{1,0:T(8,128)S(1)}, f32[32,256]{1,0:T(8,128)S(1)}, u32[]{:S(2)}, u32[]{:S(2)}) collective-permute-start(f32[32,256]{1,0:T(8,128)S(1)} %get-tuple-element.127), channel_id=1, source_target_pairs={{8,4},{12,0},{9,5},{13,1},{10,6},{14,2},{11,7},{15,3},{16,12},{20,... | collective-permute-start | bytes 98312 | tf_op jit(solution)/shard_map/ppermute | solution.py:546
  54.7 7.9 %collective-permute-start.22 = (f32[2,32,256]{2,1,0:T(8,128)S(1)}, f32[2,32,256]{2,1,0:T(8,128)S(1)}, u32[]{:S(2)}, u32[]{:S(2)}) collective-permute-start(f32[2,32,256]{2,1,0:T(8,128)S(1)} %pad_maximum_fusion), channel_id=1, source_target_pairs={{1,4},{5,0},{2,5},{6,1},{3,6},{7,2},{9,12},{13,8},{10,13},{14,9},{... | collective-permute-start | bytes 196616 | tf_op jit(solution)/shard_map/ppermute | solution.py:548
  57.8 5.5 %collective-permute-start.20 = (f32[2,2,16,16,128]{4,3,2,1,0:T(8,128)S(1)}, f32[2,2,16,16,128]{4,3,2,1,0:T(8,128)S(1)}, u32[]{:S(2)}, u32[]{:S(2)}) collective-permute-start(f32[2,2,16,16,128]{4,3,2,1,0:T(8,128)S(1)} %get-tuple-element.126), channel_id=1, source_target_pairs={{0,4},{4,0},{1,5},{5,1},{2,6},{6,2},{3,7},{7,3},{8,12},{12,8},{9,1... | collective-permute-start | bytes 1572872 | tf_op jit(solution)/shard_map/ppermute | solution.py:560
  62.6 1.5 %collective-permute-start.23 = (f32[64,256]{1,0:T(8,128)S(1)}, f32[64,256]{1,0:T(8,128)S(1)}, u32[]{:S(2)}, u32[]{:S(2)}) collective-permute-start(f32[64,256]{1,0:T(8,128)S(1)} %pad_maximum_fusion.1), channel_id=1, source_target_pairs={{0,4},{4,0},{1,5},{5,1},{2,6},{6,2},{3,7},{7,3},{8,12},{12,8},{9,1... | collective-permute-start | bytes 196616 | tf_op jit(solution)/shard_map/ppermute | solution.py:563

commit v16 on v13

--- a/solution.py
+++ b/solution.py
@@ -47,6 +47,11 @@
     return np.stack(pieces)
 
 
+def quarter_matrix(slabs_ref, index):
+    count = slabs_ref.shape[1] // 2
+    return slabs_ref[index // 2, index % 2 * count : (index % 2 + 1) * count, : 3 * count]
+
+
 def z_matrix(t, depth):
     rows = t["onward"].shape[1]
     pieces = [t["onward"][2 + n, :, :depth] for n in range(-(-depth // rows))]
@@ -78,27 +83,35 @@
     sine_y, angle_y = sine_matrix(size_y)
     sine_z, angle_z = sine_matrix(cells_z)
     half = size_x // 2
-    order = np.concatenate([np.arange(0, size_x, 2), np.arange(1, size_x, 2)])
+    assert half % 8 == 0 and size_y % 16 == 0
+    order_x, order_y = [np.arange(0, n, 2).reshape(1, -1) + [[0], [1]] for n in (size_x, size_y)]
+    pairs = [(x, y) for p in range(2) for q in range(2) for x in order_x[p] for y in order_y[q]]
+    mode_x, mode_y = np.array(pairs).T
     cells = np.concatenate([np.arange(half), np.arange(size_x - 1, half - 1, -1)])
 
     def symbol(angle):
         return 2.5 - 8.0 / 3.0 * np.cos(angle) + 1.0 / 6.0 * np.cos(2.0 * angle)
 
     real_part = (
-        symbol(angle_x)[order][:, None, None]
-        + symbol(angle_y)[None, :, None]
-        + (2.0 - 2.0 * np.cos(angle_z))[None, None, :]
+        symbol(angle_x)[mode_x][:, None]
+        + symbol(angle_y)[mode_y][:, None]
+        + (2.0 - 2.0 * np.cos(angle_z))[None, :]
         - KAPPA
-    ).reshape(size_x * size_y, cells_z)
-
-    parity = [np.kron(sine_x[order[p * half : (p + 1) * half]][:, :half], sine_y) for p in (0, 1)]
+    )
+
+    slab = half * size_y
+    lanes = 3 * slab
+    parity = [
+        np.kron(sine_x[order_x[p]][:, :half], sine_y[order_y[q]][:, : size_y // 2])
+        for p in range(2) for q in range(2)
+    ]
     forward = [left_factor(m) for m in parity]
     backward = [left_factor(m.T) for m in parity]
     high_z, low_z = halves(sine_z)
     right_z = np.concatenate([np.concatenate([high_z, low_z], axis=1)] * 2, axis=0)
 
-    full = np.kron(sine_x[order], sine_y)
-    by_cell = full.reshape(-1, size_x, size_y)
+    by_cell = sine_x[mode_x][:, :, None] * sine_y[mode_y][:, None, :]
+    full = by_cell.reshape(len(by_cell), -1)
     enter_x = np.stack([-by_cell[:, 0] / 12.0, (16.0 * by_cell[:, 0] - by_cell[:, 1]) / 12.0], 1)
     enter_y = np.stack(
         [-by_cell[:, :, 0] / 12.0, (16.0 * by_cell[:, :, 0] - by_cell[:, :, 1]) / 12.0], 1
@@ -124,17 +137,17 @@
             axis=1,
         ).T
     )
-    later = slabs(backward + [enter, leave[:, : forward[0].shape[1]]], half * size_y, forward[0].shape[1])
-    rest = leave[:, forward[0].shape[1] :]
+    later = slabs(backward + [enter, leave[:, : lanes]], slab, lanes)
+    rest = leave[:, lanes :]
     if rest.shape[1]:
         assert enter.shape[1] <= later.shape[2] - rest.shape[1]
         later[2, :, later.shape[2] - rest.shape[1] :] = rest
-    assert 2 * cells_z % (half * size_y) == 0 and 2 * cells_z <= forward[0].shape[1]
-    assert enter.shape[0] == 2 * half * size_y and enter.shape[1] <= forward[0].shape[1]
-    assert leave.shape[0] == half * size_y
+    assert 2 * cells_z % slab == 0 and 2 * cells_z <= lanes
+    assert enter.shape[0] == 2 * slab and enter.shape[1] <= lanes
+    assert leave.shape[0] == slab
     return dict(
         symbol=real_part.astype(np.float32), first=first,
-        onward=slabs(forward + [right_z], half * size_y, forward[0].shape[1]),
+        onward=slabs(forward + [right_z], slab, lanes),
         later=later,
     ), tuple(int(x) for x in cells)
 
@@ -166,19 +179,51 @@
     return jnp.concatenate([total[:rows], total[rows:]], axis=1)
 
 
+def in_four(values):
+    count = values.shape[0] // 4
+    return [values[n * count : (n + 1) * count] for n in range(4)]
+
+
+def crossed(a, b, c, d):
+    s, t, u, v = a + c, a - c, b + d, b - d
+    return s + u, s - u, t + v, t - v
+
+
 def to_modes(field, t):
-    count = field.shape[0] // 2
-    first, second = field[:count], field[count:]
+    folded = crossed(*in_four(field))
     return jnp.concatenate(
-        [left_product(t["onward"][0], first + second), left_product(t["onward"][1], first - second)], axis=0
+        [left_product(quarter_matrix(t["onward"], n), part) for n, part in enumerate(folded)], axis=0
     )
 
 
 def to_cells(modes, t):
-    count = modes.shape[0] // 2
-    even = left_product(t["later"][0], modes[:count])
-    odd = left_product(t["later"][1], modes[count:])
-    return jnp.concatenate([even + odd, even - odd], axis=0)
+    parts = [left_product(quarter_matrix(t["later"], n), part) for n, part in enumerate(in_four(modes))]
+    return jnp.concatenate(crossed(*parts), axis=0)
+
+
+def backwards(rows):
+    return jnp.concatenate([rows[n : n + 1] for n in reversed(range(rows.shape[0]))], axis=0)
+
+
+def folded_cells(load, cells_x):
+    half = len(cells_x) // 2
+    quarters = []
+    for part in (cells_x[:half], cells_x[half:]):
+        layers = [load(x) for x in part]
+        middle = layers[0].shape[0] // 2
+        quarters += [layer[:middle] for layer in layers]
+        quarters += [backwards(layer[middle:]) for layer in layers]
+    return jnp.concatenate(quarters, axis=0)
+
+
+def natural_layer(field, place, layers):
+    count = field.shape[0] // layers // 2
+    side, within = divmod(place, layers // 2)
+    start = side * (field.shape[0] // 2) + within * count
+    mirror = start + field.shape[0] // 4
+    return jnp.concatenate(
+        [field[start : start + count], backwards(field[mirror : mirror + count])], axis=0
+    )
 
 
 def times(real_part, imag_part, field):
@@ -208,10 +253,10 @@
 
 def edges(rows, lanes, layers):
     place = lax.broadcasted_iota(jnp.int32, (rows, lanes), 0)
-    size_y = rows // layers
-    along_y = lax.rem(place, size_y)
-    outer = lax.rem(place, rows // 2) < size_y
-    return (outer.astype(F32) + ((along_y == 0) | (along_y == size_y - 1)).astype(F32)) * (1.0 / 12.0)
+    count = rows // layers // 2
+    outer_y = lax.rem(place, count) == 0
+    outer_x = lax.rem(place, rows // 4) < count
+    return (outer_x.astype(F32) + outer_y.astype(F32)) * (1.0 / 12.0)
 
 
 def prepare(dense, slow, layers, place, depth, amplitude, t, modes_ref, contrast_ref):
@@ -270,8 +315,8 @@
     inverse_ref[0] = symbol * scale
     inverse_ref[1] = damping * scale
     t["inverse"] = inverse_ref
-    dense = [jnp.concatenate([right_ref[c, x] for x in cells_x], axis=0) for c in range(2)]
-    slow = jnp.concatenate([slow_ref[x] for x in cells_x], axis=0)
+    dense = [folded_cells(lambda x, c=c: right_ref[c, x], cells_x) for c in range(2)]
+    slow = folded_cells(lambda x: slow_ref[x], cells_x)
     prepare(
         jnp.concatenate(dense, axis=1), slow, len(cells_x), place_ref[...], depth_ref[...], amp_ref, t,
         modes_ref, contrast_ref,
@@ -287,8 +332,8 @@
     other = 1 - core
     modes_ref[core] = own_modes_ref[...]
     contrast_ref[core] = own_contrast_ref[...]
-    dense = [jnp.concatenate([swap_ref[c, x] for x in cells_x], axis=0) for c in range(2)]
-    slow = jnp.concatenate([slow_ref[x] for x in cells_x], axis=0)
+    dense = [folded_cells(lambda x, c=c: swap_ref[c, x], cells_x) for c in range(2)]
+    slow = folded_cells(lambda x: slow_ref[x], cells_x)
     prepare(
         jnp.concatenate(dense, axis=1), slow, len(cells_x), place_ref[...], depth_ref[...], amp_ref, named(PREP_OTHER, refs),
         modes_ref.at[other], contrast_ref.at[other],
@@ -335,13 +380,13 @@
         wave, rest = [z_transform(to_cells(ref[...], t), t) for ref in (total_ref, term_ref)]
         rest = times(contrast_ref[tile, 0], contrast_ref[tile, 1], rest)
         for place, x in enumerate(cells_x):
-            here = slice(place * size_y, (place + 1) * size_y)
+            wave_layer, rest_layer = [natural_layer(field, place, size_x) for field in (wave, rest)]
             for c in range(2):
                 there = slice(c * cells_z, (c + 1) * cells_z)
-                both_ref[tile, 0, c, x] = wave[here, there]
-                both_ref[tile, 1, c, x] = rest[here, there]
+                both_ref[tile, 0, c, x] = wave_layer[:, there]
+                both_ref[tile, 1, c, x] = rest_layer[:, there]
                 if tile == 1 and x < 2:
-                    layer = wave[here, there]
+                    layer = wave_layer[:, there]
                     if x == 0:
                         both_ref[0, 1, c, size_x - 2] += layer * (-1.0 / 12.0)
                         both_ref[0, 1, c, size_x - 1] += layer * (16.0 / 12.0)
@@ -456,8 +501,11 @@
     for tile_row in (row, row + 1 - 2 * core):
         near_x = cells // (total_y * cells_z) - tile_row * size_x
         inside = (near_x >= 0) & (near_x < size_x) & (near_y >= 0) & (near_y < size_y)
-        folded = jnp.where(near_x < size_x // 2, near_x, size_x + size_x // 2 - 1 - near_x)
-        places.append(jnp.where(inside, folded * size_y + near_y, -1))
+        far_x, far_y = near_x >= size_x // 2, near_y >= size_y // 2
+        folded_x = jnp.where(far_x, size_x - 1 - near_x, near_x)
+        folded_y = jnp.where(far_y, size_y - 1 - near_y, near_y)
+        quarter = (2 * far_x + far_y) * (rows // 4)
+        places.append(jnp.where(inside, quarter + folded_x * (size_y // 2) + folded_y, -1))
     amplitudes = lax.dynamic_index_in_dim(source_amplitudes, rhs, 0, keepdims=False).T[:, None, :]
 
     depth = cells % cells_z

time: 65.5 us -> 64.2 us (0.980)
  waiting for transfers between devices: 31.7 us -> 30.8 us
    ppermute x6, waiting for transfers between devices: 25.9 us -> 25.1 us  [body(): trace_y0 = hand_on(lax.ppermute(outs0[0], axes, along_y))]
  transfers between devices with their start and end apart: 24 -> 24, of which waited for: 3 -> 4; matrix products, arithmetic and copies ran while one was open for 0% -> 0% of each run, Pallas kernels for 13% -> 13%
where the time goes in v16:
time: 64.2 us; the launch traced here: 63.8 us
  waiting for transfers between devices  30.8 us (48%)
  starting transfers between devices  20 us (31%)
  Pallas kernels  10.1 us (16%)
  between operations  1.54 us (2%)
  local copies, waits for them, and re-layouts  1.29 us (2%)
    ppermute x6, waiting for transfers between devices, body(): trace_y0 = hand_on(lax.ppermute(outs0[0], axes, along_y))  25.1 us
    pallas_call x14, Pallas kernels, solve(): pl.pallas_call(functools.partial(beat_kernel, tile, final), out_shape=(sh...  5.35 us
    ppermute x6, starting transfers between devices, body(): trace_y0 = hand_on(lax.ppermute(outs0[0], axes, along_y))  5.24 us
    ppermute x6, starting transfers between devices, body(): trace_y1 = lax.ppermute(outs1[1], axes, along_y)  5.24 us
    ppermute x6, starting transfers between devices, body(): trace_x = lax.ppermute(outs1[0], axes, along_x)  4.61 us
    ppermute x1, waiting for transfers between devices, body(): lax.ppermute(edge_y, axes, between([((k, j), (k, j - 1)) for k, j in ever...  4.37 us
    ppermute x1, starting transfers between devices, body(): lax.ppermute(edge_y, axes, between([((k, j), (k, j - 1)) for k, j in ever...  1.92 us
    ppermute x6, waiting for transfers between devices, body(): trace_x = lax.ppermute(outs1[0], axes, along_x)  1.31 us
  transfers between devices with their start and end apart: 24, of which 4 were waited for; matrix products, arithmetic and copies ran while one was open for 0% of the time, Pallas kernels for 13%

profile of v16, /device:TPU:29, one launch (start us, length us, event | category | flops | bytes accessed | tf_op | source)
XLA Modules:
  0.0 63.8 jit_solution(9158332609473029822)
XLA Ops:
  0.8 1.2 %dynamic-slice_bitcast_fusion = (f32[2,16,16,128]{3,2,1,0:T(8,128)S(1)}, f32[2,16,16,128]{3,2,1,0:T(8,128)S(1)}) fusion(f32[2,2,16,16,128]{4,3,2,1,0:T(8,128)} %param.8, s32[]{:T(128)S(6)} %select_n.77, s32[]{:T(128)S(6)} %select_n.76), kind=kLoop, calls=%fused_computation | loop fusion | bytes 1048584 | tf_op jit(solution)/shard_map/jit(dynamic_index_in_dim)/squeeze | solution.py:495
  1.9 0.7 %collective-permute-start = (f32[2,16,16,128]{3,2,1,0:T(8,128)S(1)}, f32[2,16,16,128]{3,2,1,0:T(8,128)S(1)}, u32[]{:S(2)}, u32[]{:S(2)}) collective-permute-start(f32[2,16,16,128]{3,2,1,0:T(8,128)S(1)} %get-tuple-element.135), channel_id=1, source_target_pairs={{0,4},{4,0},{1,5},{5,1},{2,6},{6,2},{3,7},{7,3},{8,12},{12,8},{9,1... | collective-permute-start | bytes 786440 | tf_op jit(solution)/shard_map/ppermute | solution.py:493
  2.7 0.1 collective-permute-start.1
  2.9 1.1 %prep.1 = (f32[256,256]{1,0:T(8,128)S(1)}, f32[2,256,128]{2,1,0:T(8,128)S(1)}, f32[2,256,128]{2,1,0:T(8,128)S(1)}, bf16[5,128,384]{2,1,0:T(8,128)(2,1)S(1)}) custom-call(f32[2,16,16,128]{3,2,1,0:T(8,128)S(1)} %get-tuple-element.134.right_ref, f32[16,16,128]{2,1,0:T(8,128)S(1)} %copy-done.2, s32[1,16]{1,0:T(1,128)S(1)} %and_select_fusion.2.place_ref, ...), custom_call_target="tpu_custom_call" | custom-call | flops 2000000000 | bytes 2000000 | tf_op jit(solution)/shard_map/prep/pallas_call | solution.py:512
  4.0 0.7 %prep_other.1 = (f32[2,256,256]{2,1,0:T(8,128)S(1)}, f32[2,2,256,128]{3,2,1,0:T(8,128)S(1)}) custom-call(s32[1]{0:T(128)} %bitcast.1.core_ref, s32[1]{0:T(128)} %bitcast.rhs_ref, f32[2,16,16,128]{3,2,1,0:T(8,128)S(1)} %collective-permute-done.swap_ref, f32[16,16,128]{2,1,0:T(8,128)S(1)} %collective-permute-done.1.slow_ref, ...), custom_call_target="tpu_custom_call" | custom-call | flops 2000000000 | bytes 2000000 | tf_op jit(solution)/shard_map/prep_other/pallas_call | solution.py:524
  4.8 0.1 upper.7
  4.9 0.7 %collective-permute-start.3 = (f32[32,256]{1,0:T(8,128)S(1)}, f32[32,256]{1,0:T(8,128)S(1)}, u32[]{:S(2)}, u32[]{:S(2)}) collective-permute-start(f32[32,256]{1,0:T(8,128)S(1)} %get-tuple-element.74), channel_id=1, source_target_pairs={{0,5},{4,1}} | collective-permute-start | bytes 98312 | tf_op jit(solution)/shard_map/ppermute | solution.py:574
  5.6 0.1 lower.7
  5.7 0.7 %collective-permute-start.2 = (f32[32,256]{1,0:T(8,128)S(1)}, f32[32,256]{1,0:T(8,128)S(1)}, u32[]{:S(2)}, u32[]{:S(2)}) collective-permute-start(f32[32,256]{1,0:T(8,128)S(1)} %get-tuple-element.73), channel_id=1, source_target_pairs={{0,12},{4,8}} | collective-permute-start | bytes 98312 | tf_op jit(solution)/shard_map/ppermute | solution.py:577
  6.4 0.7 %collective-permute-start.4 = (f32[32,256]{1,0:T(8,128)S(1)}, f32[32,256]{1,0:T(8,128)S(1)}, u32[]{:S(2)}, u32[]{:S(2)}) collective-permute-start(f32[32,256]{1,0:T(8,128)S(1)} %get-tuple-element.78), channel_id=1, source_target_pairs={{0,5},{4,1}} | collective-permute-start | bytes 98312 | tf_op jit(solution)/shard_map/ppermute | solution.py:579
  7.1 0.1 upper.8
  7.2 0.7 %collective-permute-start.6 = (f32[32,256]{1,0:T(8,128)S(1)}, f32[32,256]{1,0:T(8,128)S(1)}, u32[]{:S(2)}, u32[]{:S(2)}) collective-permute-start(f32[32,256]{1,0:T(8,128)S(1)} %get-tuple-element.82), channel_id=1, source_target_pairs={{1,6},{5,2},{8,13},{12,9}} | collective-permute-start | bytes 98312 | tf_op jit(solution)/shard_map/ppermute | solution.py:574
  7.8 0.1 lower.8
  7.9 0.7 %collective-permute-start.5 = (f32[32,256]{1,0:T(8,128)S(1)}, f32[32,256]{1,0:T(8,128)S(1)}, u32[]{:S(2)}, u32[]{:S(2)}) collective-permute-start(f32[32,256]{1,0:T(8,128)S(1)} %get-tuple-element.81), channel_id=1, source_target_pairs={{1,13},{5,9},{8,20},{12,16}} | collective-permute-start | bytes 98312 | tf_op jit(solution)/shard_map/ppermute | solution.py:577
  8.6 0.7 %collective-permute-start.7 = (f32[32,256]{1,0:T(8,128)S(1)}, f32[32,256]{1,0:T(8,128)S(1)}, u32[]{:S(2)}, u32[]{:S(2)}) collective-permute-start(f32[32,256]{1,0:T(8,128)S(1)} %get-tuple-element.86), channel_id=1, source_target_pairs={{1,6},{5,2},{8,13},{12,9}} | collective-permute-start | bytes 98312 | tf_op jit(solution)/shard_map/ppermute | solution.py:579
  9.3 0.1 upper.9
  9.4 0.7 %collective-permute-start.9 = (f32[32,256]{1,0:T(8,128)S(1)}, f32[32,256]{1,0:T(8,128)S(1)}, u32[]{:S(2)}, u32[]{:S(2)}) collective-permute-start(f32[32,256]{1,0:T(8,128)S(1)} %get-tuple-element.90), channel_id=1, source_target_pairs={{2,7},{6,3},{9,14},{13,10},{16,21},{20,17}} | collective-permute-start | bytes 98312 | tf_op jit(solution)/shard_map/ppermute | solution.py:574
  10.1 0.1 lower.9
  10.1 0.7 %collective-permute-start.8 = (f32[32,256]{1,0:T(8,128)S(1)}, f32[32,256]{1,0:T(8,128)S(1)}, u32[]{:S(2)}, u32[]{:S(2)}) collective-permute-start(f32[32,256]{1,0:T(8,128)S(1)} %get-tuple-element.89), channel_id=1, source_target_pairs={{2,14},{6,10},{9,21},{13,17},{16,28},{20,24}} | collective-permute-start | bytes 98312 | tf_op jit(solution)/shard_map/ppermute | solution.py:577
  10.8 0.7 %collective-permute-start.10 = (f32[32,256]{1,0:T(8,128)S(1)}, f32[32,256]{1,0:T(8,128)S(1)}, u32[]{:S(2)}, u32[]{:S(2)}) collective-permute-start(f32[32,256]{1,0:T(8,128)S(1)} %get-tuple-element.94), channel_id=1, source_target_pairs={{2,7},{6,3},{9,14},{13,10},{16,21},{20,17}} | collective-permute-start | bytes 98312 | tf_op jit(solution)/shard_map/ppermute | solution.py:579
  11.5 0.1 upper.10
  11.6 0.7 %collective-permute-start.12 = (f32[32,256]{1,0:T(8,128)S(1)}, f32[32,256]{1,0:T(8,128)S(1)}, u32[]{:S(2)}, u32[]{:S(2)}) collective-permute-start(f32[32,256]{1,0:T(8,128)S(1)} %get-tuple-element.98), channel_id=1, source_target_pairs={{10,15},{14,11},{17,22},{21,18},{24,29},{28,25}} | collective-permute-start | bytes 98312 | tf_op jit(solution)/shard_map/ppermute | solution.py:574
  12.3 0.3 lower.10
  12.6 0.7 %collective-permute-start.11 = (f32[32,256]{1,0:T(8,128)S(1)}, f32[32,256]{1,0:T(8,128)S(1)}, u32[]{:S(2)}, u32[]{:S(2)}) collective-permute-start(f32[32,256]{1,0:T(8,128)S(1)} %get-tuple-element.97), channel_id=1, source_target_pairs={{3,15},{7,11},{10,22},{14,18},{17,29},{21,25}} | collective-permute-start | bytes 98312 | tf_op jit(solution)/shard_map/ppermute | solution.py:577
  13.2 0.7 %collective-permute-start.13 = (f32[32,256]{1,0:T(8,128)S(1)}, f32[32,256]{1,0:T(8,128)S(1)}, u32[]{:S(2)}, u32[]{:S(2)}) collective-permute-start(f32[32,256]{1,0:T(8,128)S(1)} %get-tuple-element.102), channel_id=1, source_target_pairs={{10,15},{14,11},{17,22},{21,18},{24,29},{28,25}} | collective-permute-start | bytes 98312 | tf_op jit(solution)/shard_map/ppermute | solution.py:579
  13.9 0.1 upper.11
  14.0 1.3 %collective-permute-start.15 = (f32[32,256]{1,0:T(8,128)S(1)}, f32[32,256]{1,0:T(8,128)S(1)}, u32[]{:S(2)}, u32[]{:S(2)}) collective-permute-start(f32[32,256]{1,0:T(8,128)S(1)} %get-tuple-element.106), channel_id=1, source_target_pairs={{18,23},{22,19},{25,30},{29,26}} | collective-permute-start | bytes 98312 | tf_op jit(solution)/shard_map/ppermute | solution.py:574
  15.3 0.1 lower.11
  15.4 1.3 %collective-permute-start.14 = (f32[32,256]{1,0:T(8,128)S(1)}, f32[32,256]{1,0:T(8,128)S(1)}, u32[]{:S(2)}, u32[]{:S(2)}) collective-permute-start(f32[32,256]{1,0:T(8,128)S(1)} %get-tuple-element.105), channel_id=1, source_target_pairs={{11,23},{15,19},{18,30},{22,26}} | collective-permute-start | bytes 98312 | tf_op jit(solution)/shard_map/ppermute | solution.py:577
  16.7 1.3 %collective-permute-start.16 = (f32[32,256]{1,0:T(8,128)S(1)}, f32[32,256]{1,0:T(8,128)S(1)}, u32[]{:S(2)}, u32[]{:S(2)}) collective-permute-start(f32[32,256]{1,0:T(8,128)S(1)} %get-tuple-element.110), channel_id=1, source_target_pairs={{18,23},{22,19},{25,30},{29,26}} | collective-permute-start | bytes 98312 | tf_op jit(solution)/shard_map/ppermute | solution.py:579
  18.0 25.0 %collective-permute-done.15.in_ref = f32[32,256]{1,0:T(8,128)S(1)} collective-permute-done((f32[32,256]{1,0:T(8,128)S(1)}, f32[32,256]{1,0:T(8,128)S(1)}, u32[]{:S(2)}, u32[]{:S(2)}) %collective-permute-start.15) | collective-permute-done | bytes 32800 | tf_op jit(solution)/shard_map/ppermute | solution.py:574
  43.1 1.3 %collective-permute-done.14.trace_x_ref = f32[32,256]{1,0:T(8,128)S(1)} collective-permute-done((f32[32,256]{1,0:T(8,128)S(1)}, f32[32,256]{1,0:T(8,128)S(1)}, u32[]{:S(2)}, u32[]{:S(2)}) %collective-permute-start.14) | collective-permute-done | bytes 32800 | tf_op jit(solution)/shard_map/ppermute | solution.py:577
  44.4 1.9 %upper.12 = (f32[256,256]{1,0:T(8,128)S(1)}, f32[256,256]{1,0:T(8,128)S(1)}, f32[32,256]{1,0:T(8,128)S(1)}, f32[32,256]{1,0:T(8,128)S(1)}) custom-call(s32[1]{0:T(128)} %bitcast.9.active_ref, f32[2,256,256]{2,1,0:T(8,128)S(1)} %get-tuple-element.69.modes_ref, ...), custom_call_target="tpu_custom_call", output_to_operand_aliasing={{0}: (5, {}), {1}: (6, {})} | custom-call | flops 2000000000 | bytes 2000000 | tf_op jit(solution)/shard_map/upper/pallas_call | solution.py:539
  46.3 1.3 %collective-permute-start.18 = (f32[32,256]{1,0:T(8,128)S(1)}, f32[32,256]{1,0:T(8,128)S(1)}, u32[]{:S(2)}, u32[]{:S(2)}) collective-permute-start(f32[32,256]{1,0:T(8,128)S(1)} %get-tuple-element.114), channel_id=1, source_target_pairs={{26,31},{30,27}} | collective-permute-start | bytes 98312 | tf_op jit(solution)/shard_map/ppermute | solution.py:574
  47.6 1.9 %lower.12 = (f32[256,256]{1,0:T(8,128)S(1)}, f32[256,256]{1,0:T(8,128)S(1)}, f32[32,256]{1,0:T(8,128)S(1)}, f32[32,256]{1,0:T(8,128)S(1)}) custom-call(s32[1]{0:T(128)} %bitcast.9.active_ref, f32[2,256,256]{2,1,0:T(8,128)S(1)} %get-tuple-element.69.modes_ref, ...), custom_call_target="tpu_custom_call", output_to_operand_aliasing={{0}: (5, {}), {1}: (6, {})} | custom-call | flops 2000000000 | bytes 2000000 | tf_op jit(solution)/shard_map/lower/pallas_call | solution.py:539
  49.6 0.7 %collective-permute-start.17 = (f32[32,256]{1,0:T(8,128)S(1)}, f32[32,256]{1,0:T(8,128)S(1)}, u32[]{:S(2)}, u32[]{:S(2)}) collective-permute-start(f32[32,256]{1,0:T(8,128)S(1)} %get-tuple-element.113), channel_id=1, source_target_pairs={{19,31},{23,27}} | collective-permute-start | bytes 98312 | tf_op jit(solution)/shard_map/ppermute | solution.py:577
  50.3 1.3 %collective-permute-start.19 = (f32[32,256]{1,0:T(8,128)S(1)}, f32[32,256]{1,0:T(8,128)S(1)}, u32[]{:S(2)}, u32[]{:S(2)}) collective-permute-start(f32[32,256]{1,0:T(8,128)S(1)} %get-tuple-element.120), channel_id=1, source_target_pairs={{26,31},{30,27}} | collective-permute-start | bytes 98312 | tf_op jit(solution)/shard_map/ppermute | solution.py:579
  51.6 0.3 upper.13
  51.9 1.3 %collective-permute-start.21 = (f32[32,256]{1,0:T(8,128)S(1)}, f32[32,256]{1,0:T(8,128)S(1)}, u32[]{:S(2)}, u32[]{:S(2)}) collective-permute-start(f32[32,256]{1,0:T(8,128)S(1)} %get-tuple-element.127), channel_id=1, source_target_pairs={{8,4},{12,0},{9,5},{13,1},{10,6},{14,2},{11,7},{15,3},{16,12},{20,... | collective-permute-start | bytes 98312 | tf_op jit(solution)/shard_map/ppermute | solution.py:585
  53.2 0.3 lower.13
  53.5 1.9 %collective-permute-start.22 = (f32[2,32,256]{2,1,0:T(8,128)S(1)}, f32[2,32,256]{2,1,0:T(8,128)S(1)}, u32[]{:S(2)}, u32[]{:S(2)}) collective-permute-start(f32[2,32,256]{2,1,0:T(8,128)S(1)} %pad_maximum_fusion), channel_id=1, source_target_pairs={{1,4},{5,0},{2,5},{6,1},{3,6},{7,2},{9,12},{13,8},{10,13},{14,9},{... | collective-permute-start | bytes 196616 | tf_op jit(solution)/shard_map/ppermute | solution.py:587
  55.4 1.0 %finish.1 = (f32[2,2,16,16,128]{4,3,2,1,0:T(8,128)S(1)}, f32[2,2,16,16,128]{4,3,2,1,0:T(8,128)S(1)}) custom-call(s32[1]{0:T(128)} %bitcast.1.core_ref, f32[256,256]{1,0:T(8,128)S(1)} %get-tuple-element.117.total0_ref, f32[256,256]{1,0:T(8,128)S(1)} %get-tuple-element.118.term0_ref, f32[256,256]{1,0:T(8,128)S(1)} %get-tuple-element.123.total1_ref, ...), custom_call_target="tpu_custom_call" | custom-call | tf_op jit(solution)/shard_map/finish/pallas_call | solution.py:590
  56.4 0.4 collective-permute-start.20
  56.9 4.4 %collective-permute-done.22.edge_y_ref = f32[2,32,256]{2,1,0:T(8,128)S(1)} collective-permute-done((f32[2,32,256]{2,1,0:T(8,128)S(1)}, f32[2,32,256]{2,1,0:T(8,128)S(1)}, u32[]{:S(2)}, u32[]{:S(2)}) %collective-permute-start.22) | collective-permute-done | bytes 65568 | tf_op jit(solution)/shard_map/ppermute | solution.py:587
  61.3 0.4 collective-permute-start.23
  61.7 0.2 keep.1.keep_rest_ref
  61.9 0.8 %place_wave.1 = f32[2,2,16,16,128]{4,3,2,1,0:T(8,128)} custom-call(s32[1]{0:T(128)} %bitcast.rhs_ref, f32[2,2,16,16,128]{4,3,2,1,0:T(8,128)S(1)} %get-tuple-element.125.keep_ref, f32[2,2,16,16,128]{4,3,2,1,0:T(8,128)S(1)} %collective-permute-done.20.got_ref), custom_call_target="tpu_custom_call" | custom-call | flops 10000000000 | bytes 1000000 | tf_op jit(solution)/shard_map/place_wave/pallas_call | solution.py:612
  62.7 0.9 %place_rest.1 = f32[2,2,16,16,128]{4,3,2,1,0:T(8,128)} custom-call(s32[1]{0:T(128)} %bitcast.1.core_ref, s32[1]{0:T(128)} %bitcast.rhs_ref, f32[2,16,16,128]{3,2,1,0:T(8,128)S(1)} %keep.1.keep_rest_ref, f32[2,2,16,16,128]{4,3,2,1,0:T(8,128)S(1)} %collective-permute-done.20.got_ref, f32[64,256]{1,0:T(8,128)S(1)} %collective-permute-done.23.got_edge_ref, ...), custom_call_target="tpu_custom_call" | custom-call | tf_op jit(solution)/shard_map/place_rest/pallas_call | solution.py:622
  (54 shorter events, 0.3 us)
Async XLA Ops:
  0.6 2.2 %copy-start = (f32[2,16,2]{1,2,0:T(2,128)S(1)}, f32[2,16,2]{1,2,0:T(2,128)}, u32[]{:S(2)}) copy-start(f32[2,16,2]{1,2,0:T(2,128)} %param.11) | copy-start | bytes 772
  0.7 2.2 %copy-start.4 = (f32[256,128]{1,0:T(8,128)S(1)}, f32[256,128]{1,0:T(8,128)}, u32[]{:S(2)}) copy-start(f32[256,128]{1,0:T(8,128)} %constant.154.clone.refs_0_) | copy-start | bytes 393220
  0.7 2.0 %copy-start.6 = (s32[2,16]{1,0:T(2,128)S(1)}, s32[2,16]{1,0:T(2,128)}, u32[]{:S(2)}) copy-start(s32[2,16]{1,0:T(2,128)} %param.10) | copy-start | bytes 388
  0.7 1.9 %copy-start.2 = (f32[16,16,128]{2,1,0:T(8,128)S(1)}, f32[16,16,128]{2,1,0:T(8,128)}, u32[]{:S(2)}) copy-start(f32[16,16,128]{2,1,0:T(8,128)} %slow_ref.1) | copy-start | bytes 393220
  0.7 2.1 %copy-start.1 = (bf16[4,128,384]{2,1,0:T(8,128)(2,1)S(1)}, bf16[4,128,384]{2,1,0:T(8,128)(2,1)}, u32[]{:S(2)}) copy-start(bf16[4,128,384]{2,1,0:T(8,128)(2,1)} %constant.156.clone.refs_1_.z_ref) | copy-start | bytes 1179652
  0.7 2.1 %copy-start.3 = (bf16[5,128,384]{2,1,0:T(8,128)(2,1)S(1)}, bf16[5,128,384]{2,1,0:T(8,128)(2,1)}, u32[]{:S(2)}) copy-start(bf16[5,128,384]{2,1,0:T(8,128)(2,1)} %constant.157.clone.refs_2_) | copy-start | bytes 1474564
  1.9 2.1 %collective-permute-start = (f32[2,16,16,128]{3,2,1,0:T(8,128)S(1)}, f32[2,16,16,128]{3,2,1,0:T(8,128)S(1)}, u32[]{:S(2)}, u32[]{:S(2)}) collective-permute-start(f32[2,16,16,128]{3,2,1,0:T(8,128)S(1)} %get-tuple-element.135), channel_id=1, source_target_pairs={{0,4},{4,0},{1,5},{5,1},{2,6},{6,2},{3,7},{7,3},{8,12},{12,8},{9,1... | collective-permute-start | bytes 786440 | tf_op jit(solution)/shard_map/ppermute | solution.py:493
  2.7 1.3 %collective-permute-start.1 = (f32[16,16,128]{2,1,0:T(8,128)S(1)}, f32[16,16,128]{2,1,0:T(8,128)S(1)}, u32[]{:S(2)}, u32[]{:S(2)}) collective-permute-start(f32[16,16,128]{2,1,0:T(8,128)S(1)} %copy-done.2), channel_id=1, source_target_pairs={{0,4},{4,0},{1,5},{5,1},{2,6},{6,2},{3,7},{7,3},{8,12},{12,8},{9,1... | collective-permute-start | bytes 393224 | tf_op jit(solution)/shard_map/ppermute | solution.py:494
  4.9 2.2 %collective-permute-start.3 = (f32[32,256]{1,0:T(8,128)S(1)}, f32[32,256]{1,0:T(8,128)S(1)}, u32[]{:S(2)}, u32[]{:S(2)}) collective-permute-start(f32[32,256]{1,0:T(8,128)S(1)} %get-tuple-element.74), channel_id=1, source_target_pairs={{0,5},{4,1}} | collective-permute-start | bytes 98312 | tf_op jit(solution)/shard_map/ppermute | solution.py:574
  5.7 1.4 %collective-permute-start.2 = (f32[32,256]{1,0:T(8,128)S(1)}, f32[32,256]{1,0:T(8,128)S(1)}, u32[]{:S(2)}, u32[]{:S(2)}) collective-permute-start(f32[32,256]{1,0:T(8,128)S(1)} %get-tuple-element.73), channel_id=1, source_target_pairs={{0,12},{4,8}} | collective-permute-start | bytes 98312 | tf_op jit(solution)/shard_map/ppermute | solution.py:577
  6.4 1.5 %collective-permute-start.4 = (f32[32,256]{1,0:T(8,128)S(1)}, f32[32,256]{1,0:T(8,128)S(1)}, u32[]{:S(2)}, u32[]{:S(2)}) collective-permute-start(f32[32,256]{1,0:T(8,128)S(1)} %get-tuple-element.78), channel_id=1, source_target_pairs={{0,5},{4,1}} | collective-permute-start | bytes 98312 | tf_op jit(solution)/shard_map/ppermute | solution.py:579
  7.2 2.1 %collective-permute-start.6 = (f32[32,256]{1,0:T(8,128)S(1)}, f32[32,256]{1,0:T(8,128)S(1)}, u32[]{:S(2)}, u32[]{:S(2)}) collective-permute-start(f32[32,256]{1,0:T(8,128)S(1)} %get-tuple-element.82), channel_id=1, source_target_pairs={{1,6},{5,2},{8,13},{12,9}} | collective-permute-start | bytes 98312 | tf_op jit(solution)/shard_map/ppermute | solution.py:574
  7.9 1.4 %collective-permute-start.5 = (f32[32,256]{1,0:T(8,128)S(1)}, f32[32,256]{1,0:T(8,128)S(1)}, u32[]{:S(2)}, u32[]{:S(2)}) collective-permute-start(f32[32,256]{1,0:T(8,128)S(1)} %get-tuple-element.81), channel_id=1, source_target_pairs={{1,13},{5,9},{8,20},{12,16}} | collective-permute-start | bytes 98312 | tf_op jit(solution)/shard_map/ppermute | solution.py:577
  8.6 1.5 %collective-permute-start.7 = (f32[32,256]{1,0:T(8,128)S(1)}, f32[32,256]{1,0:T(8,128)S(1)}, u32[]{:S(2)}, u32[]{:S(2)}) collective-permute-start(f32[32,256]{1,0:T(8,128)S(1)} %get-tuple-element.86), channel_id=1, source_target_pairs={{1,6},{5,2},{8,13},{12,9}} | collective-permute-start | bytes 98312 | tf_op jit(solution)/shard_map/ppermute | solution.py:579
  9.4 2.1 %collective-permute-start.9 = (f32[32,256]{1,0:T(8,128)S(1)}, f32[32,256]{1,0:T(8,128)S(1)}, u32[]{:S(2)}, u32[]{:S(2)}) collective-permute-start(f32[32,256]{1,0:T(8,128)S(1)} %get-tuple-element.90), channel_id=1, source_target_pairs={{2,7},{6,3},{9,14},{13,10},{16,21},{20,17}} | collective-permute-start | bytes 98312 | tf_op jit(solution)/shard_map/ppermute | solution.py:574
  10.1 1.4 %collective-permute-start.8 = (f32[32,256]{1,0:T(8,128)S(1)}, f32[32,256]{1,0:T(8,128)S(1)}, u32[]{:S(2)}, u32[]{:S(2)}) collective-permute-start(f32[32,256]{1,0:T(8,128)S(1)} %get-tuple-element.89), channel_id=1, source_target_pairs={{2,14},{6,10},{9,21},{13,17},{16,28},{20,24}} | collective-permute-start | bytes 98312 | tf_op jit(solution)/shard_map/ppermute | solution.py:577
  10.8 1.5 %collective-permute-start.10 = (f32[32,256]{1,0:T(8,128)S(1)}, f32[32,256]{1,0:T(8,128)S(1)}, u32[]{:S(2)}, u32[]{:S(2)}) collective-permute-start(f32[32,256]{1,0:T(8,128)S(1)} %get-tuple-element.94), channel_id=1, source_target_pairs={{2,7},{6,3},{9,14},{13,10},{16,21},{20,17}} | collective-permute-start | bytes 98312 | tf_op jit(solution)/shard_map/ppermute | solution.py:579
  11.6 2.3 %collective-permute-start.12 = (f32[32,256]{1,0:T(8,128)S(1)}, f32[32,256]{1,0:T(8,128)S(1)}, u32[]{:S(2)}, u32[]{:S(2)}) collective-permute-start(f32[32,256]{1,0:T(8,128)S(1)} %get-tuple-element.98), channel_id=1, source_target_pairs={{10,15},{14,11},{17,22},{21,18},{24,29},{28,25}} | collective-permute-start | bytes 98312 | tf_op jit(solution)/shard_map/ppermute | solution.py:574
  12.6 1.4 %collective-permute-start.11 = (f32[32,256]{1,0:T(8,128)S(1)}, f32[32,256]{1,0:T(8,128)S(1)}, u32[]{:S(2)}, u32[]{:S(2)}) collective-permute-start(f32[32,256]{1,0:T(8,128)S(1)} %get-tuple-element.97), channel_id=1, source_target_pairs={{3,15},{7,11},{10,22},{14,18},{17,29},{21,25}} | collective-permute-start | bytes 98312 | tf_op jit(solution)/shard_map/ppermute | solution.py:577
  13.2 2.1 %collective-permute-start.13 = (f32[32,256]{1,0:T(8,128)S(1)}, f32[32,256]{1,0:T(8,128)S(1)}, u32[]{:S(2)}, u32[]{:S(2)}) collective-permute-start(f32[32,256]{1,0:T(8,128)S(1)} %get-tuple-element.102), channel_id=1, source_target_pairs={{10,15},{14,11},{17,22},{21,18},{24,29},{28,25}} | collective-permute-start | bytes 98312 | tf_op jit(solution)/shard_map/ppermute | solution.py:579
  14.0 29.0 %collective-permute-start.15 = (f32[32,256]{1,0:T(8,128)S(1)}, f32[32,256]{1,0:T(8,128)S(1)}, u32[]{:S(2)}, u32[]{:S(2)}) collective-permute-start(f32[32,256]{1,0:T(8,128)S(1)} %get-tuple-element.106), channel_id=1, source_target_pairs={{18,23},{22,19},{25,30},{29,26}} | collective-permute-start | bytes 98312 | tf_op jit(solution)/shard_map/ppermute | solution.py:574
  15.4 29.0 %collective-permute-start.14 = (f32[32,256]{1,0:T(8,128)S(1)}, f32[32,256]{1,0:T(8,128)S(1)}, u32[]{:S(2)}, u32[]{:S(2)}) collective-permute-start(f32[32,256]{1,0:T(8,128)S(1)} %get-tuple-element.105), channel_id=1, source_target_pairs={{11,23},{15,19},{18,30},{22,26}} | collective-permute-start | bytes 98312 | tf_op jit(solution)/shard_map/ppermute | solution.py:577
  16.7 30.9 %collective-permute-start.16 = (f32[32,256]{1,0:T(8,128)S(1)}, f32[32,256]{1,0:T(8,128)S(1)}, u32[]{:S(2)}, u32[]{:S(2)}) collective-permute-start(f32[32,256]{1,0:T(8,128)S(1)} %get-tuple-element.110), channel_id=1, source_target_pairs={{18,23},{22,19},{25,30},{29,26}} | collective-permute-start | bytes 98312 | tf_op jit(solution)/shard_map/ppermute | solution.py:579
  46.3 5.3 %collective-permute-start.18 = (f32[32,256]{1,0:T(8,128)S(1)}, f32[32,256]{1,0:T(8,128)S(1)}, u32[]{:S(2)}, u32[]{:S(2)}) collective-permute-start(f32[32,256]{1,0:T(8,128)S(1)} %get-tuple-element.114), channel_id=1, source_target_pairs={{26,31},{30,27}} | collective-permute-start | bytes 98312 | tf_op jit(solution)/shard_map/ppermute | solution.py:574
  47.6 4.0 %copy-start.5 = (bf16[64,768]{1,0:T(8,128)(2,1)S(1)}, bf16[64,768]{1,0:T(8,128)(2,1)}, u32[]{:S(2)}) copy-start(bf16[64,768]{1,0:T(8,128)(2,1)} %constant.155.clone.refs_3_) | copy-start | bytes 294916
  49.6 2.0 %collective-permute-start.17 = (f32[32,256]{1,0:T(8,128)S(1)}, f32[32,256]{1,0:T(8,128)S(1)}, u32[]{:S(2)}, u32[]{:S(2)}) collective-permute-start(f32[32,256]{1,0:T(8,128)S(1)} %get-tuple-element.113), channel_id=1, source_target_pairs={{19,31},{23,27}} | collective-permute-start | bytes 98312 | tf_op jit(solution)/shard_map/ppermute | solution.py:577
  50.3 2.9 %collective-permute-start.19 = (f32[32,256]{1,0:T(8,128)S(1)}, f32[32,256]{1,0:T(8,128)S(1)}, u32[]{:S(2)}, u32[]{:S(2)}) collective-permute-start(f32[32,256]{1,0:T(8,128)S(1)} %get-tuple-element.120), channel_id=1, source_target_pairs={{26,31},{30,27}} | collective-permute-start | bytes 98312 | tf_op jit(solution)/shard_map/ppermute | solution.py:579
  51.9 5.0 %collective-permute-start.21 = (f32[32,256]{1,0:T(8,128)S(1)}, f32[32,256]{1,0:T(8,128)S(1)}, u32[]{:S(2)}, u32[]{:S(2)}) collective-permute-start(f32[32,256]{1,0:T(8,128)S(1)} %get-tuple-element.127), channel_id=1, source_target_pairs={{8,4},{12,0},{9,5},{13,1},{10,6},{14,2},{11,7},{15,3},{16,12},{20,... | collective-permute-start | bytes 98312 | tf_op jit(solution)/shard_map/ppermute | solution.py:585
  53.5 7.8 %collective-permute-start.22 = (f32[2,32,256]{2,1,0:T(8,128)S(1)}, f32[2,32,256]{2,1,0:T(8,128)S(1)}, u32[]{:S(2)}, u32[]{:S(2)}) collective-permute-start(f32[2,32,256]{2,1,0:T(8,128)S(1)} %pad_maximum_fusion), channel_id=1, source_target_pairs={{1,4},{5,0},{2,5},{6,1},{3,6},{7,2},{9,12},{13,8},{10,13},{14,9},{... | collective-permute-start | bytes 196616 | tf_op jit(solution)/shard_map/ppermute | solution.py:587
  56.4 5.4 %collective-permute-start.20 = (f32[2,2,16,16,128]{4,3,2,1,0:T(8,128)S(1)}, f32[2,2,16,16,128]{4,3,2,1,0:T(8,128)S(1)}, u32[]{:S(2)}, u32[]{:S(2)}) collective-permute-start(f32[2,2,16,16,128]{4,3,2,1,0:T(8,128)S(1)} %get-tuple-element.126), channel_id=1, source_target_pairs={{0,4},{4,0},{1,5},{5,1},{2,6},{6,2},{3,7},{7,3},{8,12},{12,8},{9,1... | collective-permute-start | bytes 1572872 | tf_op jit(solution)/shard_map/ppermute | solution.py:599
  61.3 1.5 %collective-permute-start.23 = (f32[64,256]{1,0:T(8,128)S(1)}, f32[64,256]{1,0:T(8,128)S(1)}, u32[]{:S(2)}, u32[]{:S(2)}) collective-permute-start(f32[64,256]{1,0:T(8,128)S(1)} %pad_maximum_fusion.1), channel_id=1, source_target_pairs={{0,4},{4,0},{1,5},{5,1},{2,6},{6,2},{3,7},{7,3},{8,12},{12,8},{9,1... | collective-permute-start | bytes 196616 | tf_op jit(solution)/shard_map/ppermute | solution.py:602

commit v17 on v16

--- a/solution.py
+++ b/solution.py
@@ -303,8 +303,9 @@
     later_refs = refs[len(PREP) : len(PREP) + len(LATER)]
     modes_ref, contrast_ref, inverse_ref, *held_refs, sems = refs[len(PREP) + len(LATER) :]
     copies = [
-        pltpu.make_async_copy(later_ref, held_ref, sems.at[n])
-        for n, (later_ref, held_ref) in enumerate(zip(later_refs, held_refs))
+        pltpu.make_async_copy(later_ref.at[n], held_ref.at[n], sems.at[m, n])
+        for m, (later_ref, held_ref) in enumerate(zip(later_refs, held_refs))
+        for n in range(later_ref.shape[0])
     ]
     for copy in copies:
         copy.start()
@@ -416,12 +417,20 @@
     add_later(rest_ref, edges[:count], edges[count:], (core_ref[0] == 1).astype(F32))
 
 
+def copies_in_parts(source, target, sems):
+    half = source.shape[1] // 2
+    return [
+        pltpu.make_async_copy(
+            source.at[c, pl.ds(h * half, half)], target.at[c, pl.ds(h * half, half)], sems.at[2 * c + h]
+        )
+        for c in range(2) for h in range(2)
+    ]
+
+
 def place_wave_kernel(rhs_ref, keep_ref, got_ref, wave_ref, sems):
     rhs = rhs_ref[0]
-    copies = [
-        pltpu.make_async_copy(keep_ref.at[0], wave_ref.at[rhs], sems.at[0]),
-        pltpu.make_async_copy(got_ref.at[0], wave_ref.at[1 - rhs], sems.at[1]),
-    ]
+    copies = copies_in_parts(keep_ref.at[0], wave_ref.at[rhs], sems.at[0])
+    copies += copies_in_parts(got_ref.at[0], wave_ref.at[1 - rhs], sems.at[1])
     for copy in copies:
         copy.start()
     for copy in copies:
@@ -431,14 +440,16 @@
 def place_rest_kernel(core_ref, rhs_ref, keep_rest_ref, got_ref, got_edge_ref, z_ref, rest_ref, work_ref, sems):
     rhs = rhs_ref[0]
     count = got_edge_ref.shape[0] // 2
-    copies = [pltpu.make_async_copy(keep_rest_ref, rest_ref.at[rhs], sems.at[0])]
-    copies[0].start()
+    copies = copies_in_parts(keep_rest_ref, rest_ref.at[rhs], sems.at[0])
+    for copy in copies:
+        copy.start()
     work_ref[...] = got_ref[1]
     edges = z_transform(got_edge_ref[...], dict(onward=z_ref))
     add_later(work_ref, edges[:count], edges[count:], (core_ref[0] == 1).astype(F32))
-    copies.append(pltpu.make_async_copy(work_ref, rest_ref.at[1 - rhs], sems.at[1]))
-    copies[1].start()
-    for copy in copies:
+    more = copies_in_parts(work_ref, rest_ref.at[1 - rhs], sems.at[1])
+    for copy in more:
+        copy.start()
+    for copy in copies + more:
         copy.wait()
 
 
@@ -515,7 +526,7 @@
         + tuple(jax.ShapeDtypeStruct(t[name].shape, BF16) for name in LATER),
         in_specs=[whole()] * (5 + len(PREP)) + [anywhere()] * len(LATER),
         out_specs=(whole(),) * (3 + len(LATER)),
-        scratch_shapes=[pltpu.SemaphoreType.DMA((len(LATER),))],
+        scratch_shapes=[pltpu.SemaphoreType.DMA((len(LATER), max(t[name].shape[0] for name in LATER)))],
         compiler_params=PARAMS,
         cost_estimate=SOLVE_COST,
         name="prep",
@@ -614,7 +625,7 @@
         out_shape=shaped(*right_side.shape),
         in_specs=[scalars()] + [whole()] * 2,
         out_specs=anywhere(),
-        scratch_shapes=[pltpu.SemaphoreType.DMA((2,))],
+        scratch_shapes=[pltpu.SemaphoreType.DMA((2, 4))],
         compiler_params=PARAMS,
         cost_estimate=KEEP_COST,
         name="place_wave",
@@ -626,7 +637,7 @@
         out_specs=anywhere(),
         scratch_shapes=[
             pltpu.VMEM((2, size_x, size_y, cells_z), F32),
-            pltpu.SemaphoreType.DMA((2,)),
+            pltpu.SemaphoreType.DMA((2, 4)),
         ],
         compiler_params=PARAMS,
         name="place_rest",

time: 64.2 us -> 64.8 us (level)
  transfers between devices with their start and end apart: 24 -> 24, of which waited for: 4 -> 3; matrix products, arithmetic and copies ran while one was open for 0% -> 0% of each run, Pallas kernels for 13% -> 14%
where the time goes in v17:
time: 64.8 us; the launch traced here: 64.4 us
  waiting for transfers between devices  30.9 us (48%)
  starting transfers between devices  20 us (31%)
  Pallas kernels  10.6 us (16%)
  between operations  1.55 us (2%)
  local copies, waits for them, and re-layouts  1.29 us (2%)
    ppermute x6, waiting for transfers between devices, body(): trace_y0 = hand_on(lax.ppermute(outs0[0], axes, along_y))  25.2 us
    pallas_call x14, Pallas kernels, solve(): pl.pallas_call(functools.partial(beat_kernel, tile, final), out_shape=(sh...  5.35 us
    ppermute x6, starting transfers between devices, body(): trace_y0 = hand_on(lax.ppermute(outs0[0], axes, along_y))  5.24 us
    ppermute x6, starting transfers between devices, body(): trace_y1 = lax.ppermute(outs1[1], axes, along_y)  5.24 us
    ppermute x6, starting transfers between devices, body(): trace_x = lax.ppermute(outs1[0], axes, along_x)  4.61 us
    ppermute x1, waiting for transfers between devices, body(): lax.ppermute(edge_y, axes, between([((k, j), (k, j - 1)) for k, j in ever...  4.37 us
    ppermute x1, starting transfers between devices, body(): lax.ppermute(edge_y, axes, between([((k, j), (k, j - 1)) for k, j in ever...  1.92 us
    pallas_call x1, Pallas kernels, body(): pl.pallas_call(functools.partial(prep_kernel, cells_x), out_shape=(shaped...  1.42 us
  transfers between devices with their start and end apart: 24, of which 3 were waited for; matrix products, arithmetic and copies ran while one was open for 0% of the time, Pallas kernels for 14%

profile of v17, /device:TPU:29, one launch (start us, length us, event | category | flops | bytes accessed | tf_op | source)
XLA Modules:
  0.0 64.4 jit_solution(2755827716532696373)
XLA Ops:
  0.8 1.2 %dynamic-slice_bitcast_fusion = (f32[2,16,16,128]{3,2,1,0:T(8,128)S(1)}, f32[2,16,16,128]{3,2,1,0:T(8,128)S(1)}) fusion(f32[2,2,16,16,128]{4,3,2,1,0:T(8,128)} %param.8, s32[]{:T(128)S(6)} %select_n.77, s32[]{:T(128)S(6)} %select_n.76), kind=kLoop, calls=%fused_computation | loop fusion | bytes 1048584 | tf_op jit(solution)/shard_map/jit(dynamic_index_in_dim)/squeeze | solution.py:506
  1.9 0.7 %collective-permute-start = (f32[2,16,16,128]{3,2,1,0:T(8,128)S(1)}, f32[2,16,16,128]{3,2,1,0:T(8,128)S(1)}, u32[]{:S(2)}, u32[]{:S(2)}) collective-permute-start(f32[2,16,16,128]{3,2,1,0:T(8,128)S(1)} %get-tuple-element.135), channel_id=1, source_target_pairs={{0,4},{4,0},{1,5},{5,1},{2,6},{6,2},{3,7},{7,3},{8,12},{12,8},{9,1... | collective-permute-start | bytes 786440 | tf_op jit(solution)/shard_map/ppermute | solution.py:504
  2.7 0.1 collective-permute-start.1
  2.9 1.4 %prep.1 = (f32[256,256]{1,0:T(8,128)S(1)}, f32[2,256,128]{2,1,0:T(8,128)S(1)}, f32[2,256,128]{2,1,0:T(8,128)S(1)}, bf16[5,128,384]{2,1,0:T(8,128)(2,1)S(1)}) custom-call(f32[2,16,16,128]{3,2,1,0:T(8,128)S(1)} %get-tuple-element.134.right_ref, f32[16,16,128]{2,1,0:T(8,128)S(1)} %copy-done.2, s32[1,16]{1,0:T(1,128)S(1)} %and_select_fusion.2.place_ref, ...), custom_call_target="tpu_custom_call" | custom-call | flops 2000000000 | bytes 2000000 | tf_op jit(solution)/shard_map/prep/pallas_call | solution.py:523
  4.3 0.7 %prep_other.1 = (f32[2,256,256]{2,1,0:T(8,128)S(1)}, f32[2,2,256,128]{3,2,1,0:T(8,128)S(1)}) custom-call(s32[1]{0:T(128)} %bitcast.1.core_ref, s32[1]{0:T(128)} %bitcast.rhs_ref, f32[2,16,16,128]{3,2,1,0:T(8,128)S(1)} %collective-permute-done.swap_ref, f32[16,16,128]{2,1,0:T(8,128)S(1)} %collective-permute-done.1.slow_ref, ...), custom_call_target="tpu_custom_call" | custom-call | flops 2000000000 | bytes 2000000 | tf_op jit(solution)/shard_map/prep_other/pallas_call | solution.py:535
  5.1 0.1 upper.7
  5.2 0.7 %collective-permute-start.3 = (f32[32,256]{1,0:T(8,128)S(1)}, f32[32,256]{1,0:T(8,128)S(1)}, u32[]{:S(2)}, u32[]{:S(2)}) collective-permute-start(f32[32,256]{1,0:T(8,128)S(1)} %get-tuple-element.74), channel_id=1, source_target_pairs={{0,5},{4,1}} | collective-permute-start | bytes 98312 | tf_op jit(solution)/shard_map/ppermute | solution.py:585
  5.9 0.1 lower.7
  6.0 0.7 %collective-permute-start.2 = (f32[32,256]{1,0:T(8,128)S(1)}, f32[32,256]{1,0:T(8,128)S(1)}, u32[]{:S(2)}, u32[]{:S(2)}) collective-permute-start(f32[32,256]{1,0:T(8,128)S(1)} %get-tuple-element.73), channel_id=1, source_target_pairs={{0,12},{4,8}} | collective-permute-start | bytes 98312 | tf_op jit(solution)/shard_map/ppermute | solution.py:588
  6.7 0.7 %collective-permute-start.4 = (f32[32,256]{1,0:T(8,128)S(1)}, f32[32,256]{1,0:T(8,128)S(1)}, u32[]{:S(2)}, u32[]{:S(2)}) collective-permute-start(f32[32,256]{1,0:T(8,128)S(1)} %get-tuple-element.78), channel_id=1, source_target_pairs={{0,5},{4,1}} | collective-permute-start | bytes 98312 | tf_op jit(solution)/shard_map/ppermute | solution.py:590
  7.4 0.1 upper.8
  7.5 0.7 %collective-permute-start.6 = (f32[32,256]{1,0:T(8,128)S(1)}, f32[32,256]{1,0:T(8,128)S(1)}, u32[]{:S(2)}, u32[]{:S(2)}) collective-permute-start(f32[32,256]{1,0:T(8,128)S(1)} %get-tuple-element.82), channel_id=1, source_target_pairs={{1,6},{5,2},{8,13},{12,9}} | collective-permute-start | bytes 98312 | tf_op jit(solution)/shard_map/ppermute | solution.py:585
  8.2 0.1 lower.8
  8.2 0.7 %collective-permute-start.5 = (f32[32,256]{1,0:T(8,128)S(1)}, f32[32,256]{1,0:T(8,128)S(1)}, u32[]{:S(2)}, u32[]{:S(2)}) collective-permute-start(f32[32,256]{1,0:T(8,128)S(1)} %get-tuple-element.81), channel_id=1, source_target_pairs={{1,13},{5,9},{8,20},{12,16}} | collective-permute-start | bytes 98312 | tf_op jit(solution)/shard_map/ppermute | solution.py:588
  8.9 0.7 %collective-permute-start.7 = (f32[32,256]{1,0:T(8,128)S(1)}, f32[32,256]{1,0:T(8,128)S(1)}, u32[]{:S(2)}, u32[]{:S(2)}) collective-permute-start(f32[32,256]{1,0:T(8,128)S(1)} %get-tuple-element.86), channel_id=1, source_target_pairs={{1,6},{5,2},{8,13},{12,9}} | collective-permute-start | bytes 98312 | tf_op jit(solution)/shard_map/ppermute | solution.py:590
  9.6 0.1 upper.9
  9.7 0.7 %collective-permute-start.9 = (f32[32,256]{1,0:T(8,128)S(1)}, f32[32,256]{1,0:T(8,128)S(1)}, u32[]{:S(2)}, u32[]{:S(2)}) collective-permute-start(f32[32,256]{1,0:T(8,128)S(1)} %get-tuple-element.90), channel_id=1, source_target_pairs={{2,7},{6,3},{9,14},{13,10},{16,21},{20,17}} | collective-permute-start | bytes 98312 | tf_op jit(solution)/shard_map/ppermute | solution.py:585
  10.4 0.1 lower.9
  10.5 0.7 %collective-permute-start.8 = (f32[32,256]{1,0:T(8,128)S(1)}, f32[32,256]{1,0:T(8,128)S(1)}, u32[]{:S(2)}, u32[]{:S(2)}) collective-permute-start(f32[32,256]{1,0:T(8,128)S(1)} %get-tuple-element.89), channel_id=1, source_target_pairs={{2,14},{6,10},{9,21},{13,17},{16,28},{20,24}} | collective-permute-start | bytes 98312 | tf_op jit(solution)/shard_map/ppermute | solution.py:588
  11.1 0.7 %collective-permute-start.10 = (f32[32,256]{1,0:T(8,128)S(1)}, f32[32,256]{1,0:T(8,128)S(1)}, u32[]{:S(2)}, u32[]{:S(2)}) collective-permute-start(f32[32,256]{1,0:T(8,128)S(1)} %get-tuple-element.94), channel_id=1, source_target_pairs={{2,7},{6,3},{9,14},{13,10},{16,21},{20,17}} | collective-permute-start | bytes 98312 | tf_op jit(solution)/shard_map/ppermute | solution.py:590
  11.8 0.1 upper.10
  11.9 0.7 %collective-permute-start.12 = (f32[32,256]{1,0:T(8,128)S(1)}, f32[32,256]{1,0:T(8,128)S(1)}, u32[]{:S(2)}, u32[]{:S(2)}) collective-permute-start(f32[32,256]{1,0:T(8,128)S(1)} %get-tuple-element.98), channel_id=1, source_target_pairs={{10,15},{14,11},{17,22},{21,18},{24,29},{28,25}} | collective-permute-start | bytes 98312 | tf_op jit(solution)/shard_map/ppermute | solution.py:585
  12.6 0.3 lower.10
  12.9 0.7 %collective-permute-start.11 = (f32[32,256]{1,0:T(8,128)S(1)}, f32[32,256]{1,0:T(8,128)S(1)}, u32[]{:S(2)}, u32[]{:S(2)}) collective-permute-start(f32[32,256]{1,0:T(8,128)S(1)} %get-tuple-element.97), channel_id=1, source_target_pairs={{3,15},{7,11},{10,22},{14,18},{17,29},{21,25}} | collective-permute-start | bytes 98312 | tf_op jit(solution)/shard_map/ppermute | solution.py:588
  13.5 0.7 %collective-permute-start.13 = (f32[32,256]{1,0:T(8,128)S(1)}, f32[32,256]{1,0:T(8,128)S(1)}, u32[]{:S(2)}, u32[]{:S(2)}) collective-permute-start(f32[32,256]{1,0:T(8,128)S(1)} %get-tuple-element.102), channel_id=1, source_target_pairs={{10,15},{14,11},{17,22},{21,18},{24,29},{28,25}} | collective-permute-start | bytes 98312 | tf_op jit(solution)/shard_map/ppermute | solution.py:590
  14.3 0.1 upper.11
  14.3 1.3 %collective-permute-start.15 = (f32[32,256]{1,0:T(8,128)S(1)}, f32[32,256]{1,0:T(8,128)S(1)}, u32[]{:S(2)}, u32[]{:S(2)}) collective-permute-start(f32[32,256]{1,0:T(8,128)S(1)} %get-tuple-element.106), channel_id=1, source_target_pairs={{18,23},{22,19},{25,30},{29,26}} | collective-permute-start | bytes 98312 | tf_op jit(solution)/shard_map/ppermute | solution.py:585
  15.6 0.1 lower.11
  15.7 1.3 %collective-permute-start.14 = (f32[32,256]{1,0:T(8,128)S(1)}, f32[32,256]{1,0:T(8,128)S(1)}, u32[]{:S(2)}, u32[]{:S(2)}) collective-permute-start(f32[32,256]{1,0:T(8,128)S(1)} %get-tuple-element.105), channel_id=1, source_target_pairs={{11,23},{15,19},{18,30},{22,26}} | collective-permute-start | bytes 98312 | tf_op jit(solution)/shard_map/ppermute | solution.py:588
  17.0 1.3 %collective-permute-start.16 = (f32[32,256]{1,0:T(8,128)S(1)}, f32[32,256]{1,0:T(8,128)S(1)}, u32[]{:S(2)}, u32[]{:S(2)}) collective-permute-start(f32[32,256]{1,0:T(8,128)S(1)} %get-tuple-element.110), channel_id=1, source_target_pairs={{18,23},{22,19},{25,30},{29,26}} | collective-permute-start | bytes 98312 | tf_op jit(solution)/shard_map/ppermute | solution.py:590
  18.3 25.2 %collective-permute-done.15.in_ref = f32[32,256]{1,0:T(8,128)S(1)} collective-permute-done((f32[32,256]{1,0:T(8,128)S(1)}, f32[32,256]{1,0:T(8,128)S(1)}, u32[]{:S(2)}, u32[]{:S(2)}) %collective-permute-start.15) | collective-permute-done | bytes 32800 | tf_op jit(solution)/shard_map/ppermute | solution.py:585
  43.5 1.3 %collective-permute-done.14.trace_x_ref = f32[32,256]{1,0:T(8,128)S(1)} collective-permute-done((f32[32,256]{1,0:T(8,128)S(1)}, f32[32,256]{1,0:T(8,128)S(1)}, u32[]{:S(2)}, u32[]{:S(2)}) %collective-permute-start.14) | collective-permute-done | bytes 32800 | tf_op jit(solution)/shard_map/ppermute | solution.py:588
  44.8 1.9 %upper.12 = (f32[256,256]{1,0:T(8,128)S(1)}, f32[256,256]{1,0:T(8,128)S(1)}, f32[32,256]{1,0:T(8,128)S(1)}, f32[32,256]{1,0:T(8,128)S(1)}) custom-call(s32[1]{0:T(128)} %bitcast.9.active_ref, f32[2,256,256]{2,1,0:T(8,128)S(1)} %get-tuple-element.69.modes_ref, ...), custom_call_target="tpu_custom_call", output_to_operand_aliasing={{0}: (5, {}), {1}: (6, {})} | custom-call | flops 2000000000 | bytes 2000000 | tf_op jit(solution)/shard_map/upper/pallas_call | solution.py:550
  46.7 1.3 %collective-permute-start.18 = (f32[32,256]{1,0:T(8,128)S(1)}, f32[32,256]{1,0:T(8,128)S(1)}, u32[]{:S(2)}, u32[]{:S(2)}) collective-permute-start(f32[32,256]{1,0:T(8,128)S(1)} %get-tuple-element.114), channel_id=1, source_target_pairs={{26,31},{30,27}} | collective-permute-start | bytes 98312 | tf_op jit(solution)/shard_map/ppermute | solution.py:585
  48.1 1.9 %lower.12 = (f32[256,256]{1,0:T(8,128)S(1)}, f32[256,256]{1,0:T(8,128)S(1)}, f32[32,256]{1,0:T(8,128)S(1)}, f32[32,256]{1,0:T(8,128)S(1)}) custom-call(s32[1]{0:T(128)} %bitcast.9.active_ref, f32[2,256,256]{2,1,0:T(8,128)S(1)} %get-tuple-element.69.modes_ref, ...), custom_call_target="tpu_custom_call", output_to_operand_aliasing={{0}: (5, {}), {1}: (6, {})} | custom-call | flops 2000000000 | bytes 2000000 | tf_op jit(solution)/shard_map/lower/pallas_call | solution.py:550
  50.0 0.7 %collective-permute-start.17 = (f32[32,256]{1,0:T(8,128)S(1)}, f32[32,256]{1,0:T(8,128)S(1)}, u32[]{:S(2)}, u32[]{:S(2)}) collective-permute-start(f32[32,256]{1,0:T(8,128)S(1)} %get-tuple-element.113), channel_id=1, source_target_pairs={{19,31},{23,27}} | collective-permute-start | bytes 98312 | tf_op jit(solution)/shard_map/ppermute | solution.py:588
  50.7 1.3 %collective-permute-start.19 = (f32[32,256]{1,0:T(8,128)S(1)}, f32[32,256]{1,0:T(8,128)S(1)}, u32[]{:S(2)}, u32[]{:S(2)}) collective-permute-start(f32[32,256]{1,0:T(8,128)S(1)} %get-tuple-element.120), channel_id=1, source_target_pairs={{26,31},{30,27}} | collective-permute-start | bytes 98312 | tf_op jit(solution)/shard_map/ppermute | solution.py:590
  52.0 0.3 upper.13
  52.3 1.3 %collective-permute-start.21 = (f32[32,256]{1,0:T(8,128)S(1)}, f32[32,256]{1,0:T(8,128)S(1)}, u32[]{:S(2)}, u32[]{:S(2)}) collective-permute-start(f32[32,256]{1,0:T(8,128)S(1)} %get-tuple-element.127), channel_id=1, source_target_pairs={{8,4},{12,0},{9,5},{13,1},{10,6},{14,2},{11,7},{15,3},{16,12},{20,... | collective-permute-start | bytes 98312 | tf_op jit(solution)/shard_map/ppermute | solution.py:596
  53.6 0.3 lower.13
  53.9 1.9 %collective-permute-start.22 = (f32[2,32,256]{2,1,0:T(8,128)S(1)}, f32[2,32,256]{2,1,0:T(8,128)S(1)}, u32[]{:S(2)}, u32[]{:S(2)}) collective-permute-start(f32[2,32,256]{2,1,0:T(8,128)S(1)} %pad_maximum_fusion), channel_id=1, source_target_pairs={{1,4},{5,0},{2,5},{6,1},{3,6},{7,2},{9,12},{13,8},{10,13},{14,9},{... | collective-permute-start | bytes 196616 | tf_op jit(solution)/shard_map/ppermute | solution.py:598
  55.9 1.0 %finish.1 = (f32[2,2,16,16,128]{4,3,2,1,0:T(8,128)S(1)}, f32[2,2,16,16,128]{4,3,2,1,0:T(8,128)S(1)}) custom-call(s32[1]{0:T(128)} %bitcast.1.core_ref, f32[256,256]{1,0:T(8,128)S(1)} %get-tuple-element.117.total0_ref, f32[256,256]{1,0:T(8,128)S(1)} %get-tuple-element.118.term0_ref, f32[256,256]{1,0:T(8,128)S(1)} %get-tuple-element.123.total1_ref, ...), custom_call_target="tpu_custom_call" | custom-call | tf_op jit(solution)/shard_map/finish/pallas_call | solution.py:601
  56.9 0.5 collective-permute-start.20
  57.4 4.4 %collective-permute-done.22.edge_y_ref = f32[2,32,256]{2,1,0:T(8,128)S(1)} collective-permute-done((f32[2,32,256]{2,1,0:T(8,128)S(1)}, f32[2,32,256]{2,1,0:T(8,128)S(1)}, u32[]{:S(2)}, u32[]{:S(2)}) %collective-permute-start.22) | collective-permute-done | bytes 65568 | tf_op jit(solution)/shard_map/ppermute | solution.py:598
  61.7 0.5 collective-permute-start.23
  62.2 0.2 keep.1.keep_rest_ref
  62.4 0.9 %place_wave.1 = f32[2,2,16,16,128]{4,3,2,1,0:T(8,128)} custom-call(s32[1]{0:T(128)} %bitcast.rhs_ref, f32[2,2,16,16,128]{4,3,2,1,0:T(8,128)S(1)} %get-tuple-element.125.keep_ref, f32[2,2,16,16,128]{4,3,2,1,0:T(8,128)S(1)} %collective-permute-done.20.got_ref), custom_call_target="tpu_custom_call" | custom-call | flops 10000000000 | bytes 1000000 | tf_op jit(solution)/shard_map/place_wave/pallas_call | solution.py:623
  63.3 1.0 %place_rest.1 = f32[2,2,16,16,128]{4,3,2,1,0:T(8,128)} custom-call(s32[1]{0:T(128)} %bitcast.1.core_ref, s32[1]{0:T(128)} %bitcast.rhs_ref, f32[2,16,16,128]{3,2,1,0:T(8,128)S(1)} %keep.1.keep_rest_ref, f32[2,2,16,16,128]{4,3,2,1,0:T(8,128)S(1)} %collective-permute-done.20.got_ref, f32[64,256]{1,0:T(8,128)S(1)} %collective-permute-done.23.got_edge_ref, ...), custom_call_target="tpu_custom_call" | custom-call | tf_op jit(solution)/shard_map/place_rest/pallas_call | solution.py:633
  (54 shorter events, 0.3 us)
Async XLA Ops:
  0.6 2.2 %copy-start = (f32[2,16,2]{1,2,0:T(2,128)S(1)}, f32[2,16,2]{1,2,0:T(2,128)}, u32[]{:S(2)}) copy-start(f32[2,16,2]{1,2,0:T(2,128)} %param.11) | copy-start | bytes 772
  0.7 2.2 %copy-start.4 = (f32[256,128]{1,0:T(8,128)S(1)}, f32[256,128]{1,0:T(8,128)}, u32[]{:S(2)}) copy-start(f32[256,128]{1,0:T(8,128)} %constant.154.clone.refs_0_) | copy-start | bytes 393220
  0.7 2.0 %copy-start.6 = (s32[2,16]{1,0:T(2,128)S(1)}, s32[2,16]{1,0:T(2,128)}, u32[]{:S(2)}) copy-start(s32[2,16]{1,0:T(2,128)} %param.10) | copy-start | bytes 388
  0.7 1.9 %copy-start.2 = (f32[16,16,128]{2,1,0:T(8,128)S(1)}, f32[16,16,128]{2,1,0:T(8,128)}, u32[]{:S(2)}) copy-start(f32[16,16,128]{2,1,0:T(8,128)} %slow_ref.1) | copy-start | bytes 393220
  0.7 2.1 %copy-start.1 = (bf16[4,128,384]{2,1,0:T(8,128)(2,1)S(1)}, bf16[4,128,384]{2,1,0:T(8,128)(2,1)}, u32[]{:S(2)}) copy-start(bf16[4,128,384]{2,1,0:T(8,128)(2,1)} %constant.156.clone.refs_1_.z_ref) | copy-start | bytes 1179652
  0.7 2.1 %copy-start.3 = (bf16[5,128,384]{2,1,0:T(8,128)(2,1)S(1)}, bf16[5,128,384]{2,1,0:T(8,128)(2,1)}, u32[]{:S(2)}) copy-start(bf16[5,128,384]{2,1,0:T(8,128)(2,1)} %constant.157.clone.refs_2_) | copy-start | bytes 1474564
  1.9 2.4 %collective-permute-start = (f32[2,16,16,128]{3,2,1,0:T(8,128)S(1)}, f32[2,16,16,128]{3,2,1,0:T(8,128)S(1)}, u32[]{:S(2)}, u32[]{:S(2)}) collective-permute-start(f32[2,16,16,128]{3,2,1,0:T(8,128)S(1)} %get-tuple-element.135), channel_id=1, source_target_pairs={{0,4},{4,0},{1,5},{5,1},{2,6},{6,2},{3,7},{7,3},{8,12},{12,8},{9,1... | collective-permute-start | bytes 786440 | tf_op jit(solution)/shard_map/ppermute | solution.py:504
  2.7 1.6 %collective-permute-start.1 = (f32[16,16,128]{2,1,0:T(8,128)S(1)}, f32[16,16,128]{2,1,0:T(8,128)S(1)}, u32[]{:S(2)}, u32[]{:S(2)}) collective-permute-start(f32[16,16,128]{2,1,0:T(8,128)S(1)} %copy-done.2), channel_id=1, source_target_pairs={{0,4},{4,0},{1,5},{5,1},{2,6},{6,2},{3,7},{7,3},{8,12},{12,8},{9,1... | collective-permute-start | bytes 393224 | tf_op jit(solution)/shard_map/ppermute | solution.py:505
  5.2 2.2 %collective-permute-start.3 = (f32[32,256]{1,0:T(8,128)S(1)}, f32[32,256]{1,0:T(8,128)S(1)}, u32[]{:S(2)}, u32[]{:S(2)}) collective-permute-start(f32[32,256]{1,0:T(8,128)S(1)} %get-tuple-element.74), channel_id=1, source_target_pairs={{0,5},{4,1}} | collective-permute-start | bytes 98312 | tf_op jit(solution)/shard_map/ppermute | solution.py:585
  6.0 1.4 %collective-permute-start.2 = (f32[32,256]{1,0:T(8,128)S(1)}, f32[32,256]{1,0:T(8,128)S(1)}, u32[]{:S(2)}, u32[]{:S(2)}) collective-permute-start(f32[32,256]{1,0:T(8,128)S(1)} %get-tuple-element.73), channel_id=1, source_target_pairs={{0,12},{4,8}} | collective-permute-start | bytes 98312 | tf_op jit(solution)/shard_map/ppermute | solution.py:588
  6.7 1.5 %collective-permute-start.4 = (f32[32,256]{1,0:T(8,128)S(1)}, f32[32,256]{1,0:T(8,128)S(1)}, u32[]{:S(2)}, u32[]{:S(2)}) collective-permute-start(f32[32,256]{1,0:T(8,128)S(1)} %get-tuple-element.78), channel_id=1, source_target_pairs={{0,5},{4,1}} | collective-permute-start | bytes 98312 | tf_op jit(solution)/shard_map/ppermute | solution.py:590
  7.5 2.1 %collective-permute-start.6 = (f32[32,256]{1,0:T(8,128)S(1)}, f32[32,256]{1,0:T(8,128)S(1)}, u32[]{:S(2)}, u32[]{:S(2)}) collective-permute-start(f32[32,256]{1,0:T(8,128)S(1)} %get-tuple-element.82), channel_id=1, source_target_pairs={{1,6},{5,2},{8,13},{12,9}} | collective-permute-start | bytes 98312 | tf_op jit(solution)/shard_map/ppermute | solution.py:585
  8.2 1.4 %collective-permute-start.5 = (f32[32,256]{1,0:T(8,128)S(1)}, f32[32,256]{1,0:T(8,128)S(1)}, u32[]{:S(2)}, u32[]{:S(2)}) collective-permute-start(f32[32,256]{1,0:T(8,128)S(1)} %get-tuple-element.81), channel_id=1, source_target_pairs={{1,13},{5,9},{8,20},{12,16}} | collective-permute-start | bytes 98312 | tf_op jit(solution)/shard_map/ppermute | solution.py:588
  8.9 1.5 %collective-permute-start.7 = (f32[32,256]{1,0:T(8,128)S(1)}, f32[32,256]{1,0:T(8,128)S(1)}, u32[]{:S(2)}, u32[]{:S(2)}) collective-permute-start(f32[32,256]{1,0:T(8,128)S(1)} %get-tuple-element.86), channel_id=1, source_target_pairs={{1,6},{5,2},{8,13},{12,9}} | collective-permute-start | bytes 98312 | tf_op jit(solution)/shard_map/ppermute | solution.py:590
  9.7 2.1 %collective-permute-start.9 = (f32[32,256]{1,0:T(8,128)S(1)}, f32[32,256]{1,0:T(8,128)S(1)}, u32[]{:S(2)}, u32[]{:S(2)}) collective-permute-start(f32[32,256]{1,0:T(8,128)S(1)} %get-tuple-element.90), channel_id=1, source_target_pairs={{2,7},{6,3},{9,14},{13,10},{16,21},{20,17}} | collective-permute-start | bytes 98312 | tf_op jit(solution)/shard_map/ppermute | solution.py:585
  10.5 1.4 %collective-permute-start.8 = (f32[32,256]{1,0:T(8,128)S(1)}, f32[32,256]{1,0:T(8,128)S(1)}, u32[]{:S(2)}, u32[]{:S(2)}) collective-permute-start(f32[32,256]{1,0:T(8,128)S(1)} %get-tuple-element.89), channel_id=1, source_target_pairs={{2,14},{6,10},{9,21},{13,17},{16,28},{20,24}} | collective-permute-start | bytes 98312 | tf_op jit(solution)/shard_map/ppermute | solution.py:588
  11.1 1.5 %collective-permute-start.10 = (f32[32,256]{1,0:T(8,128)S(1)}, f32[32,256]{1,0:T(8,128)S(1)}, u32[]{:S(2)}, u32[]{:S(2)}) collective-permute-start(f32[32,256]{1,0:T(8,128)S(1)} %get-tuple-element.94), channel_id=1, source_target_pairs={{2,7},{6,3},{9,14},{13,10},{16,21},{20,17}} | collective-permute-start | bytes 98312 | tf_op jit(solution)/shard_map/ppermute | solution.py:590
  11.9 2.3 %collective-permute-start.12 = (f32[32,256]{1,0:T(8,128)S(1)}, f32[32,256]{1,0:T(8,128)S(1)}, u32[]{:S(2)}, u32[]{:S(2)}) collective-permute-start(f32[32,256]{1,0:T(8,128)S(1)} %get-tuple-element.98), channel_id=1, source_target_pairs={{10,15},{14,11},{17,22},{21,18},{24,29},{28,25}} | collective-permute-start | bytes 98312 | tf_op jit(solution)/shard_map/ppermute | solution.py:585
  12.9 1.4 %collective-permute-start.11 = (f32[32,256]{1,0:T(8,128)S(1)}, f32[32,256]{1,0:T(8,128)S(1)}, u32[]{:S(2)}, u32[]{:S(2)}) collective-permute-start(f32[32,256]{1,0:T(8,128)S(1)} %get-tuple-element.97), channel_id=1, source_target_pairs={{3,15},{7,11},{10,22},{14,18},{17,29},{21,25}} | collective-permute-start | bytes 98312 | tf_op jit(solution)/shard_map/ppermute | solution.py:588
  13.5 2.1 %collective-permute-start.13 = (f32[32,256]{1,0:T(8,128)S(1)}, f32[32,256]{1,0:T(8,128)S(1)}, u32[]{:S(2)}, u32[]{:S(2)}) collective-permute-start(f32[32,256]{1,0:T(8,128)S(1)} %get-tuple-element.102), channel_id=1, source_target_pairs={{10,15},{14,11},{17,22},{21,18},{24,29},{28,25}} | collective-permute-start | bytes 98312 | tf_op jit(solution)/shard_map/ppermute | solution.py:590
  14.3 29.2 %collective-permute-start.15 = (f32[32,256]{1,0:T(8,128)S(1)}, f32[32,256]{1,0:T(8,128)S(1)}, u32[]{:S(2)}, u32[]{:S(2)}) collective-permute-start(f32[32,256]{1,0:T(8,128)S(1)} %get-tuple-element.106), channel_id=1, source_target_pairs={{18,23},{22,19},{25,30},{29,26}} | collective-permute-start | bytes 98312 | tf_op jit(solution)/shard_map/ppermute | solution.py:585
  15.7 29.1 %collective-permute-start.14 = (f32[32,256]{1,0:T(8,128)S(1)}, f32[32,256]{1,0:T(8,128)S(1)}, u32[]{:S(2)}, u32[]{:S(2)}) collective-permute-start(f32[32,256]{1,0:T(8,128)S(1)} %get-tuple-element.105), channel_id=1, source_target_pairs={{11,23},{15,19},{18,30},{22,26}} | collective-permute-start | bytes 98312 | tf_op jit(solution)/shard_map/ppermute | solution.py:588
  17.0 31.0 %collective-permute-start.16 = (f32[32,256]{1,0:T(8,128)S(1)}, f32[32,256]{1,0:T(8,128)S(1)}, u32[]{:S(2)}, u32[]{:S(2)}) collective-permute-start(f32[32,256]{1,0:T(8,128)S(1)} %get-tuple-element.110), channel_id=1, source_target_pairs={{18,23},{22,19},{25,30},{29,26}} | collective-permute-start | bytes 98312 | tf_op jit(solution)/shard_map/ppermute | solution.py:590
  46.7 5.3 %collective-permute-start.18 = (f32[32,256]{1,0:T(8,128)S(1)}, f32[32,256]{1,0:T(8,128)S(1)}, u32[]{:S(2)}, u32[]{:S(2)}) collective-permute-start(f32[32,256]{1,0:T(8,128)S(1)} %get-tuple-element.114), channel_id=1, source_target_pairs={{26,31},{30,27}} | collective-permute-start | bytes 98312 | tf_op jit(solution)/shard_map/ppermute | solution.py:585
  48.1 4.0 %copy-start.5 = (bf16[64,768]{1,0:T(8,128)(2,1)S(1)}, bf16[64,768]{1,0:T(8,128)(2,1)}, u32[]{:S(2)}) copy-start(bf16[64,768]{1,0:T(8,128)(2,1)} %constant.155.clone.refs_3_) | copy-start | bytes 294916
  50.0 2.0 %collective-permute-start.17 = (f32[32,256]{1,0:T(8,128)S(1)}, f32[32,256]{1,0:T(8,128)S(1)}, u32[]{:S(2)}, u32[]{:S(2)}) collective-permute-start(f32[32,256]{1,0:T(8,128)S(1)} %get-tuple-element.113), channel_id=1, source_target_pairs={{19,31},{23,27}} | collective-permute-start | bytes 98312 | tf_op jit(solution)/shard_map/ppermute | solution.py:588
  50.7 2.9 %collective-permute-start.19 = (f32[32,256]{1,0:T(8,128)S(1)}, f32[32,256]{1,0:T(8,128)S(1)}, u32[]{:S(2)}, u32[]{:S(2)}) collective-permute-start(f32[32,256]{1,0:T(8,128)S(1)} %get-tuple-element.120), channel_id=1, source_target_pairs={{26,31},{30,27}} | collective-permute-start | bytes 98312 | tf_op jit(solution)/shard_map/ppermute | solution.py:590
  52.3 5.0 %collective-permute-start.21 = (f32[32,256]{1,0:T(8,128)S(1)}, f32[32,256]{1,0:T(8,128)S(1)}, u32[]{:S(2)}, u32[]{:S(2)}) collective-permute-start(f32[32,256]{1,0:T(8,128)S(1)} %get-tuple-element.127), channel_id=1, source_target_pairs={{8,4},{12,0},{9,5},{13,1},{10,6},{14,2},{11,7},{15,3},{16,12},{20,... | collective-permute-start | bytes 98312 | tf_op jit(solution)/shard_map/ppermute | solution.py:596
  53.9 7.8 %collective-permute-start.22 = (f32[2,32,256]{2,1,0:T(8,128)S(1)}, f32[2,32,256]{2,1,0:T(8,128)S(1)}, u32[]{:S(2)}, u32[]{:S(2)}) collective-permute-start(f32[2,32,256]{2,1,0:T(8,128)S(1)} %pad_maximum_fusion), channel_id=1, source_target_pairs={{1,4},{5,0},{2,5},{6,1},{3,6},{7,2},{9,12},{13,8},{10,13},{14,9},{... | collective-permute-start | bytes 196616 | tf_op jit(solution)/shard_map/ppermute | solution.py:598
  56.9 5.5 %collective-permute-start.20 = (f32[2,2,16,16,128]{4,3,2,1,0:T(8,128)S(1)}, f32[2,2,16,16,128]{4,3,2,1,0:T(8,128)S(1)}, u32[]{:S(2)}, u32[]{:S(2)}) collective-permute-start(f32[2,2,16,16,128]{4,3,2,1,0:T(8,128)S(1)} %get-tuple-element.126), channel_id=1, source_target_pairs={{0,4},{4,0},{1,5},{5,1},{2,6},{6,2},{3,7},{7,3},{8,12},{12,8},{9,1... | collective-permute-start | bytes 1572872 | tf_op jit(solution)/shard_map/ppermute | solution.py:610
  61.7 1.5 %collective-permute-start.23 = (f32[64,256]{1,0:T(8,128)S(1)}, f32[64,256]{1,0:T(8,128)S(1)}, u32[]{:S(2)}, u32[]{:S(2)}) collective-permute-start(f32[64,256]{1,0:T(8,128)S(1)} %pad_maximum_fusion.1), channel_id=1, source_target_pairs={{0,4},{4,0},{1,5},{5,1},{2,6},{6,2},{3,7},{7,3},{8,12},{12,8},{9,1... | collective-permute-start | bytes 196616 | tf_op jit(solution)/shard_map/ppermute | solution.py:613

commit v18 on v16

--- a/solution.py
+++ b/solution.py
@@ -301,13 +301,9 @@
 
 def prep_kernel(cells_x, right_ref, slow_ref, place_ref, depth_ref, amp_ref, *refs):
     later_refs = refs[len(PREP) : len(PREP) + len(LATER)]
-    modes_ref, contrast_ref, inverse_ref, *held_refs, sems = refs[len(PREP) + len(LATER) :]
-    copies = [
-        pltpu.make_async_copy(later_ref, held_ref, sems.at[n])
-        for n, (later_ref, held_ref) in enumerate(zip(later_refs, held_refs))
-    ]
-    for copy in copies:
-        copy.start()
+    modes_ref, contrast_ref, inverse_ref, *held_refs = refs[len(PREP) + len(LATER) :]
+    for later_ref, held_ref in zip(later_refs, held_refs):
+        held_ref[...] = later_ref[...]
     t = named(PREP, refs)
     symbol = t["symbol"][...]
     damping = KAPPA * DAMPING
@@ -321,8 +317,6 @@
         jnp.concatenate(dense, axis=1), slow, len(cells_x), place_ref[...], depth_ref[...], amp_ref, t,
         modes_ref, contrast_ref,
     )
-    for copy in copies:
-        copy.wait()
 
 
 def prep_other_kernel(cells_x, core_ref, rhs_ref, swap_ref, slow_ref, own_modes_ref, own_contrast_ref, place_ref, depth_ref, amp_ref,
@@ -416,28 +410,22 @@
     add_later(rest_ref, edges[:count], edges[count:], (core_ref[0] == 1).astype(F32))
 
 
-def place_wave_kernel(rhs_ref, keep_ref, got_ref, wave_ref, sems):
+def place_kernel(core_ref, rhs_ref, keep_ref, keep_rest_ref, got_ref, got_edge_ref, z_ref,
+                 wave_ref, rest_ref, work_ref, sems):
     rhs = rhs_ref[0]
+    count = got_edge_ref.shape[0] // 2
     copies = [
         pltpu.make_async_copy(keep_ref.at[0], wave_ref.at[rhs], sems.at[0]),
         pltpu.make_async_copy(got_ref.at[0], wave_ref.at[1 - rhs], sems.at[1]),
+        pltpu.make_async_copy(keep_rest_ref, rest_ref.at[rhs], sems.at[2]),
     ]
     for copy in copies:
         copy.start()
-    for copy in copies:
-        copy.wait()
-
-
-def place_rest_kernel(core_ref, rhs_ref, keep_rest_ref, got_ref, got_edge_ref, z_ref, rest_ref, work_ref, sems):
-    rhs = rhs_ref[0]
-    count = got_edge_ref.shape[0] // 2
-    copies = [pltpu.make_async_copy(keep_rest_ref, rest_ref.at[rhs], sems.at[0])]
-    copies[0].start()
     work_ref[...] = got_ref[1]
     edges = z_transform(got_edge_ref[...], dict(onward=z_ref))
     add_later(work_ref, edges[:count], edges[count:], (core_ref[0] == 1).astype(F32))
-    copies.append(pltpu.make_async_copy(work_ref, rest_ref.at[1 - rhs], sems.at[1]))
-    copies[1].start()
+    copies.append(pltpu.make_async_copy(work_ref, rest_ref.at[1 - rhs], sems.at[3]))
+    copies[-1].start()
     for copy in copies:
         copy.wait()
 
@@ -513,9 +501,8 @@
         functools.partial(prep_kernel, cells_x),
         out_shape=(shaped(rows, 2 * cells_z), shaped(2, rows, cells_z), shaped(2, rows, cells_z))
         + tuple(jax.ShapeDtypeStruct(t[name].shape, BF16) for name in LATER),
-        in_specs=[whole()] * (5 + len(PREP)) + [anywhere()] * len(LATER),
+        in_specs=[whole()] * (5 + len(PREP) + len(LATER)),
         out_specs=(whole(),) * (3 + len(LATER)),
-        scratch_shapes=[pltpu.SemaphoreType.DMA((len(LATER),))],
         compiler_params=PARAMS,
         cost_estimate=SOLVE_COST,
         name="prep",
@@ -609,29 +596,18 @@
         cost_estimate=KEEP_COST,
         name="keep",
     )(core_ref, keep, after_x, after_y, t["onward"])
-    wavefield = pl.pallas_call(
-        place_wave_kernel,
-        out_shape=shaped(*right_side.shape),
-        in_specs=[scalars()] + [whole()] * 2,
-        out_specs=anywhere(),
-        scratch_shapes=[pltpu.SemaphoreType.DMA((2,))],
-        compiler_params=PARAMS,
-        cost_estimate=KEEP_COST,
-        name="place_wave",
-    )(rhs_ref, keep, got)
-    residual = pl.pallas_call(
-        place_rest_kernel,
-        out_shape=shaped(*right_side.shape),
-        in_specs=[scalars()] * 2 + [whole()] * 4,
-        out_specs=anywhere(),
+    return pl.pallas_call(
+        place_kernel,
+        out_shape=(shaped(*right_side.shape), shaped(*right_side.shape)),
+        in_specs=[scalars()] * 2 + [whole()] * 5,
+        out_specs=(anywhere(), anywhere()),
         scratch_shapes=[
             pltpu.VMEM((2, size_x, size_y, cells_z), F32),
-            pltpu.SemaphoreType.DMA((2,)),
+            pltpu.SemaphoreType.DMA((4,)),
         ],
         compiler_params=PARAMS,
-        name="place_rest",
-    )(core_ref, rhs_ref, keep_rest, got, got_edge, t["onward"])
-    return wavefield, residual
+        name="place",
+    )(core_ref, rhs_ref, keep, keep_rest, got, got_edge, t["onward"])
 
 
 def solution(mesh):

time: 64.2 us -> 64.2 us (level)
  Pallas kernels: 10.1 us -> 9.08 us
  waiting for transfers between devices: 30.8 us -> 31.8 us
    pallas_call x2 -> x1, Pallas kernels: 1.72 us -> 1 us  [body(): pl.pallas_call(place_kernel, out_shape=(shaped(*right_side.shape), shaped...]
    ppermute x1, waiting for transfers between devices: 0.01 us -> 0.7 us  [body(): lax.ppermute(jnp.concatenate([after_x, pass_y], axis=0), axes, own)]
  transfers between devices with their start and end apart: 24 -> 24, of which waited for: 4 -> 5; matrix products, arithmetic and copies ran while one was open for 0% -> 0% of each run, Pallas kernels for 13% -> 11%
where the time goes in v18:
time: 64.2 us; the launch traced here: 63.8 us
  waiting for transfers between devices  31.8 us (50%)
  starting transfers between devices  20 us (31%)
  Pallas kernels  9.08 us (14%)
  between operations  1.51 us (2%)
  local copies, waits for them, and re-layouts  1.29 us (2%)
    ppermute x6, waiting for transfers between devices, body(): trace_y0 = hand_on(lax.ppermute(outs0[0], axes, along_y))  25 us
    pallas_call x14, Pallas kernels, solve(): pl.pallas_call(functools.partial(beat_kernel, tile, final), out_shape=(sh...  5.35 us
    ppermute x6, starting transfers between devices, body(): trace_y0 = hand_on(lax.ppermute(outs0[0], axes, along_y))  5.24 us
    ppermute x6, starting transfers between devices, body(): trace_y1 = lax.ppermute(outs1[1], axes, along_y)  5.24 us
    ppermute x6, starting transfers between devices, body(): trace_x = lax.ppermute(outs1[0], axes, along_x)  4.61 us
    ppermute x1, waiting for transfers between devices, body(): lax.ppermute(edge_y, axes, between([((k, j), (k, j - 1)) for k, j in ever...  4.37 us
    ppermute x1, starting transfers between devices, body(): lax.ppermute(edge_y, axes, between([((k, j), (k, j - 1)) for k, j in ever...  1.92 us
    ppermute x6, waiting for transfers between devices, body(): trace_x = lax.ppermute(outs1[0], axes, along_x)  1.32 us
  transfers between devices with their start and end apart: 24, of which 5 were waited for; matrix products, arithmetic and copies ran while one was open for 0% of the time, Pallas kernels for 11%

profile of v18, /device:TPU:29, one launch (start us, length us, event | category | flops | bytes accessed | tf_op | source)
XLA Modules:
  0.0 63.8 jit_solution(7859291417822688647)
XLA Ops:
  0.8 1.2 %dynamic-slice_bitcast_fusion = (f32[2,16,16,128]{3,2,1,0:T(8,128)S(1)}, f32[2,16,16,128]{3,2,1,0:T(8,128)S(1)}) fusion(f32[2,2,16,16,128]{4,3,2,1,0:T(8,128)} %param.8, s32[]{:T(128)S(6)} %select_n.77, s32[]{:T(128)S(6)} %select_n.76), kind=kLoop, calls=%fused_computation | loop fusion | bytes 1048584 | tf_op jit(solution)/shard_map/jit(dynamic_index_in_dim)/squeeze | solution.py:483
  1.9 0.7 %collective-permute-start = (f32[2,16,16,128]{3,2,1,0:T(8,128)S(1)}, f32[2,16,16,128]{3,2,1,0:T(8,128)S(1)}, u32[]{:S(2)}, u32[]{:S(2)}) collective-permute-start(f32[2,16,16,128]{3,2,1,0:T(8,128)S(1)} %get-tuple-element.135), channel_id=1, source_target_pairs={{0,4},{4,0},{1,5},{5,1},{2,6},{6,2},{3,7},{7,3},{8,12},{12,8},{9,1... | collective-permute-start | bytes 786440 | tf_op jit(solution)/shard_map/ppermute | solution.py:481
  2.7 0.1 collective-permute-start.1
  2.9 0.8 %prep.1 = (f32[256,256]{1,0:T(8,128)S(1)}, f32[2,256,128]{2,1,0:T(8,128)S(1)}, f32[2,256,128]{2,1,0:T(8,128)S(1)}, bf16[5,128,384]{2,1,0:T(8,128)(2,1)S(1)}) custom-call(f32[2,16,16,128]{3,2,1,0:T(8,128)S(1)} %get-tuple-element.134.right_ref, f32[16,16,128]{2,1,0:T(8,128)S(1)} %copy-done.2, s32[1,16]{1,0:T(1,128)S(1)} %and_select_fusion.2.place_ref, ...), custom_call_target="tpu_custom_call" | custom-call | flops 2000000000 | bytes 2000000 | tf_op jit(solution)/shard_map/prep/pallas_call | solution.py:500
  3.6 0.4 collective-permute-done.1.slow_ref
  4.0 0.7 %prep_other.1 = (f32[2,256,256]{2,1,0:T(8,128)S(1)}, f32[2,2,256,128]{3,2,1,0:T(8,128)S(1)}) custom-call(s32[1]{0:T(128)} %bitcast.core_ref, s32[1]{0:T(128)} %bitcast.1.rhs_ref, f32[2,16,16,128]{3,2,1,0:T(8,128)S(1)} %collective-permute-done.swap_ref, f32[16,16,128]{2,1,0:T(8,128)S(1)} %collective-permute-done.1.slow_ref, ...), custom_call_target="tpu_custom_call" | custom-call | flops 2000000000 | bytes 2000000 | tf_op jit(solution)/shard_map/prep_other/pallas_call | solution.py:511
  4.8 0.1 upper.7
  4.9 0.7 %collective-permute-start.3 = (f32[32,256]{1,0:T(8,128)S(1)}, f32[32,256]{1,0:T(8,128)S(1)}, u32[]{:S(2)}, u32[]{:S(2)}) collective-permute-start(f32[32,256]{1,0:T(8,128)S(1)} %get-tuple-element.74), channel_id=1, source_target_pairs={{0,5},{4,1}} | collective-permute-start | bytes 98312 | tf_op jit(solution)/shard_map/ppermute | solution.py:561
  5.6 0.1 lower.7
  5.7 0.7 %collective-permute-start.2 = (f32[32,256]{1,0:T(8,128)S(1)}, f32[32,256]{1,0:T(8,128)S(1)}, u32[]{:S(2)}, u32[]{:S(2)}) collective-permute-start(f32[32,256]{1,0:T(8,128)S(1)} %get-tuple-element.73), channel_id=1, source_target_pairs={{0,12},{4,8}} | collective-permute-start | bytes 98312 | tf_op jit(solution)/shard_map/ppermute | solution.py:564
  6.4 0.7 %collective-permute-start.4 = (f32[32,256]{1,0:T(8,128)S(1)}, f32[32,256]{1,0:T(8,128)S(1)}, u32[]{:S(2)}, u32[]{:S(2)}) collective-permute-start(f32[32,256]{1,0:T(8,128)S(1)} %get-tuple-element.78), channel_id=1, source_target_pairs={{0,5},{4,1}} | collective-permute-start | bytes 98312 | tf_op jit(solution)/shard_map/ppermute | solution.py:566
  7.1 0.1 upper.8
  7.2 0.7 %collective-permute-start.6 = (f32[32,256]{1,0:T(8,128)S(1)}, f32[32,256]{1,0:T(8,128)S(1)}, u32[]{:S(2)}, u32[]{:S(2)}) collective-permute-start(f32[32,256]{1,0:T(8,128)S(1)} %get-tuple-element.82), channel_id=1, source_target_pairs={{1,6},{5,2},{8,13},{12,9}} | collective-permute-start | bytes 98312 | tf_op jit(solution)/shard_map/ppermute | solution.py:561
  7.8 0.1 lower.8
  7.9 0.7 %collective-permute-start.5 = (f32[32,256]{1,0:T(8,128)S(1)}, f32[32,256]{1,0:T(8,128)S(1)}, u32[]{:S(2)}, u32[]{:S(2)}) collective-permute-start(f32[32,256]{1,0:T(8,128)S(1)} %get-tuple-element.81), channel_id=1, source_target_pairs={{1,13},{5,9},{8,20},{12,16}} | collective-permute-start | bytes 98312 | tf_op jit(solution)/shard_map/ppermute | solution.py:564
  8.6 0.7 %collective-permute-start.7 = (f32[32,256]{1,0:T(8,128)S(1)}, f32[32,256]{1,0:T(8,128)S(1)}, u32[]{:S(2)}, u32[]{:S(2)}) collective-permute-start(f32[32,256]{1,0:T(8,128)S(1)} %get-tuple-element.86), channel_id=1, source_target_pairs={{1,6},{5,2},{8,13},{12,9}} | collective-permute-start | bytes 98312 | tf_op jit(solution)/shard_map/ppermute | solution.py:566
  9.3 0.1 upper.9
  9.4 0.7 %collective-permute-start.9 = (f32[32,256]{1,0:T(8,128)S(1)}, f32[32,256]{1,0:T(8,128)S(1)}, u32[]{:S(2)}, u32[]{:S(2)}) collective-permute-start(f32[32,256]{1,0:T(8,128)S(1)} %get-tuple-element.90), channel_id=1, source_target_pairs={{2,7},{6,3},{9,14},{13,10},{16,21},{20,17}} | collective-permute-start | bytes 98312 | tf_op jit(solution)/shard_map/ppermute | solution.py:561
  10.1 0.1 lower.9
  10.1 0.7 %collective-permute-start.8 = (f32[32,256]{1,0:T(8,128)S(1)}, f32[32,256]{1,0:T(8,128)S(1)}, u32[]{:S(2)}, u32[]{:S(2)}) collective-permute-start(f32[32,256]{1,0:T(8,128)S(1)} %get-tuple-element.89), channel_id=1, source_target_pairs={{2,14},{6,10},{9,21},{13,17},{16,28},{20,24}} | collective-permute-start | bytes 98312 | tf_op jit(solution)/shard_map/ppermute | solution.py:564
  10.8 0.7 %collective-permute-start.10 = (f32[32,256]{1,0:T(8,128)S(1)}, f32[32,256]{1,0:T(8,128)S(1)}, u32[]{:S(2)}, u32[]{:S(2)}) collective-permute-start(f32[32,256]{1,0:T(8,128)S(1)} %get-tuple-element.94), channel_id=1, source_target_pairs={{2,7},{6,3},{9,14},{13,10},{16,21},{20,17}} | collective-permute-start | bytes 98312 | tf_op jit(solution)/shard_map/ppermute | solution.py:566
  11.5 0.1 upper.10
  11.6 0.7 %collective-permute-start.12 = (f32[32,256]{1,0:T(8,128)S(1)}, f32[32,256]{1,0:T(8,128)S(1)}, u32[]{:S(2)}, u32[]{:S(2)}) collective-permute-start(f32[32,256]{1,0:T(8,128)S(1)} %get-tuple-element.98), channel_id=1, source_target_pairs={{10,15},{14,11},{17,22},{21,18},{24,29},{28,25}} | collective-permute-start | bytes 98312 | tf_op jit(solution)/shard_map/ppermute | solution.py:561
  12.3 0.3 lower.10
  12.6 0.7 %collective-permute-start.11 = (f32[32,256]{1,0:T(8,128)S(1)}, f32[32,256]{1,0:T(8,128)S(1)}, u32[]{:S(2)}, u32[]{:S(2)}) collective-permute-start(f32[32,256]{1,0:T(8,128)S(1)} %get-tuple-element.97), channel_id=1, source_target_pairs={{3,15},{7,11},{10,22},{14,18},{17,29},{21,25}} | collective-permute-start | bytes 98312 | tf_op jit(solution)/shard_map/ppermute | solution.py:564
  13.2 0.7 %collective-permute-start.13 = (f32[32,256]{1,0:T(8,128)S(1)}, f32[32,256]{1,0:T(8,128)S(1)}, u32[]{:S(2)}, u32[]{:S(2)}) collective-permute-start(f32[32,256]{1,0:T(8,128)S(1)} %get-tuple-element.102), channel_id=1, source_target_pairs={{10,15},{14,11},{17,22},{21,18},{24,29},{28,25}} | collective-permute-start | bytes 98312 | tf_op jit(solution)/shard_map/ppermute | solution.py:566
  14.0 1.3 %collective-permute-start.15 = (f32[32,256]{1,0:T(8,128)S(1)}, f32[32,256]{1,0:T(8,128)S(1)}, u32[]{:S(2)}, u32[]{:S(2)}) collective-permute-start(f32[32,256]{1,0:T(8,128)S(1)} %get-tuple-element.106), channel_id=1, source_target_pairs={{18,23},{22,19},{25,30},{29,26}} | collective-permute-start | bytes 98312 | tf_op jit(solution)/shard_map/ppermute | solution.py:561
  15.3 0.1 lower.11
  15.4 1.3 %collective-permute-start.14 = (f32[32,256]{1,0:T(8,128)S(1)}, f32[32,256]{1,0:T(8,128)S(1)}, u32[]{:S(2)}, u32[]{:S(2)}) collective-permute-start(f32[32,256]{1,0:T(8,128)S(1)} %get-tuple-element.105), channel_id=1, source_target_pairs={{11,23},{15,19},{18,30},{22,26}} | collective-permute-start | bytes 98312 | tf_op jit(solution)/shard_map/ppermute | solution.py:564
  16.7 1.3 %collective-permute-start.16 = (f32[32,256]{1,0:T(8,128)S(1)}, f32[32,256]{1,0:T(8,128)S(1)}, u32[]{:S(2)}, u32[]{:S(2)}) collective-permute-start(f32[32,256]{1,0:T(8,128)S(1)} %get-tuple-element.110), channel_id=1, source_target_pairs={{18,23},{22,19},{25,30},{29,26}} | collective-permute-start | bytes 98312 | tf_op jit(solution)/shard_map/ppermute | solution.py:566
  18.0 25.0 %collective-permute-done.15.in_ref = f32[32,256]{1,0:T(8,128)S(1)} collective-permute-done((f32[32,256]{1,0:T(8,128)S(1)}, f32[32,256]{1,0:T(8,128)S(1)}, u32[]{:S(2)}, u32[]{:S(2)}) %collective-permute-start.15) | collective-permute-done | bytes 32800 | tf_op jit(solution)/shard_map/ppermute | solution.py:561
  43.0 1.3 %collective-permute-done.14.trace_x_ref = f32[32,256]{1,0:T(8,128)S(1)} collective-permute-done((f32[32,256]{1,0:T(8,128)S(1)}, f32[32,256]{1,0:T(8,128)S(1)}, u32[]{:S(2)}, u32[]{:S(2)}) %collective-permute-start.14) | collective-permute-done | bytes 32800 | tf_op jit(solution)/shard_map/ppermute | solution.py:564
  44.4 1.9 %upper.12 = (f32[256,256]{1,0:T(8,128)S(1)}, f32[256,256]{1,0:T(8,128)S(1)}, f32[32,256]{1,0:T(8,128)S(1)}, f32[32,256]{1,0:T(8,128)S(1)}) custom-call(s32[1]{0:T(128)} %bitcast.9.active_ref, f32[2,256,256]{2,1,0:T(8,128)S(1)} %get-tuple-element.69.modes_ref, ...), custom_call_target="tpu_custom_call", output_to_operand_aliasing={{0}: (5, {}), {1}: (6, {})} | custom-call | flops 2000000000 | bytes 2000000 | tf_op jit(solution)/shard_map/upper/pallas_call | solution.py:526
  46.3 1.3 %collective-permute-start.18 = (f32[32,256]{1,0:T(8,128)S(1)}, f32[32,256]{1,0:T(8,128)S(1)}, u32[]{:S(2)}, u32[]{:S(2)}) collective-permute-start(f32[32,256]{1,0:T(8,128)S(1)} %get-tuple-element.114), channel_id=1, source_target_pairs={{26,31},{30,27}} | collective-permute-start | bytes 98312 | tf_op jit(solution)/shard_map/ppermute | solution.py:561
  47.6 1.9 %lower.12 = (f32[256,256]{1,0:T(8,128)S(1)}, f32[256,256]{1,0:T(8,128)S(1)}, f32[32,256]{1,0:T(8,128)S(1)}, f32[32,256]{1,0:T(8,128)S(1)}) custom-call(s32[1]{0:T(128)} %bitcast.9.active_ref, f32[2,256,256]{2,1,0:T(8,128)S(1)} %get-tuple-element.69.modes_ref, ...), custom_call_target="tpu_custom_call", output_to_operand_aliasing={{0}: (5, {}), {1}: (6, {})} | custom-call | flops 2000000000 | bytes 2000000 | tf_op jit(solution)/shard_map/lower/pallas_call | solution.py:526
  49.6 0.7 %collective-permute-start.17 = (f32[32,256]{1,0:T(8,128)S(1)}, f32[32,256]{1,0:T(8,128)S(1)}, u32[]{:S(2)}, u32[]{:S(2)}) collective-permute-start(f32[32,256]{1,0:T(8,128)S(1)} %get-tuple-element.113), channel_id=1, source_target_pairs={{19,31},{23,27}} | collective-permute-start | bytes 98312 | tf_op jit(solution)/shard_map/ppermute | solution.py:564
  50.3 1.3 %collective-permute-start.19 = (f32[32,256]{1,0:T(8,128)S(1)}, f32[32,256]{1,0:T(8,128)S(1)}, u32[]{:S(2)}, u32[]{:S(2)}) collective-permute-start(f32[32,256]{1,0:T(8,128)S(1)} %get-tuple-element.120), channel_id=1, source_target_pairs={{26,31},{30,27}} | collective-permute-start | bytes 98312 | tf_op jit(solution)/shard_map/ppermute | solution.py:566
  51.6 0.3 upper.13
  51.9 1.3 %collective-permute-start.20 = (f32[32,256]{1,0:T(8,128)S(1)}, f32[32,256]{1,0:T(8,128)S(1)}, u32[]{:S(2)}, u32[]{:S(2)}) collective-permute-start(f32[32,256]{1,0:T(8,128)S(1)} %get-tuple-element.126), channel_id=1, source_target_pairs={{8,4},{12,0},{9,5},{13,1},{10,6},{14,2},{11,7},{15,3},{16,12},{20,... | collective-permute-start | bytes 98312 | tf_op jit(solution)/shard_map/ppermute | solution.py:572
  53.2 0.3 lower.13
  53.5 1.9 %collective-permute-start.21 = (f32[2,32,256]{2,1,0:T(8,128)S(1)}, f32[2,32,256]{2,1,0:T(8,128)S(1)}, u32[]{:S(2)}, u32[]{:S(2)}) collective-permute-start(f32[2,32,256]{2,1,0:T(8,128)S(1)} %pad_maximum_fusion), channel_id=1, source_target_pairs={{1,4},{5,0},{2,5},{6,1},{3,6},{7,2},{9,12},{13,8},{10,13},{14,9},{... | collective-permute-start | bytes 196616 | tf_op jit(solution)/shard_map/ppermute | solution.py:574
  55.4 1.0 %finish.1 = (f32[2,2,16,16,128]{4,3,2,1,0:T(8,128)S(1)}, f32[2,2,16,16,128]{4,3,2,1,0:T(8,128)S(1)}) custom-call(s32[1]{0:T(128)} %bitcast.core_ref, f32[256,256]{1,0:T(8,128)S(1)} %get-tuple-element.117.total0_ref, f32[256,256]{1,0:T(8,128)S(1)} %get-tuple-element.118.term0_ref, f32[256,256]{1,0:T(8,128)S(1)} %get-tuple-element.123.total1_ref, ...), custom_call_target="tpu_custom_call" | custom-call | tf_op jit(solution)/shard_map/finish/pallas_call | solution.py:577
  56.4 0.4 collective-permute-start.22
  56.9 4.4 %collective-permute-done.21.edge_y_ref = f32[2,32,256]{2,1,0:T(8,128)S(1)} collective-permute-done((f32[2,32,256]{2,1,0:T(8,128)S(1)}, f32[2,32,256]{2,1,0:T(8,128)S(1)}, u32[]{:S(2)}, u32[]{:S(2)}) %collective-permute-start.21) | collective-permute-done | bytes 65568 | tf_op jit(solution)/shard_map/ppermute | solution.py:574
  61.3 0.4 collective-permute-start.23
  61.7 0.2 keep.1.keep_rest_ref
  61.9 0.7 %collective-permute-done.23.got_edge_ref = f32[64,256]{1,0:T(8,128)S(1)} collective-permute-done((f32[64,256]{1,0:T(8,128)S(1)}, f32[64,256]{1,0:T(8,128)S(1)}, u32[]{:S(2)}, u32[]{:S(2)}) %collective-permute-start.23) | collective-permute-done | bytes 65568 | tf_op jit(solution)/shard_map/ppermute | solution.py:589
  62.6 1.0 %place.1 = (f32[2,2,16,16,128]{4,3,2,1,0:T(8,128)}, f32[2,2,16,16,128]{4,3,2,1,0:T(8,128)}) custom-call(s32[1]{0:T(128)} %bitcast.core_ref, s32[1]{0:T(128)} %bitcast.1.rhs_ref, f32[2,2,16,16,128]{4,3,2,1,0:T(8,128)S(1)} %get-tuple-element.125.keep_ref, f32[2,16,16,128]{3,2,1,0:T(8,128)S(1)} %keep.1.keep_rest_ref, ...), custom_call_target="tpu_custom_call" | custom-call | tf_op jit(solution)/shard_map/place/pallas_call | solution.py:599
  (53 shorter events, 0.4 us)
Async XLA Ops:
  0.6 2.2 %copy-start = (f32[2,16,2]{1,2,0:T(2,128)S(1)}, f32[2,16,2]{1,2,0:T(2,128)}, u32[]{:S(2)}) copy-start(f32[2,16,2]{1,2,0:T(2,128)} %param.11) | copy-start | bytes 772
  0.7 2.2 %copy-start.4 = (f32[256,128]{1,0:T(8,128)S(1)}, f32[256,128]{1,0:T(8,128)}, u32[]{:S(2)}) copy-start(f32[256,128]{1,0:T(8,128)} %constant.154.clone.refs_0_) | copy-start | bytes 393220
  0.7 2.0 %copy-start.6 = (s32[2,16]{1,0:T(2,128)S(1)}, s32[2,16]{1,0:T(2,128)}, u32[]{:S(2)}) copy-start(s32[2,16]{1,0:T(2,128)} %param.10) | copy-start | bytes 388
  0.7 1.9 %copy-start.2 = (f32[16,16,128]{2,1,0:T(8,128)S(1)}, f32[16,16,128]{2,1,0:T(8,128)}, u32[]{:S(2)}) copy-start(f32[16,16,128]{2,1,0:T(8,128)} %slow_ref.1) | copy-start | bytes 393220
  0.7 2.1 %copy-start.1 = (bf16[4,128,384]{2,1,0:T(8,128)(2,1)S(1)}, bf16[4,128,384]{2,1,0:T(8,128)(2,1)}, u32[]{:S(2)}) copy-start(bf16[4,128,384]{2,1,0:T(8,128)(2,1)} %constant.156.clone.refs_1_.z_ref) | copy-start | bytes 1179652
  0.7 2.1 %copy-start.3 = (bf16[5,128,384]{2,1,0:T(8,128)(2,1)S(1)}, bf16[5,128,384]{2,1,0:T(8,128)(2,1)}, u32[]{:S(2)}) copy-start(bf16[5,128,384]{2,1,0:T(8,128)(2,1)} %constant.157.clone.refs_2_) | copy-start | bytes 1474564
  1.9 2.1 %collective-permute-start = (f32[2,16,16,128]{3,2,1,0:T(8,128)S(1)}, f32[2,16,16,128]{3,2,1,0:T(8,128)S(1)}, u32[]{:S(2)}, u32[]{:S(2)}) collective-permute-start(f32[2,16,16,128]{3,2,1,0:T(8,128)S(1)} %get-tuple-element.135), channel_id=1, source_target_pairs={{0,4},{4,0},{1,5},{5,1},{2,6},{6,2},{3,7},{7,3},{8,12},{12,8},{9,1... | collective-permute-start | bytes 786440 | tf_op jit(solution)/shard_map/ppermute | solution.py:481
  2.7 1.3 %collective-permute-start.1 = (f32[16,16,128]{2,1,0:T(8,128)S(1)}, f32[16,16,128]{2,1,0:T(8,128)S(1)}, u32[]{:S(2)}, u32[]{:S(2)}) collective-permute-start(f32[16,16,128]{2,1,0:T(8,128)S(1)} %copy-done.2), channel_id=1, source_target_pairs={{0,4},{4,0},{1,5},{5,1},{2,6},{6,2},{3,7},{7,3},{8,12},{12,8},{9,1... | collective-permute-start | bytes 393224 | tf_op jit(solution)/shard_map/ppermute | solution.py:482
  4.9 2.2 %collective-permute-start.3 = (f32[32,256]{1,0:T(8,128)S(1)}, f32[32,256]{1,0:T(8,128)S(1)}, u32[]{:S(2)}, u32[]{:S(2)}) collective-permute-start(f32[32,256]{1,0:T(8,128)S(1)} %get-tuple-element.74), channel_id=1, source_target_pairs={{0,5},{4,1}} | collective-permute-start | bytes 98312 | tf_op jit(solution)/shard_map/ppermute | solution.py:561
  5.7 1.4 %collective-permute-start.2 = (f32[32,256]{1,0:T(8,128)S(1)}, f32[32,256]{1,0:T(8,128)S(1)}, u32[]{:S(2)}, u32[]{:S(2)}) collective-permute-start(f32[32,256]{1,0:T(8,128)S(1)} %get-tuple-element.73), channel_id=1, source_target_pairs={{0,12},{4,8}} | collective-permute-start | bytes 98312 | tf_op jit(solution)/shard_map/ppermute | solution.py:564
  6.4 1.5 %collective-permute-start.4 = (f32[32,256]{1,0:T(8,128)S(1)}, f32[32,256]{1,0:T(8,128)S(1)}, u32[]{:S(2)}, u32[]{:S(2)}) collective-permute-start(f32[32,256]{1,0:T(8,128)S(1)} %get-tuple-element.78), channel_id=1, source_target_pairs={{0,5},{4,1}} | collective-permute-start | bytes 98312 | tf_op jit(solution)/shard_map/ppermute | solution.py:566
  7.2 2.1 %collective-permute-start.6 = (f32[32,256]{1,0:T(8,128)S(1)}, f32[32,256]{1,0:T(8,128)S(1)}, u32[]{:S(2)}, u32[]{:S(2)}) collective-permute-start(f32[32,256]{1,0:T(8,128)S(1)} %get-tuple-element.82), channel_id=1, source_target_pairs={{1,6},{5,2},{8,13},{12,9}} | collective-permute-start | bytes 98312 | tf_op jit(solution)/shard_map/ppermute | solution.py:561
  7.9 1.4 %collective-permute-start.5 = (f32[32,256]{1,0:T(8,128)S(1)}, f32[32,256]{1,0:T(8,128)S(1)}, u32[]{:S(2)}, u32[]{:S(2)}) collective-permute-start(f32[32,256]{1,0:T(8,128)S(1)} %get-tuple-element.81), channel_id=1, source_target_pairs={{1,13},{5,9},{8,20},{12,16}} | collective-permute-start | bytes 98312 | tf_op jit(solution)/shard_map/ppermute | solution.py:564
  8.6 1.5 %collective-permute-start.7 = (f32[32,256]{1,0:T(8,128)S(1)}, f32[32,256]{1,0:T(8,128)S(1)}, u32[]{:S(2)}, u32[]{:S(2)}) collective-permute-start(f32[32,256]{1,0:T(8,128)S(1)} %get-tuple-element.86), channel_id=1, source_target_pairs={{1,6},{5,2},{8,13},{12,9}} | collective-permute-start | bytes 98312 | tf_op jit(solution)/shard_map/ppermute | solution.py:566
  9.4 2.1 %collective-permute-start.9 = (f32[32,256]{1,0:T(8,128)S(1)}, f32[32,256]{1,0:T(8,128)S(1)}, u32[]{:S(2)}, u32[]{:S(2)}) collective-permute-start(f32[32,256]{1,0:T(8,128)S(1)} %get-tuple-element.90), channel_id=1, source_target_pairs={{2,7},{6,3},{9,14},{13,10},{16,21},{20,17}} | collective-permute-start | bytes 98312 | tf_op jit(solution)/shard_map/ppermute | solution.py:561
  10.1 1.4 %collective-permute-start.8 = (f32[32,256]{1,0:T(8,128)S(1)}, f32[32,256]{1,0:T(8,128)S(1)}, u32[]{:S(2)}, u32[]{:S(2)}) collective-permute-start(f32[32,256]{1,0:T(8,128)S(1)} %get-tuple-element.89), channel_id=1, source_target_pairs={{2,14},{6,10},{9,21},{13,17},{16,28},{20,24}} | collective-permute-start | bytes 98312 | tf_op jit(solution)/shard_map/ppermute | solution.py:564
  10.8 1.5 %collective-permute-start.10 = (f32[32,256]{1,0:T(8,128)S(1)}, f32[32,256]{1,0:T(8,128)S(1)}, u32[]{:S(2)}, u32[]{:S(2)}) collective-permute-start(f32[32,256]{1,0:T(8,128)S(1)} %get-tuple-element.94), channel_id=1, source_target_pairs={{2,7},{6,3},{9,14},{13,10},{16,21},{20,17}} | collective-permute-start | bytes 98312 | tf_op jit(solution)/shard_map/ppermute | solution.py:566
  11.6 2.3 %collective-permute-start.12 = (f32[32,256]{1,0:T(8,128)S(1)}, f32[32,256]{1,0:T(8,128)S(1)}, u32[]{:S(2)}, u32[]{:S(2)}) collective-permute-start(f32[32,256]{1,0:T(8,128)S(1)} %get-tuple-element.98), channel_id=1, source_target_pairs={{10,15},{14,11},{17,22},{21,18},{24,29},{28,25}} | collective-permute-start | bytes 98312 | tf_op jit(solution)/shard_map/ppermute | solution.py:561
  12.6 1.4 %collective-permute-start.11 = (f32[32,256]{1,0:T(8,128)S(1)}, f32[32,256]{1,0:T(8,128)S(1)}, u32[]{:S(2)}, u32[]{:S(2)}) collective-permute-start(f32[32,256]{1,0:T(8,128)S(1)} %get-tuple-element.97), channel_id=1, source_target_pairs={{3,15},{7,11},{10,22},{14,18},{17,29},{21,25}} | collective-permute-start | bytes 98312 | tf_op jit(solution)/shard_map/ppermute | solution.py:564
  13.2 2.1 %collective-permute-start.13 = (f32[32,256]{1,0:T(8,128)S(1)}, f32[32,256]{1,0:T(8,128)S(1)}, u32[]{:S(2)}, u32[]{:S(2)}) collective-permute-start(f32[32,256]{1,0:T(8,128)S(1)} %get-tuple-element.102), channel_id=1, source_target_pairs={{10,15},{14,11},{17,22},{21,18},{24,29},{28,25}} | collective-permute-start | bytes 98312 | tf_op jit(solution)/shard_map/ppermute | solution.py:566
  14.0 29.0 %collective-permute-start.15 = (f32[32,256]{1,0:T(8,128)S(1)}, f32[32,256]{1,0:T(8,128)S(1)}, u32[]{:S(2)}, u32[]{:S(2)}) collective-permute-start(f32[32,256]{1,0:T(8,128)S(1)} %get-tuple-element.106), channel_id=1, source_target_pairs={{18,23},{22,19},{25,30},{29,26}} | collective-permute-start | bytes 98312 | tf_op jit(solution)/shard_map/ppermute | solution.py:561
  15.4 28.9 %collective-permute-start.14 = (f32[32,256]{1,0:T(8,128)S(1)}, f32[32,256]{1,0:T(8,128)S(1)}, u32[]{:S(2)}, u32[]{:S(2)}) collective-permute-start(f32[32,256]{1,0:T(8,128)S(1)} %get-tuple-element.105), channel_id=1, source_target_pairs={{11,23},{15,19},{18,30},{22,26}} | collective-permute-start | bytes 98312 | tf_op jit(solution)/shard_map/ppermute | solution.py:564
  16.7 30.9 %collective-permute-start.16 = (f32[32,256]{1,0:T(8,128)S(1)}, f32[32,256]{1,0:T(8,128)S(1)}, u32[]{:S(2)}, u32[]{:S(2)}) collective-permute-start(f32[32,256]{1,0:T(8,128)S(1)} %get-tuple-element.110), channel_id=1, source_target_pairs={{18,23},{22,19},{25,30},{29,26}} | collective-permute-start | bytes 98312 | tf_op jit(solution)/shard_map/ppermute | solution.py:566
  46.3 5.3 %collective-permute-start.18 = (f32[32,256]{1,0:T(8,128)S(1)}, f32[32,256]{1,0:T(8,128)S(1)}, u32[]{:S(2)}, u32[]{:S(2)}) collective-permute-start(f32[32,256]{1,0:T(8,128)S(1)} %get-tuple-element.114), channel_id=1, source_target_pairs={{26,31},{30,27}} | collective-permute-start | bytes 98312 | tf_op jit(solution)/shard_map/ppermute | solution.py:561
  47.6 4.0 %copy-start.5 = (bf16[64,768]{1,0:T(8,128)(2,1)S(1)}, bf16[64,768]{1,0:T(8,128)(2,1)}, u32[]{:S(2)}) copy-start(bf16[64,768]{1,0:T(8,128)(2,1)} %constant.155.clone.refs_3_) | copy-start | bytes 294916
  49.6 2.0 %collective-permute-start.17 = (f32[32,256]{1,0:T(8,128)S(1)}, f32[32,256]{1,0:T(8,128)S(1)}, u32[]{:S(2)}, u32[]{:S(2)}) collective-permute-start(f32[32,256]{1,0:T(8,128)S(1)} %get-tuple-element.113), channel_id=1, source_target_pairs={{19,31},{23,27}} | collective-permute-start | bytes 98312 | tf_op jit(solution)/shard_map/ppermute | solution.py:564
  50.3 2.9 %collective-permute-start.19 = (f32[32,256]{1,0:T(8,128)S(1)}, f32[32,256]{1,0:T(8,128)S(1)}, u32[]{:S(2)}, u32[]{:S(2)}) collective-permute-start(f32[32,256]{1,0:T(8,128)S(1)} %get-tuple-element.120), channel_id=1, source_target_pairs={{26,31},{30,27}} | collective-permute-start | bytes 98312 | tf_op jit(solution)/shard_map/ppermute | solution.py:566
  51.9 5.0 %collective-permute-start.20 = (f32[32,256]{1,0:T(8,128)S(1)}, f32[32,256]{1,0:T(8,128)S(1)}, u32[]{:S(2)}, u32[]{:S(2)}) collective-permute-start(f32[32,256]{1,0:T(8,128)S(1)} %get-tuple-element.126), channel_id=1, source_target_pairs={{8,4},{12,0},{9,5},{13,1},{10,6},{14,2},{11,7},{15,3},{16,12},{20,... | collective-permute-start | bytes 98312 | tf_op jit(solution)/shard_map/ppermute | solution.py:572
  53.5 7.8 %collective-permute-start.21 = (f32[2,32,256]{2,1,0:T(8,128)S(1)}, f32[2,32,256]{2,1,0:T(8,128)S(1)}, u32[]{:S(2)}, u32[]{:S(2)}) collective-permute-start(f32[2,32,256]{2,1,0:T(8,128)S(1)} %pad_maximum_fusion), channel_id=1, source_target_pairs={{1,4},{5,0},{2,5},{6,1},{3,6},{7,2},{9,12},{13,8},{10,13},{14,9},{... | collective-permute-start | bytes 196616 | tf_op jit(solution)/shard_map/ppermute | solution.py:574
  56.4 6.2 %collective-permute-start.22 = (f32[2,2,16,16,128]{4,3,2,1,0:T(8,128)S(1)}, f32[2,2,16,16,128]{4,3,2,1,0:T(8,128)S(1)}, u32[]{:S(2)}, u32[]{:S(2)}) collective-permute-start(f32[2,2,16,16,128]{4,3,2,1,0:T(8,128)S(1)} %get-tuple-element.129), channel_id=1, source_target_pairs={{0,4},{4,0},{1,5},{5,1},{2,6},{6,2},{3,7},{7,3},{8,12},{12,8},{9,1... | collective-permute-start | bytes 1572872 | tf_op jit(solution)/shard_map/ppermute | solution.py:586
  61.3 1.3 %collective-permute-start.23 = (f32[64,256]{1,0:T(8,128)S(1)}, f32[64,256]{1,0:T(8,128)S(1)}, u32[]{:S(2)}, u32[]{:S(2)}) collective-permute-start(f32[64,256]{1,0:T(8,128)S(1)} %pad_maximum_fusion.1), channel_id=1, source_target_pairs={{0,4},{4,0},{1,5},{5,1},{2,6},{6,2},{3,7},{7,3},{8,12},{12,8},{9,1... | collective-permute-start | bytes 196616 | tf_op jit(solution)/shard_map/ppermute | solution.py:589

commit v19 on v16

--- a/solution.py
+++ b/solution.py
@@ -234,7 +234,7 @@
     )
 
 
-def apply_contrast(field, contrast, t, block=64):
+def apply_contrast(field, contrast, t, block=32):
     done = []
     for start in range(0, field.shape[0], block):
         here = slice(start, start + block)

time: 64.2 us -> 67.2 us (1.047)
  waiting for transfers between devices: 30.8 us -> 33 us
  Pallas kernels: 10.1 us -> 10.9 us
    ppermute x6, waiting for transfers between devices: 25.1 us -> 26.9 us  [body(): trace_y0 = hand_on(lax.ppermute(outs0[0], axes, along_y))]
    pallas_call x14, Pallas kernels: 5.35 us -> 6.14 us  [solve(): pl.pallas_call(functools.partial(beat_kernel, tile, final), out_shape=(sh...]
  transfers between devices with their start and end apart: 24 -> 24, of which waited for: 4 -> 4; matrix products, arithmetic and copies ran while one was open for 0% -> 0% of each run, Pallas kernels for 13% -> 14%
where the time goes in v19:
time: 67.2 us; the launch traced here: 66.8 us
  waiting for transfers between devices  33 us (49%)
  starting transfers between devices  20 us (30%)
  Pallas kernels  10.9 us (16%)
  between operations  1.56 us (2%)
  local copies, waits for them, and re-layouts  1.29 us (2%)
    ppermute x6, waiting for transfers between devices, body(): trace_y0 = hand_on(lax.ppermute(outs0[0], axes, along_y))  26.9 us
    pallas_call x14, Pallas kernels, solve(): pl.pallas_call(functools.partial(beat_kernel, tile, final), out_shape=(sh...  6.14 us
    ppermute x6, starting transfers between devices, body(): trace_y0 = hand_on(lax.ppermute(outs0[0], axes, along_y))  5.24 us
    ppermute x6, starting transfers between devices, body(): trace_y1 = lax.ppermute(outs1[1], axes, along_y)  5.24 us
    ppermute x1, waiting for transfers between devices, body(): lax.ppermute(edge_y, axes, between([((k, j), (k, j - 1)) for k, j in ever...  4.71 us
    ppermute x6, starting transfers between devices, body(): trace_x = lax.ppermute(outs1[0], axes, along_x)  4.61 us
    ppermute x1, starting transfers between devices, body(): lax.ppermute(edge_y, axes, between([((k, j), (k, j - 1)) for k, j in ever...  1.92 us
  transfers between devices with their start and end apart: 24, of which 4 were waited for; matrix products, arithmetic and copies ran while one was open for 0% of the time, Pallas kernels for 14%

profile of v19, /device:TPU:29, one launch (start us, length us, event | category | flops | bytes accessed | tf_op | source)
XLA Modules:
  0.0 66.8 jit_solution(15395223091180457747)
XLA Ops:
  0.8 1.2 %dynamic-slice_bitcast_fusion = (f32[2,16,16,128]{3,2,1,0:T(8,128)S(1)}, f32[2,16,16,128]{3,2,1,0:T(8,128)S(1)}) fusion(f32[2,2,16,16,128]{4,3,2,1,0:T(8,128)} %param.8, s32[]{:T(128)S(6)} %select_n.77, s32[]{:T(128)S(6)} %select_n.76), kind=kLoop, calls=%fused_computation | loop fusion | bytes 1048584 | tf_op jit(solution)/shard_map/jit(dynamic_index_in_dim)/squeeze | solution.py:495
  1.9 0.7 %collective-permute-start = (f32[2,16,16,128]{3,2,1,0:T(8,128)S(1)}, f32[2,16,16,128]{3,2,1,0:T(8,128)S(1)}, u32[]{:S(2)}, u32[]{:S(2)}) collective-permute-start(f32[2,16,16,128]{3,2,1,0:T(8,128)S(1)} %get-tuple-element.135), channel_id=1, source_target_pairs={{0,4},{4,0},{1,5},{5,1},{2,6},{6,2},{3,7},{7,3},{8,12},{12,8},{9,1... | collective-permute-start | bytes 786440 | tf_op jit(solution)/shard_map/ppermute | solution.py:493
  2.7 0.1 collective-permute-start.1
  2.9 1.1 %prep.1 = (f32[256,256]{1,0:T(8,128)S(1)}, f32[2,256,128]{2,1,0:T(8,128)S(1)}, f32[2,256,128]{2,1,0:T(8,128)S(1)}, bf16[5,128,384]{2,1,0:T(8,128)(2,1)S(1)}) custom-call(f32[2,16,16,128]{3,2,1,0:T(8,128)S(1)} %get-tuple-element.134.right_ref, f32[16,16,128]{2,1,0:T(8,128)S(1)} %copy-done.2, s32[1,16]{1,0:T(1,128)S(1)} %and_select_fusion.2.place_ref, ...), custom_call_target="tpu_custom_call" | custom-call | flops 2000000000 | bytes 2000000 | tf_op jit(solution)/shard_map/prep/pallas_call | solution.py:512
  4.0 0.7 %prep_other.1 = (f32[2,256,256]{2,1,0:T(8,128)S(1)}, f32[2,2,256,128]{3,2,1,0:T(8,128)S(1)}) custom-call(s32[1]{0:T(128)} %bitcast.1.core_ref, s32[1]{0:T(128)} %bitcast.rhs_ref, f32[2,16,16,128]{3,2,1,0:T(8,128)S(1)} %collective-permute-done.swap_ref, f32[16,16,128]{2,1,0:T(8,128)S(1)} %collective-permute-done.1.slow_ref, ...), custom_call_target="tpu_custom_call" | custom-call | flops 2000000000 | bytes 2000000 | tf_op jit(solution)/shard_map/prep_other/pallas_call | solution.py:524
  4.8 0.1 upper.7
  4.9 0.7 collective-permute-start.3
  5.6 0.1 lower.7
  5.7 0.7 collective-permute-start.2
  6.4 0.7 collective-permute-start.4
  7.1 0.1 upper.8
  7.2 0.7 collective-permute-start.6
  7.8 0.1 lower.8
  7.9 0.7 collective-permute-start.5
  8.6 0.7 collective-permute-start.7
  9.3 0.1 upper.9
  9.4 0.7 collective-permute-start.9
  10.1 0.1 lower.9
  10.1 0.7 collective-permute-start.8
  10.8 0.7 collective-permute-start.10
  11.5 0.3 upper.10
  11.8 0.7 collective-permute-start.12
  12.5 0.1 lower.10
  12.6 0.7 collective-permute-start.11
  13.2 0.7 collective-permute-start.13
  13.9 0.1 upper.11
  14.0 1.3 %collective-permute-start.15 = (f32[32,256]{1,0:T(8,128)S(1)}, f32[32,256]{1,0:T(8,128)S(1)}, u32[]{:S(2)}, u32[]{:S(2)}) collective-permute-start(f32[32,256]{1,0:T(8,128)S(1)} %get-tuple-element.106), channel_id=1, source_target_pairs={{18,23},{22,19},{25,30},{29,26}} | collective-permute-start | bytes 98312 | tf_op jit(solution)/shard_map/ppermute | solution.py:574
  15.3 0.1 lower.11
  15.4 1.3 %collective-permute-start.14 = (f32[32,256]{1,0:T(8,128)S(1)}, f32[32,256]{1,0:T(8,128)S(1)}, u32[]{:S(2)}, u32[]{:S(2)}) collective-permute-start(f32[32,256]{1,0:T(8,128)S(1)} %get-tuple-element.105), channel_id=1, source_target_pairs={{11,23},{15,19},{18,30},{22,26}} | collective-permute-start | bytes 98312 | tf_op jit(solution)/shard_map/ppermute | solution.py:577
  16.7 1.3 %collective-permute-start.16 = (f32[32,256]{1,0:T(8,128)S(1)}, f32[32,256]{1,0:T(8,128)S(1)}, u32[]{:S(2)}, u32[]{:S(2)}) collective-permute-start(f32[32,256]{1,0:T(8,128)S(1)} %get-tuple-element.110), channel_id=1, source_target_pairs={{18,23},{22,19},{25,30},{29,26}} | collective-permute-start | bytes 98312 | tf_op jit(solution)/shard_map/ppermute | solution.py:579
  18.0 26.9 %collective-permute-done.15.in_ref = f32[32,256]{1,0:T(8,128)S(1)} collective-permute-done((f32[32,256]{1,0:T(8,128)S(1)}, f32[32,256]{1,0:T(8,128)S(1)}, u32[]{:S(2)}, u32[]{:S(2)}) %collective-permute-start.15) | collective-permute-done | bytes 32800 | tf_op jit(solution)/shard_map/ppermute | solution.py:574
  44.9 1.3 %collective-permute-done.14.trace_x_ref = f32[32,256]{1,0:T(8,128)S(1)} collective-permute-done((f32[32,256]{1,0:T(8,128)S(1)}, f32[32,256]{1,0:T(8,128)S(1)}, u32[]{:S(2)}, u32[]{:S(2)}) %collective-permute-start.14) | collective-permute-done | bytes 32800 | tf_op jit(solution)/shard_map/ppermute | solution.py:577
  46.2 2.2 %upper.12 = (f32[256,256]{1,0:T(8,128)S(1)}, f32[256,256]{1,0:T(8,128)S(1)}, f32[32,256]{1,0:T(8,128)S(1)}, f32[32,256]{1,0:T(8,128)S(1)}) custom-call(s32[1]{0:T(128)} %bitcast.9.active_ref, f32[2,256,256]{2,1,0:T(8,128)S(1)} %get-tuple-element.69.modes_ref, ...), custom_call_target="tpu_custom_call", output_to_operand_aliasing={{0}: (5, {}), {1}: (6, {})} | custom-call | flops 2000000000 | bytes 2000000 | tf_op jit(solution)/shard_map/upper/pallas_call | solution.py:539
  48.4 1.3 %collective-permute-start.18 = (f32[32,256]{1,0:T(8,128)S(1)}, f32[32,256]{1,0:T(8,128)S(1)}, u32[]{:S(2)}, u32[]{:S(2)}) collective-permute-start(f32[32,256]{1,0:T(8,128)S(1)} %get-tuple-element.114), channel_id=1, source_target_pairs={{26,31},{30,27}} | collective-permute-start | bytes 98312 | tf_op jit(solution)/shard_map/ppermute | solution.py:574
  49.8 2.2 %lower.12 = (f32[256,256]{1,0:T(8,128)S(1)}, f32[256,256]{1,0:T(8,128)S(1)}, f32[32,256]{1,0:T(8,128)S(1)}, f32[32,256]{1,0:T(8,128)S(1)}) custom-call(s32[1]{0:T(128)} %bitcast.9.active_ref, f32[2,256,256]{2,1,0:T(8,128)S(1)} %get-tuple-element.69.modes_ref, ...), custom_call_target="tpu_custom_call", output_to_operand_aliasing={{0}: (5, {}), {1}: (6, {})} | custom-call | flops 2000000000 | bytes 2000000 | tf_op jit(solution)/shard_map/lower/pallas_call | solution.py:539
  52.0 0.7 collective-permute-start.17
  52.7 1.3 %collective-permute-start.19 = (f32[32,256]{1,0:T(8,128)S(1)}, f32[32,256]{1,0:T(8,128)S(1)}, u32[]{:S(2)}, u32[]{:S(2)}) collective-permute-start(f32[32,256]{1,0:T(8,128)S(1)} %get-tuple-element.120), channel_id=1, source_target_pairs={{26,31},{30,27}} | collective-permute-start | bytes 98312 | tf_op jit(solution)/shard_map/ppermute | solution.py:579
  54.0 0.3 upper.13
  54.3 1.3 %collective-permute-start.21 = (f32[32,256]{1,0:T(8,128)S(1)}, f32[32,256]{1,0:T(8,128)S(1)}, u32[]{:S(2)}, u32[]{:S(2)}) collective-permute-start(f32[32,256]{1,0:T(8,128)S(1)} %get-tuple-element.127), channel_id=1, source_target_pairs={{8,4},{12,0},{9,5},{13,1},{10,6},{14,2},{11,7},{15,3},{16,12},{20,... | collective-permute-start | bytes 98312 | tf_op jit(solution)/shard_map/ppermute | solution.py:585
  55.6 0.5 lower.13
  56.1 1.9 %collective-permute-start.22 = (f32[2,32,256]{2,1,0:T(8,128)S(1)}, f32[2,32,256]{2,1,0:T(8,128)S(1)}, u32[]{:S(2)}, u32[]{:S(2)}) collective-permute-start(f32[2,32,256]{2,1,0:T(8,128)S(1)} %pad_maximum_fusion), channel_id=1, source_target_pairs={{1,4},{5,0},{2,5},{6,1},{3,6},{7,2},{9,12},{13,8},{10,13},{14,9},{... | collective-permute-start | bytes 196616 | tf_op jit(solution)/shard_map/ppermute | solution.py:587
  58.1 1.0 %finish.1 = (f32[2,2,16,16,128]{4,3,2,1,0:T(8,128)S(1)}, f32[2,2,16,16,128]{4,3,2,1,0:T(8,128)S(1)}) custom-call(s32[1]{0:T(128)} %bitcast.1.core_ref, f32[256,256]{1,0:T(8,128)S(1)} %get-tuple-element.117.total0_ref, f32[256,256]{1,0:T(8,128)S(1)} %get-tuple-element.118.term0_ref, f32[256,256]{1,0:T(8,128)S(1)} %get-tuple-element.123.total1_ref, ...), custom_call_target="tpu_custom_call" | custom-call | tf_op jit(solution)/shard_map/finish/pallas_call | solution.py:590
  59.1 0.4 collective-permute-start.20
  59.5 4.7 %collective-permute-done.22.edge_y_ref = f32[2,32,256]{2,1,0:T(8,128)S(1)} collective-permute-done((f32[2,32,256]{2,1,0:T(8,128)S(1)}, f32[2,32,256]{2,1,0:T(8,128)S(1)}, u32[]{:S(2)}, u32[]{:S(2)}) %collective-permute-start.22) | collective-permute-done | bytes 65568 | tf_op jit(solution)/shard_map/ppermute | solution.py:587
  64.3 0.4 collective-permute-start.23
  64.7 0.2 keep.1.keep_rest_ref
  64.9 0.8 %place_wave.1 = f32[2,2,16,16,128]{4,3,2,1,0:T(8,128)} custom-call(s32[1]{0:T(128)} %bitcast.rhs_ref, f32[2,2,16,16,128]{4,3,2,1,0:T(8,128)S(1)} %get-tuple-element.125.keep_ref, f32[2,2,16,16,128]{4,3,2,1,0:T(8,128)S(1)} %collective-permute-done.20.got_ref), custom_call_target="tpu_custom_call" | custom-call | flops 10000000000 | bytes 1000000 | tf_op jit(solution)/shard_map/place_wave/pallas_call | solution.py:612
  65.7 0.9 %place_rest.1 = f32[2,2,16,16,128]{4,3,2,1,0:T(8,128)} custom-call(s32[1]{0:T(128)} %bitcast.1.core_ref, s32[1]{0:T(128)} %bitcast.rhs_ref, f32[2,16,16,128]{3,2,1,0:T(8,128)S(1)} %keep.1.keep_rest_ref, f32[2,2,16,16,128]{4,3,2,1,0:T(8,128)S(1)} %collective-permute-done.20.got_ref, f32[64,256]{1,0:T(8,128)S(1)} %collective-permute-done.23.got_edge_ref, ...), custom_call_target="tpu_custom_call" | custom-call | tf_op jit(solution)/shard_map/place_rest/pallas_call | solution.py:622
  (54 shorter events, 0.3 us)
Async XLA Ops:
  0.6 2.2 %copy-start = (f32[2,16,2]{1,2,0:T(2,128)S(1)}, f32[2,16,2]{1,2,0:T(2,128)}, u32[]{:S(2)}) copy-start(f32[2,16,2]{1,2,0:T(2,128)} %param.11) | copy-start | bytes 772
  0.7 2.2 %copy-start.4 = (f32[256,128]{1,0:T(8,128)S(1)}, f32[256,128]{1,0:T(8,128)}, u32[]{:S(2)}) copy-start(f32[256,128]{1,0:T(8,128)} %constant.154.clone.refs_0_) | copy-start | bytes 393220
  0.7 2.0 %copy-start.6 = (s32[2,16]{1,0:T(2,128)S(1)}, s32[2,16]{1,0:T(2,128)}, u32[]{:S(2)}) copy-start(s32[2,16]{1,0:T(2,128)} %param.10) | copy-start | bytes 388
  0.7 1.9 %copy-start.2 = (f32[16,16,128]{2,1,0:T(8,128)S(1)}, f32[16,16,128]{2,1,0:T(8,128)}, u32[]{:S(2)}) copy-start(f32[16,16,128]{2,1,0:T(8,128)} %slow_ref.1) | copy-start | bytes 393220
  0.7 2.1 %copy-start.1 = (bf16[4,128,384]{2,1,0:T(8,128)(2,1)S(1)}, bf16[4,128,384]{2,1,0:T(8,128)(2,1)}, u32[]{:S(2)}) copy-start(bf16[4,128,384]{2,1,0:T(8,128)(2,1)} %constant.156.clone.refs_1_.z_ref) | copy-start | bytes 1179652
  0.7 2.1 %copy-start.3 = (bf16[5,128,384]{2,1,0:T(8,128)(2,1)S(1)}, bf16[5,128,384]{2,1,0:T(8,128)(2,1)}, u32[]{:S(2)}) copy-start(bf16[5,128,384]{2,1,0:T(8,128)(2,1)} %constant.157.clone.refs_2_) | copy-start | bytes 1474564
  1.9 2.1 %collective-permute-start = (f32[2,16,16,128]{3,2,1,0:T(8,128)S(1)}, f32[2,16,16,128]{3,2,1,0:T(8,128)S(1)}, u32[]{:S(2)}, u32[]{:S(2)}) collective-permute-start(f32[2,16,16,128]{3,2,1,0:T(8,128)S(1)} %get-tuple-element.135), channel_id=1, source_target_pairs={{0,4},{4,0},{1,5},{5,1},{2,6},{6,2},{3,7},{7,3},{8,12},{12,8},{9,1... | collective-permute-start | bytes 786440 | tf_op jit(solution)/shard_map/ppermute | solution.py:493
  2.7 1.3 %collective-permute-start.1 = (f32[16,16,128]{2,1,0:T(8,128)S(1)}, f32[16,16,128]{2,1,0:T(8,128)S(1)}, u32[]{:S(2)}, u32[]{:S(2)}) collective-permute-start(f32[16,16,128]{2,1,0:T(8,128)S(1)} %copy-done.2), channel_id=1, source_target_pairs={{0,4},{4,0},{1,5},{5,1},{2,6},{6,2},{3,7},{7,3},{8,12},{12,8},{9,1... | collective-permute-start | bytes 393224 | tf_op jit(solution)/shard_map/ppermute | solution.py:494
  4.9 2.2 %collective-permute-start.3 = (f32[32,256]{1,0:T(8,128)S(1)}, f32[32,256]{1,0:T(8,128)S(1)}, u32[]{:S(2)}, u32[]{:S(2)}) collective-permute-start(f32[32,256]{1,0:T(8,128)S(1)} %get-tuple-element.74), channel_id=1, source_target_pairs={{0,5},{4,1}} | collective-permute-start | bytes 98312 | tf_op jit(solution)/shard_map/ppermute | solution.py:574
  5.7 1.4 %collective-permute-start.2 = (f32[32,256]{1,0:T(8,128)S(1)}, f32[32,256]{1,0:T(8,128)S(1)}, u32[]{:S(2)}, u32[]{:S(2)}) collective-permute-start(f32[32,256]{1,0:T(8,128)S(1)} %get-tuple-element.73), channel_id=1, source_target_pairs={{0,12},{4,8}} | collective-permute-start | bytes 98312 | tf_op jit(solution)/shard_map/ppermute | solution.py:577
  6.4 1.5 %collective-permute-start.4 = (f32[32,256]{1,0:T(8,128)S(1)}, f32[32,256]{1,0:T(8,128)S(1)}, u32[]{:S(2)}, u32[]{:S(2)}) collective-permute-start(f32[32,256]{1,0:T(8,128)S(1)} %get-tuple-element.78), channel_id=1, source_target_pairs={{0,5},{4,1}} | collective-permute-start | bytes 98312 | tf_op jit(solution)/shard_map/ppermute | solution.py:579
  7.2 2.1 %collective-permute-start.6 = (f32[32,256]{1,0:T(8,128)S(1)}, f32[32,256]{1,0:T(8,128)S(1)}, u32[]{:S(2)}, u32[]{:S(2)}) collective-permute-start(f32[32,256]{1,0:T(8,128)S(1)} %get-tuple-element.82), channel_id=1, source_target_pairs={{1,6},{5,2},{8,13},{12,9}} | collective-permute-start | bytes 98312 | tf_op jit(solution)/shard_map/ppermute | solution.py:574
  7.9 1.4 %collective-permute-start.5 = (f32[32,256]{1,0:T(8,128)S(1)}, f32[32,256]{1,0:T(8,128)S(1)}, u32[]{:S(2)}, u32[]{:S(2)}) collective-permute-start(f32[32,256]{1,0:T(8,128)S(1)} %get-tuple-element.81), channel_id=1, source_target_pairs={{1,13},{5,9},{8,20},{12,16}} | collective-permute-start | bytes 98312 | tf_op jit(solution)/shard_map/ppermute | solution.py:577
  8.6 1.5 %collective-permute-start.7 = (f32[32,256]{1,0:T(8,128)S(1)}, f32[32,256]{1,0:T(8,128)S(1)}, u32[]{:S(2)}, u32[]{:S(2)}) collective-permute-start(f32[32,256]{1,0:T(8,128)S(1)} %get-tuple-element.86), channel_id=1, source_target_pairs={{1,6},{5,2},{8,13},{12,9}} | collective-permute-start | bytes 98312 | tf_op jit(solution)/shard_map/ppermute | solution.py:579
  9.4 2.1 %collective-permute-start.9 = (f32[32,256]{1,0:T(8,128)S(1)}, f32[32,256]{1,0:T(8,128)S(1)}, u32[]{:S(2)}, u32[]{:S(2)}) collective-permute-start(f32[32,256]{1,0:T(8,128)S(1)} %get-tuple-element.90), channel_id=1, source_target_pairs={{2,7},{6,3},{9,14},{13,10},{16,21},{20,17}} | collective-permute-start | bytes 98312 | tf_op jit(solution)/shard_map/ppermute | solution.py:574
  10.1 1.4 %collective-permute-start.8 = (f32[32,256]{1,0:T(8,128)S(1)}, f32[32,256]{1,0:T(8,128)S(1)}, u32[]{:S(2)}, u32[]{:S(2)}) collective-permute-start(f32[32,256]{1,0:T(8,128)S(1)} %get-tuple-element.89), channel_id=1, source_target_pairs={{2,14},{6,10},{9,21},{13,17},{16,28},{20,24}} | collective-permute-start | bytes 98312 | tf_op jit(solution)/shard_map/ppermute | solution.py:577
  10.8 1.6 %collective-permute-start.10 = (f32[32,256]{1,0:T(8,128)S(1)}, f32[32,256]{1,0:T(8,128)S(1)}, u32[]{:S(2)}, u32[]{:S(2)}) collective-permute-start(f32[32,256]{1,0:T(8,128)S(1)} %get-tuple-element.94), channel_id=1, source_target_pairs={{2,7},{6,3},{9,14},{13,10},{16,21},{20,17}} | collective-permute-start | bytes 98312 | tf_op jit(solution)/shard_map/ppermute | solution.py:579
  11.8 2.1 %collective-permute-start.12 = (f32[32,256]{1,0:T(8,128)S(1)}, f32[32,256]{1,0:T(8,128)S(1)}, u32[]{:S(2)}, u32[]{:S(2)}) collective-permute-start(f32[32,256]{1,0:T(8,128)S(1)} %get-tuple-element.98), channel_id=1, source_target_pairs={{10,15},{14,11},{17,22},{21,18},{24,29},{28,25}} | collective-permute-start | bytes 98312 | tf_op jit(solution)/shard_map/ppermute | solution.py:574
  12.6 1.4 %collective-permute-start.11 = (f32[32,256]{1,0:T(8,128)S(1)}, f32[32,256]{1,0:T(8,128)S(1)}, u32[]{:S(2)}, u32[]{:S(2)}) collective-permute-start(f32[32,256]{1,0:T(8,128)S(1)} %get-tuple-element.97), channel_id=1, source_target_pairs={{3,15},{7,11},{10,22},{14,18},{17,29},{21,25}} | collective-permute-start | bytes 98312 | tf_op jit(solution)/shard_map/ppermute | solution.py:577
  13.2 2.1 %collective-permute-start.13 = (f32[32,256]{1,0:T(8,128)S(1)}, f32[32,256]{1,0:T(8,128)S(1)}, u32[]{:S(2)}, u32[]{:S(2)}) collective-permute-start(f32[32,256]{1,0:T(8,128)S(1)} %get-tuple-element.102), channel_id=1, source_target_pairs={{10,15},{14,11},{17,22},{21,18},{24,29},{28,25}} | collective-permute-start | bytes 98312 | tf_op jit(solution)/shard_map/ppermute | solution.py:579
  14.0 30.9 %collective-permute-start.15 = (f32[32,256]{1,0:T(8,128)S(1)}, f32[32,256]{1,0:T(8,128)S(1)}, u32[]{:S(2)}, u32[]{:S(2)}) collective-permute-start(f32[32,256]{1,0:T(8,128)S(1)} %get-tuple-element.106), channel_id=1, source_target_pairs={{18,23},{22,19},{25,30},{29,26}} | collective-permute-start | bytes 98312 | tf_op jit(solution)/shard_map/ppermute | solution.py:574
  15.4 30.8 %collective-permute-start.14 = (f32[32,256]{1,0:T(8,128)S(1)}, f32[32,256]{1,0:T(8,128)S(1)}, u32[]{:S(2)}, u32[]{:S(2)}) collective-permute-start(f32[32,256]{1,0:T(8,128)S(1)} %get-tuple-element.105), channel_id=1, source_target_pairs={{11,23},{15,19},{18,30},{22,26}} | collective-permute-start | bytes 98312 | tf_op jit(solution)/shard_map/ppermute | solution.py:577
  16.7 33.0 %collective-permute-start.16 = (f32[32,256]{1,0:T(8,128)S(1)}, f32[32,256]{1,0:T(8,128)S(1)}, u32[]{:S(2)}, u32[]{:S(2)}) collective-permute-start(f32[32,256]{1,0:T(8,128)S(1)} %get-tuple-element.110), channel_id=1, source_target_pairs={{18,23},{22,19},{25,30},{29,26}} | collective-permute-start | bytes 98312 | tf_op jit(solution)/shard_map/ppermute | solution.py:579
  48.4 5.5 %collective-permute-start.18 = (f32[32,256]{1,0:T(8,128)S(1)}, f32[32,256]{1,0:T(8,128)S(1)}, u32[]{:S(2)}, u32[]{:S(2)}) collective-permute-start(f32[32,256]{1,0:T(8,128)S(1)} %get-tuple-element.114), channel_id=1, source_target_pairs={{26,31},{30,27}} | collective-permute-start | bytes 98312 | tf_op jit(solution)/shard_map/ppermute | solution.py:574
  49.7 4.3 %copy-start.5 = (bf16[64,768]{1,0:T(8,128)(2,1)S(1)}, bf16[64,768]{1,0:T(8,128)(2,1)}, u32[]{:S(2)}) copy-start(bf16[64,768]{1,0:T(8,128)(2,1)} %constant.155.clone.refs_3_) | copy-start | bytes 294916
  52.0 2.0 %collective-permute-start.17 = (f32[32,256]{1,0:T(8,128)S(1)}, f32[32,256]{1,0:T(8,128)S(1)}, u32[]{:S(2)}, u32[]{:S(2)}) collective-permute-start(f32[32,256]{1,0:T(8,128)S(1)} %get-tuple-element.113), channel_id=1, source_target_pairs={{19,31},{23,27}} | collective-permute-start | bytes 98312 | tf_op jit(solution)/shard_map/ppermute | solution.py:577
  52.7 2.9 %collective-permute-start.19 = (f32[32,256]{1,0:T(8,128)S(1)}, f32[32,256]{1,0:T(8,128)S(1)}, u32[]{:S(2)}, u32[]{:S(2)}) collective-permute-start(f32[32,256]{1,0:T(8,128)S(1)} %get-tuple-element.120), channel_id=1, source_target_pairs={{26,31},{30,27}} | collective-permute-start | bytes 98312 | tf_op jit(solution)/shard_map/ppermute | solution.py:579
  54.3 5.2 %collective-permute-start.21 = (f32[32,256]{1,0:T(8,128)S(1)}, f32[32,256]{1,0:T(8,128)S(1)}, u32[]{:S(2)}, u32[]{:S(2)}) collective-permute-start(f32[32,256]{1,0:T(8,128)S(1)} %get-tuple-element.127), channel_id=1, source_target_pairs={{8,4},{12,0},{9,5},{13,1},{10,6},{14,2},{11,7},{15,3},{16,12},{20,... | collective-permute-start | bytes 98312 | tf_op jit(solution)/shard_map/ppermute | solution.py:585
  56.1 8.1 %collective-permute-start.22 = (f32[2,32,256]{2,1,0:T(8,128)S(1)}, f32[2,32,256]{2,1,0:T(8,128)S(1)}, u32[]{:S(2)}, u32[]{:S(2)}) collective-permute-start(f32[2,32,256]{2,1,0:T(8,128)S(1)} %pad_maximum_fusion), channel_id=1, source_target_pairs={{1,4},{5,0},{2,5},{6,1},{3,6},{7,2},{9,12},{13,8},{10,13},{14,9},{... | collective-permute-start | bytes 196616 | tf_op jit(solution)/shard_map/ppermute | solution.py:587
  59.1 5.8 %collective-permute-start.20 = (f32[2,2,16,16,128]{4,3,2,1,0:T(8,128)S(1)}, f32[2,2,16,16,128]{4,3,2,1,0:T(8,128)S(1)}, u32[]{:S(2)}, u32[]{:S(2)}) collective-permute-start(f32[2,2,16,16,128]{4,3,2,1,0:T(8,128)S(1)} %get-tuple-element.126), channel_id=1, source_target_pairs={{0,4},{4,0},{1,5},{5,1},{2,6},{6,2},{3,7},{7,3},{8,12},{12,8},{9,1... | collective-permute-start | bytes 1572872 | tf_op jit(solution)/shard_map/ppermute | solution.py:599
  64.3 1.5 %collective-permute-start.23 = (f32[64,256]{1,0:T(8,128)S(1)}, f32[64,256]{1,0:T(8,128)S(1)}, u32[]{:S(2)}, u32[]{:S(2)}) collective-permute-start(f32[64,256]{1,0:T(8,128)S(1)} %pad_maximum_fusion.1), channel_id=1, source_target_pairs={{0,4},{4,0},{1,5},{5,1},{2,6},{6,2},{3,7},{7,3},{8,12},{12,8},{9,1... | collective-permute-start | bytes 196616 | tf_op jit(solution)/shard_map/ppermute | solution.py:602
